TPU v7x, 512 devices: a whole 4x8x8 slice. The times are simulated.
512 devices in a mesh: group: 2 (over core), dp: 16 (over y, z_hi), tensor: 16 (over z_lo, x).
Axes of the slice: x: 4, y: 8, z: 8 (z_hi: 2, z_lo: 4; z = z_hi * 4 + z_lo), core: 2. Of those that a mesh axis runs over, the one named last changes fastest.
Arguments:
- activations: bfloat16 [2, 4096, 8192], P('group', 'dp', 'tensor'), may hold values from -6 to 6
- cotangent: bfloat16 [2, 4096, 5120], P('group', 'dp'), may hold values from -6 to 6
- weight: bfloat16 [8192, 5120], P('tensor', 'dp'), may hold values from -0.0625 to 0.0625
- moment_one: float32 [2, 8192, 5120], P('group', 'tensor', 'dp'), may hold values from -256 to 256
- moment_two: float32 [2, 8192, 5120], P('group', 'tensor', 'dp'), may hold values from 500 to 8000
- queries: bfloat16 [4, 32, 8192], P(None, 'dp', 'tensor'), may hold values from -6 to 6
- cache_keys: bfloat16 [32, 2048, 128], P('dp'), may hold values from -6 to 6
- cache_values: bfloat16 [32, 2048, 128], P('dp'), may hold values from -6 to 6
- new_keys: bfloat16 [4, 32, 1024], P(None, 'dp'), may hold values from -16 to 16
- new_values: bfloat16 [4, 32, 1024], P(None, 'dp'), may hold values from -6 to 6
- lengths: int32 [32], P('dp'), may hold values from 2 to 256, as said below
- token_ids: int32 [4, 32], P(None, 'dp'), may hold values from 0 to 151935, as said below
Outputs:
- update: bfloat16 [8192, 5120], P('tensor', 'dp')
- decoded: bfloat16 [4, 32, 5120], P(None, 'dp')
Inputs may be any that keep to these rules, and one draw needn't show every extreme that they name: Slots 0 to lengths[r] - 1 of row r hold keys and values; one row of every draw fills all 256 slots. `token_ids`: the id 151645 ends a row's response; the steps after it are padding.
All inputs are finite; a program needn't handle non-finite values.
Results may differ from a plain program's by a relative error of at most 0.0016.
The roundings to bfloat16 on the way count: a program that leaves them out, or rounds other values in their place, can miss the bound.
Values may be sent and summed in bfloat16 or wider, within the bound.
No kernel may reach another device: no remote copies, remote signals or barrier semaphores. Data moves between devices by JAX's collectives and lax.ppermute only.
A program may use at most 64 MiB of HBM per device.

v0:
```python
import math

import jax
import jax.numpy as jnp
from jax import lax
from jax.sharding import PartitionSpec as P

D = 5120
KVH = 8
HD = 128
EOS = 151645
STEPS = 4
CACHE = 256


learning_rate = 0.0003
weight_decay = 0.1
beta_one = 0.9
beta_two = 0.95
first_bias = 1.0 - 0.9**10
second_bias = 1.0 - 0.95**10
epsilon = 1e-08


def shifted(value, axis, steps):
    count = lax.axis_size(axis)
    leading, last = (max(0, -steps), min(count, count - steps))
    return lax.ppermute(value, axis, [(source, source + steps) for source in range(leading, last)])


def adam_direction(gradient, moment_one, moment_two):
    first_moment = beta_one * moment_one + (1.0 - beta_one) * gradient
    second_moment = beta_two * moment_two + (1.0 - beta_two) * gradient * gradient
    return (first_moment / first_bias / (jnp.sqrt(second_moment / second_bias) + epsilon)).astype(
        jnp.bfloat16
    )


def renew(weight, update):
    widened = weight.astype(jnp.float32)
    return (widened - learning_rate * (update.astype(jnp.float32) + weight_decay * widened)).astype(
        jnp.bfloat16
    )


def attend(
    queries, key_blocks, value_blocks, positions, fresh_keys, fresh_values, lengths, token_ids
):
    step_count = queries.shape[0]
    row_count = queries.shape[1]
    kv_count = key_blocks.shape[1]
    query_blocks = queries.reshape(step_count, row_count, kv_count, -1, HD)
    score_scale = 1.0 / math.sqrt(HD)
    cache_scores = (
        jnp.einsum(
            "trkgd,rkpd->trkgp", query_blocks, key_blocks, preferred_element_type=jnp.float32
        )
        * score_scale
    )
    step_scores = (
        jnp.einsum(
            "trkgd,urkd->trkgu", query_blocks, fresh_keys, preferred_element_type=jnp.float32
        )
        * score_scale
    )
    cache_valid = positions[None, :] < lengths[:, None]
    step_index = jnp.arange(step_count, dtype=jnp.int32)
    step_valid = step_index[None, :] <= step_index[:, None]
    cache_scores = jnp.where(cache_valid[None, :, None, None, :], cache_scores, -jnp.inf)
    step_scores = jnp.where(step_valid[:, None, None, None, :], step_scores, -jnp.inf)
    peak = jnp.maximum(jnp.max(cache_scores, axis=-1), jnp.max(step_scores, axis=-1))[..., None]
    cache_exp = jnp.exp(cache_scores - peak)
    step_exp = jnp.exp(step_scores - peak)
    denominator = jnp.sum(cache_exp, axis=-1, keepdims=True) + jnp.sum(
        step_exp, axis=-1, keepdims=True
    )
    cache_probs = (cache_exp / denominator).astype(jnp.bfloat16)
    step_probs = (step_exp / denominator).astype(jnp.bfloat16)
    mixed = jnp.einsum(
        "trkgp,rkpd->trkgd", cache_probs, value_blocks, preferred_element_type=jnp.float32
    )
    mixed = mixed + jnp.einsum(
        "trkgu,urkd->trkgd", step_probs, fresh_values, preferred_element_type=jnp.float32
    )
    finished = (token_ids == EOS).astype(jnp.int32)
    earlier = jnp.cumsum(finished, axis=0) - finished
    mixed = jnp.where((earlier == 0)[:, :, None, None, None], mixed, 0.0)
    return mixed.astype(jnp.bfloat16).reshape(step_count, row_count, -1)


def local(
    activations,
    cotangent,
    weight,
    moment_one,
    moment_two,
    queries,
    cache_keys,
    cache_values,
    new_keys,
    new_values,
    lengths,
    token_ids,
):
    side_index = lax.axis_index("group")
    columns = lax.all_to_all(cotangent[0], "dp", split_axis=1, concat_axis=0, tiled=True)
    gradient = lax.dot_general(
        lax.all_gather(activations[0], "dp", axis=0, tiled=True),
        columns,
        (((0,), (0,)), ((), ())),
        preferred_element_type=jnp.float32,
    )
    update = adam_direction(gradient, moment_one[0], moment_two[0])
    tensor_count = lax.axis_size("tensor")
    tensor_index = lax.axis_index("tensor")
    row_count = queries.shape[1]
    kv_count = max(1, KVH // tensor_count)
    kv_first = tensor_index * KVH // tensor_count
    positions = jnp.arange(CACHE, dtype=jnp.int32)
    key_blocks = lax.dynamic_slice_in_dim(
        cache_keys, kv_first * CACHE, kv_count * CACHE, 1
    ).reshape(row_count, kv_count, CACHE, HD)
    value_blocks = lax.dynamic_slice_in_dim(
        cache_values, kv_first * CACHE, kv_count * CACHE, 1
    ).reshape(row_count, kv_count, CACHE, HD)
    fresh_keys = lax.dynamic_slice_in_dim(new_keys, kv_first * HD, kv_count * HD, 2).reshape(
        STEPS, row_count, kv_count, HD
    )
    fresh_values = lax.dynamic_slice_in_dim(new_values, kv_first * HD, kv_count * HD, 2).reshape(
        STEPS, row_count, kv_count, HD
    )
    attention = attend(
        queries, key_blocks, value_blocks, positions, fresh_keys, fresh_values, lengths, token_ids
    )
    attention_flat = attention.reshape(STEPS * row_count, attention.shape[2])
    got_update = shifted(update, "group", -1)
    taken_update = jnp.where(side_index == 1, update, got_update)
    renewed = renew(weight, taken_update)
    partial_value = jnp.dot(
        attention_flat,
        lax.all_gather(renewed, "dp", axis=1, tiled=True),
        preferred_element_type=jnp.float32,
    )
    summed = lax.psum(partial_value, "tensor")
    decoded = summed.astype(jnp.bfloat16).reshape(STEPS, row_count, D)
    return (taken_update, decoded)


def solution(mesh):
    return jax.shard_map(
        local,
        mesh=mesh,
        in_specs=(
            P("group", "dp", "tensor"),
            P("group", "dp", None),
            P("tensor", "dp"),
            P("group", "tensor", "dp"),
            P("group", "tensor", "dp"),
            P(None, "dp", "tensor"),
            P("dp", None, None),
            P("dp", None, None),
            P(None, "dp", None),
            P(None, "dp", None),
            P("dp"),
            P(None, "dp"),
        ),
        out_specs=(P("tensor", "dp"), P(None, "dp", None)),
        check_vma=False,
    )
```

profile of v0, /device:TPU:56, one launch (start us, length us, event | category | flops | bytes accessed | tf_op | source)
XLA Modules:
  0.0 434.2 jit_solution(14403573345072911565)
XLA Ops:
  7.2 0.0 copy-start
  7.2 0.0 all-gather.6.cloned.1.call-start
  7.2 0.7 all-gather.6.cloned.1.call-update
  7.9 0.0 all-gather.4.cloned.1.call-start
  8.0 4.4 %copy.21 = bf16[1,256,5120]{1,2,0:T(8,128)(2,1)} copy(bf16[1,256,5120]{2,1,0:T(8,128)(2,1)} %param.13) | data formatting | bytes 5242880 | tf_op args[1]
  12.4 0.0 copy-start.4
  12.4 0.0 copy-start.5
  12.4 88.3 %all_to_all.19 = bf16[256,16,320]{0,2,1:T(8,128)(2,1)S(1)} all-to-all(bf16[256,16,320]{0,2,1:T(8,128)(2,1)} %bitcast.87), channel_id=1, replica_groups=mesh['group'=2,'dp'=16,'tensor'=16] {'dp'}, dimensions={1} | all-to-all | bytes 5242880 | tf_op jit(solution)/shard_map/all_to_all | solution.py:106
  100.7 1.9 copy.39
  102.6 89.9 %all-gather.6.cloned.1.call-done = bf16[1,4096,512]{2,1,0:T(8,128)(2,1)} async-done(((bf16[1,256,512]{2,1,0:T(8,128)(2,1)}), bf16[1,4096,512]{2,1,0:T(8,128)(2,1)}) %all-gather.6.cloned.1.call-update) | async-done | bytes 4194320 | tf_op jit(solution)/shard_map/all_gather | solution.py:108
  192.5 0.0 copy-done.4
  192.5 0.0 copy-done.5
  192.5 0.0 copy-start.1
  192.5 0.0 copy-start.2
  192.5 0.0 copy-start.3
  192.5 0.0 copy-start.6
  192.5 4.9 %fusion.19 = bf16[512,320]{0,1:T(8,128)(2,1)S(1)} fusion(f32[1,512,320]{1,2,0:T(8,128)S(1)} %copy-done.4, bf16[4096,320]{0,1:T(8,128)(2,1)} %bitcast.88, bf16[1,4096,512]{2,1,0:T(8,128)(2,1)} %all-gather.6.cloned.1.call-done, f32[1,512,320]{1,2,0:T(8,128)S(1)} %copy-done.5), kind=kOutput, calls=%fused_computation.24 | convolution fusion | flops 1344143360 | bytes 8454144 | tf_op jit(solution)/shard_map/dot_general | solution.py:107
  197.4 1.3 collective-permute-start
  198.7 2.2 collective-permute-done
  200.9 0.0 copy-done.1
  200.9 1.0 fusion.10
  202.0 0.0 all-gather.4.cloned.1.call-update
  202.0 0.0 copy-done.2
  202.0 0.0 copy-done.3
  202.1 0.2 reduce_window_sum.11
  202.2 0.7 constant_dynamic-slice_fusion
  202.9 0.2 convolution_multiply_fusion.1
  203.1 0.1 fusion.31
  203.2 0.0 copy-done.6
  203.2 0.1 iota_compare_fusion.1
  203.3 0.0 copy-done
  203.3 0.2 fusion.41
  203.6 0.1 fusion.30
  203.7 0.2 fusion.27
  203.9 0.1 fusion.36
  203.9 1.1 fusion.23
  205.1 0.2 fusion.5
  205.3 138.2 %all-gather.4.cloned.1.call-done = bf16[512,5120]{0,1:T(8,128)(2,1)} async-done(((bf16[512,320]{0,1:T(8,128)(2,1)}), bf16[512,5120]{0,1:T(8,128)(2,1)}) %all-gather.4.cloned.1.call-update) | async-done | bytes 5242896 | tf_op jit(solution)/shard_map/all_gather | solution.py:141
  343.5 3.9 fusion.32
  347.4 79.3 %all-reduce.1 = bf16[8,5120]{1,0:T(8,128)(2,1)S(1)} all-reduce(f32[8,5120]{1,0:T(8,128)S(1)} %fusion.32), channel_id=1, replica_groups=mesh['group'=2,'dp'=16,'tensor'=16] {'tensor'}, use_global_device_ids=true, to_apply=%region_5.6 | all-reduce | flops 40960 | bytes 245760 | tf_op jit(solution)/shard_map/psum | solution.py:144
  426.7 0.7 reshape.120
  (7 shorter events, 0.1 us)
Async XLA Ops:
  7.2 196.1 %copy-start = (bf16[2,2048,128]{2,1,0:T(8,128)(2,1)S(1)}, bf16[2,2048,128]{2,1,0:T(8,128)(2,1)}, u32[]{:S(2)}) copy-start(bf16[2,2048,128]{2,1,0:T(8,128)(2,1)} %param.18) | copy-start | bytes 3145732
  7.2 185.3 %all-gather.6.cloned.1.call-start = ((), (), s32[]{:S(2)}) async-start(), calls=%async_computation.2 | async-start | bytes 4456448 | tf_op jit(solution)/shard_map/all_gather | solution.py:108
  7.9 335.6 %all-gather.4.cloned.1.call-start = ((), (), s32[]{:S(2)}) async-start(), calls=%async_computation.1 | async-start | bytes 5570560 | tf_op jit(solution)/shard_map/all_gather | solution.py:141
  12.4 180.1 %copy-start.4 = (f32[1,512,320]{1,2,0:T(8,128)S(1)}, f32[1,512,320]{1,2,0:T(8,128)}, u32[]{:S(2)}) copy-start(f32[1,512,320]{1,2,0:T(8,128)} %param.16) | copy-start | bytes 1966084
  12.4 180.1 %copy-start.5 = (f32[1,512,320]{1,2,0:T(8,128)S(1)}, f32[1,512,320]{1,2,0:T(8,128)}, u32[]{:S(2)}) copy-start(f32[1,512,320]{1,2,0:T(8,128)} %param.15) | copy-start | bytes 1966084
  192.5 8.4 %copy-start.1 = (bf16[512,320]{0,1:T(8,128)(2,1)S(1)}, bf16[512,320]{0,1:T(8,128)(2,1)}, u32[]{:S(2)}) copy-start(bf16[512,320]{0,1:T(8,128)(2,1)} %param.14) | copy-start | bytes 983044
  192.5 9.5 %copy-start.2 = (bf16[4,2,512]{2,1,0:T(2,128)(2,1)S(1)}, bf16[4,2,512]{2,1,0:T(2,128)(2,1)}, u32[]{:S(2)}) copy-start(bf16[4,2,512]{2,1,0:T(2,128)(2,1)} %param.17) | copy-start | bytes 24580
  192.5 9.6 %copy-start.3 = (s32[4,2]{0,1:T(2,128)S(1)}, s32[4,2]{0,1:T(2,128)}, u32[]{:S(2)}) copy-start(s32[4,2]{0,1:T(2,128)} %param.23) | copy-start | bytes 100
  192.5 10.7 %copy-start.6 = (s32[2]{0:T(128)S(1)}, s32[2]{0:T(128)}, u32[]{:S(2)}) copy-start(s32[2]{0:T(128)} %param.22) | copy-start | bytes 28
  197.4 3.5 collective-permute-start
Sparse Core Ops, SparseCore 0:
  11.2 181.2 all-gather.5
  202.1 141.3 all-gather.3
where the time goes:
time: 436 us; the launch traced here: 434 us
  waiting for transfers between devices  231 us (53%)
  blocking collectives  168 us (39%)
  between operations  14.2 us (3%)
  matrix products  10.5 us (2%)
  local copies, waits for them, and re-layouts  7.73 us (2%)
    all_gather x1, waiting for transfers between devices, local(): lax.all_gather(renewed, 'dp', axis=1, tiled=True)  138 us
    all_gather x1, waiting for transfers between devices, local(): lax.all_gather(activations[0], 'dp', axis=0, tiled=True)  89.9 us
    all_to_all x1, blocking collectives, local(): lax.all_to_all(cotangent[0], 'dp', split_axis=1, concat_axis=0, tiled=True)  88.3 us
    psum x1, blocking collectives, local(): summed = lax.psum(partial_value, 'tensor')  79.3 us
  transfers between devices with their start and end apart: 3, of which 3 were waited for; matrix products, arithmetic and copies ran while one was open for 2% of the time, Pallas kernels for 0%

commit v1 on v0

v1 whole, which is shorter than its diff:
```python
import functools
import math

import jax
import jax.numpy as jnp
import numpy as np
from jax import lax
from jax.experimental import pallas as pl
from jax.experimental.pallas import tpu as pltpu
from jax.sharding import PartitionSpec as P

D = 5120
KVH = 8
HD = 128
EOS = 151645
STEPS = 4
CACHE = 256

learning_rate = 0.0003
weight_decay = 0.1
beta_one = 0.9
beta_two = 0.95
first_bias = 1.0 - 0.9**10
second_bias = 1.0 - 0.95**10
epsilon = 1e-08

AXES = ("group", "dp", "tensor")
SHAPE = (2, 8, 2, 4, 4)
TOK = 256
FEAT = 512
COLS = 320
ROWS = 8
PAD = 16
HOPS = (0, 1, 2, 3, 4, -1, -2, -3)
f32, bf16 = jnp.float32, jnp.bfloat16


def permute(value, target):
    pairs = []
    for flat, place in enumerate(np.ndindex(*SHAPE)):
        to = target(*place)
        if to is not None:
            pairs.append((flat, int(np.ravel_multi_index(to, SHAPE))))
    return lax.ppermute(value, AXES, pairs)


def keeper(zh, x):
    return 1 if (x & 1) == zh else 0


def to_partner(g, y, zh, zl, x):
    return (0, y, 1 - zh, zl, x) if g == 1 else None


def along_y(step):
    return lambda g, y, zh, zl, x: (g, (y + step) % 8, zh, zl, x)


def transposed(g, y, zh, zl, x):
    return (g, zl * 2 + (x >> 1), x & 1, y >> 1, (y & 1) * 2 + zh)


def cot_transposed(g, y, zh, zl, x):
    if g == 0:
        return None
    _, y2, zh2, zl2, x2 = transposed(g, y, zh, zl, x)
    return (keeper(zh2, x2), y2, zh2, zl2, x2)


def along_zl(flip):
    def target(g, y, zh, zl, x):
        return (g, y, zh, zl ^ flip, x) if g == keeper(zh, x) else None

    return target


def along_x(step):
    def target(g, y, zh, zl, x):
        return (g, y, zh, zl, (x + step) % 4) if g == keeper(zh, x) else None

    return target


def other_core(g, y, zh, zl, x):
    return (1 - g, y, zh, zl, x)


def to_rollout(g, y, zh, zl, x):
    return (0, y, zh, zl, x) if g == 1 else None


def attend_kernel(head_ref, lengths_ref, ids_ref, q_ref, k_ref, v_ref, nk_ref, nv_ref, out_ref):
    queries = q_ref[...]
    query = jnp.concatenate(
        [queries[:, h * HD : (h + 1) * HD] for h in range(4)], axis=0
    ).astype(bf16)
    keys = k_ref[...].reshape(2 * CACHE, HD)
    values = v_ref[...].reshape(2 * CACHE, HD)
    fresh_keys = nk_ref[...].astype(bf16)
    fresh_values = nv_ref[...].astype(bf16)
    scale = 1.0 / math.sqrt(HD)
    nt = (((1,), (1,)), ((), ()))
    cache_scores = lax.dot_general(query, keys, nt, preferred_element_type=f32) * scale
    step_scores = lax.dot_general(query, fresh_keys, nt, preferred_element_type=f32) * scale
    count = 4 * ROWS

    def place(width):
        place_row = lax.broadcasted_iota(jnp.int32, (count, width), 0) & (ROWS - 1)
        place_key = lax.broadcasted_iota(jnp.int32, (count, width), 1)
        return place_row >> 1, place_row & 1, place_key

    step, row, key = place(2 * CACHE)
    length = jnp.where(row == 0, lengths_ref[0], lengths_ref[1])
    cache_valid = ((key >> 8) == row) & ((key & (CACHE - 1)) < length)
    step, row, key = place(ROWS)
    step_valid = ((key & 1) == row) & ((key >> 1) <= step)
    cache_scores = jnp.where(cache_valid, cache_scores, -jnp.inf)
    step_scores = jnp.where(step_valid, step_scores, -jnp.inf)
    peak = jnp.maximum(
        jnp.max(cache_scores, axis=-1, keepdims=True), jnp.max(step_scores, axis=-1, keepdims=True)
    )
    cache_exp = jnp.exp(cache_scores - peak)
    step_exp = jnp.exp(step_scores - peak)
    denominator = jnp.sum(cache_exp, axis=-1, keepdims=True) + jnp.sum(
        step_exp, axis=-1, keepdims=True
    )
    cache_probs = (cache_exp / denominator).astype(bf16)
    step_probs = (step_exp / denominator).astype(bf16)
    nn = (((1,), (0,)), ((), ()))
    mixed = lax.dot_general(cache_probs, values, nn, preferred_element_type=f32)
    mixed = mixed + lax.dot_general(step_probs, fresh_values, nn, preferred_element_type=f32)
    step, row, _ = place(HD)
    dead = jnp.zeros((count, HD), jnp.int32)
    for u in range(STEPS - 1):
        for r in range(2):
            ended = (ids_ref[u, r] == EOS).astype(jnp.int32)
            dead = dead + jnp.where((row == r) & (step > u), ended, 0)
    mixed = jnp.where(dead == 0, mixed, 0.0)
    flat = jnp.concatenate([mixed[h * ROWS : (h + 1) * ROWS] for h in range(4)], axis=1)
    out_ref[...] = jnp.concatenate([flat, jnp.zeros_like(flat)], axis=0).astype(bf16)


def attend(head, queries, cache_keys, cache_values, new_keys, new_values, lengths, token_ids):
    whole = lambda *shape: pl.BlockSpec(shape, lambda i, *_: (0,) * len(shape))
    cache = pl.BlockSpec((2, CACHE, HD), lambda i, m, *_: (0, m[0], 0))
    fresh = pl.BlockSpec((ROWS, HD), lambda i, m, *_: (0, m[0]))
    return pl.pallas_call(
        attend_kernel,
        out_shape=jax.ShapeDtypeStruct((PAD, FEAT), bf16),
        grid_spec=pltpu.PrefetchScalarGridSpec(
            num_scalar_prefetch=3,
            grid=(1,),
            in_specs=[whole(ROWS, FEAT), cache, cache, fresh, fresh],
            out_specs=whole(PAD, FEAT),
        ),
        name="attend",
    )(
        head,
        lengths,
        token_ids,
        queries.astype(f32).reshape(ROWS, FEAT),
        cache_keys,
        cache_values,
        new_keys.astype(f32).reshape(ROWS, KVH * HD),
        new_values.astype(f32).reshape(ROWS, KVH * HD),
    )


def gradient_kernel(index_ref, *refs):
    chunks, blocks, out_ref = refs[:8], refs[8:12], refs[12]
    for n in range(8):
        slot, which = index_ref[8 + n], index_ref[16 + n]
        block = blocks[0][slot]
        for b in range(1, 4):
            block = jnp.where(which == b, blocks[b][slot], block)
        part = jnp.dot(block, chunks[n][:TOK, :], preferred_element_type=f32)
        if n == 0:
            out_ref[:COLS, :] = part
        else:
            out_ref[:COLS, :] += part
        place = pl.multiple_of(COLS + index_ref[n] * ROWS, ROWS)
        out_ref[pl.ds(place, ROWS), :] = chunks[n][TOK:, :].astype(f32)[:ROWS]


def gradient(index, chunks, blocks):
    vmem = pl.BlockSpec(memory_space=pltpu.VMEM)
    return pl.pallas_call(
        gradient_kernel,
        out_shape=jax.ShapeDtypeStruct((COLS + 8 * ROWS, FEAT), f32),
        in_specs=[pl.BlockSpec(memory_space=pltpu.SMEM)] + [vmem] * 12,
        out_specs=vmem,
        compiler_params=pltpu.CompilerParams(vmem_limit_bytes=32 * 2**20),
        cost_estimate=pl.CostEstimate(
            flops=2 * 8 * TOK * COLS * FEAT, bytes_accessed=6 * 2**20, transcendentals=0
        ),
        name="gradient",
    )(index, *chunks, *blocks)


def step_kernel(
    side_ref, mine_ref, got_ref, one_ref, one_got, two_ref, two_got, weight_ref, update_ref, out_ref
):
    learner = side_ref[0] == 1
    grad = mine_ref[:COLS, :] + got_ref[:COLS, :]
    moment_one = jnp.where(learner, one_ref[...], one_got[...])
    moment_two = jnp.where(learner, two_ref[...], two_got[...])
    first_moment = beta_one * moment_one + (1.0 - beta_one) * grad
    second_moment = beta_two * moment_two + (1.0 - beta_two) * grad * grad
    update = (
        first_moment / first_bias / (jnp.sqrt(second_moment / second_bias) + epsilon)
    ).astype(bf16)
    update_ref[...] = update
    widened = weight_ref[...].astype(f32)
    renewed = (
        widened - learning_rate * (update.astype(f32) + weight_decay * widened)
    ).astype(bf16)
    mine, got = mine_ref[COLS:, :], got_ref[COLS:, :]
    even = side_ref[1] == 0
    for zh in range(2):
        rows = jnp.where(even, mine, got) if zh == 0 else jnp.where(even, got, mine)
        part = lax.dot_general(
            rows.astype(bf16), renewed, (((1,), (1,)), ((), ())), preferred_element_type=f32
        )
        for y in range(8):
            out_ref[y * 2 + zh] = part[y * ROWS : (y + 1) * ROWS]


def step(side, mine, got, one, one_got, two, two_got, weight):
    vmem = pl.BlockSpec(memory_space=pltpu.VMEM)
    return pl.pallas_call(
        step_kernel,
        out_shape=(
            jax.ShapeDtypeStruct((COLS, FEAT), bf16),
            jax.ShapeDtypeStruct((16, ROWS, COLS), f32),
        ),
        in_specs=[pl.BlockSpec(memory_space=pltpu.SMEM)] + [vmem] * 7,
        out_specs=(vmem, vmem),
        compiler_params=pltpu.CompilerParams(vmem_limit_bytes=32 * 2**20),
        name="step",
    )(side, mine, got, one, one_got, two, two_got, weight)


def local(
    activations,
    cotangent,
    weight,
    moment_one,
    moment_two,
    queries,
    cache_keys,
    cache_values,
    new_keys,
    new_values,
    lengths,
    token_ids,
):
    g = lax.axis_index("group")
    p = lax.axis_index("dp")
    q = lax.axis_index("tensor")
    y, zh, zl, x = p >> 1, p & 1, q >> 2, q & 3

    rows = attend(
        (q >> 1).reshape(1),
        queries,
        cache_keys,
        cache_values,
        new_keys,
        new_values,
        lengths,
        token_ids,
    )
    payload = jnp.concatenate([activations[0], rows], axis=0)
    base = jnp.where(g == 1, payload, permute(payload, to_partner))

    cut = lax.dynamic_slice_in_dim(cotangent[0], q * COLS, COLS, 1).T
    own = permute(cut, cot_transposed)
    pair = jnp.stack([own, permute(own, along_zl(3))])
    four = jnp.concatenate([pair, permute(pair, along_zl(1))], axis=0)
    from_left = permute(four, along_x(1))
    from_right = permute(four, along_x(-1))
    from_far = permute(four, along_x(2))

    up, down = [base], [base]
    for n in range(4):
        up.append(permute(up[-1], along_y(1)))
        if n < 3:
            down.append(permute(down[-1], along_y(-1)))
    chunks = up + down[1:]

    one, two = moment_one[0].T, moment_two[0].T
    one_got = permute(one, to_rollout)
    two_got = permute(two, to_rollout)

    origin = (y - np.array(HOPS, np.int32)) & 7
    parity = jnp.where(g == 1, zh, 1 - zh)
    flip = (origin >> 1) ^ zl
    slot = jnp.where(flip == 0, 0, jnp.where(flip == 3, 1, jnp.where(flip == 1, 2, 3)))
    source = 2 * (origin & 1) + parity
    keeps = parity == (x & 1)
    which = jnp.where(
        keeps, jnp.where(source == x, 0, 1), jnp.where(source == ((x - 1) & 3), 2, 3)
    )
    index = jnp.concatenate([origin, slot, which]).astype(jnp.int32)
    mine = gradient(index, chunks, (four, from_far, from_left, from_right))
    got = permute(mine, other_core)

    side = jnp.stack([g, parity]).astype(jnp.int32)
    update, partial = step(side, mine, got, one, one_got, two, two_got, weight.T)

    shares = lax.all_to_all(partial, "tensor", split_axis=0, concat_axis=0, tiled=True)
    summed = jnp.sum(shares, axis=0).astype(bf16)
    block = permute(summed, transposed)
    spread = jnp.broadcast_to(block[None], (16, ROWS, COLS))
    gathered = lax.all_to_all(spread, "tensor", split_axis=0, concat_axis=0, tiled=True)
    decoded = gathered.transpose(1, 0, 2).reshape(STEPS, ROWS // STEPS, D)
    return (update.T, decoded)


def solution(mesh):
    return jax.shard_map(
        local,
        mesh=mesh,
        in_specs=(
            P("group", "dp", "tensor"),
            P("group", "dp", None),
            P("tensor", "dp"),
            P("group", "tensor", "dp"),
            P("group", "tensor", "dp"),
            P(None, "dp", "tensor"),
            P("dp", None, None),
            P("dp", None, None),
            P(None, "dp", None),
            P(None, "dp", None),
            P("dp"),
            P(None, "dp"),
        ),
        out_specs=(P("tensor", "dp"), P(None, "dp", None)),
        check_vma=False,
    )
```

time: 436 us -> 147 us (0.34)
  the two profiles are of different devices: /device:TPU:56 before, /device:TPU:32 now
where the time goes in v1:
time: 147 us; the launch traced here: 146 us
  waiting for transfers between devices  44.5 us (30%)
  starting transfers between devices  44.2 us (30%)
  blocking collectives  36.6 us (25%)
  local copies, waits for them, and re-layouts  7.52 us (5%)
  Pallas kernels  7.4 us (5%)
  other arithmetic  4.59 us (3%)
    ppermute x18, waiting for transfers between devices, permute(): return lax.ppermute(value, AXES, pairs)  44.5 us
    ppermute x18, starting transfers between devices, permute(): return lax.ppermute(value, AXES, pairs)  44.2 us
    all_to_all x1, blocking collectives, local(): lax.all_to_all(partial, 'tensor', split_axis=0, concat_axis=0, tiled=True)  22.9 us
    all_to_all x1, blocking collectives, local(): lax.all_to_all(spread, 'tensor', split_axis=0, concat_axis=0, tiled=True)  13.6 us
  transfers between devices with their start and end apart: 18, of which 9 were waited for; matrix products, arithmetic and copies ran while one was open for 2% of the time, Pallas kernels for 0%

profile of v1, /device:TPU:32, one launch (start us, length us, event | category | flops | bytes accessed | tf_op | source)
XLA Modules:
  0.0 145.7 jit_solution(7378182599700981952)
XLA Ops:
  0.6 0.0 copy-start
  0.6 0.0 copy-start.6
  0.7 1.5 %copy.19.ids_ref = s32[4,2]{1,0:T(4,128)} copy(s32[4,2]{0,1:T(2,128)} %param.24) | data formatting | bytes 64 | tf_op args[11]
  2.2 1.3 reshape.36.q_ref
  3.5 1.3 reshape.38.nk_ref
  4.8 1.3 reshape.40.nv_ref
  6.1 2.8 %attend.1 = bf16[16,512]{1,0:T(8,128)(2,1)} custom-call(s32[1]{0:T(128)} %bitcast.3.head_ref, s32[2]{0:T(128)} %lengths_ref.1, s32[4,2]{1,0:T(4,128)} %copy.19.ids_ref, f32[8,512]{1,0:T(8,128)} %reshape.36.q_ref, bf16[2,2048,128]{2,1,0:T(8,128)(2,1)} %k_ref.1, bf16[2,2048,128]{2,1,0:T(8,128)(2,1)} %v_ref.1, f32[8,1024]{1,0:T(8,128)} %reshape.38.nk_ref, ...), custom_call_target="tpu_custom_call" | custom-call | tf_op jit(solution)/shard_map/attend/pallas_call | solution.py:147
  8.9 1.7 %pad_maximum_fusion.2 = bf16[272,512]{1,0:T(8,128)(2,1)} fusion(bf16[16,512]{1,0:T(8,128)(2,1)} %attend.1, bf16[256,512]{1,0:T(8,128)(2,1)} %bitcast.23), kind=kLoop, calls=%fused_computation.2 | loop fusion | flops 557056 | bytes 557056 | tf_op jit(solution)/shard_map/concatenate | solution.py:272
  10.6 1.3 collective-permute-start
  11.9 0.0 copy-done
  11.9 0.1 constant_dynamic-slice_fusion
  12.0 0.1 copy.20
  12.2 0.7 collective-permute-start.8
  12.8 0.0 collective-permute-done.8
  12.9 0.0 copy-start.7
  12.9 0.7 collective-permute-start.9
  13.5 11.4 %collective-permute-done = bf16[272,512]{1,0:T(8,128)(2,1)} collective-permute-done((bf16[272,512]{1,0:T(8,128)(2,1)}, bf16[272,512]{1,0:T(8,128)(2,1)}, u32[]{:S(2)}, u32[]{:S(2)}) %collective-permute-start) | collective-permute-done | bytes 278560 | tf_op jit(solution)/shard_map/ppermute | solution.py:44
  24.9 0.0 copy-done.6
  24.9 1.0 broadcast_select_fusion.refs_0_
  26.0 2.6 %collective-permute-start.1 = (bf16[272,512]{1,0:T(8,128)(2,1)S(1)}, bf16[272,512]{1,0:T(8,128)(2,1)S(1)}, u32[]{:S(2)}, u32[]{:S(2)}) collective-permute-start(bf16[272,512]{1,0:T(8,128)(2,1)S(1)} %broadcast_select_fusion.refs_0_), channel_id=1, source_target_pairs={{0,32},{1,33},{2,34},{3,35},{4,36},{5,37},{6,38},{7,39},{8,40},{9,... | collective-permute-start | bytes 835592 | tf_op jit(solution)/shard_map/ppermute | solution.py:44
  28.6 0.0 collective-permute-done.9
  28.6 0.7 collective-permute-start.10
  29.3 4.5 %collective-permute-start.5 = (bf16[272,512]{1,0:T(8,128)(2,1)S(1)}, bf16[272,512]{1,0:T(8,128)(2,1)}, u32[]{:S(2)}, u32[]{:S(2)}) collective-permute-start(bf16[272,512]{1,0:T(8,128)(2,1)S(1)} %broadcast_select_fusion.refs_0_), channel_id=1, source_target_pairs={{0,224},{1,225},{2,226},{3,227},{4,228},{5,229},{6,230},{7,231},{8... | collective-permute-start | bytes 835592 | tf_op jit(solution)/shard_map/ppermute | solution.py:44
  33.8 1.8 %collective-permute-done.1.refs_1_ = bf16[272,512]{1,0:T(8,128)(2,1)S(1)} collective-permute-done((bf16[272,512]{1,0:T(8,128)(2,1)S(1)}, bf16[272,512]{1,0:T(8,128)(2,1)S(1)}, u32[]{:S(2)}, u32[]{:S(2)}) %collective-permute-start.1) | collective-permute-done | bytes 278560 | tf_op jit(solution)/shard_map/ppermute | solution.py:44
  35.6 1.9 %collective-permute-start.2 = (bf16[272,512]{1,0:T(8,128)(2,1)S(1)}, bf16[272,512]{1,0:T(8,128)(2,1)}, u32[]{:S(2)}, u32[]{:S(2)}) collective-permute-start(bf16[272,512]{1,0:T(8,128)(2,1)S(1)} %collective-permute-done.1.refs_1_), channel_id=1, source_target_pairs={{0,32},{1,33},{2,34},{3,35},{4,36},{5,37},{6,38},{7,39},{8,40},{9,... | collective-permute-start | bytes 835592 | tf_op jit(solution)/shard_map/ppermute | solution.py:44
  37.5 0.0 copy-done.7
  37.6 0.0 collective-permute-done.10
  37.6 1.0 pad_maximum_fusion.refs_8_
  38.6 1.3 collective-permute-start.13
  39.9 1.3 collective-permute-start.12
  41.2 1.5 %collective-permute-start.11 = (bf16[4,320,256]{2,1,0:T(8,128)(2,1)S(1)}, bf16[4,320,256]{2,1,0:T(8,128)(2,1)}, u32[]{:S(2)}, u32[]{:S(2)}) collective-permute-start(bf16[4,320,256]{2,1,0:T(8,128)(2,1)S(1)} %pad_maximum_fusion.refs_8_), channel_id=1, source_target_pairs={{1,3},{3,1},{5,7},{7,5},{9,11},{11,9},{13,15},{15,13},{16,18},{18,... | collective-permute-start | bytes 1966088 | tf_op jit(solution)/shard_map/ppermute | solution.py:44
  42.7 0.0 collective-permute-done.5.refs_5_
  42.7 0.0 copy-done.4
  42.7 5.1 %collective-permute-start.6 = (bf16[272,512]{1,0:T(8,128)(2,1)}, bf16[272,512]{1,0:T(8,128)(2,1)}, u32[]{:S(2)}, u32[]{:S(2)}) collective-permute-start(bf16[272,512]{1,0:T(8,128)(2,1)} %collective-permute-done.5.refs_5_), channel_id=1, source_target_pairs={{0,224},{1,225},{2,226},{3,227},{4,228},{5,229},{6,230},{7,231},{8... | collective-permute-start | bytes 835592 | tf_op jit(solution)/shard_map/ppermute | solution.py:44
  47.8 0.0 collective-permute-done.2.refs_2_
  47.8 1.9 %collective-permute-start.3 = (bf16[272,512]{1,0:T(8,128)(2,1)}, bf16[272,512]{1,0:T(8,128)(2,1)}, u32[]{:S(2)}, u32[]{:S(2)}) collective-permute-start(bf16[272,512]{1,0:T(8,128)(2,1)} %collective-permute-done.2.refs_2_), channel_id=1, source_target_pairs={{0,32},{1,33},{2,34},{3,35},{4,36},{5,37},{6,38},{7,39},{8,40},{9,... | collective-permute-start | bytes 835592 | tf_op jit(solution)/shard_map/ppermute | solution.py:44
  49.8 2.4 %collective-permute-done.6.refs_6_ = bf16[272,512]{1,0:T(8,128)(2,1)} collective-permute-done((bf16[272,512]{1,0:T(8,128)(2,1)}, bf16[272,512]{1,0:T(8,128)(2,1)}, u32[]{:S(2)}, u32[]{:S(2)}) %collective-permute-start.6) | collective-permute-done | bytes 278560 | tf_op jit(solution)/shard_map/ppermute | solution.py:44
  52.2 5.6 %collective-permute-start.7 = (bf16[272,512]{1,0:T(8,128)(2,1)}, bf16[272,512]{1,0:T(8,128)(2,1)S(1)}, u32[]{:S(2)}, u32[]{:S(2)}) collective-permute-start(bf16[272,512]{1,0:T(8,128)(2,1)} %collective-permute-done.6.refs_6_), channel_id=1, source_target_pairs={{0,224},{1,225},{2,226},{3,227},{4,228},{5,229},{6,230},{7,231},{8... | collective-permute-start | bytes 835592 | tf_op jit(solution)/shard_map/ppermute | solution.py:44
  57.8 0.0 collective-permute-done.3.refs_3_
  57.8 1.9 %collective-permute-start.4 = (bf16[272,512]{1,0:T(8,128)(2,1)}, bf16[272,512]{1,0:T(8,128)(2,1)S(1)}, u32[]{:S(2)}, u32[]{:S(2)}) collective-permute-start(bf16[272,512]{1,0:T(8,128)(2,1)} %collective-permute-done.3.refs_3_), channel_id=1, source_target_pairs={{0,32},{1,33},{2,34},{3,35},{4,36},{5,37},{6,38},{7,39},{8,40},{9,... | collective-permute-start | bytes 835592 | tf_op jit(solution)/shard_map/ppermute | solution.py:44
  59.7 0.7 add_and_fusion
  60.4 0.1 pad_add_fusion.1.index_ref
  60.5 1.7 %collective-permute-done.7.refs_7_ = bf16[272,512]{1,0:T(8,128)(2,1)S(1)} collective-permute-done((bf16[272,512]{1,0:T(8,128)(2,1)}, bf16[272,512]{1,0:T(8,128)(2,1)S(1)}, u32[]{:S(2)}, u32[]{:S(2)}) %collective-permute-start.7) | collective-permute-done | bytes 278560 | tf_op jit(solution)/shard_map/ppermute | solution.py:44
  62.2 5.5 %collective-permute-done.13.refs_11_ = bf16[4,320,256]{2,1,0:T(8,128)(2,1)} collective-permute-done((bf16[4,320,256]{2,1,0:T(8,128)(2,1)S(1)}, bf16[4,320,256]{2,1,0:T(8,128)(2,1)}, u32[]{:S(2)}, u32[]{:S(2)}) %collective-permute-start.13) | collective-permute-done | bytes 655392 | tf_op jit(solution)/shard_map/ppermute | solution.py:44
  67.7 10.0 %collective-permute-done.12.refs_10_ = bf16[4,320,256]{2,1,0:T(8,128)(2,1)} collective-permute-done((bf16[4,320,256]{2,1,0:T(8,128)(2,1)S(1)}, bf16[4,320,256]{2,1,0:T(8,128)(2,1)}, u32[]{:S(2)}, u32[]{:S(2)}) %collective-permute-start.12) | collective-permute-done | bytes 655392 | tf_op jit(solution)/shard_map/ppermute | solution.py:44
  77.7 0.0 collective-permute-done.11.refs_9_
  77.7 0.0 collective-permute-done.4.refs_4_
  77.7 1.0 copy-done.5
  78.7 2.7 %gradient.1.mine_ref = f32[384,512]{1,0:T(8,128)S(1)} custom-call(s32[24]{0:T(128)S(1)} %pad_add_fusion.1.index_ref, bf16[272,512]{1,0:T(8,128)(2,1)S(1)} %broadcast_select_fusion.refs_0_, bf16[272,512]{1,0:T(8,128)(2,1)S(1)} %copy-done.5, bf16[272,512]{1,0:T(8,128)(2,1)} %collective-permute-done.2.refs_2_, bf16[272,512]{1,0:T(8,128)(2,1)} %collective-permute-done.3.refs_3_, ...), custom_call_target="tpu_custom_call" | custom-call | flops 671088640 | bytes 6291456 | tf_op jit(solution)/shard_map/gradient/pallas_call | solution.py:187
  81.4 8.4 %collective-permute-start.14 = (f32[384,512]{1,0:T(8,128)S(1)}, f32[384,512]{1,0:T(8,128)S(1)}, u32[]{:S(2)}, u32[]{:S(2)}) collective-permute-start(f32[384,512]{1,0:T(8,128)S(1)} %gradient.1.mine_ref), channel_id=1, source_target_pairs={{0,256},{1,257},{2,258},{3,259},{4,260},{5,261},{6,262},{7,263},{8... | collective-permute-start | bytes 2359304 | tf_op jit(solution)/shard_map/ppermute | solution.py:44
  89.8 0.0 copy-done.1
  89.8 1.3 collective-permute-start.15
  91.1 1.3 collective-permute-start.16
  92.4 0.1 pad_add_fusion.side_ref
  92.5 1.3 collective-permute-done.15.one_got
  93.8 1.3 collective-permute-done.16.two_got
  95.1 0.0 collective-permute-done.14.got_ref
  95.1 0.0 copy-done.3
  95.1 1.9 %step.1 = (bf16[320,512]{1,0:T(8,128)(2,1)}, f32[16,8,320]{2,1,0:T(8,128)S(1)}) custom-call(s32[2]{0:T(128)S(1)} %pad_add_fusion.side_ref, f32[384,512]{1,0:T(8,128)S(1)} %gradient.1.mine_ref, f32[384,512]{1,0:T(8,128)S(1)} %collective-permute-done.14.got_ref, f32[320,512]{1,0:T(8,128)S(1)} %bitcast.19, f32[320,512]{1,0:T(8,128)S(1)} %collective-permute-done.15.one_got, ...), custom_call_target="tpu_custom_call" | custom-call | tf_op jit(solution)/shard_map/step/pallas_call | solution.py:230
  97.1 22.9 %all_to_all.10 = f32[16,8,320]{2,1,0:T(8,128)S(1)} all-to-all(f32[16,8,320]{2,1,0:T(8,128)S(1)} %get-tuple-element.5), channel_id=1, replica_groups=mesh['group'=2,'dp'=16,'tensor'=16] {'tensor'}, dimensions={0} | all-to-all | bytes 327680 | tf_op jit(solution)/shard_map/all_to_all | solution.py:310
  120.0 2.4 %collective-permute-start.17 = (bf16[8,320]{1,0:T(8,128)(2,1)S(1)}, bf16[8,320]{1,0:T(8,128)(2,1)S(1)}, u32[]{:S(2)}, u32[]{:S(2)}) collective-permute-start(bf16[8,320]{1,0:T(8,128)(2,1)S(1)} %reduce_sum.9), channel_id=1, source_target_pairs={{0,0},{1,16},{2,32},{3,48},{4,64},{5,80},{6,96},{7,112},{8,128},{9... | collective-permute-start | bytes 15368 | tf_op jit(solution)/shard_map/ppermute | solution.py:44
  122.4 8.9 %collective-permute-done.17 = bf16[8,320]{1,0:T(8,128)(2,1)S(1)} collective-permute-done((bf16[8,320]{1,0:T(8,128)(2,1)S(1)}, bf16[8,320]{1,0:T(8,128)(2,1)S(1)}, u32[]{:S(2)}, u32[]{:S(2)}) %collective-permute-start.17) | collective-permute-done | bytes 5152 | tf_op jit(solution)/shard_map/ppermute | solution.py:44
  131.3 13.6 %all_to_all.11 = bf16[16,8,320]{2,1,0:T(8,128)(2,1)S(1)} all-to-all(bf16[16,8,320]{2,1,0:T(8,128)(2,1)S(1)} %broadcast_in_dim.20), channel_id=1, replica_groups=mesh['group'=2,'dp'=16,'tensor'=16] {'tensor'}, dimensions={0} | all-to-all | bytes 163840 | tf_op jit(solution)/shard_map/all_to_all | solution.py:314
  144.9 0.8 reshape.34
  (10 shorter events, 0.1 us)
Async XLA Ops:
  0.6 11.2 %copy-start = (bf16[1,256,5120]{2,1,0:T(8,128)(2,1)S(1)}, bf16[1,256,5120]{2,1,0:T(8,128)(2,1)}, u32[]{:S(2)}) copy-start(bf16[1,256,5120]{2,1,0:T(8,128)(2,1)} %param.14) | copy-start | bytes 7864324
  0.6 24.3 %copy-start.6 = (bf16[1,256,512]{2,1,0:T(8,128)(2,1)S(1)}, bf16[1,256,512]{2,1,0:T(8,128)(2,1)}, u32[]{:S(2)}) copy-start(bf16[1,256,512]{2,1,0:T(8,128)(2,1)} %param.13) | copy-start | bytes 786436
  10.6 14.4 %collective-permute-start = (bf16[272,512]{1,0:T(8,128)(2,1)}, bf16[272,512]{1,0:T(8,128)(2,1)}, u32[]{:S(2)}, u32[]{:S(2)}) collective-permute-start(bf16[272,512]{1,0:T(8,128)(2,1)} %pad_maximum_fusion.2), channel_id=1, source_target_pairs={{256,16},{257,17},{258,18},{259,19},{260,20},{261,21},{262,22},{26... | collective-permute-start | bytes 835592 | tf_op jit(solution)/shard_map/ppermute | solution.py:44
  12.2 0.7 collective-permute-start.8
  12.9 24.7 %copy-start.7 = (bf16[320,256]{1,0:T(8,128)(2,1)}, bf16[320,256]{1,0:T(8,128)(2,1)S(1)}, u32[]{:S(2)}) copy-start(bf16[320,256]{1,0:T(8,128)(2,1)S(1)} %collective-permute-done.8) | copy-start | bytes 491524
  12.9 15.7 %collective-permute-start.9 = (bf16[320,256]{1,0:T(8,128)(2,1)S(1)}, bf16[320,256]{1,0:T(8,128)(2,1)S(1)}, u32[]{:S(2)}, u32[]{:S(2)}) collective-permute-start(bf16[320,256]{1,0:T(8,128)(2,1)S(1)} %collective-permute-done.8), channel_id=1, source_target_pairs={{1,13},{3,15},{5,9},{7,11},{9,5},{11,7},{13,1},{15,3},{16,28},{18,... | collective-permute-start | bytes 491528 | tf_op jit(solution)/shard_map/ppermute | solution.py:44
  26.0 9.7 %collective-permute-start.1 = (bf16[272,512]{1,0:T(8,128)(2,1)S(1)}, bf16[272,512]{1,0:T(8,128)(2,1)S(1)}, u32[]{:S(2)}, u32[]{:S(2)}) collective-permute-start(bf16[272,512]{1,0:T(8,128)(2,1)S(1)} %broadcast_select_fusion.refs_0_), channel_id=1, source_target_pairs={{0,32},{1,33},{2,34},{3,35},{4,36},{5,37},{6,38},{7,39},{8,40},{9,... | collective-permute-start | bytes 835592 | tf_op jit(solution)/shard_map/ppermute | solution.py:44
  28.6 8.9 %collective-permute-start.10 = (bf16[2,320,256]{2,1,0:T(8,128)(2,1)S(1)}, bf16[2,320,256]{2,1,0:T(8,128)(2,1)S(1)}, u32[]{:S(2)}, u32[]{:S(2)}) collective-permute-start(bf16[2,320,256]{2,1,0:T(8,128)(2,1)S(1)} %pad_maximum_fusion.1), channel_id=1, source_target_pairs={{1,5},{3,7},{5,1},{7,3},{9,13},{11,15},{13,9},{15,11},{16,20},{18,... | collective-permute-start | bytes 983048 | tf_op jit(solution)/shard_map/ppermute | solution.py:44
  29.3 13.4 %collective-permute-start.5 = (bf16[272,512]{1,0:T(8,128)(2,1)S(1)}, bf16[272,512]{1,0:T(8,128)(2,1)}, u32[]{:S(2)}, u32[]{:S(2)}) collective-permute-start(bf16[272,512]{1,0:T(8,128)(2,1)S(1)} %broadcast_select_fusion.refs_0_), channel_id=1, source_target_pairs={{0,224},{1,225},{2,226},{3,227},{4,228},{5,229},{6,230},{7,231},{8... | collective-permute-start | bytes 835592 | tf_op jit(solution)/shard_map/ppermute | solution.py:44
  35.6 7.1 %copy-start.4 = (bf16[272,512]{1,0:T(8,128)(2,1)}, bf16[272,512]{1,0:T(8,128)(2,1)S(1)}, u32[]{:S(2)}) copy-start(bf16[272,512]{1,0:T(8,128)(2,1)S(1)} %collective-permute-done.1.refs_1_) | copy-start | bytes 835588
  35.6 12.2 %collective-permute-start.2 = (bf16[272,512]{1,0:T(8,128)(2,1)S(1)}, bf16[272,512]{1,0:T(8,128)(2,1)}, u32[]{:S(2)}, u32[]{:S(2)}) collective-permute-start(bf16[272,512]{1,0:T(8,128)(2,1)S(1)} %collective-permute-done.1.refs_1_), channel_id=1, source_target_pairs={{0,32},{1,33},{2,34},{3,35},{4,36},{5,37},{6,38},{7,39},{8,40},{9,... | collective-permute-start | bytes 835592 | tf_op jit(solution)/shard_map/ppermute | solution.py:44
  38.6 29.2 %collective-permute-start.13 = (bf16[4,320,256]{2,1,0:T(8,128)(2,1)S(1)}, bf16[4,320,256]{2,1,0:T(8,128)(2,1)}, u32[]{:S(2)}, u32[]{:S(2)}) collective-permute-start(bf16[4,320,256]{2,1,0:T(8,128)(2,1)S(1)} %pad_maximum_fusion.refs_8_), channel_id=1, source_target_pairs={{1,0},{3,2},{5,4},{7,6},{9,8},{11,10},{13,12},{15,14},{16,19},{18,... | collective-permute-start | bytes 1966088 | tf_op jit(solution)/shard_map/ppermute | solution.py:44
  39.9 37.9 %collective-permute-start.12 = (bf16[4,320,256]{2,1,0:T(8,128)(2,1)S(1)}, bf16[4,320,256]{2,1,0:T(8,128)(2,1)}, u32[]{:S(2)}, u32[]{:S(2)}) collective-permute-start(bf16[4,320,256]{2,1,0:T(8,128)(2,1)S(1)} %pad_maximum_fusion.refs_8_), channel_id=1, source_target_pairs={{1,2},{3,0},{5,6},{7,4},{9,10},{11,8},{13,14},{15,12},{16,17},{18,... | collective-permute-start | bytes 1966088 | tf_op jit(solution)/shard_map/ppermute | solution.py:44
  41.2 36.6 %collective-permute-start.11 = (bf16[4,320,256]{2,1,0:T(8,128)(2,1)S(1)}, bf16[4,320,256]{2,1,0:T(8,128)(2,1)}, u32[]{:S(2)}, u32[]{:S(2)}) collective-permute-start(bf16[4,320,256]{2,1,0:T(8,128)(2,1)S(1)} %pad_maximum_fusion.refs_8_), channel_id=1, source_target_pairs={{1,3},{3,1},{5,7},{7,5},{9,11},{11,9},{13,15},{15,13},{16,18},{18,... | collective-permute-start | bytes 1966088 | tf_op jit(solution)/shard_map/ppermute | solution.py:44
  42.7 9.5 %collective-permute-start.6 = (bf16[272,512]{1,0:T(8,128)(2,1)}, bf16[272,512]{1,0:T(8,128)(2,1)}, u32[]{:S(2)}, u32[]{:S(2)}) collective-permute-start(bf16[272,512]{1,0:T(8,128)(2,1)} %collective-permute-done.5.refs_5_), channel_id=1, source_target_pairs={{0,224},{1,225},{2,226},{3,227},{4,228},{5,229},{6,230},{7,231},{8... | collective-permute-start | bytes 835592 | tf_op jit(solution)/shard_map/ppermute | solution.py:44
  47.8 10.0 %collective-permute-start.3 = (bf16[272,512]{1,0:T(8,128)(2,1)}, bf16[272,512]{1,0:T(8,128)(2,1)}, u32[]{:S(2)}, u32[]{:S(2)}) collective-permute-start(bf16[272,512]{1,0:T(8,128)(2,1)} %collective-permute-done.2.refs_2_), channel_id=1, source_target_pairs={{0,32},{1,33},{2,34},{3,35},{4,36},{5,37},{6,38},{7,39},{8,40},{9,... | collective-permute-start | bytes 835592 | tf_op jit(solution)/shard_map/ppermute | solution.py:44
  52.2 10.0 %collective-permute-start.7 = (bf16[272,512]{1,0:T(8,128)(2,1)}, bf16[272,512]{1,0:T(8,128)(2,1)S(1)}, u32[]{:S(2)}, u32[]{:S(2)}) collective-permute-start(bf16[272,512]{1,0:T(8,128)(2,1)} %collective-permute-done.6.refs_6_), channel_id=1, source_target_pairs={{0,224},{1,225},{2,226},{3,227},{4,228},{5,229},{6,230},{7,231},{8... | collective-permute-start | bytes 835592 | tf_op jit(solution)/shard_map/ppermute | solution.py:44
  57.8 19.9 %collective-permute-start.4 = (bf16[272,512]{1,0:T(8,128)(2,1)}, bf16[272,512]{1,0:T(8,128)(2,1)S(1)}, u32[]{:S(2)}, u32[]{:S(2)}) collective-permute-start(bf16[272,512]{1,0:T(8,128)(2,1)} %collective-permute-done.3.refs_3_), channel_id=1, source_target_pairs={{0,32},{1,33},{2,34},{3,35},{4,36},{5,37},{6,38},{7,39},{8,40},{9,... | collective-permute-start | bytes 835592 | tf_op jit(solution)/shard_map/ppermute | solution.py:44
  60.5 29.3 %copy-start.1 = (f32[1,512,320]{1,2,0:T(8,128)S(1)}, f32[1,512,320]{1,2,0:T(8,128)}, u32[]{:S(2)}) copy-start(f32[1,512,320]{1,2,0:T(8,128)} %param.16) | copy-start | bytes 1966084
  60.5 30.6 %copy-start.2 = (f32[1,512,320]{1,2,0:T(8,128)S(1)}, f32[1,512,320]{1,2,0:T(8,128)}, u32[]{:S(2)}) copy-start(f32[1,512,320]{1,2,0:T(8,128)} %param.17) | copy-start | bytes 1966084
  60.5 34.7 %copy-start.3 = (bf16[512,320]{0,1:T(8,128)(2,1)S(1)}, bf16[512,320]{0,1:T(8,128)(2,1)}, u32[]{:S(2)}) copy-start(bf16[512,320]{0,1:T(8,128)(2,1)} %param.15) | copy-start | bytes 983044
  77.7 1.0 copy-start.5
  81.4 13.7 %collective-permute-start.14 = (f32[384,512]{1,0:T(8,128)S(1)}, f32[384,512]{1,0:T(8,128)S(1)}, u32[]{:S(2)}, u32[]{:S(2)}) collective-permute-start(f32[384,512]{1,0:T(8,128)S(1)} %gradient.1.mine_ref), channel_id=1, source_target_pairs={{0,256},{1,257},{2,258},{3,259},{4,260},{5,261},{6,262},{7,263},{8... | collective-permute-start | bytes 2359304 | tf_op jit(solution)/shard_map/ppermute | solution.py:44
  89.8 4.0 %collective-permute-start.15 = (f32[320,512]{1,0:T(8,128)S(1)}, f32[320,512]{1,0:T(8,128)S(1)}, u32[]{:S(2)}, u32[]{:S(2)}) collective-permute-start(f32[320,512]{1,0:T(8,128)S(1)} %bitcast.18), channel_id=1, source_target_pairs={{256,0},{257,1},{258,2},{259,3},{260,4},{261,5},{262,6},{263,7},{2... | collective-permute-start | bytes 1966088 | tf_op jit(solution)/shard_map/ppermute | solution.py:44
  91.1 4.0 %collective-permute-start.16 = (f32[320,512]{1,0:T(8,128)S(1)}, f32[320,512]{1,0:T(8,128)S(1)}, u32[]{:S(2)}, u32[]{:S(2)}) collective-permute-start(f32[320,512]{1,0:T(8,128)S(1)} %bitcast.20), channel_id=1, source_target_pairs={{256,0},{257,1},{258,2},{259,3},{260,4},{261,5},{262,6},{263,7},{2... | collective-permute-start | bytes 1966088 | tf_op jit(solution)/shard_map/ppermute | solution.py:44
  120.0 11.2 %collective-permute-start.17 = (bf16[8,320]{1,0:T(8,128)(2,1)S(1)}, bf16[8,320]{1,0:T(8,128)(2,1)S(1)}, u32[]{:S(2)}, u32[]{:S(2)}) collective-permute-start(bf16[8,320]{1,0:T(8,128)(2,1)S(1)} %reduce_sum.9), channel_id=1, source_target_pairs={{0,0},{1,16},{2,32},{3,48},{4,64},{5,80},{6,96},{7,112},{8,128},{9... | collective-permute-start | bytes 15368 | tf_op jit(solution)/shard_map/ppermute | solution.py:44

commit v2 on v1

v2 whole, which is shorter than its diff:
```python
import math

import jax
import jax.numpy as jnp
import numpy as np
from jax import lax
from jax.experimental import pallas as pl
from jax.experimental.pallas import tpu as pltpu
from jax.sharding import PartitionSpec as P

D = 5120
KVH = 8
HD = 128
EOS = 151645
STEPS = 4
CACHE = 256

learning_rate = 0.0003
weight_decay = 0.1
beta_one = 0.9
beta_two = 0.95
first_bias = 1.0 - 0.9**10
second_bias = 1.0 - 0.95**10
epsilon = 1e-08

AXES = ("group", "dp", "tensor")
SHAPE = (2, 8, 2, 4, 4)
TOK = 256
FEAT = 512
COLS = 320
ROWS = 8
PAD = 16
f32, bf16 = jnp.float32, jnp.bfloat16


def permute(value, target):
    pairs = []
    for flat, place in enumerate(np.ndindex(*SHAPE)):
        to = target(*place)
        if to is not None:
            pairs.append((flat, int(np.ravel_multi_index(to, SHAPE))))
    return lax.ppermute(value, AXES, pairs)


def on_learner(y, zh, block_y, block_zh):
    return (y - block_y - (zh != block_zh)) % 8 < 4


def keeper(y, zh, zl, x):
    return int(on_learner(y, zh, 2 * zl + (x >> 1), x & 1))


def along_y(step, core, to=None):
    def target(g, y, zh, zl, x):
        return (core if to is None else to, (y + step) % 8, zh, zl, x) if g == core else None

    return target


def along_z(step, core, to):
    def target(g, y, zh, zl, x):
        z = (zh * 4 + zl + step) % 8
        return (to, y, z // 4, z % 4, x) if g == core else None

    return target


def transposed(g, y, zh, zl, x):
    return (g, zl * 2 + (x >> 1), x & 1, y >> 1, (y & 1) * 2 + zh)


def cot_transposed(g, *place):
    to = transposed(g, *place)[1:]
    return (keeper(*to), *to) if g == 1 else None


def along_zl(flip):
    def target(g, y, zh, zl, x):
        return (g, y, zh, zl ^ flip, x) if g == keeper(y, zh, zl, x) else None

    return target


def along_x(step):
    return lambda g, y, zh, zl, x: (g, y, zh, zl, (x + step) % 4)


def other_core(g, y, zh, zl, x):
    return (1 - g, y, zh, zl, x)


def to_rollout(g, y, zh, zl, x):
    return (0, y, zh, zl, x) if g == 1 else None


CHUNKS = (
    ((0, -1), (0, -2), (0, -3), (0, -4), (1, 0), (1, -1), (1, -2), (1, -3)),
    ((0, 0), (0, 1), (0, 2), (0, 3), (1, 1), (1, 2), (1, 3), (1, 4)),
)


def device_table():
    table = np.zeros((512, 32), np.int32)
    for flat, (g, y, zh, zl, x) in enumerate(np.ndindex(*SHAPE)):
        kept = [[z for z in range(4) if keeper(y, zh, z, c) == g] for c in range(4)]
        table[flat, 0] = g
        table[flat, 1:3] = [z ^ zl for z in kept[x]]
        for n, (other, hop) in enumerate(CHUNKS[g]):
            block_y, block_zh = (y - hop) % 8, zh ^ other
            block_x = 2 * (block_y & 1) + block_zh
            table[flat, 8 + n] = block_y * 2 + block_zh
            table[flat, 16 + n] = (block_x - x) % 4
            table[flat, 24 + n] = kept[block_x].index(block_y >> 1)
    return table


def attend_kernel(
    head_ref, lengths_ref, ids_ref, act_ref, q_ref, k_ref, v_ref, nk_ref, nv_ref, out_ref, q_rows, nk_rows, nv_rows
):
    out_ref[:TOK, :] = act_ref[...]
    for t in range(STEPS):
        place = slice(2 * t, 2 * t + 2)
        q_rows[place, :] = q_ref[t].astype(f32)
        nk_rows[place, :] = nk_ref[t].astype(f32)
        nv_rows[place, :] = nv_ref[t].astype(f32)
    queries = q_rows[...]
    query = jnp.concatenate(
        [queries[:, h * HD : (h + 1) * HD] for h in range(4)], axis=0
    ).astype(bf16)
    keys = k_ref[...].reshape(2 * CACHE, HD)
    values = v_ref[...].reshape(2 * CACHE, HD)
    fresh_keys = nk_rows[...].astype(bf16)
    fresh_values = nv_rows[...].astype(bf16)
    scale = 1.0 / math.sqrt(HD)
    nt = (((1,), (1,)), ((), ()))
    cache_scores = lax.dot_general(query, keys, nt, preferred_element_type=f32) * scale
    step_scores = lax.dot_general(query, fresh_keys, nt, preferred_element_type=f32) * scale
    count = 4 * ROWS

    def place(width):
        place_row = lax.broadcasted_iota(jnp.int32, (count, width), 0) & (ROWS - 1)
        place_key = lax.broadcasted_iota(jnp.int32, (count, width), 1)
        return place_row >> 1, place_row & 1, place_key

    step, row, key = place(2 * CACHE)
    length = jnp.where(row == 0, lengths_ref[0], lengths_ref[1])
    cache_valid = ((key >> 8) == row) & ((key & (CACHE - 1)) < length)
    step, row, key = place(ROWS)
    step_valid = ((key & 1) == row) & ((key >> 1) <= step)
    cache_scores = jnp.where(cache_valid, cache_scores, -jnp.inf)
    step_scores = jnp.where(step_valid, step_scores, -jnp.inf)
    peak = jnp.maximum(
        jnp.max(cache_scores, axis=-1, keepdims=True), jnp.max(step_scores, axis=-1, keepdims=True)
    )
    cache_exp = jnp.exp(cache_scores - peak)
    step_exp = jnp.exp(step_scores - peak)
    denominator = jnp.sum(cache_exp, axis=-1, keepdims=True) + jnp.sum(
        step_exp, axis=-1, keepdims=True
    )
    cache_probs = (cache_exp / denominator).astype(bf16)
    step_probs = (step_exp / denominator).astype(bf16)
    nn = (((1,), (0,)), ((), ()))
    mixed = lax.dot_general(cache_probs, values, nn, preferred_element_type=f32)
    mixed = mixed + lax.dot_general(step_probs, fresh_values, nn, preferred_element_type=f32)
    step, row, _ = place(HD)
    dead = jnp.zeros((count, HD), jnp.int32)
    for u in range(STEPS - 1):
        for r in range(2):
            ended = (ids_ref[r, u] == EOS).astype(jnp.int32)
            dead = dead + jnp.where((row == r) & (step > u), ended, 0)
    mixed = jnp.where(dead == 0, mixed, 0.0)
    flat = jnp.concatenate([mixed[h * ROWS : (h + 1) * ROWS] for h in range(4)], axis=1)
    out_ref[TOK:, :] = jnp.concatenate([flat, jnp.zeros_like(flat)], axis=0).astype(bf16)


def attend(head, act, queries, cache_keys, cache_values, new_keys, new_values, lengths, ids):
    whole = lambda *shape: pl.BlockSpec(shape, lambda i, *_: (0,) * len(shape))
    cache = pl.BlockSpec((2, CACHE, HD), lambda i, m, *_: (0, m[0], 0))
    fresh = pl.BlockSpec((STEPS, 2, HD), lambda i, m, *_: (0, 0, m[0]))
    return pl.pallas_call(
        attend_kernel,
        out_shape=jax.ShapeDtypeStruct((TOK + PAD, FEAT), bf16),
        grid_spec=pltpu.PrefetchScalarGridSpec(
            num_scalar_prefetch=3,
            grid=(1,),
            in_specs=[whole(TOK, FEAT), whole(STEPS, 2, FEAT), cache, cache, fresh, fresh],
            out_specs=whole(TOK + PAD, FEAT),
            scratch_shapes=[
                pltpu.VMEM((ROWS, FEAT), f32),
                pltpu.VMEM((ROWS, HD), f32),
                pltpu.VMEM((ROWS, HD), f32),
            ],
        ),
        name="attend",
    )(head, lengths, ids, act, queries, cache_keys, cache_values, new_keys, new_values)


def gradient_kernel(table_ref, *refs):
    chunks, pairs, out_ref = (refs[:8], refs[8:16]), refs[16:20], refs[-4]
    chunk_rows, pair_rows, sems = refs[-3:]

    def accumulate(mine):
        copies = [
            pltpu.make_async_copy(ref, chunk_rows.at[n], sems.at[n]) for n, ref in enumerate(mine)
        ] + [
            pltpu.make_async_copy(ref, pair_rows.at[n], sems.at[8 + n])
            for n, ref in enumerate(pairs)
        ]
        for copy in copies:
            copy.start()
        out_ref[COLS:, :] = jnp.zeros((16 * ROWS, FEAT), f32)
        for copy in copies[8:]:
            copy.wait()
        for n in range(8):
            copies[n].wait()
            block = pair_rows[table_ref[16 + n], table_ref[24 + n]]
            part = jnp.dot(block, chunk_rows[n, :TOK, :], preferred_element_type=f32)
            if n == 0:
                out_ref[:COLS, :] = part
            else:
                out_ref[:COLS, :] += part
            place = pl.multiple_of(COLS + table_ref[8 + n] * ROWS, ROWS)
            out_ref[pl.ds(place, ROWS), :] = chunk_rows[n, TOK:, :].astype(f32)[:ROWS]

    for side in range(2):

        @pl.when(table_ref[0] == side)
        def _():
            accumulate(chunks[side])


def gradient(table, rollout_chunks, learner_chunks, pairs, others):
    hbm = pl.BlockSpec(memory_space=pl.ANY)
    operands = (*rollout_chunks, *learner_chunks, *pairs, *others)
    return pl.pallas_call(
        gradient_kernel,
        out_shape=jax.ShapeDtypeStruct((COLS + 16 * ROWS, FEAT), f32),
        in_specs=[pl.BlockSpec(memory_space=pltpu.SMEM)] + [hbm] * len(operands),
        out_specs=pl.BlockSpec(memory_space=pltpu.VMEM),
        scratch_shapes=[
            pltpu.VMEM((8, TOK + PAD, FEAT), bf16),
            pltpu.VMEM((4, 2, COLS, TOK), bf16),
            pltpu.SemaphoreType.DMA((12,)),
        ],
        compiler_params=pltpu.CompilerParams(vmem_limit_bytes=32 * 2**20),
        cost_estimate=pl.CostEstimate(
            flops=2 * 8 * TOK * COLS * FEAT, bytes_accessed=6 * 2**20, transcendentals=0
        ),
        name="gradient",
    )(table, *operands)


def step_kernel(
    table_ref, mine_ref, got_ref, one_ref, one_got, two_ref, two_got, weight_ref, update_ref, out_ref
):
    learner = table_ref[0] == 1
    grad = mine_ref[:COLS, :] + got_ref[:COLS, :]
    moment_one = jnp.where(learner, one_ref[...], one_got[...])
    moment_two = jnp.where(learner, two_ref[...], two_got[...])
    first_moment = beta_one * moment_one + (1.0 - beta_one) * grad
    second_moment = beta_two * moment_two + (1.0 - beta_two) * grad * grad
    update = (
        first_moment / first_bias / (jnp.sqrt(second_moment / second_bias) + epsilon)
    ).astype(bf16)
    update_ref[...] = update
    widened = weight_ref[...].astype(f32)
    renewed = (
        widened - learning_rate * (update.astype(f32) + weight_decay * widened)
    ).astype(bf16)
    rows = (mine_ref[COLS:, :] + got_ref[COLS:, :]).astype(bf16)
    part = lax.dot_general(rows, renewed, (((1,), (1,)), ((), ())), preferred_element_type=f32)
    out_ref[...] = part.reshape(16, ROWS, COLS)


def step(table, mine, got, one, one_got, two, two_got, weight):
    vmem = pl.BlockSpec(memory_space=pltpu.VMEM)
    return pl.pallas_call(
        step_kernel,
        out_shape=(
            jax.ShapeDtypeStruct((COLS, FEAT), bf16),
            jax.ShapeDtypeStruct((16, ROWS, COLS), f32),
        ),
        in_specs=[pl.BlockSpec(memory_space=pltpu.SMEM)] + [vmem] * 7,
        out_specs=(vmem, vmem),
        compiler_params=pltpu.CompilerParams(vmem_limit_bytes=32 * 2**20),
        name="step",
    )(table, mine, got, one, one_got, two, two_got, weight)


def local(
    activations,
    cotangent,
    weight,
    moment_one,
    moment_two,
    queries,
    cache_keys,
    cache_values,
    new_keys,
    new_values,
    lengths,
    token_ids,
):
    g = lax.axis_index("group")
    p = lax.axis_index("dp")
    q = lax.axis_index("tensor")
    flat = (g * 16 + p) * 16 + q
    table = lax.dynamic_slice_in_dim(jnp.asarray(device_table()), flat, 1, 0)[0]

    payload = attend(
        (q >> 1).reshape(1),
        activations[0],
        queries,
        cache_keys,
        cache_values,
        new_keys,
        new_values,
        lengths,
        token_ids.T,
    )
    relay = permute(payload, along_z(2, 1, 0))
    up = [payload, permute(payload, along_y(1, 1))]
    down = [permute(payload, along_y(-1, 1, 0))]

    cut = lax.dynamic_slice_in_dim(cotangent[0], q * COLS, COLS, 1).T
    own = permute(cut, cot_transposed)

    other = permute(relay, along_z(2, 0, 0))
    for _ in range(2):
        up.append(permute(up[-1], along_y(1, 1)))
    for _ in range(3):
        down.append(permute(down[-1], along_y(-1, 0)))

    parts = [own] + [permute(own, along_zl(flip)) for flip in (1, 2, 3)]
    pair = jnp.stack(
        [
            jnp.where(
                table[s] == 0,
                parts[0],
                jnp.where(table[s] == 1, parts[1], jnp.where(table[s] == 2, parts[2], parts[3])),
            )
            for s in (1, 2)
        ]
    )
    pairs = (
        pair,
        permute(pair, along_x(-1)),
        permute(pair, along_x(2)),
        permute(pair, along_x(1)),
    )

    other_up = [permute(other, along_y(1, 0, 1))]
    other_down = [other, permute(other, along_y(-1, 0))]
    for _ in range(3):
        other_up.append(permute(other_up[-1], along_y(1, 1)))
    for _ in range(2):
        other_down.append(permute(other_down[-1], along_y(-1, 0)))

    one, two = moment_one[0].T, moment_two[0].T
    one_got = permute(one, to_rollout)
    two_got = permute(two, to_rollout)

    mine = gradient(table, down + other_down, up + other_up, pairs, (one_got, two_got))
    got = permute(mine, other_core)
    update, partial = step(table, mine, got, one, one_got, two, two_got, weight.T)

    shares = lax.all_to_all(partial, "tensor", split_axis=0, concat_axis=0, tiled=True)
    summed = jnp.sum(shares, axis=0).astype(bf16)
    block = permute(summed, transposed)
    spread = jnp.broadcast_to(block[None], (16, ROWS, COLS))
    gathered = lax.all_to_all(spread, "tensor", split_axis=0, concat_axis=0, tiled=True)
    decoded = gathered.transpose(1, 0, 2).reshape(STEPS, ROWS // STEPS, D)
    return (update.T, decoded)


def solution(mesh):
    return jax.shard_map(
        local,
        mesh=mesh,
        in_specs=(
            P("group", "dp", "tensor"),
            P("group", "dp", None),
            P("tensor", "dp"),
            P("group", "tensor", "dp"),
            P("group", "tensor", "dp"),
            P(None, "dp", "tensor"),
            P("dp", None, None),
            P("dp", None, None),
            P(None, "dp", None),
            P(None, "dp", None),
            P("dp"),
            P(None, "dp"),
        ),
        out_specs=(P("tensor", "dp"), P(None, "dp", None)),
        check_vma=False,
    )
```

time: 147 us -> 153 us (1.041)
  the two profiles are of different devices: /device:TPU:32 before, /device:TPU:56 now
where the time goes in v2:
time: 153 us; the launch traced here: 150 us
  starting transfers between devices  64.8 us (42%)
  waiting for transfers between devices  38.4 us (25%)
  blocking collectives  27.9 us (18%)
  Pallas kernels  8.76 us (6%)
  between operations  4.66 us (3%)
  local copies, waits for them, and re-layouts  4.65 us (3%)
    ppermute x27, starting transfers between devices, permute(): return lax.ppermute(value, AXES, pairs)  64.8 us
    ppermute x27, waiting for transfers between devices, permute(): return lax.ppermute(value, AXES, pairs)  38.4 us
    all_to_all x1, blocking collectives, local(): lax.all_to_all(partial, 'tensor', split_axis=0, concat_axis=0, tiled=True)  15.8 us
    all_to_all x1, blocking collectives, local(): lax.all_to_all(spread, 'tensor', split_axis=0, concat_axis=0, tiled=True)  12.1 us
    pallas_call x1, Pallas kernels, gradient(): pl.pallas_call(gradient_kernel, out_shape=jax.ShapeDtypeStruct((COLS + 16...  3.6 us
    pallas_call x1, Pallas kernels, attend(): pl.pallas_call(attend_kernel, out_shape=jax.ShapeDtypeStruct((TOK + PAD,...  3.22 us
  transfers between devices with their start and end apart: 27, of which 8 were waited for; matrix products, arithmetic and copies ran while one was open for 3% of the time, Pallas kernels for 0%

profile of v2, /device:TPU:56, one launch (start us, length us, event | category | flops | bytes accessed | tf_op | source)
XLA Modules:
  0.0 150.2 jit_solution(13654328763613036358)
XLA Ops:
  0.6 0.0 copy-start
  0.7 3.2 %attend.1.refs_8_ = bf16[272,512]{1,0:T(8,128)(2,1)} custom-call(s32[1]{0:T(128)} %bitcast.1.head_ref, s32[2]{0:T(128)} %lengths_ref.1, s32[2,4]{1,0:T(2,128)} %bitcast.35, bf16[256,512]{1,0:T(8,128)(2,1)} %bitcast.33, bf16[4,2,512]{2,1,0:T(2,128)(2,1)} %q_ref.1, bf16[2,2048,128]{2,1,0:T(8,128)(2,1)} %k_ref.1, bf16[2,2048,128]{2,1,0:T(8,128)(2,1)} %v_ref.1, ...), custom_call_target="tpu_custom_call" | custom-call | tf_op jit(solution)/shard_map/attend/pallas_call | solution.py:180
  3.9 1.5 collective-permute-start.9
  5.4 0.8 constant_dynamic-slice_fusion
  6.2 1.7 %copy.17 = bf16[1,256,320]{1,2,0:T(8,128)(2,1)} copy(bf16[1,256,320]{2,1,0:T(8,128)(2,1)} %constant_dynamic-slice_fusion) | data formatting | bytes 327680 | tf_op jit(solution)/shard_map/dynamic_slice | solution.py:325
  7.9 1.3 collective-permute-start.16
  9.2 1.3 collective-permute-start.4
  10.5 1.3 collective-permute-start
  11.8 19.1 %collective-permute-done.16 = bf16[320,256]{1,0:T(8,128)(2,1)} collective-permute-done((bf16[320,256]{1,0:T(8,128)(2,1)}, bf16[320,256]{1,0:T(8,128)(2,1)}, u32[]{:S(2)}, u32[]{:S(2)}) %collective-permute-start.16) | collective-permute-done | bytes 163872 | tf_op jit(solution)/shard_map/ppermute | solution.py:42
  30.9 1.3 collective-permute-start.19
  32.2 1.3 collective-permute-start.18
  33.5 0.0 collective-permute-done.9.refs_9_
  33.5 1.9 %collective-permute-start.17 = (bf16[320,256]{1,0:T(8,128)(2,1)}, bf16[320,256]{1,0:T(8,128)(2,1)S(1)}, u32[]{:S(2)}, u32[]{:S(2)}) collective-permute-start(bf16[320,256]{1,0:T(8,128)(2,1)} %collective-permute-done.16), channel_id=1, source_target_pairs={{1,5},{2,6},{3,7},{4,0},{5,1},{6,2},{7,3},{8,12},{16,20},{18,22},{... | collective-permute-start | bytes 491528 | tf_op jit(solution)/shard_map/ppermute | solution.py:42
  35.5 0.7 constant_dynamic-slice_fusion.1
  36.2 0.6 fusion.1
  40.3 0.0 collective-permute-done.4
  40.3 0.7 collective-permute-start.10
  41.0 0.0 collective-permute-done.refs_0_
  41.0 1.9 %collective-permute-start.5 = (bf16[272,512]{1,0:T(8,128)(2,1)}, bf16[272,512]{1,0:T(8,128)(2,1)S(1)}, u32[]{:S(2)}, u32[]{:S(2)}) collective-permute-start(bf16[272,512]{1,0:T(8,128)(2,1)} %collective-permute-done.4), channel_id=1, source_target_pairs={{0,8},{1,9},{2,10},{3,11},{4,12},{5,13},{6,14},{7,15},{8,16},{9,17... | collective-permute-start | bytes 835592 | tf_op jit(solution)/shard_map/ppermute | solution.py:42
  43.0 0.0 collective-permute-done.19
  43.0 1.9 %collective-permute-start.1 = (bf16[272,512]{1,0:T(8,128)(2,1)}, bf16[272,512]{1,0:T(8,128)(2,1)S(1)}, u32[]{:S(2)}, u32[]{:S(2)}) collective-permute-start(bf16[272,512]{1,0:T(8,128)(2,1)} %collective-permute-done.refs_0_), channel_id=1, source_target_pairs={{0,224},{1,225},{2,226},{3,227},{4,228},{5,229},{6,230},{7,231},{8... | collective-permute-start | bytes 835592 | tf_op jit(solution)/shard_map/ppermute | solution.py:42
  44.9 0.0 collective-permute-done.18
  44.9 0.0 collective-permute-done.17
  44.9 1.0 select_bitcast_fusion.1
  45.9 7.4 %collective-permute-start.22 = (bf16[2,320,256]{2,1,0:T(8,128)(2,1)S(1)}, bf16[2,320,256]{2,1,0:T(8,128)(2,1)S(1)}, u32[]{:S(2)}, u32[]{:S(2)}) collective-permute-start(bf16[2,320,256]{2,1,0:T(8,128)(2,1)S(1)} %pad_maximum_fusion.refs_16_), channel_id=1, source_target_pairs={{0,1},{1,2},{2,3},{3,0},{4,5},{5,6},{6,7},{7,4},{8,9},{9,10},{10,1... | collective-permute-start | bytes 983048 | tf_op jit(solution)/shard_map/ppermute | solution.py:42
  53.4 0.0 collective-permute-done.5.refs_4_
  53.4 1.3 collective-permute-start.12
  54.7 2.8 %collective-permute-start.21 = (bf16[2,320,256]{2,1,0:T(8,128)(2,1)S(1)}, bf16[2,320,256]{2,1,0:T(8,128)(2,1)S(1)}, u32[]{:S(2)}, u32[]{:S(2)}) collective-permute-start(bf16[2,320,256]{2,1,0:T(8,128)(2,1)S(1)} %pad_maximum_fusion.refs_16_), channel_id=1, source_target_pairs={{0,2},{1,3},{2,0},{3,1},{4,6},{5,7},{6,4},{7,5},{8,10},{9,11},{10,... | collective-permute-start | bytes 983048 | tf_op jit(solution)/shard_map/ppermute | solution.py:42
  57.5 0.0 collective-permute-done.10.refs_10_
  57.5 1.3 collective-permute-start.23
  58.8 0.0 collective-permute-done.1.refs_1_
  58.8 10.6 %collective-permute-start.20 = (bf16[2,320,256]{2,1,0:T(8,128)(2,1)S(1)}, bf16[2,320,256]{2,1,0:T(8,128)(2,1)S(1)}, u32[]{:S(2)}, u32[]{:S(2)}) collective-permute-start(bf16[2,320,256]{2,1,0:T(8,128)(2,1)S(1)} %pad_maximum_fusion.refs_16_), channel_id=1, source_target_pairs={{0,3},{1,0},{2,1},{3,2},{4,7},{5,4},{6,5},{7,6},{8,11},{9,8},{10,9... | collective-permute-start | bytes 983048 | tf_op jit(solution)/shard_map/ppermute | solution.py:42
  69.5 1.9 %collective-permute-start.6 = (bf16[272,512]{1,0:T(8,128)(2,1)S(1)}, bf16[272,512]{1,0:T(8,128)(2,1)S(1)}, u32[]{:S(2)}, u32[]{:S(2)}) collective-permute-start(bf16[272,512]{1,0:T(8,128)(2,1)S(1)} %collective-permute-done.5.refs_4_), channel_id=1, source_target_pairs={{0,224},{1,225},{2,226},{3,227},{4,228},{5,229},{6,230},{7,231},{8... | collective-permute-start | bytes 835592 | tf_op jit(solution)/shard_map/ppermute | solution.py:42
  71.4 0.0 collective-permute-done.12.refs_12_
  71.5 0.7 collective-permute-start.13
  72.1 0.0 collective-permute-done.21.refs_18_
  72.1 1.3 collective-permute-start.24
  73.4 3.9 %collective-permute-done.20.refs_17_ = bf16[2,320,256]{2,1,0:T(8,128)(2,1)S(1)} collective-permute-done((bf16[2,320,256]{2,1,0:T(8,128)(2,1)S(1)}, bf16[2,320,256]{2,1,0:T(8,128)(2,1)S(1)}, u32[]{:S(2)}, u32[]{:S(2)}) %collective-permute-start.20) | collective-permute-done | bytes 327712 | tf_op jit(solution)/shard_map/ppermute | solution.py:42
  77.4 1.9 %collective-permute-start.2 = (bf16[272,512]{1,0:T(8,128)(2,1)S(1)}, bf16[272,512]{1,0:T(8,128)(2,1)S(1)}, u32[]{:S(2)}, u32[]{:S(2)}) collective-permute-start(bf16[272,512]{1,0:T(8,128)(2,1)S(1)} %collective-permute-done.1.refs_1_), channel_id=1, source_target_pairs={{0,224},{1,225},{2,226},{3,227},{4,228},{5,229},{6,230},{7,231},{8... | collective-permute-start | bytes 835592 | tf_op jit(solution)/shard_map/ppermute | solution.py:42
  79.3 0.0 collective-permute-done.6.refs_5_
  79.3 6.2 %collective-permute-start.7 = (bf16[272,512]{1,0:T(8,128)(2,1)S(1)}, bf16[272,512]{1,0:T(8,128)(2,1)S(1)}, u32[]{:S(2)}, u32[]{:S(2)}) collective-permute-start(bf16[272,512]{1,0:T(8,128)(2,1)S(1)} %collective-permute-done.6.refs_5_), channel_id=1, source_target_pairs={{0,224},{1,225},{2,226},{3,227},{4,228},{5,229},{6,230},{7,231},{8... | collective-permute-start | bytes 835592 | tf_op jit(solution)/shard_map/ppermute | solution.py:42
  85.6 0.7 collective-permute-start.14
  86.2 0.0 collective-permute-done.23.refs_20_.one_got
  86.3 0.7 collective-permute-start.11
  86.9 0.1 collective-permute-done.2.refs_2_
  87.0 2.5 %collective-permute-start.3 = (bf16[272,512]{1,0:T(8,128)(2,1)S(1)}, bf16[272,512]{1,0:T(8,128)(2,1)S(1)}, u32[]{:S(2)}, u32[]{:S(2)}) collective-permute-start(bf16[272,512]{1,0:T(8,128)(2,1)S(1)} %collective-permute-done.2.refs_2_), channel_id=1, source_target_pairs={{0,224},{1,225},{2,226},{3,227},{4,228},{5,229},{6,230},{7,231},{8... | collective-permute-start | bytes 835592 | tf_op jit(solution)/shard_map/ppermute | solution.py:42
  89.6 0.4 collective-permute-done.7.refs_6_
  90.0 4.0 %collective-permute-start.8 = (bf16[272,512]{1,0:T(8,128)(2,1)S(1)}, bf16[272,512]{1,0:T(8,128)(2,1)S(1)}, u32[]{:S(2)}, u32[]{:S(2)}) collective-permute-start(bf16[272,512]{1,0:T(8,128)(2,1)S(1)} %collective-permute-done.7.refs_6_), channel_id=1, source_target_pairs={{0,224},{1,225},{2,226},{3,227},{4,228},{5,229},{6,230},{7,231},{8... | collective-permute-start | bytes 835592 | tf_op jit(solution)/shard_map/ppermute | solution.py:42
  94.0 0.0 collective-permute-done.14.refs_14_
  94.0 0.7 collective-permute-start.15
  94.7 0.0 collective-permute-done.24.refs_21_.two_got
  94.7 2.0 %collective-permute-done.3.refs_3_ = bf16[272,512]{1,0:T(8,128)(2,1)S(1)} collective-permute-done((bf16[272,512]{1,0:T(8,128)(2,1)S(1)}, bf16[272,512]{1,0:T(8,128)(2,1)S(1)}, u32[]{:S(2)}, u32[]{:S(2)}) %collective-permute-start.3) | collective-permute-done | bytes 278560 | tf_op jit(solution)/shard_map/ppermute | solution.py:42
  96.7 3.0 %collective-permute-done.8.refs_7_ = bf16[272,512]{1,0:T(8,128)(2,1)S(1)} collective-permute-done((bf16[272,512]{1,0:T(8,128)(2,1)S(1)}, bf16[272,512]{1,0:T(8,128)(2,1)S(1)}, u32[]{:S(2)}, u32[]{:S(2)}) %collective-permute-start.8) | collective-permute-done | bytes 278560 | tf_op jit(solution)/shard_map/ppermute | solution.py:42
  99.7 0.0 collective-permute-done.15.refs_15_
  99.7 0.0 copy-start.4
  99.7 3.6 %gradient.1.mine_ref = f32[448,512]{1,0:T(8,128)S(1)} custom-call(s32[32]{0:T(128)S(1)} %get-tuple-element.9.table_ref, bf16[272,512]{1,0:T(8,128)(2,1)} %collective-permute-done.refs_0_, bf16[272,512]{1,0:T(8,128)(2,1)S(1)} %collective-permute-done.1.refs_1_, bf16[272,512]{1,0:T(8,128)(2,1)S(1)} %collective-permute-done.2.refs_2_, ...), custom_call_target="tpu_custom_call" | custom-call | flops 671088640 | bytes 6291456 | tf_op jit(solution)/shard_map/gradient/pallas_call | solution.py:235
  103.3 1.9 %collective-permute-start.25 = (f32[448,512]{1,0:T(8,128)S(1)}, f32[448,512]{1,0:T(8,128)S(1)}, u32[]{:S(2)}, u32[]{:S(2)}) collective-permute-start(f32[448,512]{1,0:T(8,128)S(1)} %gradient.1.mine_ref), channel_id=1, source_target_pairs={{0,256},{1,257},{2,258},{3,259},{4,260},{5,261},{6,262},{7,263},{8... | collective-permute-start | bytes 2752520 | tf_op jit(solution)/shard_map/ppermute | solution.py:42
  105.2 2.4 %collective-permute-done.25.got_ref = f32[448,512]{1,0:T(8,128)S(1)} collective-permute-done((f32[448,512]{1,0:T(8,128)S(1)}, f32[448,512]{1,0:T(8,128)S(1)}, u32[]{:S(2)}, u32[]{:S(2)}) %collective-permute-start.25) | collective-permute-done | bytes 917536 | tf_op jit(solution)/shard_map/ppermute | solution.py:42
  107.7 1.9 %step.1 = (bf16[320,512]{1,0:T(8,128)(2,1)}, f32[16,8,320]{2,1,0:T(8,128)S(1)}) custom-call(s32[32]{0:T(128)S(1)} %get-tuple-element.9.table_ref, f32[448,512]{1,0:T(8,128)S(1)} %gradient.1.mine_ref, f32[448,512]{1,0:T(8,128)S(1)} %collective-permute-done.25.got_ref, f32[320,512]{1,0:T(8,128)S(1)} %bitcast.28, ...), custom_call_target="tpu_custom_call" | custom-call | tf_op jit(solution)/shard_map/step/pallas_call | solution.py:277
  109.6 15.8 %all_to_all.10 = f32[16,8,320]{2,1,0:T(8,128)S(1)} all-to-all(f32[16,8,320]{2,1,0:T(8,128)S(1)} %get-tuple-element.5), channel_id=1, replica_groups=mesh['group'=2,'dp'=16,'tensor'=16] {'tensor'}, dimensions={0} | all-to-all | bytes 327680 | tf_op jit(solution)/shard_map/all_to_all | solution.py:367
  125.5 4.4 %collective-permute-start.26 = (bf16[8,320]{1,0:T(8,128)(2,1)S(1)}, bf16[8,320]{1,0:T(8,128)(2,1)S(1)}, u32[]{:S(2)}, u32[]{:S(2)}) collective-permute-start(bf16[8,320]{1,0:T(8,128)(2,1)S(1)} %reduce_sum.9), channel_id=1, source_target_pairs={{0,0},{1,16},{2,32},{3,48},{4,64},{5,80},{6,96},{7,112},{8,128},{9... | collective-permute-start | bytes 15368 | tf_op jit(solution)/shard_map/ppermute | solution.py:42
  129.9 7.4 %collective-permute-done.26 = bf16[8,320]{1,0:T(8,128)(2,1)S(1)} collective-permute-done((bf16[8,320]{1,0:T(8,128)(2,1)S(1)}, bf16[8,320]{1,0:T(8,128)(2,1)S(1)}, u32[]{:S(2)}, u32[]{:S(2)}) %collective-permute-start.26) | collective-permute-done | bytes 5152 | tf_op jit(solution)/shard_map/ppermute | solution.py:42
  137.3 12.1 %all_to_all.11 = bf16[16,8,320]{2,1,0:T(8,128)(2,1)S(1)} all-to-all(bf16[16,8,320]{2,1,0:T(8,128)(2,1)S(1)} %broadcast_in_dim.2), channel_id=1, replica_groups=mesh['group'=2,'dp'=16,'tensor'=16] {'tensor'}, dimensions={0} | all-to-all | bytes 163840 | tf_op jit(solution)/shard_map/all_to_all | solution.py:371
  149.4 0.8 reshape.29
  (15 shorter events, 0.1 us)
Async XLA Ops:
  0.6 4.8 %copy-start = (bf16[1,256,5120]{2,1,0:T(8,128)(2,1)S(1)}, bf16[1,256,5120]{2,1,0:T(8,128)(2,1)}, u32[]{:S(2)}) copy-start(bf16[1,256,5120]{2,1,0:T(8,128)(2,1)} %param.14) | copy-start | bytes 7864324
  0.6 56.9 %copy-start.2 = (f32[1,512,320]{1,2,0:T(8,128)S(1)}, f32[1,512,320]{1,2,0:T(8,128)}, u32[]{:S(2)}) copy-start(f32[1,512,320]{1,2,0:T(8,128)} %param.16) | copy-start | bytes 1966084
  3.9 95.8 %copy-start.1 = (bf16[272,512]{1,0:T(8,128)(2,1)S(1)}, bf16[272,512]{1,0:T(8,128)(2,1)}, u32[]{:S(2)}) copy-start(bf16[272,512]{1,0:T(8,128)(2,1)} %attend.1.refs_8_) | copy-start | bytes 835588
  3.9 29.6 %collective-permute-start.9 = (bf16[272,512]{1,0:T(8,128)(2,1)}, bf16[272,512]{1,0:T(8,128)(2,1)}, u32[]{:S(2)}, u32[]{:S(2)}) collective-permute-start(bf16[272,512]{1,0:T(8,128)(2,1)} %attend.1.refs_8_), channel_id=1, source_target_pairs={{256,288},{257,289},{258,290},{259,291},{260,292},{261,293},{262,2... | collective-permute-start | bytes 835592 | tf_op jit(solution)/shard_map/ppermute | solution.py:42
  7.9 23.0 %collective-permute-start.16 = (bf16[320,256]{1,0:T(8,128)(2,1)}, bf16[320,256]{1,0:T(8,128)(2,1)}, u32[]{:S(2)}, u32[]{:S(2)}) collective-permute-start(bf16[320,256]{1,0:T(8,128)(2,1)} %bitcast.34), channel_id=1, source_target_pairs={{256,256},{257,16},{258,288},{259,304},{260,320},{261,336},{262,35... | collective-permute-start | bytes 491528 | tf_op jit(solution)/shard_map/ppermute | solution.py:42
  9.2 31.1 %collective-permute-start.4 = (bf16[272,512]{1,0:T(8,128)(2,1)}, bf16[272,512]{1,0:T(8,128)(2,1)}, u32[]{:S(2)}, u32[]{:S(2)}) collective-permute-start(bf16[272,512]{1,0:T(8,128)(2,1)} %attend.1.refs_8_), channel_id=1, source_target_pairs={{256,8},{257,9},{258,10},{259,11},{260,12},{261,13},{262,14},{263,... | collective-permute-start | bytes 835592 | tf_op jit(solution)/shard_map/ppermute | solution.py:42
  10.5 30.5 %collective-permute-start = (bf16[272,512]{1,0:T(8,128)(2,1)}, bf16[272,512]{1,0:T(8,128)(2,1)}, u32[]{:S(2)}, u32[]{:S(2)}) collective-permute-start(bf16[272,512]{1,0:T(8,128)(2,1)} %attend.1.refs_8_), channel_id=1, source_target_pairs={{256,224},{257,225},{258,226},{259,227},{260,228},{261,229},{262,2... | collective-permute-start | bytes 835592 | tf_op jit(solution)/shard_map/ppermute | solution.py:42
  30.9 12.0 %collective-permute-start.19 = (bf16[320,256]{1,0:T(8,128)(2,1)}, bf16[320,256]{1,0:T(8,128)(2,1)S(1)}, u32[]{:S(2)}, u32[]{:S(2)}) collective-permute-start(bf16[320,256]{1,0:T(8,128)(2,1)} %collective-permute-done.16), channel_id=1, source_target_pairs={{1,13},{2,14},{3,15},{4,8},{5,9},{6,10},{7,11},{8,4},{16,28},{18,3... | collective-permute-start | bytes 491528 | tf_op jit(solution)/shard_map/ppermute | solution.py:42
  32.2 12.7 %collective-permute-start.18 = (bf16[320,256]{1,0:T(8,128)(2,1)}, bf16[320,256]{1,0:T(8,128)(2,1)S(1)}, u32[]{:S(2)}, u32[]{:S(2)}) collective-permute-start(bf16[320,256]{1,0:T(8,128)(2,1)} %collective-permute-done.16), channel_id=1, source_target_pairs={{1,9},{2,10},{3,11},{4,12},{5,13},{6,14},{7,15},{8,0},{16,24},{18,... | collective-permute-start | bytes 491528 | tf_op jit(solution)/shard_map/ppermute | solution.py:42
  33.5 11.4 %collective-permute-start.17 = (bf16[320,256]{1,0:T(8,128)(2,1)}, bf16[320,256]{1,0:T(8,128)(2,1)S(1)}, u32[]{:S(2)}, u32[]{:S(2)}) collective-permute-start(bf16[320,256]{1,0:T(8,128)(2,1)} %collective-permute-done.16), channel_id=1, source_target_pairs={{1,5},{2,6},{3,7},{4,0},{5,1},{6,2},{7,3},{8,12},{16,20},{18,22},{... | collective-permute-start | bytes 491528 | tf_op jit(solution)/shard_map/ppermute | solution.py:42
  40.3 17.2 %collective-permute-start.10 = (bf16[272,512]{1,0:T(8,128)(2,1)}, bf16[272,512]{1,0:T(8,128)(2,1)S(1)}, u32[]{:S(2)}, u32[]{:S(2)}) collective-permute-start(bf16[272,512]{1,0:T(8,128)(2,1)} %collective-permute-done.9.refs_9_), channel_id=1, source_target_pairs={{256,288},{257,289},{258,290},{259,291},{260,292},{261,293},{262,2... | collective-permute-start | bytes 835592 | tf_op jit(solution)/shard_map/ppermute | solution.py:42
  41.0 12.3 %collective-permute-start.5 = (bf16[272,512]{1,0:T(8,128)(2,1)}, bf16[272,512]{1,0:T(8,128)(2,1)S(1)}, u32[]{:S(2)}, u32[]{:S(2)}) collective-permute-start(bf16[272,512]{1,0:T(8,128)(2,1)} %collective-permute-done.4), channel_id=1, source_target_pairs={{0,8},{1,9},{2,10},{3,11},{4,12},{5,13},{6,14},{7,15},{8,16},{9,17... | collective-permute-start | bytes 835592 | tf_op jit(solution)/shard_map/ppermute | solution.py:42
  43.0 15.9 %collective-permute-start.1 = (bf16[272,512]{1,0:T(8,128)(2,1)}, bf16[272,512]{1,0:T(8,128)(2,1)S(1)}, u32[]{:S(2)}, u32[]{:S(2)}) collective-permute-start(bf16[272,512]{1,0:T(8,128)(2,1)} %collective-permute-done.refs_0_), channel_id=1, source_target_pairs={{0,224},{1,225},{2,226},{3,227},{4,228},{5,229},{6,230},{7,231},{8... | collective-permute-start | bytes 835592 | tf_op jit(solution)/shard_map/ppermute | solution.py:42
  45.9 23.6 %collective-permute-start.22 = (bf16[2,320,256]{2,1,0:T(8,128)(2,1)S(1)}, bf16[2,320,256]{2,1,0:T(8,128)(2,1)S(1)}, u32[]{:S(2)}, u32[]{:S(2)}) collective-permute-start(bf16[2,320,256]{2,1,0:T(8,128)(2,1)S(1)} %pad_maximum_fusion.refs_16_), channel_id=1, source_target_pairs={{0,1},{1,2},{2,3},{3,0},{4,5},{5,6},{6,7},{7,4},{8,9},{9,10},{10,1... | collective-permute-start | bytes 983048 | tf_op jit(solution)/shard_map/ppermute | solution.py:42
  53.4 18.1 %collective-permute-start.12 = (bf16[272,512]{1,0:T(8,128)(2,1)S(1)}, bf16[272,512]{1,0:T(8,128)(2,1)S(1)}, u32[]{:S(2)}, u32[]{:S(2)}) collective-permute-start(bf16[272,512]{1,0:T(8,128)(2,1)S(1)} %collective-permute-done.5.refs_4_), channel_id=1, source_target_pairs={{0,288},{1,289},{2,290},{3,291},{4,292},{5,293},{6,294},{7,295},{8... | collective-permute-start | bytes 835592 | tf_op jit(solution)/shard_map/ppermute | solution.py:42
  54.7 17.4 %collective-permute-start.21 = (bf16[2,320,256]{2,1,0:T(8,128)(2,1)S(1)}, bf16[2,320,256]{2,1,0:T(8,128)(2,1)S(1)}, u32[]{:S(2)}, u32[]{:S(2)}) collective-permute-start(bf16[2,320,256]{2,1,0:T(8,128)(2,1)S(1)} %pad_maximum_fusion.refs_16_), channel_id=1, source_target_pairs={{0,2},{1,3},{2,0},{3,1},{4,6},{5,7},{6,4},{7,5},{8,10},{9,11},{10,... | collective-permute-start | bytes 983048 | tf_op jit(solution)/shard_map/ppermute | solution.py:42
  57.5 28.7 %collective-permute-start.23 = (f32[320,512]{1,0:T(8,128)S(1)}, f32[320,512]{1,0:T(8,128)S(1)}, u32[]{:S(2)}, u32[]{:S(2)}) collective-permute-start(f32[320,512]{1,0:T(8,128)S(1)} %bitcast.27), channel_id=1, source_target_pairs={{256,0},{257,1},{258,2},{259,3},{260,4},{261,5},{262,6},{263,7},{2... | collective-permute-start | bytes 1966088 | tf_op jit(solution)/shard_map/ppermute | solution.py:42
  58.8 18.5 %collective-permute-start.20 = (bf16[2,320,256]{2,1,0:T(8,128)(2,1)S(1)}, bf16[2,320,256]{2,1,0:T(8,128)(2,1)S(1)}, u32[]{:S(2)}, u32[]{:S(2)}) collective-permute-start(bf16[2,320,256]{2,1,0:T(8,128)(2,1)S(1)} %pad_maximum_fusion.refs_16_), channel_id=1, source_target_pairs={{0,3},{1,0},{2,1},{3,2},{4,7},{5,4},{6,5},{7,6},{8,11},{9,8},{10,9... | collective-permute-start | bytes 983048 | tf_op jit(solution)/shard_map/ppermute | solution.py:42
  69.5 9.8 %collective-permute-start.6 = (bf16[272,512]{1,0:T(8,128)(2,1)S(1)}, bf16[272,512]{1,0:T(8,128)(2,1)S(1)}, u32[]{:S(2)}, u32[]{:S(2)}) collective-permute-start(bf16[272,512]{1,0:T(8,128)(2,1)S(1)} %collective-permute-done.5.refs_4_), channel_id=1, source_target_pairs={{0,224},{1,225},{2,226},{3,227},{4,228},{5,229},{6,230},{7,231},{8... | collective-permute-start | bytes 835592 | tf_op jit(solution)/shard_map/ppermute | solution.py:42
  71.5 14.1 %collective-permute-start.13 = (bf16[272,512]{1,0:T(8,128)(2,1)S(1)}, bf16[272,512]{1,0:T(8,128)(2,1)S(1)}, u32[]{:S(2)}, u32[]{:S(2)}) collective-permute-start(bf16[272,512]{1,0:T(8,128)(2,1)S(1)} %collective-permute-done.12.refs_12_), channel_id=1, source_target_pairs={{256,288},{257,289},{258,290},{259,291},{260,292},{261,293},{262,2... | collective-permute-start | bytes 835592 | tf_op jit(solution)/shard_map/ppermute | solution.py:42
  72.1 22.5 %collective-permute-start.24 = (f32[320,512]{1,0:T(8,128)}, f32[320,512]{1,0:T(8,128)S(1)}, u32[]{:S(2)}, u32[]{:S(2)}) collective-permute-start(f32[320,512]{1,0:T(8,128)} %bitcast.29), channel_id=1, source_target_pairs={{256,0},{257,1},{258,2},{259,3},{260,4},{261,5},{262,6},{263,7},{2... | collective-permute-start | bytes 1966088 | tf_op jit(solution)/shard_map/ppermute | solution.py:42
  77.4 9.6 %collective-permute-start.2 = (bf16[272,512]{1,0:T(8,128)(2,1)S(1)}, bf16[272,512]{1,0:T(8,128)(2,1)S(1)}, u32[]{:S(2)}, u32[]{:S(2)}) collective-permute-start(bf16[272,512]{1,0:T(8,128)(2,1)S(1)} %collective-permute-done.1.refs_1_), channel_id=1, source_target_pairs={{0,224},{1,225},{2,226},{3,227},{4,228},{5,229},{6,230},{7,231},{8... | collective-permute-start | bytes 835592 | tf_op jit(solution)/shard_map/ppermute | solution.py:42
  79.3 10.7 %collective-permute-start.7 = (bf16[272,512]{1,0:T(8,128)(2,1)S(1)}, bf16[272,512]{1,0:T(8,128)(2,1)S(1)}, u32[]{:S(2)}, u32[]{:S(2)}) collective-permute-start(bf16[272,512]{1,0:T(8,128)(2,1)S(1)} %collective-permute-done.6.refs_5_), channel_id=1, source_target_pairs={{0,224},{1,225},{2,226},{3,227},{4,228},{5,229},{6,230},{7,231},{8... | collective-permute-start | bytes 835592 | tf_op jit(solution)/shard_map/ppermute | solution.py:42
  85.6 8.4 %collective-permute-start.14 = (bf16[272,512]{1,0:T(8,128)(2,1)S(1)}, bf16[272,512]{1,0:T(8,128)(2,1)S(1)}, u32[]{:S(2)}, u32[]{:S(2)}) collective-permute-start(bf16[272,512]{1,0:T(8,128)(2,1)S(1)} %collective-permute-done.13.refs_13_), channel_id=1, source_target_pairs={{256,288},{257,289},{258,290},{259,291},{260,292},{261,293},{262,2... | collective-permute-start | bytes 835592 | tf_op jit(solution)/shard_map/ppermute | solution.py:42
  86.3 8.4 %collective-permute-start.11 = (bf16[272,512]{1,0:T(8,128)(2,1)S(1)}, bf16[272,512]{1,0:T(8,128)(2,1)S(1)}, u32[]{:S(2)}, u32[]{:S(2)}) collective-permute-start(bf16[272,512]{1,0:T(8,128)(2,1)S(1)} %collective-permute-done.10.refs_10_), channel_id=1, source_target_pairs={{256,288},{257,289},{258,290},{259,291},{260,292},{261,293},{262,2... | collective-permute-start | bytes 835592 | tf_op jit(solution)/shard_map/ppermute | solution.py:42
  87.0 9.6 %collective-permute-start.3 = (bf16[272,512]{1,0:T(8,128)(2,1)S(1)}, bf16[272,512]{1,0:T(8,128)(2,1)S(1)}, u32[]{:S(2)}, u32[]{:S(2)}) collective-permute-start(bf16[272,512]{1,0:T(8,128)(2,1)S(1)} %collective-permute-done.2.refs_2_), channel_id=1, source_target_pairs={{0,224},{1,225},{2,226},{3,227},{4,228},{5,229},{6,230},{7,231},{8... | collective-permute-start | bytes 835592 | tf_op jit(solution)/shard_map/ppermute | solution.py:42
  90.0 9.6 %collective-permute-start.8 = (bf16[272,512]{1,0:T(8,128)(2,1)S(1)}, bf16[272,512]{1,0:T(8,128)(2,1)S(1)}, u32[]{:S(2)}, u32[]{:S(2)}) collective-permute-start(bf16[272,512]{1,0:T(8,128)(2,1)S(1)} %collective-permute-done.7.refs_6_), channel_id=1, source_target_pairs={{0,224},{1,225},{2,226},{3,227},{4,228},{5,229},{6,230},{7,231},{8... | collective-permute-start | bytes 835592 | tf_op jit(solution)/shard_map/ppermute | solution.py:42
  94.0 5.7 %collective-permute-start.15 = (bf16[272,512]{1,0:T(8,128)(2,1)S(1)}, bf16[272,512]{1,0:T(8,128)(2,1)S(1)}, u32[]{:S(2)}, u32[]{:S(2)}) collective-permute-start(bf16[272,512]{1,0:T(8,128)(2,1)S(1)} %collective-permute-done.14.refs_14_), channel_id=1, source_target_pairs={{256,288},{257,289},{258,290},{259,291},{260,292},{261,293},{262,2... | collective-permute-start | bytes 835592 | tf_op jit(solution)/shard_map/ppermute | solution.py:42
  99.7 8.0 %copy-start.3 = (f32[1,512,320]{1,2,0:T(8,128)S(1)}, f32[1,512,320]{1,2,0:T(8,128)}, u32[]{:S(2)}) copy-start(f32[1,512,320]{1,2,0:T(8,128)} %param.17) | copy-start | bytes 1966084
  99.7 8.0 %copy-start.4 = (bf16[512,320]{0,1:T(8,128)(2,1)S(1)}, bf16[512,320]{0,1:T(8,128)(2,1)}, u32[]{:S(2)}) copy-start(bf16[512,320]{0,1:T(8,128)(2,1)} %param.15) | copy-start | bytes 983044
  103.3 4.4 %collective-permute-start.25 = (f32[448,512]{1,0:T(8,128)S(1)}, f32[448,512]{1,0:T(8,128)S(1)}, u32[]{:S(2)}, u32[]{:S(2)}) collective-permute-start(f32[448,512]{1,0:T(8,128)S(1)} %gradient.1.mine_ref), channel_id=1, source_target_pairs={{0,256},{1,257},{2,258},{3,259},{4,260},{5,261},{6,262},{7,263},{8... | collective-permute-start | bytes 2752520 | tf_op jit(solution)/shard_map/ppermute | solution.py:42
  125.5 11.8 %collective-permute-start.26 = (bf16[8,320]{1,0:T(8,128)(2,1)S(1)}, bf16[8,320]{1,0:T(8,128)(2,1)S(1)}, u32[]{:S(2)}, u32[]{:S(2)}) collective-permute-start(bf16[8,320]{1,0:T(8,128)(2,1)S(1)} %reduce_sum.9), channel_id=1, source_target_pairs={{0,0},{1,16},{2,32},{3,48},{4,64},{5,80},{6,96},{7,112},{8,128},{9... | collective-permute-start | bytes 15368 | tf_op jit(solution)/shard_map/ppermute | solution.py:42

commit v3 on v2

v3 whole, which is shorter than its diff:
```python
import math

import jax
import jax.numpy as jnp
import numpy as np
from jax import lax
from jax.experimental import pallas as pl
from jax.experimental.pallas import tpu as pltpu
from jax.sharding import Mesh
from jax.sharding import PartitionSpec as P

D = 5120
KVH = 8
HD = 128
EOS = 151645
STEPS = 4
CACHE = 256

learning_rate = 0.0003
weight_decay = 0.1
beta_one = 0.9
beta_two = 0.95
first_bias = 1.0 - 0.9**10
second_bias = 1.0 - 0.95**10
epsilon = 1e-08

AXES = ("group", "y", "z_hi", "z_lo", "x")
SHAPE = (2, 8, 2, 4, 4)
DP, TENSOR = ("y", "z_hi"), ("z_lo", "x")
TOK = 256
FEAT = 512
COLS = 320
ROWS = 8
PAD = 16
f32, bf16 = jnp.float32, jnp.bfloat16


def permute(value, target):
    pairs = []
    for flat, place in enumerate(np.ndindex(*SHAPE)):
        to = target(*place)
        if to is not None:
            pairs.append((flat, int(np.ravel_multi_index(to, SHAPE))))
    return lax.ppermute(value, AXES, pairs)


def keeper(zh, x):
    return int((x & 1) == zh)


def to_partner(g, y, zh, zl, x):
    return (0, y, 1 - zh, zl, x) if g == 1 else None


def transposed(g, y, zh, zl, x):
    return (g, zl * 2 + (x >> 1), x & 1, y >> 1, (y & 1) * 2 + zh)


def cot_transposed(g, *place):
    _, y, zh, zl, x = transposed(g, *place)
    return (keeper(zh, x), y, zh, zl, x) if g == 1 else None


def along_zl(flip):
    return lambda g, y, zh, zl, x: (g, y, zh, zl ^ flip, x) if g == keeper(zh, x) else None


def along_x(step):
    return lambda g, y, zh, zl, x: (g, y, zh, zl, (x + step) % 4) if g == keeper(zh, x) else None


def other_core(g, y, zh, zl, x):
    return (1 - g, y, zh, zl, x)


def to_rollout(g, y, zh, zl, x):
    return (0, y, zh, zl, x) if g == 1 else None


FLIPS = (0, 3, 1, 2)


def device_table():
    table = np.zeros((512, 32), np.int32)
    for flat, (g, y, zh, zl, x) in enumerate(np.ndindex(*SHAPE)):
        token_zh = zh if g == 1 else 1 - zh
        table[flat, 0] = g
        table[flat, 1] = token_zh
        for n in range(8):
            table[flat, 8 + n] = (2 * (n & 1) + token_zh - x) % 4
            table[flat, 16 + n] = FLIPS.index(zl ^ (n >> 1))
    return table


def attend_kernel(
    head_ref, lengths_ref, ids_ref, q_ref, k_ref, v_ref, nk_ref, nv_ref, out_ref, q_rows, nk_rows, nv_rows
):
    for t in range(STEPS):
        place = slice(2 * t, 2 * t + 2)
        q_rows[place, :] = q_ref[t].astype(f32)
        nk_rows[place, :] = nk_ref[t].astype(f32)
        nv_rows[place, :] = nv_ref[t].astype(f32)
    queries = q_rows[...]
    query = jnp.concatenate(
        [queries[:, h * HD : (h + 1) * HD] for h in range(4)], axis=0
    ).astype(bf16)
    keys = k_ref[...].reshape(2 * CACHE, HD)
    values = v_ref[...].reshape(2 * CACHE, HD)
    fresh_keys = nk_rows[...].astype(bf16)
    fresh_values = nv_rows[...].astype(bf16)
    scale = 1.0 / math.sqrt(HD)
    nt = (((1,), (1,)), ((), ()))
    cache_scores = lax.dot_general(query, keys, nt, preferred_element_type=f32) * scale
    step_scores = lax.dot_general(query, fresh_keys, nt, preferred_element_type=f32) * scale
    count = 4 * ROWS

    def place(width):
        place_row = lax.broadcasted_iota(jnp.int32, (count, width), 0) & (ROWS - 1)
        place_key = lax.broadcasted_iota(jnp.int32, (count, width), 1)
        return place_row >> 1, place_row & 1, place_key

    step, row, key = place(2 * CACHE)
    length = jnp.where(row == 0, lengths_ref[0], lengths_ref[1])
    cache_valid = ((key >> 8) == row) & ((key & (CACHE - 1)) < length)
    step, row, key = place(ROWS)
    step_valid = ((key & 1) == row) & ((key >> 1) <= step)
    cache_scores = jnp.where(cache_valid, cache_scores, -jnp.inf)
    step_scores = jnp.where(step_valid, step_scores, -jnp.inf)
    peak = jnp.maximum(
        jnp.max(cache_scores, axis=-1, keepdims=True), jnp.max(step_scores, axis=-1, keepdims=True)
    )
    cache_exp = jnp.exp(cache_scores - peak)
    step_exp = jnp.exp(step_scores - peak)
    denominator = jnp.sum(cache_exp, axis=-1, keepdims=True) + jnp.sum(
        step_exp, axis=-1, keepdims=True
    )
    cache_probs = (cache_exp / denominator).astype(bf16)
    step_probs = (step_exp / denominator).astype(bf16)
    nn = (((1,), (0,)), ((), ()))
    mixed = lax.dot_general(cache_probs, values, nn, preferred_element_type=f32)
    mixed = mixed + lax.dot_general(step_probs, fresh_values, nn, preferred_element_type=f32)
    step, row, _ = place(HD)
    dead = jnp.zeros((count, HD), jnp.int32)
    for u in range(STEPS - 1):
        for r in range(2):
            ended = (ids_ref[r, u] == EOS).astype(jnp.int32)
            dead = dead + jnp.where((row == r) & (step > u), ended, 0)
    mixed = jnp.where(dead == 0, mixed, 0.0)
    flat = jnp.concatenate([mixed[h * ROWS : (h + 1) * ROWS] for h in range(4)], axis=1)
    out_ref[...] = jnp.concatenate([flat, jnp.zeros_like(flat)], axis=0).astype(bf16)


def attend(head, queries, cache_keys, cache_values, new_keys, new_values, lengths, ids):
    whole = lambda *shape: pl.BlockSpec(shape, lambda i, *_: (0,) * len(shape))
    cache = pl.BlockSpec((2, CACHE, HD), lambda i, m, *_: (0, m[0], 0))
    fresh = pl.BlockSpec((STEPS, 2, HD), lambda i, m, *_: (0, 0, m[0]))
    return pl.pallas_call(
        attend_kernel,
        out_shape=jax.ShapeDtypeStruct((PAD, FEAT), bf16),
        grid_spec=pltpu.PrefetchScalarGridSpec(
            num_scalar_prefetch=3,
            grid=(1,),
            in_specs=[whole(STEPS, 2, FEAT), cache, cache, fresh, fresh],
            out_specs=whole(PAD, FEAT),
            scratch_shapes=[
                pltpu.VMEM((ROWS, FEAT), f32),
                pltpu.VMEM((ROWS, HD), f32),
                pltpu.VMEM((ROWS, HD), f32),
            ],
        ),
        name="attend",
    )(head, lengths, ids, queries, cache_keys, cache_values, new_keys, new_values)


def base_kernel(table_ref, act_ref, act_got, rows_ref, rows_got, out_ref):
    @pl.when(table_ref[0] == 1)
    def _():
        out_ref[:TOK, :] = act_ref[...]
        out_ref[TOK:, :] = rows_ref[...]

    @pl.when(table_ref[0] == 0)
    def _():
        out_ref[:TOK, :] = act_got[...]
        out_ref[TOK:, :] = rows_got[...]


def base_of(table, *parts):
    vmem = pl.BlockSpec(memory_space=pltpu.VMEM)
    return pl.pallas_call(
        base_kernel,
        out_shape=jax.ShapeDtypeStruct((TOK + PAD, FEAT), bf16),
        in_specs=[pl.BlockSpec(memory_space=pltpu.SMEM)] + [vmem] * 4,
        out_specs=vmem,
        name="base",
    )(table, *parts)


def gradient_kernel(table_ref, chunks_ref, *refs):
    blocks, (out_ref, chunk_rows, block_rows, row_tiles, sems) = refs[:4], refs[-5:]
    act_copies = [
        pltpu.make_async_copy(
            chunks_ref.at[n, :TOK], chunk_rows.at[pl.ds(n * TOK, TOK)], sems.at[n]
        )
        for n in range(8)
    ]
    row_copies = [
        pltpu.make_async_copy(chunks_ref.at[n, TOK:], row_tiles.at[n], sems.at[16 + n])
        for n in range(8)
    ]
    for n in range(8):
        act_copies[n].start()
        for b in range(4):

            @pl.when(table_ref[8 + n] == b)
            def _():
                pltpu.make_async_copy(
                    blocks[b].at[table_ref[16 + n]],
                    block_rows.at[:, pl.ds(n * TOK, TOK)],
                    sems.at[8 + n],
                ).start()

        row_copies[n].start()
    out_ref[COLS:, :] = jnp.zeros((16 * ROWS, FEAT), f32)
    for half in range(2):
        for n in range(4 * half, 4 * half + 4):
            act_copies[n].wait()
            pltpu.make_async_copy(
                blocks[0].at[0], block_rows.at[:, pl.ds(n * TOK, TOK)], sems.at[8 + n]
            ).wait()
        span = pl.ds(half * 4 * TOK, 4 * TOK)
        part = jnp.dot(block_rows[:, span], chunk_rows[span, :], preferred_element_type=f32)
        if half == 0:
            out_ref[:COLS, :] = part
        else:
            out_ref[:COLS, :] += part
    for n in range(8):
        row_copies[n].wait()
        place = pl.multiple_of(COLS + (2 * n + table_ref[1]) * ROWS, ROWS)
        out_ref[pl.ds(place, ROWS), :] = row_tiles[n].astype(f32)[:ROWS]


def gradient(table, chunks, blocks, others):
    hbm = pl.BlockSpec(memory_space=pl.ANY)
    operands = (chunks, *blocks, *others)
    return pl.pallas_call(
        gradient_kernel,
        out_shape=jax.ShapeDtypeStruct((COLS + 16 * ROWS, FEAT), f32),
        in_specs=[pl.BlockSpec(memory_space=pltpu.SMEM)] + [hbm] * len(operands),
        out_specs=pl.BlockSpec(memory_space=pltpu.VMEM),
        scratch_shapes=[
            pltpu.VMEM((8 * TOK, FEAT), bf16),
            pltpu.VMEM((COLS, 8 * TOK), bf16),
            pltpu.VMEM((8, PAD, FEAT), bf16),
            pltpu.SemaphoreType.DMA((24,)),
        ],
        compiler_params=pltpu.CompilerParams(vmem_limit_bytes=32 * 2**20),
        cost_estimate=pl.CostEstimate(
            flops=2 * 8 * TOK * COLS * FEAT, bytes_accessed=6 * 2**20, transcendentals=0
        ),
        name="gradient",
    )(table, *operands)


def step_kernel(
    table_ref, mine_ref, got_ref, one_ref, one_got, two_ref, two_got, weight_ref, update_ref, out_ref
):
    learner = table_ref[0] == 1
    grad = mine_ref[:COLS, :] + got_ref[:COLS, :]
    moment_one = jnp.where(learner, one_ref[...], one_got[...])
    moment_two = jnp.where(learner, two_ref[...], two_got[...])
    first_moment = beta_one * moment_one + (1.0 - beta_one) * grad
    second_moment = beta_two * moment_two + (1.0 - beta_two) * grad * grad
    update = (
        first_moment / first_bias / (jnp.sqrt(second_moment / second_bias) + epsilon)
    ).astype(bf16)
    update_ref[...] = update
    widened = weight_ref[...].astype(f32)
    renewed = (
        widened - learning_rate * (update.astype(f32) + weight_decay * widened)
    ).astype(bf16)
    rows = (mine_ref[COLS:, :] + got_ref[COLS:, :]).astype(bf16)
    part = lax.dot_general(rows, renewed, (((1,), (1,)), ((), ())), preferred_element_type=f32)
    out_ref[...] = part.reshape(16, ROWS, COLS)


def step(table, mine, got, one, one_got, two, two_got, weight):
    vmem = pl.BlockSpec(memory_space=pltpu.VMEM)
    return pl.pallas_call(
        step_kernel,
        out_shape=(
            jax.ShapeDtypeStruct((COLS, FEAT), bf16),
            jax.ShapeDtypeStruct((16, ROWS, COLS), f32),
        ),
        in_specs=[pl.BlockSpec(memory_space=pltpu.SMEM)] + [vmem] * 7,
        out_specs=(vmem, vmem),
        compiler_params=pltpu.CompilerParams(vmem_limit_bytes=32 * 2**20),
        name="step",
    )(table, mine, got, one, one_got, two, two_got, weight)


def local(
    activations,
    cotangent,
    weight,
    moment_one,
    moment_two,
    queries,
    cache_keys,
    cache_values,
    new_keys,
    new_values,
    lengths,
    token_ids,
):
    flat, q = lax.axis_index(AXES), lax.axis_index(TENSOR)
    table = lax.dynamic_slice_in_dim(jnp.asarray(device_table()), flat, 1, 0)[0]

    act = activations[0]
    act_got = permute(act, to_partner)
    rows = attend(
        (q >> 1).reshape(1),
        queries,
        cache_keys,
        cache_values,
        new_keys,
        new_values,
        lengths,
        token_ids.T,
    )
    rows_got = permute(rows, to_partner)
    base = base_of(table, act, act_got, rows, rows_got)
    chunks = lax.all_gather(base, "y", axis=0)

    cut = lax.dynamic_slice_in_dim(cotangent[0], q * COLS, COLS, 1).T
    own = permute(cut, cot_transposed)
    two_blocks = jnp.stack([own, permute(own, along_zl(3))])
    four = jnp.concatenate([two_blocks, permute(two_blocks, along_zl(1))], axis=0)
    blocks = (
        four,
        permute(four, along_x(-1)),
        permute(four, along_x(2)),
        permute(four, along_x(1)),
    )

    one, two = moment_one[0].T, moment_two[0].T
    one_got = permute(one, to_rollout)
    two_got = permute(two, to_rollout)

    mine = gradient(table, chunks, blocks, (one_got, two_got))
    got = permute(mine, other_core)
    update, partial = step(table, mine, got, one, one_got, two, two_got, weight.T)

    shares = lax.all_to_all(partial, TENSOR, split_axis=0, concat_axis=0, tiled=True)
    summed = jnp.sum(shares, axis=0).astype(bf16)
    block = permute(summed, transposed)
    spread = jnp.broadcast_to(block[None], (16, ROWS, COLS))
    gathered = lax.all_to_all(spread, TENSOR, split_axis=0, concat_axis=0, tiled=True)
    decoded = gathered.transpose(1, 0, 2).reshape(STEPS, ROWS // STEPS, D)
    return (update.T, decoded)


def solution(mesh):
    fine = Mesh(mesh.devices.reshape(SHAPE), AXES)
    return jax.shard_map(
        local,
        mesh=fine,
        in_specs=(
            P("group", DP, TENSOR),
            P("group", DP, None),
            P(TENSOR, DP),
            P("group", TENSOR, DP),
            P("group", TENSOR, DP),
            P(None, DP, TENSOR),
            P(DP, None, None),
            P(DP, None, None),
            P(None, DP, None),
            P(None, DP, None),
            P(DP),
            P(None, DP),
        ),
        out_specs=(P(TENSOR, DP), P(None, DP, None)),
        check_vma=False,
    )
```

time: 153 us -> 153 us (level)
  the two profiles are of different devices: /device:TPU:56 before, /device:TPU:24 now
where the time goes in v3:
time: 153 us; the launch traced here: 152 us
  waiting for transfers between devices  68.1 us (45%)
  blocking collectives  31 us (20%)
  starting transfers between devices  15 us (10%)
  local copies, waits for them, and re-layouts  14.9 us (10%)
  between operations  14.3 us (9%)
  Pallas kernels  8.93 us (6%)
    ppermute x12, waiting for transfers between devices, permute(): return lax.ppermute(value, AXES, pairs)  68.1 us
    all_to_all x1, blocking collectives, local(): lax.all_to_all(partial, TENSOR, split_axis=0, concat_axis=0, tiled=True)  16.7 us
    ppermute x12, starting transfers between devices, permute(): return lax.ppermute(value, AXES, pairs)  14.9 us
    all_to_all x1, blocking collectives, local(): lax.all_to_all(spread, TENSOR, split_axis=0, concat_axis=0, tiled=True)  14.2 us
    unnamed x38, local copies, waits for them, and re-layouts  12.6 us
  transfers between devices with their start and end apart: 13, of which 7 were waited for; matrix products, arithmetic and copies ran while one was open for 1% of the time, Pallas kernels for 2%

profile of v3, /device:TPU:24, one launch (start us, length us, event | category | flops | bytes accessed | tf_op | source)
XLA Modules:
  0.0 152.3 jit_solution(17444775969130770047)
XLA Ops:
  7.2 0.0 copy-start
  7.2 0.0 all-gather.3.cloned.1.call-start
  7.2 1.4 collective-permute-start
  8.7 2.8 %attend.1.rows_ref = bf16[16,512]{1,0:T(8,128)(2,1)} custom-call(s32[1]{0:T(128)} %bitcast.2.head_ref, s32[2]{0:T(128)} %lengths_ref.1, s32[2,4]{1,0:T(2,128)} %bitcast.34, bf16[4,2,512]{2,1,0:T(2,128)(2,1)} %q_ref.1, bf16[2,2048,128]{2,1,0:T(8,128)(2,1)} %k_ref.1, bf16[2,2048,128]{2,1,0:T(8,128)(2,1)} %v_ref.1, bf16[4,2,1024]{2,1,0:T(2,128)(2,1)} %nk_ref.1, ...), custom_call_target="tpu_custom_call" | custom-call | tf_op jit(solution)/shard_map/attend/pallas_call | solution.py:157
  11.4 1.3 collective-permute-start.1
  12.7 1.2 dynamic-slice_bitcast_fusion.table_ref
  14.0 0.0 copy-start.16
  14.0 8.9 %collective-permute-done.1.rows_got = bf16[16,512]{1,0:T(8,128)(2,1)S(1)} collective-permute-done((bf16[16,512]{1,0:T(8,128)(2,1)}, bf16[16,512]{1,0:T(8,128)(2,1)S(1)}, u32[]{:S(2)}, u32[]{:S(2)}) %collective-permute-start.1) | collective-permute-done | bytes 16416 | tf_op jit(solution)/shard_map/ppermute | solution.py:44
  22.9 0.0 copy-start.18
  22.9 0.0 collective-permute-done.act_got
  22.9 0.6 copy-done.18
  23.5 0.0 copy-start.17
  23.5 0.7 copy-done.17
  24.2 1.8 %base.1 = bf16[272,512]{1,0:T(8,128)(2,1)} custom-call(s32[32]{0:T(128)} %dynamic-slice_bitcast_fusion.table_ref, bf16[256,512]{1,0:T(8,128)(2,1)} %bitcast.32, bf16[256,512]{1,0:T(8,128)(2,1)} %copy-done.17, bf16[16,512]{1,0:T(8,128)(2,1)} %attend.1.rows_ref, bf16[16,512]{1,0:T(8,128)(2,1)} %copy-done.18), custom_call_target="tpu_custom_call" | custom-call | tf_op jit(solution)/shard_map/base/pallas_call | solution.py:189
  26.0 0.0 all-gather.3.cloned.1.call-update
  26.0 0.0 copy-done
  26.0 0.1 constant_dynamic-slice_fusion
  26.2 0.1 copy.17
  26.3 0.7 collective-permute-start.2
  27.0 0.0 collective-permute-done.2
  27.0 0.7 collective-permute-start.3
  27.7 0.0 collective-permute-done.3
  27.7 0.7 collective-permute-start.4
  28.4 1.3 collective-permute-start.8
  29.7 1.3 collective-permute-start.9
  31.0 0.0 collective-permute-done.4
  31.0 0.1 pad_maximum_fusion.refs_0_
  31.1 1.3 collective-permute-start.7
  32.4 0.7 collective-permute-start.6
  33.1 1.3 collective-permute-start.5
  34.4 0.0 copy-start.4
  34.4 0.8 copy-done.4
  35.2 22.1 %collective-permute-done.8.refs_4_.one_got = f32[320,512]{1,0:T(8,128)S(1)} collective-permute-done((f32[320,512]{1,0:T(8,128)}, f32[320,512]{1,0:T(8,128)S(1)}, u32[]{:S(2)}, u32[]{:S(2)}) %collective-permute-start.8) | collective-permute-done | bytes 655392 | tf_op jit(solution)/shard_map/ppermute | solution.py:44
  57.3 1.3 collective-permute-done.9.refs_5_.two_got
  58.7 0.0 copy-start.1
  58.7 0.8 copy-done.1
  59.5 23.9 %collective-permute-done.7.refs_3_ = bf16[4,320,256]{2,1,0:T(8,128)(2,1)S(1)} collective-permute-done((bf16[4,320,256]{2,1,0:T(8,128)(2,1)S(1)}, bf16[4,320,256]{2,1,0:T(8,128)(2,1)S(1)}, u32[]{:S(2)}, u32[]{:S(2)}) %collective-permute-start.7) | collective-permute-done | bytes 655392 | tf_op jit(solution)/shard_map/ppermute | solution.py:44
  83.4 0.0 copy-start.9
  83.4 0.9 copy-done.9
  84.3 0.0 collective-permute-done.6.refs_2_
  84.3 0.0 copy-start.11
  84.3 0.8 copy-done.11
  85.1 1.2 collective-permute-done.5.refs_1_
  86.3 0.8 copy-done.13
  87.1 0.0 copy-done.16
  87.1 1.1 copy-done.2
  88.2 1.1 copy-done.5
  89.3 1.6 %copy-done.6 = bf16[2176,512]{1,0:T(8,128)(2,1)S(1)} copy-done((bf16[2176,512]{1,0:T(8,128)(2,1)S(1)}, bf16[2176,512]{1,0:T(8,128)(2,1)}, u32[]{:S(2)}) %copy-start.6) | copy-done | bytes 2228248
  90.9 1.1 copy-done.10
  92.0 1.1 copy-done.12
  93.1 1.1 copy-done.14
  94.2 2.4 %gradient.1.mine_ref = f32[448,512]{1,0:T(8,128)S(1)} custom-call(s32[32]{0:T(128)S(1)} %copy-done.16, bf16[8,272,512]{2,1,0:T(8,128)(2,1)S(1)} %bitcast.20, bf16[4,320,256]{2,1,0:T(8,128)(2,1)S(1)} %copy-done.5, bf16[4,320,256]{2,1,0:T(8,128)(2,1)S(1)} %copy-done.14, bf16[4,320,256]{2,1,0:T(8,128)(2,1)S(1)} %copy-done.12, ...), custom_call_target="tpu_custom_call" | custom-call | flops 671088640 | bytes 6291456 | tf_op jit(solution)/shard_map/gradient/pallas_call | solution.py:245
  96.7 1.9 %collective-permute-start.10 = (f32[448,512]{1,0:T(8,128)S(1)}, f32[448,512]{1,0:T(8,128)S(1)}, u32[]{:S(2)}, u32[]{:S(2)}) collective-permute-start(f32[448,512]{1,0:T(8,128)S(1)} %gradient.1.mine_ref), channel_id=1, source_target_pairs={{0,256},{1,257},{2,258},{3,259},{4,260},{5,261},{6,262},{7,263},{8... | collective-permute-start | bytes 2752520 | tf_op jit(solution)/shard_map/ppermute | solution.py:44
  98.6 2.4 %collective-permute-done.10.got_ref = f32[448,512]{1,0:T(8,128)S(1)} collective-permute-done((f32[448,512]{1,0:T(8,128)S(1)}, f32[448,512]{1,0:T(8,128)S(1)}, u32[]{:S(2)}, u32[]{:S(2)}) %collective-permute-start.10) | collective-permute-done | bytes 917536 | tf_op jit(solution)/shard_map/ppermute | solution.py:44
  101.0 0.0 copy-done.3
  101.0 0.0 copy-done.7
  101.0 0.0 copy-done.8
  101.0 0.0 copy-done.15
  101.1 1.9 %step.1 = (bf16[320,512]{1,0:T(8,128)(2,1)}, f32[16,8,320]{2,1,0:T(8,128)S(1)}) custom-call(s32[32]{0:T(128)S(1)} %copy-done.16, f32[448,512]{1,0:T(8,128)S(1)} %gradient.1.mine_ref, f32[448,512]{1,0:T(8,128)S(1)} %collective-permute-done.10.got_ref, f32[320,512]{1,0:T(8,128)S(1)} %bitcast.22, f32[320,512]{1,0:T(8,128)S(1)} %collective-permute-done.8.refs_4_.one_got, ...), custom_call_target="tpu_custom_call" | custom-call | tf_op jit(solution)/shard_map/step/pallas_call | solution.py:288
  103.0 16.7 %all_to_all.10 = f32[16,8,320]{2,1,0:T(8,128)S(1)} all-to-all(f32[16,8,320]{2,1,0:T(8,128)S(1)} %get-tuple-element.5), channel_id=1, replica_groups=mesh['group'=2,'y'=8,'z_hi'=2,'z_lo'=4,'x'=4] {'z_lo','x'}, dimensions={0} | all-to-all | bytes 327680 | tf_op jit(solution)/shard_map/all_to_all | solution.py:353
  119.7 2.4 %collective-permute-start.11 = (bf16[8,320]{1,0:T(8,128)(2,1)S(1)}, bf16[8,320]{1,0:T(8,128)(2,1)S(1)}, u32[]{:S(2)}, u32[]{:S(2)}) collective-permute-start(bf16[8,320]{1,0:T(8,128)(2,1)S(1)} %reduce_sum.9), channel_id=1, source_target_pairs={{0,0},{1,16},{2,32},{3,48},{4,64},{5,80},{6,96},{7,112},{8,128},{9... | collective-permute-start | bytes 15368 | tf_op jit(solution)/shard_map/ppermute | solution.py:44
  122.2 8.2 %collective-permute-done.11 = bf16[8,320]{1,0:T(8,128)(2,1)S(1)} collective-permute-done((bf16[8,320]{1,0:T(8,128)(2,1)S(1)}, bf16[8,320]{1,0:T(8,128)(2,1)S(1)}, u32[]{:S(2)}, u32[]{:S(2)}) %collective-permute-start.11) | collective-permute-done | bytes 5152 | tf_op jit(solution)/shard_map/ppermute | solution.py:44
  130.4 14.2 %all_to_all.11 = bf16[16,8,320]{2,1,0:T(8,128)(2,1)S(1)} all-to-all(bf16[16,8,320]{2,1,0:T(8,128)(2,1)S(1)} %broadcast_in_dim.2), channel_id=1, replica_groups=mesh['group'=2,'y'=8,'z_hi'=2,'z_lo'=4,'x'=4] {'z_lo','x'}, dimensions={0} | all-to-all | bytes 163840 | tf_op jit(solution)/shard_map/all_to_all | solution.py:357
  144.6 0.8 reshape.13
  (16 shorter events, 0.1 us)
Async XLA Ops:
  7.2 18.8 %copy-start = (bf16[1,256,5120]{2,1,0:T(8,128)(2,1)S(1)}, bf16[1,256,5120]{2,1,0:T(8,128)(2,1)}, u32[]{:S(2)}) copy-start(bf16[1,256,5120]{2,1,0:T(8,128)(2,1)} %param.14) | copy-start | bytes 7864324
  7.2 80.0 %all-gather.3.cloned.1.call-start = ((), (), s32[]{:S(2)}) async-start(), calls=%async_computation.2 | async-start | bytes 2506752 | tf_op jit(solution)/shard_map/all_gather | solution.py:332
  7.2 15.7 %collective-permute-start = (bf16[256,512]{1,0:T(8,128)(2,1)}, bf16[256,512]{1,0:T(8,128)(2,1)S(1)}, u32[]{:S(2)}, u32[]{:S(2)}) collective-permute-start(bf16[256,512]{1,0:T(8,128)(2,1)} %bitcast.31), channel_id=1, source_target_pairs={{256,16},{257,17},{258,18},{259,19},{260,20},{261,21},{262,22},{26... | collective-permute-start | bytes 786440 | tf_op jit(solution)/shard_map/ppermute | solution.py:44
  11.4 11.5 %collective-permute-start.1 = (bf16[16,512]{1,0:T(8,128)(2,1)}, bf16[16,512]{1,0:T(8,128)(2,1)S(1)}, u32[]{:S(2)}, u32[]{:S(2)}) collective-permute-start(bf16[16,512]{1,0:T(8,128)(2,1)} %attend.1.rows_ref), channel_id=1, source_target_pairs={{256,16},{257,17},{258,18},{259,19},{260,20},{261,21},{262,22},{26... | collective-permute-start | bytes 49160 | tf_op jit(solution)/shard_map/ppermute | solution.py:44
  14.0 73.2 %copy-start.16 = (s32[32]{0:T(128)S(1)}, s32[32]{0:T(128)}, u32[]{:S(2)}) copy-start(s32[32]{0:T(128)} %dynamic-slice_bitcast_fusion.table_ref) | copy-start | bytes 388
  22.9 0.6 copy-start.18
  23.5 0.7 copy-start.17
  26.3 0.7 collective-permute-start.2
  27.0 0.7 collective-permute-start.3
  27.7 3.3 %collective-permute-start.4 = (bf16[2,320,256]{2,1,0:T(8,128)(2,1)S(1)}, bf16[2,320,256]{2,1,0:T(8,128)(2,1)S(1)}, u32[]{:S(2)}, u32[]{:S(2)}) collective-permute-start(bf16[2,320,256]{2,1,0:T(8,128)(2,1)S(1)} %pad_maximum_fusion.1), channel_id=1, source_target_pairs={{1,5},{3,7},{5,1},{7,3},{9,13},{11,15},{13,9},{15,11},{16,20},{18,... | collective-permute-start | bytes 983048 | tf_op jit(solution)/shard_map/ppermute | solution.py:44
  28.4 28.9 %collective-permute-start.8 = (f32[320,512]{1,0:T(8,128)}, f32[320,512]{1,0:T(8,128)S(1)}, u32[]{:S(2)}, u32[]{:S(2)}) collective-permute-start(f32[320,512]{1,0:T(8,128)} %bitcast.21), channel_id=1, source_target_pairs={{256,0},{257,1},{258,2},{259,3},{260,4},{261,5},{262,6},{263,7},{2... | collective-permute-start | bytes 1966088 | tf_op jit(solution)/shard_map/ppermute | solution.py:44
  29.7 29.0 %collective-permute-start.9 = (f32[320,512]{1,0:T(8,128)}, f32[320,512]{1,0:T(8,128)S(1)}, u32[]{:S(2)}, u32[]{:S(2)}) collective-permute-start(f32[320,512]{1,0:T(8,128)} %bitcast.23), channel_id=1, source_target_pairs={{256,0},{257,1},{258,2},{259,3},{260,4},{261,5},{262,6},{263,7},{2... | collective-permute-start | bytes 1966088 | tf_op jit(solution)/shard_map/ppermute | solution.py:44
  31.1 52.4 %collective-permute-start.7 = (bf16[4,320,256]{2,1,0:T(8,128)(2,1)S(1)}, bf16[4,320,256]{2,1,0:T(8,128)(2,1)S(1)}, u32[]{:S(2)}, u32[]{:S(2)}) collective-permute-start(bf16[4,320,256]{2,1,0:T(8,128)(2,1)S(1)} %pad_maximum_fusion.refs_0_), channel_id=1, source_target_pairs={{1,2},{3,0},{5,6},{7,4},{9,10},{11,8},{13,14},{15,12},{16,17},{18,... | collective-permute-start | bytes 1966088 | tf_op jit(solution)/shard_map/ppermute | solution.py:44
  32.4 51.9 %collective-permute-start.6 = (bf16[4,320,256]{2,1,0:T(8,128)(2,1)S(1)}, bf16[4,320,256]{2,1,0:T(8,128)(2,1)S(1)}, u32[]{:S(2)}, u32[]{:S(2)}) collective-permute-start(bf16[4,320,256]{2,1,0:T(8,128)(2,1)S(1)} %pad_maximum_fusion.refs_0_), channel_id=1, source_target_pairs={{1,3},{3,1},{5,7},{7,5},{9,11},{11,9},{13,15},{15,13},{16,18},{18,... | collective-permute-start | bytes 1966088 | tf_op jit(solution)/shard_map/ppermute | solution.py:44
  33.1 53.2 %collective-permute-start.5 = (bf16[4,320,256]{2,1,0:T(8,128)(2,1)S(1)}, bf16[4,320,256]{2,1,0:T(8,128)(2,1)S(1)}, u32[]{:S(2)}, u32[]{:S(2)}) collective-permute-start(bf16[4,320,256]{2,1,0:T(8,128)(2,1)S(1)} %pad_maximum_fusion.refs_0_), channel_id=1, source_target_pairs={{1,0},{3,2},{5,4},{7,6},{9,8},{11,10},{13,12},{15,14},{16,19},{18,... | collective-permute-start | bytes 1966088 | tf_op jit(solution)/shard_map/ppermute | solution.py:44
  34.4 0.8 copy-start.4
  58.7 0.8 copy-start.1
  83.4 0.9 copy-start.9
  84.3 0.8 copy-start.11
  86.3 0.8 copy-start.13
  87.1 1.1 copy-start.2
  88.2 1.1 copy-start.5
  89.3 1.6 %copy-start.6 = (bf16[2176,512]{1,0:T(8,128)(2,1)S(1)}, bf16[2176,512]{1,0:T(8,128)(2,1)}, u32[]{:S(2)}) copy-start(bf16[2176,512]{1,0:T(8,128)(2,1)} %all-gather.3.cloned.1.call-done) | copy-start | bytes 6684676
  90.9 1.1 copy-start.10
  92.0 1.1 copy-start.12
  93.1 1.1 copy-start.14
  94.2 6.8 %copy-start.3 = (f32[320,512]{1,0:T(8,128)S(1)}, f32[320,512]{1,0:T(8,128)}, u32[]{:S(2)}) copy-start(f32[320,512]{1,0:T(8,128)} %copy-done.1) | copy-start | bytes 1966084
  94.2 6.8 %copy-start.7 = (f32[1,512,320]{1,2,0:T(8,128)S(1)}, f32[1,512,320]{1,2,0:T(8,128)}, u32[]{:S(2)}) copy-start(f32[1,512,320]{1,2,0:T(8,128)} %param.16) | copy-start | bytes 1966084
  94.2 6.8 %copy-start.8 = (f32[1,512,320]{1,2,0:T(8,128)S(1)}, f32[1,512,320]{1,2,0:T(8,128)}, u32[]{:S(2)}) copy-start(f32[1,512,320]{1,2,0:T(8,128)} %param.17) | copy-start | bytes 1966084
  94.2 6.8 %copy-start.15 = (bf16[512,320]{0,1:T(8,128)(2,1)S(1)}, bf16[512,320]{0,1:T(8,128)(2,1)}, u32[]{:S(2)}) copy-start(bf16[512,320]{0,1:T(8,128)(2,1)} %param.15) | copy-start | bytes 983044
  96.7 4.4 %collective-permute-start.10 = (f32[448,512]{1,0:T(8,128)S(1)}, f32[448,512]{1,0:T(8,128)S(1)}, u32[]{:S(2)}, u32[]{:S(2)}) collective-permute-start(f32[448,512]{1,0:T(8,128)S(1)} %gradient.1.mine_ref), channel_id=1, source_target_pairs={{0,256},{1,257},{2,258},{3,259},{4,260},{5,261},{6,262},{7,263},{8... | collective-permute-start | bytes 2752520 | tf_op jit(solution)/shard_map/ppermute | solution.py:44
  119.7 10.6 %collective-permute-start.11 = (bf16[8,320]{1,0:T(8,128)(2,1)S(1)}, bf16[8,320]{1,0:T(8,128)(2,1)S(1)}, u32[]{:S(2)}, u32[]{:S(2)}) collective-permute-start(bf16[8,320]{1,0:T(8,128)(2,1)S(1)} %reduce_sum.9), channel_id=1, source_target_pairs={{0,0},{1,16},{2,32},{3,48},{4,64},{5,80},{6,96},{7,112},{8,128},{9... | collective-permute-start | bytes 15368 | tf_op jit(solution)/shard_map/ppermute | solution.py:44
Sparse Core Ops, SparseCore 0:
  26.1 47.0 all-gather.2

commit v4 on v3

--- a/solution.py
+++ b/solution.py
@@ -28,6 +28,7 @@
 SHAPE = (2, 8, 2, 4, 4)
 DP, TENSOR = ("y", "z_hi"), ("z_lo", "x")
 TOK = 256
+HALF = 128
 FEAT = 512
 COLS = 320
 ROWS = 8
@@ -44,29 +45,28 @@
     return lax.ppermute(value, AXES, pairs)
 
 
-def keeper(zh, x):
-    return int((x & 1) == zh)
-
-
 def to_partner(g, y, zh, zl, x):
-    return (0, y, 1 - zh, zl, x) if g == 1 else None
+    return (g, y, 1 - zh, zl, x)
+
+
+def along_y(step):
+    return lambda g, y, zh, zl, x: (g, (y + step) % 8, zh, zl, x)
 
 
 def transposed(g, y, zh, zl, x):
     return (g, zl * 2 + (x >> 1), x & 1, y >> 1, (y & 1) * 2 + zh)
 
 
-def cot_transposed(g, *place):
-    _, y, zh, zl, x = transposed(g, *place)
-    return (keeper(zh, x), y, zh, zl, x) if g == 1 else None
+def cot_transposed(core):
+    return lambda g, *place: (core, *transposed(g, *place)[1:]) if g == 1 else None
 
 
 def along_zl(flip):
-    return lambda g, y, zh, zl, x: (g, y, zh, zl ^ flip, x) if g == keeper(zh, x) else None
+    return lambda g, y, zh, zl, x: (g, y, zh, zl ^ flip, x)
 
 
 def along_x(step):
-    return lambda g, y, zh, zl, x: (g, y, zh, zl, (x + step) % 4) if g == keeper(zh, x) else None
+    return lambda g, y, zh, zl, x: (g, y, zh, zl, (x + step) % 4)
 
 
 def other_core(g, y, zh, zl, x):
@@ -77,18 +77,22 @@
     return (0, y, zh, zl, x) if g == 1 else None
 
 
+HOPS = (0, 1, 2, 3, 4, -1, -2, -3)
 FLIPS = (0, 3, 1, 2)
 
 
 def device_table():
-    table = np.zeros((512, 32), np.int32)
+    table = np.zeros((512, 64), np.int32)
     for flat, (g, y, zh, zl, x) in enumerate(np.ndindex(*SHAPE)):
-        token_zh = zh if g == 1 else 1 - zh
-        table[flat, 0] = g
-        table[flat, 1] = token_zh
-        for n in range(8):
-            table[flat, 8 + n] = (2 * (n & 1) + token_zh - x) % 4
-            table[flat, 16 + n] = FLIPS.index(zl ^ (n >> 1))
+        start = (zl * 4 + x) * COLS
+        table[flat, :3] = g, start // 128, start % 128
+        for n, hop in enumerate(HOPS):
+            for other in range(2):
+                block_y, block_zh = (y - hop) % 8, zh ^ other
+                at = n * 2 + other
+                table[flat, 16 + at] = block_y * 2 + block_zh
+                table[flat, 32 + at] = (2 * (block_y & 1) + block_zh - x) % 4
+                table[flat, 48 + at] = FLIPS.index(zl ^ (block_y >> 1))
     return table
 
 
@@ -172,86 +176,134 @@
     )(head, lengths, ids, queries, cache_keys, cache_values, new_keys, new_values)
 
 
-def base_kernel(table_ref, act_ref, act_got, rows_ref, rows_got, out_ref):
+VMEM = pl.BlockSpec(memory_space=pltpu.VMEM)
+SMEM = pl.BlockSpec(memory_space=pltpu.SMEM)
+HBM = pl.BlockSpec(memory_space=pl.ANY)
+
+
+def half_kernel(table_ref, act_ref, act_got, rows_ref, out_ref):
     @pl.when(table_ref[0] == 1)
     def _():
-        out_ref[:TOK, :] = act_ref[...]
-        out_ref[TOK:, :] = rows_ref[...]
+        out_ref[:HALF, :] = act_ref[:HALF, :]
 
     @pl.when(table_ref[0] == 0)
     def _():
-        out_ref[:TOK, :] = act_got[...]
-        out_ref[TOK:, :] = rows_got[...]
-
-
-def base_of(table, *parts):
-    vmem = pl.BlockSpec(memory_space=pltpu.VMEM)
+        out_ref[:HALF, :] = act_got[HALF:, :]
+
+    out_ref[HALF:, :] = rows_ref[...]
+
+
+def half_of(table, *parts):
+    return pl.pallas_call(
+        half_kernel,
+        out_shape=jax.ShapeDtypeStruct((HALF + PAD, FEAT), bf16),
+        in_specs=[SMEM] + [VMEM] * 3,
+        out_specs=VMEM,
+        name="half",
+    )(table, *parts)
+
+
+def base_kernel(mine_ref, got_ref, out_ref):
+    out_ref[:HALF, :] = mine_ref[:HALF, :]
+    out_ref[HALF:TOK, :] = got_ref[:HALF, :]
+    rows = [ref[HALF:, :].astype(f32)[:ROWS] for ref in (mine_ref, got_ref)]
+    out_ref[TOK:, :] = jnp.concatenate(rows, axis=0).astype(bf16)
+
+
+def base_of(*parts):
     return pl.pallas_call(
         base_kernel,
         out_shape=jax.ShapeDtypeStruct((TOK + PAD, FEAT), bf16),
-        in_specs=[pl.BlockSpec(memory_space=pltpu.SMEM)] + [vmem] * 4,
-        out_specs=vmem,
+        in_specs=[VMEM] * 2,
+        out_specs=VMEM,
         name="base",
-    )(table, *parts)
-
-
-def gradient_kernel(table_ref, chunks_ref, *refs):
-    blocks, (out_ref, chunk_rows, block_rows, row_tiles, sems) = refs[:4], refs[-5:]
+    )(*parts)
+
+
+def cut_kernel(table_ref, cot_ref, one_ref, two_ref, window, turned, sem):
+    start = pl.multiple_of(table_ref[1] * 128, 128)
+    copy = pltpu.make_async_copy(cot_ref.at[:, pl.ds(start, 384)], window, sem)
+    copy.start()
+    copy.wait()
+    turned[...] = window[...].astype(f32).T
+    place = pl.ds(pl.multiple_of(table_ref[2], 64), COLS)
+    one_ref[...] = turned[place, :HALF].astype(bf16)
+    two_ref[...] = turned[place, HALF:].astype(bf16)
+
+
+def cut_of(table, cot):
+    shape = jax.ShapeDtypeStruct((COLS, HALF), bf16)
+    return pl.pallas_call(
+        cut_kernel,
+        out_shape=(shape, shape),
+        in_specs=[SMEM, HBM],
+        out_specs=(VMEM, VMEM),
+        scratch_shapes=[
+            pltpu.VMEM((TOK, 384), bf16),
+            pltpu.VMEM((384, TOK), f32),
+            pltpu.SemaphoreType.DMA(()),
+        ],
+        name="cut",
+    )(table, cot)
+
+
+def gradient_kernel(table_ref, *refs):
+    chunks, blocks, (out_ref, rows_ref) = refs[:8], refs[8:12], refs[-7:-5]
+    chunk_rows, block_tiles, block_rows, row_tiles, sems = refs[-5:]
+    copies = [
+        pltpu.make_async_copy(blocks[b], block_tiles.at[b], sems.at[b]) for b in range(4)
+    ]
     act_copies = [
         pltpu.make_async_copy(
-            chunks_ref.at[n, :TOK], chunk_rows.at[pl.ds(n * TOK, TOK)], sems.at[n]
+            chunks[n].at[:TOK], chunk_rows.at[pl.ds(n * TOK, TOK)], sems.at[4 + n]
         )
         for n in range(8)
     ]
     row_copies = [
-        pltpu.make_async_copy(chunks_ref.at[n, TOK:], row_tiles.at[n], sems.at[16 + n])
+        pltpu.make_async_copy(chunks[n].at[TOK:], row_tiles.at[n], sems.at[12 + n])
         for n in range(8)
     ]
-    for n in range(8):
-        act_copies[n].start()
-        for b in range(4):
-
-            @pl.when(table_ref[8 + n] == b)
-            def _():
-                pltpu.make_async_copy(
-                    blocks[b].at[table_ref[16 + n]],
-                    block_rows.at[:, pl.ds(n * TOK, TOK)],
-                    sems.at[8 + n],
-                ).start()
-
-        row_copies[n].start()
-    out_ref[COLS:, :] = jnp.zeros((16 * ROWS, FEAT), f32)
+    for copy in copies + act_copies + row_copies:
+        copy.start()
+    for copy in copies:
+        copy.wait()
+    for at in range(16):
+        block_rows[:, at * HALF : (at + 1) * HALF] = block_tiles[
+            table_ref[32 + at], table_ref[48 + at]
+        ]
     for half in range(2):
         for n in range(4 * half, 4 * half + 4):
             act_copies[n].wait()
-            pltpu.make_async_copy(
-                blocks[0].at[0], block_rows.at[:, pl.ds(n * TOK, TOK)], sems.at[8 + n]
-            ).wait()
         span = pl.ds(half * 4 * TOK, 4 * TOK)
         part = jnp.dot(block_rows[:, span], chunk_rows[span, :], preferred_element_type=f32)
         if half == 0:
-            out_ref[:COLS, :] = part
+            out_ref[...] = part
         else:
-            out_ref[:COLS, :] += part
+            out_ref[...] += part
     for n in range(8):
         row_copies[n].wait()
-        place = pl.multiple_of(COLS + (2 * n + table_ref[1]) * ROWS, ROWS)
-        out_ref[pl.ds(place, ROWS), :] = row_tiles[n].astype(f32)[:ROWS]
+        rows = row_tiles[n].astype(f32)
+        for other in range(2):
+            place = pl.multiple_of(table_ref[16 + 2 * n + other] * ROWS, ROWS)
+            rows_ref[pl.ds(place, ROWS), :] = rows[other * ROWS : (other + 1) * ROWS]
 
 
 def gradient(table, chunks, blocks, others):
-    hbm = pl.BlockSpec(memory_space=pl.ANY)
-    operands = (chunks, *blocks, *others)
+    operands = (*chunks, *blocks, *others)
     return pl.pallas_call(
         gradient_kernel,
-        out_shape=jax.ShapeDtypeStruct((COLS + 16 * ROWS, FEAT), f32),
-        in_specs=[pl.BlockSpec(memory_space=pltpu.SMEM)] + [hbm] * len(operands),
-        out_specs=pl.BlockSpec(memory_space=pltpu.VMEM),
+        out_shape=(
+            jax.ShapeDtypeStruct((COLS, FEAT), f32),
+            jax.ShapeDtypeStruct((16 * ROWS, FEAT), f32),
+        ),
+        in_specs=[SMEM] + [HBM] * len(operands),
+        out_specs=(VMEM, VMEM),
         scratch_shapes=[
             pltpu.VMEM((8 * TOK, FEAT), bf16),
+            pltpu.VMEM((4, 4, COLS, HALF), bf16),
             pltpu.VMEM((COLS, 8 * TOK), bf16),
             pltpu.VMEM((8, PAD, FEAT), bf16),
-            pltpu.SemaphoreType.DMA((24,)),
+            pltpu.SemaphoreType.DMA((20,)),
         ],
         compiler_params=pltpu.CompilerParams(vmem_limit_bytes=32 * 2**20),
         cost_estimate=pl.CostEstimate(
@@ -262,10 +314,10 @@
 
 
 def step_kernel(
-    table_ref, mine_ref, got_ref, one_ref, one_got, two_ref, two_got, weight_ref, update_ref, out_ref
+    table_ref, mine_ref, got_ref, rows_ref, one_ref, one_got, two_ref, two_got, weight_ref, update_ref, out_ref
 ):
     learner = table_ref[0] == 1
-    grad = mine_ref[:COLS, :] + got_ref[:COLS, :]
+    grad = mine_ref[...] + got_ref[...]
     moment_one = jnp.where(learner, one_ref[...], one_got[...])
     moment_two = jnp.where(learner, two_ref[...], two_got[...])
     first_moment = beta_one * moment_one + (1.0 - beta_one) * grad
@@ -278,24 +330,23 @@
     renewed = (
         widened - learning_rate * (update.astype(f32) + weight_decay * widened)
     ).astype(bf16)
-    rows = (mine_ref[COLS:, :] + got_ref[COLS:, :]).astype(bf16)
+    rows = rows_ref[...].astype(bf16)
     part = lax.dot_general(rows, renewed, (((1,), (1,)), ((), ())), preferred_element_type=f32)
     out_ref[...] = part.reshape(16, ROWS, COLS)
 
 
-def step(table, mine, got, one, one_got, two, two_got, weight):
-    vmem = pl.BlockSpec(memory_space=pltpu.VMEM)
+def step(table, mine, got, rows, one, one_got, two, two_got, weight):
     return pl.pallas_call(
         step_kernel,
         out_shape=(
             jax.ShapeDtypeStruct((COLS, FEAT), bf16),
             jax.ShapeDtypeStruct((16, ROWS, COLS), f32),
         ),
-        in_specs=[pl.BlockSpec(memory_space=pltpu.SMEM)] + [vmem] * 7,
-        out_specs=(vmem, vmem),
+        in_specs=[SMEM] + [VMEM] * 8,
+        out_specs=(VMEM, VMEM),
         compiler_params=pltpu.CompilerParams(vmem_limit_bytes=32 * 2**20),
         name="step",
-    )(table, mine, got, one, one_got, two, two_got, weight)
+    )(table, mine, got, rows, one, one_got, two, two_got, weight)
 
 
 def local(
@@ -316,7 +367,7 @@
     table = lax.dynamic_slice_in_dim(jnp.asarray(device_table()), flat, 1, 0)[0]
 
     act = activations[0]
-    act_got = permute(act, to_partner)
+    act_got = permute(act, to_rollout)
     rows = attend(
         (q >> 1).reshape(1),
         queries,
@@ -327,13 +378,21 @@
         lengths,
         token_ids.T,
     )
-    rows_got = permute(rows, to_partner)
-    base = base_of(table, act, act_got, rows, rows_got)
-    chunks = lax.all_gather(base, "y", axis=0)
-
-    cut = lax.dynamic_slice_in_dim(cotangent[0], q * COLS, COLS, 1).T
-    own = permute(cut, cot_transposed)
+    half = half_of(table, act, act_got, rows)
+    base = base_of(half, permute(half, to_partner))
+
+    cut_one, cut_two = cut_of(table, cotangent[0])
+    own = permute(cut_one, cot_transposed(1)), permute(cut_two, cot_transposed(0))
+
+    up, down = [base], [base]
+    up.append(permute(base, along_y(1)))
+    down.append(permute(base, along_y(-1)))
+
+    own_one, own_two, _ = lax.optimization_barrier((*own, base))
+    own = jnp.where(table[0] == 1, own_one, own_two)
     two_blocks = jnp.stack([own, permute(own, along_zl(3))])
+    up.append(permute(up[-1], along_y(1)))
+    down.append(permute(down[-1], along_y(-1)))
     four = jnp.concatenate([two_blocks, permute(two_blocks, along_zl(1))], axis=0)
     blocks = (
         four,
@@ -341,14 +400,19 @@
         permute(four, along_x(2)),
         permute(four, along_x(1)),
     )
+    up.append(permute(up[-1], along_y(1)))
+    down.append(permute(down[-1], along_y(-1)))
+    up.append(permute(up[-1], along_y(1)))
+    chunks = up + down[1:]
 
     one, two = moment_one[0].T, moment_two[0].T
-    one_got = permute(one, to_rollout)
-    two_got = permute(two, to_rollout)
-
-    mine = gradient(table, chunks, blocks, (one_got, two_got))
+    one_tied, two_tied, _ = lax.optimization_barrier((one, two, base))
+    one_got = permute(one_tied, to_rollout)
+    two_got = permute(two_tied, to_rollout)
+
+    mine, all_rows = gradient(table, chunks, blocks, (one_got, two_got))
     got = permute(mine, other_core)
-    update, partial = step(table, mine, got, one, one_got, two, two_got, weight.T)
+    update, partial = step(table, mine, got, all_rows, one, one_got, two, two_got, weight.T)
 
     shares = lax.all_to_all(partial, TENSOR, split_axis=0, concat_axis=0, tiled=True)
     summed = jnp.sum(shares, axis=0).astype(bf16)

time: 153 us -> 147 us (0.961)
  the two profiles are of different devices: /device:TPU:24 before, /device:TPU:2 now
where the time goes in v4:
time: 147 us
  starting transfers between devices  74.1 us (50%)
  blocking collectives  29.2 us (20%)
  waiting for transfers between devices  24.4 us (17%)
  Pallas kernels  13.3 us (9%)
  local copies, waits for them, and re-layouts  4.46 us (3%)
    ppermute x20, starting transfers between devices, permute(): return lax.ppermute(value, AXES, pairs)  74.1 us
    ppermute x20, waiting for transfers between devices, permute(): return lax.ppermute(value, AXES, pairs)  24.4 us
    all_to_all x1, blocking collectives, local(): lax.all_to_all(partial, TENSOR, split_axis=0, concat_axis=0, tiled=True)  15.6 us
    all_to_all x1, blocking collectives, local(): lax.all_to_all(spread, TENSOR, split_axis=0, concat_axis=0, tiled=True)  13.6 us
  transfers between devices with their start and end apart: 20, of which 9 were waited for; matrix products, arithmetic and copies ran while one was open for 1% of the time, Pallas kernels for 5%

profile of v4, /device:TPU:2, one launch (start us, length us, event | category | flops | bytes accessed | tf_op | source)
XLA Modules:
  0.0 146.6 jit_solution(2891946620289723337)
XLA Ops:
  0.6 1.3 collective-permute-start
  1.9 2.8 %attend.1.rows_ref = bf16[16,512]{1,0:T(8,128)(2,1)} custom-call(s32[1]{0:T(128)} %bitcast.2.head_ref, s32[2]{0:T(128)} %lengths_ref.1, s32[2,4]{1,0:T(2,128)} %bitcast.32, bf16[4,2,512]{2,1,0:T(2,128)(2,1)} %q_ref.1, bf16[2,2048,128]{2,1,0:T(8,128)(2,1)} %k_ref.1, bf16[2,2048,128]{2,1,0:T(8,128)(2,1)} %v_ref.1, bf16[4,2,1024]{2,1,0:T(2,128)(2,1)} %nk_ref.1, ...), custom_call_target="tpu_custom_call" | custom-call | tf_op jit(solution)/shard_map/attend/pallas_call | solution.py:161
  4.7 0.0 copy-start.1
  4.7 0.0 copy-start.2
  4.7 1.3 constant_dynamic-slice_fusion
  6.0 0.0 copy-start.4
  6.1 0.0 collective-permute-done.act_got
  6.1 0.0 copy-start.5
  6.1 0.7 copy-done.5
  6.8 1.7 %half.1.mine_ref = bf16[144,512]{1,0:T(8,128)(2,1)} custom-call(s32[64]{0:T(128)} %get-tuple-element.23.table_ref, bf16[256,512]{1,0:T(8,128)(2,1)} %bitcast.31, bf16[256,512]{1,0:T(8,128)(2,1)} %copy-done.5, bf16[16,512]{1,0:T(8,128)(2,1)} %attend.1.rows_ref), custom_call_target="tpu_custom_call" | custom-call | tf_op jit(solution)/shard_map/half/pallas_call | solution.py:197
  8.5 10.9 %collective-permute-start.1 = (bf16[144,512]{1,0:T(8,128)(2,1)}, bf16[144,512]{1,0:T(8,128)(2,1)S(1)}, u32[]{:S(2)}, u32[]{:S(2)}) collective-permute-start(bf16[144,512]{1,0:T(8,128)(2,1)} %half.1.mine_ref), channel_id=1, source_target_pairs={{0,16},{1,17},{2,18},{3,19},{4,20},{5,21},{6,22},{7,23},{8,24},{9,... | collective-permute-start | bytes 442376 | tf_op jit(solution)/shard_map/ppermute | solution.py:45
  19.4 2.4 %cut.1 = (bf16[320,128]{1,0:T(8,128)(2,1)}, bf16[320,128]{1,0:T(8,128)(2,1)}) custom-call(s32[64]{0:T(128)} %get-tuple-element.23.table_ref, bf16[256,5120]{1,0:T(8,128)(2,1)} %bitcast.24), custom_call_target="tpu_custom_call" | custom-call | tf_op jit(solution)/shard_map/cut/pallas_call | solution.py:236
  21.8 0.7 collective-permute-start.9
  22.5 1.3 collective-permute-start.10
  23.8 0.2 collective-permute-done.1.got_ref
  24.0 0.0 copy-start.6
  24.0 0.7 copy-done.6
  24.7 1.7 %base.1.refs_0_ = bf16[272,512]{1,0:T(8,128)(2,1)} custom-call(bf16[144,512]{1,0:T(8,128)(2,1)} %half.1.mine_ref, bf16[144,512]{1,0:T(8,128)(2,1)} %copy-done.6), custom_call_target="tpu_custom_call" | custom-call | tf_op jit(solution)/shard_map/base/pallas_call | solution.py:214
  26.4 5.4 %collective-permute-start.6 = (bf16[272,512]{1,0:T(8,128)(2,1)}, bf16[272,512]{1,0:T(8,128)(2,1)S(1)}, u32[]{:S(2)}, u32[]{:S(2)}) collective-permute-start(bf16[272,512]{1,0:T(8,128)(2,1)} %base.1.refs_0_), channel_id=1, source_target_pairs={{0,224},{1,225},{2,226},{3,227},{4,228},{5,229},{6,230},{7,231},{8... | collective-permute-start | bytes 835592 | tf_op jit(solution)/shard_map/ppermute | solution.py:45
  31.7 0.0 collective-permute-done.9
  31.8 2.9 %collective-permute-done.10 = bf16[320,128]{1,0:T(8,128)(2,1)S(1)} collective-permute-done((bf16[320,128]{1,0:T(8,128)(2,1)}, bf16[320,128]{1,0:T(8,128)(2,1)S(1)}, u32[]{:S(2)}, u32[]{:S(2)}) %collective-permute-start.10) | collective-permute-done | bytes 81952 | tf_op jit(solution)/shard_map/ppermute | solution.py:45
  34.6 11.5 %collective-permute-start.11 = (bf16[320,128]{1,0:T(8,128)(2,1)S(1)}, bf16[320,128]{1,0:T(8,128)(2,1)S(1)}, u32[]{:S(2)}, u32[]{:S(2)}) collective-permute-start(bf16[320,128]{1,0:T(8,128)(2,1)S(1)} %broadcast_select_fusion), channel_id=1, source_target_pairs={{0,12},{1,13},{2,14},{3,15},{4,8},{5,9},{6,10},{7,11},{8,4},{9,5},... | collective-permute-start | bytes 245768 | tf_op jit(solution)/shard_map/ppermute | solution.py:45
  46.2 1.9 %collective-permute-start.2 = (bf16[272,512]{1,0:T(8,128)(2,1)}, bf16[272,512]{1,0:T(8,128)(2,1)S(1)}, u32[]{:S(2)}, u32[]{:S(2)}) collective-permute-start(bf16[272,512]{1,0:T(8,128)(2,1)} %base.1.refs_0_), channel_id=1, source_target_pairs={{0,32},{1,33},{2,34},{3,35},{4,36},{5,37},{6,38},{7,39},{8,40},{9,... | collective-permute-start | bytes 835592 | tf_op jit(solution)/shard_map/ppermute | solution.py:45
  48.1 0.9 collective-permute-done.11
  49.0 2.4 %collective-permute-start.12 = (bf16[2,320,128]{2,1,0:T(8,128)(2,1)S(1)}, bf16[2,320,128]{2,1,0:T(8,128)(2,1)S(1)}, u32[]{:S(2)}, u32[]{:S(2)}) collective-permute-start(bf16[2,320,128]{2,1,0:T(8,128)(2,1)S(1)} %pad_maximum_fusion.1), channel_id=1, source_target_pairs={{0,4},{1,5},{2,6},{3,7},{4,0},{5,1},{6,2},{7,3},{8,12},{9,13},{10,... | collective-permute-start | bytes 491528 | tf_op jit(solution)/shard_map/ppermute | solution.py:45
  51.4 0.0 collective-permute-done.6.refs_5_
  51.4 7.0 %collective-permute-start.7 = (bf16[272,512]{1,0:T(8,128)(2,1)S(1)}, bf16[272,512]{1,0:T(8,128)(2,1)S(1)}, u32[]{:S(2)}, u32[]{:S(2)}) collective-permute-start(bf16[272,512]{1,0:T(8,128)(2,1)S(1)} %collective-permute-done.6.refs_5_), channel_id=1, source_target_pairs={{0,224},{1,225},{2,226},{3,227},{4,228},{5,229},{6,230},{7,231},{8... | collective-permute-start | bytes 835592 | tf_op jit(solution)/shard_map/ppermute | solution.py:45
  58.5 0.0 collective-permute-done.2.refs_1_
  58.5 1.9 %collective-permute-start.3 = (bf16[272,512]{1,0:T(8,128)(2,1)S(1)}, bf16[272,512]{1,0:T(8,128)(2,1)S(1)}, u32[]{:S(2)}, u32[]{:S(2)}) collective-permute-start(bf16[272,512]{1,0:T(8,128)(2,1)S(1)} %collective-permute-done.2.refs_1_), channel_id=1, source_target_pairs={{0,32},{1,33},{2,34},{3,35},{4,36},{5,37},{6,38},{7,39},{8,40},{9,... | collective-permute-start | bytes 835592 | tf_op jit(solution)/shard_map/ppermute | solution.py:45
  60.4 0.0 copy-start.3
  60.5 0.0 collective-permute-done.12
  60.5 2.1 %collective-permute-start.15 = (bf16[4,320,128]{2,1,0:T(8,128)(2,1)S(1)}, bf16[4,320,128]{2,1,0:T(8,128)(2,1)S(1)}, u32[]{:S(2)}, u32[]{:S(2)}) collective-permute-start(bf16[4,320,128]{2,1,0:T(8,128)(2,1)S(1)} %pad_maximum_fusion.refs_8_), channel_id=1, source_target_pairs={{0,1},{1,2},{2,3},{3,0},{4,5},{5,6},{6,7},{7,4},{8,9},{9,10},{10,1... | collective-permute-start | bytes 983048 | tf_op jit(solution)/shard_map/ppermute | solution.py:45
  62.6 0.0 copy-done.1
  62.6 1.3 collective-permute-start.16
  63.9 0.0 copy-done.2
  63.9 1.3 collective-permute-start.17
  65.2 0.0 collective-permute-done.7.refs_6_
  65.3 6.0 %collective-permute-start.14 = (bf16[4,320,128]{2,1,0:T(8,128)(2,1)S(1)}, bf16[4,320,128]{2,1,0:T(8,128)(2,1)S(1)}, u32[]{:S(2)}, u32[]{:S(2)}) collective-permute-start(bf16[4,320,128]{2,1,0:T(8,128)(2,1)S(1)} %pad_maximum_fusion.refs_8_), channel_id=1, source_target_pairs={{0,2},{1,3},{2,0},{3,1},{4,6},{5,7},{6,4},{7,5},{8,10},{9,11},{10,... | collective-permute-start | bytes 983048 | tf_op jit(solution)/shard_map/ppermute | solution.py:45
  71.2 0.0 collective-permute-done.3.refs_2_
  71.2 1.9 %collective-permute-start.4 = (bf16[272,512]{1,0:T(8,128)(2,1)S(1)}, bf16[272,512]{1,0:T(8,128)(2,1)S(1)}, u32[]{:S(2)}, u32[]{:S(2)}) collective-permute-start(bf16[272,512]{1,0:T(8,128)(2,1)S(1)} %collective-permute-done.3.refs_2_), channel_id=1, source_target_pairs={{0,32},{1,33},{2,34},{3,35},{4,36},{5,37},{6,38},{7,39},{8,40},{9,... | collective-permute-start | bytes 835592 | tf_op jit(solution)/shard_map/ppermute | solution.py:45
  73.2 0.0 collective-permute-done.15.refs_11_
  73.2 3.0 %collective-permute-start.13 = (bf16[4,320,128]{2,1,0:T(8,128)(2,1)S(1)}, bf16[4,320,128]{2,1,0:T(8,128)(2,1)S(1)}, u32[]{:S(2)}, u32[]{:S(2)}) collective-permute-start(bf16[4,320,128]{2,1,0:T(8,128)(2,1)S(1)} %pad_maximum_fusion.refs_8_), channel_id=1, source_target_pairs={{0,3},{1,0},{2,1},{3,2},{4,7},{5,4},{6,5},{7,6},{8,11},{9,8},{10,9... | collective-permute-start | bytes 983048 | tf_op jit(solution)/shard_map/ppermute | solution.py:45
  76.1 3.3 %collective-permute-done.14.refs_10_ = bf16[4,320,128]{2,1,0:T(8,128)(2,1)S(1)} collective-permute-done((bf16[4,320,128]{2,1,0:T(8,128)(2,1)S(1)}, bf16[4,320,128]{2,1,0:T(8,128)(2,1)S(1)}, u32[]{:S(2)}, u32[]{:S(2)}) %collective-permute-start.14) | collective-permute-done | bytes 327712 | tf_op jit(solution)/shard_map/ppermute | solution.py:45
  79.4 5.1 %collective-permute-start.8 = (bf16[272,512]{1,0:T(8,128)(2,1)S(1)}, bf16[272,512]{1,0:T(8,128)(2,1)S(1)}, u32[]{:S(2)}, u32[]{:S(2)}) collective-permute-start(bf16[272,512]{1,0:T(8,128)(2,1)S(1)} %collective-permute-done.7.refs_6_), channel_id=1, source_target_pairs={{0,224},{1,225},{2,226},{3,227},{4,228},{5,229},{6,230},{7,231},{8... | collective-permute-start | bytes 835592 | tf_op jit(solution)/shard_map/ppermute | solution.py:45
  84.5 0.0 collective-permute-done.4.refs_3_
  84.5 1.9 %collective-permute-start.5 = (bf16[272,512]{1,0:T(8,128)(2,1)S(1)}, bf16[272,512]{1,0:T(8,128)(2,1)S(1)}, u32[]{:S(2)}, u32[]{:S(2)}) collective-permute-start(bf16[272,512]{1,0:T(8,128)(2,1)S(1)} %collective-permute-done.4.refs_3_), channel_id=1, source_target_pairs={{0,32},{1,33},{2,34},{3,35},{4,36},{5,37},{6,38},{7,39},{8,40},{9,... | collective-permute-start | bytes 835592 | tf_op jit(solution)/shard_map/ppermute | solution.py:45
  86.5 0.3 collective-permute-done.13.refs_9_
  86.8 0.0 collective-permute-done.16.refs_12_.one_got
  86.8 0.0 collective-permute-done.17.refs_13_.two_got
  86.8 4.4 %collective-permute-done.8.refs_7_ = bf16[272,512]{1,0:T(8,128)(2,1)S(1)} collective-permute-done((bf16[272,512]{1,0:T(8,128)(2,1)S(1)}, bf16[272,512]{1,0:T(8,128)(2,1)S(1)}, u32[]{:S(2)}, u32[]{:S(2)}) %collective-permute-start.8) | collective-permute-done | bytes 278560 | tf_op jit(solution)/shard_map/ppermute | solution.py:45
  91.2 5.3 %collective-permute-done.5.refs_4_ = bf16[272,512]{1,0:T(8,128)(2,1)S(1)} collective-permute-done((bf16[272,512]{1,0:T(8,128)(2,1)S(1)}, bf16[272,512]{1,0:T(8,128)(2,1)S(1)}, u32[]{:S(2)}, u32[]{:S(2)}) %collective-permute-start.5) | collective-permute-done | bytes 278560 | tf_op jit(solution)/shard_map/ppermute | solution.py:45
  96.6 0.0 copy-done.4
  96.6 0.0 copy-start
  96.6 1.0 copy-done
  97.5 2.8 %gradient.1 = (f32[320,512]{1,0:T(8,128)S(1)}, f32[128,512]{1,0:T(8,128)S(1)}) custom-call(s32[64]{0:T(128)S(1)} %copy-done.4, bf16[272,512]{1,0:T(8,128)(2,1)S(1)} %copy-done, bf16[272,512]{1,0:T(8,128)(2,1)S(1)} %collective-permute-done.2.refs_1_, bf16[272,512]{1,0:T(8,128)(2,1)S(1)} %collective-permute-done.3.refs_2_, ...), custom_call_target="tpu_custom_call" | custom-call | flops 671088640 | bytes 6291456 | tf_op jit(solution)/shard_map/gradient/pallas_call | solution.py:293
  100.3 1.9 %collective-permute-start.18 = (f32[320,512]{1,0:T(8,128)S(1)}, f32[320,512]{1,0:T(8,128)S(1)}, u32[]{:S(2)}, u32[]{:S(2)}) collective-permute-start(f32[320,512]{1,0:T(8,128)S(1)} %get-tuple-element.18.mine_ref), channel_id=1, source_target_pairs={{0,256},{1,257},{2,258},{3,259},{4,260},{5,261},{6,262},{7,263},{8... | collective-permute-start | bytes 1966088 | tf_op jit(solution)/shard_map/ppermute | solution.py:45
  102.2 2.1 %collective-permute-done.18.got_ref = f32[320,512]{1,0:T(8,128)S(1)} collective-permute-done((f32[320,512]{1,0:T(8,128)S(1)}, f32[320,512]{1,0:T(8,128)S(1)}, u32[]{:S(2)}, u32[]{:S(2)}) %collective-permute-start.18) | collective-permute-done | bytes 655392 | tf_op jit(solution)/shard_map/ppermute | solution.py:45
  104.3 0.0 copy-done.3
  104.3 1.9 %step.1 = (bf16[320,512]{1,0:T(8,128)(2,1)}, f32[16,8,320]{2,1,0:T(8,128)S(1)}) custom-call(s32[64]{0:T(128)S(1)} %copy-done.4, f32[320,512]{1,0:T(8,128)S(1)} %get-tuple-element.18.mine_ref, f32[320,512]{1,0:T(8,128)S(1)} %collective-permute-done.18.got_ref, f32[128,512]{1,0:T(8,128)S(1)} %get-tuple-element.19.rows_ref, f32[320,512]{1,0:T(8,128)S(1)} %bitcast.20, ...), custom_call_target="tpu_custom_call" | custom-call | tf_op jit(solution)/shard_map/step/pallas_call | solution.py:339
  106.2 15.6 %all_to_all.10 = f32[16,8,320]{2,1,0:T(8,128)S(1)} all-to-all(f32[16,8,320]{2,1,0:T(8,128)S(1)} %get-tuple-element.21), channel_id=1, replica_groups=mesh['group'=2,'y'=8,'z_hi'=2,'z_lo'=4,'x'=4] {'z_lo','x'}, dimensions={0} | all-to-all | bytes 327680 | tf_op jit(solution)/shard_map/all_to_all | solution.py:417
  121.9 5.3 %collective-permute-start.19 = (bf16[8,320]{1,0:T(8,128)(2,1)S(1)}, bf16[8,320]{1,0:T(8,128)(2,1)S(1)}, u32[]{:S(2)}, u32[]{:S(2)}) collective-permute-start(bf16[8,320]{1,0:T(8,128)(2,1)S(1)} %reduce_sum.9), channel_id=1, source_target_pairs={{0,0},{1,16},{2,32},{3,48},{4,64},{5,80},{6,96},{7,112},{8,128},{9... | collective-permute-start | bytes 15368 | tf_op jit(solution)/shard_map/ppermute | solution.py:45
  127.1 5.1 %collective-permute-done.19 = bf16[8,320]{1,0:T(8,128)(2,1)S(1)} collective-permute-done((bf16[8,320]{1,0:T(8,128)(2,1)S(1)}, bf16[8,320]{1,0:T(8,128)(2,1)S(1)}, u32[]{:S(2)}, u32[]{:S(2)}) %collective-permute-start.19) | collective-permute-done | bytes 5152 | tf_op jit(solution)/shard_map/ppermute | solution.py:45
  132.2 13.6 %all_to_all.11 = bf16[16,8,320]{2,1,0:T(8,128)(2,1)S(1)} all-to-all(bf16[16,8,320]{2,1,0:T(8,128)(2,1)S(1)} %broadcast_in_dim.2), channel_id=1, replica_groups=mesh['group'=2,'y'=8,'z_hi'=2,'z_lo'=4,'x'=4] {'z_lo','x'}, dimensions={0} | all-to-all | bytes 163840 | tf_op jit(solution)/shard_map/all_to_all | solution.py:421
  145.8 0.8 reshape.16
  (6 shorter events, 0.1 us)
Async XLA Ops:
  0.6 5.4 %collective-permute-start = (bf16[256,512]{1,0:T(8,128)(2,1)}, bf16[256,512]{1,0:T(8,128)(2,1)S(1)}, u32[]{:S(2)}, u32[]{:S(2)}) collective-permute-start(bf16[256,512]{1,0:T(8,128)(2,1)} %bitcast.30), channel_id=1, source_target_pairs={{256,0},{257,1},{258,2},{259,3},{260,4},{261,5},{262,6},{263,7},{2... | collective-permute-start | bytes 786440 | tf_op jit(solution)/shard_map/ppermute | solution.py:45
  4.7 57.9 %copy-start.1 = (f32[1,512,320]{1,2,0:T(8,128)S(1)}, f32[1,512,320]{1,2,0:T(8,128)}, u32[]{:S(2)}) copy-start(f32[1,512,320]{1,2,0:T(8,128)} %param.16) | copy-start | bytes 1966084
  4.7 59.2 %copy-start.2 = (f32[1,512,320]{1,2,0:T(8,128)S(1)}, f32[1,512,320]{1,2,0:T(8,128)}, u32[]{:S(2)}) copy-start(f32[1,512,320]{1,2,0:T(8,128)} %param.17) | copy-start | bytes 1966084
  6.0 90.5 %copy-start.4 = (s32[64]{0:T(128)S(1)}, s32[64]{0:T(128)}, u32[]{:S(2)}) copy-start(s32[64]{0:T(128)} %get-tuple-element.23.table_ref) | copy-start | bytes 772
  6.1 0.7 copy-start.5
  8.5 15.5 %collective-permute-start.1 = (bf16[144,512]{1,0:T(8,128)(2,1)}, bf16[144,512]{1,0:T(8,128)(2,1)S(1)}, u32[]{:S(2)}, u32[]{:S(2)}) collective-permute-start(bf16[144,512]{1,0:T(8,128)(2,1)} %half.1.mine_ref), channel_id=1, source_target_pairs={{0,16},{1,17},{2,18},{3,19},{4,20},{5,21},{6,22},{7,23},{8,24},{9,... | collective-permute-start | bytes 442376 | tf_op jit(solution)/shard_map/ppermute | solution.py:45
  21.8 9.9 %collective-permute-start.9 = (bf16[320,128]{1,0:T(8,128)(2,1)}, bf16[320,128]{1,0:T(8,128)(2,1)S(1)}, u32[]{:S(2)}, u32[]{:S(2)}) collective-permute-start(bf16[320,128]{1,0:T(8,128)(2,1)} %get-tuple-element.12), channel_id=1, source_target_pairs={{256,256},{257,272},{258,288},{259,304},{260,320},{261,336},{262,3... | collective-permute-start | bytes 245768 | tf_op jit(solution)/shard_map/ppermute | solution.py:45
  22.5 12.1 %collective-permute-start.10 = (bf16[320,128]{1,0:T(8,128)(2,1)}, bf16[320,128]{1,0:T(8,128)(2,1)S(1)}, u32[]{:S(2)}, u32[]{:S(2)}) collective-permute-start(bf16[320,128]{1,0:T(8,128)(2,1)} %get-tuple-element.13), channel_id=1, source_target_pairs={{256,0},{257,16},{258,32},{259,48},{260,64},{261,80},{262,96},{263... | collective-permute-start | bytes 245768 | tf_op jit(solution)/shard_map/ppermute | solution.py:45
  24.0 0.7 copy-start.6
  26.4 25.1 %collective-permute-start.6 = (bf16[272,512]{1,0:T(8,128)(2,1)}, bf16[272,512]{1,0:T(8,128)(2,1)S(1)}, u32[]{:S(2)}, u32[]{:S(2)}) collective-permute-start(bf16[272,512]{1,0:T(8,128)(2,1)} %base.1.refs_0_), channel_id=1, source_target_pairs={{0,224},{1,225},{2,226},{3,227},{4,228},{5,229},{6,230},{7,231},{8... | collective-permute-start | bytes 835592 | tf_op jit(solution)/shard_map/ppermute | solution.py:45
  34.6 14.3 %collective-permute-start.11 = (bf16[320,128]{1,0:T(8,128)(2,1)S(1)}, bf16[320,128]{1,0:T(8,128)(2,1)S(1)}, u32[]{:S(2)}, u32[]{:S(2)}) collective-permute-start(bf16[320,128]{1,0:T(8,128)(2,1)S(1)} %broadcast_select_fusion), channel_id=1, source_target_pairs={{0,12},{1,13},{2,14},{3,15},{4,8},{5,9},{6,10},{7,11},{8,4},{9,5},... | collective-permute-start | bytes 245768 | tf_op jit(solution)/shard_map/ppermute | solution.py:45
  46.2 12.3 %collective-permute-start.2 = (bf16[272,512]{1,0:T(8,128)(2,1)}, bf16[272,512]{1,0:T(8,128)(2,1)S(1)}, u32[]{:S(2)}, u32[]{:S(2)}) collective-permute-start(bf16[272,512]{1,0:T(8,128)(2,1)} %base.1.refs_0_), channel_id=1, source_target_pairs={{0,32},{1,33},{2,34},{3,35},{4,36},{5,37},{6,38},{7,39},{8,40},{9,... | collective-permute-start | bytes 835592 | tf_op jit(solution)/shard_map/ppermute | solution.py:45
  49.0 11.5 %collective-permute-start.12 = (bf16[2,320,128]{2,1,0:T(8,128)(2,1)S(1)}, bf16[2,320,128]{2,1,0:T(8,128)(2,1)S(1)}, u32[]{:S(2)}, u32[]{:S(2)}) collective-permute-start(bf16[2,320,128]{2,1,0:T(8,128)(2,1)S(1)} %pad_maximum_fusion.1), channel_id=1, source_target_pairs={{0,4},{1,5},{2,6},{3,7},{4,0},{5,1},{6,2},{7,3},{8,12},{9,13},{10,... | collective-permute-start | bytes 491528 | tf_op jit(solution)/shard_map/ppermute | solution.py:45
  51.4 13.8 %collective-permute-start.7 = (bf16[272,512]{1,0:T(8,128)(2,1)S(1)}, bf16[272,512]{1,0:T(8,128)(2,1)S(1)}, u32[]{:S(2)}, u32[]{:S(2)}) collective-permute-start(bf16[272,512]{1,0:T(8,128)(2,1)S(1)} %collective-permute-done.6.refs_5_), channel_id=1, source_target_pairs={{0,224},{1,225},{2,226},{3,227},{4,228},{5,229},{6,230},{7,231},{8... | collective-permute-start | bytes 835592 | tf_op jit(solution)/shard_map/ppermute | solution.py:45
  58.5 12.7 %collective-permute-start.3 = (bf16[272,512]{1,0:T(8,128)(2,1)S(1)}, bf16[272,512]{1,0:T(8,128)(2,1)S(1)}, u32[]{:S(2)}, u32[]{:S(2)}) collective-permute-start(bf16[272,512]{1,0:T(8,128)(2,1)S(1)} %collective-permute-done.2.refs_1_), channel_id=1, source_target_pairs={{0,32},{1,33},{2,34},{3,35},{4,36},{5,37},{6,38},{7,39},{8,40},{9,... | collective-permute-start | bytes 835592 | tf_op jit(solution)/shard_map/ppermute | solution.py:45
  60.4 43.9 %copy-start.3 = (bf16[512,320]{0,1:T(8,128)(2,1)S(1)}, bf16[512,320]{0,1:T(8,128)(2,1)}, u32[]{:S(2)}) copy-start(bf16[512,320]{0,1:T(8,128)(2,1)} %param.15) | copy-start | bytes 983044
  60.5 12.7 %collective-permute-start.15 = (bf16[4,320,128]{2,1,0:T(8,128)(2,1)S(1)}, bf16[4,320,128]{2,1,0:T(8,128)(2,1)S(1)}, u32[]{:S(2)}, u32[]{:S(2)}) collective-permute-start(bf16[4,320,128]{2,1,0:T(8,128)(2,1)S(1)} %pad_maximum_fusion.refs_8_), channel_id=1, source_target_pairs={{0,1},{1,2},{2,3},{3,0},{4,5},{5,6},{6,7},{7,4},{8,9},{9,10},{10,1... | collective-permute-start | bytes 983048 | tf_op jit(solution)/shard_map/ppermute | solution.py:45
  62.6 24.2 %collective-permute-start.16 = (f32[320,512]{1,0:T(8,128)S(1)}, f32[320,512]{1,0:T(8,128)S(1)}, u32[]{:S(2)}, u32[]{:S(2)}) collective-permute-start(f32[320,512]{1,0:T(8,128)S(1)} %bitcast.19), channel_id=1, source_target_pairs={{256,0},{257,1},{258,2},{259,3},{260,4},{261,5},{262,6},{263,7},{2... | collective-permute-start | bytes 1966088 | tf_op jit(solution)/shard_map/ppermute | solution.py:45
  63.9 22.8 %collective-permute-start.17 = (f32[320,512]{1,0:T(8,128)S(1)}, f32[320,512]{1,0:T(8,128)S(1)}, u32[]{:S(2)}, u32[]{:S(2)}) collective-permute-start(f32[320,512]{1,0:T(8,128)S(1)} %bitcast.21), channel_id=1, source_target_pairs={{256,0},{257,1},{258,2},{259,3},{260,4},{261,5},{262,6},{263,7},{2... | collective-permute-start | bytes 1966088 | tf_op jit(solution)/shard_map/ppermute | solution.py:45
  65.3 14.1 %collective-permute-start.14 = (bf16[4,320,128]{2,1,0:T(8,128)(2,1)S(1)}, bf16[4,320,128]{2,1,0:T(8,128)(2,1)S(1)}, u32[]{:S(2)}, u32[]{:S(2)}) collective-permute-start(bf16[4,320,128]{2,1,0:T(8,128)(2,1)S(1)} %pad_maximum_fusion.refs_8_), channel_id=1, source_target_pairs={{0,2},{1,3},{2,0},{3,1},{4,6},{5,7},{6,4},{7,5},{8,10},{9,11},{10,... | collective-permute-start | bytes 983048 | tf_op jit(solution)/shard_map/ppermute | solution.py:45
  71.2 13.3 %collective-permute-start.4 = (bf16[272,512]{1,0:T(8,128)(2,1)S(1)}, bf16[272,512]{1,0:T(8,128)(2,1)S(1)}, u32[]{:S(2)}, u32[]{:S(2)}) collective-permute-start(bf16[272,512]{1,0:T(8,128)(2,1)S(1)} %collective-permute-done.3.refs_2_), channel_id=1, source_target_pairs={{0,32},{1,33},{2,34},{3,35},{4,36},{5,37},{6,38},{7,39},{8,40},{9,... | collective-permute-start | bytes 835592 | tf_op jit(solution)/shard_map/ppermute | solution.py:45
  73.2 13.6 %collective-permute-start.13 = (bf16[4,320,128]{2,1,0:T(8,128)(2,1)S(1)}, bf16[4,320,128]{2,1,0:T(8,128)(2,1)S(1)}, u32[]{:S(2)}, u32[]{:S(2)}) collective-permute-start(bf16[4,320,128]{2,1,0:T(8,128)(2,1)S(1)} %pad_maximum_fusion.refs_8_), channel_id=1, source_target_pairs={{0,3},{1,0},{2,1},{3,2},{4,7},{5,4},{6,5},{7,6},{8,11},{9,8},{10,9... | collective-permute-start | bytes 983048 | tf_op jit(solution)/shard_map/ppermute | solution.py:45
  79.4 11.8 %collective-permute-start.8 = (bf16[272,512]{1,0:T(8,128)(2,1)S(1)}, bf16[272,512]{1,0:T(8,128)(2,1)S(1)}, u32[]{:S(2)}, u32[]{:S(2)}) collective-permute-start(bf16[272,512]{1,0:T(8,128)(2,1)S(1)} %collective-permute-done.7.refs_6_), channel_id=1, source_target_pairs={{0,224},{1,225},{2,226},{3,227},{4,228},{5,229},{6,230},{7,231},{8... | collective-permute-start | bytes 835592 | tf_op jit(solution)/shard_map/ppermute | solution.py:45
  84.5 12.0 %collective-permute-start.5 = (bf16[272,512]{1,0:T(8,128)(2,1)S(1)}, bf16[272,512]{1,0:T(8,128)(2,1)S(1)}, u32[]{:S(2)}, u32[]{:S(2)}) collective-permute-start(bf16[272,512]{1,0:T(8,128)(2,1)S(1)} %collective-permute-done.4.refs_3_), channel_id=1, source_target_pairs={{0,32},{1,33},{2,34},{3,35},{4,36},{5,37},{6,38},{7,39},{8,40},{9,... | collective-permute-start | bytes 835592 | tf_op jit(solution)/shard_map/ppermute | solution.py:45
  96.6 1.0 copy-start
  100.3 4.0 %collective-permute-start.18 = (f32[320,512]{1,0:T(8,128)S(1)}, f32[320,512]{1,0:T(8,128)S(1)}, u32[]{:S(2)}, u32[]{:S(2)}) collective-permute-start(f32[320,512]{1,0:T(8,128)S(1)} %get-tuple-element.18.mine_ref), channel_id=1, source_target_pairs={{0,256},{1,257},{2,258},{3,259},{4,260},{5,261},{6,262},{7,263},{8... | collective-permute-start | bytes 1966088 | tf_op jit(solution)/shard_map/ppermute | solution.py:45
  121.9 10.3 %collective-permute-start.19 = (bf16[8,320]{1,0:T(8,128)(2,1)S(1)}, bf16[8,320]{1,0:T(8,128)(2,1)S(1)}, u32[]{:S(2)}, u32[]{:S(2)}) collective-permute-start(bf16[8,320]{1,0:T(8,128)(2,1)S(1)} %reduce_sum.9), channel_id=1, source_target_pairs={{0,0},{1,16},{2,32},{3,48},{4,64},{5,80},{6,96},{7,112},{8,128},{9... | collective-permute-start | bytes 15368 | tf_op jit(solution)/shard_map/ppermute | solution.py:45

commit v5 on v3

--- a/solution.py
+++ b/solution.py
@@ -44,12 +44,25 @@
     return lax.ppermute(value, AXES, pairs)
 
 
-def keeper(zh, x):
-    return int((x & 1) == zh)
-
-
-def to_partner(g, y, zh, zl, x):
-    return (0, y, 1 - zh, zl, x) if g == 1 else None
+def on_learner(y, block_y):
+    return (y - block_y) % 8 in (1, 2, 3, 4)
+
+
+def keeper(y, zl, x):
+    return int(on_learner(y, 2 * zl + (x >> 1)))
+
+
+def half_to_partner(g, y, zh, zl, x):
+    z = (zh * 4 + zl + (2 if g == 1 else -2)) % 8
+    return (g, y, z // 4, z % 4, x)
+
+
+def round_y(g, y, zh, zl, x):
+    return (g, (y + (1 if g == 1 else -1)) % 8, zh, zl, x)
+
+
+def last_round_y(g, y, zh, zl, x):
+    return (g, (y + 1) % 8, zh, zl, x) if g == 1 else None
 
 
 def transposed(g, y, zh, zl, x):
@@ -58,15 +71,15 @@
 
 def cot_transposed(g, *place):
     _, y, zh, zl, x = transposed(g, *place)
-    return (keeper(zh, x), y, zh, zl, x) if g == 1 else None
+    return (keeper(y, zl, x), y, zh, zl, x) if g == 1 else None
 
 
 def along_zl(flip):
-    return lambda g, y, zh, zl, x: (g, y, zh, zl ^ flip, x) if g == keeper(zh, x) else None
+    return lambda g, y, zh, zl, x: (g, y, zh, zl ^ flip, x) if g == keeper(y, zl, x) else None
 
 
 def along_x(step):
-    return lambda g, y, zh, zl, x: (g, y, zh, zl, (x + step) % 4) if g == keeper(zh, x) else None
+    return lambda g, y, zh, zl, x: (g, y, zh, zl, (x + step) % 4)
 
 
 def other_core(g, y, zh, zl, x):
@@ -77,18 +90,25 @@
     return (0, y, zh, zl, x) if g == 1 else None
 
 
-FLIPS = (0, 3, 1, 2)
+CHUNKS = (
+    ((0, -1), (0, -2), (0, -3), (1, -1), (1, -2), (1, -3), (0, 0), (1, 0)),
+    ((0, 1), (0, 2), (0, 3), (1, 1), (1, 2), (1, 3), (0, 4), (1, 4)),
+)
 
 
 def device_table():
     table = np.zeros((512, 32), np.int32)
     for flat, (g, y, zh, zl, x) in enumerate(np.ndindex(*SHAPE)):
-        token_zh = zh if g == 1 else 1 - zh
-        table[flat, 0] = g
-        table[flat, 1] = token_zh
-        for n in range(8):
-            table[flat, 8 + n] = (2 * (n & 1) + token_zh - x) % 4
-            table[flat, 16 + n] = FLIPS.index(zl ^ (n >> 1))
+        kept = [[z for z in range(4) if keeper(y, z, c) == g] for c in range(4)]
+        start = (zl * 4 + x) * COLS
+        table[flat, :3] = g, start // 128, start % 128
+        table[flat, 3:5] = [z ^ zl for z in kept[x]]
+        for n, (other, hop) in enumerate(CHUNKS[g]):
+            block_y, block_zh = (y - hop) % 8, zh ^ other
+            block_x = 2 * (block_y & 1) + block_zh
+            table[flat, 8 + n] = block_y * 2 + block_zh
+            table[flat, 16 + n] = (block_x - x) % 4
+            table[flat, 24 + n] = kept[block_x].index(block_y >> 1)
     return table
 
 
@@ -172,61 +192,95 @@
     )(head, lengths, ids, queries, cache_keys, cache_values, new_keys, new_values)
 
 
-def base_kernel(table_ref, act_ref, act_got, rows_ref, rows_got, out_ref):
+VMEM = pl.BlockSpec(memory_space=pltpu.VMEM)
+SMEM = pl.BlockSpec(memory_space=pltpu.SMEM)
+HBM = pl.BlockSpec(memory_space=pl.ANY)
+
+
+def payload_kernel(table_ref, act_ref, act_got, rows_ref, out_ref):
     @pl.when(table_ref[0] == 1)
     def _():
         out_ref[:TOK, :] = act_ref[...]
-        out_ref[TOK:, :] = rows_ref[...]
 
     @pl.when(table_ref[0] == 0)
     def _():
         out_ref[:TOK, :] = act_got[...]
-        out_ref[TOK:, :] = rows_got[...]
-
-
-def base_of(table, *parts):
-    vmem = pl.BlockSpec(memory_space=pltpu.VMEM)
+
+    out_ref[TOK:, :] = rows_ref[...]
+
+
+def payload_of(table, *parts):
     return pl.pallas_call(
-        base_kernel,
+        payload_kernel,
         out_shape=jax.ShapeDtypeStruct((TOK + PAD, FEAT), bf16),
-        in_specs=[pl.BlockSpec(memory_space=pltpu.SMEM)] + [vmem] * 4,
-        out_specs=vmem,
-        name="base",
+        in_specs=[SMEM] + [VMEM] * 3,
+        out_specs=VMEM,
+        name="payload",
     )(table, *parts)
 
 
-def gradient_kernel(table_ref, chunks_ref, *refs):
-    blocks, (out_ref, chunk_rows, block_rows, row_tiles, sems) = refs[:4], refs[-5:]
-    act_copies = [
-        pltpu.make_async_copy(
-            chunks_ref.at[n, :TOK], chunk_rows.at[pl.ds(n * TOK, TOK)], sems.at[n]
+def cut_kernel(table_ref, cot_ref, out_ref, window, turned, sem):
+    start = pl.multiple_of(table_ref[1] * 128, 128)
+    copy = pltpu.make_async_copy(cot_ref.at[:, pl.ds(start, 384)], window, sem)
+    copy.start()
+    copy.wait()
+    turned[...] = window[...].astype(f32).T
+    place = pl.ds(pl.multiple_of(table_ref[2], 64), COLS)
+    out_ref[...] = turned[place, :].astype(bf16)
+
+
+def cut_of(table, cot):
+    return pl.pallas_call(
+        cut_kernel,
+        out_shape=jax.ShapeDtypeStruct((COLS, TOK), bf16),
+        in_specs=[SMEM, HBM],
+        out_specs=VMEM,
+        scratch_shapes=[
+            pltpu.VMEM((TOK, 384), bf16),
+            pltpu.VMEM((384, TOK), f32),
+            pltpu.SemaphoreType.DMA(()),
+        ],
+        name="cut",
+    )(table, cot)
+
+
+def gradient_kernel(table_ref, *refs):
+    chunks, lasts, pairs, out_ref = refs[:6], (refs[6:8], refs[8:10]), refs[10:14], refs[-6]
+    chunk_rows, pair_tiles, block_rows, row_tiles, sems = refs[-5:]
+
+    def copies_of(n, ref):
+        return (
+            pltpu.make_async_copy(
+                ref.at[:TOK], chunk_rows.at[pl.ds(n * TOK, TOK)], sems.at[4 + n]
+            ),
+            pltpu.make_async_copy(ref.at[TOK:], row_tiles.at[n], sems.at[12 + n]),
         )
-        for n in range(8)
+
+    pair_copies = [
+        pltpu.make_async_copy(pairs[b], pair_tiles.at[b], sems.at[b]) for b in range(4)
     ]
-    row_copies = [
-        pltpu.make_async_copy(chunks_ref.at[n, TOK:], row_tiles.at[n], sems.at[16 + n])
-        for n in range(8)
-    ]
+    for copy in pair_copies:
+        copy.start()
+    for n in range(6):
+        for copy in copies_of(n, chunks[n]):
+            copy.start()
+    for side in range(2):
+
+        @pl.when(table_ref[0] == side)
+        def _():
+            for n in range(2):
+                for copy in copies_of(6 + n, lasts[side][n]):
+                    copy.start()
+
+    out_ref[COLS:, :] = jnp.zeros((16 * ROWS, FEAT), f32)
+    for copy in pair_copies:
+        copy.wait()
     for n in range(8):
-        act_copies[n].start()
-        for b in range(4):
-
-            @pl.when(table_ref[8 + n] == b)
-            def _():
-                pltpu.make_async_copy(
-                    blocks[b].at[table_ref[16 + n]],
-                    block_rows.at[:, pl.ds(n * TOK, TOK)],
-                    sems.at[8 + n],
-                ).start()
-
-        row_copies[n].start()
-    out_ref[COLS:, :] = jnp.zeros((16 * ROWS, FEAT), f32)
+        block_rows[:, n * TOK : (n + 1) * TOK] = pair_tiles[table_ref[16 + n], table_ref[24 + n]]
+    waits = [copies_of(n, chunks[n] if n < 6 else lasts[0][n - 6]) for n in range(8)]
     for half in range(2):
         for n in range(4 * half, 4 * half + 4):
-            act_copies[n].wait()
-            pltpu.make_async_copy(
-                blocks[0].at[0], block_rows.at[:, pl.ds(n * TOK, TOK)], sems.at[8 + n]
-            ).wait()
+            waits[n][0].wait()
         span = pl.ds(half * 4 * TOK, 4 * TOK)
         part = jnp.dot(block_rows[:, span], chunk_rows[span, :], preferred_element_type=f32)
         if half == 0:
@@ -234,24 +288,24 @@
         else:
             out_ref[:COLS, :] += part
     for n in range(8):
-        row_copies[n].wait()
-        place = pl.multiple_of(COLS + (2 * n + table_ref[1]) * ROWS, ROWS)
+        waits[n][1].wait()
+        place = pl.multiple_of(COLS + table_ref[8 + n] * ROWS, ROWS)
         out_ref[pl.ds(place, ROWS), :] = row_tiles[n].astype(f32)[:ROWS]
 
 
-def gradient(table, chunks, blocks, others):
-    hbm = pl.BlockSpec(memory_space=pl.ANY)
-    operands = (chunks, *blocks, *others)
+def gradient(table, chunks, rollout_lasts, learner_lasts, pairs):
+    operands = (*chunks, *rollout_lasts, *learner_lasts, *pairs)
     return pl.pallas_call(
         gradient_kernel,
         out_shape=jax.ShapeDtypeStruct((COLS + 16 * ROWS, FEAT), f32),
-        in_specs=[pl.BlockSpec(memory_space=pltpu.SMEM)] + [hbm] * len(operands),
-        out_specs=pl.BlockSpec(memory_space=pltpu.VMEM),
+        in_specs=[SMEM] + [HBM] * len(operands),
+        out_specs=VMEM,
         scratch_shapes=[
             pltpu.VMEM((8 * TOK, FEAT), bf16),
+            pltpu.VMEM((4, 2, COLS, TOK), bf16),
             pltpu.VMEM((COLS, 8 * TOK), bf16),
             pltpu.VMEM((8, PAD, FEAT), bf16),
-            pltpu.SemaphoreType.DMA((24,)),
+            pltpu.SemaphoreType.DMA((20,)),
         ],
         compiler_params=pltpu.CompilerParams(vmem_limit_bytes=32 * 2**20),
         cost_estimate=pl.CostEstimate(
@@ -284,15 +338,14 @@
 
 
 def step(table, mine, got, one, one_got, two, two_got, weight):
-    vmem = pl.BlockSpec(memory_space=pltpu.VMEM)
     return pl.pallas_call(
         step_kernel,
         out_shape=(
             jax.ShapeDtypeStruct((COLS, FEAT), bf16),
             jax.ShapeDtypeStruct((16, ROWS, COLS), f32),
         ),
-        in_specs=[pl.BlockSpec(memory_space=pltpu.SMEM)] + [vmem] * 7,
-        out_specs=(vmem, vmem),
+        in_specs=[SMEM] + [VMEM] * 7,
+        out_specs=(VMEM, VMEM),
         compiler_params=pltpu.CompilerParams(vmem_limit_bytes=32 * 2**20),
         name="step",
     )(table, mine, got, one, one_got, two, two_got, weight)
@@ -316,7 +369,7 @@
     table = lax.dynamic_slice_in_dim(jnp.asarray(device_table()), flat, 1, 0)[0]
 
     act = activations[0]
-    act_got = permute(act, to_partner)
+    act_got = permute(act, to_rollout)
     rows = attend(
         (q >> 1).reshape(1),
         queries,
@@ -327,26 +380,53 @@
         lengths,
         token_ids.T,
     )
-    rows_got = permute(rows, to_partner)
-    base = base_of(table, act, act_got, rows, rows_got)
-    chunks = lax.all_gather(base, "y", axis=0)
-
-    cut = lax.dynamic_slice_in_dim(cotangent[0], q * COLS, COLS, 1).T
+    payload = payload_of(table, act, act_got, rows)
+    relay = permute(payload, half_to_partner)
+    ring = [payload, permute(payload, round_y)]
+
+    cut = cut_of(table, cotangent[0])
     own = permute(cut, cot_transposed)
-    two_blocks = jnp.stack([own, permute(own, along_zl(3))])
-    four = jnp.concatenate([two_blocks, permute(two_blocks, along_zl(1))], axis=0)
-    blocks = (
-        four,
-        permute(four, along_x(-1)),
-        permute(four, along_x(2)),
-        permute(four, along_x(1)),
-    )
-
+
+    relay, _, _ = lax.optimization_barrier((relay, ring[1], cut))
+    other = permute(relay, half_to_partner)
+    ring.append(permute(ring[1], round_y))
     one, two = moment_one[0].T, moment_two[0].T
-    one_got = permute(one, to_rollout)
-    two_got = permute(two, to_rollout)
-
-    mine = gradient(table, chunks, blocks, (one_got, two_got))
+    one_tied, two_tied, _ = lax.optimization_barrier((one, two, relay))
+    one_got = permute(one_tied, to_rollout)
+    two_got = permute(two_tied, to_rollout)
+
+    other, one_got, two_got, own, ring[2] = lax.optimization_barrier(
+        (other, one_got, two_got, own, ring[2])
+    )
+    other_ring = [other, permute(other, round_y)]
+    ring.append(permute(ring[2], round_y))
+    parts = [own] + [permute(own, along_zl(flip)) for flip in (1, 2, 3)]
+    other_ring[1], ring[3], *parts = lax.optimization_barrier((other_ring[1], ring[3], *parts))
+    pair = jnp.stack(
+        [
+            jnp.where(
+                table[s] == 0,
+                parts[0],
+                jnp.where(table[s] == 1, parts[1], jnp.where(table[s] == 2, parts[2], parts[3])),
+            )
+            for s in (3, 4)
+        ]
+    )
+    other_ring.append(permute(other_ring[1], round_y))
+    ring.append(permute(ring[3], last_round_y))
+    pairs = [pair] + [permute(pair, along_x(step)) for step in (-1, 2, 1)]
+    other_ring[2], ring[4], pair = lax.optimization_barrier((other_ring[2], ring[4], pair))
+    other_ring.append(permute(other_ring[2], round_y))
+    other_ring[3], *pairs = lax.optimization_barrier((other_ring[3], *pairs))
+    other_ring.append(permute(other_ring[3], last_round_y))
+
+    mine = gradient(
+        table,
+        ring[1:4] + other_ring[1:4],
+        (ring[0], other_ring[0]),
+        (ring[4], other_ring[4]),
+        pairs,
+    )
     got = permute(mine, other_core)
     update, partial = step(table, mine, got, one, one_got, two, two_got, weight.T)
 

time: 153 us -> 160 us (1.046)
  the two profiles are of different devices: /device:TPU:24 before, /device:TPU:2 now
where the time goes in v5:
time: 160 us; the launch traced here: 159 us
  starting transfers between devices  81.8 us (51%)
  blocking collectives  29.4 us (18%)
  waiting for transfers between devices  27.9 us (17%)
  Pallas kernels  11.6 us (7%)
  between operations  4.76 us (3%)
  local copies, waits for them, and re-layouts  3.41 us (2%)
    ppermute x22, starting transfers between devices, permute(): return lax.ppermute(value, AXES, pairs)  81.8 us
    ppermute x22, waiting for transfers between devices, permute(): return lax.ppermute(value, AXES, pairs)  27.9 us
    all_to_all x1, blocking collectives, local(): lax.all_to_all(partial, TENSOR, split_axis=0, concat_axis=0, tiled=True)  15.8 us
    all_to_all x1, blocking collectives, local(): lax.all_to_all(spread, TENSOR, split_axis=0, concat_axis=0, tiled=True)  13.6 us
  transfers between devices with their start and end apart: 22, of which 7 were waited for; matrix products, arithmetic and copies ran while one was open for 1% of the time, Pallas kernels for 3%

profile of v5, /device:TPU:2, one launch (start us, length us, event | category | flops | bytes accessed | tf_op | source)
XLA Modules:
  0.0 159.1 jit_solution(8153397203857970678)
XLA Ops:
  0.6 1.3 collective-permute-start
  1.9 0.0 copy-start.1
  2.0 0.0 copy-start.2
  2.0 2.9 %attend.1.rows_ref = bf16[16,512]{1,0:T(8,128)(2,1)} custom-call(s32[1]{0:T(128)} %bitcast.2.head_ref, s32[2]{0:T(128)} %lengths_ref.1, s32[2,4]{1,0:T(2,128)} %bitcast.34, bf16[4,2,512]{2,1,0:T(2,128)(2,1)} %q_ref.1, bf16[2,2048,128]{2,1,0:T(8,128)(2,1)} %k_ref.1, bf16[2,2048,128]{2,1,0:T(8,128)(2,1)} %v_ref.1, bf16[4,2,1024]{2,1,0:T(2,128)(2,1)} %nk_ref.1, ...), custom_call_target="tpu_custom_call" | custom-call | tf_op jit(solution)/shard_map/attend/pallas_call | solution.py:177
  4.9 1.3 constant_dynamic-slice_fusion
  6.1 0.0 collective-permute-done.act_got
  6.1 0.7 copy-done.5
  6.8 0.0 copy-start.4
  6.8 1.8 %payload.1.refs_6_ = bf16[272,512]{1,0:T(8,128)(2,1)} custom-call(s32[32]{0:T(128)} %get-tuple-element.51.table_ref, bf16[256,512]{1,0:T(8,128)(2,1)} %bitcast.33, bf16[256,512]{1,0:T(8,128)(2,1)} %copy-done.5, bf16[16,512]{1,0:T(8,128)(2,1)} %attend.1.rows_ref), custom_call_target="tpu_custom_call" | custom-call | tf_op jit(solution)/shard_map/payload/pallas_call | solution.py:213
  8.6 11.1 %collective-permute-start.2 = (bf16[272,512]{1,0:T(8,128)(2,1)}, bf16[272,512]{1,0:T(8,128)(2,1)S(1)}, u32[]{:S(2)}, u32[]{:S(2)}) collective-permute-start(bf16[272,512]{1,0:T(8,128)(2,1)} %payload.1.refs_6_), channel_id=1, source_target_pairs={{0,24},{1,25},{2,26},{3,27},{4,28},{5,29},{6,30},{7,31},{8,0},{9,1... | collective-permute-start | bytes 835592 | tf_op jit(solution)/shard_map/ppermute | solution.py:44
  19.7 5.4 %collective-permute-start.1 = (bf16[272,512]{1,0:T(8,128)(2,1)}, bf16[272,512]{1,0:T(8,128)(2,1)S(1)}, u32[]{:S(2)}, u32[]{:S(2)}) collective-permute-start(bf16[272,512]{1,0:T(8,128)(2,1)} %payload.1.refs_6_), channel_id=1, source_target_pairs={{0,224},{1,225},{2,226},{3,227},{4,228},{5,229},{6,230},{7,231},{8... | collective-permute-start | bytes 835592 | tf_op jit(solution)/shard_map/ppermute | solution.py:44
  25.1 2.4 %cut.1 = bf16[320,256]{1,0:T(8,128)(2,1)} custom-call(s32[32]{0:T(128)} %get-tuple-element.51.table_ref, bf16[256,5120]{1,0:T(8,128)(2,1)} %bitcast.30), custom_call_target="tpu_custom_call" | custom-call | tf_op jit(solution)/shard_map/cut/pallas_call | solution.py:233
  27.5 0.0 collective-permute-done.2
  27.5 1.9 %collective-permute-done.1.refs_0_ = bf16[272,512]{1,0:T(8,128)(2,1)S(1)} collective-permute-done((bf16[272,512]{1,0:T(8,128)(2,1)}, bf16[272,512]{1,0:T(8,128)(2,1)S(1)}, u32[]{:S(2)}, u32[]{:S(2)}) %collective-permute-start.1) | collective-permute-done | bytes 278560 | tf_op jit(solution)/shard_map/ppermute | solution.py:44
  29.4 0.0 copy-done.1
  29.4 1.3 collective-permute-start.4
  30.7 0.0 copy-done.2
  30.7 1.3 collective-permute-start.5
  32.0 4.0 %collective-permute-start.3 = (bf16[272,512]{1,0:T(8,128)(2,1)S(1)}, bf16[272,512]{1,0:T(8,128)(2,1)S(1)}, u32[]{:S(2)}, u32[]{:S(2)}) collective-permute-start(bf16[272,512]{1,0:T(8,128)(2,1)S(1)} %collective-permute-done.2), channel_id=1, source_target_pairs={{0,24},{1,25},{2,26},{3,27},{4,28},{5,29},{6,30},{7,31},{8,0},{9,1... | collective-permute-start | bytes 835592 | tf_op jit(solution)/shard_map/ppermute | solution.py:44
  36.0 5.4 %collective-permute-start.7 = (bf16[272,512]{1,0:T(8,128)(2,1)S(1)}, bf16[272,512]{1,0:T(8,128)(2,1)S(1)}, u32[]{:S(2)}, u32[]{:S(2)}) collective-permute-start(bf16[272,512]{1,0:T(8,128)(2,1)S(1)} %collective-permute-done.1.refs_0_), channel_id=1, source_target_pairs={{0,224},{1,225},{2,226},{3,227},{4,228},{5,229},{6,230},{7,231},{8... | collective-permute-start | bytes 835592 | tf_op jit(solution)/shard_map/ppermute | solution.py:44
  41.4 1.3 collective-permute-start.6
  42.7 10.8 %collective-permute-done.6 = bf16[320,256]{1,0:T(8,128)(2,1)S(1)} collective-permute-done((bf16[320,256]{1,0:T(8,128)(2,1)}, bf16[320,256]{1,0:T(8,128)(2,1)S(1)}, u32[]{:S(2)}, u32[]{:S(2)}) %collective-permute-start.6) | collective-permute-done | bytes 163872 | tf_op jit(solution)/shard_map/ppermute | solution.py:44
  53.5 0.0 collective-permute-done.3.refs_7_
  53.5 0.0 collective-permute-done.7.refs_1_
  53.5 0.0 collective-permute-done.4.one_got
  53.5 0.0 collective-permute-done.5.two_got
  53.5 9.8 %collective-permute-start.9 = (bf16[272,512]{1,0:T(8,128)(2,1)S(1)}, bf16[272,512]{1,0:T(8,128)(2,1)S(1)}, u32[]{:S(2)}, u32[]{:S(2)}) collective-permute-start(bf16[272,512]{1,0:T(8,128)(2,1)S(1)} %collective-permute-done.7.refs_1_), channel_id=1, source_target_pairs={{0,224},{1,225},{2,226},{3,227},{4,228},{5,229},{6,230},{7,231},{8... | collective-permute-start | bytes 835592 | tf_op jit(solution)/shard_map/ppermute | solution.py:44
  63.4 1.9 %collective-permute-start.8 = (bf16[272,512]{1,0:T(8,128)(2,1)S(1)}, bf16[272,512]{1,0:T(8,128)(2,1)S(1)}, u32[]{:S(2)}, u32[]{:S(2)}) collective-permute-start(bf16[272,512]{1,0:T(8,128)(2,1)S(1)} %collective-permute-done.3.refs_7_), channel_id=1, source_target_pairs={{0,224},{1,225},{2,226},{3,227},{4,228},{5,229},{6,230},{7,231},{8... | collective-permute-start | bytes 835592 | tf_op jit(solution)/shard_map/ppermute | solution.py:44
  65.3 1.3 collective-permute-start.12
  66.6 1.3 collective-permute-start.11
  67.9 1.9 %collective-permute-start.10 = (bf16[320,256]{1,0:T(8,128)(2,1)S(1)}, bf16[320,256]{1,0:T(8,128)(2,1)S(1)}, u32[]{:S(2)}, u32[]{:S(2)}) collective-permute-start(bf16[320,256]{1,0:T(8,128)(2,1)S(1)} %collective-permute-done.6), channel_id=1, source_target_pairs={{0,4},{1,5},{2,6},{3,7},{4,0},{5,1},{6,2},{7,3},{16,20},{17,21},{1... | collective-permute-start | bytes 491528 | tf_op jit(solution)/shard_map/ppermute | solution.py:44
  69.9 0.6 fusion.1
  74.2 0.0 collective-permute-done.12
  74.3 0.0 collective-permute-done.11
  74.3 0.9 collective-permute-done.10
  75.1 0.0 collective-permute-done.9.refs_2_
  75.1 0.0 collective-permute-done.8.refs_3_
  75.1 0.7 collective-permute-start.14
  75.8 2.3 %collective-permute-start.13 = (bf16[272,512]{1,0:T(8,128)(2,1)S(1)}, bf16[272,512]{1,0:T(8,128)(2,1)S(1)}, u32[]{:S(2)}, u32[]{:S(2)}) collective-permute-start(bf16[272,512]{1,0:T(8,128)(2,1)S(1)} %collective-permute-done.8.refs_3_), channel_id=1, source_target_pairs={{0,224},{1,225},{2,226},{3,227},{4,228},{5,229},{6,230},{7,231},{8... | collective-permute-start | bytes 835592 | tf_op jit(solution)/shard_map/ppermute | solution.py:44
  78.2 0.0 copy-start.3
  78.2 2.5 %collective-permute-start.18 = (bf16[2,320,256]{2,1,0:T(8,128)(2,1)S(1)}, bf16[2,320,256]{2,1,0:T(8,128)(2,1)S(1)}, u32[]{:S(2)}, u32[]{:S(2)}) collective-permute-start(bf16[2,320,256]{2,1,0:T(8,128)(2,1)S(1)} %pad_maximum_fusion.refs_10_), channel_id=1, source_target_pairs={{0,1},{1,2},{2,3},{3,0},{4,5},{5,6},{6,7},{7,4},{8,9},{9,10},{10,1... | collective-permute-start | bytes 983048 | tf_op jit(solution)/shard_map/ppermute | solution.py:44
  80.8 5.7 %collective-permute-start.17 = (bf16[2,320,256]{2,1,0:T(8,128)(2,1)S(1)}, bf16[2,320,256]{2,1,0:T(8,128)(2,1)S(1)}, u32[]{:S(2)}, u32[]{:S(2)}) collective-permute-start(bf16[2,320,256]{2,1,0:T(8,128)(2,1)S(1)} %pad_maximum_fusion.refs_10_), channel_id=1, source_target_pairs={{0,2},{1,3},{2,0},{3,1},{4,6},{5,7},{6,4},{7,5},{8,10},{9,11},{10,... | collective-permute-start | bytes 983048 | tf_op jit(solution)/shard_map/ppermute | solution.py:44
  86.4 4.5 %collective-permute-start.16 = (bf16[2,320,256]{2,1,0:T(8,128)(2,1)S(1)}, bf16[2,320,256]{2,1,0:T(8,128)(2,1)S(1)}, u32[]{:S(2)}, u32[]{:S(2)}) collective-permute-start(bf16[2,320,256]{2,1,0:T(8,128)(2,1)S(1)} %pad_maximum_fusion.refs_10_), channel_id=1, source_target_pairs={{0,3},{1,0},{2,1},{3,2},{4,7},{5,4},{6,5},{7,6},{8,11},{9,8},{10,9... | collective-permute-start | bytes 983048 | tf_op jit(solution)/shard_map/ppermute | solution.py:44
  91.0 0.0 collective-permute-done.14.refs_8_
  91.0 0.0 collective-permute-done.13.refs_4_
  91.0 2.7 %collective-permute-start.15 = (bf16[272,512]{1,0:T(8,128)(2,1)S(1)}, bf16[272,512]{1,0:T(8,128)(2,1)S(1)}, u32[]{:S(2)}, u32[]{:S(2)}) collective-permute-start(bf16[272,512]{1,0:T(8,128)(2,1)S(1)} %collective-permute-done.13.refs_4_), channel_id=1, source_target_pairs={{0,224},{1,225},{2,226},{3,227},{4,228},{5,229},{6,230},{7,231},{8... | collective-permute-start | bytes 835592 | tf_op jit(solution)/shard_map/ppermute | solution.py:44
  93.7 0.0 collective-permute-done.18.refs_13_
  93.7 1.3 collective-permute-done.17.refs_12_
  95.0 6.5 %collective-permute-done.16.refs_11_ = bf16[2,320,256]{2,1,0:T(8,128)(2,1)S(1)} collective-permute-done((bf16[2,320,256]{2,1,0:T(8,128)(2,1)S(1)}, bf16[2,320,256]{2,1,0:T(8,128)(2,1)S(1)}, u32[]{:S(2)}, u32[]{:S(2)}) %collective-permute-start.16) | collective-permute-done | bytes 327712 | tf_op jit(solution)/shard_map/ppermute | solution.py:44
  101.4 0.0 collective-permute-done.15.refs_5_
  101.4 0.7 collective-permute-start.19
  102.1 0.0 collective-permute-done.19.refs_9_
  102.1 0.0 copy-done.4
  102.1 0.0 copy-done
  102.2 2.5 %gradient.1.mine_ref = f32[448,512]{1,0:T(8,128)S(1)} custom-call(s32[32]{0:T(128)S(1)} %copy-done.4, bf16[272,512]{1,0:T(8,128)(2,1)S(1)} %collective-permute-done.1.refs_0_, bf16[272,512]{1,0:T(8,128)(2,1)S(1)} %collective-permute-done.7.refs_1_, bf16[272,512]{1,0:T(8,128)(2,1)S(1)} %collective-permute-done.9.refs_2_, ...), custom_call_target="tpu_custom_call" | custom-call | flops 671088640 | bytes 6291456 | tf_op jit(solution)/shard_map/gradient/pallas_call | solution.py:298
  104.7 9.7 %collective-permute-start.20 = (f32[448,512]{1,0:T(8,128)S(1)}, f32[448,512]{1,0:T(8,128)S(1)}, u32[]{:S(2)}, u32[]{:S(2)}) collective-permute-start(f32[448,512]{1,0:T(8,128)S(1)} %gradient.1.mine_ref), channel_id=1, source_target_pairs={{0,256},{1,257},{2,258},{3,259},{4,260},{5,261},{6,262},{7,263},{8... | collective-permute-start | bytes 2752520 | tf_op jit(solution)/shard_map/ppermute | solution.py:44
  114.4 2.1 %collective-permute-done.20.got_ref = f32[448,512]{1,0:T(8,128)S(1)} collective-permute-done((f32[448,512]{1,0:T(8,128)S(1)}, f32[448,512]{1,0:T(8,128)S(1)}, u32[]{:S(2)}, u32[]{:S(2)}) %collective-permute-start.20) | collective-permute-done | bytes 917536 | tf_op jit(solution)/shard_map/ppermute | solution.py:44
  116.5 0.0 copy-done.3
  116.5 2.0 %step.1 = (bf16[320,512]{1,0:T(8,128)(2,1)}, f32[16,8,320]{2,1,0:T(8,128)S(1)}) custom-call(s32[32]{0:T(128)S(1)} %copy-done.4, f32[448,512]{1,0:T(8,128)S(1)} %gradient.1.mine_ref, f32[448,512]{1,0:T(8,128)S(1)} %collective-permute-done.20.got_ref, f32[320,512]{1,0:T(8,128)S(1)} %bitcast.26, f32[320,512]{1,0:T(8,128)S(1)} %collective-permute-done.4.one_got, ...), custom_call_target="tpu_custom_call" | custom-call | tf_op jit(solution)/shard_map/step/pallas_call | solution.py:341
  118.4 15.8 %all_to_all.10 = f32[16,8,320]{2,1,0:T(8,128)S(1)} all-to-all(f32[16,8,320]{2,1,0:T(8,128)S(1)} %get-tuple-element.47), channel_id=1, replica_groups=mesh['group'=2,'y'=8,'z_hi'=2,'z_lo'=4,'x'=4] {'z_lo','x'}, dimensions={0} | all-to-all | bytes 327680 | tf_op jit(solution)/shard_map/all_to_all | solution.py:433
  134.3 5.8 %collective-permute-start.21 = (bf16[8,320]{1,0:T(8,128)(2,1)S(1)}, bf16[8,320]{1,0:T(8,128)(2,1)S(1)}, u32[]{:S(2)}, u32[]{:S(2)}) collective-permute-start(bf16[8,320]{1,0:T(8,128)(2,1)S(1)} %reduce_sum.9), channel_id=1, source_target_pairs={{0,0},{1,16},{2,32},{3,48},{4,64},{5,80},{6,96},{7,112},{8,128},{9... | collective-permute-start | bytes 15368 | tf_op jit(solution)/shard_map/ppermute | solution.py:44
  140.1 4.5 %collective-permute-done.21 = bf16[8,320]{1,0:T(8,128)(2,1)S(1)} collective-permute-done((bf16[8,320]{1,0:T(8,128)(2,1)S(1)}, bf16[8,320]{1,0:T(8,128)(2,1)S(1)}, u32[]{:S(2)}, u32[]{:S(2)}) %collective-permute-start.21) | collective-permute-done | bytes 5152 | tf_op jit(solution)/shard_map/ppermute | solution.py:44
  144.6 13.6 %all_to_all.11 = bf16[16,8,320]{2,1,0:T(8,128)(2,1)S(1)} all-to-all(bf16[16,8,320]{2,1,0:T(8,128)(2,1)S(1)} %broadcast_in_dim.2), channel_id=1, replica_groups=mesh['group'=2,'y'=8,'z_hi'=2,'z_lo'=4,'x'=4] {'z_lo','x'}, dimensions={0} | all-to-all | bytes 163840 | tf_op jit(solution)/shard_map/all_to_all | solution.py:437
  158.3 0.8 reshape.28
  (7 shorter events, 0.1 us)
Async XLA Ops:
  0.6 5.5 %collective-permute-start = (bf16[256,512]{1,0:T(8,128)(2,1)}, bf16[256,512]{1,0:T(8,128)(2,1)S(1)}, u32[]{:S(2)}, u32[]{:S(2)}) collective-permute-start(bf16[256,512]{1,0:T(8,128)(2,1)} %bitcast.32), channel_id=1, source_target_pairs={{256,0},{257,1},{258,2},{259,3},{260,4},{261,5},{262,6},{263,7},{2... | collective-permute-start | bytes 786440 | tf_op jit(solution)/shard_map/ppermute | solution.py:44
  1.9 27.5 %copy-start.1 = (f32[1,512,320]{1,2,0:T(8,128)S(1)}, f32[1,512,320]{1,2,0:T(8,128)}, u32[]{:S(2)}) copy-start(f32[1,512,320]{1,2,0:T(8,128)} %param.16) | copy-start | bytes 1966084
  2.0 28.8 %copy-start.2 = (f32[1,512,320]{1,2,0:T(8,128)S(1)}, f32[1,512,320]{1,2,0:T(8,128)}, u32[]{:S(2)}) copy-start(f32[1,512,320]{1,2,0:T(8,128)} %param.17) | copy-start | bytes 1966084
  6.1 0.7 copy-start.5
  6.8 95.3 %copy-start.4 = (s32[32]{0:T(128)S(1)}, s32[32]{0:T(128)}, u32[]{:S(2)}) copy-start(s32[32]{0:T(128)} %get-tuple-element.51.table_ref) | copy-start | bytes 388
  8.6 93.5 %copy-start = (bf16[272,512]{1,0:T(8,128)(2,1)S(1)}, bf16[272,512]{1,0:T(8,128)(2,1)}, u32[]{:S(2)}) copy-start(bf16[272,512]{1,0:T(8,128)(2,1)} %payload.1.refs_6_) | copy-start | bytes 835588
  8.6 18.9 %collective-permute-start.2 = (bf16[272,512]{1,0:T(8,128)(2,1)}, bf16[272,512]{1,0:T(8,128)(2,1)S(1)}, u32[]{:S(2)}, u32[]{:S(2)}) collective-permute-start(bf16[272,512]{1,0:T(8,128)(2,1)} %payload.1.refs_6_), channel_id=1, source_target_pairs={{0,24},{1,25},{2,26},{3,27},{4,28},{5,29},{6,30},{7,31},{8,0},{9,1... | collective-permute-start | bytes 835592 | tf_op jit(solution)/shard_map/ppermute | solution.py:44
  19.7 9.7 %collective-permute-start.1 = (bf16[272,512]{1,0:T(8,128)(2,1)}, bf16[272,512]{1,0:T(8,128)(2,1)S(1)}, u32[]{:S(2)}, u32[]{:S(2)}) collective-permute-start(bf16[272,512]{1,0:T(8,128)(2,1)} %payload.1.refs_6_), channel_id=1, source_target_pairs={{0,224},{1,225},{2,226},{3,227},{4,228},{5,229},{6,230},{7,231},{8... | collective-permute-start | bytes 835592 | tf_op jit(solution)/shard_map/ppermute | solution.py:44
  29.4 24.1 %collective-permute-start.4 = (f32[320,512]{1,0:T(8,128)S(1)}, f32[320,512]{1,0:T(8,128)S(1)}, u32[]{:S(2)}, u32[]{:S(2)}) collective-permute-start(f32[320,512]{1,0:T(8,128)S(1)} %bitcast.25), channel_id=1, source_target_pairs={{256,0},{257,1},{258,2},{259,3},{260,4},{261,5},{262,6},{263,7},{2... | collective-permute-start | bytes 1966088 | tf_op jit(solution)/shard_map/ppermute | solution.py:44
  30.7 22.8 %collective-permute-start.5 = (f32[320,512]{1,0:T(8,128)S(1)}, f32[320,512]{1,0:T(8,128)S(1)}, u32[]{:S(2)}, u32[]{:S(2)}) collective-permute-start(f32[320,512]{1,0:T(8,128)S(1)} %bitcast.27), channel_id=1, source_target_pairs={{256,0},{257,1},{258,2},{259,3},{260,4},{261,5},{262,6},{263,7},{2... | collective-permute-start | bytes 1966088 | tf_op jit(solution)/shard_map/ppermute | solution.py:44
  32.0 21.5 %collective-permute-start.3 = (bf16[272,512]{1,0:T(8,128)(2,1)S(1)}, bf16[272,512]{1,0:T(8,128)(2,1)S(1)}, u32[]{:S(2)}, u32[]{:S(2)}) collective-permute-start(bf16[272,512]{1,0:T(8,128)(2,1)S(1)} %collective-permute-done.2), channel_id=1, source_target_pairs={{0,24},{1,25},{2,26},{3,27},{4,28},{5,29},{6,30},{7,31},{8,0},{9,1... | collective-permute-start | bytes 835592 | tf_op jit(solution)/shard_map/ppermute | solution.py:44
  36.0 17.5 %collective-permute-start.7 = (bf16[272,512]{1,0:T(8,128)(2,1)S(1)}, bf16[272,512]{1,0:T(8,128)(2,1)S(1)}, u32[]{:S(2)}, u32[]{:S(2)}) collective-permute-start(bf16[272,512]{1,0:T(8,128)(2,1)S(1)} %collective-permute-done.1.refs_0_), channel_id=1, source_target_pairs={{0,224},{1,225},{2,226},{3,227},{4,228},{5,229},{6,230},{7,231},{8... | collective-permute-start | bytes 835592 | tf_op jit(solution)/shard_map/ppermute | solution.py:44
  41.4 12.1 %collective-permute-start.6 = (bf16[320,256]{1,0:T(8,128)(2,1)}, bf16[320,256]{1,0:T(8,128)(2,1)S(1)}, u32[]{:S(2)}, u32[]{:S(2)}) collective-permute-start(bf16[320,256]{1,0:T(8,128)(2,1)} %cut.1), channel_id=1, source_target_pairs={{256,0},{257,16},{258,288},{259,304},{260,320},{261,336},{262,352}... | collective-permute-start | bytes 491528 | tf_op jit(solution)/shard_map/ppermute | solution.py:44
  53.5 21.6 %collective-permute-start.9 = (bf16[272,512]{1,0:T(8,128)(2,1)S(1)}, bf16[272,512]{1,0:T(8,128)(2,1)S(1)}, u32[]{:S(2)}, u32[]{:S(2)}) collective-permute-start(bf16[272,512]{1,0:T(8,128)(2,1)S(1)} %collective-permute-done.7.refs_1_), channel_id=1, source_target_pairs={{0,224},{1,225},{2,226},{3,227},{4,228},{5,229},{6,230},{7,231},{8... | collective-permute-start | bytes 835592 | tf_op jit(solution)/shard_map/ppermute | solution.py:44
  63.4 11.8 %collective-permute-start.8 = (bf16[272,512]{1,0:T(8,128)(2,1)S(1)}, bf16[272,512]{1,0:T(8,128)(2,1)S(1)}, u32[]{:S(2)}, u32[]{:S(2)}) collective-permute-start(bf16[272,512]{1,0:T(8,128)(2,1)S(1)} %collective-permute-done.3.refs_7_), channel_id=1, source_target_pairs={{0,224},{1,225},{2,226},{3,227},{4,228},{5,229},{6,230},{7,231},{8... | collective-permute-start | bytes 835592 | tf_op jit(solution)/shard_map/ppermute | solution.py:44
  65.3 8.9 %collective-permute-start.12 = (bf16[320,256]{1,0:T(8,128)(2,1)S(1)}, bf16[320,256]{1,0:T(8,128)(2,1)S(1)}, u32[]{:S(2)}, u32[]{:S(2)}) collective-permute-start(bf16[320,256]{1,0:T(8,128)(2,1)S(1)} %collective-permute-done.6), channel_id=1, source_target_pairs={{0,12},{1,13},{2,14},{3,15},{4,8},{5,9},{6,10},{7,11},{16,28},{17,... | collective-permute-start | bytes 491528 | tf_op jit(solution)/shard_map/ppermute | solution.py:44
  66.6 7.6 %collective-permute-start.11 = (bf16[320,256]{1,0:T(8,128)(2,1)S(1)}, bf16[320,256]{1,0:T(8,128)(2,1)S(1)}, u32[]{:S(2)}, u32[]{:S(2)}) collective-permute-start(bf16[320,256]{1,0:T(8,128)(2,1)S(1)} %collective-permute-done.6), channel_id=1, source_target_pairs={{0,8},{1,9},{2,10},{3,11},{4,12},{5,13},{6,14},{7,15},{16,24},{17,... | collective-permute-start | bytes 491528 | tf_op jit(solution)/shard_map/ppermute | solution.py:44
  67.9 7.2 %collective-permute-start.10 = (bf16[320,256]{1,0:T(8,128)(2,1)S(1)}, bf16[320,256]{1,0:T(8,128)(2,1)S(1)}, u32[]{:S(2)}, u32[]{:S(2)}) collective-permute-start(bf16[320,256]{1,0:T(8,128)(2,1)S(1)} %collective-permute-done.6), channel_id=1, source_target_pairs={{0,4},{1,5},{2,6},{3,7},{4,0},{5,1},{6,2},{7,3},{16,20},{17,21},{1... | collective-permute-start | bytes 491528 | tf_op jit(solution)/shard_map/ppermute | solution.py:44
  75.1 15.8 %collective-permute-start.14 = (bf16[272,512]{1,0:T(8,128)(2,1)S(1)}, bf16[272,512]{1,0:T(8,128)(2,1)S(1)}, u32[]{:S(2)}, u32[]{:S(2)}) collective-permute-start(bf16[272,512]{1,0:T(8,128)(2,1)S(1)} %collective-permute-done.9.refs_2_), channel_id=1, source_target_pairs={{256,288},{257,289},{258,290},{259,291},{260,292},{261,293},{262,2... | collective-permute-start | bytes 835592 | tf_op jit(solution)/shard_map/ppermute | solution.py:44
  75.8 15.2 %collective-permute-start.13 = (bf16[272,512]{1,0:T(8,128)(2,1)S(1)}, bf16[272,512]{1,0:T(8,128)(2,1)S(1)}, u32[]{:S(2)}, u32[]{:S(2)}) collective-permute-start(bf16[272,512]{1,0:T(8,128)(2,1)S(1)} %collective-permute-done.8.refs_3_), channel_id=1, source_target_pairs={{0,224},{1,225},{2,226},{3,227},{4,228},{5,229},{6,230},{7,231},{8... | collective-permute-start | bytes 835592 | tf_op jit(solution)/shard_map/ppermute | solution.py:44
  78.2 38.3 %copy-start.3 = (bf16[512,320]{0,1:T(8,128)(2,1)S(1)}, bf16[512,320]{0,1:T(8,128)(2,1)}, u32[]{:S(2)}) copy-start(bf16[512,320]{0,1:T(8,128)(2,1)} %param.15) | copy-start | bytes 983044
  78.2 15.4 %collective-permute-start.18 = (bf16[2,320,256]{2,1,0:T(8,128)(2,1)S(1)}, bf16[2,320,256]{2,1,0:T(8,128)(2,1)S(1)}, u32[]{:S(2)}, u32[]{:S(2)}) collective-permute-start(bf16[2,320,256]{2,1,0:T(8,128)(2,1)S(1)} %pad_maximum_fusion.refs_10_), channel_id=1, source_target_pairs={{0,1},{1,2},{2,3},{3,0},{4,5},{5,6},{6,7},{7,4},{8,9},{9,10},{10,1... | collective-permute-start | bytes 983048 | tf_op jit(solution)/shard_map/ppermute | solution.py:44
  80.8 14.2 %collective-permute-start.17 = (bf16[2,320,256]{2,1,0:T(8,128)(2,1)S(1)}, bf16[2,320,256]{2,1,0:T(8,128)(2,1)S(1)}, u32[]{:S(2)}, u32[]{:S(2)}) collective-permute-start(bf16[2,320,256]{2,1,0:T(8,128)(2,1)S(1)} %pad_maximum_fusion.refs_10_), channel_id=1, source_target_pairs={{0,2},{1,3},{2,0},{3,1},{4,6},{5,7},{6,4},{7,5},{8,10},{9,11},{10,... | collective-permute-start | bytes 983048 | tf_op jit(solution)/shard_map/ppermute | solution.py:44
  86.4 15.0 %collective-permute-start.16 = (bf16[2,320,256]{2,1,0:T(8,128)(2,1)S(1)}, bf16[2,320,256]{2,1,0:T(8,128)(2,1)S(1)}, u32[]{:S(2)}, u32[]{:S(2)}) collective-permute-start(bf16[2,320,256]{2,1,0:T(8,128)(2,1)S(1)} %pad_maximum_fusion.refs_10_), channel_id=1, source_target_pairs={{0,3},{1,0},{2,1},{3,2},{4,7},{5,4},{6,5},{7,6},{8,11},{9,8},{10,9... | collective-permute-start | bytes 983048 | tf_op jit(solution)/shard_map/ppermute | solution.py:44
  91.0 10.5 %collective-permute-start.15 = (bf16[272,512]{1,0:T(8,128)(2,1)S(1)}, bf16[272,512]{1,0:T(8,128)(2,1)S(1)}, u32[]{:S(2)}, u32[]{:S(2)}) collective-permute-start(bf16[272,512]{1,0:T(8,128)(2,1)S(1)} %collective-permute-done.13.refs_4_), channel_id=1, source_target_pairs={{0,224},{1,225},{2,226},{3,227},{4,228},{5,229},{6,230},{7,231},{8... | collective-permute-start | bytes 835592 | tf_op jit(solution)/shard_map/ppermute | solution.py:44
  101.4 0.7 collective-permute-start.19
  104.7 11.8 %collective-permute-start.20 = (f32[448,512]{1,0:T(8,128)S(1)}, f32[448,512]{1,0:T(8,128)S(1)}, u32[]{:S(2)}, u32[]{:S(2)}) collective-permute-start(f32[448,512]{1,0:T(8,128)S(1)} %gradient.1.mine_ref), channel_id=1, source_target_pairs={{0,256},{1,257},{2,258},{3,259},{4,260},{5,261},{6,262},{7,263},{8... | collective-permute-start | bytes 2752520 | tf_op jit(solution)/shard_map/ppermute | solution.py:44
  134.3 10.3 %collective-permute-start.21 = (bf16[8,320]{1,0:T(8,128)(2,1)S(1)}, bf16[8,320]{1,0:T(8,128)(2,1)S(1)}, u32[]{:S(2)}, u32[]{:S(2)}) collective-permute-start(bf16[8,320]{1,0:T(8,128)(2,1)S(1)} %reduce_sum.9), channel_id=1, source_target_pairs={{0,0},{1,16},{2,32},{3,48},{4,64},{5,80},{6,96},{7,112},{8,128},{9... | collective-permute-start | bytes 15368 | tf_op jit(solution)/shard_map/ppermute | solution.py:44

commit v6 on v4

--- a/solution.py
+++ b/solution.py
@@ -31,6 +31,7 @@
 HALF = 128
 FEAT = 512
 COLS = 320
+PART = 80
 ROWS = 8
 PAD = 16
 f32, bf16 = jnp.float32, jnp.bfloat16
@@ -45,55 +46,24 @@
     return lax.ppermute(value, AXES, pairs)
 
 
+def gather(value, axes):
+    return lax.all_to_all(value, axes, split_axis=0, concat_axis=0, tiled=True)
+
+
 def to_partner(g, y, zh, zl, x):
     return (g, y, 1 - zh, zl, x)
 
 
-def along_y(step):
-    return lambda g, y, zh, zl, x: (g, (y + step) % 8, zh, zl, x)
-
-
 def transposed(g, y, zh, zl, x):
     return (g, zl * 2 + (x >> 1), x & 1, y >> 1, (y & 1) * 2 + zh)
 
 
-def cot_transposed(core):
-    return lambda g, *place: (core, *transposed(g, *place)[1:]) if g == 1 else None
-
-
-def along_zl(flip):
-    return lambda g, y, zh, zl, x: (g, y, zh, zl ^ flip, x)
-
-
-def along_x(step):
-    return lambda g, y, zh, zl, x: (g, y, zh, zl, (x + step) % 4)
-
-
 def other_core(g, y, zh, zl, x):
     return (1 - g, y, zh, zl, x)
 
 
 def to_rollout(g, y, zh, zl, x):
     return (0, y, zh, zl, x) if g == 1 else None
-
-
-HOPS = (0, 1, 2, 3, 4, -1, -2, -3)
-FLIPS = (0, 3, 1, 2)
-
-
-def device_table():
-    table = np.zeros((512, 64), np.int32)
-    for flat, (g, y, zh, zl, x) in enumerate(np.ndindex(*SHAPE)):
-        start = (zl * 4 + x) * COLS
-        table[flat, :3] = g, start // 128, start % 128
-        for n, hop in enumerate(HOPS):
-            for other in range(2):
-                block_y, block_zh = (y - hop) % 8, zh ^ other
-                at = n * 2 + other
-                table[flat, 16 + at] = block_y * 2 + block_zh
-                table[flat, 32 + at] = (2 * (block_y & 1) + block_zh - x) % 4
-                table[flat, 48 + at] = FLIPS.index(zl ^ (block_y >> 1))
-    return table
 
 
 def attend_kernel(
@@ -181,115 +151,109 @@
 HBM = pl.BlockSpec(memory_space=pl.ANY)
 
 
-def half_kernel(table_ref, act_ref, act_got, rows_ref, out_ref):
-    @pl.when(table_ref[0] == 1)
+def half_kernel(place_ref, act_ref, act_got, rows_ref, out_ref, spread_ref):
+    @pl.when(place_ref[0] == 1)
     def _():
         out_ref[:HALF, :] = act_ref[:HALF, :]
 
-    @pl.when(table_ref[0] == 0)
+    @pl.when(place_ref[0] == 0)
     def _():
         out_ref[:HALF, :] = act_got[HALF:, :]
 
     out_ref[HALF:, :] = rows_ref[...]
-
-
-def half_of(table, *parts):
+    for n in range(8):
+        spread_ref[n] = out_ref[...]
+
+
+def half_of(place, *parts):
     return pl.pallas_call(
         half_kernel,
-        out_shape=jax.ShapeDtypeStruct((HALF + PAD, FEAT), bf16),
+        out_shape=(
+            jax.ShapeDtypeStruct((HALF + PAD, FEAT), bf16),
+            jax.ShapeDtypeStruct((8, HALF + PAD, FEAT), bf16),
+        ),
         in_specs=[SMEM] + [VMEM] * 3,
+        out_specs=(VMEM, VMEM),
+        name="half",
+    )(place, *parts)
+
+
+def cut_kernel(place_ref, cot_ref, cot_got, out_ref, rows, turned, sem):
+    @pl.when(place_ref[0] == 1)
+    def _():
+        pltpu.make_async_copy(cot_ref.at[:HALF], rows, sem).start()
+
+    @pl.when(place_ref[0] == 0)
+    def _():
+        pltpu.make_async_copy(cot_got, rows, sem).start()
+
+    pltpu.make_async_copy(cot_got, rows, sem).wait()
+    for n in range(D // HALF):
+        span = slice(n * HALF, (n + 1) * HALF)
+        turned[span, :] = rows[:, span].astype(f32).T
+    for n in range(16):
+        start = pl.multiple_of(n * COLS + place_ref[4] * PART, 16)
+        out_ref[n] = turned[pl.ds(start, PART), :].astype(bf16)
+
+
+def cut_of(place, cot, cot_got):
+    return pl.pallas_call(
+        cut_kernel,
+        out_shape=jax.ShapeDtypeStruct((16, PART, HALF), bf16),
+        in_specs=[SMEM, HBM, HBM],
         out_specs=VMEM,
-        name="half",
-    )(table, *parts)
-
-
-def base_kernel(mine_ref, got_ref, out_ref):
-    out_ref[:HALF, :] = mine_ref[:HALF, :]
-    out_ref[HALF:TOK, :] = got_ref[:HALF, :]
-    rows = [ref[HALF:, :].astype(f32)[:ROWS] for ref in (mine_ref, got_ref)]
-    out_ref[TOK:, :] = jnp.concatenate(rows, axis=0).astype(bf16)
-
-
-def base_of(*parts):
-    return pl.pallas_call(
-        base_kernel,
-        out_shape=jax.ShapeDtypeStruct((TOK + PAD, FEAT), bf16),
-        in_specs=[VMEM] * 2,
-        out_specs=VMEM,
-        name="base",
-    )(*parts)
-
-
-def cut_kernel(table_ref, cot_ref, one_ref, two_ref, window, turned, sem):
-    start = pl.multiple_of(table_ref[1] * 128, 128)
-    copy = pltpu.make_async_copy(cot_ref.at[:, pl.ds(start, 384)], window, sem)
-    copy.start()
-    copy.wait()
-    turned[...] = window[...].astype(f32).T
-    place = pl.ds(pl.multiple_of(table_ref[2], 64), COLS)
-    one_ref[...] = turned[place, :HALF].astype(bf16)
-    two_ref[...] = turned[place, HALF:].astype(bf16)
-
-
-def cut_of(table, cot):
-    shape = jax.ShapeDtypeStruct((COLS, HALF), bf16)
-    return pl.pallas_call(
-        cut_kernel,
-        out_shape=(shape, shape),
-        in_specs=[SMEM, HBM],
-        out_specs=(VMEM, VMEM),
         scratch_shapes=[
-            pltpu.VMEM((TOK, 384), bf16),
-            pltpu.VMEM((384, TOK), f32),
+            pltpu.VMEM((HALF, D), bf16),
+            pltpu.VMEM((D, HALF), f32),
             pltpu.SemaphoreType.DMA(()),
         ],
+        compiler_params=pltpu.CompilerParams(vmem_limit_bytes=32 * 2**20),
         name="cut",
-    )(table, cot)
-
-
-def gradient_kernel(table_ref, *refs):
-    chunks, blocks, (out_ref, rows_ref) = refs[:8], refs[8:12], refs[-7:-5]
-    chunk_rows, block_tiles, block_rows, row_tiles, sems = refs[-5:]
-    copies = [
-        pltpu.make_async_copy(blocks[b], block_tiles.at[b], sems.at[b]) for b in range(4)
-    ]
-    act_copies = [
-        pltpu.make_async_copy(
-            chunks[n].at[:TOK], chunk_rows.at[pl.ds(n * TOK, TOK)], sems.at[4 + n]
+    )(place, cot, cot_got)
+
+
+def gradient_kernel(place_ref, own_ref, other_ref, blocks_ref, *refs):
+    out_ref, rows_ref, chunk_rows, row_tiles, block_tiles, block_rows, sems = refs[-7:]
+    sides = (own_ref, other_ref)
+    copies = [pltpu.make_async_copy(blocks_ref, block_tiles, sems.at[0])]
+    for n, ref in enumerate(sides):
+        copies.append(
+            pltpu.make_async_copy(ref.at[:, :HALF], chunk_rows.at[n], sems.at[1 + n])
         )
-        for n in range(8)
-    ]
-    row_copies = [
-        pltpu.make_async_copy(chunks[n].at[TOK:], row_tiles.at[n], sems.at[12 + n])
-        for n in range(8)
-    ]
-    for copy in copies + act_copies + row_copies:
+    for n, ref in enumerate(sides):
+        copies.append(pltpu.make_async_copy(ref.at[:, HALF:], row_tiles.at[n], sems.at[3 + n]))
+    for copy in copies:
         copy.start()
-    for copy in copies:
-        copy.wait()
-    for at in range(16):
-        block_rows[:, at * HALF : (at + 1) * HALF] = block_tiles[
-            table_ref[32 + at], table_ref[48 + at]
-        ]
-    for half in range(2):
-        for n in range(4 * half, 4 * half + 4):
-            act_copies[n].wait()
-        span = pl.ds(half * 4 * TOK, 4 * TOK)
-        part = jnp.dot(block_rows[:, span], chunk_rows[span, :], preferred_element_type=f32)
-        if half == 0:
+    copies[0].wait()
+    z_hi = place_ref[2]
+    for n in range(2):
+        for y in range(8):
+            span = slice((n * 8 + y) * HALF, (n * 8 + y + 1) * HALF)
+            block = 2 * y + (z_hi if n == 0 else 1 - z_hi)
+            for x in range(4):
+                block_rows[x * PART : (x + 1) * PART, span] = block_tiles[x, block]
+    for n in range(2):
+        copies[1 + n].wait()
+        span = slice(n * 8 * HALF, (n + 1) * 8 * HALF)
+        part = jnp.dot(
+            block_rows[:, span],
+            chunk_rows[n].reshape(8 * HALF, FEAT),
+            preferred_element_type=f32,
+        )
+        if n == 0:
             out_ref[...] = part
         else:
             out_ref[...] += part
-    for n in range(8):
-        row_copies[n].wait()
-        rows = row_tiles[n].astype(f32)
-        for other in range(2):
-            place = pl.multiple_of(table_ref[16 + 2 * n + other] * ROWS, ROWS)
-            rows_ref[pl.ds(place, ROWS), :] = rows[other * ROWS : (other + 1) * ROWS]
-
-
-def gradient(table, chunks, blocks, others):
-    operands = (*chunks, *blocks, *others)
+    for n in range(2):
+        copies[3 + n].wait()
+        for y in range(8):
+            block = 2 * y + (z_hi if n == 0 else 1 - z_hi)
+            place = pl.multiple_of(block * ROWS, ROWS)
+            rows_ref[pl.ds(place, ROWS), :] = row_tiles[n, y].astype(f32)[:ROWS]
+
+
+def gradient(place, own, other, blocks, others):
+    operands = (own, other, blocks, *others)
     return pl.pallas_call(
         gradient_kernel,
         out_shape=(
@@ -299,18 +263,18 @@
         in_specs=[SMEM] + [HBM] * len(operands),
         out_specs=(VMEM, VMEM),
         scratch_shapes=[
-            pltpu.VMEM((8 * TOK, FEAT), bf16),
-            pltpu.VMEM((4, 4, COLS, HALF), bf16),
-            pltpu.VMEM((COLS, 8 * TOK), bf16),
-            pltpu.VMEM((8, PAD, FEAT), bf16),
-            pltpu.SemaphoreType.DMA((20,)),
+            pltpu.VMEM((2, 8, HALF, FEAT), bf16),
+            pltpu.VMEM((2, 8, PAD, FEAT), bf16),
+            pltpu.VMEM((4, 16, PART, HALF), bf16),
+            pltpu.VMEM((COLS, 16 * HALF), bf16),
+            pltpu.SemaphoreType.DMA((5,)),
         ],
         compiler_params=pltpu.CompilerParams(vmem_limit_bytes=32 * 2**20),
         cost_estimate=pl.CostEstimate(
             flops=2 * 8 * TOK * COLS * FEAT, bytes_accessed=6 * 2**20, transcendentals=0
         ),
         name="gradient",
-    )(table, *operands)
+    )(place, *operands)
 
 
 def step_kernel(
@@ -363,11 +327,12 @@
     lengths,
     token_ids,
 ):
-    flat, q = lax.axis_index(AXES), lax.axis_index(TENSOR)
-    table = lax.dynamic_slice_in_dim(jnp.asarray(device_table()), flat, 1, 0)[0]
-
-    act = activations[0]
+    q = lax.axis_index(TENSOR)
+    place = jnp.stack([lax.axis_index(axis) for axis in AXES]).astype(jnp.int32)
+
+    act, cot = activations[0], cotangent[0]
     act_got = permute(act, to_rollout)
+    cot_got = permute(cot[HALF:], to_rollout)
     rows = attend(
         (q >> 1).reshape(1),
         queries,
@@ -378,47 +343,29 @@
         lengths,
         token_ids.T,
     )
-    half = half_of(table, act, act_got, rows)
-    base = base_of(half, permute(half, to_partner))
-
-    cut_one, cut_two = cut_of(table, cotangent[0])
-    own = permute(cut_one, cot_transposed(1)), permute(cut_two, cot_transposed(0))
-
-    up, down = [base], [base]
-    up.append(permute(base, along_y(1)))
-    down.append(permute(base, along_y(-1)))
-
-    own_one, own_two, _ = lax.optimization_barrier((*own, base))
-    own = jnp.where(table[0] == 1, own_one, own_two)
-    two_blocks = jnp.stack([own, permute(own, along_zl(3))])
-    up.append(permute(up[-1], along_y(1)))
-    down.append(permute(down[-1], along_y(-1)))
-    four = jnp.concatenate([two_blocks, permute(two_blocks, along_zl(1))], axis=0)
-    blocks = (
-        four,
-        permute(four, along_x(-1)),
-        permute(four, along_x(2)),
-        permute(four, along_x(1)),
-    )
-    up.append(permute(up[-1], along_y(1)))
-    down.append(permute(down[-1], along_y(-1)))
-    up.append(permute(up[-1], along_y(1)))
-    chunks = up + down[1:]
+    half, spread = half_of(place, act, act_got, rows)
+    own = gather(spread, "y")
+    half_got = permute(half, to_partner)
+    other = gather(jnp.broadcast_to(half_got[None], (8, HALF + PAD, FEAT)), "y")
+
+    cut = cut_of(place, cot, cot_got)
+    parts = gather(cut, DP)
+    blocks = gather(jnp.broadcast_to(parts[None], (4, 16, PART, HALF)), "x")
 
     one, two = moment_one[0].T, moment_two[0].T
-    one_tied, two_tied, _ = lax.optimization_barrier((one, two, base))
+    one_tied, two_tied, _ = lax.optimization_barrier((one, two, half))
     one_got = permute(one_tied, to_rollout)
     two_got = permute(two_tied, to_rollout)
 
-    mine, all_rows = gradient(table, chunks, blocks, (one_got, two_got))
+    mine, all_rows = gradient(place, own, other, blocks, (one_got, two_got))
     got = permute(mine, other_core)
-    update, partial = step(table, mine, got, all_rows, one, one_got, two, two_got, weight.T)
-
-    shares = lax.all_to_all(partial, TENSOR, split_axis=0, concat_axis=0, tiled=True)
+    update, partial = step(place, mine, got, all_rows, one, one_got, two, two_got, weight.T)
+
+    shares = gather(partial, TENSOR)
     summed = jnp.sum(shares, axis=0).astype(bf16)
     block = permute(summed, transposed)
     spread = jnp.broadcast_to(block[None], (16, ROWS, COLS))
-    gathered = lax.all_to_all(spread, TENSOR, split_axis=0, concat_axis=0, tiled=True)
+    gathered = gather(spread, TENSOR)
     decoded = gathered.transpose(1, 0, 2).reshape(STEPS, ROWS // STEPS, D)
     return (update.T, decoded)
 

time: 147 us -> 180 us (1.22)
  the two profiles are of different devices: /device:TPU:2 before, /device:TPU:56 now
where the time goes in v6:
time: 180 us; the launch traced here: 176 us
  blocking collectives  60.9 us (34%)
  waiting for transfers between devices  49.8 us (28%)
  starting transfers between devices  44 us (24%)
  Pallas kernels  12.1 us (7%)
  local copies, waits for them, and re-layouts  8.79 us (5%)
    all_to_all x3, blocking collectives, gather(): return lax.all_to_all(value, axes, split_axis=0, concat_axis=0, tiled=True)  60.9 us
    all_to_all x3, waiting for transfers between devices, gather(): return lax.all_to_all(value, axes, split_axis=0, concat_axis=0, tiled=True)  28.6 us
    all_to_all x3, starting transfers between devices, gather(): return lax.all_to_all(value, axes, split_axis=0, concat_axis=0, tiled=True)  26.2 us
    ppermute x7, waiting for transfers between devices, permute(): return lax.ppermute(value, AXES, pairs)  21.2 us
    ppermute x7, starting transfers between devices, permute(): return lax.ppermute(value, AXES, pairs)  17.7 us
    unnamed x26, local copies, waits for them, and re-layouts  3.94 us
  transfers between devices with their start and end apart: 10, of which 9 were waited for; matrix products, arithmetic and copies ran while one was open for 0% of the time, Pallas kernels for 3%

profile of v6, /device:TPU:56, one launch (start us, length us, event | category | flops | bytes accessed | tf_op | source)
XLA Modules:
  0.0 176.4 jit_solution(8679208783074060129)
XLA Ops:
  0.6 0.0 copy-start
  0.6 2.6 %slice_bitcast_fusion = bf16[128,5120]{1,0:T(8,128)(2,1)} fusion(bf16[1,256,5120]{2,1,0:T(8,128)(2,1)} %param.13), kind=kLoop, calls=%fused_computation | loop fusion | bytes 2621440 | tf_op jit(solution)/shard_map/slice | solution.py:335
  3.3 1.3 collective-permute-start.2
  4.6 0.1 stack.23.place_ref.table_ref
  4.6 0.0 copy-start.8
  4.6 3.9 %collective-permute-done.2.cot_got = bf16[128,5120]{1,0:T(8,128)(2,1)} collective-permute-done((bf16[128,5120]{1,0:T(8,128)(2,1)}, bf16[128,5120]{1,0:T(8,128)(2,1)}, u32[]{:S(2)}, u32[]{:S(2)}) %collective-permute-start.2) | collective-permute-done | bytes 1310752 | tf_op jit(solution)/shard_map/ppermute | solution.py:46
  8.5 0.0 copy-done
  8.5 0.0 copy-start.10
  8.5 3.0 %cut.1 = bf16[16,80,128]{2,1,0:T(8,128)(2,1)} custom-call(s32[5]{0:T(128)S(1)} %stack.23.place_ref.table_ref, bf16[256,5120]{1,0:T(8,128)(2,1)S(1)} %bitcast.20, bf16[128,5120]{1,0:T(8,128)(2,1)} %collective-permute-done.2.cot_got), custom_call_target="tpu_custom_call" | custom-call | tf_op jit(solution)/shard_map/cut/pallas_call | solution.py:200
  11.6 0.0 copy-done.8
  11.6 15.3 %all-to-all-start.2 = ((bf16[16,80,128]{2,1,0:T(8,128)(2,1)}), bf16[16,80,128]{2,1,0:T(8,128)(2,1)S(1)}, u32[]{:S(2)}, u32[]{:S(2)}) async-start(bf16[16,80,128]{2,1,0:T(8,128)(2,1)} %cut.1), calls=%async_computation.2 | async-start | bytes 655360 | tf_op jit(solution)/shard_map/all_to_all | solution.py:50
  26.9 0.0 copy-done.10
  26.9 1.3 collective-permute-start
  28.2 2.8 %attend.1.rows_ref = bf16[16,512]{1,0:T(8,128)(2,1)} custom-call(s32[1]{0:T(128)} %bitcast.6.head_ref, s32[2]{0:T(128)} %lengths_ref.1, s32[2,4]{1,0:T(2,128)} %bitcast.29, bf16[4,2,512]{2,1,0:T(2,128)(2,1)} %q_ref.1, bf16[2,2048,128]{2,1,0:T(8,128)(2,1)} %k_ref.1, bf16[2,2048,128]{2,1,0:T(8,128)(2,1)} %v_ref.1, bf16[4,2,1024]{2,1,0:T(2,128)(2,1)} %nk_ref.1, ...), custom_call_target="tpu_custom_call" | custom-call | tf_op jit(solution)/shard_map/attend/pallas_call | solution.py:131
  31.0 0.0 collective-permute-done.act_got
  31.0 0.0 copy-start.11
  31.0 0.7 copy-done.11
  31.7 2.2 %half.1 = (bf16[144,512]{1,0:T(8,128)(2,1)}, bf16[8,144,512]{2,1,0:T(8,128)(2,1)}) custom-call(s32[5]{0:T(128)} %copy-done.8, bf16[256,512]{1,0:T(8,128)(2,1)} %bitcast.27, bf16[256,512]{1,0:T(8,128)(2,1)} %copy-done.11, bf16[16,512]{1,0:T(8,128)(2,1)} %attend.1.rows_ref), custom_call_target="tpu_custom_call" | custom-call | tf_op jit(solution)/shard_map/half/pallas_call | solution.py:169
  33.9 0.0 copy-start.12
  33.9 6.7 %all-to-all-done.2 = bf16[16,80,128]{2,1,0:T(8,128)(2,1)S(1)} async-done(((bf16[16,80,128]{2,1,0:T(8,128)(2,1)}), bf16[16,80,128]{2,1,0:T(8,128)(2,1)S(1)}, u32[]{:S(2)}, u32[]{:S(2)}) %all-to-all-start.2) | async-done | bytes 327712 | tf_op jit(solution)/shard_map/all_to_all | solution.py:50
  40.6 6.5 %all-to-all-start = ((bf16[8,144,512]{2,1,0:T(8,128)(2,1)}), bf16[8,144,512]{2,1,0:T(8,128)(2,1)S(1)}, u32[]{:S(2)}, u32[]{:S(2)}) async-start(bf16[8,144,512]{2,1,0:T(8,128)(2,1)} %get-tuple-element.10), calls=%async_computation | async-start | bytes 2359296 | tf_op jit(solution)/shard_map/all_to_all | solution.py:50
  47.1 0.0 copy-done.12
  47.1 2.3 %collective-permute-start.1 = (bf16[144,512]{1,0:T(8,128)(2,1)S(1)}, bf16[144,512]{1,0:T(8,128)(2,1)S(1)}, u32[]{:S(2)}, u32[]{:S(2)}) collective-permute-start(bf16[144,512]{1,0:T(8,128)(2,1)S(1)} %copy-done.12), channel_id=1, source_target_pairs={{0,16},{1,17},{2,18},{3,19},{4,20},{5,21},{6,22},{7,23},{8,24},{9,... | collective-permute-start | bytes 442376 | tf_op jit(solution)/shard_map/ppermute | solution.py:46
  49.4 8.8 %collective-permute-done.1 = bf16[144,512]{1,0:T(8,128)(2,1)S(1)} collective-permute-done((bf16[144,512]{1,0:T(8,128)(2,1)S(1)}, bf16[144,512]{1,0:T(8,128)(2,1)S(1)}, u32[]{:S(2)}, u32[]{:S(2)}) %collective-permute-start.1) | collective-permute-done | bytes 147488 | tf_op jit(solution)/shard_map/ppermute | solution.py:46
  58.2 14.2 %all-to-all-done.own_ref = bf16[8,144,512]{2,1,0:T(8,128)(2,1)S(1)} async-done(((bf16[8,144,512]{2,1,0:T(8,128)(2,1)}), bf16[8,144,512]{2,1,0:T(8,128)(2,1)S(1)}, u32[]{:S(2)}, u32[]{:S(2)}) %all-to-all-start) | async-done | bytes 1179680 | tf_op jit(solution)/shard_map/all_to_all | solution.py:50
  72.4 0.1 broadcast_in_dim.6
  72.5 33.0 %all_to_all.30.other_ref = bf16[8,144,512]{2,1,0:T(8,128)(2,1)} all-to-all(bf16[8,144,512]{2,1,0:T(8,128)(2,1)S(1)} %broadcast_in_dim.6), channel_id=1, replica_groups=mesh['group'=2,'y'=8,'z_hi'=2,'z_lo'=4,'x'=4] {'y'}, dimensions={0} | all-to-all | bytes 2359296 | tf_op jit(solution)/shard_map/all_to_all | solution.py:50
  105.6 1.2 broadcast_in_dim.7
  106.8 0.0 copy-start.9
  106.8 0.0 copy-start.7
  106.8 4.4 %all-to-all-start.3 = ((bf16[4,16,80,128]{3,2,1,0:T(8,128)(2,1)}), bf16[4,16,80,128]{3,2,1,0:T(8,128)(2,1)S(1)}, u32[]{:S(2)}, u32[]{:S(2)}) async-start(bf16[4,16,80,128]{3,2,1,0:T(8,128)(2,1)} %broadcast_in_dim.7), calls=%async_computation.3 | async-start | bytes 2621440 | tf_op jit(solution)/shard_map/all_to_all | solution.py:50
  111.2 1.3 collective-permute-start.3
  112.5 1.3 collective-permute-start.4
  113.8 1.6 collective-permute-done.3.refs_0_.one_got
  115.4 1.3 collective-permute-done.4.refs_1_.two_got
  116.8 0.0 copy-start.2
  116.8 0.8 copy-done.2
  117.6 7.8 %all-to-all-done.3.blocks_ref = bf16[4,16,80,128]{3,2,1,0:T(8,128)(2,1)S(1)} async-done(((bf16[4,16,80,128]{3,2,1,0:T(8,128)(2,1)}), bf16[4,16,80,128]{3,2,1,0:T(8,128)(2,1)S(1)}, u32[]{:S(2)}, u32[]{:S(2)}) %all-to-all-start.3) | async-done | bytes 1310752 | tf_op jit(solution)/shard_map/all_to_all | solution.py:50
  125.4 0.0 copy-done.9
  125.4 0.0 copy-start.1
  125.4 1.3 copy-done.1
  126.7 0.0 copy-start.3
  126.7 1.1 copy-done.3
  127.7 0.0 copy-start.4
  127.7 0.0 copy-start.5
  127.7 0.0 copy-start.6
  127.7 2.1 %gradient.1 = (f32[320,512]{1,0:T(8,128)S(1)}, f32[128,512]{1,0:T(8,128)S(1)}) custom-call(s32[5]{0:T(128)S(1)} %copy-done.9, bf16[8,144,512]{2,1,0:T(8,128)(2,1)S(1)} %all-to-all-done.own_ref, bf16[8,144,512]{2,1,0:T(8,128)(2,1)S(1)} %copy-done.1, bf16[4,16,80,128]{3,2,1,0:T(8,128)(2,1)S(1)} %all-to-all-done.3.blocks_ref, ...), custom_call_target="tpu_custom_call" | custom-call | flops 671088640 | bytes 6291456 | tf_op jit(solution)/shard_map/gradient/pallas_call | solution.py:257
  129.9 1.9 %collective-permute-start.5 = (f32[320,512]{1,0:T(8,128)S(1)}, f32[320,512]{1,0:T(8,128)S(1)}, u32[]{:S(2)}, u32[]{:S(2)}) collective-permute-start(f32[320,512]{1,0:T(8,128)S(1)} %get-tuple-element.14.mine_ref), channel_id=1, source_target_pairs={{0,256},{1,257},{2,258},{3,259},{4,260},{5,261},{6,262},{7,263},{8... | collective-permute-start | bytes 1966088 | tf_op jit(solution)/shard_map/ppermute | solution.py:46
  131.8 2.1 %collective-permute-done.5.got_ref = f32[320,512]{1,0:T(8,128)S(1)} collective-permute-done((f32[320,512]{1,0:T(8,128)S(1)}, f32[320,512]{1,0:T(8,128)S(1)}, u32[]{:S(2)}, u32[]{:S(2)}) %collective-permute-start.5) | collective-permute-done | bytes 655392 | tf_op jit(solution)/shard_map/ppermute | solution.py:46
  133.9 0.0 copy-done.7
  133.9 0.0 copy-done.4
  133.9 0.0 copy-done.5
  133.9 0.0 copy-done.6
  133.9 1.9 %step.1 = (bf16[320,512]{1,0:T(8,128)(2,1)}, f32[16,8,320]{2,1,0:T(8,128)S(1)}) custom-call(s32[5]{0:T(128)S(1)} %copy-done.9, f32[320,512]{1,0:T(8,128)S(1)} %get-tuple-element.14.mine_ref, f32[320,512]{1,0:T(8,128)S(1)} %collective-permute-done.5.got_ref, f32[128,512]{1,0:T(8,128)S(1)} %get-tuple-element.15.rows_ref, f32[320,512]{1,0:T(8,128)S(1)} %bitcast.22, ...), custom_call_target="tpu_custom_call" | custom-call | tf_op jit(solution)/shard_map/step/pallas_call | solution.py:303
  135.9 13.8 %all_to_all.31 = f32[16,8,320]{2,1,0:T(8,128)S(1)} all-to-all(f32[16,8,320]{2,1,0:T(8,128)S(1)} %get-tuple-element.17), channel_id=1, replica_groups=mesh['group'=2,'y'=8,'z_hi'=2,'z_lo'=4,'x'=4] {'z_lo','x'}, dimensions={0} | all-to-all | bytes 327680 | tf_op jit(solution)/shard_map/all_to_all | solution.py:50
  149.7 8.4 %collective-permute-start.6 = (bf16[8,320]{1,0:T(8,128)(2,1)S(1)}, bf16[8,320]{1,0:T(8,128)(2,1)S(1)}, u32[]{:S(2)}, u32[]{:S(2)}) collective-permute-start(bf16[8,320]{1,0:T(8,128)(2,1)S(1)} %reduce_sum.9), channel_id=1, source_target_pairs={{0,0},{1,16},{2,32},{3,48},{4,64},{5,80},{6,96},{7,112},{8,128},{9... | collective-permute-start | bytes 15368 | tf_op jit(solution)/shard_map/ppermute | solution.py:46
  158.0 3.5 %collective-permute-done.6 = bf16[8,320]{1,0:T(8,128)(2,1)S(1)} collective-permute-done((bf16[8,320]{1,0:T(8,128)(2,1)S(1)}, bf16[8,320]{1,0:T(8,128)(2,1)S(1)}, u32[]{:S(2)}, u32[]{:S(2)}) %collective-permute-start.6) | collective-permute-done | bytes 5152 | tf_op jit(solution)/shard_map/ppermute | solution.py:46
  161.5 14.1 %all_to_all.32 = bf16[16,8,320]{2,1,0:T(8,128)(2,1)S(1)} all-to-all(bf16[16,8,320]{2,1,0:T(8,128)(2,1)S(1)} %broadcast_in_dim.8), channel_id=1, replica_groups=mesh['group'=2,'y'=8,'z_hi'=2,'z_lo'=4,'x'=4] {'z_lo','x'}, dimensions={0} | all-to-all | bytes 163840 | tf_op jit(solution)/shard_map/all_to_all | solution.py:50
  175.6 0.8 reshape.15
  (3 shorter events, 0.0 us)
Async XLA Ops:
  0.6 7.9 %copy-start = (bf16[1,256,5120]{2,1,0:T(8,128)(2,1)S(1)}, bf16[1,256,5120]{2,1,0:T(8,128)(2,1)}, u32[]{:S(2)}) copy-start(bf16[1,256,5120]{2,1,0:T(8,128)(2,1)} %param.13) | copy-start | bytes 7864324
  3.3 5.3 %collective-permute-start.2 = (bf16[128,5120]{1,0:T(8,128)(2,1)}, bf16[128,5120]{1,0:T(8,128)(2,1)}, u32[]{:S(2)}, u32[]{:S(2)}) collective-permute-start(bf16[128,5120]{1,0:T(8,128)(2,1)} %slice_bitcast_fusion), channel_id=1, source_target_pairs={{256,0},{257,1},{258,2},{259,3},{260,4},{261,5},{262,6},{263,7},{2... | collective-permute-start | bytes 3932168 | tf_op jit(solution)/shard_map/ppermute | solution.py:46
  4.6 6.9 %copy-start.8 = (s32[5]{0:T(128)}, s32[5]{0:T(128)S(1)}, u32[]{:S(2)}) copy-start(s32[5]{0:T(128)S(1)} %stack.23.place_ref.table_ref) | copy-start | bytes 64
  8.5 18.4 %copy-start.10 = (bf16[1,256,512]{2,1,0:T(8,128)(2,1)S(1)}, bf16[1,256,512]{2,1,0:T(8,128)(2,1)}, u32[]{:S(2)}) copy-start(bf16[1,256,512]{2,1,0:T(8,128)(2,1)} %param.12) | copy-start | bytes 786436
  11.6 29.0 %all-to-all-start.2 = ((bf16[16,80,128]{2,1,0:T(8,128)(2,1)}), bf16[16,80,128]{2,1,0:T(8,128)(2,1)S(1)}, u32[]{:S(2)}, u32[]{:S(2)}) async-start(bf16[16,80,128]{2,1,0:T(8,128)(2,1)} %cut.1), calls=%async_computation.2 | async-start | bytes 655360 | tf_op jit(solution)/shard_map/all_to_all | solution.py:50
  26.9 4.1 %collective-permute-start = (bf16[256,512]{1,0:T(8,128)(2,1)S(1)}, bf16[256,512]{1,0:T(8,128)(2,1)S(1)}, u32[]{:S(2)}, u32[]{:S(2)}) collective-permute-start(bf16[256,512]{1,0:T(8,128)(2,1)S(1)} %bitcast.28), channel_id=1, source_target_pairs={{256,0},{257,1},{258,2},{259,3},{260,4},{261,5},{262,6},{263,7},{2... | collective-permute-start | bytes 786440 | tf_op jit(solution)/shard_map/ppermute | solution.py:46
  31.0 0.7 copy-start.11
  33.9 13.2 %copy-start.12 = (bf16[144,512]{1,0:T(8,128)(2,1)S(1)}, bf16[144,512]{1,0:T(8,128)(2,1)}, u32[]{:S(2)}) copy-start(bf16[144,512]{1,0:T(8,128)(2,1)} %get-tuple-element.11) | copy-start | bytes 442372
  40.6 31.8 %all-to-all-start = ((bf16[8,144,512]{2,1,0:T(8,128)(2,1)}), bf16[8,144,512]{2,1,0:T(8,128)(2,1)S(1)}, u32[]{:S(2)}, u32[]{:S(2)}) async-start(bf16[8,144,512]{2,1,0:T(8,128)(2,1)} %get-tuple-element.10), calls=%async_computation | async-start | bytes 2359296 | tf_op jit(solution)/shard_map/all_to_all | solution.py:50
  47.1 11.1 %collective-permute-start.1 = (bf16[144,512]{1,0:T(8,128)(2,1)S(1)}, bf16[144,512]{1,0:T(8,128)(2,1)S(1)}, u32[]{:S(2)}, u32[]{:S(2)}) collective-permute-start(bf16[144,512]{1,0:T(8,128)(2,1)S(1)} %copy-done.12), channel_id=1, source_target_pairs={{0,16},{1,17},{2,18},{3,19},{4,20},{5,21},{6,22},{7,23},{8,24},{9,... | collective-permute-start | bytes 442376 | tf_op jit(solution)/shard_map/ppermute | solution.py:46
  106.8 18.6 %copy-start.9 = (s32[5]{0:T(128)S(1)}, s32[5]{0:T(128)}, u32[]{:S(2)}) copy-start(s32[5]{0:T(128)} %copy-done.8) | copy-start | bytes 64
  106.8 27.1 %copy-start.7 = (bf16[512,320]{0,1:T(8,128)(2,1)S(1)}, bf16[512,320]{0,1:T(8,128)(2,1)}, u32[]{:S(2)}) copy-start(bf16[512,320]{0,1:T(8,128)(2,1)} %param.14) | copy-start | bytes 983044
  106.8 18.6 %all-to-all-start.3 = ((bf16[4,16,80,128]{3,2,1,0:T(8,128)(2,1)}), bf16[4,16,80,128]{3,2,1,0:T(8,128)(2,1)S(1)}, u32[]{:S(2)}, u32[]{:S(2)}) async-start(bf16[4,16,80,128]{3,2,1,0:T(8,128)(2,1)} %broadcast_in_dim.7), calls=%async_computation.3 | async-start | bytes 2621440 | tf_op jit(solution)/shard_map/all_to_all | solution.py:50
  111.2 4.2 %collective-permute-start.3 = (f32[320,512]{1,0:T(8,128)}, f32[320,512]{1,0:T(8,128)S(1)}, u32[]{:S(2)}, u32[]{:S(2)}) collective-permute-start(f32[320,512]{1,0:T(8,128)} %bitcast.21), channel_id=1, source_target_pairs={{256,0},{257,1},{258,2},{259,3},{260,4},{261,5},{262,6},{263,7},{2... | collective-permute-start | bytes 1966088 | tf_op jit(solution)/shard_map/ppermute | solution.py:46
  112.5 4.2 %collective-permute-start.4 = (f32[320,512]{1,0:T(8,128)}, f32[320,512]{1,0:T(8,128)S(1)}, u32[]{:S(2)}, u32[]{:S(2)}) collective-permute-start(f32[320,512]{1,0:T(8,128)} %bitcast.23), channel_id=1, source_target_pairs={{256,0},{257,1},{258,2},{259,3},{260,4},{261,5},{262,6},{263,7},{2... | collective-permute-start | bytes 1966088 | tf_op jit(solution)/shard_map/ppermute | solution.py:46
  116.8 0.8 copy-start.2
  125.4 1.3 copy-start.1
  126.7 1.1 copy-start.3
  127.7 6.2 %copy-start.4 = (f32[320,512]{1,0:T(8,128)S(1)}, f32[320,512]{1,0:T(8,128)}, u32[]{:S(2)}) copy-start(f32[320,512]{1,0:T(8,128)} %copy-done.2) | copy-start | bytes 1966084
  127.7 6.2 %copy-start.5 = (f32[1,512,320]{1,2,0:T(8,128)S(1)}, f32[1,512,320]{1,2,0:T(8,128)}, u32[]{:S(2)}) copy-start(f32[1,512,320]{1,2,0:T(8,128)} %param.15) | copy-start | bytes 1966084
  127.7 6.2 %copy-start.6 = (f32[1,512,320]{1,2,0:T(8,128)S(1)}, f32[1,512,320]{1,2,0:T(8,128)}, u32[]{:S(2)}) copy-start(f32[1,512,320]{1,2,0:T(8,128)} %param.16) | copy-start | bytes 1966084
  129.9 4.0 %collective-permute-start.5 = (f32[320,512]{1,0:T(8,128)S(1)}, f32[320,512]{1,0:T(8,128)S(1)}, u32[]{:S(2)}, u32[]{:S(2)}) collective-permute-start(f32[320,512]{1,0:T(8,128)S(1)} %get-tuple-element.14.mine_ref), channel_id=1, source_target_pairs={{0,256},{1,257},{2,258},{3,259},{4,260},{5,261},{6,262},{7,263},{8... | collective-permute-start | bytes 1966088 | tf_op jit(solution)/shard_map/ppermute | solution.py:46
  149.7 11.8 %collective-permute-start.6 = (bf16[8,320]{1,0:T(8,128)(2,1)S(1)}, bf16[8,320]{1,0:T(8,128)(2,1)S(1)}, u32[]{:S(2)}, u32[]{:S(2)}) collective-permute-start(bf16[8,320]{1,0:T(8,128)(2,1)S(1)} %reduce_sum.9), channel_id=1, source_target_pairs={{0,0},{1,16},{2,32},{3,48},{4,64},{5,80},{6,96},{7,112},{8,128},{9... | collective-permute-start | bytes 15368 | tf_op jit(solution)/shard_map/ppermute | solution.py:46

commit v7 on v4

--- a/solution.py
+++ b/solution.py
@@ -50,7 +50,7 @@
 
 
 def along_y(step):
-    return lambda g, y, zh, zl, x: (g, (y + step) % 8, zh, zl, x)
+    return lambda g, y, zh, zl, x: (g, (y + (step if g == 1 else -step)) % 8, zh, zl, x)
 
 
 def transposed(g, y, zh, zl, x):
@@ -66,7 +66,7 @@
 
 
 def along_x(step):
-    return lambda g, y, zh, zl, x: (g, y, zh, zl, (x + step) % 4)
+    return lambda g, y, zh, zl, x: (g, y, zh, zl, (x + (step if g == 1 else -step)) % 4)
 
 
 def other_core(g, y, zh, zl, x):
@@ -79,21 +79,6 @@
 
 HOPS = (0, 1, 2, 3, 4, -1, -2, -3)
 FLIPS = (0, 3, 1, 2)
-
-
-def device_table():
-    table = np.zeros((512, 64), np.int32)
-    for flat, (g, y, zh, zl, x) in enumerate(np.ndindex(*SHAPE)):
-        start = (zl * 4 + x) * COLS
-        table[flat, :3] = g, start // 128, start % 128
-        for n, hop in enumerate(HOPS):
-            for other in range(2):
-                block_y, block_zh = (y - hop) % 8, zh ^ other
-                at = n * 2 + other
-                table[flat, 16 + at] = block_y * 2 + block_zh
-                table[flat, 32 + at] = (2 * (block_y & 1) + block_zh - x) % 4
-                table[flat, 48 + at] = FLIPS.index(zl ^ (block_y >> 1))
-    return table
 
 
 def attend_kernel(
@@ -181,57 +166,59 @@
 HBM = pl.BlockSpec(memory_space=pl.ANY)
 
 
-def half_kernel(table_ref, act_ref, act_got, rows_ref, out_ref):
-    @pl.when(table_ref[0] == 1)
+def half_kernel(place_ref, act_ref, act_got, rows_ref, out_ref):
+    @pl.when(place_ref[0] == 1)
     def _():
         out_ref[:HALF, :] = act_ref[:HALF, :]
 
-    @pl.when(table_ref[0] == 0)
+    @pl.when(place_ref[0] == 0)
     def _():
         out_ref[:HALF, :] = act_got[HALF:, :]
 
     out_ref[HALF:, :] = rows_ref[...]
 
 
-def half_of(table, *parts):
+def half_of(place, *parts):
     return pl.pallas_call(
         half_kernel,
         out_shape=jax.ShapeDtypeStruct((HALF + PAD, FEAT), bf16),
         in_specs=[SMEM] + [VMEM] * 3,
         out_specs=VMEM,
         name="half",
-    )(table, *parts)
-
-
-def base_kernel(mine_ref, got_ref, out_ref):
+    )(place, *parts)
+
+
+def base_kernel(mine_ref, got_ref, *refs):
+    out_ref = refs[-1]
     out_ref[:HALF, :] = mine_ref[:HALF, :]
     out_ref[HALF:TOK, :] = got_ref[:HALF, :]
     rows = [ref[HALF:, :].astype(f32)[:ROWS] for ref in (mine_ref, got_ref)]
     out_ref[TOK:, :] = jnp.concatenate(rows, axis=0).astype(bf16)
 
 
-def base_of(*parts):
+def base_of(parts, others):
     return pl.pallas_call(
         base_kernel,
         out_shape=jax.ShapeDtypeStruct((TOK + PAD, FEAT), bf16),
-        in_specs=[VMEM] * 2,
+        in_specs=[VMEM] * 2 + [HBM] * len(others),
         out_specs=VMEM,
         name="base",
-    )(*parts)
-
-
-def cut_kernel(table_ref, cot_ref, one_ref, two_ref, window, turned, sem):
-    start = pl.multiple_of(table_ref[1] * 128, 128)
+    )(*parts, *others)
+
+
+def cut_kernel(place_ref, cot_ref, one_ref, two_ref, window, turned, sem):
+    q = place_ref[3] * 4 + place_ref[4]
+    start = pl.multiple_of(((q * 5) >> 1) * 128, 128)
     copy = pltpu.make_async_copy(cot_ref.at[:, pl.ds(start, 384)], window, sem)
     copy.start()
     copy.wait()
     turned[...] = window[...].astype(f32).T
-    place = pl.ds(pl.multiple_of(table_ref[2], 64), COLS)
+    place = pl.ds(pl.multiple_of((q & 1) * 64, 64), COLS)
     one_ref[...] = turned[place, :HALF].astype(bf16)
     two_ref[...] = turned[place, HALF:].astype(bf16)
 
 
-def cut_of(table, cot):
+def cut_of(place, cot):
     shape = jax.ShapeDtypeStruct((COLS, HALF), bf16)
     return pl.pallas_call(
         cut_kernel,
@@ -244,10 +231,10 @@
             pltpu.SemaphoreType.DMA(()),
         ],
         name="cut",
-    )(table, cot)
-
-
-def gradient_kernel(table_ref, *refs):
+    )(place, cot)
+
+
+def gradient_kernel(place_ref, *refs):
     chunks, blocks, (out_ref, rows_ref) = refs[:8], refs[8:12], refs[-7:-5]
     chunk_rows, block_tiles, block_rows, row_tiles, sems = refs[-5:]
     copies = [
@@ -267,10 +254,17 @@
         copy.start()
     for copy in copies:
         copy.wait()
+    side, y, z_hi, z_lo, x = (place_ref[n] for n in range(5))
+    places = []
     for at in range(16):
-        block_rows[:, at * HALF : (at + 1) * HALF] = block_tiles[
-            table_ref[32 + at], table_ref[48 + at]
-        ]
+        hop, block_zh = HOPS[at // 2], (z_hi if at % 2 == 0 else 1 - z_hi)
+        block_y = jnp.where(side == 1, y - hop, y + hop) & 7
+        source = 2 * (block_y & 1) + block_zh - x
+        source = jnp.where(side == 1, -source, source) & 3
+        flip = z_lo ^ (block_y >> 1)
+        slot = sum(jnp.where(flip == f, n, 0) for n, f in enumerate(FLIPS))
+        block_rows[:, at * HALF : (at + 1) * HALF] = block_tiles[source, slot]
+        places.append(2 * block_y + block_zh)
     for half in range(2):
         for n in range(4 * half, 4 * half + 4):
             act_copies[n].wait()
@@ -284,11 +278,11 @@
         row_copies[n].wait()
         rows = row_tiles[n].astype(f32)
         for other in range(2):
-            place = pl.multiple_of(table_ref[16 + 2 * n + other] * ROWS, ROWS)
+            place = pl.multiple_of(places[2 * n + other] * ROWS, ROWS)
             rows_ref[pl.ds(place, ROWS), :] = rows[other * ROWS : (other + 1) * ROWS]
 
 
-def gradient(table, chunks, blocks, others):
+def gradient(place, chunks, blocks, others):
     operands = (*chunks, *blocks, *others)
     return pl.pallas_call(
         gradient_kernel,
@@ -310,13 +304,13 @@
             flops=2 * 8 * TOK * COLS * FEAT, bytes_accessed=6 * 2**20, transcendentals=0
         ),
         name="gradient",
-    )(table, *operands)
+    )(place, *operands)
 
 
 def step_kernel(
-    table_ref, mine_ref, got_ref, rows_ref, one_ref, one_got, two_ref, two_got, weight_ref, update_ref, out_ref
+    place_ref, mine_ref, got_ref, rows_ref, one_ref, one_got, two_ref, two_got, weight_ref, update_ref, out_ref
 ):
-    learner = table_ref[0] == 1
+    learner = place_ref[0] == 1
     grad = mine_ref[...] + got_ref[...]
     moment_one = jnp.where(learner, one_ref[...], one_got[...])
     moment_two = jnp.where(learner, two_ref[...], two_got[...])
@@ -335,7 +329,7 @@
     out_ref[...] = part.reshape(16, ROWS, COLS)
 
 
-def step(table, mine, got, rows, one, one_got, two, two_got, weight):
+def step(place, mine, got, rows, one, one_got, two, two_got, weight):
     return pl.pallas_call(
         step_kernel,
         out_shape=(
@@ -346,7 +340,7 @@
         out_specs=(VMEM, VMEM),
         compiler_params=pltpu.CompilerParams(vmem_limit_bytes=32 * 2**20),
         name="step",
-    )(table, mine, got, rows, one, one_got, two, two_got, weight)
+    )(place, mine, got, rows, one, one_got, two, two_got, weight)
 
 
 def local(
@@ -363,8 +357,8 @@
     lengths,
     token_ids,
 ):
-    flat, q = lax.axis_index(AXES), lax.axis_index(TENSOR)
-    table = lax.dynamic_slice_in_dim(jnp.asarray(device_table()), flat, 1, 0)[0]
+    q = lax.axis_index(TENSOR)
+    place = jnp.stack([lax.axis_index(axis) for axis in AXES]).astype(jnp.int32)
 
     act = activations[0]
     act_got = permute(act, to_rollout)
@@ -378,41 +372,42 @@
         lengths,
         token_ids.T,
     )
-    half = half_of(table, act, act_got, rows)
-    base = base_of(half, permute(half, to_partner))
-
-    cut_one, cut_two = cut_of(table, cotangent[0])
-    own = permute(cut_one, cot_transposed(1)), permute(cut_two, cot_transposed(0))
-
-    up, down = [base], [base]
-    up.append(permute(base, along_y(1)))
-    down.append(permute(base, along_y(-1)))
-
-    own_one, own_two, _ = lax.optimization_barrier((*own, base))
-    own = jnp.where(table[0] == 1, own_one, own_two)
-    two_blocks = jnp.stack([own, permute(own, along_zl(3))])
-    up.append(permute(up[-1], along_y(1)))
-    down.append(permute(down[-1], along_y(-1)))
-    four = jnp.concatenate([two_blocks, permute(two_blocks, along_zl(1))], axis=0)
-    blocks = (
-        four,
-        permute(four, along_x(-1)),
-        permute(four, along_x(2)),
-        permute(four, along_x(1)),
-    )
-    up.append(permute(up[-1], along_y(1)))
-    down.append(permute(down[-1], along_y(-1)))
-    up.append(permute(up[-1], along_y(1)))
-    chunks = up + down[1:]
+    half = half_of(place, act, act_got, rows)
+    half_got = permute(half, to_partner)
+
+    cut_one, cut_two = cut_of(place, cotangent[0])
+    own_one = permute(cut_one, cot_transposed(1))
+    own_two = permute(cut_two, cot_transposed(0))
 
     one, two = moment_one[0].T, moment_two[0].T
-    one_tied, two_tied, _ = lax.optimization_barrier((one, two, base))
+    one_tied, two_tied, _, _ = lax.optimization_barrier((one, two, cut_one, half))
     one_got = permute(one_tied, to_rollout)
     two_got = permute(two_tied, to_rollout)
-
-    mine, all_rows = gradient(table, chunks, blocks, (one_got, two_got))
+    base = base_of((half, half_got), (one_got, two_got, cut_one, cut_two))
+
+    first, second = [base], [base]
+    first.append(permute(base, along_y(1)))
+    second.append(permute(base, along_y(-1)))
+    own_one, own_two, first[1] = lax.optimization_barrier((own_one, own_two, first[1]))
+    first.append(permute(first[1], along_y(1)))
+    own = jnp.where(place[0] == 1, own_one, own_two)
+    two_blocks = jnp.stack([own, permute(own, along_zl(3))])
+    two_blocks, second[1] = lax.optimization_barrier((two_blocks, second[1]))
+    second.append(permute(second[1], along_y(-1)))
+    two_got_blocks = permute(two_blocks, along_zl(1))
+    two_got_blocks, first[2] = lax.optimization_barrier((two_got_blocks, first[2]))
+    first.append(permute(first[2], along_y(1)))
+    four = jnp.concatenate([two_blocks, two_got_blocks], axis=0)
+    four, second[2] = lax.optimization_barrier((four, second[2]))
+    second.append(permute(second[2], along_y(-1)))
+    blocks = [four] + [permute(four, along_x(step)) for step in (1, 2, -1)]
+    blocks[1], first[3] = lax.optimization_barrier((blocks[1], first[3]))
+    first.append(permute(first[3], along_y(1)))
+    chunks = first + second[1:]
+
+    mine, all_rows = gradient(place, chunks, blocks, ())
     got = permute(mine, other_core)
-    update, partial = step(table, mine, got, all_rows, one, one_got, two, two_got, weight.T)
+    update, partial = step(place, mine, got, all_rows, one, one_got, two, two_got, weight.T)
 
     shares = lax.all_to_all(partial, TENSOR, split_axis=0, concat_axis=0, tiled=True)
     summed = jnp.sum(shares, axis=0).astype(bf16)

time: 147 us -> 157 us (1.068)
  the two profiles are of different devices: /device:TPU:2 before, /device:TPU:16 now
where the time goes in v7:
time: 157 us
  starting transfers between devices  67.4 us (43%)
  blocking collectives  35.9 us (23%)
  waiting for transfers between devices  34.3 us (22%)
  Pallas kernels  13.6 us (9%)
  local copies, waits for them, and re-layouts  4.28 us (3%)
    ppermute x20, starting transfers between devices, permute(): return lax.ppermute(value, AXES, pairs)  67.4 us
    ppermute x20, waiting for transfers between devices, permute(): return lax.ppermute(value, AXES, pairs)  34.3 us
    all_to_all x1, blocking collectives, local(): lax.all_to_all(partial, TENSOR, split_axis=0, concat_axis=0, tiled=True)  18.2 us
    all_to_all x1, blocking collectives, local(): lax.all_to_all(spread, TENSOR, split_axis=0, concat_axis=0, tiled=True)  17.7 us
  transfers between devices with their start and end apart: 20, of which 9 were waited for; matrix products, arithmetic and copies ran while one was open for 0% of the time, Pallas kernels for 3%

profile of v7, /device:TPU:16, one launch (start us, length us, event | category | flops | bytes accessed | tf_op | source)
XLA Modules:
  0.0 156.5 jit_solution(12107699723349488700)
XLA Ops:
  0.6 1.3 collective-permute-start
  1.9 0.7 stack.32.place_ref
  2.6 2.5 %cut.1 = (bf16[320,128]{1,0:T(8,128)(2,1)}, bf16[320,128]{1,0:T(8,128)(2,1)}) custom-call(s32[5]{0:T(128)} %stack.32.place_ref, bf16[256,5120]{1,0:T(8,128)(2,1)} %bitcast.25), custom_call_target="tpu_custom_call" | custom-call | tf_op jit(solution)/shard_map/cut/pallas_call | solution.py:223
  5.1 0.0 copy-start.12
  5.2 0.0 copy-start.11
  5.2 0.0 copy-start.8
  5.2 2.9 %attend.1.rows_ref = bf16[16,512]{1,0:T(8,128)(2,1)} custom-call(s32[1]{0:T(128)} %bitcast.6.head_ref, s32[2]{0:T(128)} %lengths_ref.1, s32[2,4]{1,0:T(2,128)} %bitcast.31, bf16[4,2,512]{2,1,0:T(2,128)(2,1)} %q_ref.1, bf16[2,2048,128]{2,1,0:T(8,128)(2,1)} %k_ref.1, bf16[2,2048,128]{2,1,0:T(8,128)(2,1)} %v_ref.1, bf16[4,2,1024]{2,1,0:T(2,128)(2,1)} %nk_ref.1, ...), custom_call_target="tpu_custom_call" | custom-call | tf_op jit(solution)/shard_map/attend/pallas_call | solution.py:146
  8.1 0.0 collective-permute-done.act_got
  8.1 0.7 copy-done.9
  8.8 1.7 %half.1.mine_ref = bf16[144,512]{1,0:T(8,128)(2,1)} custom-call(s32[5]{0:T(128)} %stack.32.place_ref, bf16[256,512]{1,0:T(8,128)(2,1)} %bitcast.29, bf16[256,512]{1,0:T(8,128)(2,1)} %copy-done.9, bf16[16,512]{1,0:T(8,128)(2,1)} %attend.1.rows_ref), custom_call_target="tpu_custom_call" | custom-call | tf_op jit(solution)/shard_map/half/pallas_call | solution.py:182
  10.5 0.0 copy-done.5
  10.5 1.3 collective-permute-start.2
  11.8 0.0 copy-done.6
  11.8 1.3 collective-permute-start.3
  13.1 10.9 %collective-permute-start.1 = (bf16[144,512]{1,0:T(8,128)(2,1)}, bf16[144,512]{1,0:T(8,128)(2,1)S(1)}, u32[]{:S(2)}, u32[]{:S(2)}) collective-permute-start(bf16[144,512]{1,0:T(8,128)(2,1)} %half.1.mine_ref), channel_id=1, source_target_pairs={{0,16},{1,17},{2,18},{3,19},{4,20},{5,21},{6,22},{7,23},{8,24},{9,... | collective-permute-start | bytes 442376 | tf_op jit(solution)/shard_map/ppermute | solution.py:45
  24.0 4.5 %collective-permute-done.1.got_ref = bf16[144,512]{1,0:T(8,128)(2,1)S(1)} collective-permute-done((bf16[144,512]{1,0:T(8,128)(2,1)}, bf16[144,512]{1,0:T(8,128)(2,1)S(1)}, u32[]{:S(2)}, u32[]{:S(2)}) %collective-permute-start.1) | collective-permute-done | bytes 147488 | tf_op jit(solution)/shard_map/ppermute | solution.py:45
  28.6 0.0 collective-permute-done.2.refs_0_.one_got
  28.6 0.0 collective-permute-done.3.refs_1_.two_got
  28.6 0.6 copy-done.10
  29.2 0.2 copy-done
  29.5 0.2 copy-done.2
  29.7 1.8 %base.1.refs_0_ = bf16[272,512]{1,0:T(8,128)(2,1)} custom-call(bf16[144,512]{1,0:T(8,128)(2,1)} %half.1.mine_ref, bf16[144,512]{1,0:T(8,128)(2,1)} %copy-done.10, f32[320,512]{1,0:T(8,128)} %copy-done, f32[320,512]{1,0:T(8,128)} %copy-done.2, bf16[320,128]{1,0:T(8,128)(2,1)} %get-tuple-element.21.refs_2_, bf16[320,128]{1,0:T(8,128)(2,1)} %get-tuple-element.24.refs_3_), custom_call_target="tpu_custom_call" | custom-call | tf_op jit(solution)/shard_map/base/pallas_call | solution.py:200
  31.5 2.5 %collective-permute-start.6 = (bf16[272,512]{1,0:T(8,128)(2,1)}, bf16[272,512]{1,0:T(8,128)(2,1)S(1)}, u32[]{:S(2)}, u32[]{:S(2)}) collective-permute-start(bf16[272,512]{1,0:T(8,128)(2,1)} %base.1.refs_0_), channel_id=1, source_target_pairs={{0,224},{1,225},{2,226},{3,227},{4,228},{5,229},{6,230},{7,231},{8... | collective-permute-start | bytes 835592 | tf_op jit(solution)/shard_map/ppermute | solution.py:45
  34.0 0.0 copy-done.12
  34.0 1.3 collective-permute-start.5
  35.3 0.0 copy-done.11
  35.3 1.3 collective-permute-start.4
  36.6 3.5 %collective-permute-start.8 = (bf16[272,512]{1,0:T(8,128)(2,1)}, bf16[272,512]{1,0:T(8,128)(2,1)S(1)}, u32[]{:S(2)}, u32[]{:S(2)}) collective-permute-start(bf16[272,512]{1,0:T(8,128)(2,1)} %base.1.refs_0_), channel_id=1, source_target_pairs={{0,32},{1,33},{2,34},{3,35},{4,36},{5,37},{6,38},{7,39},{8,40},{9,... | collective-permute-start | bytes 835592 | tf_op jit(solution)/shard_map/ppermute | solution.py:45
  40.0 4.5 %collective-permute-done.5 = bf16[320,128]{1,0:T(8,128)(2,1)S(1)} collective-permute-done((bf16[320,128]{1,0:T(8,128)(2,1)S(1)}, bf16[320,128]{1,0:T(8,128)(2,1)S(1)}, u32[]{:S(2)}, u32[]{:S(2)}) %collective-permute-start.5) | collective-permute-done | bytes 81952 | tf_op jit(solution)/shard_map/ppermute | solution.py:45
  44.5 0.0 collective-permute-done.4
  44.6 0.0 collective-permute-done.6.refs_1_
  44.6 7.7 %collective-permute-start.7 = (bf16[320,128]{1,0:T(8,128)(2,1)S(1)}, bf16[320,128]{1,0:T(8,128)(2,1)S(1)}, u32[]{:S(2)}, u32[]{:S(2)}) collective-permute-start(bf16[320,128]{1,0:T(8,128)(2,1)S(1)} %broadcast_select_fusion), channel_id=1, source_target_pairs={{0,12},{1,13},{2,14},{3,15},{4,8},{5,9},{6,10},{7,11},{8,4},{9,5},... | collective-permute-start | bytes 245768 | tf_op jit(solution)/shard_map/ppermute | solution.py:45
  52.3 5.3 %collective-permute-start.10 = (bf16[272,512]{1,0:T(8,128)(2,1)S(1)}, bf16[272,512]{1,0:T(8,128)(2,1)S(1)}, u32[]{:S(2)}, u32[]{:S(2)}) collective-permute-start(bf16[272,512]{1,0:T(8,128)(2,1)S(1)} %collective-permute-done.6.refs_1_), channel_id=1, source_target_pairs={{0,224},{1,225},{2,226},{3,227},{4,228},{5,229},{6,230},{7,231},{8... | collective-permute-start | bytes 835592 | tf_op jit(solution)/shard_map/ppermute | solution.py:45
  57.7 0.0 collective-permute-done.7
  57.7 0.0 collective-permute-done.8.refs_5_
  57.7 3.1 %collective-permute-start.9 = (bf16[2,320,128]{2,1,0:T(8,128)(2,1)S(1)}, bf16[2,320,128]{2,1,0:T(8,128)(2,1)S(1)}, u32[]{:S(2)}, u32[]{:S(2)}) collective-permute-start(bf16[2,320,128]{2,1,0:T(8,128)(2,1)S(1)} %pad_maximum_fusion.1), channel_id=1, source_target_pairs={{0,4},{1,5},{2,6},{3,7},{4,0},{5,1},{6,2},{7,3},{8,12},{9,13},{10,... | collective-permute-start | bytes 491528 | tf_op jit(solution)/shard_map/ppermute | solution.py:45
  60.8 2.6 %collective-permute-start.11 = (bf16[272,512]{1,0:T(8,128)(2,1)S(1)}, bf16[272,512]{1,0:T(8,128)(2,1)S(1)}, u32[]{:S(2)}, u32[]{:S(2)}) collective-permute-start(bf16[272,512]{1,0:T(8,128)(2,1)S(1)} %collective-permute-done.8.refs_5_), channel_id=1, source_target_pairs={{0,32},{1,33},{2,34},{3,35},{4,36},{5,37},{6,38},{7,39},{8,40},{9,... | collective-permute-start | bytes 835592 | tf_op jit(solution)/shard_map/ppermute | solution.py:45
  63.4 2.3 %collective-permute-done.9 = bf16[2,320,128]{2,1,0:T(8,128)(2,1)S(1)} collective-permute-done((bf16[2,320,128]{2,1,0:T(8,128)(2,1)S(1)}, bf16[2,320,128]{2,1,0:T(8,128)(2,1)S(1)}, u32[]{:S(2)}, u32[]{:S(2)}) %collective-permute-start.9) | collective-permute-done | bytes 163872 | tf_op jit(solution)/shard_map/ppermute | solution.py:45
  65.8 0.0 collective-permute-done.10.refs_2_
  65.8 6.1 %collective-permute-done.11.refs_6_ = bf16[272,512]{1,0:T(8,128)(2,1)S(1)} collective-permute-done((bf16[272,512]{1,0:T(8,128)(2,1)S(1)}, bf16[272,512]{1,0:T(8,128)(2,1)S(1)}, u32[]{:S(2)}, u32[]{:S(2)}) %collective-permute-start.11) | collective-permute-done | bytes 278560 | tf_op jit(solution)/shard_map/ppermute | solution.py:45
  71.9 4.8 %collective-permute-start.12 = (bf16[4,320,128]{2,1,0:T(8,128)(2,1)S(1)}, bf16[4,320,128]{2,1,0:T(8,128)(2,1)S(1)}, u32[]{:S(2)}, u32[]{:S(2)}) collective-permute-start(bf16[4,320,128]{2,1,0:T(8,128)(2,1)S(1)} %pad_maximum_fusion.refs_8_), channel_id=1, source_target_pairs={{0,3},{1,0},{2,1},{3,2},{4,7},{5,4},{6,5},{7,6},{8,11},{9,8},{10,9... | collective-permute-start | bytes 983048 | tf_op jit(solution)/shard_map/ppermute | solution.py:45
  76.7 4.4 %collective-permute-start.13 = (bf16[272,512]{1,0:T(8,128)(2,1)S(1)}, bf16[272,512]{1,0:T(8,128)(2,1)S(1)}, u32[]{:S(2)}, u32[]{:S(2)}) collective-permute-start(bf16[272,512]{1,0:T(8,128)(2,1)S(1)} %collective-permute-done.10.refs_2_), channel_id=1, source_target_pairs={{0,224},{1,225},{2,226},{3,227},{4,228},{5,229},{6,230},{7,231},{8... | collective-permute-start | bytes 835592 | tf_op jit(solution)/shard_map/ppermute | solution.py:45
  81.2 1.9 %collective-permute-start.17 = (bf16[4,320,128]{2,1,0:T(8,128)(2,1)S(1)}, bf16[4,320,128]{2,1,0:T(8,128)(2,1)S(1)}, u32[]{:S(2)}, u32[]{:S(2)}) collective-permute-start(bf16[4,320,128]{2,1,0:T(8,128)(2,1)S(1)} %pad_maximum_fusion.refs_8_), channel_id=1, source_target_pairs={{0,1},{1,2},{2,3},{3,0},{4,5},{5,6},{6,7},{7,4},{8,9},{9,10},{10,1... | collective-permute-start | bytes 983048 | tf_op jit(solution)/shard_map/ppermute | solution.py:45
  83.1 4.0 %collective-permute-start.16 = (bf16[4,320,128]{2,1,0:T(8,128)(2,1)S(1)}, bf16[4,320,128]{2,1,0:T(8,128)(2,1)S(1)}, u32[]{:S(2)}, u32[]{:S(2)}) collective-permute-start(bf16[4,320,128]{2,1,0:T(8,128)(2,1)S(1)} %pad_maximum_fusion.refs_8_), channel_id=1, source_target_pairs={{0,2},{1,3},{2,0},{3,1},{4,6},{5,7},{6,4},{7,5},{8,10},{9,11},{10,... | collective-permute-start | bytes 983048 | tf_op jit(solution)/shard_map/ppermute | solution.py:45
  87.1 3.5 %collective-permute-start.15 = (bf16[272,512]{1,0:T(8,128)(2,1)S(1)}, bf16[272,512]{1,0:T(8,128)(2,1)S(1)}, u32[]{:S(2)}, u32[]{:S(2)}) collective-permute-start(bf16[272,512]{1,0:T(8,128)(2,1)S(1)} %collective-permute-done.11.refs_6_), channel_id=1, source_target_pairs={{0,32},{1,33},{2,34},{3,35},{4,36},{5,37},{6,38},{7,39},{8,40},{9,... | collective-permute-start | bytes 835592 | tf_op jit(solution)/shard_map/ppermute | solution.py:45
  90.7 0.0 collective-permute-done.13.refs_3_
  90.7 0.0 collective-permute-done.12.refs_9_
  90.7 2.6 %collective-permute-start.14 = (bf16[272,512]{1,0:T(8,128)(2,1)S(1)}, bf16[272,512]{1,0:T(8,128)(2,1)S(1)}, u32[]{:S(2)}, u32[]{:S(2)}) collective-permute-start(bf16[272,512]{1,0:T(8,128)(2,1)S(1)} %collective-permute-done.13.refs_3_), channel_id=1, source_target_pairs={{0,224},{1,225},{2,226},{3,227},{4,228},{5,229},{6,230},{7,231},{8... | collective-permute-start | bytes 835592 | tf_op jit(solution)/shard_map/ppermute | solution.py:45
  93.3 2.6 %collective-permute-done.15.refs_7_ = bf16[272,512]{1,0:T(8,128)(2,1)S(1)} collective-permute-done((bf16[272,512]{1,0:T(8,128)(2,1)S(1)}, bf16[272,512]{1,0:T(8,128)(2,1)S(1)}, u32[]{:S(2)}, u32[]{:S(2)}) %collective-permute-start.15) | collective-permute-done | bytes 278560 | tf_op jit(solution)/shard_map/ppermute | solution.py:45
  95.9 0.0 collective-permute-done.17.refs_11_
  95.9 3.4 %collective-permute-done.16.refs_10_ = bf16[4,320,128]{2,1,0:T(8,128)(2,1)S(1)} collective-permute-done((bf16[4,320,128]{2,1,0:T(8,128)(2,1)S(1)}, bf16[4,320,128]{2,1,0:T(8,128)(2,1)S(1)}, u32[]{:S(2)}, u32[]{:S(2)}) %collective-permute-start.16) | collective-permute-done | bytes 327712 | tf_op jit(solution)/shard_map/ppermute | solution.py:45
  99.2 3.5 %collective-permute-done.14.refs_4_ = bf16[272,512]{1,0:T(8,128)(2,1)S(1)} collective-permute-done((bf16[272,512]{1,0:T(8,128)(2,1)S(1)}, bf16[272,512]{1,0:T(8,128)(2,1)S(1)}, u32[]{:S(2)}, u32[]{:S(2)}) %collective-permute-start.14) | collective-permute-done | bytes 278560 | tf_op jit(solution)/shard_map/ppermute | solution.py:45
  102.8 1.0 copy-done.4
  103.7 2.8 %gradient.1 = (f32[320,512]{1,0:T(8,128)S(1)}, f32[128,512]{1,0:T(8,128)S(1)}) custom-call(s32[5]{0:T(128)S(1)} %copy-done.8, bf16[272,512]{1,0:T(8,128)(2,1)S(1)} %copy-done.4, bf16[272,512]{1,0:T(8,128)(2,1)S(1)} %collective-permute-done.6.refs_1_, bf16[272,512]{1,0:T(8,128)(2,1)S(1)} %collective-permute-done.10.refs_2_, ...), custom_call_target="tpu_custom_call" | custom-call | flops 671088640 | bytes 6291456 | tf_op jit(solution)/shard_map/gradient/pallas_call | solution.py:287
  106.5 2.0 %collective-permute-start.18 = (f32[320,512]{1,0:T(8,128)S(1)}, f32[320,512]{1,0:T(8,128)S(1)}, u32[]{:S(2)}, u32[]{:S(2)}) collective-permute-start(f32[320,512]{1,0:T(8,128)S(1)} %get-tuple-element.36.mine_ref), channel_id=1, source_target_pairs={{0,256},{1,257},{2,258},{3,259},{4,260},{5,261},{6,262},{7,263},{8... | collective-permute-start | bytes 1966088 | tf_op jit(solution)/shard_map/ppermute | solution.py:45
  108.5 1.9 %collective-permute-done.18.got_ref = f32[320,512]{1,0:T(8,128)S(1)} collective-permute-done((f32[320,512]{1,0:T(8,128)S(1)}, f32[320,512]{1,0:T(8,128)S(1)}, u32[]{:S(2)}, u32[]{:S(2)}) %collective-permute-start.18) | collective-permute-done | bytes 655392 | tf_op jit(solution)/shard_map/ppermute | solution.py:45
  110.5 0.0 copy-done.7
  110.5 0.0 copy-done.3
  110.5 1.9 %step.1 = (bf16[320,512]{1,0:T(8,128)(2,1)}, f32[16,8,320]{2,1,0:T(8,128)S(1)}) custom-call(s32[5]{0:T(128)S(1)} %copy-done.8, f32[320,512]{1,0:T(8,128)S(1)} %get-tuple-element.36.mine_ref, f32[320,512]{1,0:T(8,128)S(1)} %collective-permute-done.18.got_ref, f32[128,512]{1,0:T(8,128)S(1)} %get-tuple-element.37.rows_ref, f32[320,512]{1,0:T(8,128)S(1)} %bitcast.21, ...), custom_call_target="tpu_custom_call" | custom-call | tf_op jit(solution)/shard_map/step/pallas_call | solution.py:333
  112.4 18.2 %all_to_all.10 = f32[16,8,320]{2,1,0:T(8,128)S(1)} all-to-all(f32[16,8,320]{2,1,0:T(8,128)S(1)} %get-tuple-element.39), channel_id=1, replica_groups=mesh['group'=2,'y'=8,'z_hi'=2,'z_lo'=4,'x'=4] {'z_lo','x'}, dimensions={0} | all-to-all | bytes 327680 | tf_op jit(solution)/shard_map/all_to_all | solution.py:412
  130.7 1.9 %collective-permute-start.19 = (bf16[8,320]{1,0:T(8,128)(2,1)S(1)}, bf16[8,320]{1,0:T(8,128)(2,1)S(1)}, u32[]{:S(2)}, u32[]{:S(2)}) collective-permute-start(bf16[8,320]{1,0:T(8,128)(2,1)S(1)} %reduce_sum.9), channel_id=1, source_target_pairs={{0,0},{1,16},{2,32},{3,48},{4,64},{5,80},{6,96},{7,112},{8,128},{9... | collective-permute-start | bytes 15368 | tf_op jit(solution)/shard_map/ppermute | solution.py:45
  132.6 5.4 %collective-permute-done.19 = bf16[8,320]{1,0:T(8,128)(2,1)S(1)} collective-permute-done((bf16[8,320]{1,0:T(8,128)(2,1)S(1)}, bf16[8,320]{1,0:T(8,128)(2,1)S(1)}, u32[]{:S(2)}, u32[]{:S(2)}) %collective-permute-start.19) | collective-permute-done | bytes 5152 | tf_op jit(solution)/shard_map/ppermute | solution.py:45
  138.0 17.7 %all_to_all.11 = bf16[16,8,320]{2,1,0:T(8,128)(2,1)S(1)} all-to-all(bf16[16,8,320]{2,1,0:T(8,128)(2,1)S(1)} %broadcast_in_dim.2), channel_id=1, replica_groups=mesh['group'=2,'y'=8,'z_hi'=2,'z_lo'=4,'x'=4] {'z_lo','x'}, dimensions={0} | all-to-all | bytes 163840 | tf_op jit(solution)/shard_map/all_to_all | solution.py:416
  155.7 0.8 reshape.12
  (18 shorter events, 0.1 us)
Async XLA Ops:
  0.6 7.5 %collective-permute-start = (bf16[256,512]{1,0:T(8,128)(2,1)}, bf16[256,512]{1,0:T(8,128)(2,1)S(1)}, u32[]{:S(2)}, u32[]{:S(2)}) collective-permute-start(bf16[256,512]{1,0:T(8,128)(2,1)} %bitcast.28), channel_id=1, source_target_pairs={{256,0},{257,1},{258,2},{259,3},{260,4},{261,5},{262,6},{263,7},{2... | collective-permute-start | bytes 786440 | tf_op jit(solution)/shard_map/ppermute | solution.py:45
  2.6 7.9 %copy-start.5 = (f32[1,512,320]{1,2,0:T(8,128)S(1)}, f32[1,512,320]{1,2,0:T(8,128)}, u32[]{:S(2)}) copy-start(f32[1,512,320]{1,2,0:T(8,128)} %param.15) | copy-start | bytes 1966084
  2.6 9.2 %copy-start.6 = (f32[1,512,320]{1,2,0:T(8,128)S(1)}, f32[1,512,320]{1,2,0:T(8,128)}, u32[]{:S(2)}) copy-start(f32[1,512,320]{1,2,0:T(8,128)} %param.16) | copy-start | bytes 1966084
  5.1 28.8 %copy-start.12 = (bf16[320,128]{1,0:T(8,128)(2,1)S(1)}, bf16[320,128]{1,0:T(8,128)(2,1)}, u32[]{:S(2)}) copy-start(bf16[320,128]{1,0:T(8,128)(2,1)} %get-tuple-element.24.refs_3_) | copy-start | bytes 245764
  5.2 30.1 %copy-start.11 = (bf16[320,128]{1,0:T(8,128)(2,1)S(1)}, bf16[320,128]{1,0:T(8,128)(2,1)}, u32[]{:S(2)}) copy-start(bf16[320,128]{1,0:T(8,128)(2,1)} %get-tuple-element.21.refs_2_) | copy-start | bytes 245764
  5.2 97.6 %copy-start.8 = (s32[5]{0:T(128)S(1)}, s32[5]{0:T(128)}, u32[]{:S(2)}) copy-start(s32[5]{0:T(128)} %stack.32.place_ref) | copy-start | bytes 64
  8.1 0.7 copy-start.9
  10.5 18.1 %collective-permute-start.2 = (f32[320,512]{1,0:T(8,128)S(1)}, f32[320,512]{1,0:T(8,128)S(1)}, u32[]{:S(2)}, u32[]{:S(2)}) collective-permute-start(f32[320,512]{1,0:T(8,128)S(1)} %bitcast.20), channel_id=1, source_target_pairs={{256,0},{257,1},{258,2},{259,3},{260,4},{261,5},{262,6},{263,7},{2... | collective-permute-start | bytes 1966088 | tf_op jit(solution)/shard_map/ppermute | solution.py:45
  11.8 16.8 %collective-permute-start.3 = (f32[320,512]{1,0:T(8,128)S(1)}, f32[320,512]{1,0:T(8,128)S(1)}, u32[]{:S(2)}, u32[]{:S(2)}) collective-permute-start(f32[320,512]{1,0:T(8,128)S(1)} %bitcast.22), channel_id=1, source_target_pairs={{256,0},{257,1},{258,2},{259,3},{260,4},{261,5},{262,6},{263,7},{2... | collective-permute-start | bytes 1966088 | tf_op jit(solution)/shard_map/ppermute | solution.py:45
  13.1 15.5 %collective-permute-start.1 = (bf16[144,512]{1,0:T(8,128)(2,1)}, bf16[144,512]{1,0:T(8,128)(2,1)S(1)}, u32[]{:S(2)}, u32[]{:S(2)}) collective-permute-start(bf16[144,512]{1,0:T(8,128)(2,1)} %half.1.mine_ref), channel_id=1, source_target_pairs={{0,16},{1,17},{2,18},{3,19},{4,20},{5,21},{6,22},{7,23},{8,24},{9,... | collective-permute-start | bytes 442376 | tf_op jit(solution)/shard_map/ppermute | solution.py:45
  28.6 0.7 copy-start.10
  28.6 0.9 copy-start
  28.6 1.1 copy-start.2
  29.7 80.8 %copy-start.7 = (bf16[512,320]{0,1:T(8,128)(2,1)S(1)}, bf16[512,320]{0,1:T(8,128)(2,1)}, u32[]{:S(2)}) copy-start(bf16[512,320]{0,1:T(8,128)(2,1)} %param.14) | copy-start | bytes 983044
  31.5 79.0 %copy-start.1 = (f32[320,512]{1,0:T(8,128)S(1)}, f32[320,512]{1,0:T(8,128)}, u32[]{:S(2)}) copy-start(f32[320,512]{1,0:T(8,128)} %copy-done) | copy-start | bytes 1966084
  31.5 79.0 %copy-start.3 = (f32[320,512]{1,0:T(8,128)S(1)}, f32[320,512]{1,0:T(8,128)}, u32[]{:S(2)}) copy-start(f32[320,512]{1,0:T(8,128)} %copy-done.2) | copy-start | bytes 1966084
  31.5 13.1 %collective-permute-start.6 = (bf16[272,512]{1,0:T(8,128)(2,1)}, bf16[272,512]{1,0:T(8,128)(2,1)S(1)}, u32[]{:S(2)}, u32[]{:S(2)}) collective-permute-start(bf16[272,512]{1,0:T(8,128)(2,1)} %base.1.refs_0_), channel_id=1, source_target_pairs={{0,224},{1,225},{2,226},{3,227},{4,228},{5,229},{6,230},{7,231},{8... | collective-permute-start | bytes 835592 | tf_op jit(solution)/shard_map/ppermute | solution.py:45
  34.0 10.6 %collective-permute-start.5 = (bf16[320,128]{1,0:T(8,128)(2,1)S(1)}, bf16[320,128]{1,0:T(8,128)(2,1)S(1)}, u32[]{:S(2)}, u32[]{:S(2)}) collective-permute-start(bf16[320,128]{1,0:T(8,128)(2,1)S(1)} %copy-done.12), channel_id=1, source_target_pairs={{256,0},{257,16},{258,32},{259,48},{260,64},{261,80},{262,96},{263... | collective-permute-start | bytes 245768 | tf_op jit(solution)/shard_map/ppermute | solution.py:45
  35.3 9.3 %collective-permute-start.4 = (bf16[320,128]{1,0:T(8,128)(2,1)S(1)}, bf16[320,128]{1,0:T(8,128)(2,1)}, u32[]{:S(2)}, u32[]{:S(2)}) collective-permute-start(bf16[320,128]{1,0:T(8,128)(2,1)S(1)} %copy-done.11), channel_id=1, source_target_pairs={{256,256},{257,272},{258,288},{259,304},{260,320},{261,336},{262,3... | collective-permute-start | bytes 245768 | tf_op jit(solution)/shard_map/ppermute | solution.py:45
  36.6 21.1 %collective-permute-start.8 = (bf16[272,512]{1,0:T(8,128)(2,1)}, bf16[272,512]{1,0:T(8,128)(2,1)S(1)}, u32[]{:S(2)}, u32[]{:S(2)}) collective-permute-start(bf16[272,512]{1,0:T(8,128)(2,1)} %base.1.refs_0_), channel_id=1, source_target_pairs={{0,32},{1,33},{2,34},{3,35},{4,36},{5,37},{6,38},{7,39},{8,40},{9,... | collective-permute-start | bytes 835592 | tf_op jit(solution)/shard_map/ppermute | solution.py:45
  44.6 13.1 %collective-permute-start.7 = (bf16[320,128]{1,0:T(8,128)(2,1)S(1)}, bf16[320,128]{1,0:T(8,128)(2,1)S(1)}, u32[]{:S(2)}, u32[]{:S(2)}) collective-permute-start(bf16[320,128]{1,0:T(8,128)(2,1)S(1)} %broadcast_select_fusion), channel_id=1, source_target_pairs={{0,12},{1,13},{2,14},{3,15},{4,8},{5,9},{6,10},{7,11},{8,4},{9,5},... | collective-permute-start | bytes 245768 | tf_op jit(solution)/shard_map/ppermute | solution.py:45
  52.3 13.4 %collective-permute-start.10 = (bf16[272,512]{1,0:T(8,128)(2,1)S(1)}, bf16[272,512]{1,0:T(8,128)(2,1)S(1)}, u32[]{:S(2)}, u32[]{:S(2)}) collective-permute-start(bf16[272,512]{1,0:T(8,128)(2,1)S(1)} %collective-permute-done.6.refs_1_), channel_id=1, source_target_pairs={{0,224},{1,225},{2,226},{3,227},{4,228},{5,229},{6,230},{7,231},{8... | collective-permute-start | bytes 835592 | tf_op jit(solution)/shard_map/ppermute | solution.py:45
  57.7 8.1 %collective-permute-start.9 = (bf16[2,320,128]{2,1,0:T(8,128)(2,1)S(1)}, bf16[2,320,128]{2,1,0:T(8,128)(2,1)S(1)}, u32[]{:S(2)}, u32[]{:S(2)}) collective-permute-start(bf16[2,320,128]{2,1,0:T(8,128)(2,1)S(1)} %pad_maximum_fusion.1), channel_id=1, source_target_pairs={{0,4},{1,5},{2,6},{3,7},{4,0},{5,1},{6,2},{7,3},{8,12},{9,13},{10,... | collective-permute-start | bytes 491528 | tf_op jit(solution)/shard_map/ppermute | solution.py:45
  60.8 11.1 %collective-permute-start.11 = (bf16[272,512]{1,0:T(8,128)(2,1)S(1)}, bf16[272,512]{1,0:T(8,128)(2,1)S(1)}, u32[]{:S(2)}, u32[]{:S(2)}) collective-permute-start(bf16[272,512]{1,0:T(8,128)(2,1)S(1)} %collective-permute-done.8.refs_5_), channel_id=1, source_target_pairs={{0,32},{1,33},{2,34},{3,35},{4,36},{5,37},{6,38},{7,39},{8,40},{9,... | collective-permute-start | bytes 835592 | tf_op jit(solution)/shard_map/ppermute | solution.py:45
  71.9 18.7 %collective-permute-start.12 = (bf16[4,320,128]{2,1,0:T(8,128)(2,1)S(1)}, bf16[4,320,128]{2,1,0:T(8,128)(2,1)S(1)}, u32[]{:S(2)}, u32[]{:S(2)}) collective-permute-start(bf16[4,320,128]{2,1,0:T(8,128)(2,1)S(1)} %pad_maximum_fusion.refs_8_), channel_id=1, source_target_pairs={{0,3},{1,0},{2,1},{3,2},{4,7},{5,4},{6,5},{7,6},{8,11},{9,8},{10,9... | collective-permute-start | bytes 983048 | tf_op jit(solution)/shard_map/ppermute | solution.py:45
  76.7 13.9 %collective-permute-start.13 = (bf16[272,512]{1,0:T(8,128)(2,1)S(1)}, bf16[272,512]{1,0:T(8,128)(2,1)S(1)}, u32[]{:S(2)}, u32[]{:S(2)}) collective-permute-start(bf16[272,512]{1,0:T(8,128)(2,1)S(1)} %collective-permute-done.10.refs_2_), channel_id=1, source_target_pairs={{0,224},{1,225},{2,226},{3,227},{4,228},{5,229},{6,230},{7,231},{8... | collective-permute-start | bytes 835592 | tf_op jit(solution)/shard_map/ppermute | solution.py:45
  81.2 14.7 %collective-permute-start.17 = (bf16[4,320,128]{2,1,0:T(8,128)(2,1)S(1)}, bf16[4,320,128]{2,1,0:T(8,128)(2,1)S(1)}, u32[]{:S(2)}, u32[]{:S(2)}) collective-permute-start(bf16[4,320,128]{2,1,0:T(8,128)(2,1)S(1)} %pad_maximum_fusion.refs_8_), channel_id=1, source_target_pairs={{0,1},{1,2},{2,3},{3,0},{4,5},{5,6},{6,7},{7,4},{8,9},{9,10},{10,1... | collective-permute-start | bytes 983048 | tf_op jit(solution)/shard_map/ppermute | solution.py:45
  83.1 16.1 %collective-permute-start.16 = (bf16[4,320,128]{2,1,0:T(8,128)(2,1)S(1)}, bf16[4,320,128]{2,1,0:T(8,128)(2,1)S(1)}, u32[]{:S(2)}, u32[]{:S(2)}) collective-permute-start(bf16[4,320,128]{2,1,0:T(8,128)(2,1)S(1)} %pad_maximum_fusion.refs_8_), channel_id=1, source_target_pairs={{0,2},{1,3},{2,0},{3,1},{4,6},{5,7},{6,4},{7,5},{8,10},{9,11},{10,... | collective-permute-start | bytes 983048 | tf_op jit(solution)/shard_map/ppermute | solution.py:45
  87.1 8.7 %collective-permute-start.15 = (bf16[272,512]{1,0:T(8,128)(2,1)S(1)}, bf16[272,512]{1,0:T(8,128)(2,1)S(1)}, u32[]{:S(2)}, u32[]{:S(2)}) collective-permute-start(bf16[272,512]{1,0:T(8,128)(2,1)S(1)} %collective-permute-done.11.refs_6_), channel_id=1, source_target_pairs={{0,32},{1,33},{2,34},{3,35},{4,36},{5,37},{6,38},{7,39},{8,40},{9,... | collective-permute-start | bytes 835592 | tf_op jit(solution)/shard_map/ppermute | solution.py:45
  90.7 12.1 %collective-permute-start.14 = (bf16[272,512]{1,0:T(8,128)(2,1)S(1)}, bf16[272,512]{1,0:T(8,128)(2,1)S(1)}, u32[]{:S(2)}, u32[]{:S(2)}) collective-permute-start(bf16[272,512]{1,0:T(8,128)(2,1)S(1)} %collective-permute-done.13.refs_3_), channel_id=1, source_target_pairs={{0,224},{1,225},{2,226},{3,227},{4,228},{5,229},{6,230},{7,231},{8... | collective-permute-start | bytes 835592 | tf_op jit(solution)/shard_map/ppermute | solution.py:45
  102.8 1.0 copy-start.4
  106.5 4.0 %collective-permute-start.18 = (f32[320,512]{1,0:T(8,128)S(1)}, f32[320,512]{1,0:T(8,128)S(1)}, u32[]{:S(2)}, u32[]{:S(2)}) collective-permute-start(f32[320,512]{1,0:T(8,128)S(1)} %get-tuple-element.36.mine_ref), channel_id=1, source_target_pairs={{0,256},{1,257},{2,258},{3,259},{4,260},{5,261},{6,262},{7,263},{8... | collective-permute-start | bytes 1966088 | tf_op jit(solution)/shard_map/ppermute | solution.py:45
  130.7 7.3 %collective-permute-start.19 = (bf16[8,320]{1,0:T(8,128)(2,1)S(1)}, bf16[8,320]{1,0:T(8,128)(2,1)S(1)}, u32[]{:S(2)}, u32[]{:S(2)}) collective-permute-start(bf16[8,320]{1,0:T(8,128)(2,1)S(1)} %reduce_sum.9), channel_id=1, source_target_pairs={{0,0},{1,16},{2,32},{3,48},{4,64},{5,80},{6,96},{7,112},{8,128},{9... | collective-permute-start | bytes 15368 | tf_op jit(solution)/shard_map/ppermute | solution.py:45

commit v8 on v7

--- a/solution.py
+++ b/solution.py
@@ -45,6 +45,10 @@
     return lax.ppermute(value, AXES, pairs)
 
 
+def gather(value, axes):
+    return lax.all_to_all(value, axes, split_axis=0, concat_axis=0, tiled=True)
+
+
 def to_partner(g, y, zh, zl, x):
     return (g, y, 1 - zh, zl, x)
 
@@ -61,14 +65,6 @@
     return lambda g, *place: (core, *transposed(g, *place)[1:]) if g == 1 else None
 
 
-def along_zl(flip):
-    return lambda g, y, zh, zl, x: (g, y, zh, zl ^ flip, x)
-
-
-def along_x(step):
-    return lambda g, y, zh, zl, x: (g, y, zh, zl, (x + (step if g == 1 else -step)) % 4)
-
-
 def other_core(g, y, zh, zl, x):
     return (1 - g, y, zh, zl, x)
 
@@ -78,7 +74,6 @@
 
 
 HOPS = (0, 1, 2, 3, 4, -1, -2, -3)
-FLIPS = (0, 3, 1, 2)
 
 
 def attend_kernel(
@@ -235,11 +230,9 @@
 
 
 def gradient_kernel(place_ref, *refs):
-    chunks, blocks, (out_ref, rows_ref) = refs[:8], refs[8:12], refs[-7:-5]
+    chunks, blocks, (out_ref, rows_ref) = refs[:8], refs[8], refs[-7:-5]
     chunk_rows, block_tiles, block_rows, row_tiles, sems = refs[-5:]
-    copies = [
-        pltpu.make_async_copy(blocks[b], block_tiles.at[b], sems.at[b]) for b in range(4)
-    ]
+    block_copy = pltpu.make_async_copy(blocks, block_tiles, sems.at[0])
     act_copies = [
         pltpu.make_async_copy(
             chunks[n].at[:TOK], chunk_rows.at[pl.ds(n * TOK, TOK)], sems.at[4 + n]
@@ -250,21 +243,16 @@
         pltpu.make_async_copy(chunks[n].at[TOK:], row_tiles.at[n], sems.at[12 + n])
         for n in range(8)
     ]
-    for copy in copies + act_copies + row_copies:
+    for copy in [block_copy] + act_copies + row_copies:
         copy.start()
-    for copy in copies:
-        copy.wait()
-    side, y, z_hi, z_lo, x = (place_ref[n] for n in range(5))
+    block_copy.wait()
+    side, y, z_hi = (place_ref[n] for n in range(3))
     places = []
     for at in range(16):
         hop, block_zh = HOPS[at // 2], (z_hi if at % 2 == 0 else 1 - z_hi)
-        block_y = jnp.where(side == 1, y - hop, y + hop) & 7
-        source = 2 * (block_y & 1) + block_zh - x
-        source = jnp.where(side == 1, -source, source) & 3
-        flip = z_lo ^ (block_y >> 1)
-        slot = sum(jnp.where(flip == f, n, 0) for n, f in enumerate(FLIPS))
-        block_rows[:, at * HALF : (at + 1) * HALF] = block_tiles[source, slot]
-        places.append(2 * block_y + block_zh)
+        block = 2 * (jnp.where(side == 1, y - hop, y + hop) & 7) + block_zh
+        block_rows[:, at * HALF : (at + 1) * HALF] = block_tiles[block]
+        places.append(block)
     for half in range(2):
         for n in range(4 * half, 4 * half + 4):
             act_copies[n].wait()
@@ -283,7 +271,7 @@
 
 
 def gradient(place, chunks, blocks, others):
-    operands = (*chunks, *blocks, *others)
+    operands = (*chunks, blocks, *others)
     return pl.pallas_call(
         gradient_kernel,
         out_shape=(
@@ -294,7 +282,7 @@
         out_specs=(VMEM, VMEM),
         scratch_shapes=[
             pltpu.VMEM((8 * TOK, FEAT), bf16),
-            pltpu.VMEM((4, 4, COLS, HALF), bf16),
+            pltpu.VMEM((16, COLS, HALF), bf16),
             pltpu.VMEM((COLS, 8 * TOK), bf16),
             pltpu.VMEM((8, PAD, FEAT), bf16),
             pltpu.SemaphoreType.DMA((20,)),
@@ -362,6 +350,9 @@
 
     act = activations[0]
     act_got = permute(act, to_rollout)
+    cut_one, cut_two = cut_of(place, cotangent[0])
+    own_one = permute(cut_one, cot_transposed(1))
+    own_two = permute(cut_two, cot_transposed(0))
     rows = attend(
         (q >> 1).reshape(1),
         queries,
@@ -373,47 +364,34 @@
         token_ids.T,
     )
     half = half_of(place, act, act_got, rows)
-    half_got = permute(half, to_partner)
-
-    cut_one, cut_two = cut_of(place, cotangent[0])
-    own_one = permute(cut_one, cot_transposed(1))
-    own_two = permute(cut_two, cot_transposed(0))
-
+    half_tied, _ = lax.optimization_barrier((half, cut_one))
+    half_got = permute(half_tied, to_partner)
+    own_one, own_two, half_got = lax.optimization_barrier((own_one, own_two, half_got))
+    own = jnp.where(place[0] == 1, own_one, own_two)
+    own_spread = jnp.broadcast_to(own[None], (16, COLS, HALF))
+    blocks = gather(own_spread, TENSOR)
+    base = base_of((half, half_got), (own_spread,))
+    first, second = [base], [base]
+    for n in range(3):
+        first.append(permute(first[n], along_y(1)))
+        second.append(permute(second[n], along_y(-1)))
+        first[n + 1], second[n + 1] = lax.optimization_barrier((first[n + 1], second[n + 1]))
     one, two = moment_one[0].T, moment_two[0].T
-    one_tied, two_tied, _, _ = lax.optimization_barrier((one, two, cut_one, half))
+    one_tied, two_tied, first[3] = lax.optimization_barrier((one, two, first[3]))
+    first.append(permute(first[3], along_y(1)))
     one_got = permute(one_tied, to_rollout)
     two_got = permute(two_tied, to_rollout)
-    base = base_of((half, half_got), (one_got, two_got, cut_one, cut_two))
-
-    first, second = [base], [base]
-    first.append(permute(base, along_y(1)))
-    second.append(permute(base, along_y(-1)))
-    own_one, own_two, first[1] = lax.optimization_barrier((own_one, own_two, first[1]))
-    first.append(permute(first[1], along_y(1)))
-    own = jnp.where(place[0] == 1, own_one, own_two)
-    two_blocks = jnp.stack([own, permute(own, along_zl(3))])
-    two_blocks, second[1] = lax.optimization_barrier((two_blocks, second[1]))
-    second.append(permute(second[1], along_y(-1)))
-    two_got_blocks = permute(two_blocks, along_zl(1))
-    two_got_blocks, first[2] = lax.optimization_barrier((two_got_blocks, first[2]))
-    first.append(permute(first[2], along_y(1)))
-    four = jnp.concatenate([two_blocks, two_got_blocks], axis=0)
-    four, second[2] = lax.optimization_barrier((four, second[2]))
-    second.append(permute(second[2], along_y(-1)))
-    blocks = [four] + [permute(four, along_x(step)) for step in (1, 2, -1)]
-    blocks[1], first[3] = lax.optimization_barrier((blocks[1], first[3]))
-    first.append(permute(first[3], along_y(1)))
     chunks = first + second[1:]
 
-    mine, all_rows = gradient(place, chunks, blocks, ())
+    mine, all_rows = gradient(place, chunks, blocks, (one_got, two_got))
     got = permute(mine, other_core)
     update, partial = step(place, mine, got, all_rows, one, one_got, two, two_got, weight.T)
 
-    shares = lax.all_to_all(partial, TENSOR, split_axis=0, concat_axis=0, tiled=True)
+    shares = gather(partial, TENSOR)
     summed = jnp.sum(shares, axis=0).astype(bf16)
     block = permute(summed, transposed)
     spread = jnp.broadcast_to(block[None], (16, ROWS, COLS))
-    gathered = lax.all_to_all(spread, TENSOR, split_axis=0, concat_axis=0, tiled=True)
+    gathered = gather(spread, TENSOR)
     decoded = gathered.transpose(1, 0, 2).reshape(STEPS, ROWS // STEPS, D)
     return (update.T, decoded)
 

time: 157 us -> 160 us (1.019)
  the two profiles are of different devices: /device:TPU:16 before, /device:TPU:2 now
where the time goes in v8:
time: 160 us; the launch traced here: 159 us
  starting transfers between devices  61.2 us (38%)
  waiting for transfers between devices  39 us (24%)
  blocking collectives  29.7 us (19%)
  local copies, waits for them, and re-layouts  15.1 us (9%)
  Pallas kernels  13.2 us (8%)
    ppermute x15, starting transfers between devices, permute(): return lax.ppermute(value, AXES, pairs)  49.2 us
    ppermute x15, waiting for transfers between devices, permute(): return lax.ppermute(value, AXES, pairs)  39 us
    all_to_all x2, blocking collectives, gather(): return lax.all_to_all(value, axes, split_axis=0, concat_axis=0, tiled=True)  29.7 us
    unnamed x42, local copies, waits for them, and re-layouts  12.3 us
    all_to_all x1, starting transfers between devices, gather(): return lax.all_to_all(value, axes, split_axis=0, concat_axis=0, tiled=True)  12 us
  transfers between devices with their start and end apart: 16, of which 10 were waited for; matrix products, arithmetic and copies ran while one was open for 0% of the time, Pallas kernels for 4%

profile of v8, /device:TPU:2, one launch (start us, length us, event | category | flops | bytes accessed | tf_op | source)
XLA Modules:
  0.0 159.2 jit_solution(1355829707673905340)
XLA Ops:
  0.6 1.3 collective-permute-start
  1.9 0.7 stack.23.place_ref
  2.6 2.4 %cut.1 = (bf16[320,128]{1,0:T(8,128)(2,1)}, bf16[320,128]{1,0:T(8,128)(2,1)}) custom-call(s32[5]{0:T(128)} %stack.23.place_ref, bf16[256,5120]{1,0:T(8,128)(2,1)} %bitcast.23), custom_call_target="tpu_custom_call" | custom-call | tf_op jit(solution)/shard_map/cut/pallas_call | solution.py:218
  5.0 0.0 copy-start.20
  5.0 0.0 copy-start.19
  5.0 2.9 %attend.1.rows_ref = bf16[16,512]{1,0:T(8,128)(2,1)} custom-call(s32[1]{0:T(128)} %bitcast.6.head_ref, s32[2]{0:T(128)} %lengths_ref.1, s32[2,4]{1,0:T(2,128)} %bitcast.27, bf16[4,2,512]{2,1,0:T(2,128)(2,1)} %q_ref.1, bf16[2,2048,128]{2,1,0:T(8,128)(2,1)} %k_ref.1, bf16[2,2048,128]{2,1,0:T(8,128)(2,1)} %v_ref.1, bf16[4,2,1024]{2,1,0:T(2,128)(2,1)} %nk_ref.1, ...), custom_call_target="tpu_custom_call" | custom-call | tf_op jit(solution)/shard_map/attend/pallas_call | solution.py:141
  8.0 0.0 collective-permute-done.act_got
  8.0 0.7 copy-done.17
  8.7 1.7 %half.1.mine_ref = bf16[144,512]{1,0:T(8,128)(2,1)} custom-call(s32[5]{0:T(128)} %stack.23.place_ref, bf16[256,512]{1,0:T(8,128)(2,1)} %bitcast.26, bf16[256,512]{1,0:T(8,128)(2,1)} %copy-done.17, bf16[16,512]{1,0:T(8,128)(2,1)} %attend.1.rows_ref), custom_call_target="tpu_custom_call" | custom-call | tf_op jit(solution)/shard_map/half/pallas_call | solution.py:177
  10.4 10.9 %collective-permute-start.3 = (bf16[144,512]{1,0:T(8,128)(2,1)}, bf16[144,512]{1,0:T(8,128)(2,1)S(1)}, u32[]{:S(2)}, u32[]{:S(2)}) collective-permute-start(bf16[144,512]{1,0:T(8,128)(2,1)} %half.1.mine_ref), channel_id=1, source_target_pairs={{0,16},{1,17},{2,18},{3,19},{4,20},{5,21},{6,22},{7,23},{8,24},{9,... | collective-permute-start | bytes 442376 | tf_op jit(solution)/shard_map/ppermute | solution.py:45
  21.3 0.0 copy-done.20
  21.3 1.3 collective-permute-start.2
  22.6 0.7 collective-permute-start.1
  23.3 8.6 %collective-permute-done.2 = bf16[320,128]{1,0:T(8,128)(2,1)S(1)} collective-permute-done((bf16[320,128]{1,0:T(8,128)(2,1)S(1)}, bf16[320,128]{1,0:T(8,128)(2,1)S(1)}, u32[]{:S(2)}, u32[]{:S(2)}) %collective-permute-start.2) | collective-permute-done | bytes 81952 | tf_op jit(solution)/shard_map/ppermute | solution.py:45
  31.9 0.0 collective-permute-done.1
  31.9 0.0 collective-permute-done.3.got_ref
  31.9 1.3 broadcast_in_dim.4.refs_0_
  33.2 12.0 %all-to-all-start = ((bf16[16,320,128]{2,1,0:T(8,128)(2,1)}), bf16[16,320,128]{2,1,0:T(8,128)(2,1)S(1)}, u32[]{:S(2)}, u32[]{:S(2)}) async-start(bf16[16,320,128]{2,1,0:T(8,128)(2,1)} %broadcast_in_dim.4.refs_0_), calls=%async_computation | async-start | bytes 2621440 | tf_op jit(solution)/shard_map/all_to_all | solution.py:49
  45.3 1.8 %base.1.refs_0_ = bf16[272,512]{1,0:T(8,128)(2,1)} custom-call(bf16[144,512]{1,0:T(8,128)(2,1)} %half.1.mine_ref, bf16[144,512]{1,0:T(8,128)(2,1)} %copy-done.18, bf16[16,320,128]{2,1,0:T(8,128)(2,1)} %broadcast_in_dim.4.refs_0_), custom_call_target="tpu_custom_call" | custom-call | tf_op jit(solution)/shard_map/base/pallas_call | solution.py:195
  47.1 2.6 %collective-permute-start.5 = (bf16[272,512]{1,0:T(8,128)(2,1)}, bf16[272,512]{1,0:T(8,128)(2,1)S(1)}, u32[]{:S(2)}, u32[]{:S(2)}) collective-permute-start(bf16[272,512]{1,0:T(8,128)(2,1)} %base.1.refs_0_), channel_id=1, source_target_pairs={{0,32},{1,33},{2,34},{3,35},{4,36},{5,37},{6,38},{7,39},{8,40},{9,... | collective-permute-start | bytes 835592 | tf_op jit(solution)/shard_map/ppermute | solution.py:45
  49.7 4.4 %collective-permute-start.4 = (bf16[272,512]{1,0:T(8,128)(2,1)}, bf16[272,512]{1,0:T(8,128)(2,1)S(1)}, u32[]{:S(2)}, u32[]{:S(2)}) collective-permute-start(bf16[272,512]{1,0:T(8,128)(2,1)} %base.1.refs_0_), channel_id=1, source_target_pairs={{0,224},{1,225},{2,226},{3,227},{4,228},{5,229},{6,230},{7,231},{8... | collective-permute-start | bytes 835592 | tf_op jit(solution)/shard_map/ppermute | solution.py:45
  54.1 2.8 %collective-permute-done.5.refs_5_ = bf16[272,512]{1,0:T(8,128)(2,1)S(1)} collective-permute-done((bf16[272,512]{1,0:T(8,128)(2,1)}, bf16[272,512]{1,0:T(8,128)(2,1)S(1)}, u32[]{:S(2)}, u32[]{:S(2)}) %collective-permute-start.5) | collective-permute-done | bytes 278560 | tf_op jit(solution)/shard_map/ppermute | solution.py:45
  56.9 5.1 %collective-permute-done.4.refs_1_ = bf16[272,512]{1,0:T(8,128)(2,1)S(1)} collective-permute-done((bf16[272,512]{1,0:T(8,128)(2,1)}, bf16[272,512]{1,0:T(8,128)(2,1)S(1)}, u32[]{:S(2)}, u32[]{:S(2)}) %collective-permute-start.4) | collective-permute-done | bytes 278560 | tf_op jit(solution)/shard_map/ppermute | solution.py:45
  62.0 4.5 %collective-permute-start.6 = (bf16[272,512]{1,0:T(8,128)(2,1)S(1)}, bf16[272,512]{1,0:T(8,128)(2,1)S(1)}, u32[]{:S(2)}, u32[]{:S(2)}) collective-permute-start(bf16[272,512]{1,0:T(8,128)(2,1)S(1)} %collective-permute-done.4.refs_1_), channel_id=1, source_target_pairs={{0,224},{1,225},{2,226},{3,227},{4,228},{5,229},{6,230},{7,231},{8... | collective-permute-start | bytes 835592 | tf_op jit(solution)/shard_map/ppermute | solution.py:45
  66.6 0.7 copy-done.4
  67.3 1.9 %collective-permute-start.7 = (bf16[272,512]{1,0:T(8,128)(2,1)S(1)}, bf16[272,512]{1,0:T(8,128)(2,1)S(1)}, u32[]{:S(2)}, u32[]{:S(2)}) collective-permute-start(bf16[272,512]{1,0:T(8,128)(2,1)S(1)} %collective-permute-done.5.refs_5_), channel_id=1, source_target_pairs={{0,32},{1,33},{2,34},{3,35},{4,36},{5,37},{6,38},{7,39},{8,40},{9,... | collective-permute-start | bytes 835592 | tf_op jit(solution)/shard_map/ppermute | solution.py:45
  69.2 1.4 collective-permute-done.6.refs_2_
  70.6 6.3 %collective-permute-done.7.refs_6_ = bf16[272,512]{1,0:T(8,128)(2,1)S(1)} collective-permute-done((bf16[272,512]{1,0:T(8,128)(2,1)S(1)}, bf16[272,512]{1,0:T(8,128)(2,1)S(1)}, u32[]{:S(2)}, u32[]{:S(2)}) %collective-permute-start.7) | collective-permute-done | bytes 278560 | tf_op jit(solution)/shard_map/ppermute | solution.py:45
  76.9 1.9 %collective-permute-start.8 = (bf16[272,512]{1,0:T(8,128)(2,1)S(1)}, bf16[272,512]{1,0:T(8,128)(2,1)S(1)}, u32[]{:S(2)}, u32[]{:S(2)}) collective-permute-start(bf16[272,512]{1,0:T(8,128)(2,1)S(1)} %collective-permute-done.6.refs_2_), channel_id=1, source_target_pairs={{0,224},{1,225},{2,226},{3,227},{4,228},{5,229},{6,230},{7,231},{8... | collective-permute-start | bytes 835592 | tf_op jit(solution)/shard_map/ppermute | solution.py:45
  78.8 0.0 copy-start.6
  78.8 0.7 copy-done.6
  79.5 3.9 %collective-permute-start.9 = (bf16[272,512]{1,0:T(8,128)(2,1)S(1)}, bf16[272,512]{1,0:T(8,128)(2,1)S(1)}, u32[]{:S(2)}, u32[]{:S(2)}) collective-permute-start(bf16[272,512]{1,0:T(8,128)(2,1)S(1)} %collective-permute-done.7.refs_6_), channel_id=1, source_target_pairs={{0,32},{1,33},{2,34},{3,35},{4,36},{5,37},{6,38},{7,39},{8,40},{9,... | collective-permute-start | bytes 835592 | tf_op jit(solution)/shard_map/ppermute | solution.py:45
  83.5 0.7 copy-done.8
  84.2 3.9 %collective-permute-done.8.refs_3_ = bf16[272,512]{1,0:T(8,128)(2,1)S(1)} collective-permute-done((bf16[272,512]{1,0:T(8,128)(2,1)S(1)}, bf16[272,512]{1,0:T(8,128)(2,1)S(1)}, u32[]{:S(2)}, u32[]{:S(2)}) %collective-permute-start.8) | collective-permute-done | bytes 278560 | tf_op jit(solution)/shard_map/ppermute | solution.py:45
  88.1 1.1 collective-permute-done.9.refs_7_
  89.2 0.7 copy-done.12
  89.9 0.0 copy-done.1
  89.9 1.3 collective-permute-start.11
  91.2 1.3 collective-permute-start.12
  92.5 2.0 %collective-permute-start.10 = (bf16[272,512]{1,0:T(8,128)(2,1)S(1)}, bf16[272,512]{1,0:T(8,128)(2,1)S(1)}, u32[]{:S(2)}, u32[]{:S(2)}) collective-permute-start(bf16[272,512]{1,0:T(8,128)(2,1)S(1)} %collective-permute-done.8.refs_3_), channel_id=1, source_target_pairs={{0,224},{1,225},{2,226},{3,227},{4,228},{5,229},{6,230},{7,231},{8... | collective-permute-start | bytes 835592 | tf_op jit(solution)/shard_map/ppermute | solution.py:45
  94.5 0.7 copy-done.10
  95.2 5.7 %collective-permute-done.10.refs_4_ = bf16[272,512]{1,0:T(8,128)(2,1)S(1)} collective-permute-done((bf16[272,512]{1,0:T(8,128)(2,1)S(1)}, bf16[272,512]{1,0:T(8,128)(2,1)S(1)}, u32[]{:S(2)}, u32[]{:S(2)}) %collective-permute-start.10) | collective-permute-done | bytes 278560 | tf_op jit(solution)/shard_map/ppermute | solution.py:45
  100.9 0.7 copy-done.14
  101.6 0.0 collective-permute-done.11.refs_9_.one_got
  101.6 0.0 collective-permute-done.12.refs_10_.two_got
  101.6 0.0 all-to-all-done.refs_8_
  101.6 0.0 copy-start
  101.6 0.9 copy-done
  102.6 1.0 copy-done.5
  103.5 1.0 copy-done.7
  104.5 1.0 copy-done.9
  105.5 1.0 copy-done.11
  106.4 1.0 copy-done.13
  107.4 1.0 copy-done.15
  108.3 0.7 copy-done.16
  109.0 2.4 %gradient.1 = (f32[320,512]{1,0:T(8,128)S(1)}, f32[128,512]{1,0:T(8,128)S(1)}) custom-call(s32[5]{0:T(128)S(1)} %copy-done.16, bf16[272,512]{1,0:T(8,128)(2,1)S(1)} %copy-done, bf16[272,512]{1,0:T(8,128)(2,1)S(1)} %copy-done.5, bf16[272,512]{1,0:T(8,128)(2,1)S(1)} %copy-done.7, bf16[272,512]{1,0:T(8,128)(2,1)S(1)} %copy-done.11, ...), custom_call_target="tpu_custom_call" | custom-call | flops 671088640 | bytes 6291456 | tf_op jit(solution)/shard_map/gradient/pallas_call | solution.py:275
  111.4 3.2 %collective-permute-start.13 = (f32[320,512]{1,0:T(8,128)S(1)}, f32[320,512]{1,0:T(8,128)S(1)}, u32[]{:S(2)}, u32[]{:S(2)}) collective-permute-start(f32[320,512]{1,0:T(8,128)S(1)} %get-tuple-element.36.mine_ref), channel_id=1, source_target_pairs={{0,256},{1,257},{2,258},{3,259},{4,260},{5,261},{6,262},{7,263},{8... | collective-permute-start | bytes 1966088 | tf_op jit(solution)/shard_map/ppermute | solution.py:45
  114.6 1.7 %collective-permute-done.13.got_ref = f32[320,512]{1,0:T(8,128)S(1)} collective-permute-done((f32[320,512]{1,0:T(8,128)S(1)}, f32[320,512]{1,0:T(8,128)S(1)}, u32[]{:S(2)}, u32[]{:S(2)}) %collective-permute-start.13) | collective-permute-done | bytes 655392 | tf_op jit(solution)/shard_map/ppermute | solution.py:45
  116.3 1.9 %step.1 = (bf16[320,512]{1,0:T(8,128)(2,1)}, f32[16,8,320]{2,1,0:T(8,128)S(1)}) custom-call(s32[5]{0:T(128)S(1)} %copy-done.16, f32[320,512]{1,0:T(8,128)S(1)} %get-tuple-element.36.mine_ref, f32[320,512]{1,0:T(8,128)S(1)} %collective-permute-done.13.got_ref, f32[128,512]{1,0:T(8,128)S(1)} %get-tuple-element.37.rows_ref, f32[320,512]{1,0:T(8,128)S(1)} %bitcast.19, ...), custom_call_target="tpu_custom_call" | custom-call | tf_op jit(solution)/shard_map/step/pallas_call | solution.py:321
  118.3 16.1 %all_to_all.15 = f32[16,8,320]{2,1,0:T(8,128)S(1)} all-to-all(f32[16,8,320]{2,1,0:T(8,128)S(1)} %get-tuple-element.39), channel_id=1, replica_groups=mesh['group'=2,'y'=8,'z_hi'=2,'z_lo'=4,'x'=4] {'z_lo','x'}, dimensions={0} | all-to-all | bytes 327680 | tf_op jit(solution)/shard_map/all_to_all | solution.py:49
  134.4 8.0 %collective-permute-start.14 = (bf16[8,320]{1,0:T(8,128)(2,1)S(1)}, bf16[8,320]{1,0:T(8,128)(2,1)S(1)}, u32[]{:S(2)}, u32[]{:S(2)}) collective-permute-start(bf16[8,320]{1,0:T(8,128)(2,1)S(1)} %reduce_sum.9), channel_id=1, source_target_pairs={{0,0},{1,16},{2,32},{3,48},{4,64},{5,80},{6,96},{7,112},{8,128},{9... | collective-permute-start | bytes 15368 | tf_op jit(solution)/shard_map/ppermute | solution.py:45
  142.4 2.3 %collective-permute-done.14 = bf16[8,320]{1,0:T(8,128)(2,1)S(1)} collective-permute-done((bf16[8,320]{1,0:T(8,128)(2,1)S(1)}, bf16[8,320]{1,0:T(8,128)(2,1)S(1)}, u32[]{:S(2)}, u32[]{:S(2)}) %collective-permute-start.14) | collective-permute-done | bytes 5152 | tf_op jit(solution)/shard_map/ppermute | solution.py:45
  144.7 13.6 %all_to_all.16 = bf16[16,8,320]{2,1,0:T(8,128)(2,1)S(1)} all-to-all(bf16[16,8,320]{2,1,0:T(8,128)(2,1)S(1)} %broadcast_in_dim.5), channel_id=1, replica_groups=mesh['group'=2,'y'=8,'z_hi'=2,'z_lo'=4,'x'=4] {'z_lo','x'}, dimensions={0} | all-to-all | bytes 163840 | tf_op jit(solution)/shard_map/all_to_all | solution.py:49
  158.4 0.8 reshape.13
  (25 shorter events, 0.1 us)
Async XLA Ops:
  0.6 7.3 %collective-permute-start = (bf16[256,512]{1,0:T(8,128)(2,1)}, bf16[256,512]{1,0:T(8,128)(2,1)S(1)}, u32[]{:S(2)}, u32[]{:S(2)}) collective-permute-start(bf16[256,512]{1,0:T(8,128)(2,1)} %bitcast.25), channel_id=1, source_target_pairs={{256,0},{257,1},{258,2},{259,3},{260,4},{261,5},{262,6},{263,7},{2... | collective-permute-start | bytes 786440 | tf_op jit(solution)/shard_map/ppermute | solution.py:45
  5.0 16.3 %copy-start.20 = (bf16[320,128]{1,0:T(8,128)(2,1)S(1)}, bf16[320,128]{1,0:T(8,128)(2,1)}, u32[]{:S(2)}) copy-start(bf16[320,128]{1,0:T(8,128)(2,1)} %get-tuple-element.22) | copy-start | bytes 245764
  5.0 17.6 %copy-start.19 = (bf16[320,128]{1,0:T(8,128)(2,1)S(1)}, bf16[320,128]{1,0:T(8,128)(2,1)}, u32[]{:S(2)}) copy-start(bf16[320,128]{1,0:T(8,128)(2,1)} %get-tuple-element.21) | copy-start | bytes 245764
  8.0 0.7 copy-start.17
  10.4 21.5 %collective-permute-start.3 = (bf16[144,512]{1,0:T(8,128)(2,1)}, bf16[144,512]{1,0:T(8,128)(2,1)S(1)}, u32[]{:S(2)}, u32[]{:S(2)}) collective-permute-start(bf16[144,512]{1,0:T(8,128)(2,1)} %half.1.mine_ref), channel_id=1, source_target_pairs={{0,16},{1,17},{2,18},{3,19},{4,20},{5,21},{6,22},{7,23},{8,24},{9,... | collective-permute-start | bytes 442376 | tf_op jit(solution)/shard_map/ppermute | solution.py:45
  21.3 10.6 %collective-permute-start.2 = (bf16[320,128]{1,0:T(8,128)(2,1)S(1)}, bf16[320,128]{1,0:T(8,128)(2,1)S(1)}, u32[]{:S(2)}, u32[]{:S(2)}) collective-permute-start(bf16[320,128]{1,0:T(8,128)(2,1)S(1)} %copy-done.20), channel_id=1, source_target_pairs={{256,0},{257,16},{258,32},{259,48},{260,64},{261,80},{262,96},{263... | collective-permute-start | bytes 245768 | tf_op jit(solution)/shard_map/ppermute | solution.py:45
  22.6 9.3 %collective-permute-start.1 = (bf16[320,128]{1,0:T(8,128)(2,1)S(1)}, bf16[320,128]{1,0:T(8,128)(2,1)S(1)}, u32[]{:S(2)}, u32[]{:S(2)}) collective-permute-start(bf16[320,128]{1,0:T(8,128)(2,1)S(1)} %copy-done.19), channel_id=1, source_target_pairs={{256,256},{257,272},{258,288},{259,304},{260,320},{261,336},{262,3... | collective-permute-start | bytes 245768 | tf_op jit(solution)/shard_map/ppermute | solution.py:45
  31.9 1.4 copy-start.18
  33.2 68.4 %all-to-all-start = ((bf16[16,320,128]{2,1,0:T(8,128)(2,1)}), bf16[16,320,128]{2,1,0:T(8,128)(2,1)S(1)}, u32[]{:S(2)}, u32[]{:S(2)}) async-start(bf16[16,320,128]{2,1,0:T(8,128)(2,1)} %broadcast_in_dim.4.refs_0_), calls=%async_computation | async-start | bytes 2621440 | tf_op jit(solution)/shard_map/all_to_all | solution.py:49
  45.3 44.6 %copy-start.1 = (f32[1,512,320]{1,2,0:T(8,128)S(1)}, f32[1,512,320]{1,2,0:T(8,128)}, u32[]{:S(2)}) copy-start(f32[1,512,320]{1,2,0:T(8,128)} %param.15) | copy-start | bytes 1966084
  47.1 9.8 %collective-permute-start.5 = (bf16[272,512]{1,0:T(8,128)(2,1)}, bf16[272,512]{1,0:T(8,128)(2,1)S(1)}, u32[]{:S(2)}, u32[]{:S(2)}) collective-permute-start(bf16[272,512]{1,0:T(8,128)(2,1)} %base.1.refs_0_), channel_id=1, source_target_pairs={{0,32},{1,33},{2,34},{3,35},{4,36},{5,37},{6,38},{7,39},{8,40},{9,... | collective-permute-start | bytes 835592 | tf_op jit(solution)/shard_map/ppermute | solution.py:45
  49.7 12.3 %collective-permute-start.4 = (bf16[272,512]{1,0:T(8,128)(2,1)}, bf16[272,512]{1,0:T(8,128)(2,1)S(1)}, u32[]{:S(2)}, u32[]{:S(2)}) collective-permute-start(bf16[272,512]{1,0:T(8,128)(2,1)} %base.1.refs_0_), channel_id=1, source_target_pairs={{0,224},{1,225},{2,226},{3,227},{4,228},{5,229},{6,230},{7,231},{8... | collective-permute-start | bytes 835592 | tf_op jit(solution)/shard_map/ppermute | solution.py:45
  62.0 8.6 %collective-permute-start.6 = (bf16[272,512]{1,0:T(8,128)(2,1)S(1)}, bf16[272,512]{1,0:T(8,128)(2,1)S(1)}, u32[]{:S(2)}, u32[]{:S(2)}) collective-permute-start(bf16[272,512]{1,0:T(8,128)(2,1)S(1)} %collective-permute-done.4.refs_1_), channel_id=1, source_target_pairs={{0,224},{1,225},{2,226},{3,227},{4,228},{5,229},{6,230},{7,231},{8... | collective-permute-start | bytes 835592 | tf_op jit(solution)/shard_map/ppermute | solution.py:45
  66.6 0.7 copy-start.4
  67.3 9.6 %collective-permute-start.7 = (bf16[272,512]{1,0:T(8,128)(2,1)S(1)}, bf16[272,512]{1,0:T(8,128)(2,1)S(1)}, u32[]{:S(2)}, u32[]{:S(2)}) collective-permute-start(bf16[272,512]{1,0:T(8,128)(2,1)S(1)} %collective-permute-done.5.refs_5_), channel_id=1, source_target_pairs={{0,32},{1,33},{2,34},{3,35},{4,36},{5,37},{6,38},{7,39},{8,40},{9,... | collective-permute-start | bytes 835592 | tf_op jit(solution)/shard_map/ppermute | solution.py:45
  76.9 11.2 %collective-permute-start.8 = (bf16[272,512]{1,0:T(8,128)(2,1)S(1)}, bf16[272,512]{1,0:T(8,128)(2,1)S(1)}, u32[]{:S(2)}, u32[]{:S(2)}) collective-permute-start(bf16[272,512]{1,0:T(8,128)(2,1)S(1)} %collective-permute-done.6.refs_2_), channel_id=1, source_target_pairs={{0,224},{1,225},{2,226},{3,227},{4,228},{5,229},{6,230},{7,231},{8... | collective-permute-start | bytes 835592 | tf_op jit(solution)/shard_map/ppermute | solution.py:45
  78.8 0.7 copy-start.6
  79.5 9.6 %collective-permute-start.9 = (bf16[272,512]{1,0:T(8,128)(2,1)S(1)}, bf16[272,512]{1,0:T(8,128)(2,1)S(1)}, u32[]{:S(2)}, u32[]{:S(2)}) collective-permute-start(bf16[272,512]{1,0:T(8,128)(2,1)S(1)} %collective-permute-done.7.refs_6_), channel_id=1, source_target_pairs={{0,32},{1,33},{2,34},{3,35},{4,36},{5,37},{6,38},{7,39},{8,40},{9,... | collective-permute-start | bytes 835592 | tf_op jit(solution)/shard_map/ppermute | solution.py:45
  83.4 0.7 copy-start.8
  89.2 0.7 copy-start.12
  89.9 11.7 %collective-permute-start.11 = (f32[320,512]{1,0:T(8,128)S(1)}, f32[320,512]{1,0:T(8,128)S(1)}, u32[]{:S(2)}, u32[]{:S(2)}) collective-permute-start(f32[320,512]{1,0:T(8,128)S(1)} %bitcast.18), channel_id=1, source_target_pairs={{256,0},{257,1},{258,2},{259,3},{260,4},{261,5},{262,6},{263,7},{2... | collective-permute-start | bytes 1966088 | tf_op jit(solution)/shard_map/ppermute | solution.py:45
  91.2 10.5 %collective-permute-start.12 = (f32[320,512]{1,0:T(8,128)}, f32[320,512]{1,0:T(8,128)S(1)}, u32[]{:S(2)}, u32[]{:S(2)}) collective-permute-start(f32[320,512]{1,0:T(8,128)} %bitcast.20), channel_id=1, source_target_pairs={{256,0},{257,1},{258,2},{259,3},{260,4},{261,5},{262,6},{263,7},{2... | collective-permute-start | bytes 1966088 | tf_op jit(solution)/shard_map/ppermute | solution.py:45
  92.5 8.4 %collective-permute-start.10 = (bf16[272,512]{1,0:T(8,128)(2,1)S(1)}, bf16[272,512]{1,0:T(8,128)(2,1)S(1)}, u32[]{:S(2)}, u32[]{:S(2)}) collective-permute-start(bf16[272,512]{1,0:T(8,128)(2,1)S(1)} %collective-permute-done.8.refs_3_), channel_id=1, source_target_pairs={{0,224},{1,225},{2,226},{3,227},{4,228},{5,229},{6,230},{7,231},{8... | collective-permute-start | bytes 835592 | tf_op jit(solution)/shard_map/ppermute | solution.py:45
  94.5 0.7 copy-start.10
  100.9 0.7 copy-start.14
  101.6 1.0 copy-start
  102.6 1.0 copy-start.5
  103.5 1.0 copy-start.7
  104.5 1.0 copy-start.9
  105.5 1.0 copy-start.11
  106.4 1.0 copy-start.13
  107.4 1.0 copy-start.15
  108.3 0.7 copy-start.16
  109.0 7.3 %copy-start.2 = (f32[1,512,320]{1,2,0:T(8,128)S(1)}, f32[1,512,320]{1,2,0:T(8,128)}, u32[]{:S(2)}) copy-start(f32[1,512,320]{1,2,0:T(8,128)} %param.16) | copy-start | bytes 1966084
  109.0 7.3 %copy-start.3 = (bf16[512,320]{0,1:T(8,128)(2,1)S(1)}, bf16[512,320]{0,1:T(8,128)(2,1)}, u32[]{:S(2)}) copy-start(bf16[512,320]{0,1:T(8,128)(2,1)} %param.14) | copy-start | bytes 983044
  111.4 4.9 %collective-permute-start.13 = (f32[320,512]{1,0:T(8,128)S(1)}, f32[320,512]{1,0:T(8,128)S(1)}, u32[]{:S(2)}, u32[]{:S(2)}) collective-permute-start(f32[320,512]{1,0:T(8,128)S(1)} %get-tuple-element.36.mine_ref), channel_id=1, source_target_pairs={{0,256},{1,257},{2,258},{3,259},{4,260},{5,261},{6,262},{7,263},{8... | collective-permute-start | bytes 1966088 | tf_op jit(solution)/shard_map/ppermute | solution.py:45
  134.4 10.3 %collective-permute-start.14 = (bf16[8,320]{1,0:T(8,128)(2,1)S(1)}, bf16[8,320]{1,0:T(8,128)(2,1)S(1)}, u32[]{:S(2)}, u32[]{:S(2)}) collective-permute-start(bf16[8,320]{1,0:T(8,128)(2,1)S(1)} %reduce_sum.9), channel_id=1, source_target_pairs={{0,0},{1,16},{2,32},{3,48},{4,64},{5,80},{6,96},{7,112},{8,128},{9... | collective-permute-start | bytes 15368 | tf_op jit(solution)/shard_map/ppermute | solution.py:45

commit v9 on v8

--- a/solution.py
+++ b/solution.py
@@ -65,8 +65,12 @@
     return lambda g, *place: (core, *transposed(g, *place)[1:]) if g == 1 else None
 
 
-def other_core(g, y, zh, zl, x):
-    return (1 - g, y, zh, zl, x)
+def along_x(step):
+    return lambda g, y, zh, zl, x: (g, y, zh, zl, (x + (step if g == 1 else -step)) % 4)
+
+
+def to_learner(g, y, zh, zl, x):
+    return (1, y, zh, zl, x) if g == 0 else None
 
 
 def to_rollout(g, y, zh, zl, x):
@@ -74,6 +78,9 @@
 
 
 HOPS = (0, 1, 2, 3, 4, -1, -2, -3)
+
+
+SMALL = pltpu.CompilerParams(vmem_limit_bytes=6 * 2**20)
 
 
 def attend_kernel(
@@ -152,6 +159,7 @@
                 pltpu.VMEM((ROWS, HD), f32),
             ],
         ),
+        compiler_params=SMALL,
         name="attend",
     )(head, lengths, ids, queries, cache_keys, cache_values, new_keys, new_values)
 
@@ -179,6 +187,7 @@
         out_shape=jax.ShapeDtypeStruct((HALF + PAD, FEAT), bf16),
         in_specs=[SMEM] + [VMEM] * 3,
         out_specs=VMEM,
+        compiler_params=SMALL,
         name="half",
     )(place, *parts)
 
@@ -197,6 +206,7 @@
         out_shape=jax.ShapeDtypeStruct((TOK + PAD, FEAT), bf16),
         in_specs=[VMEM] * 2 + [HBM] * len(others),
         out_specs=VMEM,
+        compiler_params=SMALL,
         name="base",
     )(*parts, *others)
 
@@ -225,89 +235,76 @@
             pltpu.VMEM((384, TOK), f32),
             pltpu.SemaphoreType.DMA(()),
         ],
+        compiler_params=SMALL,
         name="cut",
     )(place, cot)
 
 
 def gradient_kernel(place_ref, *refs):
-    chunks, blocks, (out_ref, rows_ref) = refs[:8], refs[8], refs[-7:-5]
-    chunk_rows, block_tiles, block_rows, row_tiles, sems = refs[-5:]
-    block_copy = pltpu.make_async_copy(blocks, block_tiles, sems.at[0])
-    act_copies = [
-        pltpu.make_async_copy(
-            chunks[n].at[:TOK], chunk_rows.at[pl.ds(n * TOK, TOK)], sems.at[4 + n]
-        )
-        for n in range(8)
-    ]
-    row_copies = [
-        pltpu.make_async_copy(chunks[n].at[TOK:], row_tiles.at[n], sems.at[12 + n])
-        for n in range(8)
-    ]
-    for copy in [block_copy] + act_copies + row_copies:
-        copy.start()
-    block_copy.wait()
-    side, y, z_hi = (place_ref[n] for n in range(3))
-    places = []
-    for at in range(16):
-        hop, block_zh = HOPS[at // 2], (z_hi if at % 2 == 0 else 1 - z_hi)
-        block = 2 * (jnp.where(side == 1, y - hop, y + hop) & 7) + block_zh
-        block_rows[:, at * HALF : (at + 1) * HALF] = block_tiles[block]
-        places.append(block)
-    for half in range(2):
-        for n in range(4 * half, 4 * half + 4):
-            act_copies[n].wait()
-        span = pl.ds(half * 4 * TOK, 4 * TOK)
-        part = jnp.dot(block_rows[:, span], chunk_rows[span, :], preferred_element_type=f32)
-        if half == 0:
+    chunks, blocks, (out_ref, rows_ref, block_rows) = refs[:8], refs[8:12], refs[12:]
+    side, y, z_hi, x = (place_ref[n] for n in (0, 1, 2, 4))
+    for n, hop in enumerate(HOPS):
+        block_y = jnp.where(side == 1, y - hop, y + hop) & 7
+        rows = chunks[n][TOK:, :].astype(f32)
+        for other in range(2):
+            block_zh = z_hi if other == 0 else 1 - z_hi
+            span = slice(other * HALF, (other + 1) * HALF)
+            source = 2 * (block_y & 1) + block_zh - x
+            source = jnp.where(side == 1, -source, source) & 3
+            block = blocks[0][block_y >> 1]
+            for m in range(1, 4):
+                block = jnp.where(source == m, blocks[m][block_y >> 1], block)
+            block_rows[:, span] = block
+            place = pl.multiple_of((2 * block_y + block_zh) * ROWS, ROWS)
+            rows_ref[pl.ds(place, ROWS), :] = rows[other * ROWS : (other + 1) * ROWS]
+        part = jnp.dot(block_rows[...], chunks[n][:TOK, :], preferred_element_type=f32)
+        if n == 0:
             out_ref[...] = part
         else:
             out_ref[...] += part
-    for n in range(8):
-        row_copies[n].wait()
-        rows = row_tiles[n].astype(f32)
-        for other in range(2):
-            place = pl.multiple_of(places[2 * n + other] * ROWS, ROWS)
-            rows_ref[pl.ds(place, ROWS), :] = rows[other * ROWS : (other + 1) * ROWS]
-
-
-def gradient(place, chunks, blocks, others):
-    operands = (*chunks, blocks, *others)
+
+
+def gradient(place, chunks, blocks):
     return pl.pallas_call(
         gradient_kernel,
         out_shape=(
             jax.ShapeDtypeStruct((COLS, FEAT), f32),
             jax.ShapeDtypeStruct((16 * ROWS, FEAT), f32),
         ),
-        in_specs=[SMEM] + [HBM] * len(operands),
+        in_specs=[SMEM] + [VMEM] * 12,
         out_specs=(VMEM, VMEM),
-        scratch_shapes=[
-            pltpu.VMEM((8 * TOK, FEAT), bf16),
-            pltpu.VMEM((16, COLS, HALF), bf16),
-            pltpu.VMEM((COLS, 8 * TOK), bf16),
-            pltpu.VMEM((8, PAD, FEAT), bf16),
-            pltpu.SemaphoreType.DMA((20,)),
-        ],
-        compiler_params=pltpu.CompilerParams(vmem_limit_bytes=32 * 2**20),
+        scratch_shapes=[pltpu.VMEM((COLS, TOK), bf16)],
+        compiler_params=pltpu.CompilerParams(vmem_limit_bytes=12 * 2**20),
         cost_estimate=pl.CostEstimate(
             flops=2 * 8 * TOK * COLS * FEAT, bytes_accessed=6 * 2**20, transcendentals=0
         ),
         name="gradient",
-    )(place, *operands)
-
-
-def step_kernel(
-    place_ref, mine_ref, got_ref, rows_ref, one_ref, one_got, two_ref, two_got, weight_ref, update_ref, out_ref
-):
-    learner = place_ref[0] == 1
+    )(place, *chunks, *blocks)
+
+
+def adam_kernel(mine_ref, got_ref, one_ref, two_ref, out_ref):
     grad = mine_ref[...] + got_ref[...]
-    moment_one = jnp.where(learner, one_ref[...], one_got[...])
-    moment_two = jnp.where(learner, two_ref[...], two_got[...])
-    first_moment = beta_one * moment_one + (1.0 - beta_one) * grad
-    second_moment = beta_two * moment_two + (1.0 - beta_two) * grad * grad
-    update = (
+    first_moment = beta_one * one_ref[...] + (1.0 - beta_one) * grad
+    second_moment = beta_two * two_ref[...] + (1.0 - beta_two) * grad * grad
+    out_ref[...] = (
         first_moment / first_bias / (jnp.sqrt(second_moment / second_bias) + epsilon)
     ).astype(bf16)
-    update_ref[...] = update
+
+
+def adam(*operands):
+    return pl.pallas_call(
+        adam_kernel,
+        out_shape=jax.ShapeDtypeStruct((COLS, FEAT), bf16),
+        in_specs=[VMEM] * 4,
+        out_specs=VMEM,
+        compiler_params=pltpu.CompilerParams(vmem_limit_bytes=12 * 2**20),
+        name="adam",
+    )(*operands)
+
+
+def step_kernel(place_ref, update_ref, update_got, rows_ref, weight_ref, taken_ref, out_ref):
+    update = jnp.where(place_ref[0] == 1, update_ref[...], update_got[...])
+    taken_ref[...] = update
     widened = weight_ref[...].astype(f32)
     renewed = (
         widened - learning_rate * (update.astype(f32) + weight_decay * widened)
@@ -317,18 +314,18 @@
     out_ref[...] = part.reshape(16, ROWS, COLS)
 
 
-def step(place, mine, got, rows, one, one_got, two, two_got, weight):
+def step(place, *operands):
     return pl.pallas_call(
         step_kernel,
         out_shape=(
             jax.ShapeDtypeStruct((COLS, FEAT), bf16),
             jax.ShapeDtypeStruct((16, ROWS, COLS), f32),
         ),
-        in_specs=[SMEM] + [VMEM] * 8,
+        in_specs=[SMEM] + [VMEM] * 4,
         out_specs=(VMEM, VMEM),
-        compiler_params=pltpu.CompilerParams(vmem_limit_bytes=32 * 2**20),
+        compiler_params=pltpu.CompilerParams(vmem_limit_bytes=12 * 2**20),
         name="step",
-    )(place, mine, got, rows, one, one_got, two, two_got, weight)
+    )(place, *operands)
 
 
 def local(
@@ -364,28 +361,29 @@
         token_ids.T,
     )
     half = half_of(place, act, act_got, rows)
-    half_tied, _ = lax.optimization_barrier((half, cut_one))
+    own = jnp.where(place[0] == 1, own_one, own_two)
+    half_tied, own = lax.optimization_barrier((half, own))
     half_got = permute(half_tied, to_partner)
-    own_one, own_two, half_got = lax.optimization_barrier((own_one, own_two, half_got))
-    own = jnp.where(place[0] == 1, own_one, own_two)
-    own_spread = jnp.broadcast_to(own[None], (16, COLS, HALF))
-    blocks = gather(own_spread, TENSOR)
-    base = base_of((half, half_got), (own_spread,))
-    first, second = [base], [base]
-    for n in range(3):
-        first.append(permute(first[n], along_y(1)))
-        second.append(permute(second[n], along_y(-1)))
-        first[n + 1], second[n + 1] = lax.optimization_barrier((first[n + 1], second[n + 1]))
-    one, two = moment_one[0].T, moment_two[0].T
-    one_tied, two_tied, first[3] = lax.optimization_barrier((one, two, first[3]))
-    first.append(permute(first[3], along_y(1)))
-    one_got = permute(one_tied, to_rollout)
-    two_got = permute(two_tied, to_rollout)
-    chunks = first + second[1:]
-
-    mine, all_rows = gradient(place, chunks, blocks, (one_got, two_got))
-    got = permute(mine, other_core)
-    update, partial = step(place, mine, got, all_rows, one, one_got, two, two_got, weight.T)
+    line = gather(jnp.broadcast_to(own[None], (4, COLS, HALF)), "z_lo")
+    base = base_of((half, half_got), (line,))
+    first = [permute(base, along_y(1))]
+    second = [permute(base, along_y(-1))]
+    line_tied, ahead, back = lax.optimization_barrier((line, first[0], second[0]))
+    first.append(permute(ahead, along_y(1)))
+    second.append(permute(back, along_y(-1)))
+    blocks = [line] + [permute(line_tied, along_x(step)) for step in (1, 2, -1)]
+    ahead, back, *_ = lax.optimization_barrier((first[1], second[1], blocks[1]))
+    first.append(permute(ahead, along_y(1)))
+    second.append(permute(back, along_y(-1)))
+    ahead, _ = lax.optimization_barrier((first[2], blocks[2]))
+    first.append(permute(ahead, along_y(1)))
+    chunks = [base] + first + second
+
+    mine, all_rows = gradient(place, chunks, blocks)
+    got = permute(mine, to_learner)
+    update = adam(mine, got, moment_one[0].T, moment_two[0].T)
+    update_got = permute(update, to_rollout)
+    update, partial = step(place, update, update_got, all_rows, weight.T)
 
     shares = gather(partial, TENSOR)
     summed = jnp.sum(shares, axis=0).astype(bf16)

time: 160 us -> 152 us (0.950)
  the two profiles are of different devices: /device:TPU:2 before, /device:TPU:24 now
where the time goes in v9:
time: 152 us; the launch traced here: 151 us
  starting transfers between devices  66.3 us (44%)
  waiting for transfers between devices  41.6 us (27%)
  blocking collectives  33.3 us (22%)
  Pallas kernels  5.8 us (4%)
  local copies, waits for them, and re-layouts  3.45 us (2%)
    ppermute x17, starting transfers between devices, permute(): return lax.ppermute(value, AXES, pairs)  55.4 us
    ppermute x17, waiting for transfers between devices, permute(): return lax.ppermute(value, AXES, pairs)  41.6 us
    all_to_all x2, blocking collectives, gather(): return lax.all_to_all(value, axes, split_axis=0, concat_axis=0, tiled=True)  33.3 us
    all_to_all x1, starting transfers between devices, gather(): return lax.all_to_all(value, axes, split_axis=0, concat_axis=0, tiled=True)  10.8 us
  transfers between devices with their start and end apart: 18, of which 12 were waited for; matrix products, arithmetic and copies ran while one was open for 0% of the time, Pallas kernels for 1%

profile of v9, /device:TPU:24, one launch (start us, length us, event | category | flops | bytes accessed | tf_op | source)
XLA Modules:
  0.0 151.4 jit_solution(400961130700485222)
XLA Ops:
  0.6 0.0 copy-start.10
  0.6 0.0 copy-start.11
  0.7 0.0 copy-start.8
  0.7 0.0 copy-start.7
  0.7 0.0 copy-start.9
  0.7 0.1 stack.23.place_ref
  0.8 1.7 %copy-done = bf16[1,256,5120]{2,1,0:T(8,128)(2,1)S(1)} copy-done((bf16[1,256,5120]{2,1,0:T(8,128)(2,1)S(1)}, bf16[1,256,5120]{2,1,0:T(8,128)(2,1)}, u32[]{:S(2)}) %copy-start) | copy-done | bytes 2621464
  2.5 0.8 cut.1
  3.3 0.7 collective-permute-start.1
  4.0 1.3 collective-permute-start.2
  5.3 0.0 copy-done.6
  5.3 1.3 collective-permute-start
  6.6 0.0 copy-done.10
  6.6 0.0 copy-done.11
  6.6 0.0 copy-done.8
  6.6 0.0 copy-done.7
  6.6 0.0 copy-done.9
  6.6 0.0 copy-done.1
  6.6 0.0 copy-done.2
  6.7 1.0 attend.1.rows_ref
  7.7 0.0 collective-permute-done.1
  7.7 7.2 %collective-permute-done.2 = bf16[320,128]{1,0:T(8,128)(2,1)S(1)} collective-permute-done((bf16[320,128]{1,0:T(8,128)(2,1)S(1)}, bf16[320,128]{1,0:T(8,128)(2,1)S(1)}, u32[]{:S(2)}, u32[]{:S(2)}) %collective-permute-start.2) | collective-permute-done | bytes 81952 | tf_op jit(solution)/shard_map/ppermute | solution.py:45
  15.0 0.0 collective-permute-done.act_got
  15.0 0.6 half.1.mine_ref
  15.5 0.8 broadcast_in_dim.4
  16.3 10.8 %all-to-all-start = ((bf16[4,320,128]{2,1,0:T(8,128)(2,1)}), bf16[4,320,128]{2,1,0:T(8,128)(2,1)S(1)}, u32[]{:S(2)}, u32[]{:S(2)}) async-start(bf16[4,320,128]{2,1,0:T(8,128)(2,1)} %broadcast_in_dim.4), calls=%async_computation | async-start | bytes 655360 | tf_op jit(solution)/shard_map/all_to_all | solution.py:49
  27.2 11.9 %collective-permute-start.3 = (bf16[144,512]{1,0:T(8,128)(2,1)S(1)}, bf16[144,512]{1,0:T(8,128)(2,1)S(1)}, u32[]{:S(2)}, u32[]{:S(2)}) collective-permute-start(bf16[144,512]{1,0:T(8,128)(2,1)S(1)} %half.1.mine_ref), channel_id=1, source_target_pairs={{0,16},{1,17},{2,18},{3,19},{4,20},{5,21},{6,22},{7,23},{8,24},{9,... | collective-permute-start | bytes 442376 | tf_op jit(solution)/shard_map/ppermute | solution.py:45
  39.1 5.7 %collective-permute-done.3.got_ref = bf16[144,512]{1,0:T(8,128)(2,1)S(1)} collective-permute-done((bf16[144,512]{1,0:T(8,128)(2,1)S(1)}, bf16[144,512]{1,0:T(8,128)(2,1)S(1)}, u32[]{:S(2)}, u32[]{:S(2)}) %collective-permute-start.3) | collective-permute-done | bytes 147488 | tf_op jit(solution)/shard_map/ppermute | solution.py:45
  44.9 0.0 all-to-all-done.refs_0_.refs_8_
  44.9 0.0 copy-start.5
  44.9 3.3 %collective-permute-start.5 = (bf16[272,512]{1,0:T(8,128)(2,1)S(1)}, bf16[272,512]{1,0:T(8,128)(2,1)S(1)}, u32[]{:S(2)}, u32[]{:S(2)}) collective-permute-start(bf16[272,512]{1,0:T(8,128)(2,1)S(1)} %base.1.refs_0_), channel_id=1, source_target_pairs={{0,32},{1,33},{2,34},{3,35},{4,36},{5,37},{6,38},{7,39},{8,40},{9,... | collective-permute-start | bytes 835592 | tf_op jit(solution)/shard_map/ppermute | solution.py:45
  48.2 2.7 %collective-permute-start.4 = (bf16[272,512]{1,0:T(8,128)(2,1)S(1)}, bf16[272,512]{1,0:T(8,128)(2,1)S(1)}, u32[]{:S(2)}, u32[]{:S(2)}) collective-permute-start(bf16[272,512]{1,0:T(8,128)(2,1)S(1)} %base.1.refs_0_), channel_id=1, source_target_pairs={{0,224},{1,225},{2,226},{3,227},{4,228},{5,229},{6,230},{7,231},{8... | collective-permute-start | bytes 835592 | tf_op jit(solution)/shard_map/ppermute | solution.py:45
  50.9 2.6 %collective-permute-done.5.refs_5_ = bf16[272,512]{1,0:T(8,128)(2,1)S(1)} collective-permute-done((bf16[272,512]{1,0:T(8,128)(2,1)S(1)}, bf16[272,512]{1,0:T(8,128)(2,1)S(1)}, u32[]{:S(2)}, u32[]{:S(2)}) %collective-permute-start.5) | collective-permute-done | bytes 278560 | tf_op jit(solution)/shard_map/ppermute | solution.py:45
  53.5 4.4 %collective-permute-done.4.refs_1_ = bf16[272,512]{1,0:T(8,128)(2,1)S(1)} collective-permute-done((bf16[272,512]{1,0:T(8,128)(2,1)S(1)}, bf16[272,512]{1,0:T(8,128)(2,1)S(1)}, u32[]{:S(2)}, u32[]{:S(2)}) %collective-permute-start.4) | collective-permute-done | bytes 278560 | tf_op jit(solution)/shard_map/ppermute | solution.py:45
  57.9 5.8 %collective-permute-start.8 = (bf16[4,320,128]{2,1,0:T(8,128)(2,1)S(1)}, bf16[4,320,128]{2,1,0:T(8,128)(2,1)S(1)}, u32[]{:S(2)}, u32[]{:S(2)}) collective-permute-start(bf16[4,320,128]{2,1,0:T(8,128)(2,1)S(1)} %all-to-all-done.refs_0_.refs_8_), channel_id=1, source_target_pairs={{0,3},{1,0},{2,1},{3,2},{4,7},{5,4},{6,5},{7,6},{8,11},{9,8},{10,9... | collective-permute-start | bytes 983048 | tf_op jit(solution)/shard_map/ppermute | solution.py:45
  63.7 1.9 %collective-permute-start.6 = (bf16[272,512]{1,0:T(8,128)(2,1)S(1)}, bf16[272,512]{1,0:T(8,128)(2,1)S(1)}, u32[]{:S(2)}, u32[]{:S(2)}) collective-permute-start(bf16[272,512]{1,0:T(8,128)(2,1)S(1)} %collective-permute-done.4.refs_1_), channel_id=1, source_target_pairs={{0,224},{1,225},{2,226},{3,227},{4,228},{5,229},{6,230},{7,231},{8... | collective-permute-start | bytes 835592 | tf_op jit(solution)/shard_map/ppermute | solution.py:45
  65.6 5.1 %collective-permute-start.7 = (bf16[272,512]{1,0:T(8,128)(2,1)S(1)}, bf16[272,512]{1,0:T(8,128)(2,1)S(1)}, u32[]{:S(2)}, u32[]{:S(2)}) collective-permute-start(bf16[272,512]{1,0:T(8,128)(2,1)S(1)} %collective-permute-done.5.refs_5_), channel_id=1, source_target_pairs={{0,32},{1,33},{2,34},{3,35},{4,36},{5,37},{6,38},{7,39},{8,40},{9,... | collective-permute-start | bytes 835592 | tf_op jit(solution)/shard_map/ppermute | solution.py:45
  70.7 4.8 %collective-permute-start.10 = (bf16[4,320,128]{2,1,0:T(8,128)(2,1)S(1)}, bf16[4,320,128]{2,1,0:T(8,128)(2,1)S(1)}, u32[]{:S(2)}, u32[]{:S(2)}) collective-permute-start(bf16[4,320,128]{2,1,0:T(8,128)(2,1)S(1)} %all-to-all-done.refs_0_.refs_8_), channel_id=1, source_target_pairs={{0,2},{1,3},{2,0},{3,1},{4,6},{5,7},{6,4},{7,5},{8,10},{9,11},{10,... | collective-permute-start | bytes 983048 | tf_op jit(solution)/shard_map/ppermute | solution.py:45
  75.5 0.0 collective-permute-done.6.refs_2_
  75.5 1.4 collective-permute-done.7.refs_6_
  77.0 0.0 collective-permute-done.8.refs_9_
  77.0 1.9 %collective-permute-start.9 = (bf16[272,512]{1,0:T(8,128)(2,1)S(1)}, bf16[272,512]{1,0:T(8,128)(2,1)S(1)}, u32[]{:S(2)}, u32[]{:S(2)}) collective-permute-start(bf16[272,512]{1,0:T(8,128)(2,1)S(1)} %collective-permute-done.6.refs_2_), channel_id=1, source_target_pairs={{0,224},{1,225},{2,226},{3,227},{4,228},{5,229},{6,230},{7,231},{8... | collective-permute-start | bytes 835592 | tf_op jit(solution)/shard_map/ppermute | solution.py:45
  78.9 1.9 %collective-permute-start.13 = (bf16[4,320,128]{2,1,0:T(8,128)(2,1)S(1)}, bf16[4,320,128]{2,1,0:T(8,128)(2,1)S(1)}, u32[]{:S(2)}, u32[]{:S(2)}) collective-permute-start(bf16[4,320,128]{2,1,0:T(8,128)(2,1)S(1)} %all-to-all-done.refs_0_.refs_8_), channel_id=1, source_target_pairs={{0,1},{1,2},{2,3},{3,0},{4,5},{5,6},{6,7},{7,4},{8,9},{9,10},{10,1... | collective-permute-start | bytes 983048 | tf_op jit(solution)/shard_map/ppermute | solution.py:45
  80.8 5.6 %collective-permute-start.12 = (bf16[272,512]{1,0:T(8,128)(2,1)S(1)}, bf16[272,512]{1,0:T(8,128)(2,1)S(1)}, u32[]{:S(2)}, u32[]{:S(2)}) collective-permute-start(bf16[272,512]{1,0:T(8,128)(2,1)S(1)} %collective-permute-done.7.refs_6_), channel_id=1, source_target_pairs={{0,32},{1,33},{2,34},{3,35},{4,36},{5,37},{6,38},{7,39},{8,40},{9,... | collective-permute-start | bytes 835592 | tf_op jit(solution)/shard_map/ppermute | solution.py:45
  86.4 0.0 collective-permute-done.10.refs_10_
  86.4 0.6 collective-permute-done.9.refs_3_
  87.1 1.9 %collective-permute-start.11 = (bf16[272,512]{1,0:T(8,128)(2,1)S(1)}, bf16[272,512]{1,0:T(8,128)(2,1)S(1)}, u32[]{:S(2)}, u32[]{:S(2)}) collective-permute-start(bf16[272,512]{1,0:T(8,128)(2,1)S(1)} %collective-permute-done.9.refs_3_), channel_id=1, source_target_pairs={{0,224},{1,225},{2,226},{3,227},{4,228},{5,229},{6,230},{7,231},{8... | collective-permute-start | bytes 835592 | tf_op jit(solution)/shard_map/ppermute | solution.py:45
  89.0 0.1 collective-permute-done.13.refs_11_
  89.1 1.4 collective-permute-done.12.refs_7_
  90.5 6.3 %collective-permute-done.11.refs_4_ = bf16[272,512]{1,0:T(8,128)(2,1)S(1)} collective-permute-done((bf16[272,512]{1,0:T(8,128)(2,1)S(1)}, bf16[272,512]{1,0:T(8,128)(2,1)S(1)}, u32[]{:S(2)}, u32[]{:S(2)}) %collective-permute-start.11) | collective-permute-done | bytes 278560 | tf_op jit(solution)/shard_map/ppermute | solution.py:45
  96.7 1.5 gradient.1
  98.2 1.3 collective-permute-start.14
  99.6 1.7 %collective-permute-done.14.got_ref = f32[320,512]{1,0:T(8,128)S(1)} collective-permute-done((f32[320,512]{1,0:T(8,128)S(1)}, f32[320,512]{1,0:T(8,128)S(1)}, u32[]{:S(2)}, u32[]{:S(2)}) %collective-permute-start.14) | collective-permute-done | bytes 655392 | tf_op jit(solution)/shard_map/ppermute | solution.py:45
  101.2 0.0 copy-done.3
  101.2 0.0 copy-done.4
  101.2 0.5 adam.1.update_ref
  101.7 1.3 collective-permute-start.15
  103.0 2.2 %collective-permute-done.15.update_got = bf16[320,512]{1,0:T(8,128)(2,1)S(1)} collective-permute-done((bf16[320,512]{1,0:T(8,128)(2,1)S(1)}, bf16[320,512]{1,0:T(8,128)(2,1)S(1)}, u32[]{:S(2)}, u32[]{:S(2)}) %collective-permute-start.15) | collective-permute-done | bytes 327712 | tf_op jit(solution)/shard_map/ppermute | solution.py:45
  105.2 1.5 step.1
  106.7 19.0 %all_to_all.15 = f32[16,8,320]{2,1,0:T(8,128)S(1)} all-to-all(f32[16,8,320]{2,1,0:T(8,128)S(1)} %get-tuple-element.29), channel_id=1, replica_groups=mesh['group'=2,'y'=8,'z_hi'=2,'z_lo'=4,'x'=4] {'z_lo','x'}, dimensions={0} | all-to-all | bytes 327680 | tf_op jit(solution)/shard_map/all_to_all | solution.py:49
  125.7 2.7 %collective-permute-start.16 = (bf16[8,320]{1,0:T(8,128)(2,1)S(1)}, bf16[8,320]{1,0:T(8,128)(2,1)S(1)}, u32[]{:S(2)}, u32[]{:S(2)}) collective-permute-start(bf16[8,320]{1,0:T(8,128)(2,1)S(1)} %reduce_sum.9), channel_id=1, source_target_pairs={{0,0},{1,16},{2,32},{3,48},{4,64},{5,80},{6,96},{7,112},{8,128},{9... | collective-permute-start | bytes 15368 | tf_op jit(solution)/shard_map/ppermute | solution.py:45
  128.4 7.9 %collective-permute-done.16 = bf16[8,320]{1,0:T(8,128)(2,1)S(1)} collective-permute-done((bf16[8,320]{1,0:T(8,128)(2,1)S(1)}, bf16[8,320]{1,0:T(8,128)(2,1)S(1)}, u32[]{:S(2)}, u32[]{:S(2)}) %collective-permute-start.16) | collective-permute-done | bytes 5152 | tf_op jit(solution)/shard_map/ppermute | solution.py:45
  136.3 14.2 %all_to_all.16 = bf16[16,8,320]{2,1,0:T(8,128)(2,1)S(1)} all-to-all(bf16[16,8,320]{2,1,0:T(8,128)(2,1)S(1)} %broadcast_in_dim.5), channel_id=1, replica_groups=mesh['group'=2,'y'=8,'z_hi'=2,'z_lo'=4,'x'=4] {'z_lo','x'}, dimensions={0} | all-to-all | bytes 163840 | tf_op jit(solution)/shard_map/all_to_all | solution.py:49
  150.6 0.8 reshape.13
  (12 shorter events, 0.1 us)
Async XLA Ops:
  0.6 6.0 %copy-start.10 = (s32[4,2]{0,1:T(2,128)S(1)}, s32[4,2]{0,1:T(2,128)}, u32[]{:S(2)}) copy-start(s32[4,2]{0,1:T(2,128)} %param.23) | copy-start | bytes 100
  0.6 6.0 %copy-start.11 = (s32[2]{0:T(128)S(1)}, s32[2]{0:T(128)}, u32[]{:S(2)}) copy-start(s32[2]{0:T(128)} %lengths_ref.1) | copy-start | bytes 28
  0.7 6.0 %copy-start.8 = (bf16[4,2,1024]{2,1,0:T(2,128)(2,1)S(1)}, bf16[4,2,1024]{2,1,0:T(2,128)(2,1)}, u32[]{:S(2)}) copy-start(bf16[4,2,1024]{2,1,0:T(2,128)(2,1)} %nv_ref.1) | copy-start | bytes 49156
  0.7 6.0 %copy-start.7 = (bf16[4,2,1024]{2,1,0:T(2,128)(2,1)S(1)}, bf16[4,2,1024]{2,1,0:T(2,128)(2,1)}, u32[]{:S(2)}) copy-start(bf16[4,2,1024]{2,1,0:T(2,128)(2,1)} %nk_ref.1) | copy-start | bytes 49156
  0.7 6.0 %copy-start.9 = (bf16[4,2,512]{2,1,0:T(2,128)(2,1)S(1)}, bf16[4,2,512]{2,1,0:T(2,128)(2,1)}, u32[]{:S(2)}) copy-start(bf16[4,2,512]{2,1,0:T(2,128)(2,1)} %q_ref.1) | copy-start | bytes 24580
  0.8 1.7 %copy-start = (bf16[1,256,5120]{2,1,0:T(8,128)(2,1)S(1)}, bf16[1,256,5120]{2,1,0:T(8,128)(2,1)}, u32[]{:S(2)}) copy-start(bf16[1,256,5120]{2,1,0:T(8,128)(2,1)} %param.13) | copy-start | bytes 7864324
  2.5 2.7 %copy-start.6 = (bf16[1,256,512]{2,1,0:T(8,128)(2,1)S(1)}, bf16[1,256,512]{2,1,0:T(8,128)(2,1)}, u32[]{:S(2)}) copy-start(bf16[1,256,512]{2,1,0:T(8,128)(2,1)} %param.12) | copy-start | bytes 786436
  2.5 4.1 %copy-start.1 = (bf16[2,2048,128]{2,1,0:T(8,128)(2,1)S(1)}, bf16[2,2048,128]{2,1,0:T(8,128)(2,1)}, u32[]{:S(2)}) copy-start(bf16[2,2048,128]{2,1,0:T(8,128)(2,1)} %k_ref.1) | copy-start | bytes 3145732
  2.5 4.1 %copy-start.2 = (bf16[2,2048,128]{2,1,0:T(8,128)(2,1)S(1)}, bf16[2,2048,128]{2,1,0:T(8,128)(2,1)}, u32[]{:S(2)}) copy-start(bf16[2,2048,128]{2,1,0:T(8,128)(2,1)} %v_ref.1) | copy-start | bytes 3145732
  3.3 4.4 %collective-permute-start.1 = (bf16[320,128]{1,0:T(8,128)(2,1)S(1)}, bf16[320,128]{1,0:T(8,128)(2,1)S(1)}, u32[]{:S(2)}, u32[]{:S(2)}) collective-permute-start(bf16[320,128]{1,0:T(8,128)(2,1)S(1)} %get-tuple-element.16), channel_id=1, source_target_pairs={{256,256},{257,272},{258,288},{259,304},{260,320},{261,336},{262,3... | collective-permute-start | bytes 245768 | tf_op jit(solution)/shard_map/ppermute | solution.py:45
  4.0 11.0 %collective-permute-start.2 = (bf16[320,128]{1,0:T(8,128)(2,1)S(1)}, bf16[320,128]{1,0:T(8,128)(2,1)S(1)}, u32[]{:S(2)}, u32[]{:S(2)}) collective-permute-start(bf16[320,128]{1,0:T(8,128)(2,1)S(1)} %get-tuple-element.17), channel_id=1, source_target_pairs={{256,0},{257,16},{258,32},{259,48},{260,64},{261,80},{262,96},{263... | collective-permute-start | bytes 245768 | tf_op jit(solution)/shard_map/ppermute | solution.py:45
  5.3 9.7 %collective-permute-start = (bf16[256,512]{1,0:T(8,128)(2,1)S(1)}, bf16[256,512]{1,0:T(8,128)(2,1)S(1)}, u32[]{:S(2)}, u32[]{:S(2)}) collective-permute-start(bf16[256,512]{1,0:T(8,128)(2,1)S(1)} %bitcast.22), channel_id=1, source_target_pairs={{256,0},{257,1},{258,2},{259,3},{260,4},{261,5},{262,6},{263,7},{2... | collective-permute-start | bytes 786440 | tf_op jit(solution)/shard_map/ppermute | solution.py:45
  16.3 84.9 %copy-start.3 = (f32[1,512,320]{1,2,0:T(8,128)S(1)}, f32[1,512,320]{1,2,0:T(8,128)}, u32[]{:S(2)}) copy-start(f32[1,512,320]{1,2,0:T(8,128)} %param.15) | copy-start | bytes 1966084
  16.3 84.9 %copy-start.4 = (f32[1,512,320]{1,2,0:T(8,128)S(1)}, f32[1,512,320]{1,2,0:T(8,128)}, u32[]{:S(2)}) copy-start(f32[1,512,320]{1,2,0:T(8,128)} %param.16) | copy-start | bytes 1966084
  16.3 28.5 %all-to-all-start = ((bf16[4,320,128]{2,1,0:T(8,128)(2,1)}), bf16[4,320,128]{2,1,0:T(8,128)(2,1)S(1)}, u32[]{:S(2)}, u32[]{:S(2)}) async-start(bf16[4,320,128]{2,1,0:T(8,128)(2,1)} %broadcast_in_dim.4), calls=%async_computation | async-start | bytes 655360 | tf_op jit(solution)/shard_map/all_to_all | solution.py:49
  27.2 17.7 %collective-permute-start.3 = (bf16[144,512]{1,0:T(8,128)(2,1)S(1)}, bf16[144,512]{1,0:T(8,128)(2,1)S(1)}, u32[]{:S(2)}, u32[]{:S(2)}) collective-permute-start(bf16[144,512]{1,0:T(8,128)(2,1)S(1)} %half.1.mine_ref), channel_id=1, source_target_pairs={{0,16},{1,17},{2,18},{3,19},{4,20},{5,21},{6,22},{7,23},{8,24},{9,... | collective-permute-start | bytes 442376 | tf_op jit(solution)/shard_map/ppermute | solution.py:45
  44.9 60.3 %copy-start.5 = (bf16[512,320]{0,1:T(8,128)(2,1)S(1)}, bf16[512,320]{0,1:T(8,128)(2,1)}, u32[]{:S(2)}) copy-start(bf16[512,320]{0,1:T(8,128)(2,1)} %param.14) | copy-start | bytes 983044
  44.9 8.6 %collective-permute-start.5 = (bf16[272,512]{1,0:T(8,128)(2,1)S(1)}, bf16[272,512]{1,0:T(8,128)(2,1)S(1)}, u32[]{:S(2)}, u32[]{:S(2)}) collective-permute-start(bf16[272,512]{1,0:T(8,128)(2,1)S(1)} %base.1.refs_0_), channel_id=1, source_target_pairs={{0,32},{1,33},{2,34},{3,35},{4,36},{5,37},{6,38},{7,39},{8,40},{9,... | collective-permute-start | bytes 835592 | tf_op jit(solution)/shard_map/ppermute | solution.py:45
  48.2 9.7 %collective-permute-start.4 = (bf16[272,512]{1,0:T(8,128)(2,1)S(1)}, bf16[272,512]{1,0:T(8,128)(2,1)S(1)}, u32[]{:S(2)}, u32[]{:S(2)}) collective-permute-start(bf16[272,512]{1,0:T(8,128)(2,1)S(1)} %base.1.refs_0_), channel_id=1, source_target_pairs={{0,224},{1,225},{2,226},{3,227},{4,228},{5,229},{6,230},{7,231},{8... | collective-permute-start | bytes 835592 | tf_op jit(solution)/shard_map/ppermute | solution.py:45
  57.9 19.1 %collective-permute-start.8 = (bf16[4,320,128]{2,1,0:T(8,128)(2,1)S(1)}, bf16[4,320,128]{2,1,0:T(8,128)(2,1)S(1)}, u32[]{:S(2)}, u32[]{:S(2)}) collective-permute-start(bf16[4,320,128]{2,1,0:T(8,128)(2,1)S(1)} %all-to-all-done.refs_0_.refs_8_), channel_id=1, source_target_pairs={{0,3},{1,0},{2,1},{3,2},{4,7},{5,4},{6,5},{7,6},{8,11},{9,8},{10,9... | collective-permute-start | bytes 983048 | tf_op jit(solution)/shard_map/ppermute | solution.py:45
  63.7 11.9 %collective-permute-start.6 = (bf16[272,512]{1,0:T(8,128)(2,1)S(1)}, bf16[272,512]{1,0:T(8,128)(2,1)S(1)}, u32[]{:S(2)}, u32[]{:S(2)}) collective-permute-start(bf16[272,512]{1,0:T(8,128)(2,1)S(1)} %collective-permute-done.4.refs_1_), channel_id=1, source_target_pairs={{0,224},{1,225},{2,226},{3,227},{4,228},{5,229},{6,230},{7,231},{8... | collective-permute-start | bytes 835592 | tf_op jit(solution)/shard_map/ppermute | solution.py:45
  65.6 11.4 %collective-permute-start.7 = (bf16[272,512]{1,0:T(8,128)(2,1)S(1)}, bf16[272,512]{1,0:T(8,128)(2,1)S(1)}, u32[]{:S(2)}, u32[]{:S(2)}) collective-permute-start(bf16[272,512]{1,0:T(8,128)(2,1)S(1)} %collective-permute-done.5.refs_5_), channel_id=1, source_target_pairs={{0,32},{1,33},{2,34},{3,35},{4,36},{5,37},{6,38},{7,39},{8,40},{9,... | collective-permute-start | bytes 835592 | tf_op jit(solution)/shard_map/ppermute | solution.py:45
  70.7 15.7 %collective-permute-start.10 = (bf16[4,320,128]{2,1,0:T(8,128)(2,1)S(1)}, bf16[4,320,128]{2,1,0:T(8,128)(2,1)S(1)}, u32[]{:S(2)}, u32[]{:S(2)}) collective-permute-start(bf16[4,320,128]{2,1,0:T(8,128)(2,1)S(1)} %all-to-all-done.refs_0_.refs_8_), channel_id=1, source_target_pairs={{0,2},{1,3},{2,0},{3,1},{4,6},{5,7},{6,4},{7,5},{8,10},{9,11},{10,... | collective-permute-start | bytes 983048 | tf_op jit(solution)/shard_map/ppermute | solution.py:45
  77.0 10.1 %collective-permute-start.9 = (bf16[272,512]{1,0:T(8,128)(2,1)S(1)}, bf16[272,512]{1,0:T(8,128)(2,1)S(1)}, u32[]{:S(2)}, u32[]{:S(2)}) collective-permute-start(bf16[272,512]{1,0:T(8,128)(2,1)S(1)} %collective-permute-done.6.refs_2_), channel_id=1, source_target_pairs={{0,224},{1,225},{2,226},{3,227},{4,228},{5,229},{6,230},{7,231},{8... | collective-permute-start | bytes 835592 | tf_op jit(solution)/shard_map/ppermute | solution.py:45
  78.9 10.2 %collective-permute-start.13 = (bf16[4,320,128]{2,1,0:T(8,128)(2,1)S(1)}, bf16[4,320,128]{2,1,0:T(8,128)(2,1)S(1)}, u32[]{:S(2)}, u32[]{:S(2)}) collective-permute-start(bf16[4,320,128]{2,1,0:T(8,128)(2,1)S(1)} %all-to-all-done.refs_0_.refs_8_), channel_id=1, source_target_pairs={{0,1},{1,2},{2,3},{3,0},{4,5},{5,6},{6,7},{7,4},{8,9},{9,10},{10,1... | collective-permute-start | bytes 983048 | tf_op jit(solution)/shard_map/ppermute | solution.py:45
  80.8 9.7 %collective-permute-start.12 = (bf16[272,512]{1,0:T(8,128)(2,1)S(1)}, bf16[272,512]{1,0:T(8,128)(2,1)S(1)}, u32[]{:S(2)}, u32[]{:S(2)}) collective-permute-start(bf16[272,512]{1,0:T(8,128)(2,1)S(1)} %collective-permute-done.7.refs_6_), channel_id=1, source_target_pairs={{0,32},{1,33},{2,34},{3,35},{4,36},{5,37},{6,38},{7,39},{8,40},{9,... | collective-permute-start | bytes 835592 | tf_op jit(solution)/shard_map/ppermute | solution.py:45
  87.1 9.6 %collective-permute-start.11 = (bf16[272,512]{1,0:T(8,128)(2,1)S(1)}, bf16[272,512]{1,0:T(8,128)(2,1)S(1)}, u32[]{:S(2)}, u32[]{:S(2)}) collective-permute-start(bf16[272,512]{1,0:T(8,128)(2,1)S(1)} %collective-permute-done.9.refs_3_), channel_id=1, source_target_pairs={{0,224},{1,225},{2,226},{3,227},{4,228},{5,229},{6,230},{7,231},{8... | collective-permute-start | bytes 835592 | tf_op jit(solution)/shard_map/ppermute | solution.py:45
  98.2 3.0 %collective-permute-start.14 = (f32[320,512]{1,0:T(8,128)S(1)}, f32[320,512]{1,0:T(8,128)S(1)}, u32[]{:S(2)}, u32[]{:S(2)}) collective-permute-start(f32[320,512]{1,0:T(8,128)S(1)} %get-tuple-element.26.mine_ref), channel_id=1, source_target_pairs={{0,256},{1,257},{2,258},{3,259},{4,260},{5,261},{6,262},{7,263},{8... | collective-permute-start | bytes 1966088 | tf_op jit(solution)/shard_map/ppermute | solution.py:45
  101.7 3.5 %collective-permute-start.15 = (bf16[320,512]{1,0:T(8,128)(2,1)S(1)}, bf16[320,512]{1,0:T(8,128)(2,1)S(1)}, u32[]{:S(2)}, u32[]{:S(2)}) collective-permute-start(bf16[320,512]{1,0:T(8,128)(2,1)S(1)} %adam.1.update_ref), channel_id=1, source_target_pairs={{256,0},{257,1},{258,2},{259,3},{260,4},{261,5},{262,6},{263,7},{2... | collective-permute-start | bytes 983048 | tf_op jit(solution)/shard_map/ppermute | solution.py:45
  125.7 10.6 %collective-permute-start.16 = (bf16[8,320]{1,0:T(8,128)(2,1)S(1)}, bf16[8,320]{1,0:T(8,128)(2,1)S(1)}, u32[]{:S(2)}, u32[]{:S(2)}) collective-permute-start(bf16[8,320]{1,0:T(8,128)(2,1)S(1)} %reduce_sum.9), channel_id=1, source_target_pairs={{0,0},{1,16},{2,32},{3,48},{4,64},{5,80},{6,96},{7,112},{8,128},{9... | collective-permute-start | bytes 15368 | tf_op jit(solution)/shard_map/ppermute | solution.py:45

commit v10 on v9

--- a/solution.py
+++ b/solution.py
@@ -61,8 +61,15 @@
     return (g, zl * 2 + (x >> 1), x & 1, y >> 1, (y & 1) * 2 + zh)
 
 
-def cot_transposed(core):
-    return lambda g, *place: (core, *transposed(g, *place)[1:]) if g == 1 else None
+def shift_of(z_lo, x):
+    return 4 * (z_lo >> 1) + x - 3
+
+
+def cot_shifted(core):
+    def target(g, y, zh, zl, x):
+        return (core, (y - shift_of(zl, x)) % 8, zh ^ (zl & 1), zl, x) if g == 1 else None
+
+    return target
 
 
 def along_x(step):
@@ -212,7 +219,8 @@
 
 
 def cut_kernel(place_ref, cot_ref, one_ref, two_ref, window, turned, sem):
-    q = place_ref[3] * 4 + place_ref[4]
+    z_lo = place_ref[3]
+    q = 2 * ((place_ref[1] - shift_of(z_lo, place_ref[4])) & 7) + (place_ref[2] ^ (z_lo & 1))
     start = pl.multiple_of(((q * 5) >> 1) * 128, 128)
     copy = pltpu.make_async_copy(cot_ref.at[:, pl.ds(start, 384)], window, sem)
     copy.start()
@@ -244,16 +252,18 @@
     chunks, blocks, (out_ref, rows_ref, block_rows) = refs[:8], refs[8:12], refs[12:]
     side, y, z_hi, x = (place_ref[n] for n in (0, 1, 2, 4))
     for n, hop in enumerate(HOPS):
-        block_y = jnp.where(side == 1, y - hop, y + hop) & 7
+        shift = jnp.where(side == 1, 4 if hop == 4 else -hop, hop)
+        block_y = (y + shift) & 7
         rows = chunks[n][TOK:, :].astype(f32)
         for other in range(2):
             block_zh = z_hi if other == 0 else 1 - z_hi
             span = slice(other * HALF, (other + 1) * HALF)
-            source = 2 * (block_y & 1) + block_zh - x
+            z_lo = 2 * ((shift + 3) >> 2) + other
+            source = (shift + 3) - x
             source = jnp.where(side == 1, -source, source) & 3
-            block = blocks[0][block_y >> 1]
+            block = blocks[0][z_lo]
             for m in range(1, 4):
-                block = jnp.where(source == m, blocks[m][block_y >> 1], block)
+                block = jnp.where(source == m, blocks[m][z_lo], block)
             block_rows[:, span] = block
             place = pl.multiple_of((2 * block_y + block_zh) * ROWS, ROWS)
             rows_ref[pl.ds(place, ROWS), :] = rows[other * ROWS : (other + 1) * ROWS]
@@ -348,8 +358,8 @@
     act = activations[0]
     act_got = permute(act, to_rollout)
     cut_one, cut_two = cut_of(place, cotangent[0])
-    own_one = permute(cut_one, cot_transposed(1))
-    own_two = permute(cut_two, cot_transposed(0))
+    own_one = permute(cut_one, cot_shifted(1))
+    own_two = permute(cut_two, cot_shifted(0))
     rows = attend(
         (q >> 1).reshape(1),
         queries,
@@ -361,11 +371,12 @@
         token_ids.T,
     )
     half = half_of(place, act, act_got, rows)
+    own_one, own_two, _ = lax.optimization_barrier((own_one, own_two, half))
     own = jnp.where(place[0] == 1, own_one, own_two)
-    half_tied, own = lax.optimization_barrier((half, own))
-    half_got = permute(half_tied, to_partner)
-    line = gather(jnp.broadcast_to(own[None], (4, COLS, HALF)), "z_lo")
-    base = base_of((half, half_got), (line,))
+    own_spread = jnp.broadcast_to(own[None], (4, COLS, HALF))
+    line = gather(own_spread, "z_lo")
+    half_got = permute(half, to_partner)
+    base = base_of((half, half_got), (own_spread,))
     first = [permute(base, along_y(1))]
     second = [permute(base, along_y(-1))]
     line_tied, ahead, back = lax.optimization_barrier((line, first[0], second[0]))

time: 152 us -> 152 us (level)
  waiting for transfers between devices: 41.6 us -> 50.1 us
  starting transfers between devices: 66.3 us -> 58.2 us
    ppermute x17, waiting for transfers between devices: 41.6 us -> 50.1 us  [permute(): return lax.ppermute(value, AXES, pairs)]
    ppermute x17, starting transfers between devices: 55.4 us -> 49.9 us  [permute(): return lax.ppermute(value, AXES, pairs)]
    all_to_all x1, starting transfers between devices: 10.8 us -> 8.32 us  [gather(): return lax.all_to_all(value, axes, split_axis=0, concat_axis=0, tiled=True)]
  transfers between devices with their start and end apart: 18 -> 18, of which waited for: 12 -> 13; matrix products, arithmetic and copies ran while one was open for 0% -> 0% of each run, Pallas kernels for 1% -> 2%
where the time goes in v10:
time: 152 us; the launch traced here: 151 us
  starting transfers between devices  58.2 us (38%)
  waiting for transfers between devices  50.1 us (33%)
  blocking collectives  32.3 us (21%)
  Pallas kernels  6.04 us (4%)
  local copies, waits for them, and re-layouts  3.45 us (2%)
    ppermute x17, waiting for transfers between devices, permute(): return lax.ppermute(value, AXES, pairs)  50.1 us
    ppermute x17, starting transfers between devices, permute(): return lax.ppermute(value, AXES, pairs)  49.9 us
    all_to_all x2, blocking collectives, gather(): return lax.all_to_all(value, axes, split_axis=0, concat_axis=0, tiled=True)  32.3 us
    all_to_all x1, starting transfers between devices, gather(): return lax.all_to_all(value, axes, split_axis=0, concat_axis=0, tiled=True)  8.32 us
  transfers between devices with their start and end apart: 18, of which 13 were waited for; matrix products, arithmetic and copies ran while one was open for 0% of the time, Pallas kernels for 2%

profile of v10, /device:TPU:24, one launch (start us, length us, event | category | flops | bytes accessed | tf_op | source)
XLA Modules:
  0.0 151.0 jit_solution(8847798882756960921)
XLA Ops:
  0.6 0.0 copy-start.10
  0.6 0.0 copy-start.11
  0.7 0.0 copy-start.8
  0.7 0.0 copy-start.7
  0.7 0.0 copy-start.9
  0.7 1.4 collective-permute-start
  2.1 0.1 stack.23.place_ref
  2.2 1.7 %copy-done = bf16[1,256,5120]{2,1,0:T(8,128)(2,1)S(1)} copy-done((bf16[1,256,5120]{2,1,0:T(8,128)(2,1)S(1)}, bf16[1,256,5120]{2,1,0:T(8,128)(2,1)}, u32[]{:S(2)}) %copy-start) | copy-done | bytes 2621464
  4.0 0.8 cut.1
  4.7 0.7 collective-permute-start.2
  5.4 1.3 collective-permute-start.3
  6.7 0.0 copy-done.10
  6.7 0.0 copy-done.11
  6.7 0.0 copy-done.8
  6.7 0.0 copy-done.7
  6.7 0.0 copy-done.9
  6.8 0.0 copy-done.1
  6.8 0.0 copy-done.2
  6.8 1.0 attend.1.rows_ref
  7.8 0.0 collective-permute-done.act_got
  7.8 0.0 copy-done.6
  7.8 0.6 half.1.mine_ref
  8.4 0.0 collective-permute-done.2
  8.4 10.0 %collective-permute-done.3 = bf16[320,128]{1,0:T(8,128)(2,1)S(1)} collective-permute-done((bf16[320,128]{1,0:T(8,128)(2,1)S(1)}, bf16[320,128]{1,0:T(8,128)(2,1)S(1)}, u32[]{:S(2)}, u32[]{:S(2)}) %collective-permute-start.3) | collective-permute-done | bytes 81952 | tf_op jit(solution)/shard_map/ppermute | solution.py:45
  18.4 0.8 broadcast_in_dim.4.refs_0_
  19.2 8.3 %all-to-all-start = ((bf16[4,320,128]{2,1,0:T(8,128)(2,1)}), bf16[4,320,128]{2,1,0:T(8,128)(2,1)S(1)}, u32[]{:S(2)}, u32[]{:S(2)}) async-start(bf16[4,320,128]{2,1,0:T(8,128)(2,1)} %broadcast_in_dim.4.refs_0_), calls=%async_computation | async-start | bytes 655360 | tf_op jit(solution)/shard_map/all_to_all | solution.py:49
  27.5 7.9 %collective-permute-start.1 = (bf16[144,512]{1,0:T(8,128)(2,1)S(1)}, bf16[144,512]{1,0:T(8,128)(2,1)S(1)}, u32[]{:S(2)}, u32[]{:S(2)}) collective-permute-start(bf16[144,512]{1,0:T(8,128)(2,1)S(1)} %half.1.mine_ref), channel_id=1, source_target_pairs={{0,16},{1,17},{2,18},{3,19},{4,20},{5,21},{6,22},{7,23},{8,24},{9,... | collective-permute-start | bytes 442376 | tf_op jit(solution)/shard_map/ppermute | solution.py:45
  35.4 7.1 %collective-permute-done.1.got_ref = bf16[144,512]{1,0:T(8,128)(2,1)S(1)} collective-permute-done((bf16[144,512]{1,0:T(8,128)(2,1)S(1)}, bf16[144,512]{1,0:T(8,128)(2,1)S(1)}, u32[]{:S(2)}, u32[]{:S(2)}) %collective-permute-start.1) | collective-permute-done | bytes 147488 | tf_op jit(solution)/shard_map/ppermute | solution.py:45
  42.5 0.0 copy-start.5
  42.5 6.7 %collective-permute-start.5 = (bf16[272,512]{1,0:T(8,128)(2,1)S(1)}, bf16[272,512]{1,0:T(8,128)(2,1)S(1)}, u32[]{:S(2)}, u32[]{:S(2)}) collective-permute-start(bf16[272,512]{1,0:T(8,128)(2,1)S(1)} %base.1.refs_0_), channel_id=1, source_target_pairs={{0,32},{1,33},{2,34},{3,35},{4,36},{5,37},{6,38},{7,39},{8,40},{9,... | collective-permute-start | bytes 835592 | tf_op jit(solution)/shard_map/ppermute | solution.py:45
  49.2 1.9 %collective-permute-start.4 = (bf16[272,512]{1,0:T(8,128)(2,1)S(1)}, bf16[272,512]{1,0:T(8,128)(2,1)S(1)}, u32[]{:S(2)}, u32[]{:S(2)}) collective-permute-start(bf16[272,512]{1,0:T(8,128)(2,1)S(1)} %base.1.refs_0_), channel_id=1, source_target_pairs={{0,224},{1,225},{2,226},{3,227},{4,228},{5,229},{6,230},{7,231},{8... | collective-permute-start | bytes 835592 | tf_op jit(solution)/shard_map/ppermute | solution.py:45
  51.1 2.8 %collective-permute-done.5.refs_5_ = bf16[272,512]{1,0:T(8,128)(2,1)S(1)} collective-permute-done((bf16[272,512]{1,0:T(8,128)(2,1)S(1)}, bf16[272,512]{1,0:T(8,128)(2,1)S(1)}, u32[]{:S(2)}, u32[]{:S(2)}) %collective-permute-start.5) | collective-permute-done | bytes 278560 | tf_op jit(solution)/shard_map/ppermute | solution.py:45
  53.9 4.9 %collective-permute-done.4.refs_1_ = bf16[272,512]{1,0:T(8,128)(2,1)S(1)} collective-permute-done((bf16[272,512]{1,0:T(8,128)(2,1)S(1)}, bf16[272,512]{1,0:T(8,128)(2,1)S(1)}, u32[]{:S(2)}, u32[]{:S(2)}) %collective-permute-start.4) | collective-permute-done | bytes 278560 | tf_op jit(solution)/shard_map/ppermute | solution.py:45
  58.8 0.0 all-to-all-done.refs_8_
  58.8 5.1 %collective-permute-start.8 = (bf16[4,320,128]{2,1,0:T(8,128)(2,1)S(1)}, bf16[4,320,128]{2,1,0:T(8,128)(2,1)S(1)}, u32[]{:S(2)}, u32[]{:S(2)}) collective-permute-start(bf16[4,320,128]{2,1,0:T(8,128)(2,1)S(1)} %all-to-all-done.refs_8_), channel_id=1, source_target_pairs={{0,3},{1,0},{2,1},{3,2},{4,7},{5,4},{6,5},{7,6},{8,11},{9,8},{10,9... | collective-permute-start | bytes 983048 | tf_op jit(solution)/shard_map/ppermute | solution.py:45
  64.0 1.9 %collective-permute-start.6 = (bf16[272,512]{1,0:T(8,128)(2,1)S(1)}, bf16[272,512]{1,0:T(8,128)(2,1)S(1)}, u32[]{:S(2)}, u32[]{:S(2)}) collective-permute-start(bf16[272,512]{1,0:T(8,128)(2,1)S(1)} %collective-permute-done.4.refs_1_), channel_id=1, source_target_pairs={{0,224},{1,225},{2,226},{3,227},{4,228},{5,229},{6,230},{7,231},{8... | collective-permute-start | bytes 835592 | tf_op jit(solution)/shard_map/ppermute | solution.py:45
  65.9 5.1 %collective-permute-start.7 = (bf16[272,512]{1,0:T(8,128)(2,1)S(1)}, bf16[272,512]{1,0:T(8,128)(2,1)S(1)}, u32[]{:S(2)}, u32[]{:S(2)}) collective-permute-start(bf16[272,512]{1,0:T(8,128)(2,1)S(1)} %collective-permute-done.5.refs_5_), channel_id=1, source_target_pairs={{0,32},{1,33},{2,34},{3,35},{4,36},{5,37},{6,38},{7,39},{8,40},{9,... | collective-permute-start | bytes 835592 | tf_op jit(solution)/shard_map/ppermute | solution.py:45
  71.0 1.9 %collective-permute-start.10 = (bf16[4,320,128]{2,1,0:T(8,128)(2,1)S(1)}, bf16[4,320,128]{2,1,0:T(8,128)(2,1)S(1)}, u32[]{:S(2)}, u32[]{:S(2)}) collective-permute-start(bf16[4,320,128]{2,1,0:T(8,128)(2,1)S(1)} %all-to-all-done.refs_8_), channel_id=1, source_target_pairs={{0,2},{1,3},{2,0},{3,1},{4,6},{5,7},{6,4},{7,5},{8,10},{9,11},{10,... | collective-permute-start | bytes 983048 | tf_op jit(solution)/shard_map/ppermute | solution.py:45
  73.0 0.7 collective-permute-done.6.refs_2_
  73.6 3.7 %collective-permute-done.7.refs_6_ = bf16[272,512]{1,0:T(8,128)(2,1)S(1)} collective-permute-done((bf16[272,512]{1,0:T(8,128)(2,1)S(1)}, bf16[272,512]{1,0:T(8,128)(2,1)S(1)}, u32[]{:S(2)}, u32[]{:S(2)}) %collective-permute-start.7) | collective-permute-done | bytes 278560 | tf_op jit(solution)/shard_map/ppermute | solution.py:45
  77.4 0.0 collective-permute-done.8.refs_9_
  77.4 1.9 %collective-permute-start.9 = (bf16[272,512]{1,0:T(8,128)(2,1)S(1)}, bf16[272,512]{1,0:T(8,128)(2,1)S(1)}, u32[]{:S(2)}, u32[]{:S(2)}) collective-permute-start(bf16[272,512]{1,0:T(8,128)(2,1)S(1)} %collective-permute-done.6.refs_2_), channel_id=1, source_target_pairs={{0,224},{1,225},{2,226},{3,227},{4,228},{5,229},{6,230},{7,231},{8... | collective-permute-start | bytes 835592 | tf_op jit(solution)/shard_map/ppermute | solution.py:45
  79.3 1.9 %collective-permute-start.13 = (bf16[4,320,128]{2,1,0:T(8,128)(2,1)S(1)}, bf16[4,320,128]{2,1,0:T(8,128)(2,1)S(1)}, u32[]{:S(2)}, u32[]{:S(2)}) collective-permute-start(bf16[4,320,128]{2,1,0:T(8,128)(2,1)S(1)} %all-to-all-done.refs_8_), channel_id=1, source_target_pairs={{0,1},{1,2},{2,3},{3,0},{4,5},{5,6},{6,7},{7,4},{8,9},{9,10},{10,1... | collective-permute-start | bytes 983048 | tf_op jit(solution)/shard_map/ppermute | solution.py:45
  81.2 5.6 %collective-permute-start.12 = (bf16[272,512]{1,0:T(8,128)(2,1)S(1)}, bf16[272,512]{1,0:T(8,128)(2,1)S(1)}, u32[]{:S(2)}, u32[]{:S(2)}) collective-permute-start(bf16[272,512]{1,0:T(8,128)(2,1)S(1)} %collective-permute-done.7.refs_6_), channel_id=1, source_target_pairs={{0,32},{1,33},{2,34},{3,35},{4,36},{5,37},{6,38},{7,39},{8,40},{9,... | collective-permute-start | bytes 835592 | tf_op jit(solution)/shard_map/ppermute | solution.py:45
  86.8 0.0 collective-permute-done.10.refs_10_
  86.8 0.6 collective-permute-done.9.refs_3_
  87.5 1.9 %collective-permute-start.11 = (bf16[272,512]{1,0:T(8,128)(2,1)S(1)}, bf16[272,512]{1,0:T(8,128)(2,1)S(1)}, u32[]{:S(2)}, u32[]{:S(2)}) collective-permute-start(bf16[272,512]{1,0:T(8,128)(2,1)S(1)} %collective-permute-done.9.refs_3_), channel_id=1, source_target_pairs={{0,224},{1,225},{2,226},{3,227},{4,228},{5,229},{6,230},{7,231},{8... | collective-permute-start | bytes 835592 | tf_op jit(solution)/shard_map/ppermute | solution.py:45
  89.4 0.1 collective-permute-done.13.refs_11_
  89.5 1.4 collective-permute-done.12.refs_7_
  90.9 6.3 %collective-permute-done.11.refs_4_ = bf16[272,512]{1,0:T(8,128)(2,1)S(1)} collective-permute-done((bf16[272,512]{1,0:T(8,128)(2,1)S(1)}, bf16[272,512]{1,0:T(8,128)(2,1)S(1)}, u32[]{:S(2)}, u32[]{:S(2)}) %collective-permute-start.11) | collective-permute-done | bytes 278560 | tf_op jit(solution)/shard_map/ppermute | solution.py:45
  97.1 1.7 %gradient.1 = (f32[320,512]{1,0:T(8,128)S(1)}, f32[128,512]{1,0:T(8,128)S(1)}) custom-call(s32[5]{0:T(128)S(1)} %stack.23.place_ref, bf16[272,512]{1,0:T(8,128)(2,1)S(1)} %base.1.refs_0_, bf16[272,512]{1,0:T(8,128)(2,1)S(1)} %collective-permute-done.4.refs_1_, bf16[272,512]{1,0:T(8,128)(2,1)S(1)} %collective-permute-done.6.refs_2_, ...), custom_call_target="tpu_custom_call" | custom-call | flops 671088640 | bytes 6291456 | tf_op jit(solution)/shard_map/gradient/pallas_call | solution.py:278
  98.9 1.3 collective-permute-start.14
  100.2 1.7 %collective-permute-done.14.got_ref = f32[320,512]{1,0:T(8,128)S(1)} collective-permute-done((f32[320,512]{1,0:T(8,128)S(1)}, f32[320,512]{1,0:T(8,128)S(1)}, u32[]{:S(2)}, u32[]{:S(2)}) %collective-permute-start.14) | collective-permute-done | bytes 655392 | tf_op jit(solution)/shard_map/ppermute | solution.py:45
  101.9 0.0 copy-done.3
  101.9 0.0 copy-done.4
  101.9 0.5 adam.1.update_ref
  102.3 1.3 collective-permute-start.15
  103.6 2.2 %collective-permute-done.15.update_got = bf16[320,512]{1,0:T(8,128)(2,1)S(1)} collective-permute-done((bf16[320,512]{1,0:T(8,128)(2,1)S(1)}, bf16[320,512]{1,0:T(8,128)(2,1)S(1)}, u32[]{:S(2)}, u32[]{:S(2)}) %collective-permute-start.15) | collective-permute-done | bytes 327712 | tf_op jit(solution)/shard_map/ppermute | solution.py:45
  105.8 1.5 step.1
  107.3 18.0 %all_to_all.15 = f32[16,8,320]{2,1,0:T(8,128)S(1)} all-to-all(f32[16,8,320]{2,1,0:T(8,128)S(1)} %get-tuple-element.29), channel_id=1, replica_groups=mesh['group'=2,'y'=8,'z_hi'=2,'z_lo'=4,'x'=4] {'z_lo','x'}, dimensions={0} | all-to-all | bytes 327680 | tf_op jit(solution)/shard_map/all_to_all | solution.py:49
  125.4 2.0 %collective-permute-start.16 = (bf16[8,320]{1,0:T(8,128)(2,1)S(1)}, bf16[8,320]{1,0:T(8,128)(2,1)S(1)}, u32[]{:S(2)}, u32[]{:S(2)}) collective-permute-start(bf16[8,320]{1,0:T(8,128)(2,1)S(1)} %reduce_sum.9), channel_id=1, source_target_pairs={{0,0},{1,16},{2,32},{3,48},{4,64},{5,80},{6,96},{7,112},{8,128},{9... | collective-permute-start | bytes 15368 | tf_op jit(solution)/shard_map/ppermute | solution.py:45
  127.3 8.7 %collective-permute-done.16 = bf16[8,320]{1,0:T(8,128)(2,1)S(1)} collective-permute-done((bf16[8,320]{1,0:T(8,128)(2,1)S(1)}, bf16[8,320]{1,0:T(8,128)(2,1)S(1)}, u32[]{:S(2)}, u32[]{:S(2)}) %collective-permute-start.16) | collective-permute-done | bytes 5152 | tf_op jit(solution)/shard_map/ppermute | solution.py:45
  136.0 14.2 %all_to_all.16 = bf16[16,8,320]{2,1,0:T(8,128)(2,1)S(1)} all-to-all(bf16[16,8,320]{2,1,0:T(8,128)(2,1)S(1)} %broadcast_in_dim.5), channel_id=1, replica_groups=mesh['group'=2,'y'=8,'z_hi'=2,'z_lo'=4,'x'=4] {'z_lo','x'}, dimensions={0} | all-to-all | bytes 163840 | tf_op jit(solution)/shard_map/all_to_all | solution.py:49
  150.3 0.8 reshape.13
  (12 shorter events, 0.1 us)
Async XLA Ops:
  0.6 6.1 %copy-start.10 = (s32[4,2]{0,1:T(2,128)S(1)}, s32[4,2]{0,1:T(2,128)}, u32[]{:S(2)}) copy-start(s32[4,2]{0,1:T(2,128)} %param.23) | copy-start | bytes 100
  0.6 6.1 %copy-start.11 = (s32[2]{0:T(128)S(1)}, s32[2]{0:T(128)}, u32[]{:S(2)}) copy-start(s32[2]{0:T(128)} %lengths_ref.1) | copy-start | bytes 28
  0.7 6.1 %copy-start.8 = (bf16[4,2,1024]{2,1,0:T(2,128)(2,1)S(1)}, bf16[4,2,1024]{2,1,0:T(2,128)(2,1)}, u32[]{:S(2)}) copy-start(bf16[4,2,1024]{2,1,0:T(2,128)(2,1)} %nv_ref.1) | copy-start | bytes 49156
  0.7 6.1 %copy-start.7 = (bf16[4,2,1024]{2,1,0:T(2,128)(2,1)S(1)}, bf16[4,2,1024]{2,1,0:T(2,128)(2,1)}, u32[]{:S(2)}) copy-start(bf16[4,2,1024]{2,1,0:T(2,128)(2,1)} %nk_ref.1) | copy-start | bytes 49156
  0.7 6.1 %copy-start.9 = (bf16[4,2,512]{2,1,0:T(2,128)(2,1)S(1)}, bf16[4,2,512]{2,1,0:T(2,128)(2,1)}, u32[]{:S(2)}) copy-start(bf16[4,2,512]{2,1,0:T(2,128)(2,1)} %q_ref.1) | copy-start | bytes 24580
  0.7 7.1 %collective-permute-start = (bf16[256,512]{1,0:T(8,128)(2,1)}, bf16[256,512]{1,0:T(8,128)(2,1)S(1)}, u32[]{:S(2)}, u32[]{:S(2)}) collective-permute-start(bf16[256,512]{1,0:T(8,128)(2,1)} %bitcast.22), channel_id=1, source_target_pairs={{256,0},{257,1},{258,2},{259,3},{260,4},{261,5},{262,6},{263,7},{2... | collective-permute-start | bytes 786440 | tf_op jit(solution)/shard_map/ppermute | solution.py:45
  2.2 1.7 %copy-start = (bf16[1,256,5120]{2,1,0:T(8,128)(2,1)S(1)}, bf16[1,256,5120]{2,1,0:T(8,128)(2,1)}, u32[]{:S(2)}) copy-start(bf16[1,256,5120]{2,1,0:T(8,128)(2,1)} %param.13) | copy-start | bytes 7864324
  3.9 2.8 %copy-start.1 = (bf16[2,2048,128]{2,1,0:T(8,128)(2,1)S(1)}, bf16[2,2048,128]{2,1,0:T(8,128)(2,1)}, u32[]{:S(2)}) copy-start(bf16[2,2048,128]{2,1,0:T(8,128)(2,1)} %k_ref.1) | copy-start | bytes 3145732
  4.0 2.8 %copy-start.2 = (bf16[2,2048,128]{2,1,0:T(8,128)(2,1)S(1)}, bf16[2,2048,128]{2,1,0:T(8,128)(2,1)}, u32[]{:S(2)}) copy-start(bf16[2,2048,128]{2,1,0:T(8,128)(2,1)} %v_ref.1) | copy-start | bytes 3145732
  4.0 3.9 %copy-start.6 = (bf16[1,256,512]{2,1,0:T(8,128)(2,1)S(1)}, bf16[1,256,512]{2,1,0:T(8,128)(2,1)}, u32[]{:S(2)}) copy-start(bf16[1,256,512]{2,1,0:T(8,128)(2,1)} %param.12) | copy-start | bytes 786436
  4.7 3.7 %collective-permute-start.2 = (bf16[320,128]{1,0:T(8,128)(2,1)S(1)}, bf16[320,128]{1,0:T(8,128)(2,1)S(1)}, u32[]{:S(2)}, u32[]{:S(2)}) collective-permute-start(bf16[320,128]{1,0:T(8,128)(2,1)S(1)} %get-tuple-element.16), channel_id=1, source_target_pairs={{256,352},{257,321},{258,290},{259,259},{260,372},{261,341},{262,3... | collective-permute-start | bytes 245768 | tf_op jit(solution)/shard_map/ppermute | solution.py:45
  5.4 13.0 %collective-permute-start.3 = (bf16[320,128]{1,0:T(8,128)(2,1)S(1)}, bf16[320,128]{1,0:T(8,128)(2,1)S(1)}, u32[]{:S(2)}, u32[]{:S(2)}) collective-permute-start(bf16[320,128]{1,0:T(8,128)(2,1)S(1)} %get-tuple-element.17), channel_id=1, source_target_pairs={{256,96},{257,65},{258,34},{259,3},{260,116},{261,85},{262,54},{26... | collective-permute-start | bytes 245768 | tf_op jit(solution)/shard_map/ppermute | solution.py:45
  19.2 82.7 %copy-start.3 = (f32[1,512,320]{1,2,0:T(8,128)S(1)}, f32[1,512,320]{1,2,0:T(8,128)}, u32[]{:S(2)}) copy-start(f32[1,512,320]{1,2,0:T(8,128)} %param.15) | copy-start | bytes 1966084
  19.2 82.7 %copy-start.4 = (f32[1,512,320]{1,2,0:T(8,128)S(1)}, f32[1,512,320]{1,2,0:T(8,128)}, u32[]{:S(2)}) copy-start(f32[1,512,320]{1,2,0:T(8,128)} %param.16) | copy-start | bytes 1966084
  19.2 39.6 %all-to-all-start = ((bf16[4,320,128]{2,1,0:T(8,128)(2,1)}), bf16[4,320,128]{2,1,0:T(8,128)(2,1)S(1)}, u32[]{:S(2)}, u32[]{:S(2)}) async-start(bf16[4,320,128]{2,1,0:T(8,128)(2,1)} %broadcast_in_dim.4.refs_0_), calls=%async_computation | async-start | bytes 655360 | tf_op jit(solution)/shard_map/all_to_all | solution.py:49
  27.5 14.9 %collective-permute-start.1 = (bf16[144,512]{1,0:T(8,128)(2,1)S(1)}, bf16[144,512]{1,0:T(8,128)(2,1)S(1)}, u32[]{:S(2)}, u32[]{:S(2)}) collective-permute-start(bf16[144,512]{1,0:T(8,128)(2,1)S(1)} %half.1.mine_ref), channel_id=1, source_target_pairs={{0,16},{1,17},{2,18},{3,19},{4,20},{5,21},{6,22},{7,23},{8,24},{9,... | collective-permute-start | bytes 442376 | tf_op jit(solution)/shard_map/ppermute | solution.py:45
  42.5 63.4 %copy-start.5 = (bf16[512,320]{0,1:T(8,128)(2,1)S(1)}, bf16[512,320]{0,1:T(8,128)(2,1)}, u32[]{:S(2)}) copy-start(bf16[512,320]{0,1:T(8,128)(2,1)} %param.14) | copy-start | bytes 983044
  42.5 11.4 %collective-permute-start.5 = (bf16[272,512]{1,0:T(8,128)(2,1)S(1)}, bf16[272,512]{1,0:T(8,128)(2,1)S(1)}, u32[]{:S(2)}, u32[]{:S(2)}) collective-permute-start(bf16[272,512]{1,0:T(8,128)(2,1)S(1)} %base.1.refs_0_), channel_id=1, source_target_pairs={{0,32},{1,33},{2,34},{3,35},{4,36},{5,37},{6,38},{7,39},{8,40},{9,... | collective-permute-start | bytes 835592 | tf_op jit(solution)/shard_map/ppermute | solution.py:45
  49.2 9.7 %collective-permute-start.4 = (bf16[272,512]{1,0:T(8,128)(2,1)S(1)}, bf16[272,512]{1,0:T(8,128)(2,1)S(1)}, u32[]{:S(2)}, u32[]{:S(2)}) collective-permute-start(bf16[272,512]{1,0:T(8,128)(2,1)S(1)} %base.1.refs_0_), channel_id=1, source_target_pairs={{0,224},{1,225},{2,226},{3,227},{4,228},{5,229},{6,230},{7,231},{8... | collective-permute-start | bytes 835592 | tf_op jit(solution)/shard_map/ppermute | solution.py:45
  58.8 18.5 %collective-permute-start.8 = (bf16[4,320,128]{2,1,0:T(8,128)(2,1)S(1)}, bf16[4,320,128]{2,1,0:T(8,128)(2,1)S(1)}, u32[]{:S(2)}, u32[]{:S(2)}) collective-permute-start(bf16[4,320,128]{2,1,0:T(8,128)(2,1)S(1)} %all-to-all-done.refs_8_), channel_id=1, source_target_pairs={{0,3},{1,0},{2,1},{3,2},{4,7},{5,4},{6,5},{7,6},{8,11},{9,8},{10,9... | collective-permute-start | bytes 983048 | tf_op jit(solution)/shard_map/ppermute | solution.py:45
  64.0 9.7 %collective-permute-start.6 = (bf16[272,512]{1,0:T(8,128)(2,1)S(1)}, bf16[272,512]{1,0:T(8,128)(2,1)S(1)}, u32[]{:S(2)}, u32[]{:S(2)}) collective-permute-start(bf16[272,512]{1,0:T(8,128)(2,1)S(1)} %collective-permute-done.4.refs_1_), channel_id=1, source_target_pairs={{0,224},{1,225},{2,226},{3,227},{4,228},{5,229},{6,230},{7,231},{8... | collective-permute-start | bytes 835592 | tf_op jit(solution)/shard_map/ppermute | solution.py:45
  65.9 11.5 %collective-permute-start.7 = (bf16[272,512]{1,0:T(8,128)(2,1)S(1)}, bf16[272,512]{1,0:T(8,128)(2,1)S(1)}, u32[]{:S(2)}, u32[]{:S(2)}) collective-permute-start(bf16[272,512]{1,0:T(8,128)(2,1)S(1)} %collective-permute-done.5.refs_5_), channel_id=1, source_target_pairs={{0,32},{1,33},{2,34},{3,35},{4,36},{5,37},{6,38},{7,39},{8,40},{9,... | collective-permute-start | bytes 835592 | tf_op jit(solution)/shard_map/ppermute | solution.py:45
  71.0 15.8 %collective-permute-start.10 = (bf16[4,320,128]{2,1,0:T(8,128)(2,1)S(1)}, bf16[4,320,128]{2,1,0:T(8,128)(2,1)S(1)}, u32[]{:S(2)}, u32[]{:S(2)}) collective-permute-start(bf16[4,320,128]{2,1,0:T(8,128)(2,1)S(1)} %all-to-all-done.refs_8_), channel_id=1, source_target_pairs={{0,2},{1,3},{2,0},{3,1},{4,6},{5,7},{6,4},{7,5},{8,10},{9,11},{10,... | collective-permute-start | bytes 983048 | tf_op jit(solution)/shard_map/ppermute | solution.py:45
  77.4 10.1 %collective-permute-start.9 = (bf16[272,512]{1,0:T(8,128)(2,1)S(1)}, bf16[272,512]{1,0:T(8,128)(2,1)S(1)}, u32[]{:S(2)}, u32[]{:S(2)}) collective-permute-start(bf16[272,512]{1,0:T(8,128)(2,1)S(1)} %collective-permute-done.6.refs_2_), channel_id=1, source_target_pairs={{0,224},{1,225},{2,226},{3,227},{4,228},{5,229},{6,230},{7,231},{8... | collective-permute-start | bytes 835592 | tf_op jit(solution)/shard_map/ppermute | solution.py:45
  79.3 10.2 %collective-permute-start.13 = (bf16[4,320,128]{2,1,0:T(8,128)(2,1)S(1)}, bf16[4,320,128]{2,1,0:T(8,128)(2,1)S(1)}, u32[]{:S(2)}, u32[]{:S(2)}) collective-permute-start(bf16[4,320,128]{2,1,0:T(8,128)(2,1)S(1)} %all-to-all-done.refs_8_), channel_id=1, source_target_pairs={{0,1},{1,2},{2,3},{3,0},{4,5},{5,6},{6,7},{7,4},{8,9},{9,10},{10,1... | collective-permute-start | bytes 983048 | tf_op jit(solution)/shard_map/ppermute | solution.py:45
  81.2 9.7 %collective-permute-start.12 = (bf16[272,512]{1,0:T(8,128)(2,1)S(1)}, bf16[272,512]{1,0:T(8,128)(2,1)S(1)}, u32[]{:S(2)}, u32[]{:S(2)}) collective-permute-start(bf16[272,512]{1,0:T(8,128)(2,1)S(1)} %collective-permute-done.7.refs_6_), channel_id=1, source_target_pairs={{0,32},{1,33},{2,34},{3,35},{4,36},{5,37},{6,38},{7,39},{8,40},{9,... | collective-permute-start | bytes 835592 | tf_op jit(solution)/shard_map/ppermute | solution.py:45
  87.5 9.6 %collective-permute-start.11 = (bf16[272,512]{1,0:T(8,128)(2,1)S(1)}, bf16[272,512]{1,0:T(8,128)(2,1)S(1)}, u32[]{:S(2)}, u32[]{:S(2)}) collective-permute-start(bf16[272,512]{1,0:T(8,128)(2,1)S(1)} %collective-permute-done.9.refs_3_), channel_id=1, source_target_pairs={{0,224},{1,225},{2,226},{3,227},{4,228},{5,229},{6,230},{7,231},{8... | collective-permute-start | bytes 835592 | tf_op jit(solution)/shard_map/ppermute | solution.py:45
  98.9 3.0 %collective-permute-start.14 = (f32[320,512]{1,0:T(8,128)S(1)}, f32[320,512]{1,0:T(8,128)S(1)}, u32[]{:S(2)}, u32[]{:S(2)}) collective-permute-start(f32[320,512]{1,0:T(8,128)S(1)} %get-tuple-element.26.mine_ref), channel_id=1, source_target_pairs={{0,256},{1,257},{2,258},{3,259},{4,260},{5,261},{6,262},{7,263},{8... | collective-permute-start | bytes 1966088 | tf_op jit(solution)/shard_map/ppermute | solution.py:45
  102.3 3.5 %collective-permute-start.15 = (bf16[320,512]{1,0:T(8,128)(2,1)S(1)}, bf16[320,512]{1,0:T(8,128)(2,1)S(1)}, u32[]{:S(2)}, u32[]{:S(2)}) collective-permute-start(bf16[320,512]{1,0:T(8,128)(2,1)S(1)} %adam.1.update_ref), channel_id=1, source_target_pairs={{256,0},{257,1},{258,2},{259,3},{260,4},{261,5},{262,6},{263,7},{2... | collective-permute-start | bytes 983048 | tf_op jit(solution)/shard_map/ppermute | solution.py:45
  125.4 10.6 %collective-permute-start.16 = (bf16[8,320]{1,0:T(8,128)(2,1)S(1)}, bf16[8,320]{1,0:T(8,128)(2,1)S(1)}, u32[]{:S(2)}, u32[]{:S(2)}) collective-permute-start(bf16[8,320]{1,0:T(8,128)(2,1)S(1)} %reduce_sum.9), channel_id=1, source_target_pairs={{0,0},{1,16},{2,32},{3,48},{4,64},{5,80},{6,96},{7,112},{8,128},{9... | collective-permute-start | bytes 15368 | tf_op jit(solution)/shard_map/ppermute | solution.py:45

commit v11 on v10

--- a/solution.py
+++ b/solution.py
@@ -31,6 +31,7 @@
 HALF = 128
 FEAT = 512
 COLS = 320
+PART = 80
 ROWS = 8
 PAD = 16
 f32, bf16 = jnp.float32, jnp.bfloat16
@@ -49,10 +50,6 @@
     return lax.all_to_all(value, axes, split_axis=0, concat_axis=0, tiled=True)
 
 
-def to_partner(g, y, zh, zl, x):
-    return (g, y, 1 - zh, zl, x)
-
-
 def along_y(step):
     return lambda g, y, zh, zl, x: (g, (y + (step if g == 1 else -step)) % 8, zh, zl, x)
 
@@ -65,11 +62,12 @@
     return 4 * (z_lo >> 1) + x - 3
 
 
-def cot_shifted(core):
-    def target(g, y, zh, zl, x):
-        return (core, (y - shift_of(zl, x)) % 8, zh ^ (zl & 1), zl, x) if g == 1 else None
-
-    return target
+def cot_shifted(g, y, zh, zl, x):
+    return (g, (y - shift_of(zl, x)) % 8, zh ^ (zl & 1), zl, x)
+
+
+def along_zl(flip):
+    return lambda g, y, zh, zl, x: (g, y, zh, zl ^ flip, x)
 
 
 def along_x(step):
@@ -84,6 +82,7 @@
     return (0, y, zh, zl, x) if g == 1 else None
 
 
+FLIPS = (0, 3, 1, 2)
 HOPS = (0, 1, 2, 3, 4, -1, -2, -3)
 
 
@@ -176,67 +175,30 @@
 HBM = pl.BlockSpec(memory_space=pl.ANY)
 
 
-def half_kernel(place_ref, act_ref, act_got, rows_ref, out_ref):
-    @pl.when(place_ref[0] == 1)
-    def _():
-        out_ref[:HALF, :] = act_ref[:HALF, :]
-
-    @pl.when(place_ref[0] == 0)
-    def _():
-        out_ref[:HALF, :] = act_got[HALF:, :]
-
-    out_ref[HALF:, :] = rows_ref[...]
-
-
-def half_of(place, *parts):
-    return pl.pallas_call(
-        half_kernel,
-        out_shape=jax.ShapeDtypeStruct((HALF + PAD, FEAT), bf16),
-        in_specs=[SMEM] + [VMEM] * 3,
-        out_specs=VMEM,
-        compiler_params=SMALL,
-        name="half",
-    )(place, *parts)
-
-
-def base_kernel(mine_ref, got_ref, *refs):
-    out_ref = refs[-1]
-    out_ref[:HALF, :] = mine_ref[:HALF, :]
-    out_ref[HALF:TOK, :] = got_ref[:HALF, :]
-    rows = [ref[HALF:, :].astype(f32)[:ROWS] for ref in (mine_ref, got_ref)]
-    out_ref[TOK:, :] = jnp.concatenate(rows, axis=0).astype(bf16)
-
-
-def base_of(parts, others):
-    return pl.pallas_call(
-        base_kernel,
-        out_shape=jax.ShapeDtypeStruct((TOK + PAD, FEAT), bf16),
-        in_specs=[VMEM] * 2 + [HBM] * len(others),
-        out_specs=VMEM,
-        compiler_params=SMALL,
-        name="base",
-    )(*parts, *others)
-
-
-def cut_kernel(place_ref, cot_ref, one_ref, two_ref, window, turned, sem):
+def cut_kernel(place_ref, cot_ref, act_ref, one_ref, pack_ref, window, turned, sem):
     z_lo = place_ref[3]
     q = 2 * ((place_ref[1] - shift_of(z_lo, place_ref[4])) & 7) + (place_ref[2] ^ (z_lo & 1))
     start = pl.multiple_of(((q * 5) >> 1) * 128, 128)
     copy = pltpu.make_async_copy(cot_ref.at[:, pl.ds(start, 384)], window, sem)
     copy.start()
+    pack_ref[:HALF, :] = act_ref[HALF:, :]
     copy.wait()
     turned[...] = window[...].astype(f32).T
-    place = pl.ds(pl.multiple_of((q & 1) * 64, 64), COLS)
-    one_ref[...] = turned[place, :HALF].astype(bf16)
-    two_ref[...] = turned[place, HALF:].astype(bf16)
-
-
-def cut_of(place, cot):
-    shape = jax.ShapeDtypeStruct((COLS, HALF), bf16)
+    shift = pl.multiple_of((q & 1) * 64, 64)
+    one_ref[...] = turned[pl.ds(shift, COLS), :HALF].astype(bf16)
+    for n in range(4):
+        place = pl.ds(pl.multiple_of(shift + n * PART, 16), PART)
+        pack_ref[HALF:, n * HALF : (n + 1) * HALF] = turned[place, HALF:].astype(bf16)
+
+
+def cut_of(place, cot, act):
     return pl.pallas_call(
         cut_kernel,
-        out_shape=(shape, shape),
-        in_specs=[SMEM, HBM],
+        out_shape=(
+            jax.ShapeDtypeStruct((COLS, HALF), bf16),
+            jax.ShapeDtypeStruct((HALF + PART, FEAT), bf16),
+        ),
+        in_specs=[SMEM, HBM, VMEM],
         out_specs=(VMEM, VMEM),
         scratch_shapes=[
             pltpu.VMEM((TOK, 384), bf16),
@@ -245,28 +207,76 @@
         ],
         compiler_params=SMALL,
         name="cut",
-    )(place, cot)
+    )(place, cot, act)
+
+
+def half_kernel(place_ref, act_ref, one_ref, pack_ref, rows_ref, cut_ref, out_ref):
+    @pl.when(place_ref[0] == 1)
+    def _():
+        out_ref[0, :HALF, :] = act_ref[:HALF, :]
+        cut_ref[...] = one_ref[...]
+
+    @pl.when(place_ref[0] == 0)
+    def _():
+        out_ref[0, :HALF, :] = pack_ref[:HALF, :]
+        for n in range(4):
+            cut_ref[n * PART : (n + 1) * PART, :] = pack_ref[HALF:, n * HALF : (n + 1) * HALF]
+
+    out_ref[0, HALF:, :] = rows_ref[...]
+    out_ref[1] = out_ref[0]
+
+
+def half_of(place, *parts):
+    return pl.pallas_call(
+        half_kernel,
+        out_shape=(
+            jax.ShapeDtypeStruct((COLS, HALF), bf16),
+            jax.ShapeDtypeStruct((2, HALF + PAD, FEAT), bf16),
+        ),
+        in_specs=[SMEM] + [VMEM] * 4,
+        out_specs=(VMEM, VMEM),
+        compiler_params=SMALL,
+        name="half",
+    )(place, *parts)
+
+
+def base_kernel(halves_ref, out_ref):
+    for z_hi in range(2):
+        out_ref[z_hi * HALF : (z_hi + 1) * HALF, :] = halves_ref[z_hi, :HALF, :]
+    rows = [halves_ref[z_hi, HALF:, :].astype(f32)[:ROWS] for z_hi in range(2)]
+    out_ref[TOK:, :] = jnp.concatenate(rows, axis=0).astype(bf16)
+
+
+def base_of(halves):
+    return pl.pallas_call(
+        base_kernel,
+        out_shape=jax.ShapeDtypeStruct((TOK + PAD, FEAT), bf16),
+        in_specs=[VMEM],
+        out_specs=VMEM,
+        compiler_params=SMALL,
+        name="base",
+    )(halves)
 
 
 def gradient_kernel(place_ref, *refs):
     chunks, blocks, (out_ref, rows_ref, block_rows) = refs[:8], refs[8:12], refs[12:]
-    side, y, z_hi, x = (place_ref[n] for n in (0, 1, 2, 4))
+    side, y, z_hi, own_z_lo, x = (place_ref[n] for n in range(5))
     for n, hop in enumerate(HOPS):
         shift = jnp.where(side == 1, 4 if hop == 4 else -hop, hop)
         block_y = (y + shift) & 7
         rows = chunks[n][TOK:, :].astype(f32)
-        for other in range(2):
-            block_zh = z_hi if other == 0 else 1 - z_hi
-            span = slice(other * HALF, (other + 1) * HALF)
-            z_lo = 2 * ((shift + 3) >> 2) + other
+        for block_zh in range(2):
+            span = slice(block_zh * HALF, (block_zh + 1) * HALF)
+            flip = own_z_lo ^ (2 * ((shift + 3) >> 2) + (z_hi ^ block_zh))
+            slot = sum(jnp.where(flip == f, m, 0) for m, f in enumerate(FLIPS))
             source = (shift + 3) - x
             source = jnp.where(side == 1, -source, source) & 3
-            block = blocks[0][z_lo]
+            block = blocks[0][slot]
             for m in range(1, 4):
-                block = jnp.where(source == m, blocks[m][z_lo], block)
+                block = jnp.where(source == m, blocks[m][slot], block)
             block_rows[:, span] = block
             place = pl.multiple_of((2 * block_y + block_zh) * ROWS, ROWS)
-            rows_ref[pl.ds(place, ROWS), :] = rows[other * ROWS : (other + 1) * ROWS]
+            rows_ref[pl.ds(place, ROWS), :] = rows[block_zh * ROWS : (block_zh + 1) * ROWS]
         part = jnp.dot(block_rows[...], chunks[n][:TOK, :], preferred_element_type=f32)
         if n == 0:
             out_ref[...] = part
@@ -356,10 +366,8 @@
     place = jnp.stack([lax.axis_index(axis) for axis in AXES]).astype(jnp.int32)
 
     act = activations[0]
-    act_got = permute(act, to_rollout)
-    cut_one, cut_two = cut_of(place, cotangent[0])
-    own_one = permute(cut_one, cot_shifted(1))
-    own_two = permute(cut_two, cot_shifted(0))
+    cut_one, pack = cut_of(place, cotangent[0], act)
+    pack_got = permute(pack, to_rollout)
     rows = attend(
         (q >> 1).reshape(1),
         queries,
@@ -370,13 +378,11 @@
         lengths,
         token_ids.T,
     )
-    half = half_of(place, act, act_got, rows)
-    own_one, own_two, _ = lax.optimization_barrier((own_one, own_two, half))
-    own = jnp.where(place[0] == 1, own_one, own_two)
-    own_spread = jnp.broadcast_to(own[None], (4, COLS, HALF))
-    line = gather(own_spread, "z_lo")
-    half_got = permute(half, to_partner)
-    base = base_of((half, half_got), (own_spread,))
+    cut, halves = half_of(place, act, cut_one, pack_got, rows)
+    own = permute(cut, cot_shifted)
+    base = base_of(gather(halves, "z_hi"))
+    two_blocks = jnp.stack([own, permute(own, along_zl(3))])
+    line = jnp.concatenate([two_blocks, permute(two_blocks, along_zl(1))], axis=0)
     first = [permute(base, along_y(1))]
     second = [permute(base, along_y(-1))]
     line_tied, ahead, back = lax.optimization_barrier((line, first[0], second[0]))

time: 152 us -> 151 us (level)
  the two profiles are of different devices: /device:TPU:24 before, /device:TPU:56 now
where the time goes in v11:
time: 151 us; the launch traced here: 148 us
  starting transfers between devices  66.8 us (44%)
  waiting for transfers between devices  38 us (25%)
  blocking collectives  31.8 us (21%)
  Pallas kernels  6.78 us (4%)
  local copies, waits for them, and re-layouts  3.63 us (2%)
    ppermute x17, starting transfers between devices, permute(): return lax.ppermute(value, AXES, pairs)  56.5 us
    ppermute x17, waiting for transfers between devices, permute(): return lax.ppermute(value, AXES, pairs)  38 us
    all_to_all x2, blocking collectives, gather(): return lax.all_to_all(value, axes, split_axis=0, concat_axis=0, tiled=True)  31.8 us
    all_to_all x1, starting transfers between devices, gather(): return lax.all_to_all(value, axes, split_axis=0, concat_axis=0, tiled=True)  10.3 us
  transfers between devices with their start and end apart: 18, of which 13 were waited for; matrix products, arithmetic and copies ran while one was open for 0% of the time, Pallas kernels for 1%

profile of v11, /device:TPU:56, one launch (start us, length us, event | category | flops | bytes accessed | tf_op | source)
XLA Modules:
  0.0 148.1 jit_solution(13944654042702842432)
XLA Ops:
  0.6 0.0 copy-start.11
  0.6 0.0 copy-start.12
  0.7 0.0 copy-start.9
  0.7 0.0 copy-start.8
  0.7 0.0 copy-start.10
  0.7 0.1 stack.32.place_ref
  0.8 1.7 %copy-done = bf16[1,256,5120]{2,1,0:T(8,128)(2,1)S(1)} copy-done((bf16[1,256,5120]{2,1,0:T(8,128)(2,1)S(1)}, bf16[1,256,5120]{2,1,0:T(8,128)(2,1)}, u32[]{:S(2)}) %copy-start) | copy-done | bytes 2621464
  2.5 0.9 copy-done.3
  3.5 0.8 cut.1
  4.3 1.3 collective-permute-start
  5.6 0.0 copy-done.11
  5.6 0.0 copy-done.12
  5.6 0.0 copy-done.9
  5.6 0.0 copy-done.8
  5.6 0.0 copy-done.10
  5.6 0.0 copy-done.1
  5.6 0.0 copy-done.2
  5.6 1.0 attend.1.rows_ref
  6.7 0.9 collective-permute-done.pack_ref
  7.6 0.0 copy-done.4
  7.6 1.3 half.1
  8.9 10.3 %all-to-all-start = ((bf16[2,144,512]{2,1,0:T(8,128)(2,1)}), bf16[2,144,512]{2,1,0:T(8,128)(2,1)S(1)}, u32[]{:S(2)}, u32[]{:S(2)}) async-start(bf16[2,144,512]{2,1,0:T(8,128)(2,1)} %get-tuple-element.18), calls=%async_computation | async-start | bytes 589824 | tf_op jit(solution)/shard_map/all_to_all | solution.py:50
  19.2 3.8 %collective-permute-start.2 = (bf16[320,128]{1,0:T(8,128)(2,1)S(1)}, bf16[320,128]{1,0:T(8,128)(2,1)S(1)}, u32[]{:S(2)}, u32[]{:S(2)}) collective-permute-start(bf16[320,128]{1,0:T(8,128)(2,1)S(1)} %get-tuple-element.19), channel_id=1, source_target_pairs={{0,96},{1,65},{2,34},{3,3},{4,116},{5,85},{6,54},{7,23},{8,232},{9... | collective-permute-start | bytes 245768 | tf_op jit(solution)/shard_map/ppermute | solution.py:46
  23.0 4.5 %collective-permute-done.2 = bf16[320,128]{1,0:T(8,128)(2,1)S(1)} collective-permute-done((bf16[320,128]{1,0:T(8,128)(2,1)S(1)}, bf16[320,128]{1,0:T(8,128)(2,1)S(1)}, u32[]{:S(2)}, u32[]{:S(2)}) %collective-permute-start.2) | collective-permute-done | bytes 81952 | tf_op jit(solution)/shard_map/ppermute | solution.py:46
  27.5 10.2 %collective-permute-start.3 = (bf16[320,128]{1,0:T(8,128)(2,1)S(1)}, bf16[320,128]{1,0:T(8,128)(2,1)S(1)}, u32[]{:S(2)}, u32[]{:S(2)}) collective-permute-start(bf16[320,128]{1,0:T(8,128)(2,1)S(1)} %collective-permute-done.2), channel_id=1, source_target_pairs={{0,12},{1,13},{2,14},{3,15},{4,8},{5,9},{6,10},{7,11},{8,4},{9,5},... | collective-permute-start | bytes 245768 | tf_op jit(solution)/shard_map/ppermute | solution.py:46
  37.7 2.4 %collective-permute-done.3 = bf16[320,128]{1,0:T(8,128)(2,1)S(1)} collective-permute-done((bf16[320,128]{1,0:T(8,128)(2,1)S(1)}, bf16[320,128]{1,0:T(8,128)(2,1)S(1)}, u32[]{:S(2)}, u32[]{:S(2)}) %collective-permute-start.3) | collective-permute-done | bytes 81952 | tf_op jit(solution)/shard_map/ppermute | solution.py:46
  40.2 3.3 %collective-permute-start.4 = (bf16[2,320,128]{2,1,0:T(8,128)(2,1)S(1)}, bf16[2,320,128]{2,1,0:T(8,128)(2,1)S(1)}, u32[]{:S(2)}, u32[]{:S(2)}) collective-permute-start(bf16[2,320,128]{2,1,0:T(8,128)(2,1)S(1)} %pad_maximum_fusion.1), channel_id=1, source_target_pairs={{0,4},{1,5},{2,6},{3,7},{4,0},{5,1},{6,2},{7,3},{8,12},{9,13},{10,... | collective-permute-start | bytes 491528 | tf_op jit(solution)/shard_map/ppermute | solution.py:46
  43.5 0.0 all-to-all-done.halves_ref
  43.6 4.8 %collective-permute-start.5 = (bf16[272,512]{1,0:T(8,128)(2,1)S(1)}, bf16[272,512]{1,0:T(8,128)(2,1)S(1)}, u32[]{:S(2)}, u32[]{:S(2)}) collective-permute-start(bf16[272,512]{1,0:T(8,128)(2,1)S(1)} %base.1.refs_0_), channel_id=1, source_target_pairs={{0,32},{1,33},{2,34},{3,35},{4,36},{5,37},{6,38},{7,39},{8,40},{9,... | collective-permute-start | bytes 835592 | tf_op jit(solution)/shard_map/ppermute | solution.py:46
  48.4 1.9 %collective-permute-start.1 = (bf16[272,512]{1,0:T(8,128)(2,1)S(1)}, bf16[272,512]{1,0:T(8,128)(2,1)S(1)}, u32[]{:S(2)}, u32[]{:S(2)}) collective-permute-start(bf16[272,512]{1,0:T(8,128)(2,1)S(1)} %base.1.refs_0_), channel_id=1, source_target_pairs={{0,224},{1,225},{2,226},{3,227},{4,228},{5,229},{6,230},{7,231},{8... | collective-permute-start | bytes 835592 | tf_op jit(solution)/shard_map/ppermute | solution.py:46
  50.3 0.0 collective-permute-done.4
  50.3 0.0 copy-start.7
  50.4 4.2 %collective-permute-done.5.refs_5_ = bf16[272,512]{1,0:T(8,128)(2,1)S(1)} collective-permute-done((bf16[272,512]{1,0:T(8,128)(2,1)S(1)}, bf16[272,512]{1,0:T(8,128)(2,1)S(1)}, u32[]{:S(2)}, u32[]{:S(2)}) %collective-permute-start.5) | collective-permute-done | bytes 278560 | tf_op jit(solution)/shard_map/ppermute | solution.py:46
  54.5 3.5 %collective-permute-done.1.refs_1_ = bf16[272,512]{1,0:T(8,128)(2,1)S(1)} collective-permute-done((bf16[272,512]{1,0:T(8,128)(2,1)S(1)}, bf16[272,512]{1,0:T(8,128)(2,1)S(1)}, u32[]{:S(2)}, u32[]{:S(2)}) %collective-permute-start.1) | collective-permute-done | bytes 278560 | tf_op jit(solution)/shard_map/ppermute | solution.py:46
  58.0 4.1 %collective-permute-start.8 = (bf16[4,320,128]{2,1,0:T(8,128)(2,1)S(1)}, bf16[4,320,128]{2,1,0:T(8,128)(2,1)S(1)}, u32[]{:S(2)}, u32[]{:S(2)}) collective-permute-start(bf16[4,320,128]{2,1,0:T(8,128)(2,1)S(1)} %pad_maximum_fusion.refs_8_), channel_id=1, source_target_pairs={{0,3},{1,0},{2,1},{3,2},{4,7},{5,4},{6,5},{7,6},{8,11},{9,8},{10,9... | collective-permute-start | bytes 983048 | tf_op jit(solution)/shard_map/ppermute | solution.py:46
  62.1 2.7 %collective-permute-start.6 = (bf16[272,512]{1,0:T(8,128)(2,1)S(1)}, bf16[272,512]{1,0:T(8,128)(2,1)S(1)}, u32[]{:S(2)}, u32[]{:S(2)}) collective-permute-start(bf16[272,512]{1,0:T(8,128)(2,1)S(1)} %collective-permute-done.1.refs_1_), channel_id=1, source_target_pairs={{0,224},{1,225},{2,226},{3,227},{4,228},{5,229},{6,230},{7,231},{8... | collective-permute-start | bytes 835592 | tf_op jit(solution)/shard_map/ppermute | solution.py:46
  64.8 4.3 %collective-permute-start.7 = (bf16[272,512]{1,0:T(8,128)(2,1)S(1)}, bf16[272,512]{1,0:T(8,128)(2,1)S(1)}, u32[]{:S(2)}, u32[]{:S(2)}) collective-permute-start(bf16[272,512]{1,0:T(8,128)(2,1)S(1)} %collective-permute-done.5.refs_5_), channel_id=1, source_target_pairs={{0,32},{1,33},{2,34},{3,35},{4,36},{5,37},{6,38},{7,39},{8,40},{9,... | collective-permute-start | bytes 835592 | tf_op jit(solution)/shard_map/ppermute | solution.py:46
  69.2 2.3 %collective-permute-start.10 = (bf16[4,320,128]{2,1,0:T(8,128)(2,1)S(1)}, bf16[4,320,128]{2,1,0:T(8,128)(2,1)S(1)}, u32[]{:S(2)}, u32[]{:S(2)}) collective-permute-start(bf16[4,320,128]{2,1,0:T(8,128)(2,1)S(1)} %pad_maximum_fusion.refs_8_), channel_id=1, source_target_pairs={{0,2},{1,3},{2,0},{3,1},{4,6},{5,7},{6,4},{7,5},{8,10},{9,11},{10,... | collective-permute-start | bytes 983048 | tf_op jit(solution)/shard_map/ppermute | solution.py:46
  71.5 2.6 %collective-permute-done.6.refs_2_ = bf16[272,512]{1,0:T(8,128)(2,1)S(1)} collective-permute-done((bf16[272,512]{1,0:T(8,128)(2,1)S(1)}, bf16[272,512]{1,0:T(8,128)(2,1)S(1)}, u32[]{:S(2)}, u32[]{:S(2)}) %collective-permute-start.6) | collective-permute-done | bytes 278560 | tf_op jit(solution)/shard_map/ppermute | solution.py:46
  74.1 0.0 collective-permute-done.7.refs_6_
  74.1 0.0 collective-permute-done.8.refs_9_
  74.1 2.3 %collective-permute-start.9 = (bf16[272,512]{1,0:T(8,128)(2,1)S(1)}, bf16[272,512]{1,0:T(8,128)(2,1)S(1)}, u32[]{:S(2)}, u32[]{:S(2)}) collective-permute-start(bf16[272,512]{1,0:T(8,128)(2,1)S(1)} %collective-permute-done.6.refs_2_), channel_id=1, source_target_pairs={{0,224},{1,225},{2,226},{3,227},{4,228},{5,229},{6,230},{7,231},{8... | collective-permute-start | bytes 835592 | tf_op jit(solution)/shard_map/ppermute | solution.py:46
  76.4 1.9 %collective-permute-start.13 = (bf16[4,320,128]{2,1,0:T(8,128)(2,1)S(1)}, bf16[4,320,128]{2,1,0:T(8,128)(2,1)S(1)}, u32[]{:S(2)}, u32[]{:S(2)}) collective-permute-start(bf16[4,320,128]{2,1,0:T(8,128)(2,1)S(1)} %pad_maximum_fusion.refs_8_), channel_id=1, source_target_pairs={{0,1},{1,2},{2,3},{3,0},{4,5},{5,6},{6,7},{7,4},{8,9},{9,10},{10,1... | collective-permute-start | bytes 983048 | tf_op jit(solution)/shard_map/ppermute | solution.py:46
  78.3 4.8 %collective-permute-start.12 = (bf16[272,512]{1,0:T(8,128)(2,1)S(1)}, bf16[272,512]{1,0:T(8,128)(2,1)S(1)}, u32[]{:S(2)}, u32[]{:S(2)}) collective-permute-start(bf16[272,512]{1,0:T(8,128)(2,1)S(1)} %collective-permute-done.7.refs_6_), channel_id=1, source_target_pairs={{0,32},{1,33},{2,34},{3,35},{4,36},{5,37},{6,38},{7,39},{8,40},{9,... | collective-permute-start | bytes 835592 | tf_op jit(solution)/shard_map/ppermute | solution.py:46
  83.1 0.0 collective-permute-done.10.refs_10_
  83.1 0.6 collective-permute-done.9.refs_3_
  83.8 1.9 %collective-permute-start.11 = (bf16[272,512]{1,0:T(8,128)(2,1)S(1)}, bf16[272,512]{1,0:T(8,128)(2,1)S(1)}, u32[]{:S(2)}, u32[]{:S(2)}) collective-permute-start(bf16[272,512]{1,0:T(8,128)(2,1)S(1)} %collective-permute-done.9.refs_3_), channel_id=1, source_target_pairs={{0,224},{1,225},{2,226},{3,227},{4,228},{5,229},{6,230},{7,231},{8... | collective-permute-start | bytes 835592 | tf_op jit(solution)/shard_map/ppermute | solution.py:46
  85.7 0.9 collective-permute-done.13.refs_11_
  86.6 1.7 %collective-permute-done.12.refs_7_ = bf16[272,512]{1,0:T(8,128)(2,1)S(1)} collective-permute-done((bf16[272,512]{1,0:T(8,128)(2,1)S(1)}, bf16[272,512]{1,0:T(8,128)(2,1)S(1)}, u32[]{:S(2)}, u32[]{:S(2)}) %collective-permute-start.12) | collective-permute-done | bytes 278560 | tf_op jit(solution)/shard_map/ppermute | solution.py:46
  88.2 5.2 %collective-permute-done.11.refs_4_ = bf16[272,512]{1,0:T(8,128)(2,1)S(1)} collective-permute-done((bf16[272,512]{1,0:T(8,128)(2,1)S(1)}, bf16[272,512]{1,0:T(8,128)(2,1)S(1)}, u32[]{:S(2)}, u32[]{:S(2)}) %collective-permute-start.11) | collective-permute-done | bytes 278560 | tf_op jit(solution)/shard_map/ppermute | solution.py:46
  93.4 1.7 %gradient.1 = (f32[320,512]{1,0:T(8,128)S(1)}, f32[128,512]{1,0:T(8,128)S(1)}) custom-call(s32[5]{0:T(128)S(1)} %stack.32.place_ref, bf16[272,512]{1,0:T(8,128)(2,1)S(1)} %base.1.refs_0_, bf16[272,512]{1,0:T(8,128)(2,1)S(1)} %collective-permute-done.1.refs_1_, bf16[272,512]{1,0:T(8,128)(2,1)S(1)} %collective-permute-done.6.refs_2_, ...), custom_call_target="tpu_custom_call" | custom-call | flops 671088640 | bytes 6291456 | tf_op jit(solution)/shard_map/gradient/pallas_call | solution.py:288
  95.1 1.3 collective-permute-start.14
  96.5 1.7 %collective-permute-done.14.got_ref = f32[320,512]{1,0:T(8,128)S(1)} collective-permute-done((f32[320,512]{1,0:T(8,128)S(1)}, f32[320,512]{1,0:T(8,128)S(1)}, u32[]{:S(2)}, u32[]{:S(2)}) %collective-permute-start.14) | collective-permute-done | bytes 655392 | tf_op jit(solution)/shard_map/ppermute | solution.py:46
  98.1 0.0 copy-done.5
  98.1 0.0 copy-done.6
  98.1 0.5 adam.1.update_ref
  98.6 1.3 collective-permute-start.15
  99.9 2.2 %collective-permute-done.15.update_got = bf16[320,512]{1,0:T(8,128)(2,1)S(1)} collective-permute-done((bf16[320,512]{1,0:T(8,128)(2,1)S(1)}, bf16[320,512]{1,0:T(8,128)(2,1)S(1)}, u32[]{:S(2)}, u32[]{:S(2)}) %collective-permute-start.15) | collective-permute-done | bytes 327712 | tf_op jit(solution)/shard_map/ppermute | solution.py:46
  102.1 1.5 step.1
  103.6 17.1 %all_to_all.15 = f32[16,8,320]{2,1,0:T(8,128)S(1)} all-to-all(f32[16,8,320]{2,1,0:T(8,128)S(1)} %get-tuple-element.29), channel_id=1, replica_groups=mesh['group'=2,'y'=8,'z_hi'=2,'z_lo'=4,'x'=4] {'z_lo','x'}, dimensions={0} | all-to-all | bytes 327680 | tf_op jit(solution)/shard_map/all_to_all | solution.py:50
  120.7 4.2 %collective-permute-start.16 = (bf16[8,320]{1,0:T(8,128)(2,1)S(1)}, bf16[8,320]{1,0:T(8,128)(2,1)S(1)}, u32[]{:S(2)}, u32[]{:S(2)}) collective-permute-start(bf16[8,320]{1,0:T(8,128)(2,1)S(1)} %reduce_sum.9), channel_id=1, source_target_pairs={{0,0},{1,16},{2,32},{3,48},{4,64},{5,80},{6,96},{7,112},{8,128},{9... | collective-permute-start | bytes 15368 | tf_op jit(solution)/shard_map/ppermute | solution.py:46
  124.9 7.6 %collective-permute-done.16 = bf16[8,320]{1,0:T(8,128)(2,1)S(1)} collective-permute-done((bf16[8,320]{1,0:T(8,128)(2,1)S(1)}, bf16[8,320]{1,0:T(8,128)(2,1)S(1)}, u32[]{:S(2)}, u32[]{:S(2)}) %collective-permute-start.16) | collective-permute-done | bytes 5152 | tf_op jit(solution)/shard_map/ppermute | solution.py:46
  132.5 14.7 %all_to_all.16 = bf16[16,8,320]{2,1,0:T(8,128)(2,1)S(1)} all-to-all(bf16[16,8,320]{2,1,0:T(8,128)(2,1)S(1)} %broadcast_in_dim.2), channel_id=1, replica_groups=mesh['group'=2,'y'=8,'z_hi'=2,'z_lo'=4,'x'=4] {'z_lo','x'}, dimensions={0} | all-to-all | bytes 163840 | tf_op jit(solution)/shard_map/all_to_all | solution.py:50
  147.3 0.8 reshape.12
  (14 shorter events, 0.1 us)
Async XLA Ops:
  0.6 4.9 %copy-start.11 = (s32[4,2]{0,1:T(2,128)S(1)}, s32[4,2]{0,1:T(2,128)}, u32[]{:S(2)}) copy-start(s32[4,2]{0,1:T(2,128)} %param.23) | copy-start | bytes 100
  0.6 4.9 %copy-start.12 = (s32[2]{0:T(128)S(1)}, s32[2]{0:T(128)}, u32[]{:S(2)}) copy-start(s32[2]{0:T(128)} %lengths_ref.1) | copy-start | bytes 28
  0.7 4.9 %copy-start.9 = (bf16[4,2,1024]{2,1,0:T(2,128)(2,1)S(1)}, bf16[4,2,1024]{2,1,0:T(2,128)(2,1)}, u32[]{:S(2)}) copy-start(bf16[4,2,1024]{2,1,0:T(2,128)(2,1)} %nv_ref.1) | copy-start | bytes 49156
  0.7 4.9 %copy-start.8 = (bf16[4,2,1024]{2,1,0:T(2,128)(2,1)S(1)}, bf16[4,2,1024]{2,1,0:T(2,128)(2,1)}, u32[]{:S(2)}) copy-start(bf16[4,2,1024]{2,1,0:T(2,128)(2,1)} %nk_ref.1) | copy-start | bytes 49156
  0.7 4.9 %copy-start.10 = (bf16[4,2,512]{2,1,0:T(2,128)(2,1)S(1)}, bf16[4,2,512]{2,1,0:T(2,128)(2,1)}, u32[]{:S(2)}) copy-start(bf16[4,2,512]{2,1,0:T(2,128)(2,1)} %q_ref.1) | copy-start | bytes 24580
  0.8 1.7 %copy-start = (bf16[1,256,5120]{2,1,0:T(8,128)(2,1)S(1)}, bf16[1,256,5120]{2,1,0:T(8,128)(2,1)}, u32[]{:S(2)}) copy-start(bf16[1,256,5120]{2,1,0:T(8,128)(2,1)} %param.13) | copy-start | bytes 7864324
  2.5 0.9 copy-start.3
  3.5 2.2 %copy-start.1 = (bf16[2,2048,128]{2,1,0:T(8,128)(2,1)S(1)}, bf16[2,2048,128]{2,1,0:T(8,128)(2,1)}, u32[]{:S(2)}) copy-start(bf16[2,2048,128]{2,1,0:T(8,128)(2,1)} %k_ref.1) | copy-start | bytes 3145732
  3.5 2.2 %copy-start.2 = (bf16[2,2048,128]{2,1,0:T(8,128)(2,1)S(1)}, bf16[2,2048,128]{2,1,0:T(8,128)(2,1)}, u32[]{:S(2)}) copy-start(bf16[2,2048,128]{2,1,0:T(8,128)(2,1)} %v_ref.1) | copy-start | bytes 3145732
  3.5 4.2 %copy-start.4 = (bf16[1,256,512]{2,1,0:T(8,128)(2,1)S(1)}, bf16[1,256,512]{2,1,0:T(8,128)(2,1)}, u32[]{:S(2)}) copy-start(bf16[1,256,512]{2,1,0:T(8,128)(2,1)} %param.12) | copy-start | bytes 786436
  4.3 3.4 %collective-permute-start = (bf16[208,512]{1,0:T(8,128)(2,1)S(1)}, bf16[208,512]{1,0:T(8,128)(2,1)S(1)}, u32[]{:S(2)}, u32[]{:S(2)}) collective-permute-start(bf16[208,512]{1,0:T(8,128)(2,1)S(1)} %get-tuple-element.17), channel_id=1, source_target_pairs={{256,0},{257,1},{258,2},{259,3},{260,4},{261,5},{262,6},{263,7},{2... | collective-permute-start | bytes 638984 | tf_op jit(solution)/shard_map/ppermute | solution.py:46
  8.9 34.6 %all-to-all-start = ((bf16[2,144,512]{2,1,0:T(8,128)(2,1)}), bf16[2,144,512]{2,1,0:T(8,128)(2,1)S(1)}, u32[]{:S(2)}, u32[]{:S(2)}) async-start(bf16[2,144,512]{2,1,0:T(8,128)(2,1)} %get-tuple-element.18), calls=%async_computation | async-start | bytes 589824 | tf_op jit(solution)/shard_map/all_to_all | solution.py:50
  19.2 78.9 %copy-start.5 = (f32[1,512,320]{1,2,0:T(8,128)S(1)}, f32[1,512,320]{1,2,0:T(8,128)}, u32[]{:S(2)}) copy-start(f32[1,512,320]{1,2,0:T(8,128)} %param.15) | copy-start | bytes 1966084
  19.2 78.9 %copy-start.6 = (f32[1,512,320]{1,2,0:T(8,128)S(1)}, f32[1,512,320]{1,2,0:T(8,128)}, u32[]{:S(2)}) copy-start(f32[1,512,320]{1,2,0:T(8,128)} %param.16) | copy-start | bytes 1966084
  19.2 8.3 %collective-permute-start.2 = (bf16[320,128]{1,0:T(8,128)(2,1)S(1)}, bf16[320,128]{1,0:T(8,128)(2,1)S(1)}, u32[]{:S(2)}, u32[]{:S(2)}) collective-permute-start(bf16[320,128]{1,0:T(8,128)(2,1)S(1)} %get-tuple-element.19), channel_id=1, source_target_pairs={{0,96},{1,65},{2,34},{3,3},{4,116},{5,85},{6,54},{7,23},{8,232},{9... | collective-permute-start | bytes 245768 | tf_op jit(solution)/shard_map/ppermute | solution.py:46
  27.5 12.7 %collective-permute-start.3 = (bf16[320,128]{1,0:T(8,128)(2,1)S(1)}, bf16[320,128]{1,0:T(8,128)(2,1)S(1)}, u32[]{:S(2)}, u32[]{:S(2)}) collective-permute-start(bf16[320,128]{1,0:T(8,128)(2,1)S(1)} %collective-permute-done.2), channel_id=1, source_target_pairs={{0,12},{1,13},{2,14},{3,15},{4,8},{5,9},{6,10},{7,11},{8,4},{9,5},... | collective-permute-start | bytes 245768 | tf_op jit(solution)/shard_map/ppermute | solution.py:46
  40.2 10.1 %collective-permute-start.4 = (bf16[2,320,128]{2,1,0:T(8,128)(2,1)S(1)}, bf16[2,320,128]{2,1,0:T(8,128)(2,1)S(1)}, u32[]{:S(2)}, u32[]{:S(2)}) collective-permute-start(bf16[2,320,128]{2,1,0:T(8,128)(2,1)S(1)} %pad_maximum_fusion.1), channel_id=1, source_target_pairs={{0,4},{1,5},{2,6},{3,7},{4,0},{5,1},{6,2},{7,3},{8,12},{9,13},{10,... | collective-permute-start | bytes 491528 | tf_op jit(solution)/shard_map/ppermute | solution.py:46
  43.6 10.9 %collective-permute-start.5 = (bf16[272,512]{1,0:T(8,128)(2,1)S(1)}, bf16[272,512]{1,0:T(8,128)(2,1)S(1)}, u32[]{:S(2)}, u32[]{:S(2)}) collective-permute-start(bf16[272,512]{1,0:T(8,128)(2,1)S(1)} %base.1.refs_0_), channel_id=1, source_target_pairs={{0,32},{1,33},{2,34},{3,35},{4,36},{5,37},{6,38},{7,39},{8,40},{9,... | collective-permute-start | bytes 835592 | tf_op jit(solution)/shard_map/ppermute | solution.py:46
  48.4 9.7 %collective-permute-start.1 = (bf16[272,512]{1,0:T(8,128)(2,1)S(1)}, bf16[272,512]{1,0:T(8,128)(2,1)S(1)}, u32[]{:S(2)}, u32[]{:S(2)}) collective-permute-start(bf16[272,512]{1,0:T(8,128)(2,1)S(1)} %base.1.refs_0_), channel_id=1, source_target_pairs={{0,224},{1,225},{2,226},{3,227},{4,228},{5,229},{6,230},{7,231},{8... | collective-permute-start | bytes 835592 | tf_op jit(solution)/shard_map/ppermute | solution.py:46
  50.3 51.8 %copy-start.7 = (bf16[512,320]{0,1:T(8,128)(2,1)S(1)}, bf16[512,320]{0,1:T(8,128)(2,1)}, u32[]{:S(2)}) copy-start(bf16[512,320]{0,1:T(8,128)(2,1)} %param.14) | copy-start | bytes 983044
  58.0 16.1 %collective-permute-start.8 = (bf16[4,320,128]{2,1,0:T(8,128)(2,1)S(1)}, bf16[4,320,128]{2,1,0:T(8,128)(2,1)S(1)}, u32[]{:S(2)}, u32[]{:S(2)}) collective-permute-start(bf16[4,320,128]{2,1,0:T(8,128)(2,1)S(1)} %pad_maximum_fusion.refs_8_), channel_id=1, source_target_pairs={{0,3},{1,0},{2,1},{3,2},{4,7},{5,4},{6,5},{7,6},{8,11},{9,8},{10,9... | collective-permute-start | bytes 983048 | tf_op jit(solution)/shard_map/ppermute | solution.py:46
  62.1 12.0 %collective-permute-start.6 = (bf16[272,512]{1,0:T(8,128)(2,1)S(1)}, bf16[272,512]{1,0:T(8,128)(2,1)S(1)}, u32[]{:S(2)}, u32[]{:S(2)}) collective-permute-start(bf16[272,512]{1,0:T(8,128)(2,1)S(1)} %collective-permute-done.1.refs_1_), channel_id=1, source_target_pairs={{0,224},{1,225},{2,226},{3,227},{4,228},{5,229},{6,230},{7,231},{8... | collective-permute-start | bytes 835592 | tf_op jit(solution)/shard_map/ppermute | solution.py:46
  64.8 9.3 %collective-permute-start.7 = (bf16[272,512]{1,0:T(8,128)(2,1)S(1)}, bf16[272,512]{1,0:T(8,128)(2,1)S(1)}, u32[]{:S(2)}, u32[]{:S(2)}) collective-permute-start(bf16[272,512]{1,0:T(8,128)(2,1)S(1)} %collective-permute-done.5.refs_5_), channel_id=1, source_target_pairs={{0,32},{1,33},{2,34},{3,35},{4,36},{5,37},{6,38},{7,39},{8,40},{9,... | collective-permute-start | bytes 835592 | tf_op jit(solution)/shard_map/ppermute | solution.py:46
  69.2 13.9 %collective-permute-start.10 = (bf16[4,320,128]{2,1,0:T(8,128)(2,1)S(1)}, bf16[4,320,128]{2,1,0:T(8,128)(2,1)S(1)}, u32[]{:S(2)}, u32[]{:S(2)}) collective-permute-start(bf16[4,320,128]{2,1,0:T(8,128)(2,1)S(1)} %pad_maximum_fusion.refs_8_), channel_id=1, source_target_pairs={{0,2},{1,3},{2,0},{3,1},{4,6},{5,7},{6,4},{7,5},{8,10},{9,11},{10,... | collective-permute-start | bytes 983048 | tf_op jit(solution)/shard_map/ppermute | solution.py:46
  74.1 9.6 %collective-permute-start.9 = (bf16[272,512]{1,0:T(8,128)(2,1)S(1)}, bf16[272,512]{1,0:T(8,128)(2,1)S(1)}, u32[]{:S(2)}, u32[]{:S(2)}) collective-permute-start(bf16[272,512]{1,0:T(8,128)(2,1)S(1)} %collective-permute-done.6.refs_2_), channel_id=1, source_target_pairs={{0,224},{1,225},{2,226},{3,227},{4,228},{5,229},{6,230},{7,231},{8... | collective-permute-start | bytes 835592 | tf_op jit(solution)/shard_map/ppermute | solution.py:46
  76.4 10.2 %collective-permute-start.13 = (bf16[4,320,128]{2,1,0:T(8,128)(2,1)S(1)}, bf16[4,320,128]{2,1,0:T(8,128)(2,1)S(1)}, u32[]{:S(2)}, u32[]{:S(2)}) collective-permute-start(bf16[4,320,128]{2,1,0:T(8,128)(2,1)S(1)} %pad_maximum_fusion.refs_8_), channel_id=1, source_target_pairs={{0,1},{1,2},{2,3},{3,0},{4,5},{5,6},{6,7},{7,4},{8,9},{9,10},{10,1... | collective-permute-start | bytes 983048 | tf_op jit(solution)/shard_map/ppermute | solution.py:46
  78.3 9.9 %collective-permute-start.12 = (bf16[272,512]{1,0:T(8,128)(2,1)S(1)}, bf16[272,512]{1,0:T(8,128)(2,1)S(1)}, u32[]{:S(2)}, u32[]{:S(2)}) collective-permute-start(bf16[272,512]{1,0:T(8,128)(2,1)S(1)} %collective-permute-done.7.refs_6_), channel_id=1, source_target_pairs={{0,32},{1,33},{2,34},{3,35},{4,36},{5,37},{6,38},{7,39},{8,40},{9,... | collective-permute-start | bytes 835592 | tf_op jit(solution)/shard_map/ppermute | solution.py:46
  83.8 9.6 %collective-permute-start.11 = (bf16[272,512]{1,0:T(8,128)(2,1)S(1)}, bf16[272,512]{1,0:T(8,128)(2,1)S(1)}, u32[]{:S(2)}, u32[]{:S(2)}) collective-permute-start(bf16[272,512]{1,0:T(8,128)(2,1)S(1)} %collective-permute-done.9.refs_3_), channel_id=1, source_target_pairs={{0,224},{1,225},{2,226},{3,227},{4,228},{5,229},{6,230},{7,231},{8... | collective-permute-start | bytes 835592 | tf_op jit(solution)/shard_map/ppermute | solution.py:46
  95.1 3.0 %collective-permute-start.14 = (f32[320,512]{1,0:T(8,128)S(1)}, f32[320,512]{1,0:T(8,128)S(1)}, u32[]{:S(2)}, u32[]{:S(2)}) collective-permute-start(f32[320,512]{1,0:T(8,128)S(1)} %get-tuple-element.26.mine_ref), channel_id=1, source_target_pairs={{0,256},{1,257},{2,258},{3,259},{4,260},{5,261},{6,262},{7,263},{8... | collective-permute-start | bytes 1966088 | tf_op jit(solution)/shard_map/ppermute | solution.py:46
  98.6 3.5 %collective-permute-start.15 = (bf16[320,512]{1,0:T(8,128)(2,1)S(1)}, bf16[320,512]{1,0:T(8,128)(2,1)S(1)}, u32[]{:S(2)}, u32[]{:S(2)}) collective-permute-start(bf16[320,512]{1,0:T(8,128)(2,1)S(1)} %adam.1.update_ref), channel_id=1, source_target_pairs={{256,0},{257,1},{258,2},{259,3},{260,4},{261,5},{262,6},{263,7},{2... | collective-permute-start | bytes 983048 | tf_op jit(solution)/shard_map/ppermute | solution.py:46
  120.7 11.8 %collective-permute-start.16 = (bf16[8,320]{1,0:T(8,128)(2,1)S(1)}, bf16[8,320]{1,0:T(8,128)(2,1)S(1)}, u32[]{:S(2)}, u32[]{:S(2)}) collective-permute-start(bf16[8,320]{1,0:T(8,128)(2,1)S(1)} %reduce_sum.9), channel_id=1, source_target_pairs={{0,0},{1,16},{2,32},{3,48},{4,64},{5,80},{6,96},{7,112},{8,128},{9... | collective-permute-start | bytes 15368 | tf_op jit(solution)/shard_map/ppermute | solution.py:46

commit v12 on v11

--- a/solution.py
+++ b/solution.py
@@ -54,16 +54,16 @@
     return lambda g, y, zh, zl, x: (g, (y + (step if g == 1 else -step)) % 8, zh, zl, x)
 
 
-def transposed(g, y, zh, zl, x):
-    return (g, zl * 2 + (x >> 1), x & 1, y >> 1, (y & 1) * 2 + zh)
-
-
 def shift_of(z_lo, x):
     return 4 * (z_lo >> 1) + x - 3
 
 
 def cot_shifted(g, y, zh, zl, x):
     return (g, (y - shift_of(zl, x)) % 8, zh ^ (zl & 1), zl, x)
+
+
+def rows_shifted(g, y, zh, zl, x):
+    return (g, (y + shift_of(zl, x)) % 8, zh ^ (zl & 1), zl, x)
 
 
 def along_zl(flip):
@@ -240,22 +240,22 @@
     )(place, *parts)
 
 
-def base_kernel(halves_ref, out_ref):
+def base_kernel(halves_ref, _, out_ref):
     for z_hi in range(2):
         out_ref[z_hi * HALF : (z_hi + 1) * HALF, :] = halves_ref[z_hi, :HALF, :]
     rows = [halves_ref[z_hi, HALF:, :].astype(f32)[:ROWS] for z_hi in range(2)]
     out_ref[TOK:, :] = jnp.concatenate(rows, axis=0).astype(bf16)
 
 
-def base_of(halves):
+def base_of(halves, after):
     return pl.pallas_call(
         base_kernel,
         out_shape=jax.ShapeDtypeStruct((TOK + PAD, FEAT), bf16),
-        in_specs=[VMEM],
+        in_specs=[VMEM, HBM],
         out_specs=VMEM,
         compiler_params=SMALL,
         name="base",
-    )(halves)
+    )(halves, after)
 
 
 def gradient_kernel(place_ref, *refs):
@@ -322,7 +322,9 @@
     )(*operands)
 
 
-def step_kernel(place_ref, update_ref, update_got, rows_ref, weight_ref, taken_ref, out_ref):
+def step_kernel(
+    place_ref, update_ref, update_got, rows_ref, weight_ref, taken_ref, out_ref, part_ref
+):
     update = jnp.where(place_ref[0] == 1, update_ref[...], update_got[...])
     taken_ref[...] = update
     widened = weight_ref[...].astype(f32)
@@ -330,8 +332,13 @@
         widened - learning_rate * (update.astype(f32) + weight_decay * widened)
     ).astype(bf16)
     rows = rows_ref[...].astype(bf16)
-    part = lax.dot_general(rows, renewed, (((1,), (1,)), ((), ())), preferred_element_type=f32)
-    out_ref[...] = part.reshape(16, ROWS, COLS)
+    part_ref[...] = lax.dot_general(
+        rows, renewed, (((1,), (1,)), ((), ())), preferred_element_type=f32
+    )
+    for n in range(16):
+        z_lo, x = divmod(n, 4)
+        block = 2 * ((place_ref[1] + shift_of(z_lo, x)) & 7) + (place_ref[2] ^ (z_lo & 1))
+        out_ref[n] = part_ref[pl.ds(pl.multiple_of(block * ROWS, ROWS), ROWS), :]
 
 
 def step(place, *operands):
@@ -343,9 +350,32 @@
         ),
         in_specs=[SMEM] + [VMEM] * 4,
         out_specs=(VMEM, VMEM),
+        scratch_shapes=[pltpu.VMEM((16 * ROWS, COLS), f32)],
         compiler_params=pltpu.CompilerParams(vmem_limit_bytes=12 * 2**20),
         name="step",
     )(place, *operands)
+
+
+def join_kernel(place_ref, blocks_ref, out_ref, pair):
+    for y in range(8):
+        shift = ((place_ref[1] - y + 3) & 7) - 3
+        for z_hi in range(2):
+            z_lo = 2 * ((shift + 3) >> 2) + (place_ref[2] ^ z_hi)
+            block = blocks_ref[4 * z_lo + ((shift + 3) & 3)]
+            pair[:, z_hi * COLS : (z_hi + 1) * COLS] = block.astype(f32)
+        out_ref[:, y * 2 * COLS : (y + 1) * 2 * COLS] = pair[...].astype(bf16)
+
+
+def join(place, blocks):
+    return pl.pallas_call(
+        join_kernel,
+        out_shape=jax.ShapeDtypeStruct((ROWS, D), bf16),
+        in_specs=[SMEM, VMEM],
+        out_specs=VMEM,
+        scratch_shapes=[pltpu.VMEM((ROWS, 2 * COLS), f32)],
+        compiler_params=SMALL,
+        name="join",
+    )(place, blocks)
 
 
 def local(
@@ -380,20 +410,28 @@
     )
     cut, halves = half_of(place, act, cut_one, pack_got, rows)
     own = permute(cut, cot_shifted)
-    base = base_of(gather(halves, "z_hi"))
-    two_blocks = jnp.stack([own, permute(own, along_zl(3))])
-    line = jnp.concatenate([two_blocks, permute(two_blocks, along_zl(1))], axis=0)
-    first = [permute(base, along_y(1))]
-    second = [permute(base, along_y(-1))]
-    line_tied, ahead, back = lax.optimization_barrier((line, first[0], second[0]))
+    base = base_of(gather(halves, "z_hi"), own)
+    ahead = back = base
+    first, second = [], []
+
+    def round_y():
+        first.append(permute(ahead, along_y(1)))
+        second.append(permute(back, along_y(-1)))
+
+    round_y()
+    own, _ = lax.optimization_barrier((own, base))
+    own_got = permute(own, along_zl(3))
+    ahead, back, own_got = lax.optimization_barrier((first[0], second[0], own_got))
+    round_y()
+    two_blocks = jnp.stack([own, own_got])
+    two_got = permute(two_blocks, along_zl(1))
+    ahead, back, two_got = lax.optimization_barrier((first[1], second[1], two_got))
+    round_y()
+    line = jnp.concatenate([two_blocks, two_got], axis=0)
+    blocks = [line] + [permute(line, along_x(step)) for step in (1, -1)]
+    ahead, line_tied, *_ = lax.optimization_barrier((first[2], line, blocks[1]))
     first.append(permute(ahead, along_y(1)))
-    second.append(permute(back, along_y(-1)))
-    blocks = [line] + [permute(line_tied, along_x(step)) for step in (1, 2, -1)]
-    ahead, back, *_ = lax.optimization_barrier((first[1], second[1], blocks[1]))
-    first.append(permute(ahead, along_y(1)))
-    second.append(permute(back, along_y(-1)))
-    ahead, _ = lax.optimization_barrier((first[2], blocks[2]))
-    first.append(permute(ahead, along_y(1)))
+    blocks.insert(2, permute(line_tied, along_x(2)))
     chunks = [base] + first + second
 
     mine, all_rows = gradient(place, chunks, blocks)
@@ -404,10 +442,9 @@
 
     shares = gather(partial, TENSOR)
     summed = jnp.sum(shares, axis=0).astype(bf16)
-    block = permute(summed, transposed)
+    block = permute(summed, rows_shifted)
     spread = jnp.broadcast_to(block[None], (16, ROWS, COLS))
-    gathered = gather(spread, TENSOR)
-    decoded = gathered.transpose(1, 0, 2).reshape(STEPS, ROWS // STEPS, D)
+    decoded = join(place, gather(spread, TENSOR)).reshape(STEPS, ROWS // STEPS, D)
     return (update.T, decoded)
 
 

time: 151 us -> 150 us (level); the launches traced: 148 us -> 150 us
  blocking collectives: 31.8 us -> 37.1 us
  starting transfers between devices: 66.8 us -> 62.7 us
    all_to_all x2, blocking collectives: 31.8 us -> 37.1 us  [gather(): return lax.all_to_all(value, axes, split_axis=0, concat_axis=0, tiled=True)]
    ppermute x17, waiting for transfers between devices: 38 us -> 33.2 us  [permute(): return lax.ppermute(value, AXES, pairs)]
    all_to_all x1, waiting for transfers between devices: 0.01 us -> 4.66 us  [gather(): return lax.all_to_all(value, axes, split_axis=0, concat_axis=0, tiled=True)]
    ppermute x17, starting transfers between devices: 56.5 us -> 52.5 us  [permute(): return lax.ppermute(value, AXES, pairs)]
  transfers between devices with their start and end apart: 18 -> 18, of which waited for: 13 -> 11; matrix products, arithmetic and copies ran while one was open for 0% -> 0% of each run, Pallas kernels for 1% -> 1%
where the time goes in v12:
time: 150 us
  starting transfers between devices  62.7 us (42%)
  waiting for transfers between devices  37.9 us (25%)
  blocking collectives  37.1 us (25%)
  Pallas kernels  7.45 us (5%)
  local copies, waits for them, and re-layouts  3.5 us (2%)
    ppermute x17, starting transfers between devices, permute(): return lax.ppermute(value, AXES, pairs)  52.5 us
    all_to_all x2, blocking collectives, gather(): return lax.all_to_all(value, axes, split_axis=0, concat_axis=0, tiled=True)  37.1 us
    ppermute x17, waiting for transfers between devices, permute(): return lax.ppermute(value, AXES, pairs)  33.2 us
    all_to_all x1, starting transfers between devices, gather(): return lax.all_to_all(value, axes, split_axis=0, concat_axis=0, tiled=True)  10.3 us
    all_to_all x1, waiting for transfers between devices, gather(): return lax.all_to_all(value, axes, split_axis=0, concat_axis=0, tiled=True)  4.66 us
  transfers between devices with their start and end apart: 18, of which 11 were waited for; matrix products, arithmetic and copies ran while one was open for 0% of the time, Pallas kernels for 1%

profile of v12, /device:TPU:56, one launch (start us, length us, event | category | flops | bytes accessed | tf_op | source)
XLA Modules:
  0.0 149.7 jit_solution(16724286324769556715)
XLA Ops:
  0.6 0.0 copy-start.11
  0.6 0.0 copy-start.12
  0.7 0.0 copy-start.9
  0.7 0.0 copy-start.8
  0.7 0.0 copy-start.10
  0.7 0.1 stack.32.place_ref
  0.8 1.7 %copy-done = bf16[1,256,5120]{2,1,0:T(8,128)(2,1)S(1)} copy-done((bf16[1,256,5120]{2,1,0:T(8,128)(2,1)S(1)}, bf16[1,256,5120]{2,1,0:T(8,128)(2,1)}, u32[]{:S(2)}) %copy-start) | copy-done | bytes 2621464
  2.5 0.9 copy-done.3
  3.5 0.8 cut.1
  4.3 1.3 collective-permute-start
  5.6 0.0 copy-done.11
  5.6 0.0 copy-done.12
  5.6 0.0 copy-done.9
  5.6 0.0 copy-done.8
  5.6 0.0 copy-done.10
  5.6 0.0 copy-done.1
  5.6 0.0 copy-done.2
  5.6 1.1 attend.1.rows_ref
  6.7 0.9 collective-permute-done.pack_ref
  7.6 0.0 copy-done.4
  7.6 1.3 half.1
  8.9 10.3 %all-to-all-start = ((bf16[2,144,512]{2,1,0:T(8,128)(2,1)}), bf16[2,144,512]{2,1,0:T(8,128)(2,1)S(1)}, u32[]{:S(2)}, u32[]{:S(2)}) async-start(bf16[2,144,512]{2,1,0:T(8,128)(2,1)} %get-tuple-element.21), calls=%async_computation | async-start | bytes 589824 | tf_op jit(solution)/shard_map/all_to_all | solution.py:50
  19.2 3.8 %collective-permute-start.1 = (bf16[320,128]{1,0:T(8,128)(2,1)S(1)}, bf16[320,128]{1,0:T(8,128)(2,1)S(1)}, u32[]{:S(2)}, u32[]{:S(2)}) collective-permute-start(bf16[320,128]{1,0:T(8,128)(2,1)S(1)} %get-tuple-element.22), channel_id=1, source_target_pairs={{0,96},{1,65},{2,34},{3,3},{4,116},{5,85},{6,54},{7,23},{8,232},{9... | collective-permute-start | bytes 245768 | tf_op jit(solution)/shard_map/ppermute | solution.py:46
  23.0 4.5 %collective-permute-done.1._ = bf16[320,128]{1,0:T(8,128)(2,1)S(1)} collective-permute-done((bf16[320,128]{1,0:T(8,128)(2,1)S(1)}, bf16[320,128]{1,0:T(8,128)(2,1)S(1)}, u32[]{:S(2)}, u32[]{:S(2)}) %collective-permute-start.1) | collective-permute-done | bytes 81952 | tf_op jit(solution)/shard_map/ppermute | solution.py:46
  27.5 4.7 %all-to-all-done.halves_ref = bf16[2,144,512]{2,1,0:T(8,128)(2,1)S(1)} async-done(((bf16[2,144,512]{2,1,0:T(8,128)(2,1)}), bf16[2,144,512]{2,1,0:T(8,128)(2,1)S(1)}, u32[]{:S(2)}, u32[]{:S(2)}) %all-to-all-start) | async-done | bytes 294944 | tf_op jit(solution)/shard_map/all_to_all | solution.py:50
  32.2 1.9 %collective-permute-start.3 = (bf16[272,512]{1,0:T(8,128)(2,1)S(1)}, bf16[272,512]{1,0:T(8,128)(2,1)S(1)}, u32[]{:S(2)}, u32[]{:S(2)}) collective-permute-start(bf16[272,512]{1,0:T(8,128)(2,1)S(1)} %base.1.refs_0_), channel_id=1, source_target_pairs={{0,32},{1,33},{2,34},{3,35},{4,36},{5,37},{6,38},{7,39},{8,40},{9,... | collective-permute-start | bytes 835592 | tf_op jit(solution)/shard_map/ppermute | solution.py:46
  34.1 3.9 %collective-permute-start.2 = (bf16[272,512]{1,0:T(8,128)(2,1)S(1)}, bf16[272,512]{1,0:T(8,128)(2,1)S(1)}, u32[]{:S(2)}, u32[]{:S(2)}) collective-permute-start(bf16[272,512]{1,0:T(8,128)(2,1)S(1)} %base.1.refs_0_), channel_id=1, source_target_pairs={{0,224},{1,225},{2,226},{3,227},{4,228},{5,229},{6,230},{7,231},{8... | collective-permute-start | bytes 835592 | tf_op jit(solution)/shard_map/ppermute | solution.py:46
  38.1 5.6 %collective-permute-start.4 = (bf16[320,128]{1,0:T(8,128)(2,1)S(1)}, bf16[320,128]{1,0:T(8,128)(2,1)S(1)}, u32[]{:S(2)}, u32[]{:S(2)}) collective-permute-start(bf16[320,128]{1,0:T(8,128)(2,1)S(1)} %collective-permute-done.1._), channel_id=1, source_target_pairs={{0,12},{1,13},{2,14},{3,15},{4,8},{5,9},{6,10},{7,11},{8,4},{9,5},... | collective-permute-start | bytes 245768 | tf_op jit(solution)/shard_map/ppermute | solution.py:46
  43.7 2.5 %collective-permute-done.4 = bf16[320,128]{1,0:T(8,128)(2,1)S(1)} collective-permute-done((bf16[320,128]{1,0:T(8,128)(2,1)S(1)}, bf16[320,128]{1,0:T(8,128)(2,1)S(1)}, u32[]{:S(2)}, u32[]{:S(2)}) %collective-permute-start.4) | collective-permute-done | bytes 81952 | tf_op jit(solution)/shard_map/ppermute | solution.py:46
  46.2 0.0 collective-permute-done.3.refs_5_
  46.2 0.0 collective-permute-done.2.refs_1_
  46.2 3.4 %collective-permute-start.5 = (bf16[272,512]{1,0:T(8,128)(2,1)S(1)}, bf16[272,512]{1,0:T(8,128)(2,1)S(1)}, u32[]{:S(2)}, u32[]{:S(2)}) collective-permute-start(bf16[272,512]{1,0:T(8,128)(2,1)S(1)} %collective-permute-done.2.refs_1_), channel_id=1, source_target_pairs={{0,224},{1,225},{2,226},{3,227},{4,228},{5,229},{6,230},{7,231},{8... | collective-permute-start | bytes 835592 | tf_op jit(solution)/shard_map/ppermute | solution.py:46
  49.6 3.7 %collective-permute-start.6 = (bf16[272,512]{1,0:T(8,128)(2,1)S(1)}, bf16[272,512]{1,0:T(8,128)(2,1)S(1)}, u32[]{:S(2)}, u32[]{:S(2)}) collective-permute-start(bf16[272,512]{1,0:T(8,128)(2,1)S(1)} %collective-permute-done.3.refs_5_), channel_id=1, source_target_pairs={{0,32},{1,33},{2,34},{3,35},{4,36},{5,37},{6,38},{7,39},{8,40},{9,... | collective-permute-start | bytes 835592 | tf_op jit(solution)/shard_map/ppermute | solution.py:46
  53.3 5.4 %collective-permute-start.7 = (bf16[2,320,128]{2,1,0:T(8,128)(2,1)S(1)}, bf16[2,320,128]{2,1,0:T(8,128)(2,1)S(1)}, u32[]{:S(2)}, u32[]{:S(2)}) collective-permute-start(bf16[2,320,128]{2,1,0:T(8,128)(2,1)S(1)} %pad_maximum_fusion.1), channel_id=1, source_target_pairs={{0,4},{1,5},{2,6},{3,7},{4,0},{5,1},{6,2},{7,3},{8,12},{9,13},{10,... | collective-permute-start | bytes 491528 | tf_op jit(solution)/shard_map/ppermute | solution.py:46
  58.7 3.3 %collective-permute-done.7 = bf16[2,320,128]{2,1,0:T(8,128)(2,1)S(1)} collective-permute-done((bf16[2,320,128]{2,1,0:T(8,128)(2,1)S(1)}, bf16[2,320,128]{2,1,0:T(8,128)(2,1)S(1)}, u32[]{:S(2)}, u32[]{:S(2)}) %collective-permute-start.7) | collective-permute-done | bytes 163872 | tf_op jit(solution)/shard_map/ppermute | solution.py:46
  62.0 0.0 collective-permute-done.5.refs_2_
  62.0 0.0 collective-permute-done.6.refs_6_
  62.1 0.0 copy-start.7
  62.1 7.2 %collective-permute-start.9 = (bf16[4,320,128]{2,1,0:T(8,128)(2,1)S(1)}, bf16[4,320,128]{2,1,0:T(8,128)(2,1)S(1)}, u32[]{:S(2)}, u32[]{:S(2)}) collective-permute-start(bf16[4,320,128]{2,1,0:T(8,128)(2,1)S(1)} %pad_maximum_fusion.refs_8_), channel_id=1, source_target_pairs={{0,3},{1,0},{2,1},{3,2},{4,7},{5,4},{6,5},{7,6},{8,11},{9,8},{10,9... | collective-permute-start | bytes 983048 | tf_op jit(solution)/shard_map/ppermute | solution.py:46
  69.3 1.9 %collective-permute-start.8 = (bf16[272,512]{1,0:T(8,128)(2,1)S(1)}, bf16[272,512]{1,0:T(8,128)(2,1)S(1)}, u32[]{:S(2)}, u32[]{:S(2)}) collective-permute-start(bf16[272,512]{1,0:T(8,128)(2,1)S(1)} %collective-permute-done.5.refs_2_), channel_id=1, source_target_pairs={{0,224},{1,225},{2,226},{3,227},{4,228},{5,229},{6,230},{7,231},{8... | collective-permute-start | bytes 835592 | tf_op jit(solution)/shard_map/ppermute | solution.py:46
  71.3 1.9 %collective-permute-start.13 = (bf16[4,320,128]{2,1,0:T(8,128)(2,1)S(1)}, bf16[4,320,128]{2,1,0:T(8,128)(2,1)S(1)}, u32[]{:S(2)}, u32[]{:S(2)}) collective-permute-start(bf16[4,320,128]{2,1,0:T(8,128)(2,1)S(1)} %pad_maximum_fusion.refs_8_), channel_id=1, source_target_pairs={{0,1},{1,2},{2,3},{3,0},{4,5},{5,6},{6,7},{7,4},{8,9},{9,10},{10,1... | collective-permute-start | bytes 983048 | tf_op jit(solution)/shard_map/ppermute | solution.py:46
  73.2 5.8 %collective-permute-done.8.refs_3_ = bf16[272,512]{1,0:T(8,128)(2,1)S(1)} collective-permute-done((bf16[272,512]{1,0:T(8,128)(2,1)S(1)}, bf16[272,512]{1,0:T(8,128)(2,1)S(1)}, u32[]{:S(2)}, u32[]{:S(2)}) %collective-permute-start.8) | collective-permute-done | bytes 278560 | tf_op jit(solution)/shard_map/ppermute | solution.py:46
  79.0 0.0 collective-permute-done.9.refs_9_
  79.0 1.9 %collective-permute-start.12 = (bf16[4,320,128]{2,1,0:T(8,128)(2,1)S(1)}, bf16[4,320,128]{2,1,0:T(8,128)(2,1)S(1)}, u32[]{:S(2)}, u32[]{:S(2)}) collective-permute-start(bf16[4,320,128]{2,1,0:T(8,128)(2,1)S(1)} %pad_maximum_fusion.refs_8_), channel_id=1, source_target_pairs={{0,2},{1,3},{2,0},{3,1},{4,6},{5,7},{6,4},{7,5},{8,10},{9,11},{10,... | collective-permute-start | bytes 983048 | tf_op jit(solution)/shard_map/ppermute | solution.py:46
  80.9 1.9 %collective-permute-start.11 = (bf16[272,512]{1,0:T(8,128)(2,1)S(1)}, bf16[272,512]{1,0:T(8,128)(2,1)S(1)}, u32[]{:S(2)}, u32[]{:S(2)}) collective-permute-start(bf16[272,512]{1,0:T(8,128)(2,1)S(1)} %collective-permute-done.6.refs_6_), channel_id=1, source_target_pairs={{0,32},{1,33},{2,34},{3,35},{4,36},{5,37},{6,38},{7,39},{8,40},{9,... | collective-permute-start | bytes 835592 | tf_op jit(solution)/shard_map/ppermute | solution.py:46
  82.8 3.9 %collective-permute-start.10 = (bf16[272,512]{1,0:T(8,128)(2,1)S(1)}, bf16[272,512]{1,0:T(8,128)(2,1)S(1)}, u32[]{:S(2)}, u32[]{:S(2)}) collective-permute-start(bf16[272,512]{1,0:T(8,128)(2,1)S(1)} %collective-permute-done.8.refs_3_), channel_id=1, source_target_pairs={{0,224},{1,225},{2,226},{3,227},{4,228},{5,229},{6,230},{7,231},{8... | collective-permute-start | bytes 835592 | tf_op jit(solution)/shard_map/ppermute | solution.py:46
  86.8 3.5 %collective-permute-done.11.refs_7_ = bf16[272,512]{1,0:T(8,128)(2,1)S(1)} collective-permute-done((bf16[272,512]{1,0:T(8,128)(2,1)S(1)}, bf16[272,512]{1,0:T(8,128)(2,1)S(1)}, u32[]{:S(2)}, u32[]{:S(2)}) %collective-permute-start.11) | collective-permute-done | bytes 278560 | tf_op jit(solution)/shard_map/ppermute | solution.py:46
  90.3 0.0 collective-permute-done.13.refs_11_
  90.3 2.2 %collective-permute-done.10.refs_4_ = bf16[272,512]{1,0:T(8,128)(2,1)S(1)} collective-permute-done((bf16[272,512]{1,0:T(8,128)(2,1)S(1)}, bf16[272,512]{1,0:T(8,128)(2,1)S(1)}, u32[]{:S(2)}, u32[]{:S(2)}) %collective-permute-start.10) | collective-permute-done | bytes 278560 | tf_op jit(solution)/shard_map/ppermute | solution.py:46
  92.5 0.0 collective-permute-done.12.refs_10_
  92.5 1.7 %gradient.1 = (f32[320,512]{1,0:T(8,128)S(1)}, f32[128,512]{1,0:T(8,128)S(1)}) custom-call(s32[5]{0:T(128)S(1)} %stack.32.place_ref, bf16[272,512]{1,0:T(8,128)(2,1)S(1)} %base.1.refs_0_, bf16[272,512]{1,0:T(8,128)(2,1)S(1)} %collective-permute-done.2.refs_1_, bf16[272,512]{1,0:T(8,128)(2,1)S(1)} %collective-permute-done.5.refs_2_, ...), custom_call_target="tpu_custom_call" | custom-call | flops 671088640 | bytes 6291456 | tf_op jit(solution)/shard_map/gradient/pallas_call | solution.py:288
  94.2 1.3 collective-permute-start.14
  95.5 1.7 %collective-permute-done.14.got_ref = f32[320,512]{1,0:T(8,128)S(1)} collective-permute-done((f32[320,512]{1,0:T(8,128)S(1)}, f32[320,512]{1,0:T(8,128)S(1)}, u32[]{:S(2)}, u32[]{:S(2)}) %collective-permute-start.14) | collective-permute-done | bytes 655392 | tf_op jit(solution)/shard_map/ppermute | solution.py:46
  97.2 0.0 copy-done.5
  97.2 0.5 adam.1.update_ref
  97.7 1.3 collective-permute-start.15
  99.0 2.2 %collective-permute-done.15.update_got = bf16[320,512]{1,0:T(8,128)(2,1)S(1)} collective-permute-done((bf16[320,512]{1,0:T(8,128)(2,1)S(1)}, bf16[320,512]{1,0:T(8,128)(2,1)S(1)}, u32[]{:S(2)}, u32[]{:S(2)}) %collective-permute-start.15) | collective-permute-done | bytes 327712 | tf_op jit(solution)/shard_map/ppermute | solution.py:46
  101.2 1.5 step.1
  102.7 17.9 %all_to_all.15 = f32[16,8,320]{2,1,0:T(8,128)S(1)} all-to-all(f32[16,8,320]{2,1,0:T(8,128)S(1)} %get-tuple-element.35), channel_id=1, replica_groups=mesh['group'=2,'y'=8,'z_hi'=2,'z_lo'=4,'x'=4] {'z_lo','x'}, dimensions={0} | all-to-all | bytes 327680 | tf_op jit(solution)/shard_map/all_to_all | solution.py:50
  120.6 1.9 %collective-permute-start.16 = (bf16[8,320]{1,0:T(8,128)(2,1)S(1)}, bf16[8,320]{1,0:T(8,128)(2,1)S(1)}, u32[]{:S(2)}, u32[]{:S(2)}) collective-permute-start(bf16[8,320]{1,0:T(8,128)(2,1)S(1)} %reduce_sum.9), channel_id=1, source_target_pairs={{0,160},{1,193},{2,226},{3,3},{4,180},{5,213},{6,246},{7,23},{8,40... | collective-permute-start | bytes 15368 | tf_op jit(solution)/shard_map/ppermute | solution.py:46
  122.5 6.6 %collective-permute-done.16 = bf16[8,320]{1,0:T(8,128)(2,1)S(1)} collective-permute-done((bf16[8,320]{1,0:T(8,128)(2,1)S(1)}, bf16[8,320]{1,0:T(8,128)(2,1)S(1)}, u32[]{:S(2)}, u32[]{:S(2)}) %collective-permute-start.16) | collective-permute-done | bytes 5152 | tf_op jit(solution)/shard_map/ppermute | solution.py:46
  129.1 19.3 %all_to_all.16.blocks_ref = bf16[16,8,320]{2,1,0:T(8,128)(2,1)S(1)} all-to-all(bf16[16,8,320]{2,1,0:T(8,128)(2,1)S(1)} %broadcast_in_dim.2), channel_id=1, replica_groups=mesh['group'=2,'y'=8,'z_hi'=2,'z_lo'=4,'x'=4] {'z_lo','x'}, dimensions={0} | all-to-all | bytes 163840 | tf_op jit(solution)/shard_map/all_to_all | solution.py:50
  148.4 0.7 join.1
  149.0 0.7 reshape.12
  (14 shorter events, 0.1 us)
Async XLA Ops:
  0.6 4.9 %copy-start.11 = (s32[4,2]{0,1:T(2,128)S(1)}, s32[4,2]{0,1:T(2,128)}, u32[]{:S(2)}) copy-start(s32[4,2]{0,1:T(2,128)} %param.23) | copy-start | bytes 100
  0.6 4.9 %copy-start.12 = (s32[2]{0:T(128)S(1)}, s32[2]{0:T(128)}, u32[]{:S(2)}) copy-start(s32[2]{0:T(128)} %lengths_ref.1) | copy-start | bytes 28
  0.7 4.9 %copy-start.9 = (bf16[4,2,1024]{2,1,0:T(2,128)(2,1)S(1)}, bf16[4,2,1024]{2,1,0:T(2,128)(2,1)}, u32[]{:S(2)}) copy-start(bf16[4,2,1024]{2,1,0:T(2,128)(2,1)} %nv_ref.1) | copy-start | bytes 49156
  0.7 4.9 %copy-start.8 = (bf16[4,2,1024]{2,1,0:T(2,128)(2,1)S(1)}, bf16[4,2,1024]{2,1,0:T(2,128)(2,1)}, u32[]{:S(2)}) copy-start(bf16[4,2,1024]{2,1,0:T(2,128)(2,1)} %nk_ref.1) | copy-start | bytes 49156
  0.7 4.9 %copy-start.10 = (bf16[4,2,512]{2,1,0:T(2,128)(2,1)S(1)}, bf16[4,2,512]{2,1,0:T(2,128)(2,1)}, u32[]{:S(2)}) copy-start(bf16[4,2,512]{2,1,0:T(2,128)(2,1)} %q_ref.1) | copy-start | bytes 24580
  0.8 1.7 %copy-start = (bf16[1,256,5120]{2,1,0:T(8,128)(2,1)S(1)}, bf16[1,256,5120]{2,1,0:T(8,128)(2,1)}, u32[]{:S(2)}) copy-start(bf16[1,256,5120]{2,1,0:T(8,128)(2,1)} %param.13) | copy-start | bytes 7864324
  2.5 0.9 copy-start.3
  3.5 2.2 %copy-start.1 = (bf16[2,2048,128]{2,1,0:T(8,128)(2,1)S(1)}, bf16[2,2048,128]{2,1,0:T(8,128)(2,1)}, u32[]{:S(2)}) copy-start(bf16[2,2048,128]{2,1,0:T(8,128)(2,1)} %k_ref.1) | copy-start | bytes 3145732
  3.5 2.2 %copy-start.2 = (bf16[2,2048,128]{2,1,0:T(8,128)(2,1)S(1)}, bf16[2,2048,128]{2,1,0:T(8,128)(2,1)}, u32[]{:S(2)}) copy-start(bf16[2,2048,128]{2,1,0:T(8,128)(2,1)} %v_ref.1) | copy-start | bytes 3145732
  3.5 4.2 %copy-start.4 = (bf16[1,256,512]{2,1,0:T(8,128)(2,1)S(1)}, bf16[1,256,512]{2,1,0:T(8,128)(2,1)}, u32[]{:S(2)}) copy-start(bf16[1,256,512]{2,1,0:T(8,128)(2,1)} %param.12) | copy-start | bytes 786436
  4.3 3.4 %collective-permute-start = (bf16[208,512]{1,0:T(8,128)(2,1)S(1)}, bf16[208,512]{1,0:T(8,128)(2,1)S(1)}, u32[]{:S(2)}, u32[]{:S(2)}) collective-permute-start(bf16[208,512]{1,0:T(8,128)(2,1)S(1)} %get-tuple-element.20), channel_id=1, source_target_pairs={{256,0},{257,1},{258,2},{259,3},{260,4},{261,5},{262,6},{263,7},{2... | collective-permute-start | bytes 638984 | tf_op jit(solution)/shard_map/ppermute | solution.py:46
  8.9 23.3 %all-to-all-start = ((bf16[2,144,512]{2,1,0:T(8,128)(2,1)}), bf16[2,144,512]{2,1,0:T(8,128)(2,1)S(1)}, u32[]{:S(2)}, u32[]{:S(2)}) async-start(bf16[2,144,512]{2,1,0:T(8,128)(2,1)} %get-tuple-element.21), calls=%async_computation | async-start | bytes 589824 | tf_op jit(solution)/shard_map/all_to_all | solution.py:50
  19.2 78.0 %copy-start.5 = (f32[1,512,320]{1,2,0:T(8,128)S(1)}, f32[1,512,320]{1,2,0:T(8,128)}, u32[]{:S(2)}) copy-start(f32[1,512,320]{1,2,0:T(8,128)} %param.15) | copy-start | bytes 1966084
  19.2 78.0 %copy-start.6 = (f32[1,512,320]{1,2,0:T(8,128)S(1)}, f32[1,512,320]{1,2,0:T(8,128)}, u32[]{:S(2)}) copy-start(f32[1,512,320]{1,2,0:T(8,128)} %param.16) | copy-start | bytes 1966084
  19.2 8.3 %collective-permute-start.1 = (bf16[320,128]{1,0:T(8,128)(2,1)S(1)}, bf16[320,128]{1,0:T(8,128)(2,1)S(1)}, u32[]{:S(2)}, u32[]{:S(2)}) collective-permute-start(bf16[320,128]{1,0:T(8,128)(2,1)S(1)} %get-tuple-element.22), channel_id=1, source_target_pairs={{0,96},{1,65},{2,34},{3,3},{4,116},{5,85},{6,54},{7,23},{8,232},{9... | collective-permute-start | bytes 245768 | tf_op jit(solution)/shard_map/ppermute | solution.py:46
  32.2 14.0 %collective-permute-start.3 = (bf16[272,512]{1,0:T(8,128)(2,1)S(1)}, bf16[272,512]{1,0:T(8,128)(2,1)S(1)}, u32[]{:S(2)}, u32[]{:S(2)}) collective-permute-start(bf16[272,512]{1,0:T(8,128)(2,1)S(1)} %base.1.refs_0_), channel_id=1, source_target_pairs={{0,32},{1,33},{2,34},{3,35},{4,36},{5,37},{6,38},{7,39},{8,40},{9,... | collective-permute-start | bytes 835592 | tf_op jit(solution)/shard_map/ppermute | solution.py:46
  34.1 12.1 %collective-permute-start.2 = (bf16[272,512]{1,0:T(8,128)(2,1)S(1)}, bf16[272,512]{1,0:T(8,128)(2,1)S(1)}, u32[]{:S(2)}, u32[]{:S(2)}) collective-permute-start(bf16[272,512]{1,0:T(8,128)(2,1)S(1)} %base.1.refs_0_), channel_id=1, source_target_pairs={{0,224},{1,225},{2,226},{3,227},{4,228},{5,229},{6,230},{7,231},{8... | collective-permute-start | bytes 835592 | tf_op jit(solution)/shard_map/ppermute | solution.py:46
  38.1 8.1 %collective-permute-start.4 = (bf16[320,128]{1,0:T(8,128)(2,1)S(1)}, bf16[320,128]{1,0:T(8,128)(2,1)S(1)}, u32[]{:S(2)}, u32[]{:S(2)}) collective-permute-start(bf16[320,128]{1,0:T(8,128)(2,1)S(1)} %collective-permute-done.1._), channel_id=1, source_target_pairs={{0,12},{1,13},{2,14},{3,15},{4,8},{5,9},{6,10},{7,11},{8,4},{9,5},... | collective-permute-start | bytes 245768 | tf_op jit(solution)/shard_map/ppermute | solution.py:46
  46.2 15.8 %collective-permute-start.5 = (bf16[272,512]{1,0:T(8,128)(2,1)S(1)}, bf16[272,512]{1,0:T(8,128)(2,1)S(1)}, u32[]{:S(2)}, u32[]{:S(2)}) collective-permute-start(bf16[272,512]{1,0:T(8,128)(2,1)S(1)} %collective-permute-done.2.refs_1_), channel_id=1, source_target_pairs={{0,224},{1,225},{2,226},{3,227},{4,228},{5,229},{6,230},{7,231},{8... | collective-permute-start | bytes 835592 | tf_op jit(solution)/shard_map/ppermute | solution.py:46
  49.6 12.5 %collective-permute-start.6 = (bf16[272,512]{1,0:T(8,128)(2,1)S(1)}, bf16[272,512]{1,0:T(8,128)(2,1)S(1)}, u32[]{:S(2)}, u32[]{:S(2)}) collective-permute-start(bf16[272,512]{1,0:T(8,128)(2,1)S(1)} %collective-permute-done.3.refs_5_), channel_id=1, source_target_pairs={{0,32},{1,33},{2,34},{3,35},{4,36},{5,37},{6,38},{7,39},{8,40},{9,... | collective-permute-start | bytes 835592 | tf_op jit(solution)/shard_map/ppermute | solution.py:46
  53.3 8.7 %collective-permute-start.7 = (bf16[2,320,128]{2,1,0:T(8,128)(2,1)S(1)}, bf16[2,320,128]{2,1,0:T(8,128)(2,1)S(1)}, u32[]{:S(2)}, u32[]{:S(2)}) collective-permute-start(bf16[2,320,128]{2,1,0:T(8,128)(2,1)S(1)} %pad_maximum_fusion.1), channel_id=1, source_target_pairs={{0,4},{1,5},{2,6},{3,7},{4,0},{5,1},{6,2},{7,3},{8,12},{9,13},{10,... | collective-permute-start | bytes 491528 | tf_op jit(solution)/shard_map/ppermute | solution.py:46
  62.1 39.1 %copy-start.7 = (bf16[512,320]{0,1:T(8,128)(2,1)S(1)}, bf16[512,320]{0,1:T(8,128)(2,1)}, u32[]{:S(2)}) copy-start(bf16[512,320]{0,1:T(8,128)(2,1)} %param.14) | copy-start | bytes 983044
  62.1 16.9 %collective-permute-start.9 = (bf16[4,320,128]{2,1,0:T(8,128)(2,1)S(1)}, bf16[4,320,128]{2,1,0:T(8,128)(2,1)S(1)}, u32[]{:S(2)}, u32[]{:S(2)}) collective-permute-start(bf16[4,320,128]{2,1,0:T(8,128)(2,1)S(1)} %pad_maximum_fusion.refs_8_), channel_id=1, source_target_pairs={{0,3},{1,0},{2,1},{3,2},{4,7},{5,4},{6,5},{7,6},{8,11},{9,8},{10,9... | collective-permute-start | bytes 983048 | tf_op jit(solution)/shard_map/ppermute | solution.py:46
  69.3 9.7 %collective-permute-start.8 = (bf16[272,512]{1,0:T(8,128)(2,1)S(1)}, bf16[272,512]{1,0:T(8,128)(2,1)S(1)}, u32[]{:S(2)}, u32[]{:S(2)}) collective-permute-start(bf16[272,512]{1,0:T(8,128)(2,1)S(1)} %collective-permute-done.5.refs_2_), channel_id=1, source_target_pairs={{0,224},{1,225},{2,226},{3,227},{4,228},{5,229},{6,230},{7,231},{8... | collective-permute-start | bytes 835592 | tf_op jit(solution)/shard_map/ppermute | solution.py:46
  71.3 19.0 %collective-permute-start.13 = (bf16[4,320,128]{2,1,0:T(8,128)(2,1)S(1)}, bf16[4,320,128]{2,1,0:T(8,128)(2,1)S(1)}, u32[]{:S(2)}, u32[]{:S(2)}) collective-permute-start(bf16[4,320,128]{2,1,0:T(8,128)(2,1)S(1)} %pad_maximum_fusion.refs_8_), channel_id=1, source_target_pairs={{0,1},{1,2},{2,3},{3,0},{4,5},{5,6},{6,7},{7,4},{8,9},{9,10},{10,1... | collective-permute-start | bytes 983048 | tf_op jit(solution)/shard_map/ppermute | solution.py:46
  79.0 13.5 %collective-permute-start.12 = (bf16[4,320,128]{2,1,0:T(8,128)(2,1)S(1)}, bf16[4,320,128]{2,1,0:T(8,128)(2,1)S(1)}, u32[]{:S(2)}, u32[]{:S(2)}) collective-permute-start(bf16[4,320,128]{2,1,0:T(8,128)(2,1)S(1)} %pad_maximum_fusion.refs_8_), channel_id=1, source_target_pairs={{0,2},{1,3},{2,0},{3,1},{4,6},{5,7},{6,4},{7,5},{8,10},{9,11},{10,... | collective-permute-start | bytes 983048 | tf_op jit(solution)/shard_map/ppermute | solution.py:46
  80.9 9.3 %collective-permute-start.11 = (bf16[272,512]{1,0:T(8,128)(2,1)S(1)}, bf16[272,512]{1,0:T(8,128)(2,1)S(1)}, u32[]{:S(2)}, u32[]{:S(2)}) collective-permute-start(bf16[272,512]{1,0:T(8,128)(2,1)S(1)} %collective-permute-done.6.refs_6_), channel_id=1, source_target_pairs={{0,32},{1,33},{2,34},{3,35},{4,36},{5,37},{6,38},{7,39},{8,40},{9,... | collective-permute-start | bytes 835592 | tf_op jit(solution)/shard_map/ppermute | solution.py:46
  82.8 9.7 %collective-permute-start.10 = (bf16[272,512]{1,0:T(8,128)(2,1)S(1)}, bf16[272,512]{1,0:T(8,128)(2,1)S(1)}, u32[]{:S(2)}, u32[]{:S(2)}) collective-permute-start(bf16[272,512]{1,0:T(8,128)(2,1)S(1)} %collective-permute-done.8.refs_3_), channel_id=1, source_target_pairs={{0,224},{1,225},{2,226},{3,227},{4,228},{5,229},{6,230},{7,231},{8... | collective-permute-start | bytes 835592 | tf_op jit(solution)/shard_map/ppermute | solution.py:46
  94.2 3.0 %collective-permute-start.14 = (f32[320,512]{1,0:T(8,128)S(1)}, f32[320,512]{1,0:T(8,128)S(1)}, u32[]{:S(2)}, u32[]{:S(2)}) collective-permute-start(f32[320,512]{1,0:T(8,128)S(1)} %get-tuple-element.32.mine_ref), channel_id=1, source_target_pairs={{0,256},{1,257},{2,258},{3,259},{4,260},{5,261},{6,262},{7,263},{8... | collective-permute-start | bytes 1966088 | tf_op jit(solution)/shard_map/ppermute | solution.py:46
  97.7 3.5 %collective-permute-start.15 = (bf16[320,512]{1,0:T(8,128)(2,1)S(1)}, bf16[320,512]{1,0:T(8,128)(2,1)S(1)}, u32[]{:S(2)}, u32[]{:S(2)}) collective-permute-start(bf16[320,512]{1,0:T(8,128)(2,1)S(1)} %adam.1.update_ref), channel_id=1, source_target_pairs={{256,0},{257,1},{258,2},{259,3},{260,4},{261,5},{262,6},{263,7},{2... | collective-permute-start | bytes 983048 | tf_op jit(solution)/shard_map/ppermute | solution.py:46
  120.6 8.5 %collective-permute-start.16 = (bf16[8,320]{1,0:T(8,128)(2,1)S(1)}, bf16[8,320]{1,0:T(8,128)(2,1)S(1)}, u32[]{:S(2)}, u32[]{:S(2)}) collective-permute-start(bf16[8,320]{1,0:T(8,128)(2,1)S(1)} %reduce_sum.9), channel_id=1, source_target_pairs={{0,160},{1,193},{2,226},{3,3},{4,180},{5,213},{6,246},{7,23},{8,40... | collective-permute-start | bytes 15368 | tf_op jit(solution)/shard_map/ppermute | solution.py:46

commit v13 on v12

--- a/solution.py
+++ b/solution.py
@@ -66,14 +66,6 @@
     return (g, (y + shift_of(zl, x)) % 8, zh ^ (zl & 1), zl, x)
 
 
-def along_zl(flip):
-    return lambda g, y, zh, zl, x: (g, y, zh, zl ^ flip, x)
-
-
-def along_x(step):
-    return lambda g, y, zh, zl, x: (g, y, zh, zl, (x + (step if g == 1 else -step)) % 4)
-
-
 def to_learner(g, y, zh, zl, x):
     return (1, y, zh, zl, x) if g == 0 else None
 
@@ -82,7 +74,6 @@
     return (0, y, zh, zl, x) if g == 1 else None
 
 
-FLIPS = (0, 3, 1, 2)
 HOPS = (0, 1, 2, 3, 4, -1, -2, -3)
 
 
@@ -240,48 +231,72 @@
     )(place, *parts)
 
 
-def base_kernel(halves_ref, _, out_ref):
+def base_kernel(halves_ref, cut_ref, out_ref, spread_ref):
     for z_hi in range(2):
         out_ref[z_hi * HALF : (z_hi + 1) * HALF, :] = halves_ref[z_hi, :HALF, :]
     rows = [halves_ref[z_hi, HALF:, :].astype(f32)[:ROWS] for z_hi in range(2)]
     out_ref[TOK:, :] = jnp.concatenate(rows, axis=0).astype(bf16)
-
-
-def base_of(halves, after):
+    for n in range(16):
+        spread_ref[n] = cut_ref[...]
+
+
+def base_of(*operands):
     return pl.pallas_call(
         base_kernel,
-        out_shape=jax.ShapeDtypeStruct((TOK + PAD, FEAT), bf16),
-        in_specs=[VMEM, HBM],
-        out_specs=VMEM,
+        out_shape=(
+            jax.ShapeDtypeStruct((TOK + PAD, FEAT), bf16),
+            jax.ShapeDtypeStruct((16, COLS, HALF), bf16),
+        ),
+        in_specs=[VMEM] * 2,
+        out_specs=(VMEM, VMEM),
         compiler_params=SMALL,
         name="base",
-    )(halves, after)
+    )(*operands)
 
 
 def gradient_kernel(place_ref, *refs):
-    chunks, blocks, (out_ref, rows_ref, block_rows) = refs[:8], refs[8:12], refs[12:]
-    side, y, z_hi, own_z_lo, x = (place_ref[n] for n in range(5))
+    chunks, blocks, (out_ref, rows_ref) = refs[:8], refs[8], refs[9:11]
+    chunk_rows, block_tiles, block_rows, row_tiles, sems = refs[11:]
+    block_copy = pltpu.make_async_copy(blocks, block_tiles, sems.at[0])
+    act_copies = [
+        pltpu.make_async_copy(
+            chunks[n].at[:TOK], chunk_rows.at[pl.ds(n * TOK, TOK)], sems.at[4 + n]
+        )
+        for n in range(8)
+    ]
+    row_copies = [
+        pltpu.make_async_copy(chunks[n].at[TOK:], row_tiles.at[n], sems.at[12 + n])
+        for n in range(8)
+    ]
+    for copy in [block_copy] + act_copies + row_copies:
+        copy.start()
+    block_copy.wait()
+    side, y, z_hi = (place_ref[n] for n in range(3))
+    places = []
     for n, hop in enumerate(HOPS):
         shift = jnp.where(side == 1, 4 if hop == 4 else -hop, hop)
-        block_y = (y + shift) & 7
-        rows = chunks[n][TOK:, :].astype(f32)
         for block_zh in range(2):
-            span = slice(block_zh * HALF, (block_zh + 1) * HALF)
-            flip = own_z_lo ^ (2 * ((shift + 3) >> 2) + (z_hi ^ block_zh))
-            slot = sum(jnp.where(flip == f, m, 0) for m, f in enumerate(FLIPS))
-            source = (shift + 3) - x
-            source = jnp.where(side == 1, -source, source) & 3
-            block = blocks[0][slot]
-            for m in range(1, 4):
-                block = jnp.where(source == m, blocks[m][slot], block)
-            block_rows[:, span] = block
-            place = pl.multiple_of((2 * block_y + block_zh) * ROWS, ROWS)
-            rows_ref[pl.ds(place, ROWS), :] = rows[block_zh * ROWS : (block_zh + 1) * ROWS]
-        part = jnp.dot(block_rows[...], chunks[n][:TOK, :], preferred_element_type=f32)
-        if n == 0:
+            at = 2 * n + block_zh
+            z_lo = 2 * ((shift + 3) >> 2) + (z_hi ^ block_zh)
+            block_rows[:, at * HALF : (at + 1) * HALF] = block_tiles[
+                4 * z_lo + ((shift + 3) & 3)
+            ]
+            places.append(2 * ((y + shift) & 7) + block_zh)
+    for half in range(2):
+        for n in range(4 * half, 4 * half + 4):
+            act_copies[n].wait()
+        span = pl.ds(half * 4 * TOK, 4 * TOK)
+        part = jnp.dot(block_rows[:, span], chunk_rows[span, :], preferred_element_type=f32)
+        if half == 0:
             out_ref[...] = part
         else:
             out_ref[...] += part
+    for n in range(8):
+        row_copies[n].wait()
+        rows = row_tiles[n].astype(f32)
+        for block_zh in range(2):
+            place = pl.multiple_of(places[2 * n + block_zh] * ROWS, ROWS)
+            rows_ref[pl.ds(place, ROWS), :] = rows[block_zh * ROWS : (block_zh + 1) * ROWS]
 
 
 def gradient(place, chunks, blocks):
@@ -291,15 +306,21 @@
             jax.ShapeDtypeStruct((COLS, FEAT), f32),
             jax.ShapeDtypeStruct((16 * ROWS, FEAT), f32),
         ),
-        in_specs=[SMEM] + [VMEM] * 12,
+        in_specs=[SMEM] + [HBM] * 9,
         out_specs=(VMEM, VMEM),
-        scratch_shapes=[pltpu.VMEM((COLS, TOK), bf16)],
-        compiler_params=pltpu.CompilerParams(vmem_limit_bytes=12 * 2**20),
+        scratch_shapes=[
+            pltpu.VMEM((8 * TOK, FEAT), bf16),
+            pltpu.VMEM((16, COLS, HALF), bf16),
+            pltpu.VMEM((COLS, 8 * TOK), bf16),
+            pltpu.VMEM((8, PAD, FEAT), bf16),
+            pltpu.SemaphoreType.DMA((20,)),
+        ],
+        compiler_params=pltpu.CompilerParams(vmem_limit_bytes=60 * 2**20),
         cost_estimate=pl.CostEstimate(
             flops=2 * 8 * TOK * COLS * FEAT, bytes_accessed=6 * 2**20, transcendentals=0
         ),
         name="gradient",
-    )(place, *chunks, *blocks)
+    )(place, *chunks, blocks)
 
 
 def adam_kernel(mine_ref, got_ref, one_ref, two_ref, out_ref):
@@ -410,28 +431,15 @@
     )
     cut, halves = half_of(place, act, cut_one, pack_got, rows)
     own = permute(cut, cot_shifted)
-    base = base_of(gather(halves, "z_hi"), own)
+    base, own_spread = base_of(gather(halves, "z_hi"), own)
+    blocks = gather(own_spread, TENSOR)
     ahead = back = base
     first, second = [], []
-
-    def round_y():
+    for _ in range(3):
         first.append(permute(ahead, along_y(1)))
         second.append(permute(back, along_y(-1)))
-
-    round_y()
-    own, _ = lax.optimization_barrier((own, base))
-    own_got = permute(own, along_zl(3))
-    ahead, back, own_got = lax.optimization_barrier((first[0], second[0], own_got))
-    round_y()
-    two_blocks = jnp.stack([own, own_got])
-    two_got = permute(two_blocks, along_zl(1))
-    ahead, back, two_got = lax.optimization_barrier((first[1], second[1], two_got))
-    round_y()
-    line = jnp.concatenate([two_blocks, two_got], axis=0)
-    blocks = [line] + [permute(line, along_x(step)) for step in (1, -1)]
-    ahead, line_tied, *_ = lax.optimization_barrier((first[2], line, blocks[1]))
+        ahead, back = lax.optimization_barrier((first[-1], second[-1]))
     first.append(permute(ahead, along_y(1)))
-    blocks.insert(2, permute(line_tied, along_x(2)))
     chunks = [base] + first + second
 
     mine, all_rows = gradient(place, chunks, blocks)

time: 150 us -> 151 us (level)
  starting transfers between devices: 62.7 us -> 58.4 us
  Pallas kernels: 7.45 us -> 11.4 us
  blocking collectives: 37.1 us -> 34.6 us
  local copies, waits for them, and re-layouts: 3.5 us -> 5.73 us
    ppermute x17 -> x12, starting transfers between devices: 52.5 us -> 37.3 us  [permute(): return lax.ppermute(value, AXES, pairs)]
    all_to_all x1 -> x2, starting transfers between devices: 10.3 us -> 21.1 us  [gather(): return lax.all_to_all(value, axes, split_axis=0, concat_axis=0, tiled=True)]
    pallas_call x1, Pallas kernels: 1.72 us -> 4.4 us  [gradient(): pl.pallas_call(gradient_kernel, out_shape=(jax.ShapeDtypeStruct((COLS, FE...]
    all_to_all x2, blocking collectives: 37.1 us -> 34.6 us  [gather(): return lax.all_to_all(value, axes, split_axis=0, concat_axis=0, tiled=True)]
    unnamed x26 -> x50, local copies, waits for them, and re-layouts: 2.74 us -> 4.97 us
    ppermute x17 -> x12, waiting for transfers between devices: 33.2 us -> 33.7 us  [permute(): return lax.ppermute(value, AXES, pairs)]
    all_to_all x1 -> x2, waiting for transfers between devices: 4.66 us -> 4.8 us  [gather(): return lax.all_to_all(value, axes, split_axis=0, concat_axis=0, tiled=True)]
  transfers between devices with their start and end apart: 18 -> 14, of which waited for: 11 -> 13; matrix products, arithmetic and copies ran while one was open for 0% -> 0% of each run, Pallas kernels for 1% -> 1%
where the time goes in v13:
time: 151 us; the launch traced here: 150 us
  starting transfers between devices  58.4 us (39%)
  waiting for transfers between devices  38.5 us (25%)
  blocking collectives  34.6 us (23%)
  Pallas kernels  11.4 us (8%)
  local copies, waits for them, and re-layouts  5.73 us (4%)
    ppermute x12, starting transfers between devices, permute(): return lax.ppermute(value, AXES, pairs)  37.3 us
    all_to_all x2, blocking collectives, gather(): return lax.all_to_all(value, axes, split_axis=0, concat_axis=0, tiled=True)  34.6 us
    ppermute x12, waiting for transfers between devices, permute(): return lax.ppermute(value, AXES, pairs)  33.7 us
    all_to_all x2, starting transfers between devices, gather(): return lax.all_to_all(value, axes, split_axis=0, concat_axis=0, tiled=True)  21.1 us
    unnamed x50, local copies, waits for them, and re-layouts  4.97 us
    all_to_all x2, waiting for transfers between devices, gather(): return lax.all_to_all(value, axes, split_axis=0, concat_axis=0, tiled=True)  4.8 us
    pallas_call x1, Pallas kernels, gradient(): pl.pallas_call(gradient_kernel, out_shape=(jax.ShapeDtypeStruct((COLS, FE...  4.4 us
  transfers between devices with their start and end apart: 14, of which 13 were waited for; matrix products, arithmetic and copies ran while one was open for 0% of the time, Pallas kernels for 1%

profile of v13, /device:TPU:56, one launch (start us, length us, event | category | flops | bytes accessed | tf_op | source)
XLA Modules:
  0.0 149.6 jit_solution(7775030985463235252)
XLA Ops:
  0.6 0.1 stack.23.place_ref
  0.7 1.7 %copy-done = bf16[1,256,5120]{2,1,0:T(8,128)(2,1)S(1)} copy-done((bf16[1,256,5120]{2,1,0:T(8,128)(2,1)S(1)}, bf16[1,256,5120]{2,1,0:T(8,128)(2,1)}, u32[]{:S(2)}) %copy-start) | copy-done | bytes 2621464
  2.5 0.9 copy-done.3
  3.4 0.0 copy-start.15
  3.4 0.0 copy-start.16
  3.5 0.0 copy-start.17
  3.5 0.8 cut.1
  4.3 0.0 copy-start.4
  4.3 1.4 collective-permute-start
  5.7 0.0 copy-done.1
  5.7 0.0 copy-done.2
  5.7 0.0 copy-done.13
  5.7 0.0 copy-done.14
  5.8 0.0 copy-done.15
  5.8 0.0 copy-done.16
  5.8 0.0 copy-done.17
  5.8 1.1 attend.1.rows_ref
  6.8 0.9 collective-permute-done.pack_ref
  7.8 0.0 copy-done.11
  7.8 0.0 copy-done.4
  7.8 1.3 half.1
  9.1 10.3 %all-to-all-start = ((bf16[2,144,512]{2,1,0:T(8,128)(2,1)}), bf16[2,144,512]{2,1,0:T(8,128)(2,1)S(1)}, u32[]{:S(2)}, u32[]{:S(2)}) async-start(bf16[2,144,512]{2,1,0:T(8,128)(2,1)} %get-tuple-element.19), calls=%async_computation | async-start | bytes 589824 | tf_op jit(solution)/shard_map/all_to_all | solution.py:50
  19.4 3.7 %collective-permute-start.1 = (bf16[320,128]{1,0:T(8,128)(2,1)S(1)}, bf16[320,128]{1,0:T(8,128)(2,1)S(1)}, u32[]{:S(2)}, u32[]{:S(2)}) collective-permute-start(bf16[320,128]{1,0:T(8,128)(2,1)S(1)} %get-tuple-element.20), channel_id=1, source_target_pairs={{0,96},{1,65},{2,34},{3,3},{4,116},{5,85},{6,54},{7,23},{8,232},{9... | collective-permute-start | bytes 245768 | tf_op jit(solution)/shard_map/ppermute | solution.py:46
  23.0 4.5 %collective-permute-done.1.cut_ref = bf16[320,128]{1,0:T(8,128)(2,1)S(1)} collective-permute-done((bf16[320,128]{1,0:T(8,128)(2,1)S(1)}, bf16[320,128]{1,0:T(8,128)(2,1)S(1)}, u32[]{:S(2)}, u32[]{:S(2)}) %collective-permute-start.1) | collective-permute-done | bytes 81952 | tf_op jit(solution)/shard_map/ppermute | solution.py:46
  27.5 4.8 %all-to-all-done.halves_ref = bf16[2,144,512]{2,1,0:T(8,128)(2,1)S(1)} async-done(((bf16[2,144,512]{2,1,0:T(8,128)(2,1)}), bf16[2,144,512]{2,1,0:T(8,128)(2,1)S(1)}, u32[]{:S(2)}, u32[]{:S(2)}) %all-to-all-start) | async-done | bytes 294944 | tf_op jit(solution)/shard_map/all_to_all | solution.py:50
  32.3 1.3 base.1
  33.6 10.9 %all-to-all-start.1 = ((bf16[16,320,128]{2,1,0:T(8,128)(2,1)}), bf16[16,320,128]{2,1,0:T(8,128)(2,1)S(1)}, u32[]{:S(2)}, u32[]{:S(2)}) async-start(bf16[16,320,128]{2,1,0:T(8,128)(2,1)} %get-tuple-element.27), calls=%async_computation.1 | async-start | bytes 2621440 | tf_op jit(solution)/shard_map/all_to_all | solution.py:50
  44.5 0.0 copy-start.5
  44.5 0.0 copy-start.6
  44.5 2.4 %collective-permute-start.3 = (bf16[272,512]{1,0:T(8,128)(2,1)S(1)}, bf16[272,512]{1,0:T(8,128)(2,1)S(1)}, u32[]{:S(2)}, u32[]{:S(2)}) collective-permute-start(bf16[272,512]{1,0:T(8,128)(2,1)S(1)} %get-tuple-element.21.refs_0_), channel_id=1, source_target_pairs={{0,32},{1,33},{2,34},{3,35},{4,36},{5,37},{6,38},{7,39},{8,40},{9,... | collective-permute-start | bytes 835592 | tf_op jit(solution)/shard_map/ppermute | solution.py:46
  47.0 3.5 %collective-permute-start.2 = (bf16[272,512]{1,0:T(8,128)(2,1)S(1)}, bf16[272,512]{1,0:T(8,128)(2,1)S(1)}, u32[]{:S(2)}, u32[]{:S(2)}) collective-permute-start(bf16[272,512]{1,0:T(8,128)(2,1)S(1)} %get-tuple-element.21.refs_0_), channel_id=1, source_target_pairs={{0,224},{1,225},{2,226},{3,227},{4,228},{5,229},{6,230},{7,231},{8... | collective-permute-start | bytes 835592 | tf_op jit(solution)/shard_map/ppermute | solution.py:46
  50.5 3.8 %collective-permute-done.3.refs_5_ = bf16[272,512]{1,0:T(8,128)(2,1)S(1)} collective-permute-done((bf16[272,512]{1,0:T(8,128)(2,1)S(1)}, bf16[272,512]{1,0:T(8,128)(2,1)S(1)}, u32[]{:S(2)}, u32[]{:S(2)}) %collective-permute-start.3) | collective-permute-done | bytes 278560 | tf_op jit(solution)/shard_map/ppermute | solution.py:46
  54.3 2.3 %collective-permute-done.2.refs_1_ = bf16[272,512]{1,0:T(8,128)(2,1)S(1)} collective-permute-done((bf16[272,512]{1,0:T(8,128)(2,1)S(1)}, bf16[272,512]{1,0:T(8,128)(2,1)S(1)}, u32[]{:S(2)}, u32[]{:S(2)}) %collective-permute-start.2) | collective-permute-done | bytes 278560 | tf_op jit(solution)/shard_map/ppermute | solution.py:46
  56.6 2.3 %collective-permute-start.4 = (bf16[272,512]{1,0:T(8,128)(2,1)S(1)}, bf16[272,512]{1,0:T(8,128)(2,1)S(1)}, u32[]{:S(2)}, u32[]{:S(2)}) collective-permute-start(bf16[272,512]{1,0:T(8,128)(2,1)S(1)} %collective-permute-done.2.refs_1_), channel_id=1, source_target_pairs={{0,224},{1,225},{2,226},{3,227},{4,228},{5,229},{6,230},{7,231},{8... | collective-permute-start | bytes 835592 | tf_op jit(solution)/shard_map/ppermute | solution.py:46
  58.9 4.7 %collective-permute-start.5 = (bf16[272,512]{1,0:T(8,128)(2,1)S(1)}, bf16[272,512]{1,0:T(8,128)(2,1)S(1)}, u32[]{:S(2)}, u32[]{:S(2)}) collective-permute-start(bf16[272,512]{1,0:T(8,128)(2,1)S(1)} %collective-permute-done.3.refs_5_), channel_id=1, source_target_pairs={{0,32},{1,33},{2,34},{3,35},{4,36},{5,37},{6,38},{7,39},{8,40},{9,... | collective-permute-start | bytes 835592 | tf_op jit(solution)/shard_map/ppermute | solution.py:46
  63.7 3.7 %collective-permute-done.4.refs_2_ = bf16[272,512]{1,0:T(8,128)(2,1)S(1)} collective-permute-done((bf16[272,512]{1,0:T(8,128)(2,1)S(1)}, bf16[272,512]{1,0:T(8,128)(2,1)S(1)}, u32[]{:S(2)}, u32[]{:S(2)}) %collective-permute-start.4) | collective-permute-done | bytes 278560 | tf_op jit(solution)/shard_map/ppermute | solution.py:46
  67.3 0.4 collective-permute-done.5.refs_6_
  67.7 3.9 %collective-permute-start.6 = (bf16[272,512]{1,0:T(8,128)(2,1)S(1)}, bf16[272,512]{1,0:T(8,128)(2,1)S(1)}, u32[]{:S(2)}, u32[]{:S(2)}) collective-permute-start(bf16[272,512]{1,0:T(8,128)(2,1)S(1)} %collective-permute-done.4.refs_2_), channel_id=1, source_target_pairs={{0,224},{1,225},{2,226},{3,227},{4,228},{5,229},{6,230},{7,231},{8... | collective-permute-start | bytes 835592 | tf_op jit(solution)/shard_map/ppermute | solution.py:46
  71.6 3.6 %collective-permute-start.7 = (bf16[272,512]{1,0:T(8,128)(2,1)S(1)}, bf16[272,512]{1,0:T(8,128)(2,1)S(1)}, u32[]{:S(2)}, u32[]{:S(2)}) collective-permute-start(bf16[272,512]{1,0:T(8,128)(2,1)S(1)} %collective-permute-done.5.refs_6_), channel_id=1, source_target_pairs={{0,32},{1,33},{2,34},{3,35},{4,36},{5,37},{6,38},{7,39},{8,40},{9,... | collective-permute-start | bytes 835592 | tf_op jit(solution)/shard_map/ppermute | solution.py:46
  75.2 3.7 %collective-permute-done.6.refs_3_ = bf16[272,512]{1,0:T(8,128)(2,1)S(1)} collective-permute-done((bf16[272,512]{1,0:T(8,128)(2,1)S(1)}, bf16[272,512]{1,0:T(8,128)(2,1)S(1)}, u32[]{:S(2)}, u32[]{:S(2)}) %collective-permute-start.6) | collective-permute-done | bytes 278560 | tf_op jit(solution)/shard_map/ppermute | solution.py:46
  78.9 1.1 collective-permute-done.7.refs_7_
  80.0 3.8 %collective-permute-start.8 = (bf16[272,512]{1,0:T(8,128)(2,1)S(1)}, bf16[272,512]{1,0:T(8,128)(2,1)}, u32[]{:S(2)}, u32[]{:S(2)}) collective-permute-start(bf16[272,512]{1,0:T(8,128)(2,1)S(1)} %collective-permute-done.6.refs_3_), channel_id=1, source_target_pairs={{0,224},{1,225},{2,226},{3,227},{4,228},{5,229},{6,230},{7,231},{8... | collective-permute-start | bytes 835592 | tf_op jit(solution)/shard_map/ppermute | solution.py:46
  83.9 5.9 %collective-permute-done.8.refs_4_ = bf16[272,512]{1,0:T(8,128)(2,1)} collective-permute-done((bf16[272,512]{1,0:T(8,128)(2,1)S(1)}, bf16[272,512]{1,0:T(8,128)(2,1)}, u32[]{:S(2)}, u32[]{:S(2)}) %collective-permute-start.8) | collective-permute-done | bytes 278560 | tf_op jit(solution)/shard_map/ppermute | solution.py:46
  89.8 0.0 all-to-all-done.1.refs_8_
  89.8 0.0 copy-done.20
  89.8 0.0 copy-done.21
  89.8 0.0 copy-start.18
  89.8 1.1 copy-done.18
  90.9 4.4 %gradient.1 = (f32[320,512]{1,0:T(8,128)}, f32[128,512]{1,0:T(8,128)}) custom-call(s32[5]{0:T(128)} %copy-done.11, bf16[272,512]{1,0:T(8,128)(2,1)} %copy-done.9, bf16[272,512]{1,0:T(8,128)(2,1)} %copy-done.20, bf16[272,512]{1,0:T(8,128)(2,1)} %copy-done.21, bf16[272,512]{1,0:T(8,128)(2,1)} %copy-done.23, bf16[272,512]{1,0:T(8,128)(2,1)} %collective-permute-done.8.refs_4_, ...), custom_call_target="tpu_custom_call" | custom-call | flops 671088640 | bytes 6291456 | tf_op jit(solution)/shard_map/gradient/pallas_call | solution.py:303
  95.3 1.3 collective-permute-start.9
  96.7 1.9 %collective-permute-done.9.got_ref = f32[320,512]{1,0:T(8,128)S(1)} collective-permute-done((f32[320,512]{1,0:T(8,128)}, f32[320,512]{1,0:T(8,128)S(1)}, u32[]{:S(2)}, u32[]{:S(2)}) %collective-permute-start.9) | collective-permute-done | bytes 655392 | tf_op jit(solution)/shard_map/ppermute | solution.py:46
  98.5 0.0 copy-done.5
  98.5 1.1 copy-done.7
  99.6 0.4 adam.1.update_ref
  100.1 1.3 collective-permute-start.10
  101.4 2.2 %collective-permute-done.10.update_got = bf16[320,512]{1,0:T(8,128)(2,1)S(1)} collective-permute-done((bf16[320,512]{1,0:T(8,128)(2,1)S(1)}, bf16[320,512]{1,0:T(8,128)(2,1)S(1)}, u32[]{:S(2)}, u32[]{:S(2)}) %collective-permute-start.10) | collective-permute-done | bytes 327712 | tf_op jit(solution)/shard_map/ppermute | solution.py:46
  103.6 0.0 copy-done.10
  103.6 1.5 step.1
  105.1 17.4 %all_to_all.20 = f32[16,8,320]{2,1,0:T(8,128)S(1)} all-to-all(f32[16,8,320]{2,1,0:T(8,128)S(1)} %get-tuple-element.31), channel_id=1, replica_groups=mesh['group'=2,'y'=8,'z_hi'=2,'z_lo'=4,'x'=4] {'z_lo','x'}, dimensions={0} | all-to-all | bytes 327680 | tf_op jit(solution)/shard_map/all_to_all | solution.py:50
  122.5 5.2 %collective-permute-start.11 = (bf16[8,320]{1,0:T(8,128)(2,1)S(1)}, bf16[8,320]{1,0:T(8,128)(2,1)S(1)}, u32[]{:S(2)}, u32[]{:S(2)}) collective-permute-start(bf16[8,320]{1,0:T(8,128)(2,1)S(1)} %reduce_sum.9), channel_id=1, source_target_pairs={{0,160},{1,193},{2,226},{3,3},{4,180},{5,213},{6,246},{7,23},{8,40... | collective-permute-start | bytes 15368 | tf_op jit(solution)/shard_map/ppermute | solution.py:46
  127.7 3.3 %collective-permute-done.11 = bf16[8,320]{1,0:T(8,128)(2,1)S(1)} collective-permute-done((bf16[8,320]{1,0:T(8,128)(2,1)S(1)}, bf16[8,320]{1,0:T(8,128)(2,1)S(1)}, u32[]{:S(2)}, u32[]{:S(2)}) %collective-permute-start.11) | collective-permute-done | bytes 5152 | tf_op jit(solution)/shard_map/ppermute | solution.py:46
  131.0 17.2 %all_to_all.21.blocks_ref = bf16[16,8,320]{2,1,0:T(8,128)(2,1)S(1)} all-to-all(bf16[16,8,320]{2,1,0:T(8,128)(2,1)S(1)} %broadcast_in_dim.2), channel_id=1, replica_groups=mesh['group'=2,'y'=8,'z_hi'=2,'z_lo'=4,'x'=4] {'z_lo','x'}, dimensions={0} | all-to-all | bytes 163840 | tf_op jit(solution)/shard_map/all_to_all | solution.py:50
  148.3 0.7 join.1
  148.9 0.7 reshape.12
  (28 shorter events, 0.1 us)
Async XLA Ops:
  0.7 7.0 %copy-start.11 = (s32[5]{0:T(128)}, s32[5]{0:T(128)S(1)}, u32[]{:S(2)}) copy-start(s32[5]{0:T(128)S(1)} %stack.23.place_ref) | copy-start | bytes 64
  0.7 1.7 %copy-start = (bf16[1,256,5120]{2,1,0:T(8,128)(2,1)S(1)}, bf16[1,256,5120]{2,1,0:T(8,128)(2,1)}, u32[]{:S(2)}) copy-start(bf16[1,256,5120]{2,1,0:T(8,128)(2,1)} %param.13) | copy-start | bytes 7864324
  2.5 0.9 copy-start.3
  3.4 2.3 %copy-start.1 = (bf16[2,2048,128]{2,1,0:T(8,128)(2,1)S(1)}, bf16[2,2048,128]{2,1,0:T(8,128)(2,1)}, u32[]{:S(2)}) copy-start(bf16[2,2048,128]{2,1,0:T(8,128)(2,1)} %k_ref.1) | copy-start | bytes 3145732
  3.4 2.3 %copy-start.2 = (bf16[2,2048,128]{2,1,0:T(8,128)(2,1)S(1)}, bf16[2,2048,128]{2,1,0:T(8,128)(2,1)}, u32[]{:S(2)}) copy-start(bf16[2,2048,128]{2,1,0:T(8,128)(2,1)} %v_ref.1) | copy-start | bytes 3145732
  3.4 2.3 %copy-start.13 = (bf16[4,2,1024]{2,1,0:T(2,128)(2,1)S(1)}, bf16[4,2,1024]{2,1,0:T(2,128)(2,1)}, u32[]{:S(2)}) copy-start(bf16[4,2,1024]{2,1,0:T(2,128)(2,1)} %nk_ref.1) | copy-start | bytes 49156
  3.4 2.3 %copy-start.14 = (bf16[4,2,1024]{2,1,0:T(2,128)(2,1)S(1)}, bf16[4,2,1024]{2,1,0:T(2,128)(2,1)}, u32[]{:S(2)}) copy-start(bf16[4,2,1024]{2,1,0:T(2,128)(2,1)} %nv_ref.1) | copy-start | bytes 49156
  3.4 2.3 %copy-start.15 = (bf16[4,2,512]{2,1,0:T(2,128)(2,1)S(1)}, bf16[4,2,512]{2,1,0:T(2,128)(2,1)}, u32[]{:S(2)}) copy-start(bf16[4,2,512]{2,1,0:T(2,128)(2,1)} %q_ref.1) | copy-start | bytes 24580
  3.4 2.3 %copy-start.16 = (s32[4,2]{0,1:T(2,128)S(1)}, s32[4,2]{0,1:T(2,128)}, u32[]{:S(2)}) copy-start(s32[4,2]{0,1:T(2,128)} %param.23) | copy-start | bytes 100
  3.5 2.3 %copy-start.17 = (s32[2]{0:T(128)S(1)}, s32[2]{0:T(128)}, u32[]{:S(2)}) copy-start(s32[2]{0:T(128)} %lengths_ref.1) | copy-start | bytes 28
  4.3 3.5 %copy-start.4 = (bf16[1,256,512]{2,1,0:T(8,128)(2,1)S(1)}, bf16[1,256,512]{2,1,0:T(8,128)(2,1)}, u32[]{:S(2)}) copy-start(bf16[1,256,512]{2,1,0:T(8,128)(2,1)} %param.12) | copy-start | bytes 786436
  4.3 3.5 %collective-permute-start = (bf16[208,512]{1,0:T(8,128)(2,1)S(1)}, bf16[208,512]{1,0:T(8,128)(2,1)S(1)}, u32[]{:S(2)}, u32[]{:S(2)}) collective-permute-start(bf16[208,512]{1,0:T(8,128)(2,1)S(1)} %get-tuple-element.18), channel_id=1, source_target_pairs={{256,0},{257,1},{258,2},{259,3},{260,4},{261,5},{262,6},{263,7},{2... | collective-permute-start | bytes 638984 | tf_op jit(solution)/shard_map/ppermute | solution.py:46
  9.1 23.3 %all-to-all-start = ((bf16[2,144,512]{2,1,0:T(8,128)(2,1)}), bf16[2,144,512]{2,1,0:T(8,128)(2,1)S(1)}, u32[]{:S(2)}, u32[]{:S(2)}) async-start(bf16[2,144,512]{2,1,0:T(8,128)(2,1)} %get-tuple-element.19), calls=%async_computation | async-start | bytes 589824 | tf_op jit(solution)/shard_map/all_to_all | solution.py:50
  19.4 8.2 %collective-permute-start.1 = (bf16[320,128]{1,0:T(8,128)(2,1)S(1)}, bf16[320,128]{1,0:T(8,128)(2,1)S(1)}, u32[]{:S(2)}, u32[]{:S(2)}) collective-permute-start(bf16[320,128]{1,0:T(8,128)(2,1)S(1)} %get-tuple-element.20), channel_id=1, source_target_pairs={{0,96},{1,65},{2,34},{3,3},{4,116},{5,85},{6,54},{7,23},{8,232},{9... | collective-permute-start | bytes 245768 | tf_op jit(solution)/shard_map/ppermute | solution.py:46
  33.6 13.3 %copy-start.9 = (bf16[272,512]{1,0:T(8,128)(2,1)}, bf16[272,512]{1,0:T(8,128)(2,1)S(1)}, u32[]{:S(2)}) copy-start(bf16[272,512]{1,0:T(8,128)(2,1)S(1)} %get-tuple-element.21.refs_0_) | copy-start | bytes 835588
  33.6 56.2 %all-to-all-start.1 = ((bf16[16,320,128]{2,1,0:T(8,128)(2,1)}), bf16[16,320,128]{2,1,0:T(8,128)(2,1)S(1)}, u32[]{:S(2)}, u32[]{:S(2)}) async-start(bf16[16,320,128]{2,1,0:T(8,128)(2,1)} %get-tuple-element.27), calls=%async_computation.1 | async-start | bytes 2621440 | tf_op jit(solution)/shard_map/all_to_all | solution.py:50
  44.5 54.1 %copy-start.5 = (f32[1,512,320]{1,2,0:T(8,128)S(1)}, f32[1,512,320]{1,2,0:T(8,128)}, u32[]{:S(2)}) copy-start(f32[1,512,320]{1,2,0:T(8,128)} %param.15) | copy-start | bytes 1966084
  44.5 54.0 %copy-start.6 = (f32[1,512,320]{1,2,0:T(8,128)S(1)}, f32[1,512,320]{1,2,0:T(8,128)}, u32[]{:S(2)}) copy-start(f32[1,512,320]{1,2,0:T(8,128)} %param.16) | copy-start | bytes 1966084
  44.5 9.8 %collective-permute-start.3 = (bf16[272,512]{1,0:T(8,128)(2,1)S(1)}, bf16[272,512]{1,0:T(8,128)(2,1)S(1)}, u32[]{:S(2)}, u32[]{:S(2)}) collective-permute-start(bf16[272,512]{1,0:T(8,128)(2,1)S(1)} %get-tuple-element.21.refs_0_), channel_id=1, source_target_pairs={{0,32},{1,33},{2,34},{3,35},{4,36},{5,37},{6,38},{7,39},{8,40},{9,... | collective-permute-start | bytes 835592 | tf_op jit(solution)/shard_map/ppermute | solution.py:46
  47.0 9.7 %collective-permute-start.2 = (bf16[272,512]{1,0:T(8,128)(2,1)S(1)}, bf16[272,512]{1,0:T(8,128)(2,1)S(1)}, u32[]{:S(2)}, u32[]{:S(2)}) collective-permute-start(bf16[272,512]{1,0:T(8,128)(2,1)S(1)} %get-tuple-element.21.refs_0_), channel_id=1, source_target_pairs={{0,224},{1,225},{2,226},{3,227},{4,228},{5,229},{6,230},{7,231},{8... | collective-permute-start | bytes 835592 | tf_op jit(solution)/shard_map/ppermute | solution.py:46
  54.3 35.5 %copy-start.19 = (bf16[272,512]{1,0:T(8,128)(2,1)}, bf16[272,512]{1,0:T(8,128)(2,1)S(1)}, u32[]{:S(2)}) copy-start(bf16[272,512]{1,0:T(8,128)(2,1)S(1)} %collective-permute-done.3.refs_5_) | copy-start | bytes 835588
  56.6 33.2 %copy-start.20 = (bf16[272,512]{1,0:T(8,128)(2,1)}, bf16[272,512]{1,0:T(8,128)(2,1)S(1)}, u32[]{:S(2)}) copy-start(bf16[272,512]{1,0:T(8,128)(2,1)S(1)} %collective-permute-done.2.refs_1_) | copy-start | bytes 835588
  56.6 10.7 %collective-permute-start.4 = (bf16[272,512]{1,0:T(8,128)(2,1)S(1)}, bf16[272,512]{1,0:T(8,128)(2,1)S(1)}, u32[]{:S(2)}, u32[]{:S(2)}) collective-permute-start(bf16[272,512]{1,0:T(8,128)(2,1)S(1)} %collective-permute-done.2.refs_1_), channel_id=1, source_target_pairs={{0,224},{1,225},{2,226},{3,227},{4,228},{5,229},{6,230},{7,231},{8... | collective-permute-start | bytes 835592 | tf_op jit(solution)/shard_map/ppermute | solution.py:46
  58.9 8.8 %collective-permute-start.5 = (bf16[272,512]{1,0:T(8,128)(2,1)S(1)}, bf16[272,512]{1,0:T(8,128)(2,1)S(1)}, u32[]{:S(2)}, u32[]{:S(2)}) collective-permute-start(bf16[272,512]{1,0:T(8,128)(2,1)S(1)} %collective-permute-done.3.refs_5_), channel_id=1, source_target_pairs={{0,32},{1,33},{2,34},{3,35},{4,36},{5,37},{6,38},{7,39},{8,40},{9,... | collective-permute-start | bytes 835592 | tf_op jit(solution)/shard_map/ppermute | solution.py:46
  67.3 22.5 %copy-start.21 = (bf16[272,512]{1,0:T(8,128)(2,1)}, bf16[272,512]{1,0:T(8,128)(2,1)S(1)}, u32[]{:S(2)}) copy-start(bf16[272,512]{1,0:T(8,128)(2,1)S(1)} %collective-permute-done.4.refs_2_) | copy-start | bytes 835588
  67.7 16.2 %copy-start.22 = (bf16[272,512]{1,0:T(8,128)(2,1)}, bf16[272,512]{1,0:T(8,128)(2,1)S(1)}, u32[]{:S(2)}) copy-start(bf16[272,512]{1,0:T(8,128)(2,1)S(1)} %collective-permute-done.5.refs_6_) | copy-start | bytes 835588
  67.7 11.2 %collective-permute-start.6 = (bf16[272,512]{1,0:T(8,128)(2,1)S(1)}, bf16[272,512]{1,0:T(8,128)(2,1)S(1)}, u32[]{:S(2)}, u32[]{:S(2)}) collective-permute-start(bf16[272,512]{1,0:T(8,128)(2,1)S(1)} %collective-permute-done.4.refs_2_), channel_id=1, source_target_pairs={{0,224},{1,225},{2,226},{3,227},{4,228},{5,229},{6,230},{7,231},{8... | collective-permute-start | bytes 835592 | tf_op jit(solution)/shard_map/ppermute | solution.py:46
  71.6 8.4 %collective-permute-start.7 = (bf16[272,512]{1,0:T(8,128)(2,1)S(1)}, bf16[272,512]{1,0:T(8,128)(2,1)S(1)}, u32[]{:S(2)}, u32[]{:S(2)}) collective-permute-start(bf16[272,512]{1,0:T(8,128)(2,1)S(1)} %collective-permute-done.5.refs_6_), channel_id=1, source_target_pairs={{0,32},{1,33},{2,34},{3,35},{4,36},{5,37},{6,38},{7,39},{8,40},{9,... | collective-permute-start | bytes 835592 | tf_op jit(solution)/shard_map/ppermute | solution.py:46
  78.9 5.0 %copy-start.23 = (bf16[272,512]{1,0:T(8,128)(2,1)}, bf16[272,512]{1,0:T(8,128)(2,1)S(1)}, u32[]{:S(2)}) copy-start(bf16[272,512]{1,0:T(8,128)(2,1)S(1)} %collective-permute-done.6.refs_3_) | copy-start | bytes 835588
  80.0 3.8 %copy-start.24 = (bf16[272,512]{1,0:T(8,128)(2,1)}, bf16[272,512]{1,0:T(8,128)(2,1)S(1)}, u32[]{:S(2)}) copy-start(bf16[272,512]{1,0:T(8,128)(2,1)S(1)} %collective-permute-done.7.refs_7_) | copy-start | bytes 835588
  80.0 9.7 %collective-permute-start.8 = (bf16[272,512]{1,0:T(8,128)(2,1)S(1)}, bf16[272,512]{1,0:T(8,128)(2,1)}, u32[]{:S(2)}, u32[]{:S(2)}) collective-permute-start(bf16[272,512]{1,0:T(8,128)(2,1)S(1)} %collective-permute-done.6.refs_3_), channel_id=1, source_target_pairs={{0,224},{1,225},{2,226},{3,227},{4,228},{5,229},{6,230},{7,231},{8... | collective-permute-start | bytes 835592 | tf_op jit(solution)/shard_map/ppermute | solution.py:46
  89.8 1.1 copy-start.18
  95.3 3.2 %collective-permute-start.9 = (f32[320,512]{1,0:T(8,128)}, f32[320,512]{1,0:T(8,128)S(1)}, u32[]{:S(2)}, u32[]{:S(2)}) collective-permute-start(f32[320,512]{1,0:T(8,128)} %get-tuple-element.28.mine_ref), channel_id=1, source_target_pairs={{0,256},{1,257},{2,258},{3,259},{4,260},{5,261},{6,262},{7,263},{8... | collective-permute-start | bytes 1966088 | tf_op jit(solution)/shard_map/ppermute | solution.py:46
  98.5 1.1 copy-start.7
  99.6 4.0 %copy-start.8 = (bf16[512,320]{0,1:T(8,128)(2,1)S(1)}, bf16[512,320]{0,1:T(8,128)(2,1)}, u32[]{:S(2)}) copy-start(bf16[512,320]{0,1:T(8,128)(2,1)} %param.14) | copy-start | bytes 983044
  99.6 4.0 %copy-start.10 = (f32[128,512]{1,0:T(8,128)S(1)}, f32[128,512]{1,0:T(8,128)}, u32[]{:S(2)}) copy-start(f32[128,512]{1,0:T(8,128)} %get-tuple-element.29.rows_ref) | copy-start | bytes 786436
  99.6 4.0 %copy-start.12 = (s32[5]{0:T(128)S(1)}, s32[5]{0:T(128)}, u32[]{:S(2)}) copy-start(s32[5]{0:T(128)} %copy-done.11) | copy-start | bytes 64
  100.1 3.5 %collective-permute-start.10 = (bf16[320,512]{1,0:T(8,128)(2,1)S(1)}, bf16[320,512]{1,0:T(8,128)(2,1)S(1)}, u32[]{:S(2)}, u32[]{:S(2)}) collective-permute-start(bf16[320,512]{1,0:T(8,128)(2,1)S(1)} %adam.1.update_ref), channel_id=1, source_target_pairs={{256,0},{257,1},{258,2},{259,3},{260,4},{261,5},{262,6},{263,7},{2... | collective-permute-start | bytes 983048 | tf_op jit(solution)/shard_map/ppermute | solution.py:46
  122.5 8.5 %collective-permute-start.11 = (bf16[8,320]{1,0:T(8,128)(2,1)S(1)}, bf16[8,320]{1,0:T(8,128)(2,1)S(1)}, u32[]{:S(2)}, u32[]{:S(2)}) collective-permute-start(bf16[8,320]{1,0:T(8,128)(2,1)S(1)} %reduce_sum.9), channel_id=1, source_target_pairs={{0,160},{1,193},{2,226},{3,3},{4,180},{5,213},{6,246},{7,23},{8,40... | collective-permute-start | bytes 15368 | tf_op jit(solution)/shard_map/ppermute | solution.py:46

commit v14 on v13

--- a/solution.py
+++ b/solution.py
@@ -50,6 +50,10 @@
     return lax.all_to_all(value, axes, split_axis=0, concat_axis=0, tiled=True)
 
 
+def to_partner(g, y, zh, zl, x):
+    return (g, y, 1 - zh, zl, x)
+
+
 def along_y(step):
     return lambda g, y, zh, zl, x: (g, (y + (step if g == 1 else -step)) % 8, zh, zl, x)
 
@@ -78,10 +82,11 @@
 
 
 SMALL = pltpu.CompilerParams(vmem_limit_bytes=6 * 2**20)
+LONG = pl.CostEstimate(flops=0, bytes_accessed=2**26, transcendentals=0)
 
 
 def attend_kernel(
-    head_ref, lengths_ref, ids_ref, q_ref, k_ref, v_ref, nk_ref, nv_ref, out_ref, q_rows, nk_rows, nv_rows
+    head_ref, lengths_ref, ids_ref, q_ref, k_ref, v_ref, nk_ref, nv_ref, _, out_ref, q_rows, nk_rows, nv_rows
 ):
     for t in range(STEPS):
         place = slice(2 * t, 2 * t + 2)
@@ -138,7 +143,7 @@
     out_ref[...] = jnp.concatenate([flat, jnp.zeros_like(flat)], axis=0).astype(bf16)
 
 
-def attend(head, queries, cache_keys, cache_values, new_keys, new_values, lengths, ids):
+def attend(head, queries, cache_keys, cache_values, new_keys, new_values, lengths, ids, after):
     whole = lambda *shape: pl.BlockSpec(shape, lambda i, *_: (0,) * len(shape))
     cache = pl.BlockSpec((2, CACHE, HD), lambda i, m, *_: (0, m[0], 0))
     fresh = pl.BlockSpec((STEPS, 2, HD), lambda i, m, *_: (0, 0, m[0]))
@@ -148,7 +153,7 @@
         grid_spec=pltpu.PrefetchScalarGridSpec(
             num_scalar_prefetch=3,
             grid=(1,),
-            in_specs=[whole(STEPS, 2, FEAT), cache, cache, fresh, fresh],
+            in_specs=[whole(STEPS, 2, FEAT), cache, cache, fresh, fresh, pl.BlockSpec(memory_space=pl.ANY)],
             out_specs=whole(PAD, FEAT),
             scratch_shapes=[
                 pltpu.VMEM((ROWS, FEAT), f32),
@@ -158,7 +163,7 @@
         ),
         compiler_params=SMALL,
         name="attend",
-    )(head, lengths, ids, queries, cache_keys, cache_values, new_keys, new_values)
+    )(head, lengths, ids, queries, cache_keys, cache_values, new_keys, new_values, after)
 
 
 VMEM = pl.BlockSpec(memory_space=pltpu.VMEM)
@@ -196,62 +201,92 @@
             pltpu.VMEM((384, TOK), f32),
             pltpu.SemaphoreType.DMA(()),
         ],
-        compiler_params=SMALL,
+        compiler_params=pltpu.CompilerParams(vmem_limit_bytes=60 * 2**20),
         name="cut",
     )(place, cot, act)
 
 
-def half_kernel(place_ref, act_ref, one_ref, pack_ref, rows_ref, cut_ref, out_ref):
+def unpack_kernel(place_ref, one_ref, pack_ref, out_ref):
     @pl.when(place_ref[0] == 1)
     def _():
-        out_ref[0, :HALF, :] = act_ref[:HALF, :]
-        cut_ref[...] = one_ref[...]
+        out_ref[...] = one_ref[...]
 
     @pl.when(place_ref[0] == 0)
     def _():
-        out_ref[0, :HALF, :] = pack_ref[:HALF, :]
         for n in range(4):
-            cut_ref[n * PART : (n + 1) * PART, :] = pack_ref[HALF:, n * HALF : (n + 1) * HALF]
-
-    out_ref[0, HALF:, :] = rows_ref[...]
-    out_ref[1] = out_ref[0]
+            out_ref[n * PART : (n + 1) * PART, :] = pack_ref[HALF:, n * HALF : (n + 1) * HALF]
+
+
+def unpack(place, *parts):
+    return pl.pallas_call(
+        unpack_kernel,
+        out_shape=jax.ShapeDtypeStruct((COLS, HALF), bf16),
+        in_specs=[SMEM] + [VMEM] * 2,
+        out_specs=VMEM,
+        compiler_params=SMALL,
+        name="unpack",
+    )(place, *parts)
+
+
+def half_kernel(place_ref, act_ref, pack_ref, rows_ref, _, out_ref):
+    @pl.when(place_ref[0] == 1)
+    def _():
+        out_ref[:HALF, :] = act_ref[:HALF, :]
+
+    @pl.when(place_ref[0] == 0)
+    def _():
+        out_ref[:HALF, :] = pack_ref[:HALF, :]
+
+    out_ref[HALF:, :] = rows_ref[...]
 
 
 def half_of(place, *parts):
     return pl.pallas_call(
         half_kernel,
-        out_shape=(
-            jax.ShapeDtypeStruct((COLS, HALF), bf16),
-            jax.ShapeDtypeStruct((2, HALF + PAD, FEAT), bf16),
-        ),
-        in_specs=[SMEM] + [VMEM] * 4,
-        out_specs=(VMEM, VMEM),
+        out_shape=jax.ShapeDtypeStruct((HALF + PAD, FEAT), bf16),
+        in_specs=[SMEM] + [VMEM] * 3 + [HBM],
+        out_specs=VMEM,
         compiler_params=SMALL,
+        cost_estimate=LONG,
         name="half",
     )(place, *parts)
 
 
-def base_kernel(halves_ref, cut_ref, out_ref, spread_ref):
-    for z_hi in range(2):
-        out_ref[z_hi * HALF : (z_hi + 1) * HALF, :] = halves_ref[z_hi, :HALF, :]
-    rows = [halves_ref[z_hi, HALF:, :].astype(f32)[:ROWS] for z_hi in range(2)]
+def spread_kernel(cut_ref, _, out_ref):
+    for n in range(16):
+        out_ref[n] = cut_ref[...]
+
+
+def spread_of(*operands):
+    return pl.pallas_call(
+        spread_kernel,
+        out_shape=jax.ShapeDtypeStruct((16, COLS, HALF), bf16),
+        in_specs=[VMEM, HBM],
+        out_specs=VMEM,
+        compiler_params=SMALL,
+        cost_estimate=LONG,
+        name="spread",
+    )(*operands)
+
+
+def base_kernel(place_ref, mine_ref, got_ref, _, out_ref):
+    z_hi = place_ref[2]
+    for ref, side in ((mine_ref, z_hi), (got_ref, 1 - z_hi)):
+        out_ref[pl.ds(pl.multiple_of(side * HALF, HALF), HALF), :] = ref[:HALF, :]
+    mine, got = (ref[HALF:, :].astype(f32)[:ROWS] for ref in (mine_ref, got_ref))
+    rows = [jnp.where(z_hi == 0, mine, got), jnp.where(z_hi == 0, got, mine)]
     out_ref[TOK:, :] = jnp.concatenate(rows, axis=0).astype(bf16)
-    for n in range(16):
-        spread_ref[n] = cut_ref[...]
-
-
-def base_of(*operands):
+
+
+def base_of(place, *operands):
     return pl.pallas_call(
         base_kernel,
-        out_shape=(
-            jax.ShapeDtypeStruct((TOK + PAD, FEAT), bf16),
-            jax.ShapeDtypeStruct((16, COLS, HALF), bf16),
-        ),
-        in_specs=[VMEM] * 2,
-        out_specs=(VMEM, VMEM),
+        out_shape=jax.ShapeDtypeStruct((TOK + PAD, FEAT), bf16),
+        in_specs=[SMEM] + [VMEM] * 2 + [HBM],
+        out_specs=VMEM,
         compiler_params=SMALL,
         name="base",
-    )(*operands)
+    )(place, *operands)
 
 
 def gradient_kernel(place_ref, *refs):
@@ -419,6 +454,8 @@
     act = activations[0]
     cut_one, pack = cut_of(place, cotangent[0], act)
     pack_got = permute(pack, to_rollout)
+    cut = unpack(place, cut_one, pack_got)
+    own = permute(cut, cot_shifted)
     rows = attend(
         (q >> 1).reshape(1),
         queries,
@@ -428,11 +465,13 @@
         new_values,
         lengths,
         token_ids.T,
+        cut,
     )
-    cut, halves = half_of(place, act, cut_one, pack_got, rows)
-    own = permute(cut, cot_shifted)
-    base, own_spread = base_of(gather(halves, "z_hi"), own)
+    half = half_of(place, act, pack_got, rows, own)
+    half_got = permute(half, to_partner)
+    own_spread = spread_of(own, half)
     blocks = gather(own_spread, TENSOR)
+    base = base_of(place, half, half_got, own_spread)
     ahead = back = base
     first, second = [], []
     for _ in range(3):

time: 151 us -> 178 us (1.18)
  waiting for transfers between devices: 38.5 us -> 61.7 us
  starting transfers between devices: 58.4 us -> 62.5 us
  Pallas kernels: 11.4 us -> 13.9 us
  local copies, waits for them, and re-layouts: 5.73 us -> 3.41 us
    ppermute x12 -> x13, waiting for transfers between devices: 33.7 us -> 61.7 us  [permute(): return lax.ppermute(value, AXES, pairs)]
    ppermute x12 -> x13, starting transfers between devices: 37.3 us -> 44 us  [permute(): return lax.ppermute(value, AXES, pairs)]
    all_to_all x2 -> x1, waiting for transfers between devices: 4.8 us -> 0.01 us  [gather(): return lax.all_to_all(value, axes, split_axis=0, concat_axis=0, tiled=True)]
    unnamed x50 -> x46, local copies, waits for them, and re-layouts: 4.97 us -> 2.07 us
    all_to_all x2 -> x1, starting transfers between devices: 21.1 us -> 18.5 us  [gather(): return lax.all_to_all(value, axes, split_axis=0, concat_axis=0, tiled=True)]
    pallas_call x1, Pallas kernels: 0.78 us -> 2.91 us  [cut_of(): pl.pallas_call(cut_kernel, out_shape=(jax.ShapeDtypeStruct((COLS, HALF),...]
where the time goes in v14:
time: 178 us; the launch traced here: 177 us
  starting transfers between devices  62.5 us (35%)
  waiting for transfers between devices  61.7 us (35%)
  blocking collectives  34.1 us (19%)
  Pallas kernels  13.9 us (8%)
  local copies, waits for them, and re-layouts  3.41 us (2%)
    ppermute x13, waiting for transfers between devices, permute(): return lax.ppermute(value, AXES, pairs)  61.7 us
    ppermute x13, starting transfers between devices, permute(): return lax.ppermute(value, AXES, pairs)  44 us
    all_to_all x2, blocking collectives, gather(): return lax.all_to_all(value, axes, split_axis=0, concat_axis=0, tiled=True)  34.1 us
    all_to_all x1, starting transfers between devices, gather(): return lax.all_to_all(value, axes, split_axis=0, concat_axis=0, tiled=True)  18.5 us
    pallas_call x1, Pallas kernels, gradient(): pl.pallas_call(gradient_kernel, out_shape=(jax.ShapeDtypeStruct((COLS, FE...  4.4 us
  transfers between devices with their start and end apart: 14, of which 13 were waited for; matrix products, arithmetic and copies ran while one was open for 0% of the time, Pallas kernels for 1%

profile of v14, /device:TPU:56, one launch (start us, length us, event | category | flops | bytes accessed | tf_op | source)
XLA Modules:
  0.0 176.6 jit_solution(14263938992208655580)
XLA Ops:
  0.6 0.7 stack.23.place_ref
  1.3 0.0 copy-start.13
  1.3 0.0 copy-start.14
  1.3 0.0 copy-start.15
  1.3 0.0 copy-start.16
  1.4 2.9 %cut.1 = (bf16[320,128]{1,0:T(8,128)(2,1)}, bf16[208,512]{1,0:T(8,128)(2,1)}) custom-call(s32[5]{0:T(128)} %stack.23.place_ref, bf16[256,5120]{1,0:T(8,128)(2,1)} %bitcast.23, bf16[256,512]{1,0:T(8,128)(2,1)} %bitcast.17), custom_call_target="tpu_custom_call" | custom-call | tf_op jit(solution)/shard_map/cut/pallas_call | solution.py:191
  4.3 1.3 collective-permute-start
  5.6 2.3 %collective-permute-done.pack_ref = bf16[208,512]{1,0:T(8,128)(2,1)S(1)} collective-permute-done((bf16[208,512]{1,0:T(8,128)(2,1)}, bf16[208,512]{1,0:T(8,128)(2,1)S(1)}, u32[]{:S(2)}, u32[]{:S(2)}) %collective-permute-start) | collective-permute-done | bytes 213024 | tf_op jit(solution)/shard_map/ppermute | solution.py:46
  7.8 0.0 copy-done.10
  7.8 0.9 copy-done.9
  8.7 0.6 unpack.1._
  9.3 3.7 %collective-permute-start.1 = (bf16[320,128]{1,0:T(8,128)(2,1)S(1)}, bf16[320,128]{1,0:T(8,128)(2,1)S(1)}, u32[]{:S(2)}, u32[]{:S(2)}) collective-permute-start(bf16[320,128]{1,0:T(8,128)(2,1)S(1)} %unpack.1._), channel_id=1, source_target_pairs={{0,96},{1,65},{2,34},{3,3},{4,116},{5,85},{6,54},{7,23},{8,232},{9... | collective-permute-start | bytes 245768 | tf_op jit(solution)/shard_map/ppermute | solution.py:46
  13.0 0.0 copy-done.1
  13.0 0.0 copy-done.2
  13.0 0.0 copy-done.12
  13.1 0.0 copy-done.13
  13.1 0.0 copy-done.14
  13.1 0.0 copy-done.15
  13.1 0.0 copy-done.16
  13.1 1.1 attend.1.rows_ref
  14.1 3.4 %collective-permute-done.1._.cut_ref = bf16[320,128]{1,0:T(8,128)(2,1)S(1)} collective-permute-done((bf16[320,128]{1,0:T(8,128)(2,1)S(1)}, bf16[320,128]{1,0:T(8,128)(2,1)S(1)}, u32[]{:S(2)}, u32[]{:S(2)}) %collective-permute-start.1) | collective-permute-done | bytes 81952 | tf_op jit(solution)/shard_map/ppermute | solution.py:46
  17.6 0.0 copy-done.3
  17.6 0.6 half.1._.mine_ref
  18.2 1.3 spread.1._
  19.4 18.5 %all-to-all-start = ((bf16[16,320,128]{2,1,0:T(8,128)(2,1)}), bf16[16,320,128]{2,1,0:T(8,128)(2,1)}, u32[]{:S(2)}, u32[]{:S(2)}) async-start(bf16[16,320,128]{2,1,0:T(8,128)(2,1)} %spread.1._), calls=%async_computation | async-start | bytes 2621440 | tf_op jit(solution)/shard_map/all_to_all | solution.py:50
  37.9 7.9 %collective-permute-start.2 = (bf16[144,512]{1,0:T(8,128)(2,1)S(1)}, bf16[144,512]{1,0:T(8,128)(2,1)S(1)}, u32[]{:S(2)}, u32[]{:S(2)}) collective-permute-start(bf16[144,512]{1,0:T(8,128)(2,1)S(1)} %half.1._.mine_ref), channel_id=1, source_target_pairs={{0,16},{1,17},{2,18},{3,19},{4,20},{5,21},{6,22},{7,23},{8,24},{9,... | collective-permute-start | bytes 442376 | tf_op jit(solution)/shard_map/ppermute | solution.py:46
  45.8 25.9 %collective-permute-done.2.got_ref = bf16[144,512]{1,0:T(8,128)(2,1)S(1)} collective-permute-done((bf16[144,512]{1,0:T(8,128)(2,1)S(1)}, bf16[144,512]{1,0:T(8,128)(2,1)S(1)}, u32[]{:S(2)}, u32[]{:S(2)}) %collective-permute-start.2) | collective-permute-done | bytes 147488 | tf_op jit(solution)/shard_map/ppermute | solution.py:46
  71.8 0.6 base.1.refs_0_
  72.3 0.0 copy-start
  72.4 0.0 copy-start.4
  72.4 0.0 copy-start.5
  72.4 2.1 %collective-permute-start.4 = (bf16[272,512]{1,0:T(8,128)(2,1)S(1)}, bf16[272,512]{1,0:T(8,128)(2,1)S(1)}, u32[]{:S(2)}, u32[]{:S(2)}) collective-permute-start(bf16[272,512]{1,0:T(8,128)(2,1)S(1)} %base.1.refs_0_), channel_id=1, source_target_pairs={{0,32},{1,33},{2,34},{3,35},{4,36},{5,37},{6,38},{7,39},{8,40},{9,... | collective-permute-start | bytes 835592 | tf_op jit(solution)/shard_map/ppermute | solution.py:46
  74.4 3.9 %collective-permute-start.3 = (bf16[272,512]{1,0:T(8,128)(2,1)S(1)}, bf16[272,512]{1,0:T(8,128)(2,1)S(1)}, u32[]{:S(2)}, u32[]{:S(2)}) collective-permute-start(bf16[272,512]{1,0:T(8,128)(2,1)S(1)} %base.1.refs_0_), channel_id=1, source_target_pairs={{0,224},{1,225},{2,226},{3,227},{4,228},{5,229},{6,230},{7,231},{8... | collective-permute-start | bytes 835592 | tf_op jit(solution)/shard_map/ppermute | solution.py:46
  78.4 3.6 %collective-permute-done.4.refs_5_ = bf16[272,512]{1,0:T(8,128)(2,1)S(1)} collective-permute-done((bf16[272,512]{1,0:T(8,128)(2,1)S(1)}, bf16[272,512]{1,0:T(8,128)(2,1)S(1)}, u32[]{:S(2)}, u32[]{:S(2)}) %collective-permute-start.4) | collective-permute-done | bytes 278560 | tf_op jit(solution)/shard_map/ppermute | solution.py:46
  81.9 2.2 %collective-permute-done.3.refs_1_ = bf16[272,512]{1,0:T(8,128)(2,1)S(1)} collective-permute-done((bf16[272,512]{1,0:T(8,128)(2,1)S(1)}, bf16[272,512]{1,0:T(8,128)(2,1)S(1)}, u32[]{:S(2)}, u32[]{:S(2)}) %collective-permute-start.3) | collective-permute-done | bytes 278560 | tf_op jit(solution)/shard_map/ppermute | solution.py:46
  84.1 2.7 %collective-permute-start.5 = (bf16[272,512]{1,0:T(8,128)(2,1)S(1)}, bf16[272,512]{1,0:T(8,128)(2,1)S(1)}, u32[]{:S(2)}, u32[]{:S(2)}) collective-permute-start(bf16[272,512]{1,0:T(8,128)(2,1)S(1)} %collective-permute-done.3.refs_1_), channel_id=1, source_target_pairs={{0,224},{1,225},{2,226},{3,227},{4,228},{5,229},{6,230},{7,231},{8... | collective-permute-start | bytes 835592 | tf_op jit(solution)/shard_map/ppermute | solution.py:46
  86.8 4.3 %collective-permute-start.6 = (bf16[272,512]{1,0:T(8,128)(2,1)S(1)}, bf16[272,512]{1,0:T(8,128)(2,1)S(1)}, u32[]{:S(2)}, u32[]{:S(2)}) collective-permute-start(bf16[272,512]{1,0:T(8,128)(2,1)S(1)} %collective-permute-done.4.refs_5_), channel_id=1, source_target_pairs={{0,32},{1,33},{2,34},{3,35},{4,36},{5,37},{6,38},{7,39},{8,40},{9,... | collective-permute-start | bytes 835592 | tf_op jit(solution)/shard_map/ppermute | solution.py:46
  91.1 3.9 %collective-permute-done.5.refs_2_ = bf16[272,512]{1,0:T(8,128)(2,1)S(1)} collective-permute-done((bf16[272,512]{1,0:T(8,128)(2,1)S(1)}, bf16[272,512]{1,0:T(8,128)(2,1)S(1)}, u32[]{:S(2)}, u32[]{:S(2)}) %collective-permute-start.5) | collective-permute-done | bytes 278560 | tf_op jit(solution)/shard_map/ppermute | solution.py:46
  95.1 1.2 collective-permute-done.6.refs_6_
  96.2 3.9 %collective-permute-start.7 = (bf16[272,512]{1,0:T(8,128)(2,1)S(1)}, bf16[272,512]{1,0:T(8,128)(2,1)S(1)}, u32[]{:S(2)}, u32[]{:S(2)}) collective-permute-start(bf16[272,512]{1,0:T(8,128)(2,1)S(1)} %collective-permute-done.5.refs_2_), channel_id=1, source_target_pairs={{0,224},{1,225},{2,226},{3,227},{4,228},{5,229},{6,230},{7,231},{8... | collective-permute-start | bytes 835592 | tf_op jit(solution)/shard_map/ppermute | solution.py:46
  100.2 3.1 %collective-permute-start.8 = (bf16[272,512]{1,0:T(8,128)(2,1)S(1)}, bf16[272,512]{1,0:T(8,128)(2,1)S(1)}, u32[]{:S(2)}, u32[]{:S(2)}) collective-permute-start(bf16[272,512]{1,0:T(8,128)(2,1)S(1)} %collective-permute-done.6.refs_6_), channel_id=1, source_target_pairs={{0,32},{1,33},{2,34},{3,35},{4,36},{5,37},{6,38},{7,39},{8,40},{9,... | collective-permute-start | bytes 835592 | tf_op jit(solution)/shard_map/ppermute | solution.py:46
  103.3 4.3 %collective-permute-done.7.refs_3_ = bf16[272,512]{1,0:T(8,128)(2,1)S(1)} collective-permute-done((bf16[272,512]{1,0:T(8,128)(2,1)S(1)}, bf16[272,512]{1,0:T(8,128)(2,1)S(1)}, u32[]{:S(2)}, u32[]{:S(2)}) %collective-permute-start.7) | collective-permute-done | bytes 278560 | tf_op jit(solution)/shard_map/ppermute | solution.py:46
  107.6 1.0 collective-permute-done.8.refs_7_
  108.6 3.3 %collective-permute-start.9 = (bf16[272,512]{1,0:T(8,128)(2,1)S(1)}, bf16[272,512]{1,0:T(8,128)(2,1)}, u32[]{:S(2)}, u32[]{:S(2)}) collective-permute-start(bf16[272,512]{1,0:T(8,128)(2,1)S(1)} %collective-permute-done.7.refs_3_), channel_id=1, source_target_pairs={{0,224},{1,225},{2,226},{3,227},{4,228},{5,229},{6,230},{7,231},{8... | collective-permute-start | bytes 835592 | tf_op jit(solution)/shard_map/ppermute | solution.py:46
  111.9 6.4 %collective-permute-done.9.refs_4_ = bf16[272,512]{1,0:T(8,128)(2,1)} collective-permute-done((bf16[272,512]{1,0:T(8,128)(2,1)S(1)}, bf16[272,512]{1,0:T(8,128)(2,1)}, u32[]{:S(2)}, u32[]{:S(2)}) %collective-permute-start.9) | collective-permute-done | bytes 278560 | tf_op jit(solution)/shard_map/ppermute | solution.py:46
  118.4 0.0 all-to-all-done.refs_8_
  118.4 0.0 copy-done
  118.4 0.0 copy-done.17
  118.4 0.0 copy-done.18
  118.4 4.4 %gradient.1 = (f32[320,512]{1,0:T(8,128)}, f32[128,512]{1,0:T(8,128)}) custom-call(s32[5]{0:T(128)} %stack.23.place_ref, bf16[272,512]{1,0:T(8,128)(2,1)} %copy-done, bf16[272,512]{1,0:T(8,128)(2,1)} %copy-done.18, bf16[272,512]{1,0:T(8,128)(2,1)} %copy-done.19, bf16[272,512]{1,0:T(8,128)(2,1)} %copy-done.21, ...), custom_call_target="tpu_custom_call" | custom-call | flops 671088640 | bytes 6291456 | tf_op jit(solution)/shard_map/gradient/pallas_call | solution.py:338
  122.8 1.3 collective-permute-start.10
  124.2 1.9 %collective-permute-done.10.got_ref = f32[320,512]{1,0:T(8,128)S(1)} collective-permute-done((f32[320,512]{1,0:T(8,128)}, f32[320,512]{1,0:T(8,128)S(1)}, u32[]{:S(2)}, u32[]{:S(2)}) %collective-permute-start.10) | collective-permute-done | bytes 655392 | tf_op jit(solution)/shard_map/ppermute | solution.py:46
  126.0 1.1 copy-done.6
  127.1 0.4 adam.1.update_ref
  127.6 1.3 collective-permute-start.11
  128.9 2.2 %collective-permute-done.11.update_got = bf16[320,512]{1,0:T(8,128)(2,1)S(1)} collective-permute-done((bf16[320,512]{1,0:T(8,128)(2,1)S(1)}, bf16[320,512]{1,0:T(8,128)(2,1)S(1)}, u32[]{:S(2)}, u32[]{:S(2)}) %collective-permute-start.11) | collective-permute-done | bytes 327712 | tf_op jit(solution)/shard_map/ppermute | solution.py:46
  131.1 0.0 copy-done.7
  131.1 1.5 step.1
  132.6 16.9 %all_to_all.15 = f32[16,8,320]{2,1,0:T(8,128)S(1)} all-to-all(f32[16,8,320]{2,1,0:T(8,128)S(1)} %get-tuple-element.23), channel_id=1, replica_groups=mesh['group'=2,'y'=8,'z_hi'=2,'z_lo'=4,'x'=4] {'z_lo','x'}, dimensions={0} | all-to-all | bytes 327680 | tf_op jit(solution)/shard_map/all_to_all | solution.py:50
  149.5 5.1 %collective-permute-start.12 = (bf16[8,320]{1,0:T(8,128)(2,1)S(1)}, bf16[8,320]{1,0:T(8,128)(2,1)S(1)}, u32[]{:S(2)}, u32[]{:S(2)}) collective-permute-start(bf16[8,320]{1,0:T(8,128)(2,1)S(1)} %reduce_sum.9), channel_id=1, source_target_pairs={{0,160},{1,193},{2,226},{3,3},{4,180},{5,213},{6,246},{7,23},{8,40... | collective-permute-start | bytes 15368 | tf_op jit(solution)/shard_map/ppermute | solution.py:46
  154.6 3.4 %collective-permute-done.12 = bf16[8,320]{1,0:T(8,128)(2,1)S(1)} collective-permute-done((bf16[8,320]{1,0:T(8,128)(2,1)S(1)}, bf16[8,320]{1,0:T(8,128)(2,1)S(1)}, u32[]{:S(2)}, u32[]{:S(2)}) %collective-permute-start.12) | collective-permute-done | bytes 5152 | tf_op jit(solution)/shard_map/ppermute | solution.py:46
  158.0 17.2 %all_to_all.16.blocks_ref = bf16[16,8,320]{2,1,0:T(8,128)(2,1)S(1)} all-to-all(bf16[16,8,320]{2,1,0:T(8,128)(2,1)S(1)} %broadcast_in_dim.2), channel_id=1, replica_groups=mesh['group'=2,'y'=8,'z_hi'=2,'z_lo'=4,'x'=4] {'z_lo','x'}, dimensions={0} | all-to-all | bytes 163840 | tf_op jit(solution)/shard_map/all_to_all | solution.py:50
  175.3 0.7 join.1
  175.9 0.7 reshape.12
  (26 shorter events, 0.1 us)
Async XLA Ops:
  1.3 6.6 %copy-start.10 = (s32[5]{0:T(128)S(1)}, s32[5]{0:T(128)}, u32[]{:S(2)}) copy-start(s32[5]{0:T(128)} %stack.23.place_ref) | copy-start | bytes 64
  1.3 11.7 %copy-start.1 = (bf16[2,2048,128]{2,1,0:T(8,128)(2,1)S(1)}, bf16[2,2048,128]{2,1,0:T(8,128)(2,1)}, u32[]{:S(2)}) copy-start(bf16[2,2048,128]{2,1,0:T(8,128)(2,1)} %k_ref.1) | copy-start | bytes 3145732
  1.3 11.7 %copy-start.2 = (bf16[2,2048,128]{2,1,0:T(8,128)(2,1)S(1)}, bf16[2,2048,128]{2,1,0:T(8,128)(2,1)}, u32[]{:S(2)}) copy-start(bf16[2,2048,128]{2,1,0:T(8,128)(2,1)} %v_ref.1) | copy-start | bytes 3145732
  1.3 11.7 %copy-start.12 = (bf16[4,2,1024]{2,1,0:T(2,128)(2,1)S(1)}, bf16[4,2,1024]{2,1,0:T(2,128)(2,1)}, u32[]{:S(2)}) copy-start(bf16[4,2,1024]{2,1,0:T(2,128)(2,1)} %nk_ref.1) | copy-start | bytes 49156
  1.3 11.8 %copy-start.13 = (bf16[4,2,1024]{2,1,0:T(2,128)(2,1)S(1)}, bf16[4,2,1024]{2,1,0:T(2,128)(2,1)}, u32[]{:S(2)}) copy-start(bf16[4,2,1024]{2,1,0:T(2,128)(2,1)} %nv_ref.1) | copy-start | bytes 49156
  1.3 11.8 %copy-start.14 = (bf16[4,2,512]{2,1,0:T(2,128)(2,1)S(1)}, bf16[4,2,512]{2,1,0:T(2,128)(2,1)}, u32[]{:S(2)}) copy-start(bf16[4,2,512]{2,1,0:T(2,128)(2,1)} %q_ref.1) | copy-start | bytes 24580
  1.3 11.8 %copy-start.15 = (s32[4,2]{0,1:T(2,128)S(1)}, s32[4,2]{0,1:T(2,128)}, u32[]{:S(2)}) copy-start(s32[4,2]{0,1:T(2,128)} %param.23) | copy-start | bytes 100
  1.3 11.7 %copy-start.16 = (s32[2]{0:T(128)S(1)}, s32[2]{0:T(128)}, u32[]{:S(2)}) copy-start(s32[2]{0:T(128)} %lengths_ref.1) | copy-start | bytes 28
  4.3 3.6 %collective-permute-start = (bf16[208,512]{1,0:T(8,128)(2,1)}, bf16[208,512]{1,0:T(8,128)(2,1)S(1)}, u32[]{:S(2)}, u32[]{:S(2)}) collective-permute-start(bf16[208,512]{1,0:T(8,128)(2,1)} %get-tuple-element.13), channel_id=1, source_target_pairs={{256,0},{257,1},{258,2},{259,3},{260,4},{261,5},{262,6},{263,7},{2... | collective-permute-start | bytes 638984 | tf_op jit(solution)/shard_map/ppermute | solution.py:46
  7.8 0.9 copy-start.9
  8.7 8.8 %copy-start.3 = (bf16[1,256,512]{2,1,0:T(8,128)(2,1)S(1)}, bf16[1,256,512]{2,1,0:T(8,128)(2,1)}, u32[]{:S(2)}) copy-start(bf16[1,256,512]{2,1,0:T(8,128)(2,1)} %param.12) | copy-start | bytes 786436
  9.3 8.3 %collective-permute-start.1 = (bf16[320,128]{1,0:T(8,128)(2,1)S(1)}, bf16[320,128]{1,0:T(8,128)(2,1)S(1)}, u32[]{:S(2)}, u32[]{:S(2)}) collective-permute-start(bf16[320,128]{1,0:T(8,128)(2,1)S(1)} %unpack.1._), channel_id=1, source_target_pairs={{0,96},{1,65},{2,34},{3,3},{4,116},{5,85},{6,54},{7,23},{8,232},{9... | collective-permute-start | bytes 245768 | tf_op jit(solution)/shard_map/ppermute | solution.py:46
  19.4 99.0 %all-to-all-start = ((bf16[16,320,128]{2,1,0:T(8,128)(2,1)}), bf16[16,320,128]{2,1,0:T(8,128)(2,1)}, u32[]{:S(2)}, u32[]{:S(2)}) async-start(bf16[16,320,128]{2,1,0:T(8,128)(2,1)} %spread.1._), calls=%async_computation | async-start | bytes 2621440 | tf_op jit(solution)/shard_map/all_to_all | solution.py:50
  37.9 33.8 %collective-permute-start.2 = (bf16[144,512]{1,0:T(8,128)(2,1)S(1)}, bf16[144,512]{1,0:T(8,128)(2,1)S(1)}, u32[]{:S(2)}, u32[]{:S(2)}) collective-permute-start(bf16[144,512]{1,0:T(8,128)(2,1)S(1)} %half.1._.mine_ref), channel_id=1, source_target_pairs={{0,16},{1,17},{2,18},{3,19},{4,20},{5,21},{6,22},{7,23},{8,24},{9,... | collective-permute-start | bytes 442376 | tf_op jit(solution)/shard_map/ppermute | solution.py:46
  72.3 46.0 %copy-start = (bf16[272,512]{1,0:T(8,128)(2,1)}, bf16[272,512]{1,0:T(8,128)(2,1)S(1)}, u32[]{:S(2)}) copy-start(bf16[272,512]{1,0:T(8,128)(2,1)S(1)} %base.1.refs_0_) | copy-start | bytes 835588
  72.4 53.7 %copy-start.4 = (f32[1,512,320]{1,2,0:T(8,128)S(1)}, f32[1,512,320]{1,2,0:T(8,128)}, u32[]{:S(2)}) copy-start(f32[1,512,320]{1,2,0:T(8,128)} %param.15) | copy-start | bytes 1966084
  72.4 53.7 %copy-start.5 = (f32[1,512,320]{1,2,0:T(8,128)S(1)}, f32[1,512,320]{1,2,0:T(8,128)}, u32[]{:S(2)}) copy-start(f32[1,512,320]{1,2,0:T(8,128)} %param.16) | copy-start | bytes 1966084
  72.4 9.5 %collective-permute-start.4 = (bf16[272,512]{1,0:T(8,128)(2,1)S(1)}, bf16[272,512]{1,0:T(8,128)(2,1)S(1)}, u32[]{:S(2)}, u32[]{:S(2)}) collective-permute-start(bf16[272,512]{1,0:T(8,128)(2,1)S(1)} %base.1.refs_0_), channel_id=1, source_target_pairs={{0,32},{1,33},{2,34},{3,35},{4,36},{5,37},{6,38},{7,39},{8,40},{9,... | collective-permute-start | bytes 835592 | tf_op jit(solution)/shard_map/ppermute | solution.py:46
  74.4 9.7 %collective-permute-start.3 = (bf16[272,512]{1,0:T(8,128)(2,1)S(1)}, bf16[272,512]{1,0:T(8,128)(2,1)S(1)}, u32[]{:S(2)}, u32[]{:S(2)}) collective-permute-start(bf16[272,512]{1,0:T(8,128)(2,1)S(1)} %base.1.refs_0_), channel_id=1, source_target_pairs={{0,224},{1,225},{2,226},{3,227},{4,228},{5,229},{6,230},{7,231},{8... | collective-permute-start | bytes 835592 | tf_op jit(solution)/shard_map/ppermute | solution.py:46
  81.9 36.4 %copy-start.17 = (bf16[272,512]{1,0:T(8,128)(2,1)}, bf16[272,512]{1,0:T(8,128)(2,1)S(1)}, u32[]{:S(2)}) copy-start(bf16[272,512]{1,0:T(8,128)(2,1)S(1)} %collective-permute-done.4.refs_5_) | copy-start | bytes 835588
  84.1 34.3 %copy-start.18 = (bf16[272,512]{1,0:T(8,128)(2,1)}, bf16[272,512]{1,0:T(8,128)(2,1)S(1)}, u32[]{:S(2)}) copy-start(bf16[272,512]{1,0:T(8,128)(2,1)S(1)} %collective-permute-done.3.refs_1_) | copy-start | bytes 835588
  84.1 11.0 %collective-permute-start.5 = (bf16[272,512]{1,0:T(8,128)(2,1)S(1)}, bf16[272,512]{1,0:T(8,128)(2,1)S(1)}, u32[]{:S(2)}, u32[]{:S(2)}) collective-permute-start(bf16[272,512]{1,0:T(8,128)(2,1)S(1)} %collective-permute-done.3.refs_1_), channel_id=1, source_target_pairs={{0,224},{1,225},{2,226},{3,227},{4,228},{5,229},{6,230},{7,231},{8... | collective-permute-start | bytes 835592 | tf_op jit(solution)/shard_map/ppermute | solution.py:46
  86.8 9.4 %collective-permute-start.6 = (bf16[272,512]{1,0:T(8,128)(2,1)S(1)}, bf16[272,512]{1,0:T(8,128)(2,1)S(1)}, u32[]{:S(2)}, u32[]{:S(2)}) collective-permute-start(bf16[272,512]{1,0:T(8,128)(2,1)S(1)} %collective-permute-done.4.refs_5_), channel_id=1, source_target_pairs={{0,32},{1,33},{2,34},{3,35},{4,36},{5,37},{6,38},{7,39},{8,40},{9,... | collective-permute-start | bytes 835592 | tf_op jit(solution)/shard_map/ppermute | solution.py:46
  95.1 23.3 %copy-start.19 = (bf16[272,512]{1,0:T(8,128)(2,1)}, bf16[272,512]{1,0:T(8,128)(2,1)S(1)}, u32[]{:S(2)}) copy-start(bf16[272,512]{1,0:T(8,128)(2,1)S(1)} %collective-permute-done.5.refs_2_) | copy-start | bytes 835588
  96.2 22.1 %copy-start.20 = (bf16[272,512]{1,0:T(8,128)(2,1)}, bf16[272,512]{1,0:T(8,128)(2,1)S(1)}, u32[]{:S(2)}) copy-start(bf16[272,512]{1,0:T(8,128)(2,1)S(1)} %collective-permute-done.6.refs_6_) | copy-start | bytes 835588
  96.2 11.3 %collective-permute-start.7 = (bf16[272,512]{1,0:T(8,128)(2,1)S(1)}, bf16[272,512]{1,0:T(8,128)(2,1)S(1)}, u32[]{:S(2)}, u32[]{:S(2)}) collective-permute-start(bf16[272,512]{1,0:T(8,128)(2,1)S(1)} %collective-permute-done.5.refs_2_), channel_id=1, source_target_pairs={{0,224},{1,225},{2,226},{3,227},{4,228},{5,229},{6,230},{7,231},{8... | collective-permute-start | bytes 835592 | tf_op jit(solution)/shard_map/ppermute | solution.py:46
  100.2 8.4 %collective-permute-start.8 = (bf16[272,512]{1,0:T(8,128)(2,1)S(1)}, bf16[272,512]{1,0:T(8,128)(2,1)S(1)}, u32[]{:S(2)}, u32[]{:S(2)}) collective-permute-start(bf16[272,512]{1,0:T(8,128)(2,1)S(1)} %collective-permute-done.6.refs_6_), channel_id=1, source_target_pairs={{0,32},{1,33},{2,34},{3,35},{4,36},{5,37},{6,38},{7,39},{8,40},{9,... | collective-permute-start | bytes 835592 | tf_op jit(solution)/shard_map/ppermute | solution.py:46
  107.6 10.8 %copy-start.21 = (bf16[272,512]{1,0:T(8,128)(2,1)}, bf16[272,512]{1,0:T(8,128)(2,1)S(1)}, u32[]{:S(2)}) copy-start(bf16[272,512]{1,0:T(8,128)(2,1)S(1)} %collective-permute-done.7.refs_3_) | copy-start | bytes 835588
  108.6 9.8 %copy-start.22 = (bf16[272,512]{1,0:T(8,128)(2,1)}, bf16[272,512]{1,0:T(8,128)(2,1)S(1)}, u32[]{:S(2)}) copy-start(bf16[272,512]{1,0:T(8,128)(2,1)S(1)} %collective-permute-done.8.refs_7_) | copy-start | bytes 835588
  108.6 9.7 %collective-permute-start.9 = (bf16[272,512]{1,0:T(8,128)(2,1)S(1)}, bf16[272,512]{1,0:T(8,128)(2,1)}, u32[]{:S(2)}, u32[]{:S(2)}) collective-permute-start(bf16[272,512]{1,0:T(8,128)(2,1)S(1)} %collective-permute-done.7.refs_3_), channel_id=1, source_target_pairs={{0,224},{1,225},{2,226},{3,227},{4,228},{5,229},{6,230},{7,231},{8... | collective-permute-start | bytes 835592 | tf_op jit(solution)/shard_map/ppermute | solution.py:46
  122.8 3.2 %collective-permute-start.10 = (f32[320,512]{1,0:T(8,128)}, f32[320,512]{1,0:T(8,128)S(1)}, u32[]{:S(2)}, u32[]{:S(2)}) collective-permute-start(f32[320,512]{1,0:T(8,128)} %get-tuple-element.20.mine_ref), channel_id=1, source_target_pairs={{0,256},{1,257},{2,258},{3,259},{4,260},{5,261},{6,262},{7,263},{8... | collective-permute-start | bytes 1966088 | tf_op jit(solution)/shard_map/ppermute | solution.py:46
  126.0 1.1 copy-start.6
  127.1 4.0 %copy-start.7 = (bf16[512,320]{0,1:T(8,128)(2,1)S(1)}, bf16[512,320]{0,1:T(8,128)(2,1)}, u32[]{:S(2)}) copy-start(bf16[512,320]{0,1:T(8,128)(2,1)} %param.14) | copy-start | bytes 983044
  127.1 4.0 %copy-start.8 = (f32[128,512]{1,0:T(8,128)S(1)}, f32[128,512]{1,0:T(8,128)}, u32[]{:S(2)}) copy-start(f32[128,512]{1,0:T(8,128)} %get-tuple-element.21.rows_ref) | copy-start | bytes 786436
  127.1 4.0 %copy-start.11 = (s32[5]{0:T(128)S(1)}, s32[5]{0:T(128)}, u32[]{:S(2)}) copy-start(s32[5]{0:T(128)} %stack.23.place_ref) | copy-start | bytes 64
  127.6 3.5 %collective-permute-start.11 = (bf16[320,512]{1,0:T(8,128)(2,1)S(1)}, bf16[320,512]{1,0:T(8,128)(2,1)S(1)}, u32[]{:S(2)}, u32[]{:S(2)}) collective-permute-start(bf16[320,512]{1,0:T(8,128)(2,1)S(1)} %adam.1.update_ref), channel_id=1, source_target_pairs={{256,0},{257,1},{258,2},{259,3},{260,4},{261,5},{262,6},{263,7},{2... | collective-permute-start | bytes 983048 | tf_op jit(solution)/shard_map/ppermute | solution.py:46
  149.5 8.5 %collective-permute-start.12 = (bf16[8,320]{1,0:T(8,128)(2,1)S(1)}, bf16[8,320]{1,0:T(8,128)(2,1)S(1)}, u32[]{:S(2)}, u32[]{:S(2)}) collective-permute-start(bf16[8,320]{1,0:T(8,128)(2,1)S(1)} %reduce_sum.9), channel_id=1, source_target_pairs={{0,160},{1,193},{2,226},{3,3},{4,180},{5,213},{6,246},{7,23},{8,40... | collective-permute-start | bytes 15368 | tf_op jit(solution)/shard_map/ppermute | solution.py:46

commit v15 on v3

--- a/solution.py
+++ b/solution.py
@@ -44,31 +44,39 @@
     return lax.ppermute(value, AXES, pairs)
 
 
-def keeper(zh, x):
-    return int((x & 1) == zh)
+def gather(value, axes):
+    return lax.all_to_all(value, axes, split_axis=0, concat_axis=0, tiled=True)
 
 
 def to_partner(g, y, zh, zl, x):
     return (0, y, 1 - zh, zl, x) if g == 1 else None
 
 
+def keeper(zl):
+    return 1 - (zl & 1)
+
+
+def shift_of(z_lo, x):
+    return 4 * (z_lo >> 1) + x - 3
+
+
+def cot_shifted(g, y, zh, zl, x):
+    to = (keeper(zl), (y - shift_of(zl, x)) % 8, zh ^ (zl & 1), zl, x)
+    return to if g == 1 else None
+
+
+def along_zl(flip):
+    return lambda g, y, zh, zl, x: (g, y, zh, zl ^ flip, x) if g == keeper(zl) else None
+
+
+def along_x(step):
+    return lambda g, y, zh, zl, x: (g, y, zh, zl, (x + (step if g == 1 else -step)) % 4)
+
+
 def transposed(g, y, zh, zl, x):
     return (g, zl * 2 + (x >> 1), x & 1, y >> 1, (y & 1) * 2 + zh)
 
 
-def cot_transposed(g, *place):
-    _, y, zh, zl, x = transposed(g, *place)
-    return (keeper(zh, x), y, zh, zl, x) if g == 1 else None
-
-
-def along_zl(flip):
-    return lambda g, y, zh, zl, x: (g, y, zh, zl ^ flip, x) if g == keeper(zh, x) else None
-
-
-def along_x(step):
-    return lambda g, y, zh, zl, x: (g, y, zh, zl, (x + step) % 4) if g == keeper(zh, x) else None
-
-
 def other_core(g, y, zh, zl, x):
     return (1 - g, y, zh, zl, x)
 
@@ -77,19 +85,7 @@
     return (0, y, zh, zl, x) if g == 1 else None
 
 
-FLIPS = (0, 3, 1, 2)
-
-
-def device_table():
-    table = np.zeros((512, 32), np.int32)
-    for flat, (g, y, zh, zl, x) in enumerate(np.ndindex(*SHAPE)):
-        token_zh = zh if g == 1 else 1 - zh
-        table[flat, 0] = g
-        table[flat, 1] = token_zh
-        for n in range(8):
-            table[flat, 8 + n] = (2 * (n & 1) + token_zh - x) % 4
-            table[flat, 16 + n] = FLIPS.index(zl ^ (n >> 1))
-    return table
+SMALL = pltpu.CompilerParams(vmem_limit_bytes=6 * 2**20)
 
 
 def attend_kernel(
@@ -168,35 +164,73 @@
                 pltpu.VMEM((ROWS, HD), f32),
             ],
         ),
+        compiler_params=SMALL,
         name="attend",
     )(head, lengths, ids, queries, cache_keys, cache_values, new_keys, new_values)
 
 
-def base_kernel(table_ref, act_ref, act_got, rows_ref, rows_got, out_ref):
-    @pl.when(table_ref[0] == 1)
+VMEM = pl.BlockSpec(memory_space=pltpu.VMEM)
+SMEM = pl.BlockSpec(memory_space=pltpu.SMEM)
+HBM = pl.BlockSpec(memory_space=pl.ANY)
+
+
+BIG = pltpu.CompilerParams(vmem_limit_bytes=60 * 2**20)
+
+
+def cut_kernel(place_ref, cot_ref, out_ref, window, turned, sem):
+    z_lo = place_ref[3]
+    q = 2 * ((place_ref[1] - shift_of(z_lo, place_ref[4])) & 7) + (place_ref[2] ^ (z_lo & 1))
+    start = pl.multiple_of(((q * 5) >> 1) * 128, 128)
+    copy = pltpu.make_async_copy(cot_ref.at[:, pl.ds(start, 384)], window, sem)
+    copy.start()
+    copy.wait()
+    turned[...] = window[...].astype(f32).T
+    out_ref[...] = turned[pl.ds(pl.multiple_of((q & 1) * 64, 64), COLS), :].astype(bf16)
+
+
+def cut_of(place, cot):
+    return pl.pallas_call(
+        cut_kernel,
+        out_shape=jax.ShapeDtypeStruct((COLS, TOK), bf16),
+        in_specs=[SMEM, HBM],
+        out_specs=VMEM,
+        scratch_shapes=[
+            pltpu.VMEM((TOK, 384), bf16),
+            pltpu.VMEM((384, TOK), f32),
+            pltpu.SemaphoreType.DMA(()),
+        ],
+        compiler_params=BIG,
+        name="cut",
+    )(place, cot)
+
+
+def base_kernel(place_ref, act_ref, act_got, rows_ref, rows_got, out_ref):
+    @pl.when(place_ref[0] == 1)
     def _():
         out_ref[:TOK, :] = act_ref[...]
         out_ref[TOK:, :] = rows_ref[...]
 
-    @pl.when(table_ref[0] == 0)
+    @pl.when(place_ref[0] == 0)
     def _():
         out_ref[:TOK, :] = act_got[...]
         out_ref[TOK:, :] = rows_got[...]
 
 
-def base_of(table, *parts):
-    vmem = pl.BlockSpec(memory_space=pltpu.VMEM)
+def base_of(place, *parts):
     return pl.pallas_call(
         base_kernel,
         out_shape=jax.ShapeDtypeStruct((TOK + PAD, FEAT), bf16),
-        in_specs=[pl.BlockSpec(memory_space=pltpu.SMEM)] + [vmem] * 4,
-        out_specs=vmem,
+        in_specs=[SMEM] + [VMEM] * 4,
+        out_specs=VMEM,
+        compiler_params=SMALL,
         name="base",
-    )(table, *parts)
-
-
-def gradient_kernel(table_ref, chunks_ref, *refs):
+    )(place, *parts)
+
+
+def gradient_kernel(place_ref, chunks_ref, *refs):
     blocks, (out_ref, chunk_rows, block_rows, row_tiles, sems) = refs[:4], refs[-5:]
+    side, y, z_hi, own_z_lo, x = (place_ref[n] for n in range(5))
+    token_zh = jnp.where(side == 1, z_hi, 1 - z_hi)
     act_copies = [
         pltpu.make_async_copy(
             chunks_ref.at[n, :TOK], chunk_rows.at[pl.ds(n * TOK, TOK)], sems.at[n]
@@ -208,15 +242,17 @@
         for n in range(8)
     ]
     for n in range(8):
+        shift = ((n - y + 3) & 7) - 3
+        slot = ((shift + 3) >> 2) ^ (own_z_lo >> 1)
+        source = (shift + 3) - x
+        source = jnp.where(side == 1, -source, source) & 3
         act_copies[n].start()
         for b in range(4):
 
-            @pl.when(table_ref[8 + n] == b)
+            @pl.when(source == b)
             def _():
                 pltpu.make_async_copy(
-                    blocks[b].at[table_ref[16 + n]],
-                    block_rows.at[:, pl.ds(n * TOK, TOK)],
-                    sems.at[8 + n],
+                    blocks[b].at[slot], block_rows.at[:, pl.ds(n * TOK, TOK)], sems.at[8 + n]
                 ).start()
 
         row_copies[n].start()
@@ -235,36 +271,32 @@
             out_ref[:COLS, :] += part
     for n in range(8):
         row_copies[n].wait()
-        place = pl.multiple_of(COLS + (2 * n + table_ref[1]) * ROWS, ROWS)
+        place = pl.multiple_of(COLS + (2 * n + token_zh) * ROWS, ROWS)
         out_ref[pl.ds(place, ROWS), :] = row_tiles[n].astype(f32)[:ROWS]
 
 
-def gradient(table, chunks, blocks, others):
-    hbm = pl.BlockSpec(memory_space=pl.ANY)
+def gradient(place, chunks, blocks, others):
     operands = (chunks, *blocks, *others)
     return pl.pallas_call(
         gradient_kernel,
         out_shape=jax.ShapeDtypeStruct((COLS + 16 * ROWS, FEAT), f32),
-        in_specs=[pl.BlockSpec(memory_space=pltpu.SMEM)] + [hbm] * len(operands),
-        out_specs=pl.BlockSpec(memory_space=pltpu.VMEM),
+        in_specs=[SMEM] + [HBM] * len(operands),
+        out_specs=VMEM,
         scratch_shapes=[
             pltpu.VMEM((8 * TOK, FEAT), bf16),
             pltpu.VMEM((COLS, 8 * TOK), bf16),
             pltpu.VMEM((8, PAD, FEAT), bf16),
             pltpu.SemaphoreType.DMA((24,)),
         ],
-        compiler_params=pltpu.CompilerParams(vmem_limit_bytes=32 * 2**20),
-        cost_estimate=pl.CostEstimate(
-            flops=2 * 8 * TOK * COLS * FEAT, bytes_accessed=6 * 2**20, transcendentals=0
-        ),
+        compiler_params=BIG,
         name="gradient",
-    )(table, *operands)
+    )(place, *operands)
 
 
 def step_kernel(
-    table_ref, mine_ref, got_ref, one_ref, one_got, two_ref, two_got, weight_ref, update_ref, out_ref
+    place_ref, mine_ref, got_ref, one_ref, one_got, two_ref, two_got, weight_ref, update_ref, out_ref
 ):
-    learner = table_ref[0] == 1
+    learner = place_ref[0] == 1
     grad = mine_ref[:COLS, :] + got_ref[:COLS, :]
     moment_one = jnp.where(learner, one_ref[...], one_got[...])
     moment_two = jnp.where(learner, two_ref[...], two_got[...])
@@ -283,19 +315,18 @@
     out_ref[...] = part.reshape(16, ROWS, COLS)
 
 
-def step(table, mine, got, one, one_got, two, two_got, weight):
-    vmem = pl.BlockSpec(memory_space=pltpu.VMEM)
+def step(place, mine, got, one, one_got, two, two_got, weight):
     return pl.pallas_call(
         step_kernel,
         out_shape=(
             jax.ShapeDtypeStruct((COLS, FEAT), bf16),
             jax.ShapeDtypeStruct((16, ROWS, COLS), f32),
         ),
-        in_specs=[pl.BlockSpec(memory_space=pltpu.SMEM)] + [vmem] * 7,
-        out_specs=(vmem, vmem),
-        compiler_params=pltpu.CompilerParams(vmem_limit_bytes=32 * 2**20),
+        in_specs=[SMEM] + [VMEM] * 7,
+        out_specs=(VMEM, VMEM),
+        compiler_params=pltpu.CompilerParams(vmem_limit_bytes=16 * 2**20),
         name="step",
-    )(table, mine, got, one, one_got, two, two_got, weight)
+    )(place, mine, got, one, one_got, two, two_got, weight)
 
 
 def local(
@@ -312,11 +343,13 @@
     lengths,
     token_ids,
 ):
-    flat, q = lax.axis_index(AXES), lax.axis_index(TENSOR)
-    table = lax.dynamic_slice_in_dim(jnp.asarray(device_table()), flat, 1, 0)[0]
+    q = lax.axis_index(TENSOR)
+    place = jnp.stack([lax.axis_index(axis) for axis in AXES]).astype(jnp.int32)
 
     act = activations[0]
     act_got = permute(act, to_partner)
+    cut = cut_of(place, cotangent[0])
+    own = permute(cut, cot_shifted)
     rows = attend(
         (q >> 1).reshape(1),
         queries,
@@ -328,33 +361,27 @@
         token_ids.T,
     )
     rows_got = permute(rows, to_partner)
-    base = base_of(table, act, act_got, rows, rows_got)
+    base = base_of(place, act, act_got, rows, rows_got)
     chunks = lax.all_gather(base, "y", axis=0)
 
-    cut = lax.dynamic_slice_in_dim(cotangent[0], q * COLS, COLS, 1).T
-    own = permute(cut, cot_transposed)
-    two_blocks = jnp.stack([own, permute(own, along_zl(3))])
-    four = jnp.concatenate([two_blocks, permute(two_blocks, along_zl(1))], axis=0)
-    blocks = (
-        four,
-        permute(four, along_x(-1)),
-        permute(four, along_x(2)),
-        permute(four, along_x(1)),
-    )
-
     one, two = moment_one[0].T, moment_two[0].T
-    one_got = permute(one, to_rollout)
-    two_got = permute(two, to_rollout)
-
-    mine = gradient(table, chunks, blocks, (one_got, two_got))
+    one_tied, two_tied, own, _ = lax.optimization_barrier((one, two, own, base))
+    pair = jnp.stack([own, permute(own, along_zl(2))])
+    pair_got = permute(pair, along_zl(1))
+    pair = jnp.where(place[0] == keeper(place[3]), pair, pair_got)
+    blocks = [pair] + [permute(pair, along_x(step)) for step in (1, 2, -1)]
+    one_got = permute(one_tied, to_rollout)
+    two_got = permute(two_tied, to_rollout)
+
+    mine = gradient(place, chunks, blocks, (one_got, two_got))
     got = permute(mine, other_core)
-    update, partial = step(table, mine, got, one, one_got, two, two_got, weight.T)
-
-    shares = lax.all_to_all(partial, TENSOR, split_axis=0, concat_axis=0, tiled=True)
+    update, partial = step(place, mine, got, one, one_got, two, two_got, weight.T)
+
+    shares = gather(partial, TENSOR)
     summed = jnp.sum(shares, axis=0).astype(bf16)
     block = permute(summed, transposed)
     spread = jnp.broadcast_to(block[None], (16, ROWS, COLS))
-    gathered = lax.all_to_all(spread, TENSOR, split_axis=0, concat_axis=0, tiled=True)
+    gathered = gather(spread, TENSOR)
     decoded = gathered.transpose(1, 0, 2).reshape(STEPS, ROWS // STEPS, D)
     return (update.T, decoded)
 

time: 153 us -> 153 us (level)
  the two profiles are of different devices: /device:TPU:24 before, /device:TPU:2 now
where the time goes in v15:
time: 153 us; the launch traced here: 152 us
  waiting for transfers between devices  43.9 us (29%)
  blocking collectives  38.9 us (25%)
  starting transfers between devices  30.6 us (20%)
  between operations  14.3 us (9%)
  local copies, waits for them, and re-layouts  11.9 us (8%)
  Pallas kernels  11.2 us (7%)
    ppermute x12, waiting for transfers between devices, permute(): return lax.ppermute(value, AXES, pairs)  43.9 us
    all_to_all x2, blocking collectives, gather(): return lax.all_to_all(value, axes, split_axis=0, concat_axis=0, tiled=True)  38.9 us
    ppermute x12, starting transfers between devices, permute(): return lax.ppermute(value, AXES, pairs)  30.6 us
    unnamed x42, local copies, waits for them, and re-layouts  11 us
    pallas_call x1, Pallas kernels, gradient(): pl.pallas_call(gradient_kernel, out_shape=jax.ShapeDtypeStruct((COLS + 16...  4.48 us
  transfers between devices with their start and end apart: 13, of which 7 were waited for; matrix products, arithmetic and copies ran while one was open for 1% of the time, Pallas kernels for 2%

profile of v15, /device:TPU:2, one launch (start us, length us, event | category | flops | bytes accessed | tf_op | source)
XLA Modules:
  0.0 151.9 jit_solution(12174751959723958900)
XLA Ops:
  7.2 0.0 all-gather.3.cloned.1.call-start
  7.2 1.3 collective-permute-start
  8.5 0.0 copy-start.5
  8.5 1.2 copy-done.5
  9.7 1.2 copy-done.6
  11.0 0.7 copy-done.11
  11.7 0.7 copy-done.12
  12.4 0.7 copy-done.15
  13.1 0.7 copy-done.16
  13.8 0.7 copy-done.17
  14.4 1.0 attend.1.rows_ref
  15.5 0.0 copy-start.7
  15.5 0.0 copy-start.8
  15.5 1.4 collective-permute-start.1
  16.9 0.1 stack.32.place_ref
  17.0 12.2 %collective-permute-done.1.rows_got = bf16[16,512]{1,0:T(8,128)(2,1)S(1)} collective-permute-done((bf16[16,512]{1,0:T(8,128)(2,1)S(1)}, bf16[16,512]{1,0:T(8,128)(2,1)S(1)}, u32[]{:S(2)}, u32[]{:S(2)}) %collective-permute-start.1) | collective-permute-done | bytes 16416 | tf_op jit(solution)/shard_map/ppermute | solution.py:44
  29.2 0.0 collective-permute-done.act_got
  29.2 0.9 copy-done.10
  30.2 1.3 base.1
  31.5 0.0 all-gather.3.cloned.1.call-update
  31.5 0.0 copy-done.13
  31.5 2.4 %cut.1 = bf16[320,256]{1,0:T(8,128)(2,1)} custom-call(s32[5]{0:T(128)} %copy-done.13, bf16[256,5120]{1,0:T(8,128)(2,1)} %bitcast.29), custom_call_target="tpu_custom_call" | custom-call | tf_op jit(solution)/shard_map/cut/pallas_call | solution.py:192
  33.9 0.7 collective-permute-start.2
  34.6 0.0 collective-permute-done.2
  34.6 0.7 collective-permute-start.3
  35.3 0.0 collective-permute-done.3
  35.4 1.3 collective-permute-start.4
  36.7 0.0 copy-done.7
  36.7 1.3 collective-permute-start.8
  38.0 0.0 copy-done.8
  38.0 1.3 collective-permute-start.9
  39.3 22.9 %collective-permute-done.4 = bf16[2,320,256]{2,1,0:T(8,128)(2,1)} collective-permute-done((bf16[2,320,256]{2,1,0:T(8,128)(2,1)S(1)}, bf16[2,320,256]{2,1,0:T(8,128)(2,1)}, u32[]{:S(2)}, u32[]{:S(2)}) %collective-permute-start.4) | collective-permute-done | bytes 327712 | tf_op jit(solution)/shard_map/ppermute | solution.py:44
  62.2 1.0 broadcast_select_fusion.refs_0_
  63.2 0.0 copy-start.18
  63.2 2.3 %collective-permute-start.7 = (bf16[2,320,256]{2,1,0:T(8,128)(2,1)S(1)}, bf16[2,320,256]{2,1,0:T(8,128)(2,1)S(1)}, u32[]{:S(2)}, u32[]{:S(2)}) collective-permute-start(bf16[2,320,256]{2,1,0:T(8,128)(2,1)S(1)} %broadcast_select_fusion.refs_0_), channel_id=1, source_target_pairs={{0,1},{1,2},{2,3},{3,0},{4,5},{5,6},{6,7},{7,4},{8,9},{9,10},{10,1... | collective-permute-start | bytes 983048 | tf_op jit(solution)/shard_map/ppermute | solution.py:44
  65.5 6.0 %collective-permute-start.6 = (bf16[2,320,256]{2,1,0:T(8,128)(2,1)S(1)}, bf16[2,320,256]{2,1,0:T(8,128)(2,1)S(1)}, u32[]{:S(2)}, u32[]{:S(2)}) collective-permute-start(bf16[2,320,256]{2,1,0:T(8,128)(2,1)S(1)} %broadcast_select_fusion.refs_0_), channel_id=1, source_target_pairs={{0,2},{1,3},{2,0},{3,1},{4,6},{5,7},{6,4},{7,5},{8,10},{9,11},{10,... | collective-permute-start | bytes 983048 | tf_op jit(solution)/shard_map/ppermute | solution.py:44
  71.5 4.2 %collective-permute-start.5 = (bf16[2,320,256]{2,1,0:T(8,128)(2,1)S(1)}, bf16[2,320,256]{2,1,0:T(8,128)(2,1)}, u32[]{:S(2)}, u32[]{:S(2)}) collective-permute-start(bf16[2,320,256]{2,1,0:T(8,128)(2,1)S(1)} %broadcast_select_fusion.refs_0_), channel_id=1, source_target_pairs={{0,3},{1,0},{2,1},{3,2},{4,7},{5,4},{6,5},{7,6},{8,11},{9,8},{10,9... | collective-permute-start | bytes 983048 | tf_op jit(solution)/shard_map/ppermute | solution.py:44
  75.7 0.0 collective-permute-done.8.refs_4_.one_got
  75.7 0.0 copy-start.1
  75.7 0.0 collective-permute-done.9.refs_5_.two_got
  75.7 0.0 copy-start.3
  75.7 0.4 collective-permute-done.7.refs_3_
  76.1 0.5 collective-permute-done.6.refs_2_
  76.5 0.7 copy-done.20
  77.3 3.3 %collective-permute-done.5.refs_1_ = bf16[2,320,256]{2,1,0:T(8,128)(2,1)} collective-permute-done((bf16[2,320,256]{2,1,0:T(8,128)(2,1)S(1)}, bf16[2,320,256]{2,1,0:T(8,128)(2,1)}, u32[]{:S(2)}, u32[]{:S(2)}) %collective-permute-start.5) | collective-permute-done | bytes 327712 | tf_op jit(solution)/shard_map/ppermute | solution.py:44
  80.6 0.0 copy-done.18
  80.6 0.0 copy-done.1
  80.6 0.0 copy-done.3
  80.6 0.0 copy-done.19
  80.6 0.0 copy-start.9
  80.6 0.0 copy-start.14
  80.6 4.5 %gradient.1.mine_ref = f32[448,512]{1,0:T(8,128)} custom-call(s32[5]{0:T(128)} %copy-done.13, bf16[8,272,512]{2,1,0:T(8,128)(2,1)} %bitcast.30, bf16[2,320,256]{2,1,0:T(8,128)(2,1)} %copy-done.18, bf16[2,320,256]{2,1,0:T(8,128)(2,1)} %collective-permute-done.5.refs_1_, bf16[2,320,256]{2,1,0:T(8,128)(2,1)} %copy-done.20, bf16[2,320,256]{2,1,0:T(8,128)(2,1)} %copy-done.19, ...), custom_call_target="tpu_custom_call" | custom-call | tf_op jit(solution)/shard_map/gradient/pallas_call | solution.py:280
  85.1 1.9 %collective-permute-start.10 = (f32[448,512]{1,0:T(8,128)}, f32[448,512]{1,0:T(8,128)S(1)}, u32[]{:S(2)}, u32[]{:S(2)}) collective-permute-start(f32[448,512]{1,0:T(8,128)} %gradient.1.mine_ref), channel_id=1, source_target_pairs={{0,256},{1,257},{2,258},{3,259},{4,260},{5,261},{6,262},{7,263},{8... | collective-permute-start | bytes 2752520 | tf_op jit(solution)/shard_map/ppermute | solution.py:44
  87.0 2.6 %collective-permute-done.10.got_ref = f32[448,512]{1,0:T(8,128)S(1)} collective-permute-done((f32[448,512]{1,0:T(8,128)}, f32[448,512]{1,0:T(8,128)S(1)}, u32[]{:S(2)}, u32[]{:S(2)}) %collective-permute-start.10) | collective-permute-done | bytes 917536 | tf_op jit(solution)/shard_map/ppermute | solution.py:44
  89.7 0.0 copy-done.9
  89.7 1.2 copy-done
  90.9 1.1 copy-done.2
  92.0 1.1 copy-done.4
  93.1 1.9 %step.1 = (bf16[320,512]{1,0:T(8,128)(2,1)}, f32[16,8,320]{2,1,0:T(8,128)S(1)}) custom-call(s32[5]{0:T(128)S(1)} %copy-done.14, f32[448,512]{1,0:T(8,128)S(1)} %copy-done, f32[448,512]{1,0:T(8,128)S(1)} %collective-permute-done.10.got_ref, f32[320,512]{1,0:T(8,128)S(1)} %bitcast.22, f32[320,512]{1,0:T(8,128)S(1)} %copy-done.2, f32[320,512]{1,0:T(8,128)S(1)} %bitcast.24, ...), custom_call_target="tpu_custom_call" | custom-call | tf_op jit(solution)/shard_map/step/pallas_call | solution.py:319
  95.0 18.6 %all_to_all.10 = f32[16,8,320]{2,1,0:T(8,128)S(1)} all-to-all(f32[16,8,320]{2,1,0:T(8,128)S(1)} %get-tuple-element.11), channel_id=1, replica_groups=mesh['group'=2,'y'=8,'z_hi'=2,'z_lo'=4,'x'=4] {'z_lo','x'}, dimensions={0} | all-to-all | bytes 327680 | tf_op jit(solution)/shard_map/all_to_all | solution.py:48
  113.6 8.2 %collective-permute-start.11 = (bf16[8,320]{1,0:T(8,128)(2,1)S(1)}, bf16[8,320]{1,0:T(8,128)(2,1)S(1)}, u32[]{:S(2)}, u32[]{:S(2)}) collective-permute-start(bf16[8,320]{1,0:T(8,128)(2,1)S(1)} %reduce_sum.9), channel_id=1, source_target_pairs={{0,0},{1,16},{2,32},{3,48},{4,64},{5,80},{6,96},{7,112},{8,128},{9... | collective-permute-start | bytes 15368 | tf_op jit(solution)/shard_map/ppermute | solution.py:44
  121.8 2.1 %collective-permute-done.11 = bf16[8,320]{1,0:T(8,128)(2,1)S(1)} collective-permute-done((bf16[8,320]{1,0:T(8,128)(2,1)S(1)}, bf16[8,320]{1,0:T(8,128)(2,1)S(1)}, u32[]{:S(2)}, u32[]{:S(2)}) %collective-permute-start.11) | collective-permute-done | bytes 5152 | tf_op jit(solution)/shard_map/ppermute | solution.py:44
  123.9 20.3 %all_to_all.11 = bf16[16,8,320]{2,1,0:T(8,128)(2,1)S(1)} all-to-all(bf16[16,8,320]{2,1,0:T(8,128)(2,1)S(1)} %broadcast_in_dim.2), channel_id=1, replica_groups=mesh['group'=2,'y'=8,'z_hi'=2,'z_lo'=4,'x'=4] {'z_lo','x'}, dimensions={0} | all-to-all | bytes 163840 | tf_op jit(solution)/shard_map/all_to_all | solution.py:48
  144.2 0.8 reshape.12
  (19 shorter events, 0.1 us)
Async XLA Ops:
  7.2 73.4 %all-gather.3.cloned.1.call-start = ((), (), s32[]{:S(2)}) async-start(), calls=%async_computation.2 | async-start | bytes 2506752 | tf_op jit(solution)/shard_map/all_gather | solution.py:365
  7.2 22.0 %collective-permute-start = (bf16[256,512]{1,0:T(8,128)(2,1)}, bf16[256,512]{1,0:T(8,128)(2,1)S(1)}, u32[]{:S(2)}, u32[]{:S(2)}) collective-permute-start(bf16[256,512]{1,0:T(8,128)(2,1)} %bitcast.26), channel_id=1, source_target_pairs={{256,16},{257,17},{258,18},{259,19},{260,20},{261,21},{262,22},{26... | collective-permute-start | bytes 786440 | tf_op jit(solution)/shard_map/ppermute | solution.py:44
  8.5 1.2 copy-start.5
  9.7 1.2 copy-start.6
  11.0 0.7 copy-start.11
  11.7 0.7 copy-start.12
  12.4 0.7 copy-start.15
  13.1 0.7 copy-start.16
  13.8 0.7 copy-start.17
  15.5 21.2 %copy-start.7 = (f32[1,512,320]{1,2,0:T(8,128)S(1)}, f32[1,512,320]{1,2,0:T(8,128)}, u32[]{:S(2)}) copy-start(f32[1,512,320]{1,2,0:T(8,128)} %param.15) | copy-start | bytes 1966084
  15.5 22.5 %copy-start.8 = (f32[1,512,320]{1,2,0:T(8,128)S(1)}, f32[1,512,320]{1,2,0:T(8,128)}, u32[]{:S(2)}) copy-start(f32[1,512,320]{1,2,0:T(8,128)} %param.16) | copy-start | bytes 1966084
  15.5 13.7 %collective-permute-start.1 = (bf16[16,512]{1,0:T(8,128)(2,1)S(1)}, bf16[16,512]{1,0:T(8,128)(2,1)S(1)}, u32[]{:S(2)}, u32[]{:S(2)}) collective-permute-start(bf16[16,512]{1,0:T(8,128)(2,1)S(1)} %attend.1.rows_ref), channel_id=1, source_target_pairs={{256,16},{257,17},{258,18},{259,19},{260,20},{261,21},{262,22},{26... | collective-permute-start | bytes 49160 | tf_op jit(solution)/shard_map/ppermute | solution.py:44
  17.0 14.5 %copy-start.13 = (s32[5]{0:T(128)}, s32[5]{0:T(128)S(1)}, u32[]{:S(2)}) copy-start(s32[5]{0:T(128)S(1)} %stack.32.place_ref) | copy-start | bytes 64
  29.2 1.0 copy-start.10
  33.9 0.7 collective-permute-start.2
  34.6 0.7 collective-permute-start.3
  35.4 26.8 %collective-permute-start.4 = (bf16[2,320,256]{2,1,0:T(8,128)(2,1)S(1)}, bf16[2,320,256]{2,1,0:T(8,128)(2,1)}, u32[]{:S(2)}, u32[]{:S(2)}) collective-permute-start(bf16[2,320,256]{2,1,0:T(8,128)(2,1)S(1)} %pad_maximum_fusion), channel_id=1, source_target_pairs={{4,0},{5,1},{6,2},{7,3},{12,8},{13,9},{14,10},{15,11},{20,16},{21,... | collective-permute-start | bytes 983048 | tf_op jit(solution)/shard_map/ppermute | solution.py:44
  36.7 39.0 %collective-permute-start.8 = (f32[320,512]{1,0:T(8,128)S(1)}, f32[320,512]{1,0:T(8,128)S(1)}, u32[]{:S(2)}, u32[]{:S(2)}) collective-permute-start(f32[320,512]{1,0:T(8,128)S(1)} %bitcast.21), channel_id=1, source_target_pairs={{256,0},{257,1},{258,2},{259,3},{260,4},{261,5},{262,6},{263,7},{2... | collective-permute-start | bytes 1966088 | tf_op jit(solution)/shard_map/ppermute | solution.py:44
  38.0 37.7 %collective-permute-start.9 = (f32[320,512]{1,0:T(8,128)S(1)}, f32[320,512]{1,0:T(8,128)S(1)}, u32[]{:S(2)}, u32[]{:S(2)}) collective-permute-start(f32[320,512]{1,0:T(8,128)S(1)} %bitcast.23), channel_id=1, source_target_pairs={{256,0},{257,1},{258,2},{259,3},{260,4},{261,5},{262,6},{263,7},{2... | collective-permute-start | bytes 1966088 | tf_op jit(solution)/shard_map/ppermute | solution.py:44
  63.2 17.4 %copy-start.18 = (bf16[2,320,256]{2,1,0:T(8,128)(2,1)}, bf16[2,320,256]{2,1,0:T(8,128)(2,1)S(1)}, u32[]{:S(2)}) copy-start(bf16[2,320,256]{2,1,0:T(8,128)(2,1)S(1)} %broadcast_select_fusion.refs_0_) | copy-start | bytes 983044
  63.2 12.9 %collective-permute-start.7 = (bf16[2,320,256]{2,1,0:T(8,128)(2,1)S(1)}, bf16[2,320,256]{2,1,0:T(8,128)(2,1)S(1)}, u32[]{:S(2)}, u32[]{:S(2)}) collective-permute-start(bf16[2,320,256]{2,1,0:T(8,128)(2,1)S(1)} %broadcast_select_fusion.refs_0_), channel_id=1, source_target_pairs={{0,1},{1,2},{2,3},{3,0},{4,5},{5,6},{6,7},{7,4},{8,9},{9,10},{10,1... | collective-permute-start | bytes 983048 | tf_op jit(solution)/shard_map/ppermute | solution.py:44
  65.5 11.0 %collective-permute-start.6 = (bf16[2,320,256]{2,1,0:T(8,128)(2,1)S(1)}, bf16[2,320,256]{2,1,0:T(8,128)(2,1)S(1)}, u32[]{:S(2)}, u32[]{:S(2)}) collective-permute-start(bf16[2,320,256]{2,1,0:T(8,128)(2,1)S(1)} %broadcast_select_fusion.refs_0_), channel_id=1, source_target_pairs={{0,2},{1,3},{2,0},{3,1},{4,6},{5,7},{6,4},{7,5},{8,10},{9,11},{10,... | collective-permute-start | bytes 983048 | tf_op jit(solution)/shard_map/ppermute | solution.py:44
  71.5 9.1 %collective-permute-start.5 = (bf16[2,320,256]{2,1,0:T(8,128)(2,1)S(1)}, bf16[2,320,256]{2,1,0:T(8,128)(2,1)}, u32[]{:S(2)}, u32[]{:S(2)}) collective-permute-start(bf16[2,320,256]{2,1,0:T(8,128)(2,1)S(1)} %broadcast_select_fusion.refs_0_), channel_id=1, source_target_pairs={{0,3},{1,0},{2,1},{3,2},{4,7},{5,4},{6,5},{7,6},{8,11},{9,8},{10,9... | collective-permute-start | bytes 983048 | tf_op jit(solution)/shard_map/ppermute | solution.py:44
  75.7 4.9 %copy-start.1 = (f32[320,512]{1,0:T(8,128)}, f32[320,512]{1,0:T(8,128)S(1)}, u32[]{:S(2)}) copy-start(f32[320,512]{1,0:T(8,128)S(1)} %collective-permute-done.8.refs_4_.one_got) | copy-start | bytes 1966084
  75.7 4.9 %copy-start.3 = (f32[320,512]{1,0:T(8,128)}, f32[320,512]{1,0:T(8,128)S(1)}, u32[]{:S(2)}) copy-start(f32[320,512]{1,0:T(8,128)S(1)} %collective-permute-done.9.refs_5_.two_got) | copy-start | bytes 1966084
  76.1 4.5 %copy-start.19 = (bf16[2,320,256]{2,1,0:T(8,128)(2,1)}, bf16[2,320,256]{2,1,0:T(8,128)(2,1)S(1)}, u32[]{:S(2)}) copy-start(bf16[2,320,256]{2,1,0:T(8,128)(2,1)S(1)} %collective-permute-done.7.refs_3_) | copy-start | bytes 983044
  76.5 0.7 copy-start.20
  80.6 9.1 %copy-start.9 = (bf16[512,320]{0,1:T(8,128)(2,1)S(1)}, bf16[512,320]{0,1:T(8,128)(2,1)}, u32[]{:S(2)}) copy-start(bf16[512,320]{0,1:T(8,128)(2,1)} %param.14) | copy-start | bytes 983044
  80.6 9.1 %copy-start.14 = (s32[5]{0:T(128)S(1)}, s32[5]{0:T(128)}, u32[]{:S(2)}) copy-start(s32[5]{0:T(128)} %copy-done.13) | copy-start | bytes 64
  85.1 4.6 %collective-permute-start.10 = (f32[448,512]{1,0:T(8,128)}, f32[448,512]{1,0:T(8,128)S(1)}, u32[]{:S(2)}, u32[]{:S(2)}) collective-permute-start(f32[448,512]{1,0:T(8,128)} %gradient.1.mine_ref), channel_id=1, source_target_pairs={{0,256},{1,257},{2,258},{3,259},{4,260},{5,261},{6,262},{7,263},{8... | collective-permute-start | bytes 2752520 | tf_op jit(solution)/shard_map/ppermute | solution.py:44
  89.7 1.2 copy-start
  90.9 1.1 copy-start.2
  92.0 1.1 copy-start.4
  113.6 10.3 %collective-permute-start.11 = (bf16[8,320]{1,0:T(8,128)(2,1)S(1)}, bf16[8,320]{1,0:T(8,128)(2,1)S(1)}, u32[]{:S(2)}, u32[]{:S(2)}) collective-permute-start(bf16[8,320]{1,0:T(8,128)(2,1)S(1)} %reduce_sum.9), channel_id=1, source_target_pairs={{0,0},{1,16},{2,32},{3,48},{4,64},{5,80},{6,96},{7,112},{8,128},{9... | collective-permute-start | bytes 15368 | tf_op jit(solution)/shard_map/ppermute | solution.py:44
Sparse Core Ops, SparseCore 0:
  31.6 44.1 all-gather.2

commit v16 on v15

--- a/solution.py
+++ b/solution.py
@@ -174,9 +174,6 @@
 HBM = pl.BlockSpec(memory_space=pl.ANY)
 
 
-BIG = pltpu.CompilerParams(vmem_limit_bytes=60 * 2**20)
-
-
 def cut_kernel(place_ref, cot_ref, out_ref, window, turned, sem):
     z_lo = place_ref[3]
     q = 2 * ((place_ref[1] - shift_of(z_lo, place_ref[4])) & 7) + (place_ref[2] ^ (z_lo & 1))
@@ -199,12 +196,12 @@
             pltpu.VMEM((384, TOK), f32),
             pltpu.SemaphoreType.DMA(()),
         ],
-        compiler_params=BIG,
+        compiler_params=SMALL,
         name="cut",
     )(place, cot)
 
 
-def base_kernel(place_ref, act_ref, act_got, rows_ref, rows_got, out_ref):
+def base_kernel(place_ref, act_ref, act_got, rows_ref, rows_got, _, out_ref):
     @pl.when(place_ref[0] == 1)
     def _():
         out_ref[:TOK, :] = act_ref[...]
@@ -220,7 +217,7 @@
     return pl.pallas_call(
         base_kernel,
         out_shape=jax.ShapeDtypeStruct((TOK + PAD, FEAT), bf16),
-        in_specs=[SMEM] + [VMEM] * 4,
+        in_specs=[SMEM] + [VMEM] * 4 + [HBM],
         out_specs=VMEM,
         compiler_params=SMALL,
         name="base",
@@ -288,7 +285,7 @@
             pltpu.VMEM((8, PAD, FEAT), bf16),
             pltpu.SemaphoreType.DMA((24,)),
         ],
-        compiler_params=BIG,
+        compiler_params=pltpu.CompilerParams(vmem_limit_bytes=16 * 2**20),
         name="gradient",
     )(place, *operands)
 
@@ -361,15 +358,16 @@
         token_ids.T,
     )
     rows_got = permute(rows, to_partner)
-    base = base_of(place, act, act_got, rows, rows_got)
+    base = base_of(place, act, act_got, rows, rows_got, own)
     chunks = lax.all_gather(base, "y", axis=0)
 
     one, two = moment_one[0].T, moment_two[0].T
-    one_tied, two_tied, own, _ = lax.optimization_barrier((one, two, own, base))
+    own, _ = lax.optimization_barrier((own, base))
     pair = jnp.stack([own, permute(own, along_zl(2))])
     pair_got = permute(pair, along_zl(1))
     pair = jnp.where(place[0] == keeper(place[3]), pair, pair_got)
     blocks = [pair] + [permute(pair, along_x(step)) for step in (1, 2, -1)]
+    one_tied, two_tied, blocks[1] = lax.optimization_barrier((one, two, blocks[1]))
     one_got = permute(one_tied, to_rollout)
     two_got = permute(two_tied, to_rollout)
 

time: 153 us -> 144 us (0.941)
  the two profiles are of different devices: /device:TPU:2 before, /device:TPU:56 now
where the time goes in v16:
time: 144 us; the launch traced here: 142 us
  waiting for transfers between devices  54.5 us (38%)
  blocking collectives  28.9 us (20%)
  starting transfers between devices  28.7 us (20%)
  between operations  14.3 us (10%)
  Pallas kernels  7.76 us (5%)
  local copies, waits for them, and re-layouts  7.7 us (5%)
    ppermute x12, waiting for transfers between devices, permute(): return lax.ppermute(value, AXES, pairs)  54.5 us
    all_to_all x2, blocking collectives, gather(): return lax.all_to_all(value, axes, split_axis=0, concat_axis=0, tiled=True)  28.9 us
    ppermute x12, starting transfers between devices, permute(): return lax.ppermute(value, AXES, pairs)  28.6 us
    unnamed x34, local copies, waits for them, and re-layouts  6.81 us
  transfers between devices with their start and end apart: 13, of which 7 were waited for; matrix products, arithmetic and copies ran while one was open for 0% of the time, Pallas kernels for 1%

profile of v16, /device:TPU:56, one launch (start us, length us, event | category | flops | bytes accessed | tf_op | source)
XLA Modules:
  0.0 141.9 jit_solution(17154530457077333354)
XLA Ops:
  7.2 0.0 copy-start.15
  7.2 0.0 copy-start.16
  7.2 0.0 copy-start.13
  7.2 0.0 copy-start.12
  7.2 0.0 copy-start.14
  7.2 0.0 all-gather.3.cloned.1.call-start
  7.3 1.3 collective-permute-start
  8.6 0.1 stack.32.place_ref
  8.7 0.0 copy-start
  8.7 1.7 %copy-done = bf16[1,256,5120]{2,1,0:T(8,128)(2,1)S(1)} copy-done((bf16[1,256,5120]{2,1,0:T(8,128)(2,1)S(1)}, bf16[1,256,5120]{2,1,0:T(8,128)(2,1)}, u32[]{:S(2)}) %copy-start) | copy-done | bytes 2621464
  10.4 0.0 copy-start.2
  10.4 0.0 copy-start.11
  10.4 0.8 cut.1
  11.2 0.0 copy-start.4
  11.2 0.8 collective-permute-start.2
  12.0 0.0 copy-done.15
  12.0 0.0 copy-done.16
  12.0 0.0 copy-done.13
  12.0 0.0 copy-done.12
  12.0 0.0 copy-done.14
  12.1 0.0 copy-done.2
  12.1 0.0 copy-done.3
  12.1 1.1 attend.1.rows_ref
  13.1 0.0 copy-start.5
  13.1 1.4 %collective-permute-start.1 = (bf16[16,512]{1,0:T(8,128)(2,1)S(1)}, bf16[16,512]{1,0:T(8,128)(2,1)S(1)}, u32[]{:S(2)}, u32[]{:S(2)}) collective-permute-start(bf16[16,512]{1,0:T(8,128)(2,1)S(1)} %attend.1.rows_ref), channel_id=1, source_target_pairs={{256,16},{257,17},{258,18},{259,19},{260,20},{261,21},{262,22},{26... | collective-permute-start | bytes 49160 | tf_op jit(solution)/shard_map/ppermute | solution.py:44
  14.6 14.7 %collective-permute-done.1.rows_got = bf16[16,512]{1,0:T(8,128)(2,1)S(1)} collective-permute-done((bf16[16,512]{1,0:T(8,128)(2,1)S(1)}, bf16[16,512]{1,0:T(8,128)(2,1)S(1)}, u32[]{:S(2)}, u32[]{:S(2)}) %collective-permute-start.1) | collective-permute-done | bytes 16416 | tf_op jit(solution)/shard_map/ppermute | solution.py:44
  29.2 0.0 collective-permute-done.2._
  29.2 0.0 collective-permute-done.act_got
  29.3 0.0 copy-done.11
  29.3 1.7 %base.1 = bf16[272,512]{1,0:T(8,128)(2,1)} custom-call(s32[5]{0:T(128)S(1)} %stack.32.place_ref, bf16[256,512]{1,0:T(8,128)(2,1)S(1)} %bitcast.31, bf16[256,512]{1,0:T(8,128)(2,1)} %collective-permute-done.act_got, bf16[16,512]{1,0:T(8,128)(2,1)S(1)} %attend.1.rows_ref, bf16[16,512]{1,0:T(8,128)(2,1)S(1)} %collective-permute-done.1.rows_got, ...), custom_call_target="tpu_custom_call" | custom-call | tf_op jit(solution)/shard_map/base/pallas_call | solution.py:217
  31.0 0.0 all-gather.3.cloned.1.call-update
  31.0 0.7 collective-permute-start.3
  31.7 0.0 collective-permute-done.3
  31.7 1.3 collective-permute-start.4
  33.0 15.5 %collective-permute-done.4 = bf16[2,320,256]{2,1,0:T(8,128)(2,1)S(1)} collective-permute-done((bf16[2,320,256]{2,1,0:T(8,128)(2,1)S(1)}, bf16[2,320,256]{2,1,0:T(8,128)(2,1)S(1)}, u32[]{:S(2)}, u32[]{:S(2)}) %collective-permute-start.4) | collective-permute-done | bytes 327712 | tf_op jit(solution)/shard_map/ppermute | solution.py:44
  48.6 6.2 %collective-permute-start.5 = (bf16[2,320,256]{2,1,0:T(8,128)(2,1)S(1)}, bf16[2,320,256]{2,1,0:T(8,128)(2,1)S(1)}, u32[]{:S(2)}, u32[]{:S(2)}) collective-permute-start(bf16[2,320,256]{2,1,0:T(8,128)(2,1)S(1)} %broadcast_select_fusion.refs_0_), channel_id=1, source_target_pairs={{0,3},{1,0},{2,1},{3,2},{4,7},{5,4},{6,5},{7,6},{8,11},{9,8},{10,9... | collective-permute-start | bytes 983048 | tf_op jit(solution)/shard_map/ppermute | solution.py:44
  54.8 4.6 %collective-permute-done.5.refs_1_ = bf16[2,320,256]{2,1,0:T(8,128)(2,1)S(1)} collective-permute-done((bf16[2,320,256]{2,1,0:T(8,128)(2,1)S(1)}, bf16[2,320,256]{2,1,0:T(8,128)(2,1)S(1)}, u32[]{:S(2)}, u32[]{:S(2)}) %collective-permute-start.5) | collective-permute-done | bytes 327712 | tf_op jit(solution)/shard_map/ppermute | solution.py:44
  59.4 0.0 copy-done.4
  59.4 1.3 collective-permute-start.8
  60.7 0.0 copy-done.5
  60.7 1.3 collective-permute-start.9
  62.0 2.0 %collective-permute-start.7 = (bf16[2,320,256]{2,1,0:T(8,128)(2,1)S(1)}, bf16[2,320,256]{2,1,0:T(8,128)(2,1)S(1)}, u32[]{:S(2)}, u32[]{:S(2)}) collective-permute-start(bf16[2,320,256]{2,1,0:T(8,128)(2,1)S(1)} %broadcast_select_fusion.refs_0_), channel_id=1, source_target_pairs={{0,1},{1,2},{2,3},{3,0},{4,5},{5,6},{6,7},{7,4},{8,9},{9,10},{10,1... | collective-permute-start | bytes 983048 | tf_op jit(solution)/shard_map/ppermute | solution.py:44
  64.0 7.0 %collective-permute-start.6 = (bf16[2,320,256]{2,1,0:T(8,128)(2,1)S(1)}, bf16[2,320,256]{2,1,0:T(8,128)(2,1)S(1)}, u32[]{:S(2)}, u32[]{:S(2)}) collective-permute-start(bf16[2,320,256]{2,1,0:T(8,128)(2,1)S(1)} %broadcast_select_fusion.refs_0_), channel_id=1, source_target_pairs={{0,2},{1,3},{2,0},{3,1},{4,6},{5,7},{6,4},{7,5},{8,10},{9,11},{10,... | collective-permute-start | bytes 983048 | tf_op jit(solution)/shard_map/ppermute | solution.py:44
  71.0 1.7 %collective-permute-done.7.refs_3_ = bf16[2,320,256]{2,1,0:T(8,128)(2,1)S(1)} collective-permute-done((bf16[2,320,256]{2,1,0:T(8,128)(2,1)S(1)}, bf16[2,320,256]{2,1,0:T(8,128)(2,1)S(1)}, u32[]{:S(2)}, u32[]{:S(2)}) %collective-permute-start.7) | collective-permute-done | bytes 327712 | tf_op jit(solution)/shard_map/ppermute | solution.py:44
  72.6 0.0 copy-start.7
  72.6 0.7 copy-done.7
  73.4 7.2 %collective-permute-done.6.refs_2_ = bf16[2,320,256]{2,1,0:T(8,128)(2,1)S(1)} collective-permute-done((bf16[2,320,256]{2,1,0:T(8,128)(2,1)S(1)}, bf16[2,320,256]{2,1,0:T(8,128)(2,1)S(1)}, u32[]{:S(2)}, u32[]{:S(2)}) %collective-permute-start.6) | collective-permute-done | bytes 327712 | tf_op jit(solution)/shard_map/ppermute | solution.py:44
  80.6 0.7 copy-done.9
  81.3 0.0 collective-permute-done.8.refs_4_.one_got
  81.3 0.0 collective-permute-done.9.refs_5_.two_got
  81.3 0.0 copy-start.1
  81.4 1.6 %copy-done.1 = bf16[2176,512]{1,0:T(8,128)(2,1)S(1)} copy-done((bf16[2176,512]{1,0:T(8,128)(2,1)S(1)}, bf16[2176,512]{1,0:T(8,128)(2,1)}, u32[]{:S(2)}) %copy-start.1) | copy-done | bytes 2228248
  83.0 1.0 copy-done.8
  84.0 1.0 copy-done.10
  84.9 2.3 %gradient.1.mine_ref = f32[448,512]{1,0:T(8,128)S(1)} custom-call(s32[5]{0:T(128)S(1)} %stack.32.place_ref, bf16[8,272,512]{2,1,0:T(8,128)(2,1)S(1)} %bitcast.22, bf16[2,320,256]{2,1,0:T(8,128)(2,1)S(1)} %broadcast_select_fusion.refs_0_, bf16[2,320,256]{2,1,0:T(8,128)(2,1)S(1)} %collective-permute-done.5.refs_1_, bf16[2,320,256]{2,1,0:T(8,128)(2,1)S(1)} %copy-done.10, ...), custom_call_target="tpu_custom_call" | custom-call | tf_op jit(solution)/shard_map/gradient/pallas_call | solution.py:277
  87.2 2.2 %collective-permute-start.10 = (f32[448,512]{1,0:T(8,128)S(1)}, f32[448,512]{1,0:T(8,128)S(1)}, u32[]{:S(2)}, u32[]{:S(2)}) collective-permute-start(f32[448,512]{1,0:T(8,128)S(1)} %gradient.1.mine_ref), channel_id=1, source_target_pairs={{0,256},{1,257},{2,258},{3,259},{4,260},{5,261},{6,262},{7,263},{8... | collective-permute-start | bytes 2752520 | tf_op jit(solution)/shard_map/ppermute | solution.py:44
  89.5 2.1 %collective-permute-done.10.got_ref = f32[448,512]{1,0:T(8,128)S(1)} collective-permute-done((f32[448,512]{1,0:T(8,128)S(1)}, f32[448,512]{1,0:T(8,128)S(1)}, u32[]{:S(2)}, u32[]{:S(2)}) %collective-permute-start.10) | collective-permute-done | bytes 917536 | tf_op jit(solution)/shard_map/ppermute | solution.py:44
  91.6 0.0 copy-done.6
  91.6 1.9 %step.1 = (bf16[320,512]{1,0:T(8,128)(2,1)}, f32[16,8,320]{2,1,0:T(8,128)S(1)}) custom-call(s32[5]{0:T(128)S(1)} %stack.32.place_ref, f32[448,512]{1,0:T(8,128)S(1)} %gradient.1.mine_ref, f32[448,512]{1,0:T(8,128)S(1)} %collective-permute-done.10.got_ref, f32[320,512]{1,0:T(8,128)S(1)} %bitcast.26, f32[320,512]{1,0:T(8,128)S(1)} %collective-permute-done.8.refs_4_.one_got, ...), custom_call_target="tpu_custom_call" | custom-call | tf_op jit(solution)/shard_map/step/pallas_call | solution.py:316
  93.5 16.8 %all_to_all.10 = f32[16,8,320]{2,1,0:T(8,128)S(1)} all-to-all(f32[16,8,320]{2,1,0:T(8,128)S(1)} %get-tuple-element.13), channel_id=1, replica_groups=mesh['group'=2,'y'=8,'z_hi'=2,'z_lo'=4,'x'=4] {'z_lo','x'}, dimensions={0} | all-to-all | bytes 327680 | tf_op jit(solution)/shard_map/all_to_all | solution.py:48
  110.4 3.2 %collective-permute-start.11 = (bf16[8,320]{1,0:T(8,128)(2,1)S(1)}, bf16[8,320]{1,0:T(8,128)(2,1)S(1)}, u32[]{:S(2)}, u32[]{:S(2)}) collective-permute-start(bf16[8,320]{1,0:T(8,128)(2,1)S(1)} %reduce_sum.9), channel_id=1, source_target_pairs={{0,0},{1,16},{2,32},{3,48},{4,64},{5,80},{6,96},{7,112},{8,128},{9... | collective-permute-start | bytes 15368 | tf_op jit(solution)/shard_map/ppermute | solution.py:44
  113.6 8.6 %collective-permute-done.11 = bf16[8,320]{1,0:T(8,128)(2,1)S(1)} collective-permute-done((bf16[8,320]{1,0:T(8,128)(2,1)S(1)}, bf16[8,320]{1,0:T(8,128)(2,1)S(1)}, u32[]{:S(2)}, u32[]{:S(2)}) %collective-permute-start.11) | collective-permute-done | bytes 5152 | tf_op jit(solution)/shard_map/ppermute | solution.py:44
  122.2 12.1 %all_to_all.11 = bf16[16,8,320]{2,1,0:T(8,128)(2,1)S(1)} all-to-all(bf16[16,8,320]{2,1,0:T(8,128)(2,1)S(1)} %broadcast_in_dim.2), channel_id=1, replica_groups=mesh['group'=2,'y'=8,'z_hi'=2,'z_lo'=4,'x'=4] {'z_lo','x'}, dimensions={0} | all-to-all | bytes 163840 | tf_op jit(solution)/shard_map/all_to_all | solution.py:48
  134.3 0.8 reshape.12
  (11 shorter events, 0.1 us)
Async XLA Ops:
  7.2 4.8 %copy-start.15 = (s32[4,2]{0,1:T(2,128)S(1)}, s32[4,2]{0,1:T(2,128)}, u32[]{:S(2)}) copy-start(s32[4,2]{0,1:T(2,128)} %param.23) | copy-start | bytes 100
  7.2 4.8 %copy-start.16 = (s32[2]{0:T(128)S(1)}, s32[2]{0:T(128)}, u32[]{:S(2)}) copy-start(s32[2]{0:T(128)} %lengths_ref.1) | copy-start | bytes 28
  7.2 4.8 %copy-start.13 = (bf16[4,2,1024]{2,1,0:T(2,128)(2,1)S(1)}, bf16[4,2,1024]{2,1,0:T(2,128)(2,1)}, u32[]{:S(2)}) copy-start(bf16[4,2,1024]{2,1,0:T(2,128)(2,1)} %nv_ref.1) | copy-start | bytes 49156
  7.2 4.8 %copy-start.12 = (bf16[4,2,1024]{2,1,0:T(2,128)(2,1)S(1)}, bf16[4,2,1024]{2,1,0:T(2,128)(2,1)}, u32[]{:S(2)}) copy-start(bf16[4,2,1024]{2,1,0:T(2,128)(2,1)} %nk_ref.1) | copy-start | bytes 49156
  7.2 4.8 %copy-start.14 = (bf16[4,2,512]{2,1,0:T(2,128)(2,1)S(1)}, bf16[4,2,512]{2,1,0:T(2,128)(2,1)}, u32[]{:S(2)}) copy-start(bf16[4,2,512]{2,1,0:T(2,128)(2,1)} %q_ref.1) | copy-start | bytes 24580
  7.2 74.1 %all-gather.3.cloned.1.call-start = ((), (), s32[]{:S(2)}) async-start(), calls=%async_computation.2 | async-start | bytes 2506752 | tf_op jit(solution)/shard_map/all_gather | solution.py:362
  7.3 22.0 %collective-permute-start = (bf16[256,512]{1,0:T(8,128)(2,1)}, bf16[256,512]{1,0:T(8,128)(2,1)}, u32[]{:S(2)}, u32[]{:S(2)}) collective-permute-start(bf16[256,512]{1,0:T(8,128)(2,1)} %bitcast.30), channel_id=1, source_target_pairs={{256,16},{257,17},{258,18},{259,19},{260,20},{261,21},{262,22},{26... | collective-permute-start | bytes 786440 | tf_op jit(solution)/shard_map/ppermute | solution.py:44
  8.7 1.7 %copy-start = (bf16[1,256,5120]{2,1,0:T(8,128)(2,1)S(1)}, bf16[1,256,5120]{2,1,0:T(8,128)(2,1)}, u32[]{:S(2)}) copy-start(bf16[1,256,5120]{2,1,0:T(8,128)(2,1)} %param.13) | copy-start | bytes 7864324
  10.4 1.7 %copy-start.2 = (bf16[2,2048,128]{2,1,0:T(8,128)(2,1)S(1)}, bf16[2,2048,128]{2,1,0:T(8,128)(2,1)}, u32[]{:S(2)}) copy-start(bf16[2,2048,128]{2,1,0:T(8,128)(2,1)} %k_ref.1) | copy-start | bytes 3145732
  10.4 1.7 %copy-start.3 = (bf16[2,2048,128]{2,1,0:T(8,128)(2,1)S(1)}, bf16[2,2048,128]{2,1,0:T(8,128)(2,1)}, u32[]{:S(2)}) copy-start(bf16[2,2048,128]{2,1,0:T(8,128)(2,1)} %v_ref.1) | copy-start | bytes 3145732
  10.4 18.9 %copy-start.11 = (bf16[1,256,512]{2,1,0:T(8,128)(2,1)S(1)}, bf16[1,256,512]{2,1,0:T(8,128)(2,1)}, u32[]{:S(2)}) copy-start(bf16[1,256,512]{2,1,0:T(8,128)(2,1)} %param.12) | copy-start | bytes 786436
  11.2 48.2 %copy-start.4 = (f32[1,512,320]{1,2,0:T(8,128)S(1)}, f32[1,512,320]{1,2,0:T(8,128)}, u32[]{:S(2)}) copy-start(f32[1,512,320]{1,2,0:T(8,128)} %param.15) | copy-start | bytes 1966084
  11.2 18.1 %collective-permute-start.2 = (bf16[320,256]{1,0:T(8,128)(2,1)S(1)}, bf16[320,256]{1,0:T(8,128)(2,1)S(1)}, u32[]{:S(2)}, u32[]{:S(2)}) collective-permute-start(bf16[320,256]{1,0:T(8,128)(2,1)S(1)} %cut.1), channel_id=1, source_target_pairs={{256,352},{257,321},{258,290},{259,259},{260,116},{261,85},{262,54... | collective-permute-start | bytes 491528 | tf_op jit(solution)/shard_map/ppermute | solution.py:44
  13.1 47.6 %copy-start.5 = (f32[1,512,320]{1,2,0:T(8,128)S(1)}, f32[1,512,320]{1,2,0:T(8,128)}, u32[]{:S(2)}) copy-start(f32[1,512,320]{1,2,0:T(8,128)} %param.16) | copy-start | bytes 1966084
  13.1 16.1 %collective-permute-start.1 = (bf16[16,512]{1,0:T(8,128)(2,1)S(1)}, bf16[16,512]{1,0:T(8,128)(2,1)S(1)}, u32[]{:S(2)}, u32[]{:S(2)}) collective-permute-start(bf16[16,512]{1,0:T(8,128)(2,1)S(1)} %attend.1.rows_ref), channel_id=1, source_target_pairs={{256,16},{257,17},{258,18},{259,19},{260,20},{261,21},{262,22},{26... | collective-permute-start | bytes 49160 | tf_op jit(solution)/shard_map/ppermute | solution.py:44
  31.0 0.7 collective-permute-start.3
  31.7 16.9 %collective-permute-start.4 = (bf16[2,320,256]{2,1,0:T(8,128)(2,1)S(1)}, bf16[2,320,256]{2,1,0:T(8,128)(2,1)S(1)}, u32[]{:S(2)}, u32[]{:S(2)}) collective-permute-start(bf16[2,320,256]{2,1,0:T(8,128)(2,1)S(1)} %pad_maximum_fusion), channel_id=1, source_target_pairs={{4,0},{5,1},{6,2},{7,3},{12,8},{13,9},{14,10},{15,11},{20,16},{21,... | collective-permute-start | bytes 983048 | tf_op jit(solution)/shard_map/ppermute | solution.py:44
  48.6 10.8 %collective-permute-start.5 = (bf16[2,320,256]{2,1,0:T(8,128)(2,1)S(1)}, bf16[2,320,256]{2,1,0:T(8,128)(2,1)S(1)}, u32[]{:S(2)}, u32[]{:S(2)}) collective-permute-start(bf16[2,320,256]{2,1,0:T(8,128)(2,1)S(1)} %broadcast_select_fusion.refs_0_), channel_id=1, source_target_pairs={{0,3},{1,0},{2,1},{3,2},{4,7},{5,4},{6,5},{7,6},{8,11},{9,8},{10,9... | collective-permute-start | bytes 983048 | tf_op jit(solution)/shard_map/ppermute | solution.py:44
  59.4 22.0 %collective-permute-start.8 = (f32[320,512]{1,0:T(8,128)S(1)}, f32[320,512]{1,0:T(8,128)S(1)}, u32[]{:S(2)}, u32[]{:S(2)}) collective-permute-start(f32[320,512]{1,0:T(8,128)S(1)} %bitcast.25), channel_id=1, source_target_pairs={{256,0},{257,1},{258,2},{259,3},{260,4},{261,5},{262,6},{263,7},{2... | collective-permute-start | bytes 1966088 | tf_op jit(solution)/shard_map/ppermute | solution.py:44
  60.7 20.7 %collective-permute-start.9 = (f32[320,512]{1,0:T(8,128)S(1)}, f32[320,512]{1,0:T(8,128)S(1)}, u32[]{:S(2)}, u32[]{:S(2)}) collective-permute-start(f32[320,512]{1,0:T(8,128)S(1)} %bitcast.27), channel_id=1, source_target_pairs={{256,0},{257,1},{258,2},{259,3},{260,4},{261,5},{262,6},{263,7},{2... | collective-permute-start | bytes 1966088 | tf_op jit(solution)/shard_map/ppermute | solution.py:44
  62.0 10.6 %collective-permute-start.7 = (bf16[2,320,256]{2,1,0:T(8,128)(2,1)S(1)}, bf16[2,320,256]{2,1,0:T(8,128)(2,1)S(1)}, u32[]{:S(2)}, u32[]{:S(2)}) collective-permute-start(bf16[2,320,256]{2,1,0:T(8,128)(2,1)S(1)} %broadcast_select_fusion.refs_0_), channel_id=1, source_target_pairs={{0,1},{1,2},{2,3},{3,0},{4,5},{5,6},{6,7},{7,4},{8,9},{9,10},{10,1... | collective-permute-start | bytes 983048 | tf_op jit(solution)/shard_map/ppermute | solution.py:44
  64.0 16.6 %collective-permute-start.6 = (bf16[2,320,256]{2,1,0:T(8,128)(2,1)S(1)}, bf16[2,320,256]{2,1,0:T(8,128)(2,1)S(1)}, u32[]{:S(2)}, u32[]{:S(2)}) collective-permute-start(bf16[2,320,256]{2,1,0:T(8,128)(2,1)S(1)} %broadcast_select_fusion.refs_0_), channel_id=1, source_target_pairs={{0,2},{1,3},{2,0},{3,1},{4,6},{5,7},{6,4},{7,5},{8,10},{9,11},{10,... | collective-permute-start | bytes 983048 | tf_op jit(solution)/shard_map/ppermute | solution.py:44
  72.6 0.7 copy-start.7
  80.6 0.7 copy-start.9
  81.3 1.6 %copy-start.1 = (bf16[2176,512]{1,0:T(8,128)(2,1)S(1)}, bf16[2176,512]{1,0:T(8,128)(2,1)}, u32[]{:S(2)}) copy-start(bf16[2176,512]{1,0:T(8,128)(2,1)} %all-gather.3.cloned.1.call-done) | copy-start | bytes 6684676
  83.0 1.0 copy-start.8
  83.9 1.0 copy-start.10
  84.9 6.7 %copy-start.6 = (bf16[512,320]{0,1:T(8,128)(2,1)S(1)}, bf16[512,320]{0,1:T(8,128)(2,1)}, u32[]{:S(2)}) copy-start(bf16[512,320]{0,1:T(8,128)(2,1)} %param.14) | copy-start | bytes 983044
  87.2 4.4 %collective-permute-start.10 = (f32[448,512]{1,0:T(8,128)S(1)}, f32[448,512]{1,0:T(8,128)S(1)}, u32[]{:S(2)}, u32[]{:S(2)}) collective-permute-start(f32[448,512]{1,0:T(8,128)S(1)} %gradient.1.mine_ref), channel_id=1, source_target_pairs={{0,256},{1,257},{2,258},{3,259},{4,260},{5,261},{6,262},{7,263},{8... | collective-permute-start | bytes 2752520 | tf_op jit(solution)/shard_map/ppermute | solution.py:44
  110.4 11.8 %collective-permute-start.11 = (bf16[8,320]{1,0:T(8,128)(2,1)S(1)}, bf16[8,320]{1,0:T(8,128)(2,1)S(1)}, u32[]{:S(2)}, u32[]{:S(2)}) collective-permute-start(bf16[8,320]{1,0:T(8,128)(2,1)S(1)} %reduce_sum.9), channel_id=1, source_target_pairs={{0,0},{1,16},{2,32},{3,48},{4,64},{5,80},{6,96},{7,112},{8,128},{9... | collective-permute-start | bytes 15368 | tf_op jit(solution)/shard_map/ppermute | solution.py:44
Sparse Core Ops, SparseCore 0:
  31.1 46.3 all-gather.2

commit v17 on v16

--- a/solution.py
+++ b/solution.py
@@ -367,7 +367,7 @@
     pair_got = permute(pair, along_zl(1))
     pair = jnp.where(place[0] == keeper(place[3]), pair, pair_got)
     blocks = [pair] + [permute(pair, along_x(step)) for step in (1, 2, -1)]
-    one_tied, two_tied, blocks[1] = lax.optimization_barrier((one, two, blocks[1]))
+    one_tied, two_tied, _ = lax.optimization_barrier((one, two, base))
     one_got = permute(one_tied, to_rollout)
     two_got = permute(two_tied, to_rollout)
 

time: 144 us -> 139 us (0.965)
  local copies, waits for them, and re-layouts: 7.7 us -> 4.31 us
  starting transfers between devices: 28.7 us -> 27.1 us
    ppermute x12, waiting for transfers between devices: 54.5 us -> 46.9 us  [permute(): return lax.ppermute(value, AXES, pairs)]
    all_gather x1, waiting for transfers between devices: 0.01 us -> 6.95 us  [local(): chunks = lax.all_gather(base, 'y', axis=0)]
    unnamed x34 -> x26, local copies, waits for them, and re-layouts: 6.81 us -> 3.41 us
    ppermute x12, starting transfers between devices: 28.6 us -> 27.1 us  [permute(): return lax.ppermute(value, AXES, pairs)]
  transfers between devices with their start and end apart: 13 -> 13, of which waited for: 7 -> 7; matrix products, arithmetic and copies ran while one was open for 0% -> 0% of each run, Pallas kernels for 1% -> 2%
where the time goes in v17:
time: 139 us; the launch traced here: 137 us
  waiting for transfers between devices  53.9 us (39%)
  blocking collectives  29.4 us (21%)
  starting transfers between devices  27.1 us (19%)
  between operations  14.3 us (10%)
  Pallas kernels  7.99 us (6%)
  local copies, waits for them, and re-layouts  4.31 us (3%)
    ppermute x12, waiting for transfers between devices, permute(): return lax.ppermute(value, AXES, pairs)  46.9 us
    all_to_all x2, blocking collectives, gather(): return lax.all_to_all(value, axes, split_axis=0, concat_axis=0, tiled=True)  29.4 us
    ppermute x12, starting transfers between devices, permute(): return lax.ppermute(value, AXES, pairs)  27.1 us
    all_gather x1, waiting for transfers between devices, local(): chunks = lax.all_gather(base, 'y', axis=0)  6.95 us
    unnamed x26, local copies, waits for them, and re-layouts  3.41 us
  transfers between devices with their start and end apart: 13, of which 7 were waited for; matrix products, arithmetic and copies ran while one was open for 0% of the time, Pallas kernels for 2%

profile of v17, /device:TPU:56, one launch (start us, length us, event | category | flops | bytes accessed | tf_op | source)
XLA Modules:
  0.0 137.1 jit_solution(3372972027740208942)
XLA Ops:
  7.2 0.0 copy-start.11
  7.2 0.0 copy-start.12
  7.2 0.0 copy-start.9
  7.2 0.0 copy-start.8
  7.2 0.0 copy-start.10
  7.2 0.0 all-gather.3.cloned.1.call-start
  7.3 1.3 collective-permute-start
  8.6 0.1 stack.32.place_ref
  8.7 0.0 copy-start
  8.7 1.7 %copy-done = bf16[1,256,5120]{2,1,0:T(8,128)(2,1)S(1)} copy-done((bf16[1,256,5120]{2,1,0:T(8,128)(2,1)S(1)}, bf16[1,256,5120]{2,1,0:T(8,128)(2,1)}, u32[]{:S(2)}) %copy-start) | copy-done | bytes 2621464
  10.4 0.0 copy-start.2
  10.4 0.0 copy-start.3
  10.4 0.0 copy-start.7
  10.4 1.4 %cut.1 = bf16[320,256]{1,0:T(8,128)(2,1)} custom-call(s32[5]{0:T(128)S(1)} %stack.32.place_ref, bf16[256,5120]{1,0:T(8,128)(2,1)S(1)} %bitcast.21), custom_call_target="tpu_custom_call" | custom-call | tf_op jit(solution)/shard_map/cut/pallas_call | solution.py:189
  11.8 0.0 copy-start.4
  11.8 0.8 collective-permute-start.2
  12.7 0.0 copy-done.11
  12.7 0.0 copy-done.12
  12.7 0.0 copy-done.9
  12.7 0.0 copy-done.8
  12.7 0.0 copy-done.10
  12.7 0.0 copy-done.2
  12.7 0.0 copy-done.3
  12.7 1.1 attend.1.rows_ref
  13.8 1.3 collective-permute-start.1
  15.1 14.2 %collective-permute-done.1.rows_got = bf16[16,512]{1,0:T(8,128)(2,1)S(1)} collective-permute-done((bf16[16,512]{1,0:T(8,128)(2,1)S(1)}, bf16[16,512]{1,0:T(8,128)(2,1)S(1)}, u32[]{:S(2)}, u32[]{:S(2)}) %collective-permute-start.1) | collective-permute-done | bytes 16416 | tf_op jit(solution)/shard_map/ppermute | solution.py:44
  29.2 0.0 collective-permute-done.2._
  29.2 0.0 collective-permute-done.act_got
  29.3 0.0 copy-done.7
  29.3 1.3 base.1
  30.5 0.0 all-gather.3.cloned.1.call-update
  30.6 0.7 collective-permute-start.3
  31.2 0.0 collective-permute-done.3
  31.3 1.3 collective-permute-start.4
  32.6 0.0 copy-done.4
  32.6 1.3 collective-permute-start.8
  33.9 1.3 collective-permute-start.9
  35.2 12.8 %collective-permute-done.4 = bf16[2,320,256]{2,1,0:T(8,128)(2,1)S(1)} collective-permute-done((bf16[2,320,256]{2,1,0:T(8,128)(2,1)S(1)}, bf16[2,320,256]{2,1,0:T(8,128)(2,1)S(1)}, u32[]{:S(2)}, u32[]{:S(2)}) %collective-permute-start.4) | collective-permute-done | bytes 327712 | tf_op jit(solution)/shard_map/ppermute | solution.py:44
  48.1 3.2 %collective-permute-start.7 = (bf16[2,320,256]{2,1,0:T(8,128)(2,1)S(1)}, bf16[2,320,256]{2,1,0:T(8,128)(2,1)S(1)}, u32[]{:S(2)}, u32[]{:S(2)}) collective-permute-start(bf16[2,320,256]{2,1,0:T(8,128)(2,1)S(1)} %broadcast_select_fusion.refs_0_), channel_id=1, source_target_pairs={{0,1},{1,2},{2,3},{3,0},{4,5},{5,6},{6,7},{7,4},{8,9},{9,10},{10,1... | collective-permute-start | bytes 983048 | tf_op jit(solution)/shard_map/ppermute | solution.py:44
  51.3 7.2 %collective-permute-start.6 = (bf16[2,320,256]{2,1,0:T(8,128)(2,1)S(1)}, bf16[2,320,256]{2,1,0:T(8,128)(2,1)S(1)}, u32[]{:S(2)}, u32[]{:S(2)}) collective-permute-start(bf16[2,320,256]{2,1,0:T(8,128)(2,1)S(1)} %broadcast_select_fusion.refs_0_), channel_id=1, source_target_pairs={{0,2},{1,3},{2,0},{3,1},{4,6},{5,7},{6,4},{7,5},{8,10},{9,11},{10,... | collective-permute-start | bytes 983048 | tf_op jit(solution)/shard_map/ppermute | solution.py:44
  58.5 2.2 %collective-permute-start.5 = (bf16[2,320,256]{2,1,0:T(8,128)(2,1)S(1)}, bf16[2,320,256]{2,1,0:T(8,128)(2,1)S(1)}, u32[]{:S(2)}, u32[]{:S(2)}) collective-permute-start(bf16[2,320,256]{2,1,0:T(8,128)(2,1)S(1)} %broadcast_select_fusion.refs_0_), channel_id=1, source_target_pairs={{0,3},{1,0},{2,1},{3,2},{4,7},{5,4},{6,5},{7,6},{8,11},{9,8},{10,9... | collective-permute-start | bytes 983048 | tf_op jit(solution)/shard_map/ppermute | solution.py:44
  60.7 0.0 collective-permute-done.8.refs_4_.one_got
  60.7 0.0 collective-permute-done.9.refs_5_.two_got
  60.7 0.3 collective-permute-done.7.refs_3_
  61.1 9.9 %collective-permute-done.6.refs_2_ = bf16[2,320,256]{2,1,0:T(8,128)(2,1)S(1)} collective-permute-done((bf16[2,320,256]{2,1,0:T(8,128)(2,1)S(1)}, bf16[2,320,256]{2,1,0:T(8,128)(2,1)S(1)}, u32[]{:S(2)}, u32[]{:S(2)}) %collective-permute-start.6) | collective-permute-done | bytes 327712 | tf_op jit(solution)/shard_map/ppermute | solution.py:44
  71.0 0.0 collective-permute-done.5.refs_1_
  71.0 7.0 %all-gather.3.cloned.1.call-done = bf16[2176,512]{1,0:T(8,128)(2,1)} async-done(((bf16[272,512]{1,0:T(8,128)(2,1)}), bf16[2176,512]{1,0:T(8,128)(2,1)}) %all-gather.3.cloned.1.call-update) | async-done | bytes 2228240 | tf_op jit(solution)/shard_map/all_gather | solution.py:362
  77.9 0.0 copy-start.1
  77.9 1.6 %copy-done.1 = bf16[2176,512]{1,0:T(8,128)(2,1)S(1)} copy-done((bf16[2176,512]{1,0:T(8,128)(2,1)S(1)}, bf16[2176,512]{1,0:T(8,128)(2,1)}, u32[]{:S(2)}) %copy-start.1) | copy-done | bytes 2228248
  79.6 0.0 copy-start.5
  79.6 0.0 copy-start.6
  79.6 2.3 %gradient.1.mine_ref = f32[448,512]{1,0:T(8,128)S(1)} custom-call(s32[5]{0:T(128)S(1)} %stack.32.place_ref, bf16[8,272,512]{2,1,0:T(8,128)(2,1)S(1)} %bitcast.22, bf16[2,320,256]{2,1,0:T(8,128)(2,1)S(1)} %broadcast_select_fusion.refs_0_, bf16[2,320,256]{2,1,0:T(8,128)(2,1)S(1)} %collective-permute-done.5.refs_1_, ...), custom_call_target="tpu_custom_call" | custom-call | tf_op jit(solution)/shard_map/gradient/pallas_call | solution.py:277
  81.9 1.9 %collective-permute-start.10 = (f32[448,512]{1,0:T(8,128)S(1)}, f32[448,512]{1,0:T(8,128)S(1)}, u32[]{:S(2)}, u32[]{:S(2)}) collective-permute-start(f32[448,512]{1,0:T(8,128)S(1)} %gradient.1.mine_ref), channel_id=1, source_target_pairs={{0,256},{1,257},{2,258},{3,259},{4,260},{5,261},{6,262},{7,263},{8... | collective-permute-start | bytes 2752520 | tf_op jit(solution)/shard_map/ppermute | solution.py:44
  83.8 2.4 %collective-permute-done.10.got_ref = f32[448,512]{1,0:T(8,128)S(1)} collective-permute-done((f32[448,512]{1,0:T(8,128)S(1)}, f32[448,512]{1,0:T(8,128)S(1)}, u32[]{:S(2)}, u32[]{:S(2)}) %collective-permute-start.10) | collective-permute-done | bytes 917536 | tf_op jit(solution)/shard_map/ppermute | solution.py:44
  86.3 0.0 copy-done.5
  86.3 0.0 copy-done.6
  86.3 1.9 %step.1 = (bf16[320,512]{1,0:T(8,128)(2,1)}, f32[16,8,320]{2,1,0:T(8,128)S(1)}) custom-call(s32[5]{0:T(128)S(1)} %stack.32.place_ref, f32[448,512]{1,0:T(8,128)S(1)} %gradient.1.mine_ref, f32[448,512]{1,0:T(8,128)S(1)} %collective-permute-done.10.got_ref, f32[320,512]{1,0:T(8,128)S(1)} %bitcast.26, f32[320,512]{1,0:T(8,128)S(1)} %collective-permute-done.8.refs_4_.one_got, ...), custom_call_target="tpu_custom_call" | custom-call | tf_op jit(solution)/shard_map/step/pallas_call | solution.py:316
  88.2 17.3 %all_to_all.10 = f32[16,8,320]{2,1,0:T(8,128)S(1)} all-to-all(f32[16,8,320]{2,1,0:T(8,128)S(1)} %get-tuple-element.11), channel_id=1, replica_groups=mesh['group'=2,'y'=8,'z_hi'=2,'z_lo'=4,'x'=4] {'z_lo','x'}, dimensions={0} | all-to-all | bytes 327680 | tf_op jit(solution)/shard_map/all_to_all | solution.py:48
  105.5 4.6 %collective-permute-start.11 = (bf16[8,320]{1,0:T(8,128)(2,1)S(1)}, bf16[8,320]{1,0:T(8,128)(2,1)S(1)}, u32[]{:S(2)}, u32[]{:S(2)}) collective-permute-start(bf16[8,320]{1,0:T(8,128)(2,1)S(1)} %reduce_sum.9), channel_id=1, source_target_pairs={{0,0},{1,16},{2,32},{3,48},{4,64},{5,80},{6,96},{7,112},{8,128},{9... | collective-permute-start | bytes 15368 | tf_op jit(solution)/shard_map/ppermute | solution.py:44
  110.2 7.2 %collective-permute-done.11 = bf16[8,320]{1,0:T(8,128)(2,1)S(1)} collective-permute-done((bf16[8,320]{1,0:T(8,128)(2,1)S(1)}, bf16[8,320]{1,0:T(8,128)(2,1)S(1)}, u32[]{:S(2)}, u32[]{:S(2)}) %collective-permute-start.11) | collective-permute-done | bytes 5152 | tf_op jit(solution)/shard_map/ppermute | solution.py:44
  117.4 12.1 %all_to_all.11 = bf16[16,8,320]{2,1,0:T(8,128)(2,1)S(1)} all-to-all(bf16[16,8,320]{2,1,0:T(8,128)(2,1)S(1)} %broadcast_in_dim.2), channel_id=1, replica_groups=mesh['group'=2,'y'=8,'z_hi'=2,'z_lo'=4,'x'=4] {'z_lo','x'}, dimensions={0} | all-to-all | bytes 163840 | tf_op jit(solution)/shard_map/all_to_all | solution.py:48
  129.5 0.8 reshape.12
  (5 shorter events, 0.1 us)
Async XLA Ops:
  7.2 5.5 %copy-start.11 = (s32[4,2]{0,1:T(2,128)S(1)}, s32[4,2]{0,1:T(2,128)}, u32[]{:S(2)}) copy-start(s32[4,2]{0,1:T(2,128)} %param.23) | copy-start | bytes 100
  7.2 5.5 %copy-start.12 = (s32[2]{0:T(128)S(1)}, s32[2]{0:T(128)}, u32[]{:S(2)}) copy-start(s32[2]{0:T(128)} %lengths_ref.1) | copy-start | bytes 28
  7.2 5.5 %copy-start.9 = (bf16[4,2,1024]{2,1,0:T(2,128)(2,1)S(1)}, bf16[4,2,1024]{2,1,0:T(2,128)(2,1)}, u32[]{:S(2)}) copy-start(bf16[4,2,1024]{2,1,0:T(2,128)(2,1)} %nv_ref.1) | copy-start | bytes 49156
  7.2 5.5 %copy-start.8 = (bf16[4,2,1024]{2,1,0:T(2,128)(2,1)S(1)}, bf16[4,2,1024]{2,1,0:T(2,128)(2,1)}, u32[]{:S(2)}) copy-start(bf16[4,2,1024]{2,1,0:T(2,128)(2,1)} %nk_ref.1) | copy-start | bytes 49156
  7.2 5.5 %copy-start.10 = (bf16[4,2,512]{2,1,0:T(2,128)(2,1)S(1)}, bf16[4,2,512]{2,1,0:T(2,128)(2,1)}, u32[]{:S(2)}) copy-start(bf16[4,2,512]{2,1,0:T(2,128)(2,1)} %q_ref.1) | copy-start | bytes 24580
  7.2 70.7 %all-gather.3.cloned.1.call-start = ((), (), s32[]{:S(2)}) async-start(), calls=%async_computation.2 | async-start | bytes 2506752 | tf_op jit(solution)/shard_map/all_gather | solution.py:362
  7.3 22.0 %collective-permute-start = (bf16[256,512]{1,0:T(8,128)(2,1)}, bf16[256,512]{1,0:T(8,128)(2,1)S(1)}, u32[]{:S(2)}, u32[]{:S(2)}) collective-permute-start(bf16[256,512]{1,0:T(8,128)(2,1)} %bitcast.30), channel_id=1, source_target_pairs={{256,16},{257,17},{258,18},{259,19},{260,20},{261,21},{262,22},{26... | collective-permute-start | bytes 786440 | tf_op jit(solution)/shard_map/ppermute | solution.py:44
  8.7 1.7 %copy-start = (bf16[1,256,5120]{2,1,0:T(8,128)(2,1)S(1)}, bf16[1,256,5120]{2,1,0:T(8,128)(2,1)}, u32[]{:S(2)}) copy-start(bf16[1,256,5120]{2,1,0:T(8,128)(2,1)} %param.13) | copy-start | bytes 7864324
  10.4 2.3 %copy-start.2 = (bf16[2,2048,128]{2,1,0:T(8,128)(2,1)S(1)}, bf16[2,2048,128]{2,1,0:T(8,128)(2,1)}, u32[]{:S(2)}) copy-start(bf16[2,2048,128]{2,1,0:T(8,128)(2,1)} %k_ref.1) | copy-start | bytes 3145732
  10.4 2.3 %copy-start.3 = (bf16[2,2048,128]{2,1,0:T(8,128)(2,1)S(1)}, bf16[2,2048,128]{2,1,0:T(8,128)(2,1)}, u32[]{:S(2)}) copy-start(bf16[2,2048,128]{2,1,0:T(8,128)(2,1)} %v_ref.1) | copy-start | bytes 3145732
  10.4 18.9 %copy-start.7 = (bf16[1,256,512]{2,1,0:T(8,128)(2,1)S(1)}, bf16[1,256,512]{2,1,0:T(8,128)(2,1)}, u32[]{:S(2)}) copy-start(bf16[1,256,512]{2,1,0:T(8,128)(2,1)} %param.12) | copy-start | bytes 786436
  11.8 20.8 %copy-start.4 = (f32[1,512,320]{1,2,0:T(8,128)S(1)}, f32[1,512,320]{1,2,0:T(8,128)}, u32[]{:S(2)}) copy-start(f32[1,512,320]{1,2,0:T(8,128)} %param.15) | copy-start | bytes 1966084
  11.8 17.4 %collective-permute-start.2 = (bf16[320,256]{1,0:T(8,128)(2,1)}, bf16[320,256]{1,0:T(8,128)(2,1)S(1)}, u32[]{:S(2)}, u32[]{:S(2)}) collective-permute-start(bf16[320,256]{1,0:T(8,128)(2,1)} %cut.1), channel_id=1, source_target_pairs={{256,352},{257,321},{258,290},{259,259},{260,116},{261,85},{262,54... | collective-permute-start | bytes 491528 | tf_op jit(solution)/shard_map/ppermute | solution.py:44
  13.8 15.5 %collective-permute-start.1 = (bf16[16,512]{1,0:T(8,128)(2,1)S(1)}, bf16[16,512]{1,0:T(8,128)(2,1)S(1)}, u32[]{:S(2)}, u32[]{:S(2)}) collective-permute-start(bf16[16,512]{1,0:T(8,128)(2,1)S(1)} %attend.1.rows_ref), channel_id=1, source_target_pairs={{256,16},{257,17},{258,18},{259,19},{260,20},{261,21},{262,22},{26... | collective-permute-start | bytes 49160 | tf_op jit(solution)/shard_map/ppermute | solution.py:44
  30.6 0.7 collective-permute-start.3
  31.3 16.7 %collective-permute-start.4 = (bf16[2,320,256]{2,1,0:T(8,128)(2,1)S(1)}, bf16[2,320,256]{2,1,0:T(8,128)(2,1)S(1)}, u32[]{:S(2)}, u32[]{:S(2)}) collective-permute-start(bf16[2,320,256]{2,1,0:T(8,128)(2,1)S(1)} %pad_maximum_fusion), channel_id=1, source_target_pairs={{4,0},{5,1},{6,2},{7,3},{12,8},{13,9},{14,10},{15,11},{20,16},{21,... | collective-permute-start | bytes 983048 | tf_op jit(solution)/shard_map/ppermute | solution.py:44
  32.6 28.1 %collective-permute-start.8 = (f32[320,512]{1,0:T(8,128)S(1)}, f32[320,512]{1,0:T(8,128)S(1)}, u32[]{:S(2)}, u32[]{:S(2)}) collective-permute-start(f32[320,512]{1,0:T(8,128)S(1)} %bitcast.25), channel_id=1, source_target_pairs={{256,0},{257,1},{258,2},{259,3},{260,4},{261,5},{262,6},{263,7},{2... | collective-permute-start | bytes 1966088 | tf_op jit(solution)/shard_map/ppermute | solution.py:44
  33.9 26.8 %collective-permute-start.9 = (f32[320,512]{1,0:T(8,128)}, f32[320,512]{1,0:T(8,128)S(1)}, u32[]{:S(2)}, u32[]{:S(2)}) collective-permute-start(f32[320,512]{1,0:T(8,128)} %bitcast.27), channel_id=1, source_target_pairs={{256,0},{257,1},{258,2},{259,3},{260,4},{261,5},{262,6},{263,7},{2... | collective-permute-start | bytes 1966088 | tf_op jit(solution)/shard_map/ppermute | solution.py:44
  48.1 13.0 %collective-permute-start.7 = (bf16[2,320,256]{2,1,0:T(8,128)(2,1)S(1)}, bf16[2,320,256]{2,1,0:T(8,128)(2,1)S(1)}, u32[]{:S(2)}, u32[]{:S(2)}) collective-permute-start(bf16[2,320,256]{2,1,0:T(8,128)(2,1)S(1)} %broadcast_select_fusion.refs_0_), channel_id=1, source_target_pairs={{0,1},{1,2},{2,3},{3,0},{4,5},{5,6},{6,7},{7,4},{8,9},{9,10},{10,1... | collective-permute-start | bytes 983048 | tf_op jit(solution)/shard_map/ppermute | solution.py:44
  51.3 19.7 %collective-permute-start.6 = (bf16[2,320,256]{2,1,0:T(8,128)(2,1)S(1)}, bf16[2,320,256]{2,1,0:T(8,128)(2,1)S(1)}, u32[]{:S(2)}, u32[]{:S(2)}) collective-permute-start(bf16[2,320,256]{2,1,0:T(8,128)(2,1)S(1)} %broadcast_select_fusion.refs_0_), channel_id=1, source_target_pairs={{0,2},{1,3},{2,0},{3,1},{4,6},{5,7},{6,4},{7,5},{8,10},{9,11},{10,... | collective-permute-start | bytes 983048 | tf_op jit(solution)/shard_map/ppermute | solution.py:44
  58.5 12.5 %collective-permute-start.5 = (bf16[2,320,256]{2,1,0:T(8,128)(2,1)S(1)}, bf16[2,320,256]{2,1,0:T(8,128)(2,1)S(1)}, u32[]{:S(2)}, u32[]{:S(2)}) collective-permute-start(bf16[2,320,256]{2,1,0:T(8,128)(2,1)S(1)} %broadcast_select_fusion.refs_0_), channel_id=1, source_target_pairs={{0,3},{1,0},{2,1},{3,2},{4,7},{5,4},{6,5},{7,6},{8,11},{9,8},{10,9... | collective-permute-start | bytes 983048 | tf_op jit(solution)/shard_map/ppermute | solution.py:44
  77.9 1.6 %copy-start.1 = (bf16[2176,512]{1,0:T(8,128)(2,1)S(1)}, bf16[2176,512]{1,0:T(8,128)(2,1)}, u32[]{:S(2)}) copy-start(bf16[2176,512]{1,0:T(8,128)(2,1)} %all-gather.3.cloned.1.call-done) | copy-start | bytes 6684676
  79.6 6.7 %copy-start.5 = (f32[1,512,320]{1,2,0:T(8,128)S(1)}, f32[1,512,320]{1,2,0:T(8,128)}, u32[]{:S(2)}) copy-start(f32[1,512,320]{1,2,0:T(8,128)} %param.16) | copy-start | bytes 1966084
  79.6 6.7 %copy-start.6 = (bf16[512,320]{0,1:T(8,128)(2,1)S(1)}, bf16[512,320]{0,1:T(8,128)(2,1)}, u32[]{:S(2)}) copy-start(bf16[512,320]{0,1:T(8,128)(2,1)} %param.14) | copy-start | bytes 983044
  81.9 4.4 %collective-permute-start.10 = (f32[448,512]{1,0:T(8,128)S(1)}, f32[448,512]{1,0:T(8,128)S(1)}, u32[]{:S(2)}, u32[]{:S(2)}) collective-permute-start(f32[448,512]{1,0:T(8,128)S(1)} %gradient.1.mine_ref), channel_id=1, source_target_pairs={{0,256},{1,257},{2,258},{3,259},{4,260},{5,261},{6,262},{7,263},{8... | collective-permute-start | bytes 2752520 | tf_op jit(solution)/shard_map/ppermute | solution.py:44
  105.5 11.8 %collective-permute-start.11 = (bf16[8,320]{1,0:T(8,128)(2,1)S(1)}, bf16[8,320]{1,0:T(8,128)(2,1)S(1)}, u32[]{:S(2)}, u32[]{:S(2)}) collective-permute-start(bf16[8,320]{1,0:T(8,128)(2,1)S(1)} %reduce_sum.9), channel_id=1, source_target_pairs={{0,0},{1,16},{2,32},{3,48},{4,64},{5,80},{6,96},{7,112},{8,128},{9... | collective-permute-start | bytes 15368 | tf_op jit(solution)/shard_map/ppermute | solution.py:44
Sparse Core Ops, SparseCore 0:
  30.7 47.2 all-gather.2

commit v18 on v17

--- a/solution.py
+++ b/solution.py
@@ -50,6 +50,21 @@
 
 def to_partner(g, y, zh, zl, x):
     return (0, y, 1 - zh, zl, x) if g == 1 else None
+
+
+def back_two(zh, zl):
+    z = (zh * 4 + zl - 2) % 8
+    return z // 4, z % 4
+
+
+def to_partner_or_back(g, y, zh, zl, x):
+    if g == 0:
+        return None
+    return (0, y, 1 - zh, zl, x) if zl % 2 == 0 else (0, y, *back_two(zh, zl), x)
+
+
+def rest_back(g, y, zh, zl, x):
+    return (0, y, *back_two(zh, zl), x) if g == 0 and zl % 2 == 1 else None
 
 
 def keeper(zl):
@@ -201,15 +216,22 @@
     )(place, cot)
 
 
-def base_kernel(place_ref, act_ref, act_got, rows_ref, rows_got, _, out_ref):
+def base_kernel(place_ref, act_ref, act_got, act_passed, rows_ref, rows_got, _, out_ref):
     @pl.when(place_ref[0] == 1)
     def _():
         out_ref[:TOK, :] = act_ref[...]
         out_ref[TOK:, :] = rows_ref[...]
 
+    @pl.when((place_ref[0] == 0) & ((place_ref[3] & 1) == 0))
+    def _():
+        out_ref[:TOK, :] = act_got[...]
+
+    @pl.when((place_ref[0] == 0) & ((place_ref[3] & 1) == 1))
+    def _():
+        out_ref[:TOK, :] = act_passed[...]
+
     @pl.when(place_ref[0] == 0)
     def _():
-        out_ref[:TOK, :] = act_got[...]
         out_ref[TOK:, :] = rows_got[...]
 
 
@@ -217,7 +239,7 @@
     return pl.pallas_call(
         base_kernel,
         out_shape=jax.ShapeDtypeStruct((TOK + PAD, FEAT), bf16),
-        in_specs=[SMEM] + [VMEM] * 4 + [HBM],
+        in_specs=[SMEM] + [VMEM] * 5 + [HBM],
         out_specs=VMEM,
         compiler_params=SMALL,
         name="base",
@@ -344,7 +366,7 @@
     place = jnp.stack([lax.axis_index(axis) for axis in AXES]).astype(jnp.int32)
 
     act = activations[0]
-    act_got = permute(act, to_partner)
+    act_got = permute(act, to_partner_or_back)
     cut = cut_of(place, cotangent[0])
     own = permute(cut, cot_shifted)
     rows = attend(
@@ -358,7 +380,9 @@
         token_ids.T,
     )
     rows_got = permute(rows, to_partner)
-    base = base_of(place, act, act_got, rows, rows_got, own)
+    act_relay, _, _ = lax.optimization_barrier((act_got, cut, rows))
+    act_passed = permute(act_relay, rest_back)
+    base = base_of(place, act, act_got, act_passed, rows, rows_got, own)
     chunks = lax.all_gather(base, "y", axis=0)
 
     one, two = moment_one[0].T, moment_two[0].T

time: 139 us -> 149 us (1.072)
  waiting for transfers between devices: 53.9 us -> 58.5 us
  local copies, waits for them, and re-layouts: 4.31 us -> 8.4 us
    ppermute x12 -> x13, waiting for transfers between devices: 46.9 us -> 51.8 us  [permute(): return lax.ppermute(value, AXES, pairs)]
    unnamed x26 -> x34, local copies, waits for them, and re-layouts: 3.41 us -> 7.51 us
    ppermute x12 -> x13, starting transfers between devices: 27.1 us -> 27 us  [permute(): return lax.ppermute(value, AXES, pairs)]
  transfers between devices with their start and end apart: 13 -> 14, of which waited for: 7 -> 8; matrix products, arithmetic and copies ran while one was open for 0% -> 1% of each run, Pallas kernels for 2% -> 1%
where the time goes in v18:
time: 149 us; the launch traced here: 146 us
  waiting for transfers between devices  58.5 us (39%)
  blocking collectives  29.5 us (20%)
  starting transfers between devices  27 us (18%)
  between operations  14.3 us (10%)
  local copies, waits for them, and re-layouts  8.4 us (6%)
  Pallas kernels  7.39 us (5%)
    ppermute x13, waiting for transfers between devices, permute(): return lax.ppermute(value, AXES, pairs)  51.8 us
    all_to_all x2, blocking collectives, gather(): return lax.all_to_all(value, axes, split_axis=0, concat_axis=0, tiled=True)  29.5 us
    ppermute x13, starting transfers between devices, permute(): return lax.ppermute(value, AXES, pairs)  27 us
    unnamed x34, local copies, waits for them, and re-layouts  7.51 us
    all_gather x1, waiting for transfers between devices, local(): chunks = lax.all_gather(base, 'y', axis=0)  6.76 us
  transfers between devices with their start and end apart: 14, of which 8 were waited for; matrix products, arithmetic and copies ran while one was open for 1% of the time, Pallas kernels for 1%

profile of v18, /device:TPU:56, one launch (start us, length us, event | category | flops | bytes accessed | tf_op | source)
XLA Modules:
  0.0 146.3 jit_solution(1038973573686920162)
XLA Ops:
  7.2 0.0 copy-start.15
  7.2 0.0 copy-start.16
  7.2 0.0 copy-start.13
  7.2 0.0 copy-start.12
  7.2 0.0 copy-start.14
  7.2 0.0 all-gather.3.cloned.1.call-start
  7.3 1.3 collective-permute-start
  8.6 0.1 stack.32.place_ref
  8.7 0.0 copy-start
  8.7 1.7 %copy-done = bf16[1,256,5120]{2,1,0:T(8,128)(2,1)S(1)} copy-done((bf16[1,256,5120]{2,1,0:T(8,128)(2,1)S(1)}, bf16[1,256,5120]{2,1,0:T(8,128)(2,1)}, u32[]{:S(2)}) %copy-start) | copy-done | bytes 2621464
  10.4 0.8 cut.1
  11.2 0.0 copy-start.4
  11.2 0.0 copy-start.5
  11.2 0.0 copy-done.15
  11.2 0.0 copy-done.16
  11.2 0.0 copy-done.13
  11.2 0.0 copy-done.12
  11.2 0.0 copy-done.14
  11.2 0.4 copy-done.2
  11.6 0.3 copy-done.3
  11.9 1.0 attend.1.rows_ref
  13.0 8.4 %collective-permute-done.act_got = bf16[256,512]{1,0:T(8,128)(2,1)S(1)} collective-permute-done((bf16[256,512]{1,0:T(8,128)(2,1)}, bf16[256,512]{1,0:T(8,128)(2,1)S(1)}, u32[]{:S(2)}, u32[]{:S(2)}) %collective-permute-start) | collective-permute-done | bytes 262176 | tf_op jit(solution)/shard_map/ppermute | solution.py:44
  21.4 0.7 collective-permute-start.1
  22.0 0.7 collective-permute-start.3
  22.7 1.3 collective-permute-start.2
  24.0 7.7 %collective-permute-done.2.rows_got = bf16[16,512]{1,0:T(8,128)(2,1)S(1)} collective-permute-done((bf16[16,512]{1,0:T(8,128)(2,1)S(1)}, bf16[16,512]{1,0:T(8,128)(2,1)S(1)}, u32[]{:S(2)}, u32[]{:S(2)}) %collective-permute-start.2) | collective-permute-done | bytes 16416 | tf_op jit(solution)/shard_map/ppermute | solution.py:44
  31.7 0.0 collective-permute-done.3._
  31.7 0.0 collective-permute-done.1.act_passed
  31.7 0.0 copy-done.11
  31.7 1.3 base.1
  33.0 0.0 all-gather.3.cloned.1.call-update
  33.0 0.7 collective-permute-start.4
  33.7 0.0 collective-permute-done.4
  33.8 1.3 collective-permute-start.5
  35.1 0.0 copy-done.4
  35.1 1.3 collective-permute-start.9
  36.4 0.0 copy-done.5
  36.4 1.3 collective-permute-start.10
  37.7 22.2 %collective-permute-done.5 = bf16[2,320,256]{2,1,0:T(8,128)(2,1)} collective-permute-done((bf16[2,320,256]{2,1,0:T(8,128)(2,1)S(1)}, bf16[2,320,256]{2,1,0:T(8,128)(2,1)}, u32[]{:S(2)}, u32[]{:S(2)}) %collective-permute-start.5) | collective-permute-done | bytes 327712 | tf_op jit(solution)/shard_map/ppermute | solution.py:44
  59.9 1.0 broadcast_select_fusion.refs_0_
  60.9 3.6 %collective-permute-start.8 = (bf16[2,320,256]{2,1,0:T(8,128)(2,1)S(1)}, bf16[2,320,256]{2,1,0:T(8,128)(2,1)S(1)}, u32[]{:S(2)}, u32[]{:S(2)}) collective-permute-start(bf16[2,320,256]{2,1,0:T(8,128)(2,1)S(1)} %broadcast_select_fusion.refs_0_), channel_id=1, source_target_pairs={{0,1},{1,2},{2,3},{3,0},{4,5},{5,6},{6,7},{7,4},{8,9},{9,10},{10,1... | collective-permute-start | bytes 983048 | tf_op jit(solution)/shard_map/ppermute | solution.py:44
  64.5 3.9 %collective-permute-start.7 = (bf16[2,320,256]{2,1,0:T(8,128)(2,1)S(1)}, bf16[2,320,256]{2,1,0:T(8,128)(2,1)S(1)}, u32[]{:S(2)}, u32[]{:S(2)}) collective-permute-start(bf16[2,320,256]{2,1,0:T(8,128)(2,1)S(1)} %broadcast_select_fusion.refs_0_), channel_id=1, source_target_pairs={{0,2},{1,3},{2,0},{3,1},{4,6},{5,7},{6,4},{7,5},{8,10},{9,11},{10,... | collective-permute-start | bytes 983048 | tf_op jit(solution)/shard_map/ppermute | solution.py:44
  68.4 4.5 %collective-permute-start.6 = (bf16[2,320,256]{2,1,0:T(8,128)(2,1)S(1)}, bf16[2,320,256]{2,1,0:T(8,128)(2,1)S(1)}, u32[]{:S(2)}, u32[]{:S(2)}) collective-permute-start(bf16[2,320,256]{2,1,0:T(8,128)(2,1)S(1)} %broadcast_select_fusion.refs_0_), channel_id=1, source_target_pairs={{0,3},{1,0},{2,1},{3,2},{4,7},{5,4},{6,5},{7,6},{8,11},{9,8},{10,9... | collective-permute-start | bytes 983048 | tf_op jit(solution)/shard_map/ppermute | solution.py:44
  73.0 0.0 collective-permute-done.9.refs_4_.one_got
  73.0 0.0 collective-permute-done.10.refs_5_.two_got
  73.0 0.0 collective-permute-done.8.refs_3_
  73.0 2.1 %collective-permute-done.7.refs_2_ = bf16[2,320,256]{2,1,0:T(8,128)(2,1)S(1)} collective-permute-done((bf16[2,320,256]{2,1,0:T(8,128)(2,1)S(1)}, bf16[2,320,256]{2,1,0:T(8,128)(2,1)S(1)}, u32[]{:S(2)}, u32[]{:S(2)}) %collective-permute-start.7) | collective-permute-done | bytes 327712 | tf_op jit(solution)/shard_map/ppermute | solution.py:44
  75.1 0.7 copy-done.7
  75.8 1.7 %collective-permute-done.6.refs_1_ = bf16[2,320,256]{2,1,0:T(8,128)(2,1)S(1)} collective-permute-done((bf16[2,320,256]{2,1,0:T(8,128)(2,1)S(1)}, bf16[2,320,256]{2,1,0:T(8,128)(2,1)S(1)}, u32[]{:S(2)}, u32[]{:S(2)}) %collective-permute-start.6) | collective-permute-done | bytes 327712 | tf_op jit(solution)/shard_map/ppermute | solution.py:44
  77.5 0.7 copy-done.9
  78.3 6.8 %all-gather.3.cloned.1.call-done = bf16[2176,512]{1,0:T(8,128)(2,1)} async-done(((bf16[272,512]{1,0:T(8,128)(2,1)}), bf16[2176,512]{1,0:T(8,128)(2,1)}) %all-gather.3.cloned.1.call-update) | async-done | bytes 2228240 | tf_op jit(solution)/shard_map/all_gather | solution.py:386
  85.0 1.6 %copy-done.1 = bf16[2176,512]{1,0:T(8,128)(2,1)S(1)} copy-done((bf16[2176,512]{1,0:T(8,128)(2,1)S(1)}, bf16[2176,512]{1,0:T(8,128)(2,1)}, u32[]{:S(2)}) %copy-start.1) | copy-done | bytes 2228248
  86.7 1.0 copy-done.8
  87.6 1.0 copy-done.10
  88.6 2.3 %gradient.1.mine_ref = f32[448,512]{1,0:T(8,128)S(1)} custom-call(s32[5]{0:T(128)S(1)} %stack.32.place_ref, bf16[8,272,512]{2,1,0:T(8,128)(2,1)S(1)} %bitcast.22, bf16[2,320,256]{2,1,0:T(8,128)(2,1)S(1)} %broadcast_select_fusion.refs_0_, bf16[2,320,256]{2,1,0:T(8,128)(2,1)S(1)} %copy-done.10, bf16[2,320,256]{2,1,0:T(8,128)(2,1)S(1)} %copy-done.8, ...), custom_call_target="tpu_custom_call" | custom-call | tf_op jit(solution)/shard_map/gradient/pallas_call | solution.py:299
  90.9 1.9 %collective-permute-start.11 = (f32[448,512]{1,0:T(8,128)S(1)}, f32[448,512]{1,0:T(8,128)S(1)}, u32[]{:S(2)}, u32[]{:S(2)}) collective-permute-start(f32[448,512]{1,0:T(8,128)S(1)} %gradient.1.mine_ref), channel_id=1, source_target_pairs={{0,256},{1,257},{2,258},{3,259},{4,260},{5,261},{6,262},{7,263},{8... | collective-permute-start | bytes 2752520 | tf_op jit(solution)/shard_map/ppermute | solution.py:44
  92.8 2.4 %collective-permute-done.11.got_ref = f32[448,512]{1,0:T(8,128)S(1)} collective-permute-done((f32[448,512]{1,0:T(8,128)S(1)}, f32[448,512]{1,0:T(8,128)S(1)}, u32[]{:S(2)}, u32[]{:S(2)}) %collective-permute-start.11) | collective-permute-done | bytes 917536 | tf_op jit(solution)/shard_map/ppermute | solution.py:44
  95.3 0.0 copy-done.6
  95.3 2.0 %step.1 = (bf16[320,512]{1,0:T(8,128)(2,1)}, f32[16,8,320]{2,1,0:T(8,128)S(1)}) custom-call(s32[5]{0:T(128)S(1)} %stack.32.place_ref, f32[448,512]{1,0:T(8,128)S(1)} %gradient.1.mine_ref, f32[448,512]{1,0:T(8,128)S(1)} %collective-permute-done.11.got_ref, f32[320,512]{1,0:T(8,128)S(1)} %bitcast.26, f32[320,512]{1,0:T(8,128)S(1)} %collective-permute-done.9.refs_4_.one_got, ...), custom_call_target="tpu_custom_call" | custom-call | tf_op jit(solution)/shard_map/step/pallas_call | solution.py:338
  97.2 17.4 %all_to_all.10 = f32[16,8,320]{2,1,0:T(8,128)S(1)} all-to-all(f32[16,8,320]{2,1,0:T(8,128)S(1)} %get-tuple-element.13), channel_id=1, replica_groups=mesh['group'=2,'y'=8,'z_hi'=2,'z_lo'=4,'x'=4] {'z_lo','x'}, dimensions={0} | all-to-all | bytes 327680 | tf_op jit(solution)/shard_map/all_to_all | solution.py:48
  114.7 4.5 %collective-permute-start.12 = (bf16[8,320]{1,0:T(8,128)(2,1)S(1)}, bf16[8,320]{1,0:T(8,128)(2,1)S(1)}, u32[]{:S(2)}, u32[]{:S(2)}) collective-permute-start(bf16[8,320]{1,0:T(8,128)(2,1)S(1)} %reduce_sum.9), channel_id=1, source_target_pairs={{0,0},{1,16},{2,32},{3,48},{4,64},{5,80},{6,96},{7,112},{8,128},{9... | collective-permute-start | bytes 15368 | tf_op jit(solution)/shard_map/ppermute | solution.py:44
  119.2 7.3 %collective-permute-done.12 = bf16[8,320]{1,0:T(8,128)(2,1)S(1)} collective-permute-done((bf16[8,320]{1,0:T(8,128)(2,1)S(1)}, bf16[8,320]{1,0:T(8,128)(2,1)S(1)}, u32[]{:S(2)}, u32[]{:S(2)}) %collective-permute-start.12) | collective-permute-done | bytes 5152 | tf_op jit(solution)/shard_map/ppermute | solution.py:44
  126.5 12.1 %all_to_all.11 = bf16[16,8,320]{2,1,0:T(8,128)(2,1)S(1)} all-to-all(bf16[16,8,320]{2,1,0:T(8,128)(2,1)S(1)} %broadcast_in_dim.2), channel_id=1, replica_groups=mesh['group'=2,'y'=8,'z_hi'=2,'z_lo'=4,'x'=4] {'z_lo','x'}, dimensions={0} | all-to-all | bytes 163840 | tf_op jit(solution)/shard_map/all_to_all | solution.py:48
  138.6 0.8 reshape.12
  (13 shorter events, 0.1 us)
Async XLA Ops:
  7.2 4.0 %copy-start.15 = (s32[4,2]{0,1:T(2,128)S(1)}, s32[4,2]{0,1:T(2,128)}, u32[]{:S(2)}) copy-start(s32[4,2]{0,1:T(2,128)} %param.23) | copy-start | bytes 100
  7.2 4.0 %copy-start.16 = (s32[2]{0:T(128)S(1)}, s32[2]{0:T(128)}, u32[]{:S(2)}) copy-start(s32[2]{0:T(128)} %lengths_ref.1) | copy-start | bytes 28
  7.2 4.0 %copy-start.13 = (bf16[4,2,1024]{2,1,0:T(2,128)(2,1)S(1)}, bf16[4,2,1024]{2,1,0:T(2,128)(2,1)}, u32[]{:S(2)}) copy-start(bf16[4,2,1024]{2,1,0:T(2,128)(2,1)} %nv_ref.1) | copy-start | bytes 49156
  7.2 4.0 %copy-start.12 = (bf16[4,2,1024]{2,1,0:T(2,128)(2,1)S(1)}, bf16[4,2,1024]{2,1,0:T(2,128)(2,1)}, u32[]{:S(2)}) copy-start(bf16[4,2,1024]{2,1,0:T(2,128)(2,1)} %nk_ref.1) | copy-start | bytes 49156
  7.2 4.0 %copy-start.14 = (bf16[4,2,512]{2,1,0:T(2,128)(2,1)S(1)}, bf16[4,2,512]{2,1,0:T(2,128)(2,1)}, u32[]{:S(2)}) copy-start(bf16[4,2,512]{2,1,0:T(2,128)(2,1)} %q_ref.1) | copy-start | bytes 24580
  7.2 77.8 %all-gather.3.cloned.1.call-start = ((), (), s32[]{:S(2)}) async-start(), calls=%async_computation.2 | async-start | bytes 2506752 | tf_op jit(solution)/shard_map/all_gather | solution.py:386
  7.3 14.1 %collective-permute-start = (bf16[256,512]{1,0:T(8,128)(2,1)}, bf16[256,512]{1,0:T(8,128)(2,1)S(1)}, u32[]{:S(2)}, u32[]{:S(2)}) collective-permute-start(bf16[256,512]{1,0:T(8,128)(2,1)} %bitcast.30), channel_id=1, source_target_pairs={{256,16},{257,17},{258,18},{259,19},{260,28},{261,29},{262,30},{26... | collective-permute-start | bytes 786440 | tf_op jit(solution)/shard_map/ppermute | solution.py:44
  8.7 1.7 %copy-start = (bf16[1,256,5120]{2,1,0:T(8,128)(2,1)S(1)}, bf16[1,256,5120]{2,1,0:T(8,128)(2,1)}, u32[]{:S(2)}) copy-start(bf16[1,256,5120]{2,1,0:T(8,128)(2,1)} %param.13) | copy-start | bytes 7864324
  10.4 1.2 copy-start.2
  10.4 1.5 %copy-start.3 = (bf16[2,2048,128]{2,1,0:T(8,128)(2,1)S(1)}, bf16[2,2048,128]{2,1,0:T(8,128)(2,1)}, u32[]{:S(2)}) copy-start(bf16[2,2048,128]{2,1,0:T(8,128)(2,1)} %v_ref.1) | copy-start | bytes 3145732
  10.4 21.3 %copy-start.11 = (bf16[1,256,512]{2,1,0:T(8,128)(2,1)S(1)}, bf16[1,256,512]{2,1,0:T(8,128)(2,1)}, u32[]{:S(2)}) copy-start(bf16[1,256,512]{2,1,0:T(8,128)(2,1)} %param.12) | copy-start | bytes 786436
  11.2 23.9 %copy-start.4 = (f32[1,512,320]{1,2,0:T(8,128)S(1)}, f32[1,512,320]{1,2,0:T(8,128)}, u32[]{:S(2)}) copy-start(f32[1,512,320]{1,2,0:T(8,128)} %param.15) | copy-start | bytes 1966084
  11.2 25.2 %copy-start.5 = (f32[1,512,320]{1,2,0:T(8,128)S(1)}, f32[1,512,320]{1,2,0:T(8,128)}, u32[]{:S(2)}) copy-start(f32[1,512,320]{1,2,0:T(8,128)} %param.16) | copy-start | bytes 1966084
  21.4 10.3 %collective-permute-start.1 = (bf16[256,512]{1,0:T(8,128)(2,1)S(1)}, bf16[256,512]{1,0:T(8,128)(2,1)S(1)}, u32[]{:S(2)}, u32[]{:S(2)}) collective-permute-start(bf16[256,512]{1,0:T(8,128)(2,1)S(1)} %collective-permute-done.act_got), channel_id=1, source_target_pairs={{4,28},{5,29},{6,30},{7,31},{12,4},{13,5},{14,6},{15,7},{20,12},{2... | collective-permute-start | bytes 786440 | tf_op jit(solution)/shard_map/ppermute | solution.py:44
  22.0 9.6 %collective-permute-start.3 = (bf16[320,256]{1,0:T(8,128)(2,1)S(1)}, bf16[320,256]{1,0:T(8,128)(2,1)S(1)}, u32[]{:S(2)}, u32[]{:S(2)}) collective-permute-start(bf16[320,256]{1,0:T(8,128)(2,1)S(1)} %cut.1), channel_id=1, source_target_pairs={{256,352},{257,321},{258,290},{259,259},{260,116},{261,85},{262,54... | collective-permute-start | bytes 491528 | tf_op jit(solution)/shard_map/ppermute | solution.py:44
  22.7 9.0 %collective-permute-start.2 = (bf16[16,512]{1,0:T(8,128)(2,1)S(1)}, bf16[16,512]{1,0:T(8,128)(2,1)S(1)}, u32[]{:S(2)}, u32[]{:S(2)}) collective-permute-start(bf16[16,512]{1,0:T(8,128)(2,1)S(1)} %attend.1.rows_ref), channel_id=1, source_target_pairs={{256,16},{257,17},{258,18},{259,19},{260,20},{261,21},{262,22},{26... | collective-permute-start | bytes 49160 | tf_op jit(solution)/shard_map/ppermute | solution.py:44
  33.0 0.7 collective-permute-start.4
  33.8 26.1 %collective-permute-start.5 = (bf16[2,320,256]{2,1,0:T(8,128)(2,1)S(1)}, bf16[2,320,256]{2,1,0:T(8,128)(2,1)}, u32[]{:S(2)}, u32[]{:S(2)}) collective-permute-start(bf16[2,320,256]{2,1,0:T(8,128)(2,1)S(1)} %pad_maximum_fusion), channel_id=1, source_target_pairs={{4,0},{5,1},{6,2},{7,3},{12,8},{13,9},{14,10},{15,11},{20,16},{21,... | collective-permute-start | bytes 983048 | tf_op jit(solution)/shard_map/ppermute | solution.py:44
  35.1 37.9 %collective-permute-start.9 = (f32[320,512]{1,0:T(8,128)S(1)}, f32[320,512]{1,0:T(8,128)S(1)}, u32[]{:S(2)}, u32[]{:S(2)}) collective-permute-start(f32[320,512]{1,0:T(8,128)S(1)} %bitcast.25), channel_id=1, source_target_pairs={{256,0},{257,1},{258,2},{259,3},{260,4},{261,5},{262,6},{263,7},{2... | collective-permute-start | bytes 1966088 | tf_op jit(solution)/shard_map/ppermute | solution.py:44
  36.4 36.6 %collective-permute-start.10 = (f32[320,512]{1,0:T(8,128)S(1)}, f32[320,512]{1,0:T(8,128)S(1)}, u32[]{:S(2)}, u32[]{:S(2)}) collective-permute-start(f32[320,512]{1,0:T(8,128)S(1)} %bitcast.27), channel_id=1, source_target_pairs={{256,0},{257,1},{258,2},{259,3},{260,4},{261,5},{262,6},{263,7},{2... | collective-permute-start | bytes 1966088 | tf_op jit(solution)/shard_map/ppermute | solution.py:44
  60.9 12.1 %collective-permute-start.8 = (bf16[2,320,256]{2,1,0:T(8,128)(2,1)S(1)}, bf16[2,320,256]{2,1,0:T(8,128)(2,1)S(1)}, u32[]{:S(2)}, u32[]{:S(2)}) collective-permute-start(bf16[2,320,256]{2,1,0:T(8,128)(2,1)S(1)} %broadcast_select_fusion.refs_0_), channel_id=1, source_target_pairs={{0,1},{1,2},{2,3},{3,0},{4,5},{5,6},{6,7},{7,4},{8,9},{9,10},{10,1... | collective-permute-start | bytes 983048 | tf_op jit(solution)/shard_map/ppermute | solution.py:44
  64.5 10.6 %collective-permute-start.7 = (bf16[2,320,256]{2,1,0:T(8,128)(2,1)S(1)}, bf16[2,320,256]{2,1,0:T(8,128)(2,1)S(1)}, u32[]{:S(2)}, u32[]{:S(2)}) collective-permute-start(bf16[2,320,256]{2,1,0:T(8,128)(2,1)S(1)} %broadcast_select_fusion.refs_0_), channel_id=1, source_target_pairs={{0,2},{1,3},{2,0},{3,1},{4,6},{5,7},{6,4},{7,5},{8,10},{9,11},{10,... | collective-permute-start | bytes 983048 | tf_op jit(solution)/shard_map/ppermute | solution.py:44
  68.4 9.1 %collective-permute-start.6 = (bf16[2,320,256]{2,1,0:T(8,128)(2,1)S(1)}, bf16[2,320,256]{2,1,0:T(8,128)(2,1)S(1)}, u32[]{:S(2)}, u32[]{:S(2)}) collective-permute-start(bf16[2,320,256]{2,1,0:T(8,128)(2,1)S(1)} %broadcast_select_fusion.refs_0_), channel_id=1, source_target_pairs={{0,3},{1,0},{2,1},{3,2},{4,7},{5,4},{6,5},{7,6},{8,11},{9,8},{10,9... | collective-permute-start | bytes 983048 | tf_op jit(solution)/shard_map/ppermute | solution.py:44
  75.1 0.7 copy-start.7
  77.5 0.7 copy-start.9
  85.0 1.6 %copy-start.1 = (bf16[2176,512]{1,0:T(8,128)(2,1)S(1)}, bf16[2176,512]{1,0:T(8,128)(2,1)}, u32[]{:S(2)}) copy-start(bf16[2176,512]{1,0:T(8,128)(2,1)} %all-gather.3.cloned.1.call-done) | copy-start | bytes 6684676
  86.6 1.0 copy-start.8
  87.6 1.0 copy-start.10
  88.6 6.7 %copy-start.6 = (bf16[512,320]{0,1:T(8,128)(2,1)S(1)}, bf16[512,320]{0,1:T(8,128)(2,1)}, u32[]{:S(2)}) copy-start(bf16[512,320]{0,1:T(8,128)(2,1)} %param.14) | copy-start | bytes 983044
  90.9 4.4 %collective-permute-start.11 = (f32[448,512]{1,0:T(8,128)S(1)}, f32[448,512]{1,0:T(8,128)S(1)}, u32[]{:S(2)}, u32[]{:S(2)}) collective-permute-start(f32[448,512]{1,0:T(8,128)S(1)} %gradient.1.mine_ref), channel_id=1, source_target_pairs={{0,256},{1,257},{2,258},{3,259},{4,260},{5,261},{6,262},{7,263},{8... | collective-permute-start | bytes 2752520 | tf_op jit(solution)/shard_map/ppermute | solution.py:44
  114.7 11.8 %collective-permute-start.12 = (bf16[8,320]{1,0:T(8,128)(2,1)S(1)}, bf16[8,320]{1,0:T(8,128)(2,1)S(1)}, u32[]{:S(2)}, u32[]{:S(2)}) collective-permute-start(bf16[8,320]{1,0:T(8,128)(2,1)S(1)} %reduce_sum.9), channel_id=1, source_target_pairs={{0,0},{1,16},{2,32},{3,48},{4,64},{5,80},{6,96},{7,112},{8,128},{9... | collective-permute-start | bytes 15368 | tf_op jit(solution)/shard_map/ppermute | solution.py:44
Sparse Core Ops, SparseCore 0:
  33.2 51.8 all-gather.2

commit v19 on v17

--- a/solution.py
+++ b/solution.py
@@ -344,7 +344,6 @@
     place = jnp.stack([lax.axis_index(axis) for axis in AXES]).astype(jnp.int32)
 
     act = activations[0]
-    act_got = permute(act, to_partner)
     cut = cut_of(place, cotangent[0])
     own = permute(cut, cot_shifted)
     rows = attend(
@@ -357,6 +356,8 @@
         lengths,
         token_ids.T,
     )
+    act_tied, rows, _ = lax.optimization_barrier((act, rows, cut))
+    act_got = permute(act_tied, to_partner)
     rows_got = permute(rows, to_partner)
     base = base_of(place, act, act_got, rows, rows_got, own)
     chunks = lax.all_gather(base, "y", axis=0)

time: 139 us -> 142 us (1.022)
  local copies, waits for them, and re-layouts: 4.31 us -> 8.39 us
  starting transfers between devices: 27.1 us -> 25.6 us
    unnamed x26 -> x34, local copies, waits for them, and re-layouts: 3.41 us -> 7.5 us
    ppermute x12, waiting for transfers between devices: 46.9 us -> 50.5 us  [permute(): return lax.ppermute(value, AXES, pairs)]
    all_gather x1, waiting for transfers between devices: 6.95 us -> 3.55 us  [local(): chunks = lax.all_gather(base, 'y', axis=0)]
    ppermute x12, starting transfers between devices: 27.1 us -> 25.6 us  [permute(): return lax.ppermute(value, AXES, pairs)]
  transfers between devices with their start and end apart: 13 -> 13, of which waited for: 7 -> 7; matrix products, arithmetic and copies ran while one was open for 0% -> 1% of each run, Pallas kernels for 2% -> 0%
where the time goes in v19:
time: 142 us; the launch traced here: 140 us
  waiting for transfers between devices  54.1 us (38%)
  blocking collectives  29.3 us (21%)
  starting transfers between devices  25.6 us (18%)
  between operations  14.3 us (10%)
  local copies, waits for them, and re-layouts  8.39 us (6%)
  Pallas kernels  7.36 us (5%)
    ppermute x12, waiting for transfers between devices, permute(): return lax.ppermute(value, AXES, pairs)  50.5 us
    all_to_all x2, blocking collectives, gather(): return lax.all_to_all(value, axes, split_axis=0, concat_axis=0, tiled=True)  29.3 us
    ppermute x12, starting transfers between devices, permute(): return lax.ppermute(value, AXES, pairs)  25.6 us
    unnamed x34, local copies, waits for them, and re-layouts  7.5 us
    all_gather x1, waiting for transfers between devices, local(): chunks = lax.all_gather(base, 'y', axis=0)  3.55 us
  transfers between devices with their start and end apart: 13, of which 7 were waited for; matrix products, arithmetic and copies ran while one was open for 1% of the time, Pallas kernels for 0%

profile of v19, /device:TPU:56, one launch (start us, length us, event | category | flops | bytes accessed | tf_op | source)
XLA Modules:
  0.0 140.1 jit_solution(11426735220528756150)
XLA Ops:
  7.2 0.0 copy-start.15
  7.2 0.0 copy-start.16
  7.2 0.0 copy-start.13
  7.2 0.0 copy-start.12
  7.2 0.0 copy-start.14
  7.2 0.0 all-gather.3.cloned.1.call-start
  7.3 0.1 stack.32.place_ref
  7.4 0.0 copy-start
  7.4 1.7 %copy-done = bf16[1,256,5120]{2,1,0:T(8,128)(2,1)S(1)} copy-done((bf16[1,256,5120]{2,1,0:T(8,128)(2,1)S(1)}, bf16[1,256,5120]{2,1,0:T(8,128)(2,1)}, u32[]{:S(2)}) %copy-start) | copy-done | bytes 2621464
  9.1 0.0 copy-start.2
  9.1 0.0 copy-start.3
  9.1 0.8 cut.1
  9.9 0.0 copy-start.4
  9.9 0.0 copy-start.5
  9.9 0.0 copy-done.15
  9.9 0.0 copy-done.16
  9.9 0.0 copy-done.13
  9.9 0.0 copy-done.12
  9.9 0.0 copy-done.14
  9.9 0.4 copy-done.2
  10.3 0.3 copy-done.3
  10.6 1.0 attend.1.rows_ref
  11.7 0.0 copy-done.11
  11.7 1.3 collective-permute-start
  13.0 0.7 collective-permute-start.2
  13.7 1.3 collective-permute-start.1
  15.0 12.7 %collective-permute-done.1.rows_got = bf16[16,512]{1,0:T(8,128)(2,1)S(1)} collective-permute-done((bf16[16,512]{1,0:T(8,128)(2,1)S(1)}, bf16[16,512]{1,0:T(8,128)(2,1)S(1)}, u32[]{:S(2)}, u32[]{:S(2)}) %collective-permute-start.1) | collective-permute-done | bytes 16416 | tf_op jit(solution)/shard_map/ppermute | solution.py:44
  27.7 0.0 collective-permute-done.2._
  27.7 0.0 collective-permute-done.act_got
  27.7 1.3 base.1
  29.0 0.0 all-gather.3.cloned.1.call-update
  29.0 0.7 collective-permute-start.3
  29.7 0.0 collective-permute-done.3
  29.7 1.3 collective-permute-start.4
  31.0 0.0 copy-done.4
  31.1 1.3 collective-permute-start.8
  32.4 0.0 copy-done.5
  32.4 1.3 collective-permute-start.9
  33.7 16.6 %collective-permute-done.4 = bf16[2,320,256]{2,1,0:T(8,128)(2,1)} collective-permute-done((bf16[2,320,256]{2,1,0:T(8,128)(2,1)S(1)}, bf16[2,320,256]{2,1,0:T(8,128)(2,1)}, u32[]{:S(2)}, u32[]{:S(2)}) %collective-permute-start.4) | collective-permute-done | bytes 327712 | tf_op jit(solution)/shard_map/ppermute | solution.py:44
  50.2 1.0 broadcast_select_fusion.refs_0_
  51.3 2.5 %collective-permute-start.7 = (bf16[2,320,256]{2,1,0:T(8,128)(2,1)S(1)}, bf16[2,320,256]{2,1,0:T(8,128)(2,1)S(1)}, u32[]{:S(2)}, u32[]{:S(2)}) collective-permute-start(bf16[2,320,256]{2,1,0:T(8,128)(2,1)S(1)} %broadcast_select_fusion.refs_0_), channel_id=1, source_target_pairs={{0,1},{1,2},{2,3},{3,0},{4,5},{5,6},{6,7},{7,4},{8,9},{9,10},{10,1... | collective-permute-start | bytes 983048 | tf_op jit(solution)/shard_map/ppermute | solution.py:44
  53.8 6.9 %collective-permute-start.6 = (bf16[2,320,256]{2,1,0:T(8,128)(2,1)S(1)}, bf16[2,320,256]{2,1,0:T(8,128)(2,1)S(1)}, u32[]{:S(2)}, u32[]{:S(2)}) collective-permute-start(bf16[2,320,256]{2,1,0:T(8,128)(2,1)S(1)} %broadcast_select_fusion.refs_0_), channel_id=1, source_target_pairs={{0,2},{1,3},{2,0},{3,1},{4,6},{5,7},{6,4},{7,5},{8,10},{9,11},{10,... | collective-permute-start | bytes 983048 | tf_op jit(solution)/shard_map/ppermute | solution.py:44
  60.7 1.9 %collective-permute-start.5 = (bf16[2,320,256]{2,1,0:T(8,128)(2,1)S(1)}, bf16[2,320,256]{2,1,0:T(8,128)(2,1)S(1)}, u32[]{:S(2)}, u32[]{:S(2)}) collective-permute-start(bf16[2,320,256]{2,1,0:T(8,128)(2,1)S(1)} %broadcast_select_fusion.refs_0_), channel_id=1, source_target_pairs={{0,3},{1,0},{2,1},{3,2},{4,7},{5,4},{6,5},{7,6},{8,11},{9,8},{10,9... | collective-permute-start | bytes 983048 | tf_op jit(solution)/shard_map/ppermute | solution.py:44
  62.6 0.0 collective-permute-done.8.refs_4_.one_got
  62.6 0.0 collective-permute-done.9.refs_5_.two_got
  62.7 4.9 %collective-permute-done.7.refs_3_ = bf16[2,320,256]{2,1,0:T(8,128)(2,1)S(1)} collective-permute-done((bf16[2,320,256]{2,1,0:T(8,128)(2,1)S(1)}, bf16[2,320,256]{2,1,0:T(8,128)(2,1)S(1)}, u32[]{:S(2)}, u32[]{:S(2)}) %collective-permute-start.7) | collective-permute-done | bytes 327712 | tf_op jit(solution)/shard_map/ppermute | solution.py:44
  67.6 6.5 %collective-permute-done.6.refs_2_ = bf16[2,320,256]{2,1,0:T(8,128)(2,1)S(1)} collective-permute-done((bf16[2,320,256]{2,1,0:T(8,128)(2,1)S(1)}, bf16[2,320,256]{2,1,0:T(8,128)(2,1)S(1)}, u32[]{:S(2)}, u32[]{:S(2)}) %collective-permute-start.6) | collective-permute-done | bytes 327712 | tf_op jit(solution)/shard_map/ppermute | solution.py:44
  74.1 0.7 copy-done.7
  74.8 0.0 collective-permute-done.5.refs_1_
  74.8 0.7 copy-done.9
  75.5 3.6 %all-gather.3.cloned.1.call-done = bf16[2176,512]{1,0:T(8,128)(2,1)} async-done(((bf16[272,512]{1,0:T(8,128)(2,1)}), bf16[2176,512]{1,0:T(8,128)(2,1)}) %all-gather.3.cloned.1.call-update) | async-done | bytes 2228240 | tf_op jit(solution)/shard_map/all_gather | solution.py:363
  79.1 1.6 %copy-done.1 = bf16[2176,512]{1,0:T(8,128)(2,1)S(1)} copy-done((bf16[2176,512]{1,0:T(8,128)(2,1)S(1)}, bf16[2176,512]{1,0:T(8,128)(2,1)}, u32[]{:S(2)}) %copy-start.1) | copy-done | bytes 2228248
  80.7 1.0 copy-done.8
  81.7 1.0 copy-done.10
  82.7 2.3 %gradient.1.mine_ref = f32[448,512]{1,0:T(8,128)S(1)} custom-call(s32[5]{0:T(128)S(1)} %stack.32.place_ref, bf16[8,272,512]{2,1,0:T(8,128)(2,1)S(1)} %bitcast.22, bf16[2,320,256]{2,1,0:T(8,128)(2,1)S(1)} %broadcast_select_fusion.refs_0_, bf16[2,320,256]{2,1,0:T(8,128)(2,1)S(1)} %copy-done.10, bf16[2,320,256]{2,1,0:T(8,128)(2,1)S(1)} %copy-done.8, ...), custom_call_target="tpu_custom_call" | custom-call | tf_op jit(solution)/shard_map/gradient/pallas_call | solution.py:277
  85.0 1.9 %collective-permute-start.10 = (f32[448,512]{1,0:T(8,128)S(1)}, f32[448,512]{1,0:T(8,128)S(1)}, u32[]{:S(2)}, u32[]{:S(2)}) collective-permute-start(f32[448,512]{1,0:T(8,128)S(1)} %gradient.1.mine_ref), channel_id=1, source_target_pairs={{0,256},{1,257},{2,258},{3,259},{4,260},{5,261},{6,262},{7,263},{8... | collective-permute-start | bytes 2752520 | tf_op jit(solution)/shard_map/ppermute | solution.py:44
  86.9 2.4 %collective-permute-done.10.got_ref = f32[448,512]{1,0:T(8,128)S(1)} collective-permute-done((f32[448,512]{1,0:T(8,128)S(1)}, f32[448,512]{1,0:T(8,128)S(1)}, u32[]{:S(2)}, u32[]{:S(2)}) %collective-permute-start.10) | collective-permute-done | bytes 917536 | tf_op jit(solution)/shard_map/ppermute | solution.py:44
  89.4 0.0 copy-done.6
  89.4 2.0 %step.1 = (bf16[320,512]{1,0:T(8,128)(2,1)}, f32[16,8,320]{2,1,0:T(8,128)S(1)}) custom-call(s32[5]{0:T(128)S(1)} %stack.32.place_ref, f32[448,512]{1,0:T(8,128)S(1)} %gradient.1.mine_ref, f32[448,512]{1,0:T(8,128)S(1)} %collective-permute-done.10.got_ref, f32[320,512]{1,0:T(8,128)S(1)} %bitcast.26, f32[320,512]{1,0:T(8,128)S(1)} %collective-permute-done.8.refs_4_.one_got, ...), custom_call_target="tpu_custom_call" | custom-call | tf_op jit(solution)/shard_map/step/pallas_call | solution.py:316
  91.3 17.2 %all_to_all.10 = f32[16,8,320]{2,1,0:T(8,128)S(1)} all-to-all(f32[16,8,320]{2,1,0:T(8,128)S(1)} %get-tuple-element.15), channel_id=1, replica_groups=mesh['group'=2,'y'=8,'z_hi'=2,'z_lo'=4,'x'=4] {'z_lo','x'}, dimensions={0} | all-to-all | bytes 327680 | tf_op jit(solution)/shard_map/all_to_all | solution.py:48
  108.5 4.5 %collective-permute-start.11 = (bf16[8,320]{1,0:T(8,128)(2,1)S(1)}, bf16[8,320]{1,0:T(8,128)(2,1)S(1)}, u32[]{:S(2)}, u32[]{:S(2)}) collective-permute-start(bf16[8,320]{1,0:T(8,128)(2,1)S(1)} %reduce_sum.9), channel_id=1, source_target_pairs={{0,0},{1,16},{2,32},{3,48},{4,64},{5,80},{6,96},{7,112},{8,128},{9... | collective-permute-start | bytes 15368 | tf_op jit(solution)/shard_map/ppermute | solution.py:44
  113.0 7.3 %collective-permute-done.11 = bf16[8,320]{1,0:T(8,128)(2,1)S(1)} collective-permute-done((bf16[8,320]{1,0:T(8,128)(2,1)S(1)}, bf16[8,320]{1,0:T(8,128)(2,1)S(1)}, u32[]{:S(2)}, u32[]{:S(2)}) %collective-permute-start.11) | collective-permute-done | bytes 5152 | tf_op jit(solution)/shard_map/ppermute | solution.py:44
  120.4 12.1 %all_to_all.11 = bf16[16,8,320]{2,1,0:T(8,128)(2,1)S(1)} all-to-all(bf16[16,8,320]{2,1,0:T(8,128)(2,1)S(1)} %broadcast_in_dim.2), channel_id=1, replica_groups=mesh['group'=2,'y'=8,'z_hi'=2,'z_lo'=4,'x'=4] {'z_lo','x'}, dimensions={0} | all-to-all | bytes 163840 | tf_op jit(solution)/shard_map/all_to_all | solution.py:48
  132.5 0.8 reshape.12
  (11 shorter events, 0.1 us)
Async XLA Ops:
  7.2 2.7 %copy-start.15 = (s32[4,2]{0,1:T(2,128)S(1)}, s32[4,2]{0,1:T(2,128)}, u32[]{:S(2)}) copy-start(s32[4,2]{0,1:T(2,128)} %param.23) | copy-start | bytes 100
  7.2 2.7 %copy-start.16 = (s32[2]{0:T(128)S(1)}, s32[2]{0:T(128)}, u32[]{:S(2)}) copy-start(s32[2]{0:T(128)} %lengths_ref.1) | copy-start | bytes 28
  7.2 2.7 %copy-start.13 = (bf16[4,2,1024]{2,1,0:T(2,128)(2,1)S(1)}, bf16[4,2,1024]{2,1,0:T(2,128)(2,1)}, u32[]{:S(2)}) copy-start(bf16[4,2,1024]{2,1,0:T(2,128)(2,1)} %nv_ref.1) | copy-start | bytes 49156
  7.2 2.7 %copy-start.12 = (bf16[4,2,1024]{2,1,0:T(2,128)(2,1)S(1)}, bf16[4,2,1024]{2,1,0:T(2,128)(2,1)}, u32[]{:S(2)}) copy-start(bf16[4,2,1024]{2,1,0:T(2,128)(2,1)} %nk_ref.1) | copy-start | bytes 49156
  7.2 2.7 %copy-start.14 = (bf16[4,2,512]{2,1,0:T(2,128)(2,1)S(1)}, bf16[4,2,512]{2,1,0:T(2,128)(2,1)}, u32[]{:S(2)}) copy-start(bf16[4,2,512]{2,1,0:T(2,128)(2,1)} %q_ref.1) | copy-start | bytes 24580
  7.2 71.9 %all-gather.3.cloned.1.call-start = ((), (), s32[]{:S(2)}) async-start(), calls=%async_computation.2 | async-start | bytes 2506752 | tf_op jit(solution)/shard_map/all_gather | solution.py:363
  7.4 1.7 %copy-start = (bf16[1,256,5120]{2,1,0:T(8,128)(2,1)S(1)}, bf16[1,256,5120]{2,1,0:T(8,128)(2,1)}, u32[]{:S(2)}) copy-start(bf16[1,256,5120]{2,1,0:T(8,128)(2,1)} %param.13) | copy-start | bytes 7864324
  9.1 1.2 copy-start.2
  9.1 1.5 %copy-start.3 = (bf16[2,2048,128]{2,1,0:T(8,128)(2,1)S(1)}, bf16[2,2048,128]{2,1,0:T(8,128)(2,1)}, u32[]{:S(2)}) copy-start(bf16[2,2048,128]{2,1,0:T(8,128)(2,1)} %v_ref.1) | copy-start | bytes 3145732
  9.1 2.6 %copy-start.11 = (bf16[1,256,512]{2,1,0:T(8,128)(2,1)S(1)}, bf16[1,256,512]{2,1,0:T(8,128)(2,1)}, u32[]{:S(2)}) copy-start(bf16[1,256,512]{2,1,0:T(8,128)(2,1)} %param.12) | copy-start | bytes 786436
  9.9 21.2 %copy-start.4 = (f32[1,512,320]{1,2,0:T(8,128)S(1)}, f32[1,512,320]{1,2,0:T(8,128)}, u32[]{:S(2)}) copy-start(f32[1,512,320]{1,2,0:T(8,128)} %param.15) | copy-start | bytes 1966084
  9.9 22.5 %copy-start.5 = (f32[1,512,320]{1,2,0:T(8,128)S(1)}, f32[1,512,320]{1,2,0:T(8,128)}, u32[]{:S(2)}) copy-start(f32[1,512,320]{1,2,0:T(8,128)} %param.16) | copy-start | bytes 1966084
  11.7 16.0 %collective-permute-start = (bf16[256,512]{1,0:T(8,128)(2,1)S(1)}, bf16[256,512]{1,0:T(8,128)(2,1)S(1)}, u32[]{:S(2)}, u32[]{:S(2)}) collective-permute-start(bf16[256,512]{1,0:T(8,128)(2,1)S(1)} %bitcast.30), channel_id=1, source_target_pairs={{256,16},{257,17},{258,18},{259,19},{260,20},{261,21},{262,22},{26... | collective-permute-start | bytes 786440 | tf_op jit(solution)/shard_map/ppermute | solution.py:44
  13.0 14.7 %collective-permute-start.2 = (bf16[320,256]{1,0:T(8,128)(2,1)S(1)}, bf16[320,256]{1,0:T(8,128)(2,1)S(1)}, u32[]{:S(2)}, u32[]{:S(2)}) collective-permute-start(bf16[320,256]{1,0:T(8,128)(2,1)S(1)} %cut.1), channel_id=1, source_target_pairs={{256,352},{257,321},{258,290},{259,259},{260,116},{261,85},{262,54... | collective-permute-start | bytes 491528 | tf_op jit(solution)/shard_map/ppermute | solution.py:44
  13.7 14.0 %collective-permute-start.1 = (bf16[16,512]{1,0:T(8,128)(2,1)S(1)}, bf16[16,512]{1,0:T(8,128)(2,1)S(1)}, u32[]{:S(2)}, u32[]{:S(2)}) collective-permute-start(bf16[16,512]{1,0:T(8,128)(2,1)S(1)} %attend.1.rows_ref), channel_id=1, source_target_pairs={{256,16},{257,17},{258,18},{259,19},{260,20},{261,21},{262,22},{26... | collective-permute-start | bytes 49160 | tf_op jit(solution)/shard_map/ppermute | solution.py:44
  29.0 0.7 collective-permute-start.3
  29.7 20.5 %collective-permute-start.4 = (bf16[2,320,256]{2,1,0:T(8,128)(2,1)S(1)}, bf16[2,320,256]{2,1,0:T(8,128)(2,1)}, u32[]{:S(2)}, u32[]{:S(2)}) collective-permute-start(bf16[2,320,256]{2,1,0:T(8,128)(2,1)S(1)} %pad_maximum_fusion), channel_id=1, source_target_pairs={{4,0},{5,1},{6,2},{7,3},{12,8},{13,9},{14,10},{15,11},{20,16},{21,... | collective-permute-start | bytes 983048 | tf_op jit(solution)/shard_map/ppermute | solution.py:44
  31.1 31.6 %collective-permute-start.8 = (f32[320,512]{1,0:T(8,128)S(1)}, f32[320,512]{1,0:T(8,128)S(1)}, u32[]{:S(2)}, u32[]{:S(2)}) collective-permute-start(f32[320,512]{1,0:T(8,128)S(1)} %bitcast.25), channel_id=1, source_target_pairs={{256,0},{257,1},{258,2},{259,3},{260,4},{261,5},{262,6},{263,7},{2... | collective-permute-start | bytes 1966088 | tf_op jit(solution)/shard_map/ppermute | solution.py:44
  32.4 30.3 %collective-permute-start.9 = (f32[320,512]{1,0:T(8,128)S(1)}, f32[320,512]{1,0:T(8,128)S(1)}, u32[]{:S(2)}, u32[]{:S(2)}) collective-permute-start(f32[320,512]{1,0:T(8,128)S(1)} %bitcast.27), channel_id=1, source_target_pairs={{256,0},{257,1},{258,2},{259,3},{260,4},{261,5},{262,6},{263,7},{2... | collective-permute-start | bytes 1966088 | tf_op jit(solution)/shard_map/ppermute | solution.py:44
  51.3 16.3 %collective-permute-start.7 = (bf16[2,320,256]{2,1,0:T(8,128)(2,1)S(1)}, bf16[2,320,256]{2,1,0:T(8,128)(2,1)S(1)}, u32[]{:S(2)}, u32[]{:S(2)}) collective-permute-start(bf16[2,320,256]{2,1,0:T(8,128)(2,1)S(1)} %broadcast_select_fusion.refs_0_), channel_id=1, source_target_pairs={{0,1},{1,2},{2,3},{3,0},{4,5},{5,6},{6,7},{7,4},{8,9},{9,10},{10,1... | collective-permute-start | bytes 983048 | tf_op jit(solution)/shard_map/ppermute | solution.py:44
  53.8 20.3 %collective-permute-start.6 = (bf16[2,320,256]{2,1,0:T(8,128)(2,1)S(1)}, bf16[2,320,256]{2,1,0:T(8,128)(2,1)S(1)}, u32[]{:S(2)}, u32[]{:S(2)}) collective-permute-start(bf16[2,320,256]{2,1,0:T(8,128)(2,1)S(1)} %broadcast_select_fusion.refs_0_), channel_id=1, source_target_pairs={{0,2},{1,3},{2,0},{3,1},{4,6},{5,7},{6,4},{7,5},{8,10},{9,11},{10,... | collective-permute-start | bytes 983048 | tf_op jit(solution)/shard_map/ppermute | solution.py:44
  60.7 14.1 %collective-permute-start.5 = (bf16[2,320,256]{2,1,0:T(8,128)(2,1)S(1)}, bf16[2,320,256]{2,1,0:T(8,128)(2,1)S(1)}, u32[]{:S(2)}, u32[]{:S(2)}) collective-permute-start(bf16[2,320,256]{2,1,0:T(8,128)(2,1)S(1)} %broadcast_select_fusion.refs_0_), channel_id=1, source_target_pairs={{0,3},{1,0},{2,1},{3,2},{4,7},{5,4},{6,5},{7,6},{8,11},{9,8},{10,9... | collective-permute-start | bytes 983048 | tf_op jit(solution)/shard_map/ppermute | solution.py:44
  74.1 0.7 copy-start.7
  74.8 0.7 copy-start.9
  79.1 1.6 %copy-start.1 = (bf16[2176,512]{1,0:T(8,128)(2,1)S(1)}, bf16[2176,512]{1,0:T(8,128)(2,1)}, u32[]{:S(2)}) copy-start(bf16[2176,512]{1,0:T(8,128)(2,1)} %all-gather.3.cloned.1.call-done) | copy-start | bytes 6684676
  80.7 1.0 copy-start.8
  81.7 1.0 copy-start.10
  82.7 6.7 %copy-start.6 = (bf16[512,320]{0,1:T(8,128)(2,1)S(1)}, bf16[512,320]{0,1:T(8,128)(2,1)}, u32[]{:S(2)}) copy-start(bf16[512,320]{0,1:T(8,128)(2,1)} %param.14) | copy-start | bytes 983044
  85.0 4.4 %collective-permute-start.10 = (f32[448,512]{1,0:T(8,128)S(1)}, f32[448,512]{1,0:T(8,128)S(1)}, u32[]{:S(2)}, u32[]{:S(2)}) collective-permute-start(f32[448,512]{1,0:T(8,128)S(1)} %gradient.1.mine_ref), channel_id=1, source_target_pairs={{0,256},{1,257},{2,258},{3,259},{4,260},{5,261},{6,262},{7,263},{8... | collective-permute-start | bytes 2752520 | tf_op jit(solution)/shard_map/ppermute | solution.py:44
  108.5 11.8 %collective-permute-start.11 = (bf16[8,320]{1,0:T(8,128)(2,1)S(1)}, bf16[8,320]{1,0:T(8,128)(2,1)S(1)}, u32[]{:S(2)}, u32[]{:S(2)}) collective-permute-start(bf16[8,320]{1,0:T(8,128)(2,1)S(1)} %reduce_sum.9), channel_id=1, source_target_pairs={{0,0},{1,16},{2,32},{3,48},{4,64},{5,80},{6,96},{7,112},{8,128},{9... | collective-permute-start | bytes 15368 | tf_op jit(solution)/shard_map/ppermute | solution.py:44
Sparse Core Ops, SparseCore 0:
  29.1 49.9 all-gather.2

commit v20 on v17

--- a/solution.py
+++ b/solution.py
@@ -358,7 +358,7 @@
         token_ids.T,
     )
     rows_got = permute(rows, to_partner)
-    base = base_of(place, act, act_got, rows, rows_got, own)
+    base = base_of(place, act, act_got, rows, rows_got, cut)
     chunks = lax.all_gather(base, "y", axis=0)
 
     one, two = moment_one[0].T, moment_two[0].T

time: 139 us -> 147 us (1.058)
  the two profiles are of different devices: /device:TPU:56 before, /device:TPU:2 now
where the time goes in v20:
time: 147 us; the launch traced here: 146 us
  waiting for transfers between devices  41.1 us (28%)
  blocking collectives  37.7 us (26%)
  starting transfers between devices  31.4 us (21%)
  between operations  14.3 us (10%)
  local copies, waits for them, and re-layouts  13.6 us (9%)
  Pallas kernels  7.36 us (5%)
    ppermute x12, waiting for transfers between devices, permute(): return lax.ppermute(value, AXES, pairs)  41.1 us
    all_to_all x2, blocking collectives, gather(): return lax.all_to_all(value, axes, split_axis=0, concat_axis=0, tiled=True)  37.7 us
    ppermute x12, starting transfers between devices, permute(): return lax.ppermute(value, AXES, pairs)  31.4 us
    unnamed x34, local copies, waits for them, and re-layouts  12.7 us
  transfers between devices with their start and end apart: 13, of which 6 were waited for; matrix products, arithmetic and copies ran while one was open for 1% of the time, Pallas kernels for 1%

profile of v20, /device:TPU:2, one launch (start us, length us, event | category | flops | bytes accessed | tf_op | source)
XLA Modules:
  0.0 146.4 jit_solution(17149402636890423035)
XLA Ops:
  7.2 0.0 all-gather.3.cloned.1.call-start
  7.2 1.3 collective-permute-start
  8.5 0.0 copy-start.2
  8.5 1.2 copy-done.2
  9.7 0.0 copy-start.3
  9.7 1.2 copy-done.3
  11.0 0.0 copy-start.12
  11.0 0.7 copy-done.12
  11.7 0.0 copy-start.13
  11.7 0.7 copy-done.13
  12.4 0.0 copy-start.14
  12.4 0.7 copy-done.14
  13.1 0.0 copy-start.15
  13.1 0.7 copy-done.15
  13.8 0.0 copy-start.16
  13.8 0.7 copy-done.16
  14.4 0.0 copy-start.11
  14.4 0.0 copy-start.4
  14.4 0.0 copy-start.5
  14.4 1.0 attend.1.rows_ref
  15.5 1.3 collective-permute-start.1
  16.8 0.1 stack.32.place_ref
  16.9 0.0 copy-start
  16.9 1.7 %copy-done = bf16[1,256,5120]{2,1,0:T(8,128)(2,1)S(1)} copy-done((bf16[1,256,5120]{2,1,0:T(8,128)(2,1)S(1)}, bf16[1,256,5120]{2,1,0:T(8,128)(2,1)}, u32[]{:S(2)}) %copy-start) | copy-done | bytes 2621464
  18.6 0.8 cut.1._
  19.4 9.8 %collective-permute-done.1.rows_got = bf16[16,512]{1,0:T(8,128)(2,1)S(1)} collective-permute-done((bf16[16,512]{1,0:T(8,128)(2,1)S(1)}, bf16[16,512]{1,0:T(8,128)(2,1)S(1)}, u32[]{:S(2)}, u32[]{:S(2)}) %collective-permute-start.1) | collective-permute-done | bytes 16416 | tf_op jit(solution)/shard_map/ppermute | solution.py:44
  29.2 0.0 collective-permute-done.act_got
  29.2 0.0 copy-done.11
  29.2 1.3 base.1
  30.5 0.0 all-gather.3.cloned.1.call-update
  30.5 0.7 collective-permute-start.2
  31.2 0.0 collective-permute-done.2
  31.2 0.7 collective-permute-start.3
  31.9 0.0 collective-permute-done.3
  31.9 1.3 collective-permute-start.4
  33.2 0.0 copy-done.4
  33.3 1.3 collective-permute-start.8
  34.6 0.0 copy-done.5
  34.6 1.3 collective-permute-start.9
  35.9 22.5 %collective-permute-done.4 = bf16[2,320,256]{2,1,0:T(8,128)(2,1)} collective-permute-done((bf16[2,320,256]{2,1,0:T(8,128)(2,1)S(1)}, bf16[2,320,256]{2,1,0:T(8,128)(2,1)}, u32[]{:S(2)}, u32[]{:S(2)}) %collective-permute-start.4) | collective-permute-done | bytes 327712 | tf_op jit(solution)/shard_map/ppermute | solution.py:44
  58.4 1.0 broadcast_select_fusion.refs_0_
  59.4 3.7 %collective-permute-start.7 = (bf16[2,320,256]{2,1,0:T(8,128)(2,1)S(1)}, bf16[2,320,256]{2,1,0:T(8,128)(2,1)S(1)}, u32[]{:S(2)}, u32[]{:S(2)}) collective-permute-start(bf16[2,320,256]{2,1,0:T(8,128)(2,1)S(1)} %broadcast_select_fusion.refs_0_), channel_id=1, source_target_pairs={{0,1},{1,2},{2,3},{3,0},{4,5},{5,6},{6,7},{7,4},{8,9},{9,10},{10,1... | collective-permute-start | bytes 983048 | tf_op jit(solution)/shard_map/ppermute | solution.py:44
  63.1 4.6 %collective-permute-start.6 = (bf16[2,320,256]{2,1,0:T(8,128)(2,1)S(1)}, bf16[2,320,256]{2,1,0:T(8,128)(2,1)S(1)}, u32[]{:S(2)}, u32[]{:S(2)}) collective-permute-start(bf16[2,320,256]{2,1,0:T(8,128)(2,1)S(1)} %broadcast_select_fusion.refs_0_), channel_id=1, source_target_pairs={{0,2},{1,3},{2,0},{3,1},{4,6},{5,7},{6,4},{7,5},{8,10},{9,11},{10,... | collective-permute-start | bytes 983048 | tf_op jit(solution)/shard_map/ppermute | solution.py:44
  67.7 4.1 %collective-permute-start.5 = (bf16[2,320,256]{2,1,0:T(8,128)(2,1)S(1)}, bf16[2,320,256]{2,1,0:T(8,128)(2,1)S(1)}, u32[]{:S(2)}, u32[]{:S(2)}) collective-permute-start(bf16[2,320,256]{2,1,0:T(8,128)(2,1)S(1)} %broadcast_select_fusion.refs_0_), channel_id=1, source_target_pairs={{0,3},{1,0},{2,1},{3,2},{4,7},{5,4},{6,5},{7,6},{8,11},{9,8},{10,9... | collective-permute-start | bytes 983048 | tf_op jit(solution)/shard_map/ppermute | solution.py:44
  71.9 0.0 collective-permute-done.8.refs_4_.one_got
  71.9 0.0 collective-permute-done.9.refs_5_.two_got
  71.9 3.8 %collective-permute-done.7.refs_3_ = bf16[2,320,256]{2,1,0:T(8,128)(2,1)S(1)} collective-permute-done((bf16[2,320,256]{2,1,0:T(8,128)(2,1)S(1)}, bf16[2,320,256]{2,1,0:T(8,128)(2,1)S(1)}, u32[]{:S(2)}, u32[]{:S(2)}) %collective-permute-start.7) | collective-permute-done | bytes 327712 | tf_op jit(solution)/shard_map/ppermute | solution.py:44
  75.7 0.0 collective-permute-done.6.refs_2_
  75.7 0.7 copy-done.7
  76.4 0.7 collective-permute-done.5.refs_1_
  77.1 0.7 copy-done.9
  77.8 1.6 %copy-done.1 = bf16[2176,512]{1,0:T(8,128)(2,1)S(1)} copy-done((bf16[2176,512]{1,0:T(8,128)(2,1)S(1)}, bf16[2176,512]{1,0:T(8,128)(2,1)}, u32[]{:S(2)}) %copy-start.1) | copy-done | bytes 2228248
  79.5 1.0 copy-done.8
  80.4 1.0 copy-done.10
  81.4 2.3 %gradient.1.mine_ref = f32[448,512]{1,0:T(8,128)S(1)} custom-call(s32[5]{0:T(128)S(1)} %stack.32.place_ref, bf16[8,272,512]{2,1,0:T(8,128)(2,1)S(1)} %bitcast.22, bf16[2,320,256]{2,1,0:T(8,128)(2,1)S(1)} %broadcast_select_fusion.refs_0_, bf16[2,320,256]{2,1,0:T(8,128)(2,1)S(1)} %copy-done.10, bf16[2,320,256]{2,1,0:T(8,128)(2,1)S(1)} %copy-done.8, ...), custom_call_target="tpu_custom_call" | custom-call | tf_op jit(solution)/shard_map/gradient/pallas_call | solution.py:277
  83.7 3.0 %collective-permute-start.10 = (f32[448,512]{1,0:T(8,128)S(1)}, f32[448,512]{1,0:T(8,128)S(1)}, u32[]{:S(2)}, u32[]{:S(2)}) collective-permute-start(f32[448,512]{1,0:T(8,128)S(1)} %gradient.1.mine_ref), channel_id=1, source_target_pairs={{0,256},{1,257},{2,258},{3,259},{4,260},{5,261},{6,262},{7,263},{8... | collective-permute-start | bytes 2752520 | tf_op jit(solution)/shard_map/ppermute | solution.py:44
  86.7 2.1 %collective-permute-done.10.got_ref = f32[448,512]{1,0:T(8,128)S(1)} collective-permute-done((f32[448,512]{1,0:T(8,128)S(1)}, f32[448,512]{1,0:T(8,128)S(1)}, u32[]{:S(2)}, u32[]{:S(2)}) %collective-permute-start.10) | collective-permute-done | bytes 917536 | tf_op jit(solution)/shard_map/ppermute | solution.py:44
  88.8 0.0 copy-done.6
  88.8 1.9 %step.1 = (bf16[320,512]{1,0:T(8,128)(2,1)}, f32[16,8,320]{2,1,0:T(8,128)S(1)}) custom-call(s32[5]{0:T(128)S(1)} %stack.32.place_ref, f32[448,512]{1,0:T(8,128)S(1)} %gradient.1.mine_ref, f32[448,512]{1,0:T(8,128)S(1)} %collective-permute-done.10.got_ref, f32[320,512]{1,0:T(8,128)S(1)} %bitcast.24, f32[320,512]{1,0:T(8,128)S(1)} %collective-permute-done.8.refs_4_.one_got, ...), custom_call_target="tpu_custom_call" | custom-call | tf_op jit(solution)/shard_map/step/pallas_call | solution.py:316
  90.8 17.5 %all_to_all.10 = f32[16,8,320]{2,1,0:T(8,128)S(1)} all-to-all(f32[16,8,320]{2,1,0:T(8,128)S(1)} %get-tuple-element.11), channel_id=1, replica_groups=mesh['group'=2,'y'=8,'z_hi'=2,'z_lo'=4,'x'=4] {'z_lo','x'}, dimensions={0} | all-to-all | bytes 327680 | tf_op jit(solution)/shard_map/all_to_all | solution.py:48
  108.3 8.1 %collective-permute-start.11 = (bf16[8,320]{1,0:T(8,128)(2,1)S(1)}, bf16[8,320]{1,0:T(8,128)(2,1)S(1)}, u32[]{:S(2)}, u32[]{:S(2)}) collective-permute-start(bf16[8,320]{1,0:T(8,128)(2,1)S(1)} %reduce_sum.9), channel_id=1, source_target_pairs={{0,0},{1,16},{2,32},{3,48},{4,64},{5,80},{6,96},{7,112},{8,128},{9... | collective-permute-start | bytes 15368 | tf_op jit(solution)/shard_map/ppermute | solution.py:44
  116.5 2.2 %collective-permute-done.11 = bf16[8,320]{1,0:T(8,128)(2,1)S(1)} collective-permute-done((bf16[8,320]{1,0:T(8,128)(2,1)S(1)}, bf16[8,320]{1,0:T(8,128)(2,1)S(1)}, u32[]{:S(2)}, u32[]{:S(2)}) %collective-permute-start.11) | collective-permute-done | bytes 5152 | tf_op jit(solution)/shard_map/ppermute | solution.py:44
  118.7 20.1 %all_to_all.11 = bf16[16,8,320]{2,1,0:T(8,128)(2,1)S(1)} all-to-all(bf16[16,8,320]{2,1,0:T(8,128)(2,1)S(1)} %broadcast_in_dim.2), channel_id=1, replica_groups=mesh['group'=2,'y'=8,'z_hi'=2,'z_lo'=4,'x'=4] {'z_lo','x'}, dimensions={0} | all-to-all | bytes 163840 | tf_op jit(solution)/shard_map/all_to_all | solution.py:48
  138.8 0.8 reshape.12
  (11 shorter events, 0.1 us)
Async XLA Ops:
  7.2 70.7 %all-gather.3.cloned.1.call-start = ((), (), s32[]{:S(2)}) async-start(), calls=%async_computation.2 | async-start | bytes 2506752 | tf_op jit(solution)/shard_map/all_gather | solution.py:362
  7.2 22.0 %collective-permute-start = (bf16[256,512]{1,0:T(8,128)(2,1)}, bf16[256,512]{1,0:T(8,128)(2,1)S(1)}, u32[]{:S(2)}, u32[]{:S(2)}) collective-permute-start(bf16[256,512]{1,0:T(8,128)(2,1)} %bitcast.28), channel_id=1, source_target_pairs={{256,16},{257,17},{258,18},{259,19},{260,20},{261,21},{262,22},{26... | collective-permute-start | bytes 786440 | tf_op jit(solution)/shard_map/ppermute | solution.py:44
  8.5 1.2 copy-start.2
  9.7 1.2 copy-start.3
  11.0 0.7 copy-start.12
  11.7 0.7 copy-start.13
  12.4 0.7 copy-start.14
  13.1 0.7 copy-start.15
  13.8 0.7 copy-start.16
  14.4 14.8 %copy-start.11 = (bf16[1,256,512]{2,1,0:T(8,128)(2,1)S(1)}, bf16[1,256,512]{2,1,0:T(8,128)(2,1)}, u32[]{:S(2)}) copy-start(bf16[1,256,512]{2,1,0:T(8,128)(2,1)} %param.12) | copy-start | bytes 786436
  14.4 18.8 %copy-start.4 = (f32[1,512,320]{1,2,0:T(8,128)S(1)}, f32[1,512,320]{1,2,0:T(8,128)}, u32[]{:S(2)}) copy-start(f32[1,512,320]{1,2,0:T(8,128)} %param.15) | copy-start | bytes 1966084
  14.4 20.1 %copy-start.5 = (f32[1,512,320]{1,2,0:T(8,128)S(1)}, f32[1,512,320]{1,2,0:T(8,128)}, u32[]{:S(2)}) copy-start(f32[1,512,320]{1,2,0:T(8,128)} %param.16) | copy-start | bytes 1966084
  15.5 13.7 %collective-permute-start.1 = (bf16[16,512]{1,0:T(8,128)(2,1)S(1)}, bf16[16,512]{1,0:T(8,128)(2,1)S(1)}, u32[]{:S(2)}, u32[]{:S(2)}) collective-permute-start(bf16[16,512]{1,0:T(8,128)(2,1)S(1)} %attend.1.rows_ref), channel_id=1, source_target_pairs={{256,16},{257,17},{258,18},{259,19},{260,20},{261,21},{262,22},{26... | collective-permute-start | bytes 49160 | tf_op jit(solution)/shard_map/ppermute | solution.py:44
  16.9 1.7 %copy-start = (bf16[1,256,5120]{2,1,0:T(8,128)(2,1)S(1)}, bf16[1,256,5120]{2,1,0:T(8,128)(2,1)}, u32[]{:S(2)}) copy-start(bf16[1,256,5120]{2,1,0:T(8,128)(2,1)} %param.13) | copy-start | bytes 7864324
  30.5 0.7 collective-permute-start.2
  31.2 0.7 collective-permute-start.3
  31.9 26.4 %collective-permute-start.4 = (bf16[2,320,256]{2,1,0:T(8,128)(2,1)S(1)}, bf16[2,320,256]{2,1,0:T(8,128)(2,1)}, u32[]{:S(2)}, u32[]{:S(2)}) collective-permute-start(bf16[2,320,256]{2,1,0:T(8,128)(2,1)S(1)} %pad_maximum_fusion), channel_id=1, source_target_pairs={{4,0},{5,1},{6,2},{7,3},{12,8},{13,9},{14,10},{15,11},{20,16},{21,... | collective-permute-start | bytes 983048 | tf_op jit(solution)/shard_map/ppermute | solution.py:44
  33.3 38.6 %collective-permute-start.8 = (f32[320,512]{1,0:T(8,128)S(1)}, f32[320,512]{1,0:T(8,128)S(1)}, u32[]{:S(2)}, u32[]{:S(2)}) collective-permute-start(f32[320,512]{1,0:T(8,128)S(1)} %bitcast.23), channel_id=1, source_target_pairs={{256,0},{257,1},{258,2},{259,3},{260,4},{261,5},{262,6},{263,7},{2... | collective-permute-start | bytes 1966088 | tf_op jit(solution)/shard_map/ppermute | solution.py:44
  34.6 37.3 %collective-permute-start.9 = (f32[320,512]{1,0:T(8,128)S(1)}, f32[320,512]{1,0:T(8,128)S(1)}, u32[]{:S(2)}, u32[]{:S(2)}) collective-permute-start(f32[320,512]{1,0:T(8,128)S(1)} %bitcast.25), channel_id=1, source_target_pairs={{256,0},{257,1},{258,2},{259,3},{260,4},{261,5},{262,6},{263,7},{2... | collective-permute-start | bytes 1966088 | tf_op jit(solution)/shard_map/ppermute | solution.py:44
  59.4 16.3 %collective-permute-start.7 = (bf16[2,320,256]{2,1,0:T(8,128)(2,1)S(1)}, bf16[2,320,256]{2,1,0:T(8,128)(2,1)S(1)}, u32[]{:S(2)}, u32[]{:S(2)}) collective-permute-start(bf16[2,320,256]{2,1,0:T(8,128)(2,1)S(1)} %broadcast_select_fusion.refs_0_), channel_id=1, source_target_pairs={{0,1},{1,2},{2,3},{3,0},{4,5},{5,6},{6,7},{7,4},{8,9},{9,10},{10,1... | collective-permute-start | bytes 983048 | tf_op jit(solution)/shard_map/ppermute | solution.py:44
  63.1 12.5 %collective-permute-start.6 = (bf16[2,320,256]{2,1,0:T(8,128)(2,1)S(1)}, bf16[2,320,256]{2,1,0:T(8,128)(2,1)S(1)}, u32[]{:S(2)}, u32[]{:S(2)}) collective-permute-start(bf16[2,320,256]{2,1,0:T(8,128)(2,1)S(1)} %broadcast_select_fusion.refs_0_), channel_id=1, source_target_pairs={{0,2},{1,3},{2,0},{3,1},{4,6},{5,7},{6,4},{7,5},{8,10},{9,11},{10,... | collective-permute-start | bytes 983048 | tf_op jit(solution)/shard_map/ppermute | solution.py:44
  67.7 9.4 %collective-permute-start.5 = (bf16[2,320,256]{2,1,0:T(8,128)(2,1)S(1)}, bf16[2,320,256]{2,1,0:T(8,128)(2,1)S(1)}, u32[]{:S(2)}, u32[]{:S(2)}) collective-permute-start(bf16[2,320,256]{2,1,0:T(8,128)(2,1)S(1)} %broadcast_select_fusion.refs_0_), channel_id=1, source_target_pairs={{0,3},{1,0},{2,1},{3,2},{4,7},{5,4},{6,5},{7,6},{8,11},{9,8},{10,9... | collective-permute-start | bytes 983048 | tf_op jit(solution)/shard_map/ppermute | solution.py:44
  75.7 0.7 copy-start.7
  77.1 0.7 copy-start.9
  77.8 1.6 %copy-start.1 = (bf16[2176,512]{1,0:T(8,128)(2,1)S(1)}, bf16[2176,512]{1,0:T(8,128)(2,1)}, u32[]{:S(2)}) copy-start(bf16[2176,512]{1,0:T(8,128)(2,1)} %all-gather.3.cloned.1.call-done) | copy-start | bytes 6684676
  79.5 1.0 copy-start.8
  80.4 1.0 copy-start.10
  81.4 7.4 %copy-start.6 = (bf16[512,320]{0,1:T(8,128)(2,1)S(1)}, bf16[512,320]{0,1:T(8,128)(2,1)}, u32[]{:S(2)}) copy-start(bf16[512,320]{0,1:T(8,128)(2,1)} %param.14) | copy-start | bytes 983044
  83.7 5.1 %collective-permute-start.10 = (f32[448,512]{1,0:T(8,128)S(1)}, f32[448,512]{1,0:T(8,128)S(1)}, u32[]{:S(2)}, u32[]{:S(2)}) collective-permute-start(f32[448,512]{1,0:T(8,128)S(1)} %gradient.1.mine_ref), channel_id=1, source_target_pairs={{0,256},{1,257},{2,258},{3,259},{4,260},{5,261},{6,262},{7,263},{8... | collective-permute-start | bytes 2752520 | tf_op jit(solution)/shard_map/ppermute | solution.py:44
  108.3 10.3 %collective-permute-start.11 = (bf16[8,320]{1,0:T(8,128)(2,1)S(1)}, bf16[8,320]{1,0:T(8,128)(2,1)S(1)}, u32[]{:S(2)}, u32[]{:S(2)}) collective-permute-start(bf16[8,320]{1,0:T(8,128)(2,1)S(1)} %reduce_sum.9), channel_id=1, source_target_pairs={{0,0},{1,16},{2,32},{3,48},{4,64},{5,80},{6,96},{7,112},{8,128},{9... | collective-permute-start | bytes 15368 | tf_op jit(solution)/shard_map/ppermute | solution.py:44
Sparse Core Ops, SparseCore 0:
  30.6 43.9 all-gather.2

commit v21 on v20

--- a/solution.py
+++ b/solution.py
@@ -89,7 +89,7 @@
 
 
 def attend_kernel(
-    head_ref, lengths_ref, ids_ref, q_ref, k_ref, v_ref, nk_ref, nv_ref, out_ref, q_rows, nk_rows, nv_rows
+    head_ref, lengths_ref, ids_ref, q_ref, k_ref, v_ref, nk_ref, nv_ref, _, out_ref, q_rows, nk_rows, nv_rows
 ):
     for t in range(STEPS):
         place = slice(2 * t, 2 * t + 2)
@@ -146,7 +146,7 @@
     out_ref[...] = jnp.concatenate([flat, jnp.zeros_like(flat)], axis=0).astype(bf16)
 
 
-def attend(head, queries, cache_keys, cache_values, new_keys, new_values, lengths, ids):
+def attend(head, queries, cache_keys, cache_values, new_keys, new_values, lengths, ids, after):
     whole = lambda *shape: pl.BlockSpec(shape, lambda i, *_: (0,) * len(shape))
     cache = pl.BlockSpec((2, CACHE, HD), lambda i, m, *_: (0, m[0], 0))
     fresh = pl.BlockSpec((STEPS, 2, HD), lambda i, m, *_: (0, 0, m[0]))
@@ -156,7 +156,7 @@
         grid_spec=pltpu.PrefetchScalarGridSpec(
             num_scalar_prefetch=3,
             grid=(1,),
-            in_specs=[whole(STEPS, 2, FEAT), cache, cache, fresh, fresh],
+            in_specs=[whole(STEPS, 2, FEAT), cache, cache, fresh, fresh, pl.BlockSpec(memory_space=pl.ANY)],
             out_specs=whole(PAD, FEAT),
             scratch_shapes=[
                 pltpu.VMEM((ROWS, FEAT), f32),
@@ -166,7 +166,7 @@
         ),
         compiler_params=SMALL,
         name="attend",
-    )(head, lengths, ids, queries, cache_keys, cache_values, new_keys, new_values)
+    )(head, lengths, ids, queries, cache_keys, cache_values, new_keys, new_values, after)
 
 
 VMEM = pl.BlockSpec(memory_space=pltpu.VMEM)
@@ -201,7 +201,7 @@
     )(place, cot)
 
 
-def base_kernel(place_ref, act_ref, act_got, rows_ref, rows_got, _, out_ref):
+def base_kernel(place_ref, act_ref, act_got, rows_ref, rows_got, out_ref):
     @pl.when(place_ref[0] == 1)
     def _():
         out_ref[:TOK, :] = act_ref[...]
@@ -217,7 +217,7 @@
     return pl.pallas_call(
         base_kernel,
         out_shape=jax.ShapeDtypeStruct((TOK + PAD, FEAT), bf16),
-        in_specs=[SMEM] + [VMEM] * 4 + [HBM],
+        in_specs=[SMEM] + [VMEM] * 4,
         out_specs=VMEM,
         compiler_params=SMALL,
         name="base",
@@ -356,22 +356,24 @@
         new_values,
         lengths,
         token_ids.T,
+        cut,
     )
     rows_got = permute(rows, to_partner)
-    base = base_of(place, act, act_got, rows, rows_got, cut)
+    base = base_of(place, act, act_got, rows, rows_got)
     chunks = lax.all_gather(base, "y", axis=0)
 
     one, two = moment_one[0].T, moment_two[0].T
+    one_tied, two_tied, _ = lax.optimization_barrier((one, two, base))
     own, _ = lax.optimization_barrier((own, base))
     pair = jnp.stack([own, permute(own, along_zl(2))])
     pair_got = permute(pair, along_zl(1))
     pair = jnp.where(place[0] == keeper(place[3]), pair, pair_got)
     blocks = [pair] + [permute(pair, along_x(step)) for step in (1, 2, -1)]
-    one_tied, two_tied, _ = lax.optimization_barrier((one, two, base))
     one_got = permute(one_tied, to_rollout)
     two_got = permute(two_tied, to_rollout)
 
-    mine = gradient(place, chunks, blocks, (one_got, two_got))
+    chunks, one_got, two_got = lax.optimization_barrier((chunks, one_got, two_got))
+    mine = gradient(place, chunks, blocks, ())
     got = permute(mine, other_core)
     update, partial = step(place, mine, got, one, one_got, two, two_got, weight.T)
 

time: 147 us -> 143 us (0.973)
  local copies, waits for them, and re-layouts: 13.6 us -> 5 us
  waiting for transfers between devices: 41.1 us -> 44.9 us
  blocking collectives: 37.7 us -> 39.2 us
    unnamed x34 -> x28, local copies, waits for them, and re-layouts: 12.7 us -> 4.11 us
    all_gather x1, waiting for transfers between devices: 0.01 us -> 2.76 us  [local(): chunks = lax.all_gather(base, 'y', axis=0)]
    all_to_all x2, blocking collectives: 37.7 us -> 39.2 us  [gather(): return lax.all_to_all(value, axes, split_axis=0, concat_axis=0, tiled=True)]
where the time goes in v21:
time: 143 us
  waiting for transfers between devices  44.9 us (31%)
  blocking collectives  39.2 us (27%)
  starting transfers between devices  30.1 us (21%)
  between operations  14.4 us (10%)
  Pallas kernels  7.87 us (6%)
  local copies, waits for them, and re-layouts  5 us (3%)
    ppermute x12, waiting for transfers between devices, permute(): return lax.ppermute(value, AXES, pairs)  42.1 us
    all_to_all x2, blocking collectives, gather(): return lax.all_to_all(value, axes, split_axis=0, concat_axis=0, tiled=True)  39.2 us
    ppermute x12, starting transfers between devices, permute(): return lax.ppermute(value, AXES, pairs)  30.1 us
    unnamed x28, local copies, waits for them, and re-layouts  4.11 us
  transfers between devices with their start and end apart: 13, of which 6 were waited for; matrix products, arithmetic and copies ran while one was open for 1% of the time, Pallas kernels for 1%

profile of v21, /device:TPU:2, one launch (start us, length us, event | category | flops | bytes accessed | tf_op | source)
XLA Modules:
  0.0 142.5 jit_solution(13407711899470841868)
XLA Ops:
  7.2 0.0 copy-start.11
  7.2 0.0 copy-start.12
  7.2 0.0 copy-start.9
  7.2 0.0 copy-start.8
  7.2 0.0 copy-start.10
  7.2 0.0 all-gather.3.cloned.1.call-start
  7.3 1.3 collective-permute-start
  8.6 0.1 stack.32.place_ref
  8.7 0.0 copy-start
  8.7 1.7 %copy-done = bf16[1,256,5120]{2,1,0:T(8,128)(2,1)S(1)} copy-done((bf16[1,256,5120]{2,1,0:T(8,128)(2,1)S(1)}, bf16[1,256,5120]{2,1,0:T(8,128)(2,1)}, u32[]{:S(2)}) %copy-start) | copy-done | bytes 2621464
  10.4 0.0 copy-start.2
  10.4 0.0 copy-start.3
  10.4 0.0 copy-start.7
  10.4 0.8 cut.1._
  11.2 0.0 copy-start.4
  11.2 0.0 copy-start.5
  11.2 0.0 copy-done.11
  11.2 0.0 copy-done.12
  11.2 0.0 copy-done.9
  11.2 0.0 copy-done.8
  11.2 0.0 copy-done.10
  11.2 0.4 copy-done.2
  11.6 0.3 copy-done.3
  11.9 1.0 attend.1.rows_ref
  13.0 1.3 collective-permute-start.1
  14.3 10.0 %collective-permute-done.1.rows_got = bf16[16,512]{1,0:T(8,128)(2,1)S(1)} collective-permute-done((bf16[16,512]{1,0:T(8,128)(2,1)S(1)}, bf16[16,512]{1,0:T(8,128)(2,1)S(1)}, u32[]{:S(2)}, u32[]{:S(2)}) %collective-permute-start.1) | collective-permute-done | bytes 16416 | tf_op jit(solution)/shard_map/ppermute | solution.py:44
  24.3 0.0 collective-permute-done.act_got
  24.3 0.0 copy-done.7
  24.3 1.3 base.1
  25.6 0.0 all-gather.3.cloned.1.call-update
  25.6 0.7 collective-permute-start.4
  26.3 0.0 collective-permute-done.4
  26.3 0.7 collective-permute-start.5
  27.0 0.0 collective-permute-done.5
  27.0 0.0 copy-start.13
  27.0 1.3 collective-permute-start.6
  28.3 0.0 copy-done.13
  28.3 0.0 copy-done.4
  28.4 1.3 collective-permute-start.2
  29.7 0.0 copy-done.5
  29.7 1.3 collective-permute-start.3
  31.0 0.0 copy-start.6
  31.0 25.1 %collective-permute-done.6 = bf16[2,320,256]{2,1,0:T(8,128)(2,1)} collective-permute-done((bf16[2,320,256]{2,1,0:T(8,128)(2,1)S(1)}, bf16[2,320,256]{2,1,0:T(8,128)(2,1)}, u32[]{:S(2)}, u32[]{:S(2)}) %collective-permute-start.6) | collective-permute-done | bytes 327712 | tf_op jit(solution)/shard_map/ppermute | solution.py:44
  56.1 1.1 broadcast_select_fusion.refs_0_
  57.1 2.4 %collective-permute-start.9 = (bf16[2,320,256]{2,1,0:T(8,128)(2,1)S(1)}, bf16[2,320,256]{2,1,0:T(8,128)(2,1)}, u32[]{:S(2)}, u32[]{:S(2)}) collective-permute-start(bf16[2,320,256]{2,1,0:T(8,128)(2,1)S(1)} %broadcast_select_fusion.refs_0_), channel_id=1, source_target_pairs={{0,1},{1,2},{2,3},{3,0},{4,5},{5,6},{6,7},{7,4},{8,9},{9,10},{10,1... | collective-permute-start | bytes 983048 | tf_op jit(solution)/shard_map/ppermute | solution.py:44
  59.5 5.9 %collective-permute-start.8 = (bf16[2,320,256]{2,1,0:T(8,128)(2,1)S(1)}, bf16[2,320,256]{2,1,0:T(8,128)(2,1)}, u32[]{:S(2)}, u32[]{:S(2)}) collective-permute-start(bf16[2,320,256]{2,1,0:T(8,128)(2,1)S(1)} %broadcast_select_fusion.refs_0_), channel_id=1, source_target_pairs={{0,2},{1,3},{2,0},{3,1},{4,6},{5,7},{6,4},{7,5},{8,10},{9,11},{10,... | collective-permute-start | bytes 983048 | tf_op jit(solution)/shard_map/ppermute | solution.py:44
  65.5 4.0 %collective-permute-start.7 = (bf16[2,320,256]{2,1,0:T(8,128)(2,1)S(1)}, bf16[2,320,256]{2,1,0:T(8,128)(2,1)}, u32[]{:S(2)}, u32[]{:S(2)}) collective-permute-start(bf16[2,320,256]{2,1,0:T(8,128)(2,1)S(1)} %broadcast_select_fusion.refs_0_), channel_id=1, source_target_pairs={{0,3},{1,0},{2,1},{3,2},{4,7},{5,4},{6,5},{7,6},{8,11},{9,8},{10,9... | collective-permute-start | bytes 983048 | tf_op jit(solution)/shard_map/ppermute | solution.py:44
  69.5 0.0 collective-permute-done.2.one_got
  69.5 0.0 collective-permute-done.3.two_got
  69.5 2.8 %all-gather.3.cloned.1.call-done = bf16[2176,512]{1,0:T(8,128)(2,1)} async-done(((bf16[272,512]{1,0:T(8,128)(2,1)}), bf16[2176,512]{1,0:T(8,128)(2,1)}) %all-gather.3.cloned.1.call-update) | async-done | bytes 2228240 | tf_op jit(solution)/shard_map/all_gather | solution.py:363
  72.3 0.0 collective-permute-done.9.refs_3_
  72.3 0.0 collective-permute-done.8.refs_2_
  72.3 2.3 %collective-permute-done.7.refs_1_ = bf16[2,320,256]{2,1,0:T(8,128)(2,1)} collective-permute-done((bf16[2,320,256]{2,1,0:T(8,128)(2,1)S(1)}, bf16[2,320,256]{2,1,0:T(8,128)(2,1)}, u32[]{:S(2)}, u32[]{:S(2)}) %collective-permute-start.7) | collective-permute-done | bytes 327712 | tf_op jit(solution)/shard_map/ppermute | solution.py:44
  74.5 1.6 %copy-done.1 = bf16[2176,512]{1,0:T(8,128)(2,1)S(1)} copy-done((bf16[2176,512]{1,0:T(8,128)(2,1)S(1)}, bf16[2176,512]{1,0:T(8,128)(2,1)}, u32[]{:S(2)}) %copy-start.1) | copy-done | bytes 2228248
  76.2 2.8 %gradient.1.mine_ref = f32[448,512]{1,0:T(8,128)S(1)} custom-call(s32[5]{0:T(128)S(1)} %stack.32.place_ref, bf16[8,272,512]{2,1,0:T(8,128)(2,1)S(1)} %bitcast.22, bf16[2,320,256]{2,1,0:T(8,128)(2,1)S(1)} %broadcast_select_fusion.refs_0_, bf16[2,320,256]{2,1,0:T(8,128)(2,1)} %collective-permute-done.7.refs_1_, ...), custom_call_target="tpu_custom_call" | custom-call | tf_op jit(solution)/shard_map/gradient/pallas_call | solution.py:277
  79.0 1.9 %collective-permute-start.10 = (f32[448,512]{1,0:T(8,128)S(1)}, f32[448,512]{1,0:T(8,128)S(1)}, u32[]{:S(2)}, u32[]{:S(2)}) collective-permute-start(f32[448,512]{1,0:T(8,128)S(1)} %gradient.1.mine_ref), channel_id=1, source_target_pairs={{0,256},{1,257},{2,258},{3,259},{4,260},{5,261},{6,262},{7,263},{8... | collective-permute-start | bytes 2752520 | tf_op jit(solution)/shard_map/ppermute | solution.py:44
  80.9 2.4 %collective-permute-done.10.got_ref = f32[448,512]{1,0:T(8,128)S(1)} collective-permute-done((f32[448,512]{1,0:T(8,128)S(1)}, f32[448,512]{1,0:T(8,128)S(1)}, u32[]{:S(2)}, u32[]{:S(2)}) %collective-permute-start.10) | collective-permute-done | bytes 917536 | tf_op jit(solution)/shard_map/ppermute | solution.py:44
  83.4 0.0 copy-done.6
  83.4 1.9 %step.1 = (bf16[320,512]{1,0:T(8,128)(2,1)}, f32[16,8,320]{2,1,0:T(8,128)S(1)}) custom-call(s32[5]{0:T(128)S(1)} %stack.32.place_ref, f32[448,512]{1,0:T(8,128)S(1)} %gradient.1.mine_ref, f32[448,512]{1,0:T(8,128)S(1)} %collective-permute-done.10.got_ref, f32[320,512]{1,0:T(8,128)S(1)} %bitcast.24, f32[320,512]{1,0:T(8,128)S(1)} %collective-permute-done.2.one_got, ...), custom_call_target="tpu_custom_call" | custom-call | tf_op jit(solution)/shard_map/step/pallas_call | solution.py:316
  85.3 18.6 %all_to_all.10 = f32[16,8,320]{2,1,0:T(8,128)S(1)} all-to-all(f32[16,8,320]{2,1,0:T(8,128)S(1)} %get-tuple-element.17), channel_id=1, replica_groups=mesh['group'=2,'y'=8,'z_hi'=2,'z_lo'=4,'x'=4] {'z_lo','x'}, dimensions={0} | all-to-all | bytes 327680 | tf_op jit(solution)/shard_map/all_to_all | solution.py:48
  104.0 8.1 %collective-permute-start.11 = (bf16[8,320]{1,0:T(8,128)(2,1)S(1)}, bf16[8,320]{1,0:T(8,128)(2,1)S(1)}, u32[]{:S(2)}, u32[]{:S(2)}) collective-permute-start(bf16[8,320]{1,0:T(8,128)(2,1)S(1)} %reduce_sum.9), channel_id=1, source_target_pairs={{0,0},{1,16},{2,32},{3,48},{4,64},{5,80},{6,96},{7,112},{8,128},{9... | collective-permute-start | bytes 15368 | tf_op jit(solution)/shard_map/ppermute | solution.py:44
  112.0 2.3 %collective-permute-done.11 = bf16[8,320]{1,0:T(8,128)(2,1)S(1)} collective-permute-done((bf16[8,320]{1,0:T(8,128)(2,1)S(1)}, bf16[8,320]{1,0:T(8,128)(2,1)S(1)}, u32[]{:S(2)}, u32[]{:S(2)}) %collective-permute-start.11) | collective-permute-done | bytes 5152 | tf_op jit(solution)/shard_map/ppermute | solution.py:44
  114.3 20.5 %all_to_all.11 = bf16[16,8,320]{2,1,0:T(8,128)(2,1)S(1)} all-to-all(bf16[16,8,320]{2,1,0:T(8,128)(2,1)S(1)} %broadcast_in_dim.2), channel_id=1, replica_groups=mesh['group'=2,'y'=8,'z_hi'=2,'z_lo'=4,'x'=4] {'z_lo','x'}, dimensions={0} | all-to-all | bytes 163840 | tf_op jit(solution)/shard_map/all_to_all | solution.py:48
  134.9 0.8 reshape.12
  (5 shorter events, 0.1 us)
Async XLA Ops:
  7.2 4.0 %copy-start.11 = (s32[4,2]{0,1:T(2,128)S(1)}, s32[4,2]{0,1:T(2,128)}, u32[]{:S(2)}) copy-start(s32[4,2]{0,1:T(2,128)} %param.23) | copy-start | bytes 100
  7.2 4.0 %copy-start.12 = (s32[2]{0:T(128)S(1)}, s32[2]{0:T(128)}, u32[]{:S(2)}) copy-start(s32[2]{0:T(128)} %lengths_ref.1) | copy-start | bytes 28
  7.2 4.0 %copy-start.9 = (bf16[4,2,1024]{2,1,0:T(2,128)(2,1)S(1)}, bf16[4,2,1024]{2,1,0:T(2,128)(2,1)}, u32[]{:S(2)}) copy-start(bf16[4,2,1024]{2,1,0:T(2,128)(2,1)} %nv_ref.1) | copy-start | bytes 49156
  7.2 4.0 %copy-start.8 = (bf16[4,2,1024]{2,1,0:T(2,128)(2,1)S(1)}, bf16[4,2,1024]{2,1,0:T(2,128)(2,1)}, u32[]{:S(2)}) copy-start(bf16[4,2,1024]{2,1,0:T(2,128)(2,1)} %nk_ref.1) | copy-start | bytes 49156
  7.2 4.0 %copy-start.10 = (bf16[4,2,512]{2,1,0:T(2,128)(2,1)S(1)}, bf16[4,2,512]{2,1,0:T(2,128)(2,1)}, u32[]{:S(2)}) copy-start(bf16[4,2,512]{2,1,0:T(2,128)(2,1)} %q_ref.1) | copy-start | bytes 24580
  7.2 65.1 %all-gather.3.cloned.1.call-start = ((), (), s32[]{:S(2)}) async-start(), calls=%async_computation.2 | async-start | bytes 2506752 | tf_op jit(solution)/shard_map/all_gather | solution.py:363
  7.3 17.0 %collective-permute-start = (bf16[256,512]{1,0:T(8,128)(2,1)}, bf16[256,512]{1,0:T(8,128)(2,1)S(1)}, u32[]{:S(2)}, u32[]{:S(2)}) collective-permute-start(bf16[256,512]{1,0:T(8,128)(2,1)} %bitcast.28), channel_id=1, source_target_pairs={{256,16},{257,17},{258,18},{259,19},{260,20},{261,21},{262,22},{26... | collective-permute-start | bytes 786440 | tf_op jit(solution)/shard_map/ppermute | solution.py:44
  8.7 1.7 %copy-start = (bf16[1,256,5120]{2,1,0:T(8,128)(2,1)S(1)}, bf16[1,256,5120]{2,1,0:T(8,128)(2,1)}, u32[]{:S(2)}) copy-start(bf16[1,256,5120]{2,1,0:T(8,128)(2,1)} %param.13) | copy-start | bytes 7864324
  10.4 1.2 copy-start.2
  10.4 1.5 %copy-start.3 = (bf16[2,2048,128]{2,1,0:T(8,128)(2,1)S(1)}, bf16[2,2048,128]{2,1,0:T(8,128)(2,1)}, u32[]{:S(2)}) copy-start(bf16[2,2048,128]{2,1,0:T(8,128)(2,1)} %v_ref.1) | copy-start | bytes 3145732
  10.4 13.9 %copy-start.7 = (bf16[1,256,512]{2,1,0:T(8,128)(2,1)S(1)}, bf16[1,256,512]{2,1,0:T(8,128)(2,1)}, u32[]{:S(2)}) copy-start(bf16[1,256,512]{2,1,0:T(8,128)(2,1)} %param.12) | copy-start | bytes 786436
  11.2 17.2 %copy-start.4 = (f32[1,512,320]{1,2,0:T(8,128)S(1)}, f32[1,512,320]{1,2,0:T(8,128)}, u32[]{:S(2)}) copy-start(f32[1,512,320]{1,2,0:T(8,128)} %param.15) | copy-start | bytes 1966084
  11.2 18.5 %copy-start.5 = (f32[1,512,320]{1,2,0:T(8,128)S(1)}, f32[1,512,320]{1,2,0:T(8,128)}, u32[]{:S(2)}) copy-start(f32[1,512,320]{1,2,0:T(8,128)} %param.16) | copy-start | bytes 1966084
  13.0 11.3 %collective-permute-start.1 = (bf16[16,512]{1,0:T(8,128)(2,1)S(1)}, bf16[16,512]{1,0:T(8,128)(2,1)S(1)}, u32[]{:S(2)}, u32[]{:S(2)}) collective-permute-start(bf16[16,512]{1,0:T(8,128)(2,1)S(1)} %attend.1.rows_ref), channel_id=1, source_target_pairs={{256,16},{257,17},{258,18},{259,19},{260,20},{261,21},{262,22},{26... | collective-permute-start | bytes 49160 | tf_op jit(solution)/shard_map/ppermute | solution.py:44
  25.6 0.7 collective-permute-start.4
  26.3 0.7 collective-permute-start.5
  27.0 1.4 copy-start.13
  27.0 29.0 %collective-permute-start.6 = (bf16[2,320,256]{2,1,0:T(8,128)(2,1)S(1)}, bf16[2,320,256]{2,1,0:T(8,128)(2,1)}, u32[]{:S(2)}, u32[]{:S(2)}) collective-permute-start(bf16[2,320,256]{2,1,0:T(8,128)(2,1)S(1)} %pad_maximum_fusion), channel_id=1, source_target_pairs={{4,0},{5,1},{6,2},{7,3},{12,8},{13,9},{14,10},{15,11},{20,16},{21,... | collective-permute-start | bytes 983048 | tf_op jit(solution)/shard_map/ppermute | solution.py:44
  28.4 41.1 %collective-permute-start.2 = (f32[320,512]{1,0:T(8,128)S(1)}, f32[320,512]{1,0:T(8,128)S(1)}, u32[]{:S(2)}, u32[]{:S(2)}) collective-permute-start(f32[320,512]{1,0:T(8,128)S(1)} %bitcast.23), channel_id=1, source_target_pairs={{256,0},{257,1},{258,2},{259,3},{260,4},{261,5},{262,6},{263,7},{2... | collective-permute-start | bytes 1966088 | tf_op jit(solution)/shard_map/ppermute | solution.py:44
  29.7 39.8 %collective-permute-start.3 = (f32[320,512]{1,0:T(8,128)S(1)}, f32[320,512]{1,0:T(8,128)S(1)}, u32[]{:S(2)}, u32[]{:S(2)}) collective-permute-start(f32[320,512]{1,0:T(8,128)S(1)} %bitcast.25), channel_id=1, source_target_pairs={{256,0},{257,1},{258,2},{259,3},{260,4},{261,5},{262,6},{263,7},{2... | collective-permute-start | bytes 1966088 | tf_op jit(solution)/shard_map/ppermute | solution.py:44
  31.0 52.4 %copy-start.6 = (bf16[512,320]{0,1:T(8,128)(2,1)S(1)}, bf16[512,320]{0,1:T(8,128)(2,1)}, u32[]{:S(2)}) copy-start(bf16[512,320]{0,1:T(8,128)(2,1)} %param.14) | copy-start | bytes 983044
  57.1 15.1 %collective-permute-start.9 = (bf16[2,320,256]{2,1,0:T(8,128)(2,1)S(1)}, bf16[2,320,256]{2,1,0:T(8,128)(2,1)}, u32[]{:S(2)}, u32[]{:S(2)}) collective-permute-start(bf16[2,320,256]{2,1,0:T(8,128)(2,1)S(1)} %broadcast_select_fusion.refs_0_), channel_id=1, source_target_pairs={{0,1},{1,2},{2,3},{3,0},{4,5},{5,6},{6,7},{7,4},{8,9},{9,10},{10,1... | collective-permute-start | bytes 983048 | tf_op jit(solution)/shard_map/ppermute | solution.py:44
  59.5 12.7 %collective-permute-start.8 = (bf16[2,320,256]{2,1,0:T(8,128)(2,1)S(1)}, bf16[2,320,256]{2,1,0:T(8,128)(2,1)}, u32[]{:S(2)}, u32[]{:S(2)}) collective-permute-start(bf16[2,320,256]{2,1,0:T(8,128)(2,1)S(1)} %broadcast_select_fusion.refs_0_), channel_id=1, source_target_pairs={{0,2},{1,3},{2,0},{3,1},{4,6},{5,7},{6,4},{7,5},{8,10},{9,11},{10,... | collective-permute-start | bytes 983048 | tf_op jit(solution)/shard_map/ppermute | solution.py:44
  65.5 9.1 %collective-permute-start.7 = (bf16[2,320,256]{2,1,0:T(8,128)(2,1)S(1)}, bf16[2,320,256]{2,1,0:T(8,128)(2,1)}, u32[]{:S(2)}, u32[]{:S(2)}) collective-permute-start(bf16[2,320,256]{2,1,0:T(8,128)(2,1)S(1)} %broadcast_select_fusion.refs_0_), channel_id=1, source_target_pairs={{0,3},{1,0},{2,1},{3,2},{4,7},{5,4},{6,5},{7,6},{8,11},{9,8},{10,9... | collective-permute-start | bytes 983048 | tf_op jit(solution)/shard_map/ppermute | solution.py:44
  74.5 1.6 %copy-start.1 = (bf16[2176,512]{1,0:T(8,128)(2,1)S(1)}, bf16[2176,512]{1,0:T(8,128)(2,1)}, u32[]{:S(2)}) copy-start(bf16[2176,512]{1,0:T(8,128)(2,1)} %all-gather.3.cloned.1.call-done) | copy-start | bytes 6684676
  79.0 4.4 %collective-permute-start.10 = (f32[448,512]{1,0:T(8,128)S(1)}, f32[448,512]{1,0:T(8,128)S(1)}, u32[]{:S(2)}, u32[]{:S(2)}) collective-permute-start(f32[448,512]{1,0:T(8,128)S(1)} %gradient.1.mine_ref), channel_id=1, source_target_pairs={{0,256},{1,257},{2,258},{3,259},{4,260},{5,261},{6,262},{7,263},{8... | collective-permute-start | bytes 2752520 | tf_op jit(solution)/shard_map/ppermute | solution.py:44
  104.0 10.3 %collective-permute-start.11 = (bf16[8,320]{1,0:T(8,128)(2,1)S(1)}, bf16[8,320]{1,0:T(8,128)(2,1)S(1)}, u32[]{:S(2)}, u32[]{:S(2)}) collective-permute-start(bf16[8,320]{1,0:T(8,128)(2,1)S(1)} %reduce_sum.9), channel_id=1, source_target_pairs={{0,0},{1,16},{2,32},{3,48},{4,64},{5,80},{6,96},{7,112},{8,128},{9... | collective-permute-start | bytes 15368 | tf_op jit(solution)/shard_map/ppermute | solution.py:44
Sparse Core Ops, SparseCore 0:
  25.7 46.4 all-gather.2

commit v22 on v17

--- a/solution.py
+++ b/solution.py
@@ -366,7 +366,8 @@
     pair = jnp.stack([own, permute(own, along_zl(2))])
     pair_got = permute(pair, along_zl(1))
     pair = jnp.where(place[0] == keeper(place[3]), pair, pair_got)
-    blocks = [pair] + [permute(pair, along_x(step)) for step in (1, 2, -1)]
+    near, other = permute(pair, along_x(1)), permute(pair, along_x(-1))
+    blocks = [pair, near, permute(pair, along_x(2)), other]
     one_tied, two_tied, _ = lax.optimization_barrier((one, two, base))
     one_got = permute(one_tied, to_rollout)
     two_got = permute(two_tied, to_rollout)

time: 139 us -> 139 us (level)
  no operation moved by 1% of the time
where the time goes in v22:
time: 139 us; the launch traced here: 137 us
  waiting for transfers between devices  53.9 us (39%)
  blocking collectives  29.4 us (21%)
  starting transfers between devices  27.1 us (19%)
  between operations  14.3 us (10%)
  Pallas kernels  7.99 us (6%)
  local copies, waits for them, and re-layouts  4.31 us (3%)
    ppermute x12, waiting for transfers between devices, permute(): return lax.ppermute(value, AXES, pairs)  46.9 us
    all_to_all x2, blocking collectives, gather(): return lax.all_to_all(value, axes, split_axis=0, concat_axis=0, tiled=True)  29.4 us
    ppermute x12, starting transfers between devices, permute(): return lax.ppermute(value, AXES, pairs)  27.1 us
    all_gather x1, waiting for transfers between devices, local(): chunks = lax.all_gather(base, 'y', axis=0)  6.95 us
    unnamed x26, local copies, waits for them, and re-layouts  3.41 us
  transfers between devices with their start and end apart: 13, of which 7 were waited for; matrix products, arithmetic and copies ran while one was open for 0% of the time, Pallas kernels for 2%

profile of v22, /device:TPU:56, one launch (start us, length us, event | category | flops | bytes accessed | tf_op | source)
XLA Modules:
  0.0 137.1 jit_solution(3372972027740208942)
XLA Ops:
  7.2 0.0 copy-start.11
  7.2 0.0 copy-start.12
  7.2 0.0 copy-start.9
  7.2 0.0 copy-start.8
  7.2 0.0 copy-start.10
  7.2 0.0 all-gather.3.cloned.1.call-start
  7.3 1.3 collective-permute-start
  8.6 0.1 stack.32.place_ref
  8.7 0.0 copy-start
  8.7 1.7 %copy-done = bf16[1,256,5120]{2,1,0:T(8,128)(2,1)S(1)} copy-done((bf16[1,256,5120]{2,1,0:T(8,128)(2,1)S(1)}, bf16[1,256,5120]{2,1,0:T(8,128)(2,1)}, u32[]{:S(2)}) %copy-start) | copy-done | bytes 2621464
  10.4 0.0 copy-start.2
  10.4 0.0 copy-start.3
  10.4 0.0 copy-start.7
  10.4 1.4 %cut.1 = bf16[320,256]{1,0:T(8,128)(2,1)} custom-call(s32[5]{0:T(128)S(1)} %stack.32.place_ref, bf16[256,5120]{1,0:T(8,128)(2,1)S(1)} %bitcast.21), custom_call_target="tpu_custom_call" | custom-call | tf_op jit(solution)/shard_map/cut/pallas_call | solution.py:189
  11.8 0.0 copy-start.4
  11.8 0.8 collective-permute-start.2
  12.7 0.0 copy-done.11
  12.7 0.0 copy-done.12
  12.7 0.0 copy-done.9
  12.7 0.0 copy-done.8
  12.7 0.0 copy-done.10
  12.7 0.0 copy-done.2
  12.7 0.0 copy-done.3
  12.7 1.1 attend.1.rows_ref
  13.8 1.3 collective-permute-start.1
  15.1 14.2 %collective-permute-done.1.rows_got = bf16[16,512]{1,0:T(8,128)(2,1)S(1)} collective-permute-done((bf16[16,512]{1,0:T(8,128)(2,1)S(1)}, bf16[16,512]{1,0:T(8,128)(2,1)S(1)}, u32[]{:S(2)}, u32[]{:S(2)}) %collective-permute-start.1) | collective-permute-done | bytes 16416 | tf_op jit(solution)/shard_map/ppermute | solution.py:44
  29.2 0.0 collective-permute-done.2._
  29.2 0.0 collective-permute-done.act_got
  29.3 0.0 copy-done.7
  29.3 1.3 base.1
  30.5 0.0 all-gather.3.cloned.1.call-update
  30.6 0.7 collective-permute-start.3
  31.2 0.0 collective-permute-done.3
  31.3 1.3 collective-permute-start.4
  32.6 0.0 copy-done.4
  32.6 1.3 collective-permute-start.8
  33.9 1.3 collective-permute-start.9
  35.2 12.8 %collective-permute-done.4 = bf16[2,320,256]{2,1,0:T(8,128)(2,1)S(1)} collective-permute-done((bf16[2,320,256]{2,1,0:T(8,128)(2,1)S(1)}, bf16[2,320,256]{2,1,0:T(8,128)(2,1)S(1)}, u32[]{:S(2)}, u32[]{:S(2)}) %collective-permute-start.4) | collective-permute-done | bytes 327712 | tf_op jit(solution)/shard_map/ppermute | solution.py:44
  48.1 3.2 %collective-permute-start.7 = (bf16[2,320,256]{2,1,0:T(8,128)(2,1)S(1)}, bf16[2,320,256]{2,1,0:T(8,128)(2,1)S(1)}, u32[]{:S(2)}, u32[]{:S(2)}) collective-permute-start(bf16[2,320,256]{2,1,0:T(8,128)(2,1)S(1)} %broadcast_select_fusion.refs_0_), channel_id=1, source_target_pairs={{0,1},{1,2},{2,3},{3,0},{4,5},{5,6},{6,7},{7,4},{8,9},{9,10},{10,1... | collective-permute-start | bytes 983048 | tf_op jit(solution)/shard_map/ppermute | solution.py:44
  51.3 7.2 %collective-permute-start.6 = (bf16[2,320,256]{2,1,0:T(8,128)(2,1)S(1)}, bf16[2,320,256]{2,1,0:T(8,128)(2,1)S(1)}, u32[]{:S(2)}, u32[]{:S(2)}) collective-permute-start(bf16[2,320,256]{2,1,0:T(8,128)(2,1)S(1)} %broadcast_select_fusion.refs_0_), channel_id=1, source_target_pairs={{0,2},{1,3},{2,0},{3,1},{4,6},{5,7},{6,4},{7,5},{8,10},{9,11},{10,... | collective-permute-start | bytes 983048 | tf_op jit(solution)/shard_map/ppermute | solution.py:44
  58.5 2.2 %collective-permute-start.5 = (bf16[2,320,256]{2,1,0:T(8,128)(2,1)S(1)}, bf16[2,320,256]{2,1,0:T(8,128)(2,1)S(1)}, u32[]{:S(2)}, u32[]{:S(2)}) collective-permute-start(bf16[2,320,256]{2,1,0:T(8,128)(2,1)S(1)} %broadcast_select_fusion.refs_0_), channel_id=1, source_target_pairs={{0,3},{1,0},{2,1},{3,2},{4,7},{5,4},{6,5},{7,6},{8,11},{9,8},{10,9... | collective-permute-start | bytes 983048 | tf_op jit(solution)/shard_map/ppermute | solution.py:44
  60.7 0.0 collective-permute-done.8.refs_4_.one_got
  60.7 0.0 collective-permute-done.9.refs_5_.two_got
  60.7 0.3 collective-permute-done.7.refs_3_
  61.1 9.9 %collective-permute-done.6.refs_2_ = bf16[2,320,256]{2,1,0:T(8,128)(2,1)S(1)} collective-permute-done((bf16[2,320,256]{2,1,0:T(8,128)(2,1)S(1)}, bf16[2,320,256]{2,1,0:T(8,128)(2,1)S(1)}, u32[]{:S(2)}, u32[]{:S(2)}) %collective-permute-start.6) | collective-permute-done | bytes 327712 | tf_op jit(solution)/shard_map/ppermute | solution.py:44
  71.0 0.0 collective-permute-done.5.refs_1_
  71.0 7.0 %all-gather.3.cloned.1.call-done = bf16[2176,512]{1,0:T(8,128)(2,1)} async-done(((bf16[272,512]{1,0:T(8,128)(2,1)}), bf16[2176,512]{1,0:T(8,128)(2,1)}) %all-gather.3.cloned.1.call-update) | async-done | bytes 2228240 | tf_op jit(solution)/shard_map/all_gather | solution.py:362
  77.9 0.0 copy-start.1
  77.9 1.6 %copy-done.1 = bf16[2176,512]{1,0:T(8,128)(2,1)S(1)} copy-done((bf16[2176,512]{1,0:T(8,128)(2,1)S(1)}, bf16[2176,512]{1,0:T(8,128)(2,1)}, u32[]{:S(2)}) %copy-start.1) | copy-done | bytes 2228248
  79.6 0.0 copy-start.5
  79.6 0.0 copy-start.6
  79.6 2.3 %gradient.1.mine_ref = f32[448,512]{1,0:T(8,128)S(1)} custom-call(s32[5]{0:T(128)S(1)} %stack.32.place_ref, bf16[8,272,512]{2,1,0:T(8,128)(2,1)S(1)} %bitcast.22, bf16[2,320,256]{2,1,0:T(8,128)(2,1)S(1)} %broadcast_select_fusion.refs_0_, bf16[2,320,256]{2,1,0:T(8,128)(2,1)S(1)} %collective-permute-done.5.refs_1_, ...), custom_call_target="tpu_custom_call" | custom-call | tf_op jit(solution)/shard_map/gradient/pallas_call | solution.py:277
  81.9 1.9 %collective-permute-start.10 = (f32[448,512]{1,0:T(8,128)S(1)}, f32[448,512]{1,0:T(8,128)S(1)}, u32[]{:S(2)}, u32[]{:S(2)}) collective-permute-start(f32[448,512]{1,0:T(8,128)S(1)} %gradient.1.mine_ref), channel_id=1, source_target_pairs={{0,256},{1,257},{2,258},{3,259},{4,260},{5,261},{6,262},{7,263},{8... | collective-permute-start | bytes 2752520 | tf_op jit(solution)/shard_map/ppermute | solution.py:44
  83.8 2.4 %collective-permute-done.10.got_ref = f32[448,512]{1,0:T(8,128)S(1)} collective-permute-done((f32[448,512]{1,0:T(8,128)S(1)}, f32[448,512]{1,0:T(8,128)S(1)}, u32[]{:S(2)}, u32[]{:S(2)}) %collective-permute-start.10) | collective-permute-done | bytes 917536 | tf_op jit(solution)/shard_map/ppermute | solution.py:44
  86.3 0.0 copy-done.5
  86.3 0.0 copy-done.6
  86.3 1.9 %step.1 = (bf16[320,512]{1,0:T(8,128)(2,1)}, f32[16,8,320]{2,1,0:T(8,128)S(1)}) custom-call(s32[5]{0:T(128)S(1)} %stack.32.place_ref, f32[448,512]{1,0:T(8,128)S(1)} %gradient.1.mine_ref, f32[448,512]{1,0:T(8,128)S(1)} %collective-permute-done.10.got_ref, f32[320,512]{1,0:T(8,128)S(1)} %bitcast.26, f32[320,512]{1,0:T(8,128)S(1)} %collective-permute-done.8.refs_4_.one_got, ...), custom_call_target="tpu_custom_call" | custom-call | tf_op jit(solution)/shard_map/step/pallas_call | solution.py:316
  88.2 17.3 %all_to_all.10 = f32[16,8,320]{2,1,0:T(8,128)S(1)} all-to-all(f32[16,8,320]{2,1,0:T(8,128)S(1)} %get-tuple-element.11), channel_id=1, replica_groups=mesh['group'=2,'y'=8,'z_hi'=2,'z_lo'=4,'x'=4] {'z_lo','x'}, dimensions={0} | all-to-all | bytes 327680 | tf_op jit(solution)/shard_map/all_to_all | solution.py:48
  105.5 4.6 %collective-permute-start.11 = (bf16[8,320]{1,0:T(8,128)(2,1)S(1)}, bf16[8,320]{1,0:T(8,128)(2,1)S(1)}, u32[]{:S(2)}, u32[]{:S(2)}) collective-permute-start(bf16[8,320]{1,0:T(8,128)(2,1)S(1)} %reduce_sum.9), channel_id=1, source_target_pairs={{0,0},{1,16},{2,32},{3,48},{4,64},{5,80},{6,96},{7,112},{8,128},{9... | collective-permute-start | bytes 15368 | tf_op jit(solution)/shard_map/ppermute | solution.py:44
  110.2 7.2 %collective-permute-done.11 = bf16[8,320]{1,0:T(8,128)(2,1)S(1)} collective-permute-done((bf16[8,320]{1,0:T(8,128)(2,1)S(1)}, bf16[8,320]{1,0:T(8,128)(2,1)S(1)}, u32[]{:S(2)}, u32[]{:S(2)}) %collective-permute-start.11) | collective-permute-done | bytes 5152 | tf_op jit(solution)/shard_map/ppermute | solution.py:44
  117.4 12.1 %all_to_all.11 = bf16[16,8,320]{2,1,0:T(8,128)(2,1)S(1)} all-to-all(bf16[16,8,320]{2,1,0:T(8,128)(2,1)S(1)} %broadcast_in_dim.2), channel_id=1, replica_groups=mesh['group'=2,'y'=8,'z_hi'=2,'z_lo'=4,'x'=4] {'z_lo','x'}, dimensions={0} | all-to-all | bytes 163840 | tf_op jit(solution)/shard_map/all_to_all | solution.py:48
  129.5 0.8 reshape.12
  (5 shorter events, 0.1 us)
Async XLA Ops:
  7.2 5.5 %copy-start.11 = (s32[4,2]{0,1:T(2,128)S(1)}, s32[4,2]{0,1:T(2,128)}, u32[]{:S(2)}) copy-start(s32[4,2]{0,1:T(2,128)} %param.23) | copy-start | bytes 100
  7.2 5.5 %copy-start.12 = (s32[2]{0:T(128)S(1)}, s32[2]{0:T(128)}, u32[]{:S(2)}) copy-start(s32[2]{0:T(128)} %lengths_ref.1) | copy-start | bytes 28
  7.2 5.5 %copy-start.9 = (bf16[4,2,1024]{2,1,0:T(2,128)(2,1)S(1)}, bf16[4,2,1024]{2,1,0:T(2,128)(2,1)}, u32[]{:S(2)}) copy-start(bf16[4,2,1024]{2,1,0:T(2,128)(2,1)} %nv_ref.1) | copy-start | bytes 49156
  7.2 5.5 %copy-start.8 = (bf16[4,2,1024]{2,1,0:T(2,128)(2,1)S(1)}, bf16[4,2,1024]{2,1,0:T(2,128)(2,1)}, u32[]{:S(2)}) copy-start(bf16[4,2,1024]{2,1,0:T(2,128)(2,1)} %nk_ref.1) | copy-start | bytes 49156
  7.2 5.5 %copy-start.10 = (bf16[4,2,512]{2,1,0:T(2,128)(2,1)S(1)}, bf16[4,2,512]{2,1,0:T(2,128)(2,1)}, u32[]{:S(2)}) copy-start(bf16[4,2,512]{2,1,0:T(2,128)(2,1)} %q_ref.1) | copy-start | bytes 24580
  7.2 70.7 %all-gather.3.cloned.1.call-start = ((), (), s32[]{:S(2)}) async-start(), calls=%async_computation.2 | async-start | bytes 2506752 | tf_op jit(solution)/shard_map/all_gather | solution.py:362
  7.3 22.0 %collective-permute-start = (bf16[256,512]{1,0:T(8,128)(2,1)}, bf16[256,512]{1,0:T(8,128)(2,1)S(1)}, u32[]{:S(2)}, u32[]{:S(2)}) collective-permute-start(bf16[256,512]{1,0:T(8,128)(2,1)} %bitcast.30), channel_id=1, source_target_pairs={{256,16},{257,17},{258,18},{259,19},{260,20},{261,21},{262,22},{26... | collective-permute-start | bytes 786440 | tf_op jit(solution)/shard_map/ppermute | solution.py:44
  8.7 1.7 %copy-start = (bf16[1,256,5120]{2,1,0:T(8,128)(2,1)S(1)}, bf16[1,256,5120]{2,1,0:T(8,128)(2,1)}, u32[]{:S(2)}) copy-start(bf16[1,256,5120]{2,1,0:T(8,128)(2,1)} %param.13) | copy-start | bytes 7864324
  10.4 2.3 %copy-start.2 = (bf16[2,2048,128]{2,1,0:T(8,128)(2,1)S(1)}, bf16[2,2048,128]{2,1,0:T(8,128)(2,1)}, u32[]{:S(2)}) copy-start(bf16[2,2048,128]{2,1,0:T(8,128)(2,1)} %k_ref.1) | copy-start | bytes 3145732
  10.4 2.3 %copy-start.3 = (bf16[2,2048,128]{2,1,0:T(8,128)(2,1)S(1)}, bf16[2,2048,128]{2,1,0:T(8,128)(2,1)}, u32[]{:S(2)}) copy-start(bf16[2,2048,128]{2,1,0:T(8,128)(2,1)} %v_ref.1) | copy-start | bytes 3145732
  10.4 18.9 %copy-start.7 = (bf16[1,256,512]{2,1,0:T(8,128)(2,1)S(1)}, bf16[1,256,512]{2,1,0:T(8,128)(2,1)}, u32[]{:S(2)}) copy-start(bf16[1,256,512]{2,1,0:T(8,128)(2,1)} %param.12) | copy-start | bytes 786436
  11.8 20.8 %copy-start.4 = (f32[1,512,320]{1,2,0:T(8,128)S(1)}, f32[1,512,320]{1,2,0:T(8,128)}, u32[]{:S(2)}) copy-start(f32[1,512,320]{1,2,0:T(8,128)} %param.15) | copy-start | bytes 1966084
  11.8 17.4 %collective-permute-start.2 = (bf16[320,256]{1,0:T(8,128)(2,1)}, bf16[320,256]{1,0:T(8,128)(2,1)S(1)}, u32[]{:S(2)}, u32[]{:S(2)}) collective-permute-start(bf16[320,256]{1,0:T(8,128)(2,1)} %cut.1), channel_id=1, source_target_pairs={{256,352},{257,321},{258,290},{259,259},{260,116},{261,85},{262,54... | collective-permute-start | bytes 491528 | tf_op jit(solution)/shard_map/ppermute | solution.py:44
  13.8 15.5 %collective-permute-start.1 = (bf16[16,512]{1,0:T(8,128)(2,1)S(1)}, bf16[16,512]{1,0:T(8,128)(2,1)S(1)}, u32[]{:S(2)}, u32[]{:S(2)}) collective-permute-start(bf16[16,512]{1,0:T(8,128)(2,1)S(1)} %attend.1.rows_ref), channel_id=1, source_target_pairs={{256,16},{257,17},{258,18},{259,19},{260,20},{261,21},{262,22},{26... | collective-permute-start | bytes 49160 | tf_op jit(solution)/shard_map/ppermute | solution.py:44
  30.6 0.7 collective-permute-start.3
  31.3 16.7 %collective-permute-start.4 = (bf16[2,320,256]{2,1,0:T(8,128)(2,1)S(1)}, bf16[2,320,256]{2,1,0:T(8,128)(2,1)S(1)}, u32[]{:S(2)}, u32[]{:S(2)}) collective-permute-start(bf16[2,320,256]{2,1,0:T(8,128)(2,1)S(1)} %pad_maximum_fusion), channel_id=1, source_target_pairs={{4,0},{5,1},{6,2},{7,3},{12,8},{13,9},{14,10},{15,11},{20,16},{21,... | collective-permute-start | bytes 983048 | tf_op jit(solution)/shard_map/ppermute | solution.py:44
  32.6 28.1 %collective-permute-start.8 = (f32[320,512]{1,0:T(8,128)S(1)}, f32[320,512]{1,0:T(8,128)S(1)}, u32[]{:S(2)}, u32[]{:S(2)}) collective-permute-start(f32[320,512]{1,0:T(8,128)S(1)} %bitcast.25), channel_id=1, source_target_pairs={{256,0},{257,1},{258,2},{259,3},{260,4},{261,5},{262,6},{263,7},{2... | collective-permute-start | bytes 1966088 | tf_op jit(solution)/shard_map/ppermute | solution.py:44
  33.9 26.8 %collective-permute-start.9 = (f32[320,512]{1,0:T(8,128)}, f32[320,512]{1,0:T(8,128)S(1)}, u32[]{:S(2)}, u32[]{:S(2)}) collective-permute-start(f32[320,512]{1,0:T(8,128)} %bitcast.27), channel_id=1, source_target_pairs={{256,0},{257,1},{258,2},{259,3},{260,4},{261,5},{262,6},{263,7},{2... | collective-permute-start | bytes 1966088 | tf_op jit(solution)/shard_map/ppermute | solution.py:44
  48.1 13.0 %collective-permute-start.7 = (bf16[2,320,256]{2,1,0:T(8,128)(2,1)S(1)}, bf16[2,320,256]{2,1,0:T(8,128)(2,1)S(1)}, u32[]{:S(2)}, u32[]{:S(2)}) collective-permute-start(bf16[2,320,256]{2,1,0:T(8,128)(2,1)S(1)} %broadcast_select_fusion.refs_0_), channel_id=1, source_target_pairs={{0,1},{1,2},{2,3},{3,0},{4,5},{5,6},{6,7},{7,4},{8,9},{9,10},{10,1... | collective-permute-start | bytes 983048 | tf_op jit(solution)/shard_map/ppermute | solution.py:44
  51.3 19.7 %collective-permute-start.6 = (bf16[2,320,256]{2,1,0:T(8,128)(2,1)S(1)}, bf16[2,320,256]{2,1,0:T(8,128)(2,1)S(1)}, u32[]{:S(2)}, u32[]{:S(2)}) collective-permute-start(bf16[2,320,256]{2,1,0:T(8,128)(2,1)S(1)} %broadcast_select_fusion.refs_0_), channel_id=1, source_target_pairs={{0,2},{1,3},{2,0},{3,1},{4,6},{5,7},{6,4},{7,5},{8,10},{9,11},{10,... | collective-permute-start | bytes 983048 | tf_op jit(solution)/shard_map/ppermute | solution.py:44
  58.5 12.5 %collective-permute-start.5 = (bf16[2,320,256]{2,1,0:T(8,128)(2,1)S(1)}, bf16[2,320,256]{2,1,0:T(8,128)(2,1)S(1)}, u32[]{:S(2)}, u32[]{:S(2)}) collective-permute-start(bf16[2,320,256]{2,1,0:T(8,128)(2,1)S(1)} %broadcast_select_fusion.refs_0_), channel_id=1, source_target_pairs={{0,3},{1,0},{2,1},{3,2},{4,7},{5,4},{6,5},{7,6},{8,11},{9,8},{10,9... | collective-permute-start | bytes 983048 | tf_op jit(solution)/shard_map/ppermute | solution.py:44
  77.9 1.6 %copy-start.1 = (bf16[2176,512]{1,0:T(8,128)(2,1)S(1)}, bf16[2176,512]{1,0:T(8,128)(2,1)}, u32[]{:S(2)}) copy-start(bf16[2176,512]{1,0:T(8,128)(2,1)} %all-gather.3.cloned.1.call-done) | copy-start | bytes 6684676
  79.6 6.7 %copy-start.5 = (f32[1,512,320]{1,2,0:T(8,128)S(1)}, f32[1,512,320]{1,2,0:T(8,128)}, u32[]{:S(2)}) copy-start(f32[1,512,320]{1,2,0:T(8,128)} %param.16) | copy-start | bytes 1966084
  79.6 6.7 %copy-start.6 = (bf16[512,320]{0,1:T(8,128)(2,1)S(1)}, bf16[512,320]{0,1:T(8,128)(2,1)}, u32[]{:S(2)}) copy-start(bf16[512,320]{0,1:T(8,128)(2,1)} %param.14) | copy-start | bytes 983044
  81.9 4.4 %collective-permute-start.10 = (f32[448,512]{1,0:T(8,128)S(1)}, f32[448,512]{1,0:T(8,128)S(1)}, u32[]{:S(2)}, u32[]{:S(2)}) collective-permute-start(f32[448,512]{1,0:T(8,128)S(1)} %gradient.1.mine_ref), channel_id=1, source_target_pairs={{0,256},{1,257},{2,258},{3,259},{4,260},{5,261},{6,262},{7,263},{8... | collective-permute-start | bytes 2752520 | tf_op jit(solution)/shard_map/ppermute | solution.py:44
  105.5 11.8 %collective-permute-start.11 = (bf16[8,320]{1,0:T(8,128)(2,1)S(1)}, bf16[8,320]{1,0:T(8,128)(2,1)S(1)}, u32[]{:S(2)}, u32[]{:S(2)}) collective-permute-start(bf16[8,320]{1,0:T(8,128)(2,1)S(1)} %reduce_sum.9), channel_id=1, source_target_pairs={{0,0},{1,16},{2,32},{3,48},{4,64},{5,80},{6,96},{7,112},{8,128},{9... | collective-permute-start | bytes 15368 | tf_op jit(solution)/shard_map/ppermute | solution.py:44
Sparse Core Ops, SparseCore 0:
  30.7 47.2 all-gather.2
